TPU v7x, 32 devices: a whole 2x2x4 slice. The times are simulated.
32 devices in a mesh: grp: 2 (over x), slab: 16 (over z, y, core).
Axes of the slice: x: 2, y: 2, z: 4, core: 2. Of those that a mesh axis runs over, the one named last changes fastest.
Arguments:
- volume: float32 [2048, 16, 1024], P('slab', 'grp'), parts along dimension 1, may hold values from -6 to 6
- sinogram: bfloat16 [2048, 16, 1024], P('slab', 'grp'), parts along dimension 1, may hold values from -6 to 6
- weights: bfloat16 [8, 128, 128], replicated, may hold values from -0.21875 to 0.21875
- coverage: int32 [16, 6], replicated, may hold values 0 or 1
- offsets: int32 [16, 6], replicated, may hold values from 0 to 7
Outputs:
- gradient: float32 [2048, 16, 1024], P('slab', 'grp'), parts along dimension 1
- residual: bfloat16 [2048, 16, 1024], P('slab', 'grp'), parts along dimension 1
There are 2 independent parts, one for each index of `grp`. A program takes and returns all parts, laid end to end along the dimension named above; an argument that names none is the same for every part. Nothing has to cross between parts.
All inputs are finite; a program needn't handle non-finite values.
Results may differ from a plain program's by a relative error of at most 0.0034.
Values may be sent and summed in bfloat16 or wider, within the bound.
No kernel may reach another device: no remote copies, remote signals or barrier semaphores. Data moves between devices by JAX's collectives and lax.ppermute only.
A program may use at most 128 MiB of HBM per device.

v0:
```python
import jax
import jax.numpy as jnp
from jax import lax
from jax.sharding import PartitionSpec as P


def shifted(value, axis, steps):
    count = lax.axis_size(axis)
    first, last = (max(0, -steps), min(count, count - steps))
    return lax.ppermute(value, axis, [(source, source + steps) for source in range(first, last)])


def padded_2(block, sides, width):
    for axis, dim in sides:
        count = lax.axis_size(axis)
        forward = [(i, i + 1) for i in range(count - 1)]
        backward = [(target, source) for source, target in forward]
        low = lax.ppermute(
            lax.slice_in_dim(block, block.shape[dim] - width, None, axis=dim), axis, forward
        )
        high = lax.ppermute(lax.slice_in_dim(block, 0, width, axis=dim), axis, backward)
        block = jnp.concatenate([low, block, high], axis=dim)
    return block


def tv_from(full):
    base = full[:-1, :-1, :-1]
    diff_z = full[1:, :-1, :-1] - base
    diff_y = full[:-1, 1:, :-1] - base
    diff_x = full[:-1, :-1, 1:] - base
    scale = 1.0 / jnp.sqrt(diff_z * diff_z + diff_y * diff_y + diff_x * diff_x + 0.25)
    flux_z = diff_z * scale
    flux_y = diff_y * scale
    flux_x = diff_x * scale
    total = flux_z[:-1, 1:, 1:] - flux_z[1:, 1:, 1:]
    total = total + flux_y[1:, :-1, 1:] - flux_y[1:, 1:, 1:]
    total = total + flux_x[1:, 1:, :-1] - flux_x[1:, 1:, 1:]
    return total


def local(volume, sinogram, weights, coverage, offsets):
    slabs = lax.axis_size("slab")
    here = lax.axis_index("slab")
    depth, strip_rows, strip_cols = volume.shape
    span = coverage.shape[1]
    group = sinogram.shape[0]
    flat = volume.astype(jnp.bfloat16).reshape(depth, strip_rows * strip_cols)

    def pick(source, k):
        safe = jnp.clip(source, 0, slabs - 1)
        inside = jnp.logical_and(source >= 0, source < slabs).astype(jnp.float32)
        seen = lax.dynamic_index_in_dim(coverage[:, k], safe, 0, keepdims=False).astype(jnp.float32)
        which = lax.dynamic_index_in_dim(offsets[:, k], safe, 0, keepdims=False)
        block_w = lax.dynamic_index_in_dim(weights, which, 0, keepdims=False)
        return (block_w, inside * seen)

    def own_term(k, slices):
        block_w, live = pick(here, k)
        return live * jnp.dot(block_w, slices, preferred_element_type=jnp.float32)

    projection = own_term(0, flat)
    moving = flat
    for k in range(1, span):
        moving = shifted(moving, "slab", -1)
        projection = projection + own_term(k, moving)
    measured = sinogram.reshape(group, strip_rows * strip_cols).astype(jnp.float32)
    residual = (projection - measured).astype(jnp.bfloat16)

    def back_term(k, resid_piece):
        block_w, live = pick(here - k, k)
        return live * jnp.dot(block_w.T, resid_piece, preferred_element_type=jnp.float32)

    backproj = back_term(0, residual)
    carried = residual
    for k in range(1, span):
        carried = shifted(carried, "slab", 1)
        backproj = backproj + back_term(k, carried)
    padded = padded_2(volume.astype(jnp.bfloat16), (("slab", 0),), 1).astype(volume.dtype)
    tvgrad = tv_from(jnp.pad(padded, ((0, 0), (1, 1), (1, 1))))
    gradient = backproj.reshape(volume.shape) + 0.5 * tvgrad
    return (gradient, residual.reshape(sinogram.shape))


def solution(mesh):
    placed = (P("slab", "grp", None), P("slab", "grp", None), P(), P(), P())
    return jax.shard_map(
        local,
        mesh=mesh,
        in_specs=placed,
        out_specs=(P("slab", "grp", None), P("slab", "grp", None)),
        check_vma=False,
    )
```

profile of v0, /device:TPU:10, one launch (start us, length us, event | category | flops | bytes accessed | tf_op | source)
XLA Modules:
  0.0 333.5 jit_solution(5113780329869946093)
XLA Ops:
  0.7 2.5 convert_element_type.97
  3.2 1.4 copy.7
  4.6 1.3 copy-done.4
  6.0 2.7 collective-permute-start
  8.7 23.5 %collective-permute-done = bf16[128,8192]{1,0:T(8,128)(2,1)S(1)} collective-permute-done((bf16[128,8192]{1,0:T(8,128)(2,1)S(1)}, bf16[128,8192]{1,0:T(8,128)(2,1)S(1)}, u32[]{:S(2)}, u32[]{:S(2)}) %collective-permute-start) | collective-permute-done | bytes 2097184 | tf_op jit(solution)/shard_map/ppermute | solution.py:10
  32.2 1.4 copy-done.5
  33.6 4.7 %collective-permute-start.1 = (bf16[128,8192]{1,0:T(8,128)(2,1)S(1)}, bf16[128,8192]{1,0:T(8,128)(2,1)S(1)}, u32[]{:S(2)}, u32[]{:S(2)}) collective-permute-start(bf16[128,8192]{1,0:T(8,128)(2,1)S(1)} %collective-permute-done), channel_id=1, source_target_pairs={{1,0},{2,1},{3,2},{4,3},{5,4},{6,5},{7,6},{8,7},{9,8},{10,9},{11,1... | collective-permute-start | bytes 6291464 | tf_op jit(solution)/shard_map/ppermute | solution.py:10
  38.3 23.5 %collective-permute-done.1 = bf16[128,8192]{1,0:T(8,128)(2,1)S(1)} collective-permute-done((bf16[128,8192]{1,0:T(8,128)(2,1)S(1)}, bf16[128,8192]{1,0:T(8,128)(2,1)S(1)}, u32[]{:S(2)}, u32[]{:S(2)}) %collective-permute-start.1) | collective-permute-done | bytes 2097184 | tf_op jit(solution)/shard_map/ppermute | solution.py:10
  61.8 1.4 copy-done.6
  63.2 4.7 %collective-permute-start.2 = (bf16[128,8192]{1,0:T(8,128)(2,1)S(1)}, bf16[128,8192]{1,0:T(8,128)(2,1)}, u32[]{:S(2)}, u32[]{:S(2)}) collective-permute-start(bf16[128,8192]{1,0:T(8,128)(2,1)S(1)} %collective-permute-done.1), channel_id=1, source_target_pairs={{1,0},{2,1},{3,2},{4,3},{5,4},{6,5},{7,6},{8,7},{9,8},{10,9},{11,1... | collective-permute-start | bytes 6291464 | tf_op jit(solution)/shard_map/ppermute | solution.py:10
  67.9 23.5 %collective-permute-done.2 = bf16[128,8192]{1,0:T(8,128)(2,1)} collective-permute-done((bf16[128,8192]{1,0:T(8,128)(2,1)S(1)}, bf16[128,8192]{1,0:T(8,128)(2,1)}, u32[]{:S(2)}, u32[]{:S(2)}) %collective-permute-start.2) | collective-permute-done | bytes 2097184 | tf_op jit(solution)/shard_map/ppermute | solution.py:10
  91.5 4.8 %collective-permute-start.3 = (bf16[128,8192]{1,0:T(8,128)(2,1)}, bf16[128,8192]{1,0:T(8,128)(2,1)}, u32[]{:S(2)}, u32[]{:S(2)}) collective-permute-start(bf16[128,8192]{1,0:T(8,128)(2,1)} %collective-permute-done.2), channel_id=1, source_target_pairs={{1,0},{2,1},{3,2},{4,3},{5,4},{6,5},{7,6},{8,7},{9,8},{10,9},{11,1... | collective-permute-start | bytes 6291464 | tf_op jit(solution)/shard_map/ppermute | solution.py:10
  96.3 0.7 constant_dynamic-slice_fusion.8
  100.2 19.9 %collective-permute-done.3 = bf16[128,8192]{1,0:T(8,128)(2,1)} collective-permute-done((bf16[128,8192]{1,0:T(8,128)(2,1)}, bf16[128,8192]{1,0:T(8,128)(2,1)}, u32[]{:S(2)}, u32[]{:S(2)}) %collective-permute-start.3) | collective-permute-done | bytes 2097184 | tf_op jit(solution)/shard_map/ppermute | solution.py:10
  120.1 4.7 %collective-permute-start.4 = (bf16[128,8192]{1,0:T(8,128)(2,1)}, bf16[128,8192]{1,0:T(8,128)(2,1)}, u32[]{:S(2)}, u32[]{:S(2)}) collective-permute-start(bf16[128,8192]{1,0:T(8,128)(2,1)} %collective-permute-done.3), channel_id=1, source_target_pairs={{1,0},{2,1},{3,2},{4,3},{5,4},{6,5},{7,6},{8,7},{9,8},{10,9},{11,1... | collective-permute-start | bytes 6291464 | tf_op jit(solution)/shard_map/ppermute | solution.py:10
  124.8 4.3 %convolution_multiply_fusion.11 = f32[128,8192]{1,0:T(8,128)} fusion(bf16[128,8192]{1,0:T(8,128)(2,1)} %bitcast.84, f32[]{:T(128)S(6)} %mul.128, bf16[8,128,128]{2,1,0:T(8,128)(2,1)S(1)} %copy-done, s32[]{:T(128)S(6)} %select_n.60), kind=kOutput, calls=%fused_computation.25 | convolution fusion | flops 269484032 | bytes 6324232 | tf_op jit(solution)/shard_map/dot_general | solution.py:59
  139.4 0.7 constant_dynamic-slice_fusion.5
  141.3 5.3 %copy.8 = f32[16,8,8,1024]{3,1,2,0:T(8,128)} copy(bf16[16,8,8,1024]{3,2,1,0:T(8,128)(2,1)} %bitcast.85) | data formatting | bytes 6291456
  149.8 3.7 %fusion.9 = f32[128,8192]{1,0:T(8,128)S(1)} fusion(f32[128,8192]{1,0:T(8,128)} %convolution_multiply_fusion.11, bf16[128,8192]{1,0:T(8,128)(2,1)} %copy-done.5, f32[]{:T(128)S(6)} %mul.131, bf16[8,128,128]{2,1,0:T(8,128)(2,1)S(1)} %copy-done, s32[]{:T(128)S(6)} %select_n.61), kind=kOutput, calls=%fused_computation.24 | convolution fusion | flops 270532608 | bytes 10518536 | tf_op jit(solution)/shard_map/dot_general | solution.py:59
  153.5 0.7 fusion.8
  154.2 2.4 fusion.7
  156.6 2.5 fusion.6
  159.4 2.3 fusion.11
  161.8 1.3 copy-done.1
  163.1 1.9 collective-permute-start.5
  165.0 26.4 %collective-permute-done.5 = bf16[128,8192]{1,0:T(8,128)(2,1)} collective-permute-done((bf16[128,8192]{1,0:T(8,128)(2,1)S(1)}, bf16[128,8192]{1,0:T(8,128)(2,1)}, u32[]{:S(2)}, u32[]{:S(2)}) %collective-permute-start.5) | collective-permute-done | bytes 2097184 | tf_op jit(solution)/shard_map/ppermute | solution.py:10
  191.4 1.9 collective-permute-start.6
  193.3 1.9 collective-permute-start.10
  195.3 4.5 %collective-permute-start.11 = (bf16[1,8,1024]{2,1,0:T(8,128)(2,1)S(1)}, bf16[1,8,1024]{2,1,0:T(8,128)(2,1)S(1)}, u32[]{:S(2)}, u32[]{:S(2)}) collective-permute-start(bf16[1,8,1024]{2,1,0:T(8,128)(2,1)S(1)} %get-tuple-element.7), channel_id=1, source_target_pairs={{1,0},{2,1},{3,2},{4,3},{5,4},{6,5},{7,6},{8,7},{9,8},{10,9},{11,1... | collective-permute-start | bytes 49160 | tf_op jit(solution)/shard_map/ppermute | solution.py:21
  212.5 7.6 %collective-permute-done.6 = bf16[128,8192]{1,0:T(8,128)(2,1)} collective-permute-done((bf16[128,8192]{1,0:T(8,128)(2,1)}, bf16[128,8192]{1,0:T(8,128)(2,1)}, u32[]{:S(2)}, u32[]{:S(2)}) %collective-permute-start.6) | collective-permute-done | bytes 2097184 | tf_op jit(solution)/shard_map/ppermute | solution.py:10
  220.1 2.1 collective-permute-start.7
  222.2 10.4 %fusion.15 = f32[130,10,1026]{2,1,0:T(8,128)S(1)} fusion(bf16[1,8,1024]{2,1,0:T(8,128)(2,1)S(1)} %collective-permute-done.11, bf16[128,8,1024]{2,1,0:T(8,128)(2,1)S(1)} %convert_element_type.97, bf16[1,8,1024]{2,1,0:T(8,128)(2,1)S(1)} %collective-permute-done.10), kind=kLoop, calls=%fused_computation.36 | loop fusion | flops 25342200 | bytes 7465120 | tf_op jit(solution)/shard_map/jit(_pad)/pad | solution.py:79
  232.6 6.6 %fusion.20 = (f32[129,9,1025]{2,1,0:T(8,128)}, f32[129,9,1025]{2,1,0:T(8,128)S(1)}) fusion(f32[130,10,1026]{2,1,0:T(8,128)S(1)} %fusion.15), kind=kLoop, calls=%fused_computation.48 | loop fusion | flops 11900250 | bytes 28560600 | tf_op jit(solution)/shard_map/mul | solution.py:32
  239.2 9.4 %collective-permute-done.7 = bf16[128,8192]{1,0:T(8,128)(2,1)} collective-permute-done((bf16[128,8192]{1,0:T(8,128)(2,1)}, bf16[128,8192]{1,0:T(8,128)(2,1)}, u32[]{:S(2)}, u32[]{:S(2)}) %collective-permute-start.7) | collective-permute-done | bytes 2097184 | tf_op jit(solution)/shard_map/ppermute | solution.py:10
  248.6 1.9 collective-permute-start.8
  250.6 7.4 %fusion.21 = (f32[129,9,1025]{2,1,0:T(8,128)}, f32[129,9,1025]{2,1,0:T(8,128)}) fusion(f32[129,9,1025]{2,1,0:T(8,128)S(1)} %get-tuple-element.3, f32[130,10,1026]{2,1,0:T(8,128)S(1)} %fusion.15), kind=kLoop, calls=%fused_computation.49 | loop fusion | flops 4760100 | bytes 28560600 | tf_op jit(solution)/shard_map/mul | solution.py:33
  258.0 19.2 %collective-permute-done.8 = bf16[128,8192]{1,0:T(8,128)(2,1)} collective-permute-done((bf16[128,8192]{1,0:T(8,128)(2,1)}, bf16[128,8192]{1,0:T(8,128)(2,1)}, u32[]{:S(2)}, u32[]{:S(2)}) %collective-permute-start.8) | collective-permute-done | bytes 2097184 | tf_op jit(solution)/shard_map/ppermute | solution.py:10
  277.2 1.9 collective-permute-start.9
  279.1 2.3 convolution_multiply_fusion.5
  281.5 2.7 copy.10
  284.2 2.4 fusion.4
  286.6 2.4 fusion.3
  289.0 2.4 fusion.2
  291.3 2.4 fusion.1
  293.7 11.9 %collective-permute-done.9 = bf16[128,8192]{1,0:T(8,128)(2,1)S(1)} collective-permute-done((bf16[128,8192]{1,0:T(8,128)(2,1)}, bf16[128,8192]{1,0:T(8,128)(2,1)S(1)}, u32[]{:S(2)}, u32[]{:S(2)}) %collective-permute-start.9) | collective-permute-done | bytes 2097184 | tf_op jit(solution)/shard_map/ppermute | solution.py:10
  305.6 0.8 fusion
  306.4 5.2 %copy.9 = f32[16,8,8,1024]{3,2,1,0:T(8,128)} copy(f32[16,8,8,1024]{3,1,2,0:T(8,128)S(1)} %bitcast.82) | data formatting | bytes 8388608
  311.6 22.0 %bitcast_add_fusion = f32[128,8,1024]{2,1,0:T(8,128)} fusion(f32[16,8,8,1024]{3,2,1,0:T(8,128)} %copy.9, f32[129,9,1025]{2,1,0:T(8,128)} %get-tuple-element.5, f32[129,9,1025]{2,1,0:T(8,128)} %get-tuple-element.4, f32[129,9,1025]{2,1,0:T(8,128)} %get-tuple-element.2), kind=kLoop, calls=%fused_computation.41 | loop fusion | flops 7340032 | bytes 33554432 | tf_op jit(solution)/shard_map/add | solution.py:80
  (26 shorter events, 2.9 us)
Async XLA Ops:
  0.6 124.2 %copy-start = (bf16[8,128,128]{2,1,0:T(8,128)(2,1)S(1)}, bf16[8,128,128]{2,1,0:T(8,128)(2,1)}, u32[]{:S(2)}) copy-start(bf16[8,128,128]{2,1,0:T(8,128)(2,1)} %param.7) | copy-start | bytes 786436
  0.6 95.6 %copy-start.8 = (s32[16,6]{0,1:T(8,128)S(1)}, s32[16,6]{0,1:T(8,128)}, u32[]{:S(2)}) copy-start(s32[16,6]{0,1:T(8,128)} %param.9) | copy-start | bytes 1156
  0.7 98.3 %copy-start.9 = (s32[16,6]{0,1:T(8,128)S(1)}, s32[16,6]{0,1:T(8,128)}, u32[]{:S(2)}) copy-start(s32[16,6]{0,1:T(8,128)} %param.8) | copy-start | bytes 1156
  4.6 1.3 copy-start.4
  6.0 26.3 %collective-permute-start = (bf16[128,8192]{1,0:T(8,128)(2,1)S(1)}, bf16[128,8192]{1,0:T(8,128)(2,1)S(1)}, u32[]{:S(2)}, u32[]{:S(2)}) collective-permute-start(bf16[128,8192]{1,0:T(8,128)(2,1)S(1)} %bitcast.83), channel_id=1, source_target_pairs={{1,0},{2,1},{3,2},{4,3},{5,4},{6,5},{7,6},{8,7},{9,8},{10,9},{11,1... | collective-permute-start | bytes 6291464 | tf_op jit(solution)/shard_map/ppermute | solution.py:10
  32.2 1.4 copy-start.5
  33.6 28.2 %collective-permute-start.1 = (bf16[128,8192]{1,0:T(8,128)(2,1)S(1)}, bf16[128,8192]{1,0:T(8,128)(2,1)S(1)}, u32[]{:S(2)}, u32[]{:S(2)}) collective-permute-start(bf16[128,8192]{1,0:T(8,128)(2,1)S(1)} %collective-permute-done), channel_id=1, source_target_pairs={{1,0},{2,1},{3,2},{4,3},{5,4},{6,5},{7,6},{8,7},{9,8},{10,9},{11,1... | collective-permute-start | bytes 6291464 | tf_op jit(solution)/shard_map/ppermute | solution.py:10
  61.8 1.4 copy-start.6
  63.2 28.2 %collective-permute-start.2 = (bf16[128,8192]{1,0:T(8,128)(2,1)S(1)}, bf16[128,8192]{1,0:T(8,128)(2,1)}, u32[]{:S(2)}, u32[]{:S(2)}) collective-permute-start(bf16[128,8192]{1,0:T(8,128)(2,1)S(1)} %collective-permute-done.1), channel_id=1, source_target_pairs={{1,0},{2,1},{3,2},{4,3},{5,4},{6,5},{7,6},{8,7},{9,8},{10,9},{11,1... | collective-permute-start | bytes 6291464 | tf_op jit(solution)/shard_map/ppermute | solution.py:10
  91.5 28.7 %collective-permute-start.3 = (bf16[128,8192]{1,0:T(8,128)(2,1)}, bf16[128,8192]{1,0:T(8,128)(2,1)}, u32[]{:S(2)}, u32[]{:S(2)}) collective-permute-start(bf16[128,8192]{1,0:T(8,128)(2,1)} %collective-permute-done.2), channel_id=1, source_target_pairs={{1,0},{2,1},{3,2},{4,3},{5,4},{6,5},{7,6},{8,7},{9,8},{10,9},{11,1... | collective-permute-start | bytes 6291464 | tf_op jit(solution)/shard_map/ppermute | solution.py:10
  120.1 39.0 %collective-permute-start.4 = (bf16[128,8192]{1,0:T(8,128)(2,1)}, bf16[128,8192]{1,0:T(8,128)(2,1)}, u32[]{:S(2)}, u32[]{:S(2)}) collective-permute-start(bf16[128,8192]{1,0:T(8,128)(2,1)} %collective-permute-done.3), channel_id=1, source_target_pairs={{1,0},{2,1},{3,2},{4,3},{5,4},{6,5},{7,6},{8,7},{9,8},{10,9},{11,1... | collective-permute-start | bytes 6291464 | tf_op jit(solution)/shard_map/ppermute | solution.py:10
  149.8 3.7 %copy-start.7 = (bf16[128,8192]{1,0:T(8,128)(2,1)S(1)}, bf16[128,8192]{1,0:T(8,128)(2,1)}, u32[]{:S(2)}) copy-start(bf16[128,8192]{1,0:T(8,128)(2,1)} %copy-done.6) | copy-start | bytes 6291460
  156.6 2.8 copy-start.3
  161.7 1.3 copy-start.1
  163.1 28.3 %collective-permute-start.5 = (bf16[128,8192]{1,0:T(8,128)(2,1)S(1)}, bf16[128,8192]{1,0:T(8,128)(2,1)}, u32[]{:S(2)}, u32[]{:S(2)}) collective-permute-start(bf16[128,8192]{1,0:T(8,128)(2,1)S(1)} %fusion.11), channel_id=1, source_target_pairs={{0,1},{1,2},{2,3},{3,4},{4,5},{5,6},{6,7},{7,8},{8,9},{9,10},{10,1... | collective-permute-start | bytes 6291464 | tf_op jit(solution)/shard_map/ppermute | solution.py:10
  191.4 28.7 %collective-permute-start.6 = (bf16[128,8192]{1,0:T(8,128)(2,1)}, bf16[128,8192]{1,0:T(8,128)(2,1)}, u32[]{:S(2)}, u32[]{:S(2)}) collective-permute-start(bf16[128,8192]{1,0:T(8,128)(2,1)} %collective-permute-done.5), channel_id=1, source_target_pairs={{0,1},{1,2},{2,3},{3,4},{4,5},{5,6},{6,7},{7,8},{8,9},{9,10},{10,1... | collective-permute-start | bytes 6291464 | tf_op jit(solution)/shard_map/ppermute | solution.py:10
  193.3 28.8 %collective-permute-start.10 = (bf16[1,8,1024]{2,1,0:T(8,128)(2,1)S(1)}, bf16[1,8,1024]{2,1,0:T(8,128)(2,1)S(1)}, u32[]{:S(2)}, u32[]{:S(2)}) collective-permute-start(bf16[1,8,1024]{2,1,0:T(8,128)(2,1)S(1)} %get-tuple-element.6), channel_id=1, source_target_pairs={{0,1},{1,2},{2,3},{3,4},{4,5},{5,6},{6,7},{7,8},{8,9},{9,10},{10,1... | collective-permute-start | bytes 49160 | tf_op jit(solution)/shard_map/ppermute | solution.py:18
  195.3 26.9 %collective-permute-start.11 = (bf16[1,8,1024]{2,1,0:T(8,128)(2,1)S(1)}, bf16[1,8,1024]{2,1,0:T(8,128)(2,1)S(1)}, u32[]{:S(2)}, u32[]{:S(2)}) collective-permute-start(bf16[1,8,1024]{2,1,0:T(8,128)(2,1)S(1)} %get-tuple-element.7), channel_id=1, source_target_pairs={{1,0},{2,1},{3,2},{4,3},{5,4},{6,5},{7,6},{8,7},{9,8},{10,9},{11,1... | collective-permute-start | bytes 49160 | tf_op jit(solution)/shard_map/ppermute | solution.py:21
  220.1 28.6 %collective-permute-start.7 = (bf16[128,8192]{1,0:T(8,128)(2,1)}, bf16[128,8192]{1,0:T(8,128)(2,1)}, u32[]{:S(2)}, u32[]{:S(2)}) collective-permute-start(bf16[128,8192]{1,0:T(8,128)(2,1)} %collective-permute-done.6), channel_id=1, source_target_pairs={{0,1},{1,2},{2,3},{3,4},{4,5},{5,6},{6,7},{7,8},{8,9},{9,10},{10,1... | collective-permute-start | bytes 6291464 | tf_op jit(solution)/shard_map/ppermute | solution.py:10
  248.6 28.6 %collective-permute-start.8 = (bf16[128,8192]{1,0:T(8,128)(2,1)}, bf16[128,8192]{1,0:T(8,128)(2,1)}, u32[]{:S(2)}, u32[]{:S(2)}) collective-permute-start(bf16[128,8192]{1,0:T(8,128)(2,1)} %collective-permute-done.7), channel_id=1, source_target_pairs={{0,1},{1,2},{2,3},{3,4},{4,5},{5,6},{6,7},{7,8},{8,9},{9,10},{10,1... | collective-permute-start | bytes 6291464 | tf_op jit(solution)/shard_map/ppermute | solution.py:10
  258.0 23.5 %copy-start.2 = (bf16[128,8192]{1,0:T(8,128)(2,1)S(1)}, bf16[128,8192]{1,0:T(8,128)(2,1)}, u32[]{:S(2)}) copy-start(bf16[128,8192]{1,0:T(8,128)(2,1)} %copy-done.1) | copy-start | bytes 6291460
  277.2 28.5 %collective-permute-start.9 = (bf16[128,8192]{1,0:T(8,128)(2,1)}, bf16[128,8192]{1,0:T(8,128)(2,1)S(1)}, u32[]{:S(2)}, u32[]{:S(2)}) collective-permute-start(bf16[128,8192]{1,0:T(8,128)(2,1)} %collective-permute-done.8), channel_id=1, source_target_pairs={{0,1},{1,2},{2,3},{3,4},{4,5},{5,6},{6,7},{7,8},{8,9},{9,10},{10,1... | collective-permute-start | bytes 6291464 | tf_op jit(solution)/shard_map/ppermute | solution.py:10
where the time goes:
time: 335 us; the launch traced here: 334 us
  waiting for transfers between devices  165 us (49%)
  other arithmetic  49.6 us (15%)
  starting transfers between devices  37.8 us (11%)
  between operations  29 us (9%)
  matrix products  28.4 us (8%)
  local copies, waits for them, and re-layouts  23.6 us (7%)
    ppermute x10, waiting for transfers between devices, shifted(): lax.ppermute(value, axis, [(source, source + steps) for source in range(f...  165 us
    ppermute x10, starting transfers between devices, shifted(): lax.ppermute(value, axis, [(source, source + steps) for source in range(f...  31.4 us
    add x1, other arithmetic, local(): gradient = backproj.reshape(volume.shape) + 0.5 * tvgrad  22 us
    unnamed x24, local copies, waits for them, and re-layouts  20.3 us
    dot_general x6, matrix products, own_term(): return live * jnp.dot(block_w, slices, preferred_element_type=jnp.float32)  15.8 us
    dot_general x6, matrix products, back_term(): jnp.dot(block_w.T, resid_piece, preferred_element_type=jnp.float32)  12.6 us
    pad x1, other arithmetic, local(): tvgrad = tv_from(jnp.pad(padded, ((0, 0), (1, 1), (1, 1))))  10.4 us
    mul x1, other arithmetic, tv_from(): flux_y = diff_y * scale  7.44 us
  transfers between devices with their start and end apart: 12, of which 9 were waited for; matrix products, arithmetic and copies ran while one was open for 19% of the time, Pallas kernels for 0%

commit v1 on v0

v1 whole, which is shorter than its diff:
```python
import functools

import jax
import jax.numpy as jnp
from jax import lax
from jax.experimental import pallas as pl
from jax.experimental.pallas import tpu as pltpu
from jax.sharding import PartitionSpec as P

G = 4
CHUNKS = 2
F32 = jnp.float32
BF16 = jnp.bfloat16
VMEM_LIMIT = 40 * 1024 * 1024


def moved(value, steps):
    count = lax.axis_size("slab")
    first, last = max(0, -steps), min(count, count - steps)
    return lax.ppermute(value, "slab", [(source, source + steps) for source in range(first, last)])


def exchanged(value):
    count = lax.axis_size("slab")
    sets = [list(range(first, first + G)) for first in range(0, count, G)]
    return lax.all_to_all(value, "slab", 0, 0, axis_index_groups=sets, tiled=True)


def params(*semantics):
    return pltpu.CompilerParams(vmem_limit_bytes=VMEM_LIMIT)


def cost(flops, nbytes):
    return pl.CostEstimate(flops=int(flops), bytes_accessed=int(nbytes), transcendentals=0)


def cast_kernel(vol_ref, *out_refs):
    depth = out_refs[0].shape[1]
    per = 2
    for c in range(CHUNKS):
        for q in range(G):
            row = per * q + c
            out_refs[c][q] = vol_ref[pl.ds(row, depth, stride=8), :].astype(BF16)


def cast_rows(volume):
    depth, rows, cols = volume.shape
    tile = 128
    shape = jax.ShapeDtypeStruct((G, depth, cols), BF16)
    return pl.pallas_call(
        cast_kernel,
        grid=(cols // tile,),
        in_specs=[pl.BlockSpec((depth * rows, tile), lambda i: (0, i))],
        out_specs=[pl.BlockSpec((G, depth, tile), lambda i: (0, 0, i))] * CHUNKS,
        out_shape=[shape] * CHUNKS,
        compiler_params=params(),
        cost_estimate=cost(volume.size, volume.size * 6),
    )(volume.reshape(depth * rows, cols))


def split_kernel(in_ref, *refs):
    out_refs, wide = refs[:-1], refs[-1]
    depth = out_refs[0].shape[1]
    wide[...] = in_ref[...].astype(F32).reshape(wide.shape)
    for c in range(CHUNKS):
        for q in range(G):
            out_refs[c][q] = wide[pl.ds(2 * q + c, depth, stride=8), :].astype(BF16)


def split_rows(array):
    depth, rows, cols = array.shape
    tile = 128
    shape = jax.ShapeDtypeStruct((G, depth, cols), BF16)
    return pl.pallas_call(
        split_kernel,
        grid=(cols // tile,),
        in_specs=[pl.BlockSpec((depth, rows, tile), lambda i: (0, 0, i))],
        out_specs=[pl.BlockSpec((G, depth, tile), lambda i: (0, 0, i))] * CHUNKS,
        out_shape=[shape] * CHUNKS,
        scratch_shapes=[pltpu.VMEM((depth * rows, tile), F32)],
        compiler_params=params(),
        cost_estimate=cost(array.size, array.size * 4),
    )(array)


def join_kernel(*refs):
    in_refs, out_ref, wide = refs[:-2], refs[-2], refs[-1]
    depth = in_refs[0].shape[1]
    for c in range(CHUNKS):
        for q in range(G):
            wide[pl.ds(2 * q + c, depth, stride=8), :] = in_refs[c][q].astype(F32)
    out_ref[...] = wide[...].reshape(out_ref.shape).astype(out_ref.dtype)


def join_rows(chunks, rows):
    _, depth, cols = chunks[0].shape
    tile = 128
    return pl.pallas_call(
        join_kernel,
        grid=(cols // tile,),
        in_specs=[pl.BlockSpec((G, depth, tile), lambda i: (0, 0, i))] * CHUNKS,
        out_specs=pl.BlockSpec((depth, rows, tile), lambda i: (0, 0, i)),
        out_shape=jax.ShapeDtypeStruct((depth, rows, cols), BF16),
        scratch_shapes=[pltpu.VMEM((depth * rows, tile), F32)],
        compiler_params=params(),
        cost_estimate=cost(depth * rows * cols, depth * rows * cols * 4),
    )(*chunks)


def finish_kernel(tv_ref, *refs):
    in_refs, out_ref, wide = refs[:-2], refs[-2], refs[-1]
    depth = in_refs[0].shape[1]
    for c in range(CHUNKS):
        for q in range(G):
            wide[pl.ds(2 * q + c, depth, stride=8), :] = in_refs[c][q].astype(F32)
    out_ref[...] = tv_ref[...] + wide[...].reshape(out_ref.shape)


def finish(tv, chunks):
    depth, rows, cols = tv.shape
    tile = 128
    whole = pl.BlockSpec((depth, rows, tile), lambda i: (0, 0, i))
    return pl.pallas_call(
        finish_kernel,
        grid=(cols // tile,),
        in_specs=[whole] + [pl.BlockSpec((G, depth, tile), lambda i: (0, 0, i))] * CHUNKS,
        out_specs=whole,
        out_shape=jax.ShapeDtypeStruct((depth, rows, cols), F32),
        scratch_shapes=[pltpu.VMEM((depth * rows, tile), F32)],
        compiler_params=params(),
        cost_estimate=cost(depth * rows * cols, depth * rows * cols * 10),
    )(tv, *chunks)


def band_kernel(slabs, span, here_ref, cover_ref, offset_ref, w_ref, proj_ref, back_ref):
    side = w_ref.shape[1]
    first = (here_ref[0] // G) * G
    last_level = first + G >= slabs
    zero = jnp.zeros((side, side), BF16)

    def block(i, j, k, extra):
        safe = jnp.clip(i, 0, slabs - 1)
        inside = jnp.logical_and(jnp.logical_and(i >= 0, j < slabs), extra)
        live = jnp.logical_and(inside, cover_ref[safe, k] == 1)
        value = w_ref[offset_ref[safe, k]]
        return jnp.where(live, value, zero)

    for r in range(G + 1):
        for s in range(2 * G + 1):
            k = s - r
            value = zero
            if 0 <= k < span:
                extra = last_level if r == G else True
                value = block(first - 1 + r, first - 1 + s, k, extra)
            proj_ref[pl.ds(r * side, side), pl.ds(s * side, side)] = value
    for r in range(G):
        for s in range(2 * G + 1):
            k = (r + G + 1) - s
            value = zero
            if 0 <= k < span:
                value = block(first - G - 1 + s, first + r, k, True).astype(F32).T.astype(BF16)
            back_ref[pl.ds(r * side, side), pl.ds(s * side, side)] = value


def bands(here, coverage, offsets, weights):
    slabs, span = coverage.shape
    side = weights.shape[1]
    smem = pl.BlockSpec(memory_space=pltpu.SMEM)
    vmem = pl.BlockSpec(memory_space=pltpu.VMEM)
    return pl.pallas_call(
        functools.partial(band_kernel, slabs, span),
        in_specs=[smem, smem, smem, vmem],
        out_specs=[vmem, vmem],
        out_shape=[
            jax.ShapeDtypeStruct(((G + 1) * side, (2 * G + 1) * side), BF16),
            jax.ShapeDtypeStruct((G * side, (2 * G + 1) * side), BF16),
        ],
        compiler_params=params(),
        cost_estimate=cost(1e6, 4e6),
    )(here, coverage, offsets, weights)


def project_kernel(band_ref, low_ref, own_ref, high_ref, slow_ref, sown_ref, r_ref, last_ref, down_ref):
    side = low_ref.shape[0]
    n = G * side
    total = jnp.dot(band_ref[:, side : side + n], own_ref[...], preferred_element_type=F32)
    total += jnp.dot(band_ref[:, side + n :], high_ref[...], preferred_element_type=F32)
    total += jnp.dot(band_ref[:, :side], low_ref[...], preferred_element_type=F32)
    first = (total[:side] - slow_ref[...].astype(F32)).astype(BF16)
    rest = (total[side:] - sown_ref[...].astype(F32)).astype(BF16)
    r_ref[:side] = first
    r_ref[side:] = rest[: n - side]
    down_ref[...] = first
    last_ref[...] = rest[n - side :]


def project(band, low, own, high, slow, sown):
    side, cols = low.shape
    n = G * side
    tile = 256
    one = pl.BlockSpec((side, tile), lambda i: (0, i))
    many = pl.BlockSpec((n, tile), lambda i: (0, i))
    return pl.pallas_call(
        project_kernel,
        grid=(cols // tile,),
        in_specs=[pl.BlockSpec(band.shape, lambda i: (0, 0)), one, many, many, one, many],
        out_specs=[many, one, one],
        out_shape=[
            jax.ShapeDtypeStruct((n, cols), BF16),
            jax.ShapeDtypeStruct((side, cols), BF16),
            jax.ShapeDtypeStruct((side, cols), BF16),
        ],
        compiler_params=params(),
        cost_estimate=cost(2 * band.size * cols, 6e6),
    )(band, low, own, high, slow, sown)


def back_kernel(band_ref, low_ref, own_ref, high_ref, out_ref):
    side = high_ref.shape[0]
    n = G * side
    total = jnp.dot(band_ref[:, n : 2 * n], own_ref[...], preferred_element_type=F32)
    total += jnp.dot(band_ref[:, :n], low_ref[...], preferred_element_type=F32)
    total += jnp.dot(band_ref[:, 2 * n :], high_ref[...], preferred_element_type=F32)
    out_ref[...] = total.astype(BF16)


def back(band, low, own, high):
    side, cols = high.shape
    n = G * side
    tile = 256
    one = pl.BlockSpec((side, tile), lambda i: (0, i))
    many = pl.BlockSpec((n, tile), lambda i: (0, i))
    return pl.pallas_call(
        back_kernel,
        grid=(cols // tile,),
        in_specs=[pl.BlockSpec(band.shape, lambda i: (0, 0)), many, many, one],
        out_specs=many,
        out_shape=jax.ShapeDtypeStruct((n, cols), BF16),
        compiler_params=params(),
        cost_estimate=cost(2 * band.size * cols, 6e6),
    )(band, low, own, high)


def tv_kernel(low_ref, high_ref, next_ref, vol_ref, out_ref, flux_ref):
    step = pl.program_id(0)
    steps = pl.num_programs(0)
    deep, rows, cols = vol_ref.shape
    row = lax.broadcasted_iota(jnp.int32, (rows, cols), 0)
    col = lax.broadcasted_iota(jnp.int32, (rows, cols), 1)

    def up_y(v):
        return jnp.where(row == rows - 1, 0.0, pltpu.roll(v, rows - 1, 0))

    def up_x(v):
        return jnp.where(col == cols - 1, 0.0, pltpu.roll(v, cols - 1, 1))

    def scale_of(cur, above):
        dz = above - cur
        dy = up_y(cur) - cur
        dx = up_x(cur) - cur
        return dz, dy, dx, 0.5 * lax.rsqrt(dz * dz + dy * dy + dx * dx + 0.25)

    def edge(v):
        return 0.5 * v * lax.rsqrt(v * v + 0.25)

    @pl.when(step == 0)
    def _():
        dz, _, _, scale = scale_of(low_ref[0], vol_ref[0])
        flux_ref[...] = dz * scale

    def one(z, cur, above, below_flux):
        dz, dy, dx, scale = scale_of(cur, above)
        fz, fy, fx = dz * scale, dy * scale, dx * scale
        fy_low = jnp.where(row == 0, edge(cur), pltpu.roll(fy, 1, 0))
        fx_low = jnp.where(col == 0, edge(cur), pltpu.roll(fx, 1, 1))
        out_ref[z] = (below_flux - fz) + (fy_low - fy) + (fx_low - fx)
        return fz

    def body(z, flux):
        return one(z, vol_ref[z], vol_ref[z + 1], flux)

    flux = lax.fori_loop(0, deep - 1, body, flux_ref[...])
    above = jnp.where(step == steps - 1, high_ref[0], next_ref[0])
    flux_ref[...] = one(deep - 1, vol_ref[deep - 1], above, flux)


def half_tv(volume, low, high):
    depth, rows, cols = volume.shape
    deep = 16
    steps = depth // deep
    edge = pl.BlockSpec((1, rows, cols), lambda i: (0, 0, 0))
    body = pl.BlockSpec((deep, rows, cols), lambda i: (i, 0, 0))
    after = pl.BlockSpec((1, rows, cols), lambda i: (jnp.minimum((i + 1) * deep, depth - 1), 0, 0))
    return pl.pallas_call(
        tv_kernel,
        grid=(steps,),
        in_specs=[edge, edge, after, body],
        out_specs=body,
        out_shape=jax.ShapeDtypeStruct(volume.shape, F32),
        scratch_shapes=[pltpu.VMEM((rows, cols), F32)],
        compiler_params=params(),
        cost_estimate=cost(volume.size * 40, volume.size * 8),
    )(low, high, volume, volume)


def local(volume, sinogram, weights, coverage, offsets):
    slabs = lax.axis_size("slab")
    here = lax.axis_index("slab").astype(jnp.int32)
    depth, rows, cols = volume.shape
    last_level = here >= slabs - G

    vol_rows = cast_rows(volume)
    band_p, band_b = bands(here.reshape(1), coverage, offsets, weights)
    sino_rows = split_rows(sinogram)

    own = [exchanged(v).reshape(G * depth, cols) for v in vol_rows]
    high = [moved(v, -G) for v in own]
    low = [moved(v[(G - 1) * depth :], G) for v in own]
    sown = [exchanged(s).reshape(G * depth, cols) for s in sino_rows]
    slow = [moved(s[(G - 1) * depth :], G) for s in sown]

    below = moved(volume[-1:], 1)
    above = moved(volume[:1], -1)
    tv = half_tv(volume, below, above)

    resid_back, back_back = [], []
    for c in range(CHUNKS):
        resid, last, down = project(band_p, low[c], own[c], high[c], slow[c], sown[c])
        r_low = moved(resid, G)
        r_high = moved(down, -G)
        r_high = jnp.where(last_level, last, r_high)
        mine = jnp.concatenate([resid[depth:], r_high], axis=0)
        resid_back.append(exchanged(mine.reshape(G, depth, cols)))
        backproj = back(band_b, r_low, resid, r_high)
        back_back.append(exchanged(backproj.reshape(G, depth, cols)))

    residual = join_rows(resid_back, rows)
    gradient = finish(tv, back_back)
    return (gradient, residual)


def solution(mesh):
    placed = (P("slab", "grp", None), P("slab", "grp", None), P(), P(), P())
    return jax.shard_map(
        local,
        mesh=mesh,
        in_specs=placed,
        out_specs=(P("slab", "grp", None), P("slab", "grp", None)),
        check_vma=False,
    )
```

time: 335 us -> 233 us (0.70)
  the two profiles are of different devices: /device:TPU:10 before, /device:TPU:1 now
where the time goes in v1:
time: 233 us; the launch traced here: 231 us
  starting transfers between devices  68.3 us (29%)
  waiting for transfers between devices  60.9 us (26%)
  Pallas kernels  54.6 us (23%)
  local copies, waits for them, and re-layouts  26 us (11%)
  blocking collectives  17.7 us (8%)
  other arithmetic  3.14 us (1%)
    ppermute x12, waiting for transfers between devices, moved(): lax.ppermute(value, 'slab', [(source, source + steps) for source in range...  40.9 us
    ppermute x12, starting transfers between devices, moved(): lax.ppermute(value, 'slab', [(source, source + steps) for source in range...  35.9 us
    all_to_all x7, starting transfers between devices, exchanged(): lax.all_to_all(value, 'slab', 0, 0, axis_index_groups=sets, tiled=True)  32.4 us
    pallas_call x1, Pallas kernels, half_tv(): pl.pallas_call(tv_kernel, grid=(steps,), in_specs=[edge, edge, after, bod...  21 us
    unnamed x52, local copies, waits for them, and re-layouts  20.1 us
    all_to_all x7, waiting for transfers between devices, exchanged(): lax.all_to_all(value, 'slab', 0, 0, axis_index_groups=sets, tiled=True)  20 us
    all_to_all x1, blocking collectives, exchanged(): lax.all_to_all(value, 'slab', 0, 0, axis_index_groups=sets, tiled=True)  17.7 us
    pallas_call x2, Pallas kernels, project(): pl.pallas_call(project_kernel, grid=(cols // tile,), in_specs=[pl.BlockSp...  8.87 us
  transfers between devices with their start and end apart: 19, of which 8 were waited for; matrix products, arithmetic and copies ran while one was open for 4% of the time, Pallas kernels for 20%

profile of v1, /device:TPU:1, one launch (start us, length us, event | category | flops | bytes accessed | tf_op | source)
XLA Modules:
  0.0 231.4 jit_solution(14656068282832235770)
XLA Ops:
  0.6 1.6 copy-done.12
  2.2 3.7 %shard_map.71 = (bf16[4,128,1024]{2,1,0:T(8,128)(2,1)S(1)}, bf16[4,128,1024]{2,1,0:T(8,128)(2,1)}) custom-call(bf16[128,8,1024]{2,1,0:T(8,128)(2,1)S(1)} %copy-done.12), custom_call_target="tpu_custom_call" | custom-call | flops 1048576 | bytes 4194304 | tf_op jit(solution)/shard_map/pallas_call | solution.py:74
  6.9 4.3 %all-to-all-start.4 = ((bf16[4,128,1024]{2,1,0:T(8,128)(2,1)}), bf16[4,128,1024]{2,1,0:T(8,128)(2,1)S(1)}, u32[]{:S(2)}, u32[]{:S(2)}) async-start(bf16[4,128,1024]{2,1,0:T(8,128)(2,1)} %get-tuple-element.22), calls=%async_computation.4 | async-start | bytes 2097152 | tf_op jit(solution)/shard_map/all_to_all | solution.py:26
  11.2 2.2 copy-done
  13.4 3.5 %shard_map.70 = (bf16[4,128,1024]{2,1,0:T(8,128)(2,1)}, bf16[4,128,1024]{2,1,0:T(8,128)(2,1)S(1)}) custom-call(f32[1024,1024]{1,0:T(8,128)S(1)} %bitcast.18), custom_call_target="tpu_custom_call" | custom-call | flops 1048576 | bytes 6291456 | tf_op jit(solution)/shard_map/pallas_call | solution.py:50
  16.9 7.7 %all-to-all-done.4 = bf16[4,128,1024]{2,1,0:T(8,128)(2,1)S(1)} async-done(((bf16[4,128,1024]{2,1,0:T(8,128)(2,1)}), bf16[4,128,1024]{2,1,0:T(8,128)(2,1)S(1)}, u32[]{:S(2)}, u32[]{:S(2)}) %all-to-all-start.4) | async-done | bytes 1048608 | tf_op jit(solution)/shard_map/all_to_all | solution.py:26
  24.6 17.7 %all_to_all.40 = bf16[4,128,1024]{2,1,0:T(8,128)(2,1)} all-to-all(bf16[4,128,1024]{2,1,0:T(8,128)(2,1)S(1)} %get-tuple-element.21), channel_id=1, replica_groups={{0,1,2,3},{4,5,6,7},{8,9,10,11},{12,13,14,15},{16,17,18,19},{20,21,22,2..., dimensions={0} | all-to-all | bytes 2097152 | tf_op jit(solution)/shard_map/all_to_all | solution.py:26
  42.2 4.5 %all-to-all-start = ((bf16[4,128,1024]{2,1,0:T(8,128)(2,1)}), bf16[4,128,1024]{2,1,0:T(8,128)(2,1)S(1)}, u32[]{:S(2)}, u32[]{:S(2)}) async-start(bf16[4,128,1024]{2,1,0:T(8,128)(2,1)} %get-tuple-element.16), calls=%async_computation | async-start | bytes 2097152 | tf_op jit(solution)/shard_map/all_to_all | solution.py:26
  46.8 1.4 collective-permute-start.8
  48.2 12.3 %all-to-all-done = bf16[4,128,1024]{2,1,0:T(8,128)(2,1)S(1)} async-done(((bf16[4,128,1024]{2,1,0:T(8,128)(2,1)}), bf16[4,128,1024]{2,1,0:T(8,128)(2,1)S(1)}, u32[]{:S(2)}, u32[]{:S(2)}) %all-to-all-start) | async-done | bytes 1048608 | tf_op jit(solution)/shard_map/all_to_all | solution.py:26
  60.5 4.2 %all-to-all-start.1 = ((bf16[4,128,1024]{2,1,0:T(8,128)(2,1)}), bf16[4,128,1024]{2,1,0:T(8,128)(2,1)S(1)}, u32[]{:S(2)}, u32[]{:S(2)}) async-start(bf16[4,128,1024]{2,1,0:T(8,128)(2,1)} %copy-done.17), calls=%async_computation.1 | async-start | bytes 2097152 | tf_op jit(solution)/shard_map/all_to_all | solution.py:26
  65.4 4.6 %collective-permute-start.9 = (bf16[128,1024]{1,0:T(8,128)(2,1)}, bf16[128,1024]{1,0:T(8,128)(2,1)}, u32[]{:S(2)}, u32[]{:S(2)}) collective-permute-start(bf16[128,1024]{1,0:T(8,128)(2,1)} %slice_bitcast_fusion), channel_id=1, source_target_pairs={{0,4},{1,5},{2,6},{3,7},{4,8},{5,9},{6,10},{7,11},{8,12},{9,13},{1... | collective-permute-start | bytes 786440 | tf_op jit(solution)/shard_map/ppermute | solution.py:20
  70.0 1.7 slice_bitcast_fusion.1
  71.7 3.2 %collective-permute-start.7 = (bf16[128,1024]{1,0:T(8,128)(2,1)}, bf16[128,1024]{1,0:T(8,128)(2,1)}, u32[]{:S(2)}, u32[]{:S(2)}) collective-permute-start(bf16[128,1024]{1,0:T(8,128)(2,1)} %slice_bitcast_fusion.1), channel_id=1, source_target_pairs={{0,4},{1,5},{2,6},{3,7},{4,8},{5,9},{6,10},{7,11},{8,12},{9,13},{1... | collective-permute-start | bytes 786440 | tf_op jit(solution)/shard_map/ppermute | solution.py:20
  74.9 1.3 collective-permute-start.3
  76.4 1.4 shard_map.69
  77.8 3.1 %collective-permute-done.7.low_ref = bf16[128,1024]{1,0:T(8,128)(2,1)} collective-permute-done((bf16[128,1024]{1,0:T(8,128)(2,1)}, bf16[128,1024]{1,0:T(8,128)(2,1)}, u32[]{:S(2)}, u32[]{:S(2)}) %collective-permute-start.7) | collective-permute-done | bytes 262176 | tf_op jit(solution)/shard_map/ppermute | solution.py:20
  80.9 1.2 copy-done.16
  82.2 4.8 %shard_map.74 = (bf16[512,1024]{1,0:T(8,128)(2,1)}, bf16[128,1024]{1,0:T(8,128)(2,1)S(1)}, bf16[128,1024]{1,0:T(8,128)(2,1)S(1)}) custom-call(bf16[640,1152]{1,0:T(8,128)(2,1)S(1)} %get-tuple-element.15.band_ref, bf16[128,1024]{1,0:T(8,128)(2,1)} %collective-permute-done.7.low_ref, bf16[512,1024]{1,0:T(8,128)(2,1)} %bitcast.8.own_ref, ...), custom_call_target="tpu_custom_call" | custom-call | flops 1509949440 | bytes 6000000 | tf_op jit(solution)/shard_map/pallas_call | solution.py:203
  87.7 1.3 collective-permute-start.11
  89.8 5.4 %collective-permute-start.4 = (bf16[128,1024]{1,0:T(8,128)(2,1)}, bf16[128,1024]{1,0:T(8,128)(2,1)}, u32[]{:S(2)}, u32[]{:S(2)}) collective-permute-start(bf16[128,1024]{1,0:T(8,128)(2,1)} %slice_bitcast_fusion.2), channel_id=1, source_target_pairs={{0,4},{1,5},{2,6},{3,7},{4,8},{5,9},{6,10},{7,11},{8,12},{9,13},{1... | collective-permute-start | bytes 786440 | tf_op jit(solution)/shard_map/ppermute | solution.py:20
  95.9 3.4 %collective-permute-start.2 = (bf16[128,1024]{1,0:T(8,128)(2,1)}, bf16[128,1024]{1,0:T(8,128)(2,1)}, u32[]{:S(2)}, u32[]{:S(2)}) collective-permute-start(bf16[128,1024]{1,0:T(8,128)(2,1)} %slice_bitcast_fusion.3), channel_id=1, source_target_pairs={{0,4},{1,5},{2,6},{3,7},{4,8},{5,9},{6,10},{7,11},{8,12},{9,13},{1... | collective-permute-start | bytes 786440 | tf_op jit(solution)/shard_map/ppermute | solution.py:20
  100.5 6.1 %collective-permute-done.11 = bf16[128,1024]{1,0:T(8,128)(2,1)} collective-permute-done((bf16[128,1024]{1,0:T(8,128)(2,1)S(1)}, bf16[128,1024]{1,0:T(8,128)(2,1)}, u32[]{:S(2)}, u32[]{:S(2)}) %collective-permute-start.11) | collective-permute-done | bytes 262176 | tf_op jit(solution)/shard_map/ppermute | solution.py:20
  108.7 5.0 %all-to-all-start.7 = ((bf16[4,128,1024]{2,1,0:T(8,128)(2,1)}), bf16[4,128,1024]{2,1,0:T(8,128)(2,1)S(1)}, u32[]{:S(2)}, u32[]{:S(2)}) async-start(bf16[4,128,1024]{2,1,0:T(8,128)(2,1)} %bitcast.25), calls=%async_computation.7 | async-start | bytes 2097152 | tf_op jit(solution)/shard_map/all_to_all | solution.py:26
  113.6 1.2 copy-done.14
  114.9 1.4 copy-done.22
  116.2 4.1 %shard_map.72 = (bf16[512,1024]{1,0:T(8,128)(2,1)S(1)}, bf16[128,1024]{1,0:T(8,128)(2,1)S(1)}, bf16[128,1024]{1,0:T(8,128)(2,1)S(1)}) custom-call(bf16[640,1152]{1,0:T(8,128)(2,1)S(1)} %copy-done.22, bf16[128,1024]{1,0:T(8,128)(2,1)} %collective-permute-done.2.low_ref, bf16[512,1024]{1,0:T(8,128)(2,1)S(1)} %bitcast.22, ...), custom_call_target="tpu_custom_call" | custom-call | flops 1509949440 | bytes 6000000 | tf_op jit(solution)/shard_map/pallas_call | solution.py:203
  120.3 1.3 collective-permute-start.6
  121.6 5.0 %collective-permute-start.10 = (bf16[512,1024]{1,0:T(8,128)(2,1)}, bf16[512,1024]{1,0:T(8,128)(2,1)}, u32[]{:S(2)}, u32[]{:S(2)}) collective-permute-start(bf16[512,1024]{1,0:T(8,128)(2,1)} %get-tuple-element.23.own_ref), channel_id=1, source_target_pairs={{0,4},{1,5},{2,6},{3,7},{4,8},{5,9},{6,10},{7,11},{8,12},{9,13},{1... | collective-permute-start | bytes 3145736 | tf_op jit(solution)/shard_map/ppermute | solution.py:20
  126.6 3.4 %collective-permute-done.6 = bf16[128,1024]{1,0:T(8,128)(2,1)S(1)} collective-permute-done((bf16[128,1024]{1,0:T(8,128)(2,1)S(1)}, bf16[128,1024]{1,0:T(8,128)(2,1)S(1)}, u32[]{:S(2)}, u32[]{:S(2)}) %collective-permute-start.6) | collective-permute-done | bytes 262176 | tf_op jit(solution)/shard_map/ppermute | solution.py:20
  131.2 4.3 %all-to-all-start.6 = ((bf16[4,128,1024]{2,1,0:T(8,128)(2,1)}), bf16[4,128,1024]{2,1,0:T(8,128)(2,1)S(1)}, u32[]{:S(2)}, u32[]{:S(2)}) async-start(bf16[4,128,1024]{2,1,0:T(8,128)(2,1)} %bitcast.26), calls=%async_computation.6 | async-start | bytes 2097152 | tf_op jit(solution)/shard_map/all_to_all | solution.py:26
  135.5 3.5 %collective-permute-start.5 = (bf16[512,1024]{1,0:T(8,128)(2,1)}, bf16[512,1024]{1,0:T(8,128)(2,1)}, u32[]{:S(2)}, u32[]{:S(2)}) collective-permute-start(bf16[512,1024]{1,0:T(8,128)(2,1)} %copy-done.8), channel_id=1, source_target_pairs={{0,4},{1,5},{2,6},{3,7},{4,8},{5,9},{6,10},{7,11},{8,12},{9,13},{1... | collective-permute-start | bytes 3145736 | tf_op jit(solution)/shard_map/ppermute | solution.py:20
  139.0 9.1 %collective-permute-done.10.low_ref = bf16[512,1024]{1,0:T(8,128)(2,1)} collective-permute-done((bf16[512,1024]{1,0:T(8,128)(2,1)}, bf16[512,1024]{1,0:T(8,128)(2,1)}, u32[]{:S(2)}, u32[]{:S(2)}) %collective-permute-start.10) | collective-permute-done | bytes 1048608 | tf_op jit(solution)/shard_map/ppermute | solution.py:20
  148.1 3.7 %shard_map.75 = bf16[512,1024]{1,0:T(8,128)(2,1)S(1)} custom-call(bf16[512,1152]{1,0:T(8,128)(2,1)S(1)} %get-tuple-element.14.band_ref, bf16[512,1024]{1,0:T(8,128)(2,1)} %collective-permute-done.10.low_ref, bf16[512,1024]{1,0:T(8,128)(2,1)} %get-tuple-element.23.own_ref, bf16[128,1024]{1,0:T(8,128)(2,1)S(1)} %broadcast_select_fusion.high_ref), custom_call_target="tpu_custom_call" | custom-call | flops 1207959552 | bytes 6000000 | tf_op jit(solution)/shard_map/pallas_call | solution.py:233
  153.8 5.4 %all-to-all-start.5 = ((bf16[4,128,1024]{2,1,0:T(8,128)(2,1)}), bf16[4,128,1024]{2,1,0:T(8,128)(2,1)S(1)}, u32[]{:S(2)}, u32[]{:S(2)}) async-start(bf16[4,128,1024]{2,1,0:T(8,128)(2,1)} %bitcast.20), calls=%async_computation.5 | async-start | bytes 2097152 | tf_op jit(solution)/shard_map/all_to_all | solution.py:26
  159.2 11.3 %collective-permute-done.5.low_ref = bf16[512,1024]{1,0:T(8,128)(2,1)} collective-permute-done((bf16[512,1024]{1,0:T(8,128)(2,1)}, bf16[512,1024]{1,0:T(8,128)(2,1)}, u32[]{:S(2)}, u32[]{:S(2)}) %collective-permute-start.5) | collective-permute-done | bytes 1048608 | tf_op jit(solution)/shard_map/ppermute | solution.py:20
  170.6 1.2 copy-done.9
  171.8 3.6 %shard_map.73 = bf16[512,1024]{1,0:T(8,128)(2,1)S(1)} custom-call(bf16[512,1152]{1,0:T(8,128)(2,1)S(1)} %get-tuple-element.14.band_ref, bf16[512,1024]{1,0:T(8,128)(2,1)} %collective-permute-done.5.low_ref, bf16[512,1024]{1,0:T(8,128)(2,1)S(1)} %copy-done.9, bf16[128,1024]{1,0:T(8,128)(2,1)S(1)} %copy-done.11), custom_call_target="tpu_custom_call" | custom-call | flops 1207959552 | bytes 6000000 | tf_op jit(solution)/shard_map/pallas_call | solution.py:233
  176.4 4.6 %all-to-all-start.2 = ((bf16[4,128,1024]{2,1,0:T(8,128)(2,1)}), bf16[4,128,1024]{2,1,0:T(8,128)(2,1)S(1)}, u32[]{:S(2)}, u32[]{:S(2)}) async-start(bf16[4,128,1024]{2,1,0:T(8,128)(2,1)} %bitcast.19), calls=%async_computation.2 | async-start | bytes 2097152 | tf_op jit(solution)/shard_map/all_to_all | solution.py:26
  181.8 1.9 collective-permute-start.1
  183.8 3.6 %collective-permute-start = (f32[1,8,1024]{2,1,0:T(8,128)S(1)}, f32[1,8,1024]{2,1,0:T(8,128)S(1)}, u32[]{:S(2)}, u32[]{:S(2)}) collective-permute-start(f32[1,8,1024]{2,1,0:T(8,128)S(1)} %get-tuple-element.27), channel_id=1, source_target_pairs={{0,1},{1,2},{2,3},{3,4},{4,5},{5,6},{6,7},{7,8},{8,9},{9,10},{10,1... | collective-permute-start | bytes 98312 | tf_op jit(solution)/shard_map/ppermute | solution.py:20
  187.4 7.8 %collective-permute-done.1.high_ref = f32[1,8,1024]{2,1,0:T(8,128)S(1)} collective-permute-done((f32[1,8,1024]{2,1,0:T(8,128)S(1)}, f32[1,8,1024]{2,1,0:T(8,128)S(1)}, u32[]{:S(2)}, u32[]{:S(2)}) %collective-permute-start.1) | collective-permute-done | bytes 32800 | tf_op jit(solution)/shard_map/ppermute | solution.py:20
  195.2 2.2 copy-done.1
  197.4 21.0 %shard_map.68.tv_ref = f32[128,8,1024]{2,1,0:T(8,128)S(1)} custom-call(f32[1,8,1024]{2,1,0:T(8,128)S(1)} %collective-permute-done.low_ref, f32[1,8,1024]{2,1,0:T(8,128)S(1)} %collective-permute-done.1.high_ref, f32[128,8,1024]{2,1,0:T(8,128)S(1)} %copy-done.1, f32[128,8,1024]{2,1,0:T(8,128)S(1)} %copy-done.1), custom_call_target="tpu_custom_call" | custom-call | flops 41943040 | bytes 8388608 | tf_op jit(solution)/shard_map/pallas_call | solution.py:294
  218.4 2.0 copy-done.2
  220.4 4.0 %shard_map.77 = bf16[128,8,1024]{2,1,0:T(8,128)(2,1)} custom-call(bf16[4,128,1024]{2,1,0:T(8,128)(2,1)S(1)} %copy-done.5, bf16[4,128,1024]{2,1,0:T(8,128)(2,1)S(1)} %all-to-all-done.7.refs_1_), custom_call_target="tpu_custom_call" | custom-call | flops 1048576 | bytes 4194304 | tf_op jit(solution)/shard_map/pallas_call | solution.py:98
  224.4 2.2 copy-done.3
  226.6 4.8 %shard_map.76 = f32[128,8,1024]{2,1,0:T(8,128)} custom-call(f32[128,8,1024]{2,1,0:T(8,128)S(1)} %copy-done.3, bf16[4,128,1024]{2,1,0:T(8,128)(2,1)S(1)} %all-to-all-done.2.refs_0_, bf16[4,128,1024]{2,1,0:T(8,128)(2,1)S(1)} %all-to-all-done.5.refs_1_), custom_call_target="tpu_custom_call" | custom-call | flops 1048576 | bytes 10485760 | tf_op jit(solution)/shard_map/pallas_call | solution.py:123
  (64 shorter events, 12.3 us)
Async XLA Ops:
  0.6 1.6 copy-start.12
  5.9 1.0 copy-start.17
  6.9 17.7 %all-to-all-start.4 = ((bf16[4,128,1024]{2,1,0:T(8,128)(2,1)}), bf16[4,128,1024]{2,1,0:T(8,128)(2,1)S(1)}, u32[]{:S(2)}, u32[]{:S(2)}) async-start(bf16[4,128,1024]{2,1,0:T(8,128)(2,1)} %get-tuple-element.22), calls=%async_computation.4 | async-start | bytes 2097152 | tf_op jit(solution)/shard_map/all_to_all | solution.py:26
  11.2 2.2 copy-start
  24.6 40.1 %copy-start.15 = (bf16[4,128,1024]{2,1,0:T(8,128)(2,1)}, bf16[4,128,1024]{2,1,0:T(8,128)(2,1)S(1)}, u32[]{:S(2)}) copy-start(bf16[4,128,1024]{2,1,0:T(8,128)(2,1)S(1)} %all-to-all-done.4) | copy-start | bytes 3145732
  42.2 18.2 %all-to-all-start = ((bf16[4,128,1024]{2,1,0:T(8,128)(2,1)}), bf16[4,128,1024]{2,1,0:T(8,128)(2,1)S(1)}, u32[]{:S(2)}, u32[]{:S(2)}) async-start(bf16[4,128,1024]{2,1,0:T(8,128)(2,1)} %get-tuple-element.16), calls=%async_computation | async-start | bytes 2097152 | tf_op jit(solution)/shard_map/all_to_all | solution.py:26
  46.8 29.5 %copy-start.23 = (s32[16,6]{0,1:T(8,128)S(1)}, s32[16,6]{0,1:T(8,128)}, u32[]{:S(2)}) copy-start(s32[16,6]{0,1:T(8,128)} %param.8) | copy-start | bytes 1156
  46.8 29.5 %copy-start.24 = (s32[16,6]{0,1:T(8,128)S(1)}, s32[16,6]{0,1:T(8,128)}, u32[]{:S(2)}) copy-start(s32[16,6]{0,1:T(8,128)} %param.9) | copy-start | bytes 1156
  46.8 29.6 %copy-start.18 = (bf16[8,128,128]{2,1,0:T(8,128)(2,1)S(1)}, bf16[8,128,128]{2,1,0:T(8,128)(2,1)}, u32[]{:S(2)}) copy-start(bf16[8,128,128]{2,1,0:T(8,128)(2,1)} %w_ref.1) | copy-start | bytes 786436
  46.8 34.2 %collective-permute-start.8 = (bf16[512,1024]{1,0:T(8,128)(2,1)}, bf16[512,1024]{1,0:T(8,128)(2,1)}, u32[]{:S(2)}, u32[]{:S(2)}) collective-permute-start(bf16[512,1024]{1,0:T(8,128)(2,1)} %bitcast.8.own_ref), channel_id=1, source_target_pairs={{4,0},{5,1},{6,2},{7,3},{8,4},{9,5},{10,6},{11,7},{12,8},{13,9},{1... | collective-permute-start | bytes 3145736 | tf_op jit(solution)/shard_map/ppermute | solution.py:20
  60.5 28.5 %all-to-all-start.1 = ((bf16[4,128,1024]{2,1,0:T(8,128)(2,1)}), bf16[4,128,1024]{2,1,0:T(8,128)(2,1)S(1)}, u32[]{:S(2)}, u32[]{:S(2)}) async-start(bf16[4,128,1024]{2,1,0:T(8,128)(2,1)} %copy-done.17), calls=%async_computation.1 | async-start | bytes 2097152 | tf_op jit(solution)/shard_map/all_to_all | solution.py:26
  65.4 12.4 %collective-permute-start.9 = (bf16[128,1024]{1,0:T(8,128)(2,1)}, bf16[128,1024]{1,0:T(8,128)(2,1)}, u32[]{:S(2)}, u32[]{:S(2)}) collective-permute-start(bf16[128,1024]{1,0:T(8,128)(2,1)} %slice_bitcast_fusion), channel_id=1, source_target_pairs={{0,4},{1,5},{2,6},{3,7},{4,8},{5,9},{6,10},{7,11},{8,12},{9,13},{1... | collective-permute-start | bytes 786440 | tf_op jit(solution)/shard_map/ppermute | solution.py:20
  71.7 9.2 %collective-permute-start.7 = (bf16[128,1024]{1,0:T(8,128)(2,1)}, bf16[128,1024]{1,0:T(8,128)(2,1)}, u32[]{:S(2)}, u32[]{:S(2)}) collective-permute-start(bf16[128,1024]{1,0:T(8,128)(2,1)} %slice_bitcast_fusion.1), channel_id=1, source_target_pairs={{0,4},{1,5},{2,6},{3,7},{4,8},{5,9},{6,10},{7,11},{8,12},{9,13},{1... | collective-permute-start | bytes 786440 | tf_op jit(solution)/shard_map/ppermute | solution.py:20
  74.9 38.7 %collective-permute-start.3 = (bf16[512,1024]{1,0:T(8,128)(2,1)S(1)}, bf16[512,1024]{1,0:T(8,128)(2,1)}, u32[]{:S(2)}, u32[]{:S(2)}) collective-permute-start(bf16[512,1024]{1,0:T(8,128)(2,1)S(1)} %bitcast.21), channel_id=1, source_target_pairs={{4,0},{5,1},{6,2},{7,3},{8,4},{9,5},{10,6},{11,7},{12,8},{13,9},{1... | collective-permute-start | bytes 3145736 | tf_op jit(solution)/shard_map/ppermute | solution.py:20
  77.8 9.2 %copy-start.21 = (bf16[640,1152]{1,0:T(8,128)(2,1)}, bf16[640,1152]{1,0:T(8,128)(2,1)S(1)}, u32[]{:S(2)}) copy-start(bf16[640,1152]{1,0:T(8,128)(2,1)S(1)} %get-tuple-element.15.band_ref) | copy-start | bytes 4423684
  80.9 1.2 copy-start.16
  87.0 0.7 copy-start.19
  87.7 18.9 %collective-permute-start.11 = (bf16[128,1024]{1,0:T(8,128)(2,1)S(1)}, bf16[128,1024]{1,0:T(8,128)(2,1)}, u32[]{:S(2)}, u32[]{:S(2)}) collective-permute-start(bf16[128,1024]{1,0:T(8,128)(2,1)S(1)} %get-tuple-element.25), channel_id=1, source_target_pairs={{4,0},{5,1},{6,2},{7,3},{8,4},{9,5},{10,6},{11,7},{12,8},{13,9},{1... | collective-permute-start | bytes 786440 | tf_op jit(solution)/shard_map/ppermute | solution.py:20
  89.0 19.7 %copy-start.13 = (bf16[4,128,1024]{2,1,0:T(8,128)(2,1)}, bf16[4,128,1024]{2,1,0:T(8,128)(2,1)S(1)}, u32[]{:S(2)}) copy-start(bf16[4,128,1024]{2,1,0:T(8,128)(2,1)S(1)} %all-to-all-done.1) | copy-start | bytes 3145732
  89.0 17.6 %copy-start.20 = (bf16[128,1024]{1,0:T(8,128)(2,1)S(1)}, bf16[128,1024]{1,0:T(8,128)(2,1)}, u32[]{:S(2)}) copy-start(bf16[128,1024]{1,0:T(8,128)(2,1)} %copy-done.19) | copy-start | bytes 786436
  89.8 23.9 %collective-permute-start.4 = (bf16[128,1024]{1,0:T(8,128)(2,1)}, bf16[128,1024]{1,0:T(8,128)(2,1)}, u32[]{:S(2)}, u32[]{:S(2)}) collective-permute-start(bf16[128,1024]{1,0:T(8,128)(2,1)} %slice_bitcast_fusion.2), channel_id=1, source_target_pairs={{0,4},{1,5},{2,6},{3,7},{4,8},{5,9},{6,10},{7,11},{8,12},{9,13},{1... | collective-permute-start | bytes 786440 | tf_op jit(solution)/shard_map/ppermute | solution.py:20
  95.9 17.7 %collective-permute-start.2 = (bf16[128,1024]{1,0:T(8,128)(2,1)}, bf16[128,1024]{1,0:T(8,128)(2,1)}, u32[]{:S(2)}, u32[]{:S(2)}) collective-permute-start(bf16[128,1024]{1,0:T(8,128)(2,1)} %slice_bitcast_fusion.3), channel_id=1, source_target_pairs={{0,4},{1,5},{2,6},{3,7},{4,8},{5,9},{6,10},{7,11},{8,12},{9,13},{1... | collective-permute-start | bytes 786440 | tf_op jit(solution)/shard_map/ppermute | solution.py:20
  108.7 22.5 %all-to-all-start.7 = ((bf16[4,128,1024]{2,1,0:T(8,128)(2,1)}), bf16[4,128,1024]{2,1,0:T(8,128)(2,1)S(1)}, u32[]{:S(2)}, u32[]{:S(2)}) async-start(bf16[4,128,1024]{2,1,0:T(8,128)(2,1)} %bitcast.25), calls=%async_computation.7 | async-start | bytes 2097152 | tf_op jit(solution)/shard_map/all_to_all | solution.py:26
  113.6 1.2 copy-start.14
  114.9 1.4 copy-start.22
  120.3 9.8 %copy-start.8 = (bf16[512,1024]{1,0:T(8,128)(2,1)}, bf16[512,1024]{1,0:T(8,128)(2,1)S(1)}, u32[]{:S(2)}) copy-start(bf16[512,1024]{1,0:T(8,128)(2,1)S(1)} %get-tuple-element.18.own_ref) | copy-start | bytes 3145732
  120.3 9.8 %collective-permute-start.6 = (bf16[128,1024]{1,0:T(8,128)(2,1)S(1)}, bf16[128,1024]{1,0:T(8,128)(2,1)S(1)}, u32[]{:S(2)}, u32[]{:S(2)}) collective-permute-start(bf16[128,1024]{1,0:T(8,128)(2,1)S(1)} %get-tuple-element.20), channel_id=1, source_target_pairs={{4,0},{5,1},{6,2},{7,3},{8,4},{9,5},{10,6},{11,7},{12,8},{13,9},{1... | collective-permute-start | bytes 786440 | tf_op jit(solution)/shard_map/ppermute | solution.py:20
  121.6 26.5 %collective-permute-start.10 = (bf16[512,1024]{1,0:T(8,128)(2,1)}, bf16[512,1024]{1,0:T(8,128)(2,1)}, u32[]{:S(2)}, u32[]{:S(2)}) collective-permute-start(bf16[512,1024]{1,0:T(8,128)(2,1)} %get-tuple-element.23.own_ref), channel_id=1, source_target_pairs={{0,4},{1,5},{2,6},{3,7},{4,8},{5,9},{6,10},{7,11},{8,12},{9,13},{1... | collective-permute-start | bytes 3145736 | tf_op jit(solution)/shard_map/ppermute | solution.py:20
  130.1 1.1 copy-start.10
  131.2 21.6 %all-to-all-start.6 = ((bf16[4,128,1024]{2,1,0:T(8,128)(2,1)}), bf16[4,128,1024]{2,1,0:T(8,128)(2,1)S(1)}, u32[]{:S(2)}, u32[]{:S(2)}) async-start(bf16[4,128,1024]{2,1,0:T(8,128)(2,1)} %bitcast.26), calls=%async_computation.6 | async-start | bytes 2097152 | tf_op jit(solution)/shard_map/all_to_all | solution.py:26
  135.5 35.1 %collective-permute-start.5 = (bf16[512,1024]{1,0:T(8,128)(2,1)}, bf16[512,1024]{1,0:T(8,128)(2,1)}, u32[]{:S(2)}, u32[]{:S(2)}) collective-permute-start(bf16[512,1024]{1,0:T(8,128)(2,1)} %copy-done.8), channel_id=1, source_target_pairs={{0,4},{1,5},{2,6},{3,7},{4,8},{5,9},{6,10},{7,11},{8,12},{9,13},{1... | collective-permute-start | bytes 3145736 | tf_op jit(solution)/shard_map/ppermute | solution.py:20
  151.8 1.0 copy-start.7
  152.8 17.8 %copy-start.11 = (bf16[128,1024]{1,0:T(8,128)(2,1)S(1)}, bf16[128,1024]{1,0:T(8,128)(2,1)}, u32[]{:S(2)}) copy-start(bf16[128,1024]{1,0:T(8,128)(2,1)} %copy-done.10) | copy-start | bytes 786436
  152.8 1.0 copy-start.4
  153.8 22.5 %all-to-all-start.5 = ((bf16[4,128,1024]{2,1,0:T(8,128)(2,1)}), bf16[4,128,1024]{2,1,0:T(8,128)(2,1)S(1)}, u32[]{:S(2)}, u32[]{:S(2)}) async-start(bf16[4,128,1024]{2,1,0:T(8,128)(2,1)} %bitcast.20), calls=%async_computation.5 | async-start | bytes 2097152 | tf_op jit(solution)/shard_map/all_to_all | solution.py:26
  170.6 1.2 copy-start.9
  175.4 1.0 copy-start.6
  176.4 48.0 %all-to-all-start.2 = ((bf16[4,128,1024]{2,1,0:T(8,128)(2,1)}), bf16[4,128,1024]{2,1,0:T(8,128)(2,1)S(1)}, u32[]{:S(2)}, u32[]{:S(2)}) async-start(bf16[4,128,1024]{2,1,0:T(8,128)(2,1)} %bitcast.19), calls=%async_computation.2 | async-start | bytes 2097152 | tf_op jit(solution)/shard_map/all_to_all | solution.py:26
  181.8 13.4 %collective-permute-start.1 = (f32[1,8,1024]{2,1,0:T(8,128)S(1)}, f32[1,8,1024]{2,1,0:T(8,128)S(1)}, u32[]{:S(2)}, u32[]{:S(2)}) collective-permute-start(f32[1,8,1024]{2,1,0:T(8,128)S(1)} %get-tuple-element.26), channel_id=1, source_target_pairs={{1,0},{2,1},{3,2},{4,3},{5,4},{6,5},{7,6},{8,7},{9,8},{10,9},{11,1... | collective-permute-start | bytes 98312 | tf_op jit(solution)/shard_map/ppermute | solution.py:20
  183.8 11.4 %collective-permute-start = (f32[1,8,1024]{2,1,0:T(8,128)S(1)}, f32[1,8,1024]{2,1,0:T(8,128)S(1)}, u32[]{:S(2)}, u32[]{:S(2)}) collective-permute-start(f32[1,8,1024]{2,1,0:T(8,128)S(1)} %get-tuple-element.27), channel_id=1, source_target_pairs={{0,1},{1,2},{2,3},{3,4},{4,5},{5,6},{6,7},{7,8},{8,9},{9,10},{10,1... | collective-permute-start | bytes 98312 | tf_op jit(solution)/shard_map/ppermute | solution.py:20
  195.2 2.2 copy-start.1
  197.4 23.1 %copy-start.5 = (bf16[4,128,1024]{2,1,0:T(8,128)(2,1)S(1)}, bf16[4,128,1024]{2,1,0:T(8,128)(2,1)}, u32[]{:S(2)}) copy-start(bf16[4,128,1024]{2,1,0:T(8,128)(2,1)} %copy-done.4) | copy-start | bytes 3145732
  218.4 2.0 copy-start.2
  224.4 2.2 copy-start.3

commit v2 on v1

v2 whole, which is shorter than its diff:
```python
import functools

import jax
import jax.numpy as jnp
from jax import lax
from jax.experimental import pallas as pl
from jax.experimental.pallas import tpu as pltpu
from jax.sharding import PartitionSpec as P

G = 4
CHUNKS = 2
F32 = jnp.float32
BF16 = jnp.bfloat16
MIB = 1024 * 1024
SMEM = pl.BlockSpec(memory_space=pltpu.SMEM)
VMEM = pl.BlockSpec(memory_space=pltpu.VMEM)
ANY = pl.BlockSpec(memory_space=pl.ANY)


def moved(value, steps, only=None):
    count = lax.axis_size("slab")
    first, last = max(0, -steps), min(count, count - steps)
    pairs = [(i, i + steps) for i in range(first, last) if only is None or i % G == only]
    return lax.ppermute(value, "slab", pairs)


def swapped(value, bits):
    count = lax.axis_size("slab")
    return lax.ppermute(value, "slab", [(i, i ^ bits) for i in range(count)])


def exchanged(value):
    count = lax.axis_size("slab")
    sets = [list(range(first, first + G)) for first in range(0, count, G)]
    return lax.all_to_all(value, "slab", 0, 0, axis_index_groups=sets, tiled=True)


def call(kernel, us, nbytes, vmem=16, **how):
    return pl.pallas_call(
        kernel,
        compiler_params=pltpu.CompilerParams(vmem_limit_bytes=vmem * MIB),
        cost_estimate=pl.CostEstimate(flops=int(us * 1.15e9), bytes_accessed=int(nbytes), transcendentals=0),
        **how,
    )


def cast_kernel(chunk, vol_ref, out_ref):
    depth = out_ref.shape[1]
    for p in range(G):
        out_ref[p] = vol_ref[pl.ds(2 * p + chunk, depth, stride=8), :].astype(BF16)


def cast_rows(volume, chunk):
    depth, rows, cols = volume.shape
    tile = 128
    return call(
        functools.partial(cast_kernel, chunk),
        2,
        5 * MIB,
        grid=(cols // tile,),
        in_specs=[pl.BlockSpec((depth * rows, tile), lambda i: (0, i))],
        out_specs=pl.BlockSpec((G, depth, tile), lambda i: (0, 0, i)),
        out_shape=jax.ShapeDtypeStruct((G, depth, cols), BF16),
    )(volume.reshape(depth * rows, cols))


def split_kernel(here_ref, own_ref, got_ref, *refs):
    out_refs, wide = refs[:-1], refs[-1]
    depth = out_refs[0].shape[0]
    place = lax.rem(here_ref[0], G)

    @pl.when(place == G - 1)
    def _():
        wide[...] = got_ref[...].astype(F32).reshape(wide.shape)

    @pl.when(place != G - 1)
    def _():
        wide[...] = own_ref[...].astype(F32).reshape(wide.shape)

    for c in range(CHUNKS):
        for m in range(G):
            row = 2 * jnp.bitwise_xor(place, m) + c
            out_refs[c * G + m][...] = wide[pl.ds(row, depth, stride=8), :].astype(BF16)


def split_rows(here, own, got):
    depth, rows, cols = own.shape
    tile = 128
    block = pl.BlockSpec((depth, rows, tile), lambda i: (0, 0, i))
    return call(
        split_kernel,
        4,
        6 * MIB,
        grid=(cols // tile,),
        in_specs=[SMEM, block, block],
        out_specs=[pl.BlockSpec((depth, tile), lambda i: (0, i))] * (CHUNKS * G),
        out_shape=[jax.ShapeDtypeStruct((depth, cols), BF16)] * (CHUNKS * G),
        scratch_shapes=[pltpu.VMEM((depth * rows, tile), F32)],
    )(here, own, got)


def last_kernel(slabs, here_ref, cover_ref, offset_ref, w_ref, v0_ref, v1_ref, sino_ref, r_ref, b_ref, v, s, r, b, wide):
    depth, rows, cols = sino_ref.shape
    tile = 128

    @pl.when(here_ref[0] == slabs - 1)
    def _():
        pltpu.sync_copy(v0_ref, v.at[0])
        pltpu.sync_copy(v1_ref, v.at[1])
        pltpu.sync_copy(sino_ref, s)
        block = w_ref[offset_ref[slabs - 1, 0]]
        block = jnp.where(cover_ref[slabs - 1, 0] == 1, block, jnp.zeros_like(block))
        turned = block.astype(F32).T.astype(BF16)

        def column(j, _):
            at = pl.ds(pl.multiple_of(j * tile, tile), tile)
            wide[...] = s[:, :, at].astype(F32).reshape(wide.shape)
            for row in range(rows):
                p, c = row // CHUNKS, row % CHUNKS
                seen = jnp.dot(block, v[c, p, :, at], preferred_element_type=F32)
                resid = (seen - wide[pl.ds(row, depth, stride=rows), :]).astype(BF16)
                r[row, :, at] = resid
                b[row, :, at] = jnp.dot(turned, resid, preferred_element_type=F32)
            return 0

        lax.fori_loop(0, cols // tile, column, 0)
        pltpu.sync_copy(r, r_ref)
        pltpu.sync_copy(b, b_ref)


def last_group(here, coverage, offsets, weights, v0, v1, sinogram):
    slabs = coverage.shape[0]
    depth, rows, cols = sinogram.shape
    return call(
        functools.partial(last_kernel, slabs),
        1,
        MIB,
        in_specs=[SMEM, SMEM, SMEM, VMEM, ANY, ANY, ANY],
        out_specs=[ANY, ANY],
        out_shape=[
            jax.ShapeDtypeStruct((rows, depth, cols), BF16),
            jax.ShapeDtypeStruct((rows, depth, cols), F32),
        ],
        scratch_shapes=[
            pltpu.VMEM((CHUNKS,) + v0.shape, BF16),
            pltpu.VMEM(sinogram.shape, BF16),
            pltpu.VMEM((rows, depth, cols), BF16),
            pltpu.VMEM((rows, depth, cols), F32),
            pltpu.VMEM((depth * rows, 128), F32),
        ],
    )(here, coverage, offsets, weights, v0, v1, sinogram)


def join_kernel(slabs, here_ref, *refs):
    in_refs, last_ref, out_ref, wide, held = refs[:-4], refs[-4], refs[-3], refs[-2], refs[-1]
    depth = in_refs[0].shape[0]
    rows, tile = held.shape[0], held.shape[2]
    place = lax.rem(here_ref[0], G)
    last = here_ref[0] == slabs - 1

    @pl.when(last)
    def _():
        at = pl.ds(pl.multiple_of(pl.program_id(0) * tile, tile), tile)
        pltpu.sync_copy(last_ref.at[:, :, at], held)
        for row in range(rows):
            wide[pl.ds(row, depth, stride=rows), :] = held[row].astype(F32)

    @pl.when(jnp.logical_not(last))
    def _():
        for c in range(CHUNKS):
            for m in range(G):
                row = 2 * jnp.bitwise_xor(place, m) + c
                wide[pl.ds(row, depth, stride=rows), :] = in_refs[c * G + m][...].astype(F32)

    out_ref[...] = wide[...].reshape(out_ref.shape).astype(out_ref.dtype)


def join_rows(here, slabs, blocks, last):
    rows, depth, cols = last.shape
    tile = 128
    return call(
        functools.partial(join_kernel, slabs),
        4,
        4 * MIB,
        grid=(cols // tile,),
        in_specs=[SMEM] + [pl.BlockSpec((depth, tile), lambda i: (0, i))] * len(blocks) + [ANY],
        out_specs=pl.BlockSpec((depth, rows, tile), lambda i: (0, 0, i)),
        out_shape=jax.ShapeDtypeStruct((depth, rows, cols), BF16),
        scratch_shapes=[pltpu.VMEM((depth * rows, tile), F32), pltpu.VMEM((rows, depth, tile), BF16)],
    )(here, *blocks, last)


def finish_kernel(slabs, here_ref, tv_ref, b0_ref, b1_ref, last_ref, out_ref, wide, held):
    depth = b0_ref.shape[1]
    rows, tile = held.shape[0], held.shape[2]
    last = here_ref[0] == slabs - 1
    for p in range(G):
        wide[pl.ds(2 * p, depth, stride=rows), :] = b0_ref[p].astype(F32)
        wide[pl.ds(2 * p + 1, depth, stride=rows), :] = b1_ref[p].astype(F32)

    @pl.when(last)
    def _():
        at = pl.ds(pl.multiple_of(pl.program_id(0) * tile, tile), tile)
        pltpu.sync_copy(last_ref.at[:, :, at], held)
        for row in range(rows):
            spot = pl.ds(row, depth, stride=rows)
            wide[spot, :] = wide[spot, :] + held[row]

    out_ref[...] = tv_ref[...] + wide[...].reshape(out_ref.shape)


def finish(here, slabs, tv, chunks, last):
    depth, rows, cols = tv.shape
    tile = 128
    whole = pl.BlockSpec((depth, rows, tile), lambda i: (0, 0, i))
    return call(
        functools.partial(finish_kernel, slabs),
        5,
        10 * MIB,
        grid=(cols // tile,),
        in_specs=[SMEM, whole] + [pl.BlockSpec((G, depth, tile), lambda i: (0, 0, i))] * CHUNKS + [ANY],
        out_specs=whole,
        out_shape=jax.ShapeDtypeStruct((depth, rows, cols), F32),
        scratch_shapes=[pltpu.VMEM((depth * rows, tile), F32), pltpu.VMEM((rows, depth, tile), F32)],
    )(here, tv, *chunks, last)


def band_kernel(slabs, span, here_ref, cover_ref, offset_ref, w_ref, proj_ref, back_ref):
    side = w_ref.shape[1]
    first = (here_ref[0] // G) * G
    zero = jnp.zeros((side, side), BF16)

    def block(i, j, k):
        safe = jnp.clip(i, 0, slabs - 1)
        inside = jnp.logical_and(i >= 0, j < slabs)
        live = jnp.logical_and(inside, cover_ref[safe, k] == 1)
        return jnp.where(live, w_ref[offset_ref[safe, k]], zero)

    for r in range(G):
        for s in range(2 * G + 1):
            at = (pl.ds(r * side, side), pl.ds(s * side, side))
            k = s - r
            proj_ref[at] = block(first - 1 + r, first - 1 + s, k) if 0 <= k < span else zero
            k = (r + G + 1) - s
            value = zero
            if 0 <= k < span:
                value = block(first - G - 1 + s, first + r, k).astype(F32).T.astype(BF16)
            back_ref[at] = value


def bands(here, coverage, offsets, weights):
    slabs, span = coverage.shape
    side = weights.shape[1]
    shape = jax.ShapeDtypeStruct((G * side, (2 * G + 1) * side), BF16)
    return call(
        functools.partial(band_kernel, slabs, span),
        1.5,
        3 * MIB,
        in_specs=[SMEM, SMEM, SMEM, VMEM],
        out_specs=[VMEM, VMEM],
        out_shape=[shape, shape],
    )(here, coverage, offsets, weights)


def project_kernel(here_ref, band_ref, low_ref, own_ref, high_ref, *refs):
    s_refs, (_, r_ref, down_ref, total) = refs[:G], refs[G:]
    side = low_ref.shape[0]
    n = G * side
    place = lax.rem(here_ref[0], G)
    sums = jnp.dot(band_ref[:, side : side + n], own_ref[...], preferred_element_type=F32)
    sums += jnp.dot(band_ref[:, side + n :], high_ref[...], preferred_element_type=F32)
    sums += jnp.dot(band_ref[:, :side], low_ref[...], preferred_element_type=F32)
    total[...] = sums
    for m in range(G):
        spot = lax.rem(jnp.bitwise_xor(place, m) + 1, G)
        at = pl.ds(pl.multiple_of(spot * side, side), side)
        r_ref[at, :] = (total[at, :] - s_refs[m][...].astype(F32)).astype(BF16)
    down_ref[...] = r_ref[:side]


def project(here, band, low, own, high, sinos, token):
    side, cols = low.shape
    n = G * side
    tile = 256
    one = pl.BlockSpec((side, tile), lambda i: (0, i))
    many = pl.BlockSpec((n, tile), lambda i: (0, i))
    return call(
        project_kernel,
        4,
        6 * MIB,
        grid=(cols // tile,),
        in_specs=[SMEM, pl.BlockSpec(band.shape, lambda i: (0, 0)), one, many, many] + [one] * G + [ANY],
        out_specs=[many, one],
        out_shape=[jax.ShapeDtypeStruct((n, cols), BF16), jax.ShapeDtypeStruct((side, cols), BF16)],
        scratch_shapes=[pltpu.VMEM((n, tile), F32)],
    )(here, band, low, own, high, *sinos, token)


def deal_kernel(here_ref, r_ref, high_ref, *out_refs):
    side = high_ref.shape[0]
    place = lax.rem(here_ref[0], G)
    for m in range(G):
        to = jnp.bitwise_xor(place, m)

        @pl.when(to == G - 1)
        def _():
            out_refs[m][...] = high_ref[...]

        @pl.when(to != G - 1)
        def _():
            spot = lax.rem(to + 1, G)
            out_refs[m][...] = r_ref[pl.ds(pl.multiple_of(spot * side, side), side), :]


def deal(here, resid, high):
    return call(
        deal_kernel,
        1,
        2 * MIB,
        in_specs=[SMEM, VMEM, VMEM],
        out_specs=[VMEM] * G,
        out_shape=[jax.ShapeDtypeStruct(high.shape, BF16)] * G,
    )(here, resid, high)


def back_kernel(band_ref, low_ref, own_ref, high_ref, out_ref):
    side = high_ref.shape[0]
    n = G * side
    total = jnp.dot(band_ref[:, n : 2 * n], own_ref[...], preferred_element_type=F32)
    total += jnp.dot(band_ref[:, :n], low_ref[...], preferred_element_type=F32)
    total += jnp.dot(band_ref[:, 2 * n :], high_ref[...], preferred_element_type=F32)
    out_ref[...] = total.astype(BF16)


def back(band, low, own, high):
    side, cols = high.shape
    n = G * side
    tile = 256
    one = pl.BlockSpec((side, tile), lambda i: (0, i))
    many = pl.BlockSpec((n, tile), lambda i: (0, i))
    return call(
        back_kernel,
        4,
        6 * MIB,
        grid=(cols // tile,),
        in_specs=[pl.BlockSpec(band.shape, lambda i: (0, 0)), many, many, one],
        out_specs=many,
        out_shape=jax.ShapeDtypeStruct((n, cols), BF16),
    )(band, low, own, high)


def tv_kernel(low_ref, high_ref, next_ref, vol_ref, out_ref, flux_ref):
    step = pl.program_id(0)
    steps = pl.num_programs(0)
    deep, rows, cols = vol_ref.shape
    row = lax.broadcasted_iota(jnp.int32, (rows, cols), 0)
    col = lax.broadcasted_iota(jnp.int32, (rows, cols), 1)

    def up_y(v):
        return jnp.where(row == rows - 1, 0.0, pltpu.roll(v, rows - 1, 0))

    def up_x(v):
        return jnp.where(col == cols - 1, 0.0, pltpu.roll(v, cols - 1, 1))

    def scale_of(cur, above):
        dz = above - cur
        dy = up_y(cur) - cur
        dx = up_x(cur) - cur
        return dz, dy, dx, 0.5 * lax.rsqrt(dz * dz + dy * dy + dx * dx + 0.25)

    def edge(v):
        return 0.5 * v * lax.rsqrt(v * v + 0.25)

    @pl.when(step == 0)
    def _():
        dz, _, _, scale = scale_of(low_ref[0], vol_ref[0])
        flux_ref[...] = dz * scale

    def one(z, cur, above, below_flux):
        dz, dy, dx, scale = scale_of(cur, above)
        fz, fy, fx = dz * scale, dy * scale, dx * scale
        sides = edge(cur)
        fy_low = jnp.where(row == 0, sides, pltpu.roll(fy, 1, 0))
        fx_low = jnp.where(col == 0, sides, pltpu.roll(fx, 1, 1))
        out_ref[z] = (below_flux - fz) + (fy_low - fy) + (fx_low - fx)
        return fz

    def body(z, flux):
        return one(z, vol_ref[z], vol_ref[z + 1], flux)

    flux = lax.fori_loop(0, deep - 1, body, flux_ref[...], unroll=5)
    above = jnp.where(step == steps - 1, high_ref[0], next_ref[0])
    flux_ref[...] = one(deep - 1, vol_ref[deep - 1], above, flux)


def half_tv(volume, low, high):
    depth, rows, cols = volume.shape
    deep = 16
    steps = depth // deep
    edge = pl.BlockSpec((1, rows, cols), lambda i: (0, 0, 0))
    body = pl.BlockSpec((deep, rows, cols), lambda i: (i, 0, 0))
    after = pl.BlockSpec((1, rows, cols), lambda i: (jnp.minimum((i + 1) * deep, depth - 1), 0, 0))
    return call(
        tv_kernel,
        10,
        8 * MIB,
        grid=(steps,),
        in_specs=[edge, edge, after, body],
        out_specs=body,
        out_shape=jax.ShapeDtypeStruct(volume.shape, F32),
        scratch_shapes=[pltpu.VMEM((rows, cols), F32)],
    )(low, high, volume, volume)


def local(volume, sinogram, weights, coverage, offsets):
    slabs = lax.axis_size("slab")
    here = lax.axis_index("slab").astype(jnp.int32).reshape(1)
    depth, rows, cols = volume.shape
    whole = (G * depth, cols)

    got = moved(sinogram, G, only=G - 1)
    vol_rows = [cast_rows(volume, c) for c in range(CHUNKS)]
    band_p, band_b = bands(here, coverage, offsets, weights)
    below = moved(volume[-1:], 1)
    above = moved(volume[:1], -1)
    r_last, b_last = last_group(here, coverage, offsets, weights, *vol_rows, sinogram)

    own = [exchanged(v).reshape(whole) for v in vol_rows]
    high = [moved(v, -G) for v in own]
    low = [moved(v[(G - 1) * depth :], G) for v in own]
    sino = split_rows(here, sinogram, got)
    sinos = []
    for c in range(CHUNKS):
        mine = sino[c * G : (c + 1) * G]
        sinos.append([mine[0]] + [swapped(mine[m], m) for m in range(1, G)])
    tv = half_tv(volume, below, above)

    resid_blocks, back_rows = [], []
    for c in range(CHUNKS):
        token = tv if c else band_b
        resid, down = project(here, band_p, low[c], own[c], high[c], sinos[c], token)
        r_low = moved(resid, G)
        r_high = moved(down, -G)
        dealt = deal(here, resid, r_high)
        resid_blocks += [dealt[0]] + [swapped(dealt[m], m) for m in range(1, G)]
        backproj = back(band_b, r_low, resid, r_high)
        back_rows.append(exchanged(backproj.reshape(G, depth, cols)))

    residual = join_rows(here, slabs, resid_blocks, r_last)
    gradient = finish(here, slabs, tv, back_rows, b_last)
    return (gradient, residual)


def solution(mesh):
    placed = (P("slab", "grp", None), P("slab", "grp", None), P(), P(), P())
    return jax.shard_map(
        local,
        mesh=mesh,
        in_specs=placed,
        out_specs=(P("slab", "grp", None), P("slab", "grp", None)),
        check_vma=False,
    )
```

time: 233 us -> 180 us (0.77)
  blocking collectives: 17.7 us -> 0 us
  waiting for transfers between devices: 60.9 us -> 47.1 us
  starting transfers between devices: 68.3 us -> 58.1 us
  Pallas kernels: 54.6 us -> 49.7 us
  local copies, waits for them, and re-layouts: 26 us -> 22 us
  other arithmetic: 3.14 us -> 0 us
    all_to_all x1 -> x0, blocking collectives: 17.7 us -> none  [exchanged(): lax.all_to_all(value, 'slab', 0, 0, axis_index_groups=sets, tiled=True)]
    all_to_all x7 -> x4, starting transfers between devices: 32.4 us -> 19.7 us  [exchanged(): lax.all_to_all(value, 'slab', 0, 0, axis_index_groups=sets, tiled=True)]
    all_to_all x7 -> x4, waiting for transfers between devices: 20 us -> 8.9 us  [exchanged(): lax.all_to_all(value, 'slab', 0, 0, axis_index_groups=sets, tiled=True)]
    pallas_call x10 -> x14, Pallas kernels: 54.6 us -> 49.7 us  [the longest x2 8.15 us: project(): call(project_kernel, 4, 6 * MIB, grid=(cols // tile,), in_specs=[SMEM, pl...]
    ppermute x12 -> x23, waiting for transfers between devices: 40.9 us -> 38.2 us  [the longest x12 22.9 us: swapped(): return lax.ppermute(value, 'slab', [(i, i ^ bits) for i in range(count)])]
    slice x4 -> x0, local copies, waits for them, and re-layouts: 2.7 us -> none  [the longest x2 1.46 us: local(): slow = [moved(s[(G - 1) * depth:], G) for s in sown]]
    ppermute x12 -> x23, starting transfers between devices: 35.9 us -> 38.4 us  [the longest x11 27.2 us: moved(): return lax.ppermute(value, 'slab', pairs)]
    unnamed x52 -> x56, local copies, waits for them, and re-layouts: 20.1 us -> 19.5 us
  transfers between devices with their start and end apart: 19 -> 27, of which waited for: 8 -> 9; matrix products, arithmetic and copies ran while one was open for 4% -> 1% of each run, Pallas kernels for 20% -> 24%
where the time goes in v2:
time: 180 us; the launch traced here: 178 us
  starting transfers between devices  58.1 us (32%)
  Pallas kernels  49.7 us (28%)
  waiting for transfers between devices  47.1 us (26%)
  local copies, waits for them, and re-layouts  22 us (12%)
    ppermute x11, starting transfers between devices, moved(): return lax.ppermute(value, 'slab', pairs)  27.2 us
    ppermute x12, waiting for transfers between devices, swapped(): return lax.ppermute(value, 'slab', [(i, i ^ bits) for i in range(count)])  22.9 us
    all_to_all x4, starting transfers between devices, exchanged(): lax.all_to_all(value, 'slab', 0, 0, axis_index_groups=sets, tiled=True)  19.7 us
    unnamed x56, local copies, waits for them, and re-layouts  19.5 us
    ppermute x11, waiting for transfers between devices, moved(): return lax.ppermute(value, 'slab', pairs)  15.2 us
    ppermute x12, starting transfers between devices, swapped(): return lax.ppermute(value, 'slab', [(i, i ^ bits) for i in range(count)])  11.2 us
    all_to_all x4, waiting for transfers between devices, exchanged(): lax.all_to_all(value, 'slab', 0, 0, axis_index_groups=sets, tiled=True)  8.9 us
    pallas_call x2, Pallas kernels, project(): call(project_kernel, 4, 6 * MIB, grid=(cols // tile,), in_specs=[SMEM, pl...  8.15 us
  transfers between devices with their start and end apart: 27, of which 9 were waited for; matrix products, arithmetic and copies ran while one was open for 1% of the time, Pallas kernels for 24%

profile of v2, /device:TPU:1, one launch (start us, length us, event | category | flops | bytes accessed | tf_op | source)
XLA Modules:
  0.0 177.7 jit_solution(3082156943321322053)
XLA Ops:
  0.6 2.0 %collective-permute-start.4 = (bf16[128,8,1024]{2,1,0:T(8,128)(2,1)}, bf16[128,8,1024]{2,1,0:T(8,128)(2,1)}, u32[]{:S(2)}, u32[]{:S(2)}) collective-permute-start(bf16[128,8,1024]{2,1,0:T(8,128)(2,1)} %sino_ref.1), channel_id=1, source_target_pairs={{3,7},{7,11},{11,15},{19,23},{23,27},{27,31}} | collective-permute-start | bytes 6291464 | tf_op jit(solution)/shard_map/ppermute | solution.py:24
  2.6 2.2 %copy-done.4 = f32[128,8,1024]{2,1,0:T(8,128)S(1)} copy-done((f32[128,8,1024]{2,1,0:T(8,128)S(1)}, f32[128,8,1024]{2,1,0:T(8,128)}, u32[]{:S(2)}) %copy-start.4) | copy-done | bytes 4194328
  4.8 3.3 %shard_map.74.v1_ref = bf16[4,128,1024]{2,1,0:T(8,128)(2,1)} custom-call(f32[1024,1024]{1,0:T(8,128)S(1)} %bitcast.14), custom_call_target="tpu_custom_call" | custom-call | flops 2300000000 | bytes 5242880 | tf_op jit(solution)/shard_map/pallas_call | solution.py:56
  8.2 6.3 %all-to-all-start.2 = ((bf16[4,128,1024]{2,1,0:T(8,128)(2,1)}), bf16[4,128,1024]{2,1,0:T(8,128)(2,1)}, u32[]{:S(2)}, u32[]{:S(2)}) async-start(bf16[4,128,1024]{2,1,0:T(8,128)(2,1)} %shard_map.74.v1_ref), calls=%async_computation.2 | async-start | bytes 2097152 | tf_op jit(solution)/shard_map/all_to_all | solution.py:35
  14.4 2.2 %copy-done.5 = f32[128,8,1024]{2,1,0:T(8,128)S(1)} copy-done((f32[128,8,1024]{2,1,0:T(8,128)S(1)}, f32[128,8,1024]{2,1,0:T(8,128)}, u32[]{:S(2)}) %copy-start.5) | copy-done | bytes 4194328
  16.6 3.3 %shard_map.70.v0_ref = bf16[4,128,1024]{2,1,0:T(8,128)(2,1)} custom-call(f32[1024,1024]{1,0:T(8,128)S(1)} %bitcast.15), custom_call_target="tpu_custom_call" | custom-call | flops 2300000000 | bytes 5242880 | tf_op jit(solution)/shard_map/pallas_call | solution.py:56
  20.0 8.9 %all-to-all-done.2 = bf16[4,128,1024]{2,1,0:T(8,128)(2,1)} async-done(((bf16[4,128,1024]{2,1,0:T(8,128)(2,1)}), bf16[4,128,1024]{2,1,0:T(8,128)(2,1)}, u32[]{:S(2)}, u32[]{:S(2)}) %all-to-all-start.2) | async-done | bytes 1048608 | tf_op jit(solution)/shard_map/all_to_all | solution.py:35
  28.9 3.6 %all-to-all-start = ((bf16[4,128,1024]{2,1,0:T(8,128)(2,1)}), bf16[4,128,1024]{2,1,0:T(8,128)(2,1)S(1)}, u32[]{:S(2)}, u32[]{:S(2)}) async-start(bf16[4,128,1024]{2,1,0:T(8,128)(2,1)} %shard_map.70.v0_ref), calls=%async_computation | async-start | bytes 2097152 | tf_op jit(solution)/shard_map/all_to_all | solution.py:35
  33.2 3.5 %collective-permute-start = (f32[1,8,1024]{2,1,0:T(8,128)S(1)}, f32[1,8,1024]{2,1,0:T(8,128)S(1)}, u32[]{:S(2)}, u32[]{:S(2)}) collective-permute-start(f32[1,8,1024]{2,1,0:T(8,128)S(1)} %get-tuple-element.51), channel_id=1, source_target_pairs={{0,1},{1,2},{2,3},{3,4},{4,5},{5,6},{6,7},{7,8},{8,9},{9,10},{10,1... | collective-permute-start | bytes 98312 | tf_op jit(solution)/shard_map/ppermute | solution.py:24
  36.8 1.9 %collective-permute-start.1 = (f32[1,8,1024]{2,1,0:T(8,128)S(1)}, f32[1,8,1024]{2,1,0:T(8,128)S(1)}, u32[]{:S(2)}, u32[]{:S(2)}) collective-permute-start(f32[1,8,1024]{2,1,0:T(8,128)S(1)} %get-tuple-element.50), channel_id=1, source_target_pairs={{1,0},{2,1},{3,2},{4,3},{5,4},{6,5},{7,6},{8,7},{9,8},{10,9},{11,1... | collective-permute-start | bytes 98312 | tf_op jit(solution)/shard_map/ppermute | solution.py:24
  38.9 1.3 shard_map.69
  41.2 1.0 copy-done.21
  42.2 1.3 collective-permute-start.11
  43.5 1.7 slice_bitcast_fusion
  45.2 4.7 %collective-permute-start.10 = (bf16[128,1024]{1,0:T(8,128)(2,1)}, bf16[128,1024]{1,0:T(8,128)(2,1)}, u32[]{:S(2)}, u32[]{:S(2)}) collective-permute-start(bf16[128,1024]{1,0:T(8,128)(2,1)} %slice_bitcast_fusion), channel_id=1, source_target_pairs={{0,4},{1,5},{2,6},{3,7},{4,8},{5,9},{6,10},{7,11},{8,12},{9,13},{1... | collective-permute-start | bytes 786440 | tf_op jit(solution)/shard_map/ppermute | solution.py:24
  49.9 1.6 collective-permute-start.3
  51.5 5.4 %shard_map.71 = (bf16[128,1024]{1,0:T(8,128)(2,1)S(1)}, bf16[128,1024]{1,0:T(8,128)(2,1)S(1)}, bf16[128,1024]{1,0:T(8,128)(2,1)S(1)}, bf16[128,1024]{1,0:T(8,128...) custom-call(s32[1]{0:T(128)} %bitcast.here_ref, ...), custom_call_target="tpu_custom_call" | custom-call | flops 4600000000 | bytes 6291456 | tf_op jit(solution)/shard_map/pallas_call | solution.py:90
  57.0 1.1 collective-permute-start.12
  58.1 1.3 collective-permute-start.13
  59.8 6.7 %shard_map.68.refs_4_.tv_ref = f32[128,8,1024]{2,1,0:T(8,128)S(1)} custom-call(f32[1,8,1024]{2,1,0:T(8,128)S(1)} %collective-permute-done.low_ref, f32[1,8,1024]{2,1,0:T(8,128)S(1)} %collective-permute-done.1.high_ref, f32[128,8,1024]{2,1,0:T(8,128)S(1)} %copy-done.6, f32[128,8,1024]{2,1,0:T(8,128)S(1)} %copy-done.6), custom_call_target="tpu_custom_call" | custom-call | flops 11500000256 | bytes 8388608 | tf_op jit(solution)/shard_map/pallas_call | solution.py:403
  66.5 2.1 %collective-permute-done.11.high_ref = bf16[512,1024]{1,0:T(8,128)(2,1)} collective-permute-done((bf16[512,1024]{1,0:T(8,128)(2,1)}, bf16[512,1024]{1,0:T(8,128)(2,1)}, u32[]{:S(2)}, u32[]{:S(2)}) %collective-permute-start.11) | collective-permute-done | bytes 1048608 | tf_op jit(solution)/shard_map/ppermute | solution.py:24
  68.7 2.5 %collective-permute-start.2 = (bf16[128,1024]{1,0:T(8,128)(2,1)S(1)}, bf16[128,1024]{1,0:T(8,128)(2,1)S(1)}, u32[]{:S(2)}, u32[]{:S(2)}) collective-permute-start(bf16[128,1024]{1,0:T(8,128)(2,1)S(1)} %slice_bitcast_fusion.1), channel_id=1, source_target_pairs={{0,4},{1,5},{2,6},{3,7},{4,8},{5,9},{6,10},{7,11},{8,12},{9,13},{1... | collective-permute-start | bytes 786440 | tf_op jit(solution)/shard_map/ppermute | solution.py:24
  72.1 4.3 %shard_map.75 = (bf16[512,1024]{1,0:T(8,128)(2,1)S(1)}, bf16[128,1024]{1,0:T(8,128)(2,1)S(1)}) custom-call(s32[1]{0:T(128)} %bitcast.here_ref, bf16[512,1152]{1,0:T(8,128)(2,1)S(1)} %copy-done.22, bf16[128,1024]{1,0:T(8,128)(2,1)} %collective-permute-done.10.low_ref, bf16[512,1024]{1,0:T(8,128)(2,1)} %bitcast.6.own_ref, ...), custom_call_target="tpu_custom_call" | custom-call | flops 4600000000 | bytes 6291456 | tf_op jit(solution)/shard_map/pallas_call | solution.py:287
  76.4 4.3 %collective-permute-start.15 = (bf16[512,1024]{1,0:T(8,128)(2,1)S(1)}, bf16[512,1024]{1,0:T(8,128)(2,1)S(1)}, u32[]{:S(2)}, u32[]{:S(2)}) collective-permute-start(bf16[512,1024]{1,0:T(8,128)(2,1)S(1)} %get-tuple-element.38.own_ref.r_ref), channel_id=1, source_target_pairs={{0,4},{1,5},{2,6},{3,7},{4,8},{5,9},{6,10},{7,11},{8,12},{9,13},{1... | collective-permute-start | bytes 3145736 | tf_op jit(solution)/shard_map/ppermute | solution.py:24
  80.8 2.3 %collective-permute-start.5 = (bf16[128,1024]{1,0:T(8,128)(2,1)S(1)}, bf16[128,1024]{1,0:T(8,128)(2,1)S(1)}, u32[]{:S(2)}, u32[]{:S(2)}) collective-permute-start(bf16[128,1024]{1,0:T(8,128)(2,1)S(1)} %get-tuple-element.29), channel_id=1, source_target_pairs={{0,1},{1,0},{2,3},{3,2},{4,5},{5,4},{6,7},{7,6},{8,9},{9,8},{10,11... | collective-permute-start | bytes 786440 | tf_op jit(solution)/shard_map/ppermute | solution.py:29
  84.7 6.3 %collective-permute-done.3.high_ref = bf16[512,1024]{1,0:T(8,128)(2,1)S(1)} collective-permute-done((bf16[512,1024]{1,0:T(8,128)(2,1)S(1)}, bf16[512,1024]{1,0:T(8,128)(2,1)S(1)}, u32[]{:S(2)}, u32[]{:S(2)}) %collective-permute-start.3) | collective-permute-done | bytes 1048608 | tf_op jit(solution)/shard_map/ppermute | solution.py:24
  91.0 1.3 collective-permute-start.16
  92.4 4.3 %collective-permute-done.7.refs_3_ = bf16[128,1024]{1,0:T(8,128)(2,1)S(1)} collective-permute-done((bf16[128,1024]{1,0:T(8,128)(2,1)S(1)}, bf16[128,1024]{1,0:T(8,128)(2,1)S(1)}, u32[]{:S(2)}, u32[]{:S(2)}) %collective-permute-start.7) | collective-permute-done | bytes 262176 | tf_op jit(solution)/shard_map/ppermute | solution.py:29
  96.7 3.8 %shard_map.72 = (bf16[512,1024]{1,0:T(8,128)(2,1)}, bf16[128,1024]{1,0:T(8,128)(2,1)S(1)}) custom-call(s32[1]{0:T(128)} %bitcast.here_ref, bf16[512,1152]{1,0:T(8,128)(2,1)S(1)} %copy-done.22, bf16[128,1024]{1,0:T(8,128)(2,1)S(1)} %collective-permute-done.2.low_ref, bf16[512,1024]{1,0:T(8,128)(2,1)S(1)} %bitcast.11, ...), custom_call_target="tpu_custom_call" | custom-call | flops 4600000000 | bytes 6291456 | tf_op jit(solution)/shard_map/pallas_call | solution.py:287
  100.5 2.8 %collective-permute-start.8 = (bf16[512,1024]{1,0:T(8,128)(2,1)}, bf16[512,1024]{1,0:T(8,128)(2,1)}, u32[]{:S(2)}, u32[]{:S(2)}) collective-permute-start(bf16[512,1024]{1,0:T(8,128)(2,1)} %get-tuple-element.32.own_ref.r_ref), channel_id=1, source_target_pairs={{0,4},{1,5},{2,6},{3,7},{4,8},{5,9},{6,10},{7,11},{8,12},{9,13},{1... | collective-permute-start | bytes 3145736 | tf_op jit(solution)/shard_map/ppermute | solution.py:24
  103.4 2.5 %shard_map.76 = bf16[512,1024]{1,0:T(8,128)(2,1)S(1)} custom-call(bf16[512,1152]{1,0:T(8,128)(2,1)S(1)} %copy-done.19, bf16[512,1024]{1,0:T(8,128)(2,1)S(1)} %collective-permute-done.15.low_ref, bf16[512,1024]{1,0:T(8,128)(2,1)S(1)} %get-tuple-element.38.own_ref.r_ref, bf16[128,1024]{1,0:T(8,128)(2,1)S(1)} %collective-permute-done.16.high_ref), custom_call_target="tpu_custom_call" | custom-call | flops 4600000000 | bytes 6291456 | tf_op jit(solution)/shard_map/pallas_call | solution.py:341
  106.9 4.7 %all-to-all-start.3 = ((bf16[4,128,1024]{2,1,0:T(8,128)(2,1)}), bf16[4,128,1024]{2,1,0:T(8,128)(2,1)S(1)}, u32[]{:S(2)}, u32[]{:S(2)}) async-start(bf16[4,128,1024]{2,1,0:T(8,128)(2,1)} %bitcast.13), calls=%async_computation.3 | async-start | bytes 2097152 | tf_op jit(solution)/shard_map/all_to_all | solution.py:35
  111.6 1.3 collective-permute-start.9
  112.9 1.2 copy-done.10
  116.8 1.9 %collective-permute-start.21 = (bf16[128,1024]{1,0:T(8,128)(2,1)}, bf16[128,1024]{1,0:T(8,128)(2,1)}, u32[]{:S(2)}, u32[]{:S(2)}) collective-permute-start(bf16[128,1024]{1,0:T(8,128)(2,1)} %get-tuple-element.47), channel_id=1, source_target_pairs={{0,2},{1,3},{2,0},{3,1},{4,6},{5,7},{6,4},{7,5},{8,10},{9,11},{10,... | collective-permute-start | bytes 786440 | tf_op jit(solution)/shard_map/ppermute | solution.py:29
  118.9 3.6 %collective-permute-done.9.high_ref = bf16[128,1024]{1,0:T(8,128)(2,1)S(1)} collective-permute-done((bf16[128,1024]{1,0:T(8,128)(2,1)}, bf16[128,1024]{1,0:T(8,128)(2,1)S(1)}, u32[]{:S(2)}, u32[]{:S(2)}) %collective-permute-start.9) | collective-permute-done | bytes 262176 | tf_op jit(solution)/shard_map/ppermute | solution.py:24
  122.5 3.2 %collective-permute-done.8.low_ref = bf16[512,1024]{1,0:T(8,128)(2,1)} collective-permute-done((bf16[512,1024]{1,0:T(8,128)(2,1)}, bf16[512,1024]{1,0:T(8,128)(2,1)}, u32[]{:S(2)}, u32[]{:S(2)}) %collective-permute-start.8) | collective-permute-done | bytes 1048608 | tf_op jit(solution)/shard_map/ppermute | solution.py:24
  125.7 3.7 %shard_map.73 = bf16[512,1024]{1,0:T(8,128)(2,1)S(1)} custom-call(bf16[512,1152]{1,0:T(8,128)(2,1)S(1)} %copy-done.20, bf16[512,1024]{1,0:T(8,128)(2,1)} %collective-permute-done.8.low_ref, bf16[512,1024]{1,0:T(8,128)(2,1)} %get-tuple-element.32.own_ref.r_ref, bf16[128,1024]{1,0:T(8,128)(2,1)S(1)} %collective-permute-done.9.high_ref), custom_call_target="tpu_custom_call" | custom-call | flops 4600000000 | bytes 6291456 | tf_op jit(solution)/shard_map/pallas_call | solution.py:341
  131.1 5.1 %all-to-all-start.1 = ((bf16[4,128,1024]{2,1,0:T(8,128)(2,1)}), bf16[4,128,1024]{2,1,0:T(8,128)(2,1)}, u32[]{:S(2)}, u32[]{:S(2)}) async-start(bf16[4,128,1024]{2,1,0:T(8,128)(2,1)} %bitcast.12), calls=%async_computation.1 | async-start | bytes 2097152 | tf_op jit(solution)/shard_map/all_to_all | solution.py:35
  137.2 1.3 shard_map.79
  138.7 1.7 collective-permute-start.18
  141.6 2.0 %copy-done.7 = f32[8,128,1024]{2,1,0:T(8,128)} copy-done((f32[8,128,1024]{2,1,0:T(8,128)}, f32[8,128,1024]{2,1,0:T(8,128)S(1)}, u32[]{:S(2)}) %copy-start.7) | copy-done | bytes 4194328
  143.6 11.9 %collective-permute-done.18.refs_2_ = bf16[128,1024]{1,0:T(8,128)(2,1)S(1)} collective-permute-done((bf16[128,1024]{1,0:T(8,128)(2,1)S(1)}, bf16[128,1024]{1,0:T(8,128)(2,1)S(1)}, u32[]{:S(2)}, u32[]{:S(2)}) %collective-permute-start.18) | collective-permute-done | bytes 262176 | tf_op jit(solution)/shard_map/ppermute | solution.py:29
  155.5 5.8 %collective-permute-done.19.refs_3_ = bf16[128,1024]{1,0:T(8,128)(2,1)S(1)} collective-permute-done((bf16[128,1024]{1,0:T(8,128)(2,1)S(1)}, bf16[128,1024]{1,0:T(8,128)(2,1)S(1)}, u32[]{:S(2)}, u32[]{:S(2)}) %collective-permute-start.19) | collective-permute-done | bytes 262176 | tf_op jit(solution)/shard_map/ppermute | solution.py:29
  161.3 5.5 %shard_map.81 = bf16[128,8,1024]{2,1,0:T(8,128)(2,1)} custom-call(s32[1]{0:T(128)} %bitcast.here_ref, bf16[128,1024]{1,0:T(8,128)(2,1)S(1)} %get-tuple-element.41.refs_0_, bf16[128,1024]{1,0:T(8,128)(2,1)S(1)} %collective-permute-done.17.refs_1_, bf16[128,1024]{1,0:T(8,128)(2,1)S(1)} %collective-permute-done.18.refs_2_, ...), custom_call_target="tpu_custom_call" | custom-call | flops 4600000000 | bytes 4194304 | tf_op jit(solution)/shard_map/pallas_call | solution.py:181
  166.8 2.2 %copy-done.8 = f32[8,128,1024]{2,1,0:T(8,128)S(1)} copy-done((f32[8,128,1024]{2,1,0:T(8,128)S(1)}, f32[8,128,1024]{2,1,0:T(8,128)}, u32[]{:S(2)}) %copy-start.8) | copy-done | bytes 4194328
  169.0 2.2 %copy-done.17 = f32[128,8,1024]{2,1,0:T(8,128)S(1)} copy-done((f32[128,8,1024]{2,1,0:T(8,128)S(1)}, f32[128,8,1024]{2,1,0:T(8,128)}, u32[]{:S(2)}) %copy-start.17) | copy-done | bytes 4194328
  171.2 6.5 %shard_map.78 = f32[128,8,1024]{2,1,0:T(8,128)} custom-call(s32[1]{0:T(128)} %bitcast.here_ref, f32[128,8,1024]{2,1,0:T(8,128)S(1)} %copy-done.17, bf16[4,128,1024]{2,1,0:T(8,128)(2,1)} %all-to-all-done.1.b0_ref, bf16[4,128,1024]{2,1,0:T(8,128)(2,1)S(1)} %all-to-all-done.3.b1_ref, f32[8,128,1024]{2,1,0:T(8,128)S(1)} %copy-done.8), custom_call_target="tpu_custom_call" | custom-call | flops 5750000128 | bytes 10485760 | tf_op jit(solution)/shard_map/pallas_call | solution.py:216
  (79 shorter events, 13.0 us)
Async XLA Ops:
  0.6 49.3 %collective-permute-start.4 = (bf16[128,8,1024]{2,1,0:T(8,128)(2,1)}, bf16[128,8,1024]{2,1,0:T(8,128)(2,1)}, u32[]{:S(2)}, u32[]{:S(2)}) collective-permute-start(bf16[128,8,1024]{2,1,0:T(8,128)(2,1)} %sino_ref.1), channel_id=1, source_target_pairs={{3,7},{7,11},{11,15},{19,23},{23,27},{27,31}} | collective-permute-start | bytes 6291464 | tf_op jit(solution)/shard_map/ppermute | solution.py:24
  2.6 2.2 %copy-start.4 = (f32[128,8,1024]{2,1,0:T(8,128)S(1)}, f32[128,8,1024]{2,1,0:T(8,128)}, u32[]{:S(2)}) copy-start(f32[128,8,1024]{2,1,0:T(8,128)} %vol_ref.1) | copy-start | bytes 12582916
  8.2 20.7 %all-to-all-start.2 = ((bf16[4,128,1024]{2,1,0:T(8,128)(2,1)}), bf16[4,128,1024]{2,1,0:T(8,128)(2,1)}, u32[]{:S(2)}, u32[]{:S(2)}) async-start(bf16[4,128,1024]{2,1,0:T(8,128)(2,1)} %shard_map.74.v1_ref), calls=%async_computation.2 | async-start | bytes 2097152 | tf_op jit(solution)/shard_map/all_to_all | solution.py:35
  14.4 2.2 %copy-start.5 = (f32[128,8,1024]{2,1,0:T(8,128)S(1)}, f32[128,8,1024]{2,1,0:T(8,128)}, u32[]{:S(2)}) copy-start(f32[128,8,1024]{2,1,0:T(8,128)} %vol_ref.1) | copy-start | bytes 12582916
  20.0 18.7 %copy-start.25 = (s32[16,6]{0,1:T(8,128)S(1)}, s32[16,6]{0,1:T(8,128)}, u32[]{:S(2)}) copy-start(s32[16,6]{0,1:T(8,128)} %param.8) | copy-start | bytes 1156
  20.0 18.8 %copy-start.26 = (s32[16,6]{0,1:T(8,128)S(1)}, s32[16,6]{0,1:T(8,128)}, u32[]{:S(2)}) copy-start(s32[16,6]{0,1:T(8,128)} %param.9) | copy-start | bytes 1156
  20.0 18.9 %copy-start.3 = (bf16[8,128,128]{2,1,0:T(8,128)(2,1)S(1)}, bf16[8,128,128]{2,1,0:T(8,128)(2,1)}, u32[]{:S(2)}) copy-start(bf16[8,128,128]{2,1,0:T(8,128)(2,1)} %w_ref.3) | copy-start | bytes 786436
  28.9 21.1 %all-to-all-start = ((bf16[4,128,1024]{2,1,0:T(8,128)(2,1)}), bf16[4,128,1024]{2,1,0:T(8,128)(2,1)S(1)}, u32[]{:S(2)}, u32[]{:S(2)}) async-start(bf16[4,128,1024]{2,1,0:T(8,128)(2,1)} %shard_map.70.v0_ref), calls=%async_computation | async-start | bytes 2097152 | tf_op jit(solution)/shard_map/all_to_all | solution.py:35
  33.2 23.7 %collective-permute-start = (f32[1,8,1024]{2,1,0:T(8,128)S(1)}, f32[1,8,1024]{2,1,0:T(8,128)S(1)}, u32[]{:S(2)}, u32[]{:S(2)}) collective-permute-start(f32[1,8,1024]{2,1,0:T(8,128)S(1)} %get-tuple-element.51), channel_id=1, source_target_pairs={{0,1},{1,2},{2,3},{3,4},{4,5},{5,6},{6,7},{7,8},{8,9},{9,10},{10,1... | collective-permute-start | bytes 98312 | tf_op jit(solution)/shard_map/ppermute | solution.py:24
  36.8 21.3 %collective-permute-start.1 = (f32[1,8,1024]{2,1,0:T(8,128)S(1)}, f32[1,8,1024]{2,1,0:T(8,128)S(1)}, u32[]{:S(2)}, u32[]{:S(2)}) collective-permute-start(f32[1,8,1024]{2,1,0:T(8,128)S(1)} %get-tuple-element.50), channel_id=1, source_target_pairs={{1,0},{2,1},{3,2},{4,3},{5,4},{6,5},{7,6},{8,7},{9,8},{10,9},{11,1... | collective-permute-start | bytes 98312 | tf_op jit(solution)/shard_map/ppermute | solution.py:24
  38.9 12.6 %copy-start = (bf16[128,8,1024]{2,1,0:T(8,128)(2,1)S(1)}, bf16[128,8,1024]{2,1,0:T(8,128)(2,1)}, u32[]{:S(2)}) copy-start(bf16[128,8,1024]{2,1,0:T(8,128)(2,1)} %sino_ref.1) | copy-start | bytes 6291460
  40.2 1.0 copy-start.18
  41.2 1.0 copy-start.21
  42.2 26.4 %collective-permute-start.11 = (bf16[512,1024]{1,0:T(8,128)(2,1)}, bf16[512,1024]{1,0:T(8,128)(2,1)}, u32[]{:S(2)}, u32[]{:S(2)}) collective-permute-start(bf16[512,1024]{1,0:T(8,128)(2,1)} %bitcast.6.own_ref), channel_id=1, source_target_pairs={{4,0},{5,1},{6,2},{7,3},{8,4},{9,5},{10,6},{11,7},{12,8},{13,9},{1... | collective-permute-start | bytes 3145736 | tf_op jit(solution)/shard_map/ppermute | solution.py:24
  45.2 14.2 %collective-permute-start.10 = (bf16[128,1024]{1,0:T(8,128)(2,1)}, bf16[128,1024]{1,0:T(8,128)(2,1)}, u32[]{:S(2)}, u32[]{:S(2)}) collective-permute-start(bf16[128,1024]{1,0:T(8,128)(2,1)} %slice_bitcast_fusion), channel_id=1, source_target_pairs={{0,4},{1,5},{2,6},{3,7},{4,8},{5,9},{6,10},{7,11},{8,12},{9,13},{1... | collective-permute-start | bytes 786440 | tf_op jit(solution)/shard_map/ppermute | solution.py:24
  49.9 9.9 %copy-start.6 = (f32[128,8,1024]{2,1,0:T(8,128)S(1)}, f32[128,8,1024]{2,1,0:T(8,128)}, u32[]{:S(2)}) copy-start(f32[128,8,1024]{2,1,0:T(8,128)} %vol_ref.1) | copy-start | bytes 12582916
  49.9 41.1 %collective-permute-start.3 = (bf16[512,1024]{1,0:T(8,128)(2,1)S(1)}, bf16[512,1024]{1,0:T(8,128)(2,1)S(1)}, u32[]{:S(2)}, u32[]{:S(2)}) collective-permute-start(bf16[512,1024]{1,0:T(8,128)(2,1)S(1)} %bitcast.10), channel_id=1, source_target_pairs={{4,0},{5,1},{6,2},{7,3},{8,4},{9,5},{10,6},{11,7},{12,8},{13,9},{1... | collective-permute-start | bytes 3145736 | tf_op jit(solution)/shard_map/ppermute | solution.py:24
  57.0 14.2 %collective-permute-start.12 = (bf16[128,1024]{1,0:T(8,128)(2,1)S(1)}, bf16[128,1024]{1,0:T(8,128)(2,1)S(1)}, u32[]{:S(2)}, u32[]{:S(2)}) collective-permute-start(bf16[128,1024]{1,0:T(8,128)(2,1)S(1)} %get-tuple-element.35), channel_id=1, source_target_pairs={{0,1},{1,0},{2,3},{3,2},{4,5},{5,4},{6,7},{7,6},{8,9},{9,8},{10,11... | collective-permute-start | bytes 786440 | tf_op jit(solution)/shard_map/ppermute | solution.py:29
  58.1 13.1 %collective-permute-start.13 = (bf16[128,1024]{1,0:T(8,128)(2,1)S(1)}, bf16[128,1024]{1,0:T(8,128)(2,1)S(1)}, u32[]{:S(2)}, u32[]{:S(2)}) collective-permute-start(bf16[128,1024]{1,0:T(8,128)(2,1)S(1)} %get-tuple-element.36), channel_id=1, source_target_pairs={{0,2},{1,3},{2,0},{3,1},{4,6},{5,7},{6,4},{7,5},{8,10},{9,11},{10,... | collective-permute-start | bytes 786440 | tf_op jit(solution)/shard_map/ppermute | solution.py:29
  59.4 12.6 %copy-start.22 = (bf16[512,1152]{1,0:T(8,128)(2,1)S(1)}, bf16[512,1152]{1,0:T(8,128)(2,1)}, u32[]{:S(2)}) copy-start(bf16[512,1152]{1,0:T(8,128)(2,1)} %copy-done.21) | copy-start | bytes 3538948
  59.4 12.6 %collective-permute-start.14 = (bf16[128,1024]{1,0:T(8,128)(2,1)S(1)}, bf16[128,1024]{1,0:T(8,128)(2,1)S(1)}, u32[]{:S(2)}, u32[]{:S(2)}) collective-permute-start(bf16[128,1024]{1,0:T(8,128)(2,1)S(1)} %get-tuple-element.37), channel_id=1, source_target_pairs={{0,3},{1,2},{2,1},{3,0},{4,7},{5,6},{6,5},{7,4},{8,11},{9,10},{10,... | collective-permute-start | bytes 786440 | tf_op jit(solution)/shard_map/ppermute | solution.py:29
  66.5 9.9 %copy-start.16 = (f32[128,8,1024]{2,1,0:T(8,128)}, f32[128,8,1024]{2,1,0:T(8,128)S(1)}, u32[]{:S(2)}) copy-start(f32[128,8,1024]{2,1,0:T(8,128)S(1)} %shard_map.68.refs_4_.tv_ref) | copy-start | bytes 12582916
  68.7 15.2 %collective-permute-start.2 = (bf16[128,1024]{1,0:T(8,128)(2,1)S(1)}, bf16[128,1024]{1,0:T(8,128)(2,1)S(1)}, u32[]{:S(2)}, u32[]{:S(2)}) collective-permute-start(bf16[128,1024]{1,0:T(8,128)(2,1)S(1)} %slice_bitcast_fusion.1), channel_id=1, source_target_pairs={{0,4},{1,5},{2,6},{3,7},{4,8},{5,9},{6,10},{7,11},{8,12},{9,13},{1... | collective-permute-start | bytes 786440 | tf_op jit(solution)/shard_map/ppermute | solution.py:24
  72.1 24.6 %copy-start.19 = (bf16[512,1152]{1,0:T(8,128)(2,1)S(1)}, bf16[512,1152]{1,0:T(8,128)(2,1)}, u32[]{:S(2)}) copy-start(bf16[512,1152]{1,0:T(8,128)(2,1)} %copy-done.18) | copy-start | bytes 3538948
  76.4 26.9 %copy-start.9 = (bf16[512,1024]{1,0:T(8,128)(2,1)}, bf16[512,1024]{1,0:T(8,128)(2,1)S(1)}, u32[]{:S(2)}) copy-start(bf16[512,1024]{1,0:T(8,128)(2,1)S(1)} %get-tuple-element.38.own_ref.r_ref) | copy-start | bytes 3145732
  76.4 26.9 %collective-permute-start.15 = (bf16[512,1024]{1,0:T(8,128)(2,1)S(1)}, bf16[512,1024]{1,0:T(8,128)(2,1)S(1)}, u32[]{:S(2)}, u32[]{:S(2)}) collective-permute-start(bf16[512,1024]{1,0:T(8,128)(2,1)S(1)} %get-tuple-element.38.own_ref.r_ref), channel_id=1, source_target_pairs={{0,4},{1,5},{2,6},{3,7},{4,8},{5,9},{6,10},{7,11},{8,12},{9,13},{1... | collective-permute-start | bytes 3145736 | tf_op jit(solution)/shard_map/ppermute | solution.py:24
  80.8 11.6 %collective-permute-start.5 = (bf16[128,1024]{1,0:T(8,128)(2,1)S(1)}, bf16[128,1024]{1,0:T(8,128)(2,1)S(1)}, u32[]{:S(2)}, u32[]{:S(2)}) collective-permute-start(bf16[128,1024]{1,0:T(8,128)(2,1)S(1)} %get-tuple-element.29), channel_id=1, source_target_pairs={{0,1},{1,0},{2,3},{3,2},{4,5},{5,4},{6,7},{7,6},{8,9},{9,8},{10,11... | collective-permute-start | bytes 786440 | tf_op jit(solution)/shard_map/ppermute | solution.py:29
  83.0 9.3 %collective-permute-start.6 = (bf16[128,1024]{1,0:T(8,128)(2,1)S(1)}, bf16[128,1024]{1,0:T(8,128)(2,1)S(1)}, u32[]{:S(2)}, u32[]{:S(2)}) collective-permute-start(bf16[128,1024]{1,0:T(8,128)(2,1)S(1)} %get-tuple-element.30), channel_id=1, source_target_pairs={{0,2},{1,3},{2,0},{3,1},{4,6},{5,7},{6,4},{7,5},{8,10},{9,11},{10,... | collective-permute-start | bytes 786440 | tf_op jit(solution)/shard_map/ppermute | solution.py:29
  83.8 12.9 %collective-permute-start.7 = (bf16[128,1024]{1,0:T(8,128)(2,1)S(1)}, bf16[128,1024]{1,0:T(8,128)(2,1)S(1)}, u32[]{:S(2)}, u32[]{:S(2)}) collective-permute-start(bf16[128,1024]{1,0:T(8,128)(2,1)S(1)} %get-tuple-element.31), channel_id=1, source_target_pairs={{0,3},{1,2},{2,1},{3,0},{4,7},{5,6},{6,5},{7,4},{8,11},{9,10},{10,... | collective-permute-start | bytes 786440 | tf_op jit(solution)/shard_map/ppermute | solution.py:29
  91.0 12.3 %collective-permute-start.16 = (bf16[128,1024]{1,0:T(8,128)(2,1)S(1)}, bf16[128,1024]{1,0:T(8,128)(2,1)S(1)}, u32[]{:S(2)}, u32[]{:S(2)}) collective-permute-start(bf16[128,1024]{1,0:T(8,128)(2,1)S(1)} %get-tuple-element.39), channel_id=1, source_target_pairs={{4,0},{5,1},{6,2},{7,3},{8,4},{9,5},{10,6},{11,7},{12,8},{13,9},{1... | collective-permute-start | bytes 786440 | tf_op jit(solution)/shard_map/ppermute | solution.py:24
  100.5 5.4 %copy-start.13 = (bf16[128,1024]{1,0:T(8,128)(2,1)}, bf16[128,1024]{1,0:T(8,128)(2,1)S(1)}, u32[]{:S(2)}) copy-start(bf16[128,1024]{1,0:T(8,128)(2,1)S(1)} %get-tuple-element.33) | copy-start | bytes 786436
  100.5 25.2 %collective-permute-start.8 = (bf16[512,1024]{1,0:T(8,128)(2,1)}, bf16[512,1024]{1,0:T(8,128)(2,1)}, u32[]{:S(2)}, u32[]{:S(2)}) collective-permute-start(bf16[512,1024]{1,0:T(8,128)(2,1)} %get-tuple-element.32.own_ref.r_ref), channel_id=1, source_target_pairs={{0,4},{1,5},{2,6},{3,7},{4,8},{5,9},{6,10},{7,11},{8,12},{9,13},{1... | collective-permute-start | bytes 3145736 | tf_op jit(solution)/shard_map/ppermute | solution.py:24
  103.3 2.5 %copy-start.11 = (bf16[128,1024]{1,0:T(8,128)(2,1)}, bf16[128,1024]{1,0:T(8,128)(2,1)S(1)}, u32[]{:S(2)}) copy-start(bf16[128,1024]{1,0:T(8,128)(2,1)S(1)} %collective-permute-done.16.high_ref) | copy-start | bytes 786436
  106.9 24.3 %all-to-all-start.3 = ((bf16[4,128,1024]{2,1,0:T(8,128)(2,1)}), bf16[4,128,1024]{2,1,0:T(8,128)(2,1)S(1)}, u32[]{:S(2)}, u32[]{:S(2)}) async-start(bf16[4,128,1024]{2,1,0:T(8,128)(2,1)} %bitcast.13), calls=%async_computation.3 | async-start | bytes 2097152 | tf_op jit(solution)/shard_map/all_to_all | solution.py:35
  111.6 10.9 %collective-permute-start.9 = (bf16[128,1024]{1,0:T(8,128)(2,1)}, bf16[128,1024]{1,0:T(8,128)(2,1)S(1)}, u32[]{:S(2)}, u32[]{:S(2)}) collective-permute-start(bf16[128,1024]{1,0:T(8,128)(2,1)} %copy-done.13), channel_id=1, source_target_pairs={{4,0},{5,1},{6,2},{7,3},{8,4},{9,5},{10,6},{11,7},{12,8},{13,9},{1... | collective-permute-start | bytes 786440 | tf_op jit(solution)/shard_map/ppermute | solution.py:24
  112.9 1.2 copy-start.10
  115.0 10.7 %copy-start.20 = (bf16[512,1152]{1,0:T(8,128)(2,1)S(1)}, bf16[512,1152]{1,0:T(8,128)(2,1)}, u32[]{:S(2)}) copy-start(bf16[512,1152]{1,0:T(8,128)(2,1)} %copy-done.18) | copy-start | bytes 3538948
  116.8 23.6 %collective-permute-start.20 = (bf16[128,1024]{1,0:T(8,128)(2,1)}, bf16[128,1024]{1,0:T(8,128)(2,1)}, u32[]{:S(2)}, u32[]{:S(2)}) collective-permute-start(bf16[128,1024]{1,0:T(8,128)(2,1)} %get-tuple-element.46), channel_id=1, source_target_pairs={{0,1},{1,0},{2,3},{3,2},{4,5},{5,4},{6,7},{7,6},{8,9},{9,8},{10,11... | collective-permute-start | bytes 786440 | tf_op jit(solution)/shard_map/ppermute | solution.py:29
  116.8 26.7 %collective-permute-start.21 = (bf16[128,1024]{1,0:T(8,128)(2,1)}, bf16[128,1024]{1,0:T(8,128)(2,1)}, u32[]{:S(2)}, u32[]{:S(2)}) collective-permute-start(bf16[128,1024]{1,0:T(8,128)(2,1)} %get-tuple-element.47), channel_id=1, source_target_pairs={{0,2},{1,3},{2,0},{3,1},{4,6},{5,7},{6,4},{7,5},{8,10},{9,11},{10,... | collective-permute-start | bytes 786440 | tf_op jit(solution)/shard_map/ppermute | solution.py:29
  118.7 24.9 %collective-permute-start.22 = (bf16[128,1024]{1,0:T(8,128)(2,1)}, bf16[128,1024]{1,0:T(8,128)(2,1)}, u32[]{:S(2)}, u32[]{:S(2)}) collective-permute-start(bf16[128,1024]{1,0:T(8,128)(2,1)} %get-tuple-element.48), channel_id=1, source_target_pairs={{0,3},{1,2},{2,1},{3,0},{4,7},{5,6},{6,5},{7,4},{8,11},{9,10},{10,... | collective-permute-start | bytes 786440 | tf_op jit(solution)/shard_map/ppermute | solution.py:29
  131.1 35.7 %all-to-all-start.1 = ((bf16[4,128,1024]{2,1,0:T(8,128)(2,1)}), bf16[4,128,1024]{2,1,0:T(8,128)(2,1)}, u32[]{:S(2)}, u32[]{:S(2)}) async-start(bf16[4,128,1024]{2,1,0:T(8,128)(2,1)} %bitcast.12), calls=%async_computation.1 | async-start | bytes 2097152 | tf_op jit(solution)/shard_map/all_to_all | solution.py:35
  138.6 5.0 %collective-permute-start.17 = (bf16[128,1024]{1,0:T(8,128)(2,1)S(1)}, bf16[128,1024]{1,0:T(8,128)(2,1)S(1)}, u32[]{:S(2)}, u32[]{:S(2)}) collective-permute-start(bf16[128,1024]{1,0:T(8,128)(2,1)S(1)} %get-tuple-element.42), channel_id=1, source_target_pairs={{0,1},{1,0},{2,3},{3,2},{4,5},{5,4},{6,7},{7,6},{8,9},{9,8},{10,11... | collective-permute-start | bytes 786440 | tf_op jit(solution)/shard_map/ppermute | solution.py:29
  138.7 16.8 %collective-permute-start.18 = (bf16[128,1024]{1,0:T(8,128)(2,1)S(1)}, bf16[128,1024]{1,0:T(8,128)(2,1)S(1)}, u32[]{:S(2)}, u32[]{:S(2)}) collective-permute-start(bf16[128,1024]{1,0:T(8,128)(2,1)S(1)} %get-tuple-element.43), channel_id=1, source_target_pairs={{0,2},{1,3},{2,0},{3,1},{4,6},{5,7},{6,4},{7,5},{8,10},{9,11},{10,... | collective-permute-start | bytes 786440 | tf_op jit(solution)/shard_map/ppermute | solution.py:29
  140.4 20.9 %copy-start.24 = (bf16[128,1024]{1,0:T(8,128)(2,1)S(1)}, bf16[128,1024]{1,0:T(8,128)(2,1)}, u32[]{:S(2)}) copy-start(bf16[128,1024]{1,0:T(8,128)(2,1)} %copy-done.23) | copy-start | bytes 786436
  140.4 20.9 %collective-permute-start.19 = (bf16[128,1024]{1,0:T(8,128)(2,1)S(1)}, bf16[128,1024]{1,0:T(8,128)(2,1)S(1)}, u32[]{:S(2)}, u32[]{:S(2)}) collective-permute-start(bf16[128,1024]{1,0:T(8,128)(2,1)S(1)} %get-tuple-element.44), channel_id=1, source_target_pairs={{0,3},{1,2},{2,1},{3,0},{4,7},{5,6},{6,5},{7,4},{8,11},{9,10},{10,... | collective-permute-start | bytes 786440 | tf_op jit(solution)/shard_map/ppermute | solution.py:29
  141.6 2.0 %copy-start.7 = (f32[8,128,1024]{2,1,0:T(8,128)}, f32[8,128,1024]{2,1,0:T(8,128)S(1)}, u32[]{:S(2)}) copy-start(f32[8,128,1024]{2,1,0:T(8,128)S(1)} %get-tuple-element.40.last_ref) | copy-start | bytes 12582916
  166.8 2.2 %copy-start.8 = (f32[8,128,1024]{2,1,0:T(8,128)S(1)}, f32[8,128,1024]{2,1,0:T(8,128)}, u32[]{:S(2)}) copy-start(f32[8,128,1024]{2,1,0:T(8,128)} %copy-done.7) | copy-start | bytes 12582916
  169.0 2.2 %copy-start.17 = (f32[128,8,1024]{2,1,0:T(8,128)S(1)}, f32[128,8,1024]{2,1,0:T(8,128)}, u32[]{:S(2)}) copy-start(f32[128,8,1024]{2,1,0:T(8,128)} %copy-done.16) | copy-start | bytes 12582916
  (6 other events, 5.3 us)

commit v3 on v2

v3 whole, which is shorter than its diff:
```python
import functools

import jax
import jax.numpy as jnp
from jax import lax
from jax.experimental import pallas as pl
from jax.experimental.pallas import tpu as pltpu
from jax.sharding import PartitionSpec as P

G = 4
CHUNKS = 2
F32 = jnp.float32
BF16 = jnp.bfloat16
MIB = 1024 * 1024
LANES = 128
SMEM = pl.BlockSpec(memory_space=pltpu.SMEM)
VMEM = pl.BlockSpec(memory_space=pltpu.VMEM)
ANY = pl.BlockSpec(memory_space=pl.ANY)


def moved(value, steps, only=None):
    count = lax.axis_size("slab")
    first, last = max(0, -steps), min(count, count - steps)
    pairs = [(i, i + steps) for i in range(first, last) if only is None or i % G == only]
    return lax.ppermute(value, "slab", pairs)


def swapped(value, bits):
    count = lax.axis_size("slab")
    return lax.ppermute(value, "slab", [(i, i ^ bits) for i in range(count)])


def dealt_out(blocks):
    got = {m: swapped(blocks[m], m) for m in reversed(range(1, G))}
    return [blocks[0]] + [got[m] for m in range(1, G)]


def exchanged(array):
    count = lax.axis_size("slab")
    sets = [list(range(first, first + G)) for first in range(0, count, G)]
    return lax.all_to_all(array, "slab", 0, 0, axis_index_groups=sets, tiled=True)


def call(kernel, *, results, vmem=16, **how):
    return pl.pallas_call(
        kernel,
        out_shape=results,
        compiler_params=pltpu.CompilerParams(vmem_limit_bytes=vmem * MIB),
        cost_estimate=pl.CostEstimate(flops=1000, bytes_accessed=1000, transcendentals=0),
        **how,
    )


def value(shape, dtype):
    return jax.ShapeDtypeStruct(shape, dtype)


def far(array):
    return pltpu.with_memory_space_constraint(array, pltpu.HBM)


def across(shape, tile):
    block = shape[:-1] + (tile,)
    return pl.BlockSpec(block, lambda i: (0,) * (len(shape) - 1) + (i,))


def lanes(array, tile, parts):
    block = array.shape[:-1] + (tile,)
    zeros = (0,) * (len(block) - 1)
    return [pl.BlockSpec(block, lambda i, j=j: zeros + (i * parts + j,)) for j in range(parts)]


def row_of(place, m, chunk):
    return CHUNKS * jnp.bitwise_xor(place, m) + chunk


def cast_kernel(chunk, parts, *refs):
    vol_refs, out_ref = refs[:parts], refs[-1]
    depth = out_ref.shape[1]
    for j, vol_ref in enumerate(vol_refs):
        for p in range(G):
            spot = pl.ds(CHUNKS * p + chunk, depth, stride=CHUNKS * G)
            out_ref[p, :, j * LANES : (j + 1) * LANES] = vol_ref[spot, :].astype(BF16)


def cast_rows(volume, chunk, *tokens):
    depth, rows, cols = volume.shape
    flat = far(volume.reshape(depth * rows, cols))
    parts = 4
    return call(
        functools.partial(cast_kernel, chunk, parts),
        grid=(cols // (LANES * parts),),
        in_specs=lanes(flat, LANES, parts) + [ANY] * len(tokens),
        out_specs=across((G, depth, cols), LANES * parts),
        results=value((G, depth, cols), BF16),
    )(*[flat] * parts, *tokens)


def split_kernel(here_ref, own_ref, got_ref, *refs):
    out_refs, wide = refs[:-1], refs[-1]
    depth, rows, cols = own_ref.shape
    place = lax.rem(here_ref[0], G)

    def fill(ref):
        for j in range(cols // LANES):
            wide[j] = ref[:, :, j * LANES : (j + 1) * LANES].astype(F32).reshape(wide.shape[1:])

    @pl.when(place == G - 1)
    def _():
        fill(got_ref)

    @pl.when(place != G - 1)
    def _():
        fill(own_ref)

    for j in range(cols // LANES):
        at = pl.ds(j * LANES, LANES)
        for c in range(CHUNKS):
            for m in range(G):
                spot = pl.ds(row_of(place, m, c), depth, stride=rows)
                out_refs[c * G + m][:, at] = wide.at[j][spot, :].astype(BF16)


def split_rows(here, own, got):
    depth, rows, cols = own.shape
    tile = 512
    block = across(own.shape, tile)
    return call(
        split_kernel,
        grid=(cols // tile,),
        in_specs=[SMEM, block, block],
        out_specs=[across((depth, cols), tile)] * (CHUNKS * G),
        results=[value((depth, cols), BF16)] * (CHUNKS * G),
        scratch_shapes=[pltpu.VMEM((tile // LANES, depth * rows, LANES), F32)],
    )(here, far(own), got)


def last_kernel(slabs, here_ref, cover_ref, offset_ref, w_ref, *refs):
    v_refs, (sino_ref, r_ref, b_ref, v, s, r, b, wide) = refs[:CHUNKS], refs[CHUNKS:]
    depth, rows, cols = sino_ref.shape

    @pl.when(here_ref[0] == slabs - 1)
    def _():
        for i, v_ref in enumerate(v_refs):
            pltpu.sync_copy(v_ref, v.at[i])
        pltpu.sync_copy(sino_ref, s)
        block = w_ref[offset_ref[slabs - 1, 0]]
        block = jnp.where(cover_ref[slabs - 1, 0] == 1, block, jnp.zeros_like(block))
        turned = block.astype(F32).T.astype(BF16)

        def column(j, _):
            at = pl.ds(pl.multiple_of(j * LANES, LANES), LANES)
            wide[...] = s[:, :, at].astype(F32).reshape(wide.shape)
            for c in range(CHUNKS):
                for p in range(G):
                    row = CHUNKS * p + c
                    seen = jnp.dot(block, v[c, p, :, at], preferred_element_type=F32)
                    resid = (seen - wide[pl.ds(row, depth, stride=rows), :]).astype(BF16)
                    r[row, :, at] = resid
                    b[row, :, at] = jnp.dot(turned, resid, preferred_element_type=F32)
            return 0

        lax.fori_loop(0, cols // LANES, column, 0)
        pltpu.sync_copy(r, r_ref)
        pltpu.sync_copy(b, b_ref)


def last_group(here, coverage, offsets, weights, vols, sinogram):
    slabs = coverage.shape[0]
    depth, rows, cols = sinogram.shape
    return call(
        functools.partial(last_kernel, slabs),
        in_specs=[SMEM, SMEM, SMEM, VMEM] + [ANY] * (CHUNKS + 1),
        out_specs=[ANY, ANY],
        results=[pltpu.HBM((rows, depth, cols), BF16), pltpu.HBM((rows, depth, cols), F32)],
        scratch_shapes=[
            pltpu.VMEM((CHUNKS, G, depth, cols), BF16),
            pltpu.VMEM(sinogram.shape, BF16),
            pltpu.VMEM((rows, depth, cols), BF16),
            pltpu.VMEM((rows, depth, cols), F32),
            pltpu.VMEM((depth * rows, LANES), F32),
        ],
    )(here, coverage, offsets, weights, *vols, far(sinogram))


def join_kernel(slabs, here_ref, *refs):
    in_refs, (last_ref, out_ref, wide, held) = refs[: CHUNKS * G], refs[CHUNKS * G :]
    depth, rows, cols = out_ref.shape
    place = lax.rem(here_ref[0], G)
    last = here_ref[0] == slabs - 1

    @pl.when(last)
    def _():
        at = pl.ds(pl.multiple_of(pl.program_id(0) * cols, cols), cols)
        pltpu.sync_copy(last_ref.at[:, :, at], held)
        for j in range(cols // LANES):
            for row in range(rows):
                value = held[row, :, j * LANES : (j + 1) * LANES].astype(F32)
                wide.at[j][pl.ds(row, depth, stride=rows), :] = value

    @pl.when(jnp.logical_not(last))
    def _():
        for j in range(cols // LANES):
            at = pl.ds(j * LANES, LANES)
            for c in range(CHUNKS):
                for m in range(G):
                    spot = pl.ds(row_of(place, m, c), depth, stride=rows)
                    wide.at[j][spot, :] = in_refs[c * G + m][:, at].astype(F32)

    for j in range(cols // LANES):
        out_ref[:, :, j * LANES : (j + 1) * LANES] = wide[j].reshape(depth, rows, LANES).astype(out_ref.dtype)


def join_rows(here, slabs, blocks, last):
    rows, depth, cols = last.shape
    tile = 512
    return call(
        functools.partial(join_kernel, slabs),
        grid=(cols // tile,),
        in_specs=[SMEM] + [across((depth, cols), tile)] * len(blocks) + [ANY],
        out_specs=across((depth, rows, cols), tile),
        results=value((depth, rows, cols), BF16),
        scratch_shapes=[
            pltpu.VMEM((tile // LANES, depth * rows, LANES), F32),
            pltpu.VMEM((rows, depth, tile), BF16),
        ],
    )(here, *blocks, far(last))


def finish_kernel(slabs, here_ref, tv_ref, *refs):
    in_refs, (last_ref, out_ref, wide, held) = refs[:CHUNKS], refs[CHUNKS:]
    depth, rows, cols = out_ref.shape
    for j in range(cols // LANES):
        at = pl.ds(j * LANES, LANES)
        for c in range(CHUNKS):
            for p in range(G):
                spot = pl.ds(CHUNKS * p + c, depth, stride=rows)
                wide.at[j][spot, :] = in_refs[c][p, :, at].astype(F32)

    @pl.when(here_ref[0] == slabs - 1)
    def _():
        at = pl.ds(pl.multiple_of(pl.program_id(0) * cols, cols), cols)
        pltpu.sync_copy(last_ref.at[:, :, at], held)
        for j in range(cols // LANES):
            for row in range(rows):
                spot = pl.ds(row, depth, stride=rows)
                wide.at[j][spot, :] = wide.at[j][spot, :] + held[row, :, j * LANES : (j + 1) * LANES]

    for j in range(cols // LANES):
        at = pl.ds(j * LANES, LANES)
        out_ref[:, :, at] = tv_ref[:, :, at] + wide[j].reshape(depth, rows, LANES)


def finish(here, slabs, tv, blocks, last):
    depth, rows, cols = tv.shape
    tile = 256
    whole = across(tv.shape, tile)
    return call(
        functools.partial(finish_kernel, slabs),
        grid=(cols // tile,),
        in_specs=[SMEM, whole] + [across(blocks[0].shape, tile)] * len(blocks) + [ANY],
        out_specs=whole,
        results=value((depth, rows, cols), F32),
        scratch_shapes=[
            pltpu.VMEM((tile // LANES, depth * rows, LANES), F32),
            pltpu.VMEM((rows, depth, tile), F32),
        ],
    )(here, far(tv), *blocks, far(last))


def band_kernel(slabs, span, here_ref, cover_ref, offset_ref, w_ref, proj_ref, back_ref, turned):
    side = w_ref.shape[1]
    place = lax.rem(here_ref[0], G)
    first = here_ref[0] - place
    zero = jnp.zeros((side, side), BF16)
    for i in range(w_ref.shape[0]):
        turned[i] = w_ref[i].astype(F32).T.astype(BF16)

    def block(ref, i, j):
        k = j - i
        known, step = jnp.clip(i, 0, slabs - 1), jnp.clip(k, 0, span - 1)
        inside = (i >= 0) & (i < slabs) & (j >= 0) & (j < slabs) & (k >= 0) & (k < span)
        live = inside & (cover_ref[known, step] == 1)
        return jnp.where(live, ref[offset_ref[known, step]], zero)

    def group(m):
        to = jnp.bitwise_xor(place, m)
        return first + jnp.where(to == G - 1, -1, to)

    seen = [first + s for s in range(2 * G)] + [first - 1]
    seeing = [group(m) for m in range(G)] + [group(m) - G for m in range(G)] + [first + G - 1]
    for r in range(G):
        for s in range(2 * G + 1):
            at = (pl.ds(r * side, side), pl.ds(s * side, side))
            proj_ref[at] = block(w_ref, group(r), seen[s])
            back_ref[at] = block(turned, seeing[s], first + r)


def bands(here, coverage, offsets, weights):
    slabs, span = coverage.shape
    side = weights.shape[1]
    shape = (G * side, (2 * G + 1) * side)
    return call(
        functools.partial(band_kernel, slabs, span),
        in_specs=[SMEM, SMEM, SMEM, pl.BlockSpec(weights.shape, lambda i: (0, 0, 0))],
        grid=(1,),
        out_specs=[pl.BlockSpec(shape, lambda i: (0, 0))] * 2,
        results=[value(shape, BF16)] * 2,
        scratch_shapes=[pltpu.VMEM(weights.shape, BF16)],
    )(here, coverage, offsets, weights)


def project_kernel(here_ref, band_ref, own_ref, high_ref, low_ref, *refs):
    sinos, (r_ref, down_ref) = refs[:G], refs[-2:]
    side = low_ref.shape[0]
    seen = jnp.concatenate([own_ref[...], high_ref[...], low_ref[...]], axis=0)
    total = jnp.dot(band_ref[...], seen, preferred_element_type=F32)
    for m in range(G):
        at = pl.ds(m * side, side)
        r_ref[at, :] = (total[m * side : (m + 1) * side] - sinos[m][...].astype(F32)).astype(BF16)
    spot = jnp.bitwise_xor(lax.rem(here_ref[0], G), G - 1)
    down_ref[...] = r_ref[pl.ds(pl.multiple_of(spot * side, side), side), :]


def project(here, band, own, high, low, sinos, *tokens):
    side, cols = low.shape
    tile = 512
    one = across((side, cols), tile)
    many = across(own.shape, tile)
    return call(
        project_kernel,
        grid=(cols // tile,),
        in_specs=[SMEM, pl.BlockSpec(band.shape, lambda i: (0, 0)), many, many] + [one] * (G + 1) + [ANY] * len(tokens),
        out_specs=[many, one],
        results=[value(own.shape, BF16), value((side, cols), BF16)],
    )(here, band, own, high, low, *sinos, *tokens)


def deal_kernel(here_ref, r_ref, high_ref, *out_refs):
    side = high_ref.shape[0]
    place = lax.rem(here_ref[0], G)
    for m in range(G):
        last = jnp.bitwise_xor(place, m) == G - 1
        out_refs[m][...] = jnp.where(last, high_ref[...], r_ref[m * side : (m + 1) * side])


def deal(here, resid, high):
    side, cols = high.shape
    tile = 512
    one = across((side, cols), tile)
    return call(
        deal_kernel,
        grid=(cols // tile,),
        in_specs=[SMEM, across(resid.shape, tile), one],
        out_specs=[one] * G,
        results=[value((side, cols), BF16)] * G,
    )(here, resid, high)


def back_kernel(band_ref, own_ref, low_ref, high_ref, out_ref):
    seeing = jnp.concatenate([own_ref[...], low_ref[...], high_ref[...]], axis=0)
    total = jnp.dot(band_ref[...], seeing, preferred_element_type=F32)
    out_ref[...] = total.astype(BF16).reshape(out_ref.shape)


def back(band, own, low, high):
    side, cols = high.shape
    tile = 512
    many = across(own.shape, tile)
    return call(
        back_kernel,
        grid=(cols // tile,),
        in_specs=[pl.BlockSpec(band.shape, lambda i: (0, 0)), many, many, across((side, cols), tile)],
        out_specs=across((G, side, cols), tile),
        results=value((G, side, cols), BF16),
    )(band, own, low, high)


def tv_kernel(low_ref, high_ref, next_ref, vol_ref, out_ref, flux_ref):
    step = pl.program_id(0)
    steps = pl.num_programs(0)
    deep, rows, cols = vol_ref.shape
    row = lax.broadcasted_iota(jnp.int32, (rows, cols), 0)
    col = lax.broadcasted_iota(jnp.int32, (rows, cols), 1)

    def up_y(v):
        return jnp.where(row == rows - 1, 0.0, pltpu.roll(v, rows - 1, 0))

    def up_x(v):
        return jnp.where(col == cols - 1, 0.0, pltpu.roll(v, cols - 1, 1))

    def scale_of(cur, above):
        dz = above - cur
        dy = up_y(cur) - cur
        dx = up_x(cur) - cur
        return dz, dy, dx, 0.5 * lax.rsqrt(dz * dz + dy * dy + dx * dx + 0.25)

    def edge(v):
        return 0.5 * v * lax.rsqrt(v * v + 0.25)

    @pl.when(step == 0)
    def _():
        dz, _, _, scale = scale_of(low_ref[0], vol_ref[0])
        flux_ref[...] = dz * scale

    def one(z, cur, above, below_flux):
        dz, dy, dx, scale = scale_of(cur, above)
        fz, fy, fx = dz * scale, dy * scale, dx * scale
        sides = edge(cur)
        fy_low = jnp.where(row == 0, sides, pltpu.roll(fy, 1, 0))
        fx_low = jnp.where(col == 0, sides, pltpu.roll(fx, 1, 1))
        out_ref[z] = (below_flux - fz) + (fy_low - fy) + (fx_low - fx)
        return fz

    def body(z, flux):
        return one(z, vol_ref[z], vol_ref[z + 1], flux)

    flux = lax.fori_loop(0, deep - 1, body, flux_ref[...], unroll=5)
    above = jnp.where(step == steps - 1, high_ref[0], next_ref[0])
    flux_ref[...] = one(deep - 1, vol_ref[deep - 1], above, flux)


def half_tv(volume, low, high):
    depth, rows, cols = volume.shape
    deep = 16
    steps = depth // deep
    edge = pl.BlockSpec((1, rows, cols), lambda i: (0, 0, 0))
    body = pl.BlockSpec((deep, rows, cols), lambda i: (i, 0, 0))
    after = pl.BlockSpec((1, rows, cols), lambda i: (jnp.minimum((i + 1) * deep, depth - 1), 0, 0))
    return call(
        tv_kernel,
        grid=(steps,),
        in_specs=[edge, edge, after, body],
        out_specs=body,
        results=pltpu.HBM(volume.shape, F32),
        scratch_shapes=[pltpu.VMEM((rows, cols), F32)],
    )(low, high, far(volume), far(volume))


def local(volume, sinogram, weights, coverage, offsets):
    slabs = lax.axis_size("slab")
    here = lax.axis_index("slab").astype(jnp.int32).reshape(1)
    depth, rows, cols = volume.shape

    vols0 = cast_rows(volume, 0)
    got = moved(lax.optimization_barrier((sinogram, vols0))[0], G, only=G - 1)
    own0 = exchanged(vols0)
    band_p, band_b = bands(here, coverage, offsets, weights)
    below = moved(volume[-1:], 1)
    above = moved(volume[:1], -1)
    vols1 = cast_rows(volume, 1, own0)
    own1 = exchanged(vols1)
    r_last, b_last = last_group(here, coverage, offsets, weights, [vols0, vols1], sinogram)
    sino = split_rows(here, sinogram, got)
    sinos = [dealt_out(sino[c * G : (c + 1) * G]) for c in range(CHUNKS)]
    tv = half_tv(volume, below, above)

    resid_blocks, back_rows = [], []
    for c, own in enumerate((own0, own1)):
        own = own.reshape(G * depth, cols)
        high = moved(own, -G)
        low = moved(own[(G - 1) * depth :], G)
        resid, down = project(here, band_p, own, high, low, sinos[c], *([tv] if c else []))
        r_low = moved(resid, G)
        r_high = moved(down, -G)
        resid_blocks += dealt_out(deal(here, resid, r_high))
        back_rows.append(exchanged(back(band_b, resid, r_low, r_high)))

    residual = join_rows(here, slabs, resid_blocks, r_last)
    gradient = finish(here, slabs, tv, back_rows, b_last)
    return (gradient, residual)


def solution(mesh):
    placed = (P("slab", "grp", None), P("slab", "grp", None), P(), P(), P())
    return jax.shard_map(
        local,
        mesh=mesh,
        in_specs=placed,
        out_specs=(P("slab", "grp", None), P("slab", "grp", None)),
        check_vma=False,
    )
```

time: 180 us -> 207 us (1.15)
  the two profiles are of different devices: /device:TPU:1 before, /device:TPU:29 now
where the time goes in v3:
time: 207 us; the launch traced here: 206 us
  starting transfers between devices  78.6 us (38%)
  Pallas kernels  61.3 us (30%)
  waiting for transfers between devices  34.7 us (17%)
  blocking collectives  16.7 us (8%)
  local copies, waits for them, and re-layouts  13.2 us (6%)
    ppermute x12, starting transfers between devices, swapped(): return lax.ppermute(value, 'slab', [(i, i ^ bits) for i in range(count)])  34.6 us
    ppermute x11, starting transfers between devices, moved(): return lax.ppermute(value, 'slab', pairs)  26.1 us
    ppermute x12, waiting for transfers between devices, swapped(): return lax.ppermute(value, 'slab', [(i, i ^ bits) for i in range(count)])  21.6 us
    all_to_all x3, starting transfers between devices, exchanged(): lax.all_to_all(array, 'slab', 0, 0, axis_index_groups=sets, tiled=True)  17.9 us
    all_to_all x1, blocking collectives, exchanged(): lax.all_to_all(array, 'slab', 0, 0, axis_index_groups=sets, tiled=True)  16.7 us
    ppermute x11, waiting for transfers between devices, moved(): return lax.ppermute(value, 'slab', pairs)  12.1 us
    unnamed x50, local copies, waits for them, and re-layouts  11.7 us
    pallas_call x1, Pallas kernels, finish(): call(functools.partial(finish_kernel, slabs), grid=(cols // tile,), in_sp...  10.8 us
  transfers between devices with their start and end apart: 26, of which 7 were waited for; matrix products, arithmetic and copies ran while one was open for 1% of the time, Pallas kernels for 23%

profile of v3, /device:TPU:29, one launch (start us, length us, event | category | flops | bytes accessed | tf_op | source)
XLA Modules:
  0.0 205.5 jit_solution(17020210768817376977)
XLA Ops:
  0.6 2.5 %shard_map.70.refs_0_ = bf16[4,128,1024]{2,1,0:T(8,128)(2,1)S(1)} custom-call(f32[1024,1024]{1,0:T(8,128)} %bitcast.12, f32[1024,1024]{1,0:T(8,128)} %bitcast.13, f32[1024,1024]{1,0:T(8,128)} %bitcast.14, f32[1024,1024]{1,0:T(8,128)} %bitcast.15), custom_call_target="tpu_custom_call" | custom-call | flops 1000 | bytes 1000 | tf_op jit(solution)/shard_map/pallas_call | solution.py:90
  3.2 1.3 collective-permute-start.4
  4.5 16.7 %all_to_all.20.refs_4_ = bf16[4,128,1024]{2,1,0:T(8,128)(2,1)S(1)} all-to-all(bf16[4,128,1024]{2,1,0:T(8,128)(2,1)S(1)} %shard_map.70.refs_0_), channel_id=1, replica_groups={{0,1,2,3},{4,5,6,7},{8,9,10,11},{12,13,14,15},{16,17,18,19},{20,21,22,2..., dimensions={0} | all-to-all | bytes 2097152 | tf_op jit(solution)/shard_map/all_to_all | solution.py:41
  21.2 3.7 %collective-permute-start.2 = (bf16[512,1024]{1,0:T(8,128)(2,1)S(1)}, bf16[512,1024]{1,0:T(8,128)(2,1)}, u32[]{:S(2)}, u32[]{:S(2)}) collective-permute-start(bf16[512,1024]{1,0:T(8,128)(2,1)S(1)} %bitcast.8), channel_id=1, source_target_pairs={{4,0},{5,1},{6,2},{7,3},{8,4},{9,5},{10,6},{11,7},{12,8},{13,9},{1... | collective-permute-start | bytes 3145736 | tf_op jit(solution)/shard_map/ppermute | solution.py:25
  24.9 3.2 %shard_map.74.refs_1_ = bf16[4,128,1024]{2,1,0:T(8,128)(2,1)} custom-call(f32[1024,1024]{1,0:T(8,128)} %bitcast.16, f32[1024,1024]{1,0:T(8,128)} %bitcast.17, f32[1024,1024]{1,0:T(8,128)} %bitcast.18, f32[1024,1024]{1,0:T(8,128)} %bitcast.19, bf16[4,128,1024]{2,1,0:T(8,128)(2,1)S(1)} %all_to_all.20.refs_4_), custom_call_target="tpu_custom_call" | custom-call | flops 1000 | bytes 1000 | tf_op jit(solution)/shard_map/pallas_call | solution.py:90
  28.1 5.7 %all-to-all-start.2 = ((bf16[4,128,1024]{2,1,0:T(8,128)(2,1)}), bf16[4,128,1024]{2,1,0:T(8,128)(2,1)S(1)}, u32[]{:S(2)}, u32[]{:S(2)}) async-start(bf16[4,128,1024]{2,1,0:T(8,128)(2,1)} %shard_map.74.refs_1_), calls=%async_computation.2 | async-start | bytes 2097152 | tf_op jit(solution)/shard_map/all_to_all | solution.py:41
  33.8 0.7 slice_bitcast_fusion.1
  34.5 1.3 collective-permute-start.3
  35.8 3.7 %shard_map.71 = (bf16[128,1024]{1,0:T(8,128)(2,1)S(1)}, bf16[128,1024]{1,0:T(8,128)(2,1)}, bf16[128,1024]{1,0:T(8,128)(2,1)}, bf16[128,1024]{1,0:T(8,128)(2,1)},...) custom-call(s32[1]{0:T(128)} %bitcast.here_ref, ...), custom_call_target="tpu_custom_call" | custom-call | flops 1000 | bytes 1000 | tf_op jit(solution)/shard_map/pallas_call | solution.py:128
  43.4 1.8 collective-permute-start.7
  45.2 1.1 all-to-all-done.2
  46.3 4.1 %collective-permute-start.10 = (bf16[512,1024]{1,0:T(8,128)(2,1)S(1)}, bf16[512,1024]{1,0:T(8,128)(2,1)}, u32[]{:S(2)}, u32[]{:S(2)}) collective-permute-start(bf16[512,1024]{1,0:T(8,128)(2,1)S(1)} %bitcast.10), channel_id=1, source_target_pairs={{4,0},{5,1},{6,2},{7,3},{8,4},{9,5},{10,6},{11,7},{12,8},{13,9},{1... | collective-permute-start | bytes 3145736 | tf_op jit(solution)/shard_map/ppermute | solution.py:25
  50.5 1.6 shard_map.69
  52.2 5.4 %collective-permute-done.7.refs_3_ = bf16[128,1024]{1,0:T(8,128)(2,1)} collective-permute-done((bf16[128,1024]{1,0:T(8,128)(2,1)}, bf16[128,1024]{1,0:T(8,128)(2,1)}, u32[]{:S(2)}, u32[]{:S(2)}) %collective-permute-start.7) | collective-permute-done | bytes 262176 | tf_op jit(solution)/shard_map/ppermute | solution.py:30
  57.6 0.9 copy-done.14
  58.5 3.1 %shard_map.72 = (bf16[512,1024]{1,0:T(8,128)(2,1)S(1)}, bf16[128,1024]{1,0:T(8,128)(2,1)S(1)}) custom-call(s32[1]{0:T(128)} %bitcast.here_ref, bf16[512,1152]{1,0:T(8,128)(2,1)S(1)} %get-tuple-element.28.band_ref, bf16[512,1024]{1,0:T(8,128)(2,1)S(1)} %bitcast.9, bf16[512,1024]{1,0:T(8,128)(2,1)} %collective-permute-done.2.high_ref, ...), custom_call_target="tpu_custom_call" | custom-call | flops 1000 | bytes 1000 | tf_op jit(solution)/shard_map/pallas_call | solution.py:330
  61.7 1.3 collective-permute-start.8
  63.0 1.3 collective-permute-start.11
  64.3 0.8 fusion
  65.1 1.3 collective-permute-start
  66.4 3.0 %collective-permute-start.1 = (f32[1,8,1024]{2,1,0:T(8,128)S(1)}, f32[1,8,1024]{2,1,0:T(8,128)S(1)}, u32[]{:S(2)}, u32[]{:S(2)}) collective-permute-start(f32[1,8,1024]{2,1,0:T(8,128)S(1)} %get-tuple-element.52), channel_id=1, source_target_pairs={{1,0},{2,1},{3,2},{4,3},{5,4},{6,5},{7,6},{8,7},{9,8},{10,9},{11,1... | collective-permute-start | bytes 98312 | tf_op jit(solution)/shard_map/ppermute | solution.py:25
  69.4 1.6 collective-permute-start.12
  71.0 26.3 %collective-permute-start.13 = (bf16[128,1024]{1,0:T(8,128)(2,1)S(1)}, bf16[128,1024]{1,0:T(8,128)(2,1)S(1)}, u32[]{:S(2)}, u32[]{:S(2)}) collective-permute-start(bf16[128,1024]{1,0:T(8,128)(2,1)S(1)} %copy-done.18), channel_id=1, source_target_pairs={{0,2},{1,3},{2,0},{3,1},{4,6},{5,7},{6,4},{7,5},{8,10},{9,11},{10,... | collective-permute-start | bytes 786440 | tf_op jit(solution)/shard_map/ppermute | solution.py:30
  97.4 10.0 %shard_map.68.refs_4_.tv_ref = f32[128,8,1024]{2,1,0:T(8,128)} custom-call(f32[1,8,1024]{2,1,0:T(8,128)S(1)} %collective-permute-done.low_ref, f32[1,8,1024]{2,1,0:T(8,128)S(1)} %collective-permute-done.1.high_ref, f32[128,8,1024]{2,1,0:T(8,128)} %vol_ref.1, f32[128,8,1024]{2,1,0:T(8,128)} %vol_ref.1), custom_call_target="tpu_custom_call" | custom-call | flops 1000 | bytes 1000 | tf_op jit(solution)/shard_map/pallas_call | solution.py:430
  107.4 3.3 %collective-permute-start.9 = (bf16[128,1024]{1,0:T(8,128)(2,1)S(1)}, bf16[128,1024]{1,0:T(8,128)(2,1)S(1)}, u32[]{:S(2)}, u32[]{:S(2)}) collective-permute-start(bf16[128,1024]{1,0:T(8,128)(2,1)S(1)} %get-tuple-element.35), channel_id=1, source_target_pairs={{4,0},{5,1},{6,2},{7,3},{8,4},{9,5},{10,6},{11,7},{12,8},{13,9},{1... | collective-permute-start | bytes 786440 | tf_op jit(solution)/shard_map/ppermute | solution.py:25
  110.8 2.2 %copy-done = f32[128,8,1024]{2,1,0:T(8,128)S(1)} copy-done((f32[128,8,1024]{2,1,0:T(8,128)S(1)}, f32[128,8,1024]{2,1,0:T(8,128)}, u32[]{:S(2)}) %copy-start) | copy-done | bytes 4194328
  113.0 3.6 %shard_map.75 = (bf16[512,1024]{1,0:T(8,128)(2,1)}, bf16[128,1024]{1,0:T(8,128)(2,1)S(1)}) custom-call(s32[1]{0:T(128)} %bitcast.here_ref, bf16[512,1152]{1,0:T(8,128)(2,1)S(1)} %get-tuple-element.28.band_ref, bf16[512,1024]{1,0:T(8,128)(2,1)S(1)} %bitcast.11, bf16[512,1024]{1,0:T(8,128)(2,1)} %collective-permute-done.10.high_ref, ...), custom_call_target="tpu_custom_call" | custom-call | flops 1000 | bytes 1000 | tf_op jit(solution)/shard_map/pallas_call | solution.py:330
  116.7 1.3 collective-permute-start.15
  118.0 2.0 shard_map.73
  120.0 1.0 copy-done.6
  120.9 5.6 %all-to-all-start.1 = ((bf16[4,128,1024]{2,1,0:T(8,128)(2,1)}), bf16[4,128,1024]{2,1,0:T(8,128)(2,1)S(1)}, u32[]{:S(2)}, u32[]{:S(2)}) async-start(bf16[4,128,1024]{2,1,0:T(8,128)(2,1)} %copy-done.6), calls=%async_computation.1 | async-start | bytes 2097152 | tf_op jit(solution)/shard_map/all_to_all | solution.py:41
  126.6 4.3 %collective-permute-start.16 = (bf16[128,1024]{1,0:T(8,128)(2,1)}, bf16[128,1024]{1,0:T(8,128)(2,1)S(1)}, u32[]{:S(2)}, u32[]{:S(2)}) collective-permute-start(bf16[128,1024]{1,0:T(8,128)(2,1)} %copy-done.21), channel_id=1, source_target_pairs={{4,0},{5,1},{6,2},{7,3},{8,4},{9,5},{10,6},{11,7},{12,8},{13,9},{1... | collective-permute-start | bytes 786440 | tf_op jit(solution)/shard_map/ppermute | solution.py:25
  130.9 5.6 %collective-permute-done.16.high_ref = bf16[128,1024]{1,0:T(8,128)(2,1)S(1)} collective-permute-done((bf16[128,1024]{1,0:T(8,128)(2,1)}, bf16[128,1024]{1,0:T(8,128)(2,1)S(1)}, u32[]{:S(2)}, u32[]{:S(2)}) %collective-permute-start.16) | collective-permute-done | bytes 262176 | tf_op jit(solution)/shard_map/ppermute | solution.py:25
  136.5 6.4 %collective-permute-done.15.low_ref = bf16[512,1024]{1,0:T(8,128)(2,1)} collective-permute-done((bf16[512,1024]{1,0:T(8,128)(2,1)}, bf16[512,1024]{1,0:T(8,128)(2,1)}, u32[]{:S(2)}, u32[]{:S(2)}) %collective-permute-start.15) | collective-permute-done | bytes 1048608 | tf_op jit(solution)/shard_map/ppermute | solution.py:25
  142.9 3.0 %shard_map.76 = bf16[4,128,1024]{2,1,0:T(8,128)(2,1)S(1)} custom-call(bf16[512,1152]{1,0:T(8,128)(2,1)S(1)} %copy-done.2, bf16[512,1024]{1,0:T(8,128)(2,1)} %get-tuple-element.40.own_ref.r_ref, bf16[512,1024]{1,0:T(8,128)(2,1)} %collective-permute-done.15.low_ref, bf16[128,1024]{1,0:T(8,128)(2,1)S(1)} %collective-permute-done.16.high_ref), custom_call_target="tpu_custom_call" | custom-call | flops 1000 | bytes 1000 | tf_op jit(solution)/shard_map/pallas_call | solution.py:370
  145.9 1.0 copy-done.5
  147.5 6.6 %all-to-all-start.3 = ((bf16[4,128,1024]{2,1,0:T(8,128)(2,1)}), bf16[4,128,1024]{2,1,0:T(8,128)(2,1)S(1)}, u32[]{:S(2)}, u32[]{:S(2)}) async-start(bf16[4,128,1024]{2,1,0:T(8,128)(2,1)} %copy-done.5), calls=%async_computation.3 | async-start | bytes 2097152 | tf_op jit(solution)/shard_map/all_to_all | solution.py:41
  154.1 1.2 copy-done.4
  156.1 1.8 collective-permute-start.19
  157.9 0.9 copy-done.8
  158.9 1.3 shard_map.80
  160.4 2.0 collective-permute-start.22
  162.4 10.5 %shard_map.77 = (bf16[8,128,1024]{2,1,0:T(8,128)(2,1)}, f32[8,128,1024]{2,1,0:T(8,128)}) custom-call(s32[1]{0:T(128)} %bitcast.here_ref, s32[16,6]{1,0:T(8,128)S(1)} %copy.7.cover_ref, s32[16,6]{1,0:T(8,128)S(1)} %copy.8.offset_ref, bf16[8,128,128]{2,1,0:T(8,128)(2,1)S(1)} %copy-done.10, bf16[4,128,1024]{2,1,0:T(8,128)(2,1)S(1)} %shard_map.70.refs_0_, ...), custom_call_target="tpu_custom_call" | custom-call | flops 1000 | bytes 1000 | tf_op jit(solution)/shard_map/pallas_call | solution.py:171
  172.9 5.1 %collective-permute-done.19.refs_3_ = bf16[128,1024]{1,0:T(8,128)(2,1)S(1)} collective-permute-done((bf16[128,1024]{1,0:T(8,128)(2,1)S(1)}, bf16[128,1024]{1,0:T(8,128)(2,1)S(1)}, u32[]{:S(2)}, u32[]{:S(2)}) %collective-permute-start.19) | collective-permute-done | bytes 262176 | tf_op jit(solution)/shard_map/ppermute | solution.py:30
  178.1 5.5 %collective-permute-done.21.refs_6_ = bf16[128,1024]{1,0:T(8,128)(2,1)S(1)} collective-permute-done((bf16[128,1024]{1,0:T(8,128)(2,1)S(1)}, bf16[128,1024]{1,0:T(8,128)(2,1)S(1)}, u32[]{:S(2)}, u32[]{:S(2)}) %collective-permute-start.21) | collective-permute-done | bytes 262176 | tf_op jit(solution)/shard_map/ppermute | solution.py:30
  183.6 5.6 %collective-permute-done.22.refs_7_ = bf16[128,1024]{1,0:T(8,128)(2,1)S(1)} collective-permute-done((bf16[128,1024]{1,0:T(8,128)(2,1)S(1)}, bf16[128,1024]{1,0:T(8,128)(2,1)S(1)}, u32[]{:S(2)}, u32[]{:S(2)}) %collective-permute-start.22) | collective-permute-done | bytes 262176 | tf_op jit(solution)/shard_map/ppermute | solution.py:30
  189.2 5.5 %shard_map.81 = bf16[128,8,1024]{2,1,0:T(8,128)(2,1)} custom-call(s32[1]{0:T(128)} %bitcast.here_ref, bf16[128,1024]{1,0:T(8,128)(2,1)S(1)} %get-tuple-element.43.refs_0_, bf16[128,1024]{1,0:T(8,128)(2,1)S(1)} %collective-permute-done.17.refs_1_, bf16[128,1024]{1,0:T(8,128)(2,1)S(1)} %collective-permute-done.18.refs_2_, ...), custom_call_target="tpu_custom_call" | custom-call | flops 1000 | bytes 1000 | tf_op jit(solution)/shard_map/pallas_call | solution.py:217
  194.7 10.8 %shard_map.78 = f32[128,8,1024]{2,1,0:T(8,128)} custom-call(s32[1]{0:T(128)} %bitcast.here_ref, f32[128,8,1024]{2,1,0:T(8,128)} %shard_map.68.refs_4_.tv_ref, bf16[4,128,1024]{2,1,0:T(8,128)(2,1)S(1)} %all-to-all-done.1.refs_0_, bf16[4,128,1024]{2,1,0:T(8,128)(2,1)S(1)} %all-to-all-done.3.refs_1_, f32[8,128,1024]{2,1,0:T(8,128)} %get-tuple-element.42.refs_2_), custom_call_target="tpu_custom_call" | custom-call | flops 1000 | bytes 1000 | tf_op jit(solution)/shard_map/pallas_call | solution.py:258
  (72 shorter events, 5.9 us)
Async XLA Ops:
  3.2 32.6 %collective-permute-start.4 = (bf16[128,8,1024]{2,1,0:T(8,128)(2,1)}, bf16[128,8,1024]{2,1,0:T(8,128)(2,1)}, u32[]{:S(2)}, u32[]{:S(2)}) collective-permute-start(bf16[128,8,1024]{2,1,0:T(8,128)(2,1)} %refs_2_.1), channel_id=1, source_target_pairs={{3,7},{7,11},{11,15},{19,23},{23,27},{27,31}} | collective-permute-start | bytes 6291464 | tf_op jit(solution)/shard_map/ppermute | solution.py:25
  21.2 31.0 %collective-permute-start.2 = (bf16[512,1024]{1,0:T(8,128)(2,1)S(1)}, bf16[512,1024]{1,0:T(8,128)(2,1)}, u32[]{:S(2)}, u32[]{:S(2)}) collective-permute-start(bf16[512,1024]{1,0:T(8,128)(2,1)S(1)} %bitcast.8), channel_id=1, source_target_pairs={{4,0},{5,1},{6,2},{7,3},{8,4},{9,5},{10,6},{11,7},{12,8},{13,9},{1... | collective-permute-start | bytes 3145736 | tf_op jit(solution)/shard_map/ppermute | solution.py:25
  28.1 18.2 %all-to-all-start.2 = ((bf16[4,128,1024]{2,1,0:T(8,128)(2,1)}), bf16[4,128,1024]{2,1,0:T(8,128)(2,1)S(1)}, u32[]{:S(2)}, u32[]{:S(2)}) async-start(bf16[4,128,1024]{2,1,0:T(8,128)(2,1)} %shard_map.74.refs_1_), calls=%async_computation.2 | async-start | bytes 2097152 | tf_op jit(solution)/shard_map/all_to_all | solution.py:41
  34.5 10.8 %collective-permute-start.3 = (bf16[128,1024]{1,0:T(8,128)(2,1)}, bf16[128,1024]{1,0:T(8,128)(2,1)}, u32[]{:S(2)}, u32[]{:S(2)}) collective-permute-start(bf16[128,1024]{1,0:T(8,128)(2,1)} %slice_bitcast_fusion.1), channel_id=1, source_target_pairs={{0,4},{1,5},{2,6},{3,7},{4,8},{5,9},{6,10},{7,11},{8,12},{9,13},{1... | collective-permute-start | bytes 786440 | tf_op jit(solution)/shard_map/ppermute | solution.py:25
  35.8 14.6 %copy-start.22 = (s32[16,6]{0,1:T(8,128)S(1)}, s32[16,6]{0,1:T(8,128)}, u32[]{:S(2)}) copy-start(s32[16,6]{0,1:T(8,128)} %param.8) | copy-start | bytes 1156
  35.8 14.7 %copy-start.23 = (s32[16,6]{0,1:T(8,128)S(1)}, s32[16,6]{0,1:T(8,128)}, u32[]{:S(2)}) copy-start(s32[16,6]{0,1:T(8,128)} %param.9) | copy-start | bytes 1156
  35.8 14.7 %copy-start.9 = (bf16[8,128,128]{2,1,0:T(8,128)(2,1)S(1)}, bf16[8,128,128]{2,1,0:T(8,128)(2,1)}, u32[]{:S(2)}) copy-start(bf16[8,128,128]{2,1,0:T(8,128)(2,1)} %w_ref.3) | copy-start | bytes 786436
  39.5 0.7 copy-start.11
  41.7 0.7 copy-start.17
  42.4 0.7 copy-start.19
  43.1 9.1 %collective-permute-start.5 = (bf16[128,1024]{1,0:T(8,128)(2,1)}, bf16[128,1024]{1,0:T(8,128)(2,1)}, u32[]{:S(2)}, u32[]{:S(2)}) collective-permute-start(bf16[128,1024]{1,0:T(8,128)(2,1)} %get-tuple-element.31), channel_id=1, source_target_pairs={{0,1},{1,0},{2,3},{3,2},{4,5},{5,4},{6,7},{7,6},{8,9},{9,8},{10,11... | collective-permute-start | bytes 786440 | tf_op jit(solution)/shard_map/ppermute | solution.py:30
  43.4 8.8 %collective-permute-start.6 = (bf16[128,1024]{1,0:T(8,128)(2,1)}, bf16[128,1024]{1,0:T(8,128)(2,1)}, u32[]{:S(2)}, u32[]{:S(2)}) collective-permute-start(bf16[128,1024]{1,0:T(8,128)(2,1)} %get-tuple-element.32), channel_id=1, source_target_pairs={{0,2},{1,3},{2,0},{3,1},{4,6},{5,7},{6,4},{7,5},{8,10},{9,11},{10,... | collective-permute-start | bytes 786440 | tf_op jit(solution)/shard_map/ppermute | solution.py:30
  43.4 14.1 %collective-permute-start.7 = (bf16[128,1024]{1,0:T(8,128)(2,1)}, bf16[128,1024]{1,0:T(8,128)(2,1)}, u32[]{:S(2)}, u32[]{:S(2)}) collective-permute-start(bf16[128,1024]{1,0:T(8,128)(2,1)} %get-tuple-element.33), channel_id=1, source_target_pairs={{0,3},{1,2},{2,1},{3,0},{4,7},{5,6},{6,5},{7,4},{8,11},{9,10},{10,... | collective-permute-start | bytes 786440 | tf_op jit(solution)/shard_map/ppermute | solution.py:30
  46.3 64.5 %collective-permute-start.10 = (bf16[512,1024]{1,0:T(8,128)(2,1)S(1)}, bf16[512,1024]{1,0:T(8,128)(2,1)}, u32[]{:S(2)}, u32[]{:S(2)}) collective-permute-start(bf16[512,1024]{1,0:T(8,128)(2,1)S(1)} %bitcast.10), channel_id=1, source_target_pairs={{4,0},{5,1},{6,2},{7,3},{8,4},{9,5},{10,6},{11,7},{12,8},{13,9},{1... | collective-permute-start | bytes 3145736 | tf_op jit(solution)/shard_map/ppermute | solution.py:25
  52.2 65.8 %copy-start.1 = (bf16[512,1152]{1,0:T(8,128)(2,1)}, bf16[512,1152]{1,0:T(8,128)(2,1)S(1)}, u32[]{:S(2)}) copy-start(bf16[512,1152]{1,0:T(8,128)(2,1)S(1)} %get-tuple-element.27.band_ref) | copy-start | bytes 3538948
  57.6 1.0 copy-start.14
  58.5 10.9 %copy-start.20 = (bf16[128,1024]{1,0:T(8,128)(2,1)S(1)}, bf16[128,1024]{1,0:T(8,128)(2,1)}, u32[]{:S(2)}) copy-start(bf16[128,1024]{1,0:T(8,128)(2,1)} %copy-done.19) | copy-start | bytes 786436
  58.5 12.5 %copy-start.18 = (bf16[128,1024]{1,0:T(8,128)(2,1)S(1)}, bf16[128,1024]{1,0:T(8,128)(2,1)}, u32[]{:S(2)}) copy-start(bf16[128,1024]{1,0:T(8,128)(2,1)} %copy-done.17) | copy-start | bytes 786436
  58.5 38.8 %copy-start.16 = (bf16[128,1024]{1,0:T(8,128)(2,1)S(1)}, bf16[128,1024]{1,0:T(8,128)(2,1)}, u32[]{:S(2)}) copy-start(bf16[128,1024]{1,0:T(8,128)(2,1)} %copy-done.15) | copy-start | bytes 786436
  61.7 56.3 %copy-start.3 = (bf16[512,1024]{1,0:T(8,128)(2,1)}, bf16[512,1024]{1,0:T(8,128)(2,1)S(1)}, u32[]{:S(2)}) copy-start(bf16[512,1024]{1,0:T(8,128)(2,1)S(1)} %get-tuple-element.34.own_ref.r_ref) | copy-start | bytes 3145732
  61.7 56.3 %collective-permute-start.8 = (bf16[512,1024]{1,0:T(8,128)(2,1)S(1)}, bf16[512,1024]{1,0:T(8,128)(2,1)S(1)}, u32[]{:S(2)}, u32[]{:S(2)}) collective-permute-start(bf16[512,1024]{1,0:T(8,128)(2,1)S(1)} %get-tuple-element.34.own_ref.r_ref), channel_id=1, source_target_pairs={{0,4},{1,5},{2,6},{3,7},{4,8},{5,9},{6,10},{7,11},{8,12},{9,13},{1... | collective-permute-start | bytes 3145736 | tf_op jit(solution)/shard_map/ppermute | solution.py:25
  63.0 34.4 %collective-permute-start.11 = (bf16[128,1024]{1,0:T(8,128)(2,1)S(1)}, bf16[128,1024]{1,0:T(8,128)(2,1)S(1)}, u32[]{:S(2)}, u32[]{:S(2)}) collective-permute-start(bf16[128,1024]{1,0:T(8,128)(2,1)S(1)} %slice_bitcast_fusion), channel_id=1, source_target_pairs={{0,4},{1,5},{2,6},{3,7},{4,8},{5,9},{6,10},{7,11},{8,12},{9,13},{1... | collective-permute-start | bytes 786440 | tf_op jit(solution)/shard_map/ppermute | solution.py:25
  65.1 4.3 %collective-permute-start = (f32[1,8,1024]{2,1,0:T(8,128)S(1)}, f32[1,8,1024]{2,1,0:T(8,128)S(1)}, u32[]{:S(2)}, u32[]{:S(2)}) collective-permute-start(f32[1,8,1024]{2,1,0:T(8,128)S(1)} %get-tuple-element.53), channel_id=1, source_target_pairs={{0,1},{1,2},{2,3},{3,4},{4,5},{5,6},{6,7},{7,8},{8,9},{9,10},{10,1... | collective-permute-start | bytes 98312 | tf_op jit(solution)/shard_map/ppermute | solution.py:25
  66.4 4.6 %collective-permute-start.1 = (f32[1,8,1024]{2,1,0:T(8,128)S(1)}, f32[1,8,1024]{2,1,0:T(8,128)S(1)}, u32[]{:S(2)}, u32[]{:S(2)}) collective-permute-start(f32[1,8,1024]{2,1,0:T(8,128)S(1)} %get-tuple-element.52), channel_id=1, source_target_pairs={{1,0},{2,1},{3,2},{4,3},{5,4},{6,5},{7,6},{8,7},{9,8},{10,9},{11,1... | collective-permute-start | bytes 98312 | tf_op jit(solution)/shard_map/ppermute | solution.py:25
  69.4 38.0 %collective-permute-start.12 = (bf16[128,1024]{1,0:T(8,128)(2,1)S(1)}, bf16[128,1024]{1,0:T(8,128)(2,1)S(1)}, u32[]{:S(2)}, u32[]{:S(2)}) collective-permute-start(bf16[128,1024]{1,0:T(8,128)(2,1)S(1)} %copy-done.20), channel_id=1, source_target_pairs={{0,1},{1,0},{2,3},{3,2},{4,5},{5,4},{6,7},{7,6},{8,9},{9,8},{10,11... | collective-permute-start | bytes 786440 | tf_op jit(solution)/shard_map/ppermute | solution.py:30
  71.0 39.8 %collective-permute-start.13 = (bf16[128,1024]{1,0:T(8,128)(2,1)S(1)}, bf16[128,1024]{1,0:T(8,128)(2,1)S(1)}, u32[]{:S(2)}, u32[]{:S(2)}) collective-permute-start(bf16[128,1024]{1,0:T(8,128)(2,1)S(1)} %copy-done.18), channel_id=1, source_target_pairs={{0,2},{1,3},{2,0},{3,1},{4,6},{5,7},{6,4},{7,5},{8,10},{9,11},{10,... | collective-permute-start | bytes 786440 | tf_op jit(solution)/shard_map/ppermute | solution.py:30
  97.4 13.5 %copy-start.12 = (bf16[128,1024]{1,0:T(8,128)(2,1)S(1)}, bf16[128,1024]{1,0:T(8,128)(2,1)}, u32[]{:S(2)}) copy-start(bf16[128,1024]{1,0:T(8,128)(2,1)} %copy-done.11) | copy-start | bytes 786436
  97.4 13.4 %collective-permute-start.14 = (bf16[128,1024]{1,0:T(8,128)(2,1)S(1)}, bf16[128,1024]{1,0:T(8,128)(2,1)S(1)}, u32[]{:S(2)}, u32[]{:S(2)}) collective-permute-start(bf16[128,1024]{1,0:T(8,128)(2,1)S(1)} %copy-done.16), channel_id=1, source_target_pairs={{0,3},{1,2},{2,1},{3,0},{4,7},{5,6},{6,5},{7,4},{8,11},{9,10},{10,... | collective-permute-start | bytes 786440 | tf_op jit(solution)/shard_map/ppermute | solution.py:30
  107.4 10.5 %collective-permute-start.9 = (bf16[128,1024]{1,0:T(8,128)(2,1)S(1)}, bf16[128,1024]{1,0:T(8,128)(2,1)S(1)}, u32[]{:S(2)}, u32[]{:S(2)}) collective-permute-start(bf16[128,1024]{1,0:T(8,128)(2,1)S(1)} %get-tuple-element.35), channel_id=1, source_target_pairs={{4,0},{5,1},{6,2},{7,3},{8,4},{9,5},{10,6},{11,7},{12,8},{13,9},{1... | collective-permute-start | bytes 786440 | tf_op jit(solution)/shard_map/ppermute | solution.py:25
  110.8 2.2 %copy-start = (f32[128,8,1024]{2,1,0:T(8,128)S(1)}, f32[128,8,1024]{2,1,0:T(8,128)}, u32[]{:S(2)}) copy-start(f32[128,8,1024]{2,1,0:T(8,128)} %shard_map.68.refs_4_.tv_ref) | copy-start | bytes 12582916
  116.7 1.3 copy-start.21
  116.7 26.2 %collective-permute-start.15 = (bf16[512,1024]{1,0:T(8,128)(2,1)}, bf16[512,1024]{1,0:T(8,128)(2,1)}, u32[]{:S(2)}, u32[]{:S(2)}) collective-permute-start(bf16[512,1024]{1,0:T(8,128)(2,1)} %get-tuple-element.40.own_ref.r_ref), channel_id=1, source_target_pairs={{0,4},{1,5},{2,6},{3,7},{4,8},{5,9},{6,10},{7,11},{8,12},{9,13},{1... | collective-permute-start | bytes 3145736 | tf_op jit(solution)/shard_map/ppermute | solution.py:25
  120.0 1.0 copy-start.6
  120.9 22.0 %copy-start.2 = (bf16[512,1152]{1,0:T(8,128)(2,1)S(1)}, bf16[512,1152]{1,0:T(8,128)(2,1)}, u32[]{:S(2)}) copy-start(bf16[512,1152]{1,0:T(8,128)(2,1)} %copy-done.1) | copy-start | bytes 3538948
  120.9 26.6 %all-to-all-start.1 = ((bf16[4,128,1024]{2,1,0:T(8,128)(2,1)}), bf16[4,128,1024]{2,1,0:T(8,128)(2,1)S(1)}, u32[]{:S(2)}, u32[]{:S(2)}) async-start(bf16[4,128,1024]{2,1,0:T(8,128)(2,1)} %copy-done.6), calls=%async_computation.1 | async-start | bytes 2097152 | tf_op jit(solution)/shard_map/all_to_all | solution.py:41
  126.6 9.9 %collective-permute-start.16 = (bf16[128,1024]{1,0:T(8,128)(2,1)}, bf16[128,1024]{1,0:T(8,128)(2,1)S(1)}, u32[]{:S(2)}, u32[]{:S(2)}) collective-permute-start(bf16[128,1024]{1,0:T(8,128)(2,1)} %copy-done.21), channel_id=1, source_target_pairs={{4,0},{5,1},{6,2},{7,3},{8,4},{9,5},{10,6},{11,7},{12,8},{13,9},{1... | collective-permute-start | bytes 786440 | tf_op jit(solution)/shard_map/ppermute | solution.py:25
  145.9 1.0 copy-start.5
  146.8 0.7 copy-start.7
  147.5 47.1 %all-to-all-start.3 = ((bf16[4,128,1024]{2,1,0:T(8,128)(2,1)}), bf16[4,128,1024]{2,1,0:T(8,128)(2,1)S(1)}, u32[]{:S(2)}, u32[]{:S(2)}) async-start(bf16[4,128,1024]{2,1,0:T(8,128)(2,1)} %copy-done.5), calls=%async_computation.3 | async-start | bytes 2097152 | tf_op jit(solution)/shard_map/all_to_all | solution.py:41
  154.1 1.2 copy-start.4
  155.4 7.0 %copy-start.10 = (bf16[8,128,128]{2,1,0:T(8,128)(2,1)S(1)}, bf16[8,128,128]{2,1,0:T(8,128)(2,1)}, u32[]{:S(2)}) copy-start(bf16[8,128,128]{2,1,0:T(8,128)(2,1)} %w_ref.3) | copy-start | bytes 786436
  155.7 4.7 %collective-permute-start.17 = (bf16[128,1024]{1,0:T(8,128)(2,1)S(1)}, bf16[128,1024]{1,0:T(8,128)(2,1)S(1)}, u32[]{:S(2)}, u32[]{:S(2)}) collective-permute-start(bf16[128,1024]{1,0:T(8,128)(2,1)S(1)} %get-tuple-element.44), channel_id=1, source_target_pairs={{0,1},{1,0},{2,3},{3,2},{4,5},{5,4},{6,7},{7,6},{8,9},{9,8},{10,11... | collective-permute-start | bytes 786440 | tf_op jit(solution)/shard_map/ppermute | solution.py:30
  156.1 16.8 %collective-permute-start.18 = (bf16[128,1024]{1,0:T(8,128)(2,1)S(1)}, bf16[128,1024]{1,0:T(8,128)(2,1)S(1)}, u32[]{:S(2)}, u32[]{:S(2)}) collective-permute-start(bf16[128,1024]{1,0:T(8,128)(2,1)S(1)} %get-tuple-element.45), channel_id=1, source_target_pairs={{0,2},{1,3},{2,0},{3,1},{4,6},{5,7},{6,4},{7,5},{8,10},{9,11},{10,... | collective-permute-start | bytes 786440 | tf_op jit(solution)/shard_map/ppermute | solution.py:30
  156.1 21.9 %collective-permute-start.19 = (bf16[128,1024]{1,0:T(8,128)(2,1)S(1)}, bf16[128,1024]{1,0:T(8,128)(2,1)S(1)}, u32[]{:S(2)}, u32[]{:S(2)}) collective-permute-start(bf16[128,1024]{1,0:T(8,128)(2,1)S(1)} %get-tuple-element.46), channel_id=1, source_target_pairs={{0,3},{1,2},{2,1},{3,0},{4,7},{5,6},{6,5},{7,4},{8,11},{9,10},{10,... | collective-permute-start | bytes 786440 | tf_op jit(solution)/shard_map/ppermute | solution.py:30
  157.9 0.9 copy-start.8
  160.2 17.9 %collective-permute-start.20 = (bf16[128,1024]{1,0:T(8,128)(2,1)S(1)}, bf16[128,1024]{1,0:T(8,128)(2,1)S(1)}, u32[]{:S(2)}, u32[]{:S(2)}) collective-permute-start(bf16[128,1024]{1,0:T(8,128)(2,1)S(1)} %get-tuple-element.48), channel_id=1, source_target_pairs={{0,1},{1,0},{2,3},{3,2},{4,5},{5,4},{6,7},{7,6},{8,9},{9,8},{10,11... | collective-permute-start | bytes 786440 | tf_op jit(solution)/shard_map/ppermute | solution.py:30
  160.3 23.3 %collective-permute-start.21 = (bf16[128,1024]{1,0:T(8,128)(2,1)S(1)}, bf16[128,1024]{1,0:T(8,128)(2,1)S(1)}, u32[]{:S(2)}, u32[]{:S(2)}) collective-permute-start(bf16[128,1024]{1,0:T(8,128)(2,1)S(1)} %get-tuple-element.49), channel_id=1, source_target_pairs={{0,2},{1,3},{2,0},{3,1},{4,6},{5,7},{6,4},{7,5},{8,10},{9,11},{10,... | collective-permute-start | bytes 786440 | tf_op jit(solution)/shard_map/ppermute | solution.py:30
  160.4 28.8 %collective-permute-start.22 = (bf16[128,1024]{1,0:T(8,128)(2,1)S(1)}, bf16[128,1024]{1,0:T(8,128)(2,1)S(1)}, u32[]{:S(2)}, u32[]{:S(2)}) collective-permute-start(bf16[128,1024]{1,0:T(8,128)(2,1)S(1)} %get-tuple-element.50), channel_id=1, source_target_pairs={{0,3},{1,2},{2,1},{3,0},{4,7},{5,6},{6,5},{7,4},{8,11},{9,10},{10,... | collective-permute-start | bytes 786440 | tf_op jit(solution)/shard_map/ppermute | solution.py:30
  (2 other events, 1.4 us)

commit v4 on v3

v4 whole, which is shorter than its diff:
```python
import functools

import jax
import jax.numpy as jnp
from jax import lax
from jax.experimental import pallas as pl
from jax.experimental.pallas import tpu as pltpu
from jax.sharding import PartitionSpec as P

G = 4
CHUNKS = 2
F32 = jnp.float32
BF16 = jnp.bfloat16
MIB = 1024 * 1024
LANES = 128
OTHERS = (0, 2, 3)
SMEM = pl.BlockSpec(memory_space=pltpu.SMEM)
VMEM = pl.BlockSpec(memory_space=pltpu.VMEM)
ANY = pl.BlockSpec(memory_space=pl.ANY)


def moved(value, steps, only=None):
    count = lax.axis_size("slab")
    first, last = max(0, -steps), min(count, count - steps)
    pairs = [(i, i + steps) for i in range(first, last) if only is None or i % G == only]
    return lax.ppermute(value, "slab", pairs)


def swapped(value, bits):
    count = lax.axis_size("slab")
    return lax.ppermute(value, "slab", [(i, i ^ bits) for i in range(count)])


def exchanged(blocks):
    return [block if m == 0 else swapped(block, m) for m, block in blocks]


def call(kernel, us, *, results, vmem=16, **how):
    return pl.pallas_call(
        kernel,
        out_shape=results,
        compiler_params=pltpu.CompilerParams(vmem_limit_bytes=vmem * MIB),
        cost_estimate=pl.CostEstimate(flops=int(us * 1.15e9), bytes_accessed=1000, transcendentals=0),
        **how,
    )


def value(shape, dtype):
    return jax.ShapeDtypeStruct(shape, dtype)


def far(array):
    return pltpu.with_memory_space_constraint(array, pltpu.HBM)


def across(shape, tile):
    block = shape[:-1] + (tile,)
    return pl.BlockSpec(block, lambda i: (0,) * (len(shape) - 1) + (i,))


def lanes(array, tile, parts):
    block = array.shape[:-1] + (tile,)
    zeros = (0,) * (len(block) - 1)
    return [pl.BlockSpec(block, lambda i, j=j: zeros + (i * parts + j,)) for j in range(parts)]


def row_of(place, m, chunk):
    return CHUNKS * jnp.bitwise_xor(place, m) + chunk


def cast_kernel(parts, here_ref, *refs):
    vol_refs, out_refs = refs[:parts], refs[parts:]
    rows = CHUNKS * G
    depth = vol_refs[0].shape[0] // rows
    place = lax.rem(here_ref[0], G)
    for j, vol_ref in enumerate(vol_refs):
        at = pl.ds(j * LANES, LANES)
        ends = jnp.concatenate([vol_ref[:rows, :], vol_ref[(depth - 1) * rows :, :]], axis=0).astype(BF16)
        for c in range(CHUNKS):
            for m in range(G):
                out_ref = out_refs[c * G + m]
                spot = pl.ds(row_of(place, m, c), depth, stride=rows)
                out_ref[:depth, at] = vol_ref[spot, :].astype(BF16)
                if out_ref.shape[0] > depth:
                    out_ref[depth:, at] = ends


def cast_rows(here, volume):
    depth, rows, cols = volume.shape
    flat = far(volume.reshape(depth * rows, cols))
    parts = 2
    shapes = [(depth + (2 * rows if c == 0 and m % 2 else 0), cols) for c in range(CHUNKS) for m in range(G)]
    return call(
        functools.partial(cast_kernel, parts),
        3.5,
        grid=(cols // (LANES * parts),),
        in_specs=[SMEM] + lanes(flat, LANES, parts),
        out_specs=[across(shape, LANES * parts) for shape in shapes],
        results=[value(shape, BF16) for shape in shapes],
    )(here, *[flat] * parts)


def pack_kernel(here_ref, *refs):
    in_refs, (all_ref, last_ref) = refs[:G], refs[-2:]
    side = in_refs[0].shape[0]
    for m in range(G):
        all_ref[m * side : (m + 1) * side] = in_refs[m][:side]
    spot = jnp.bitwise_xor(lax.rem(here_ref[0], G), G - 1)
    last_ref[:side] = all_ref[pl.ds(pl.multiple_of(spot * side, side), side), :]
    if last_ref.shape[0] > side:
        all_ref[G * side :] = in_refs[G - 1][side:]
        last_ref[side:] = in_refs[G - 1][side:]


def pack(here, blocks, *tokens):
    side, cols = blocks[0].shape
    more = blocks[G - 1].shape[0] - side
    tile = 512
    shapes = [(G * side + more, cols), (side + more, cols)]
    return call(
        pack_kernel,
        1,
        grid=(cols // tile,),
        in_specs=[SMEM] + [across(block.shape, tile) for block in blocks] + [ANY] * len(tokens),
        out_specs=[across(shape, tile) for shape in shapes],
        results=[value(shape, BF16) for shape in shapes],
    )(here, *blocks, *tokens)


def blocks_of(refs, depth):
    both, rest = refs[0], refs[1:]
    found = []
    for c in range(CHUNKS):
        found.append((c, 1, both.at[c * depth : (c + 1) * depth]))
        for n, m in enumerate(OTHERS):
            found.append((c, m, rest[c * len(OTHERS) + n]))
    return found


def split_kernel(here_ref, own_ref, got_ref, *refs):
    out_refs, wide = refs[-CHUNKS * len(OTHERS) - 2 : -1], refs[-1]
    depth, rows, cols = own_ref.shape
    place = lax.rem(here_ref[0], G)

    def fill(ref):
        for j in range(cols // LANES):
            wide[j] = ref[:, :, j * LANES : (j + 1) * LANES].astype(F32).reshape(wide.shape[1:])

    @pl.when(place == G - 1)
    def _():
        fill(got_ref)

    @pl.when(place != G - 1)
    def _():
        fill(own_ref)

    for j in range(cols // LANES):
        at = pl.ds(j * LANES, LANES)
        for c, m, ref in blocks_of(out_refs, depth):
            spot = pl.ds(row_of(place, m, c), depth, stride=rows)
            ref[:, at] = wide.at[j][spot, :].astype(BF16)


def split_rows(here, own, got, *tokens):
    depth, rows, cols = own.shape
    tile = 512
    block = across(own.shape, tile)
    both, one = (CHUNKS * depth, cols), (depth, cols)
    count = CHUNKS * len(OTHERS)
    return call(
        split_kernel,
        4,
        grid=(cols // tile,),
        in_specs=[SMEM, block, block] + [ANY] * len(tokens),
        out_specs=[across(both, tile)] + [across(one, tile)] * count,
        results=[pltpu.HBM(both, BF16)] + [pltpu.HBM(one, BF16)] * count,
        scratch_shapes=[pltpu.VMEM((tile // LANES, depth * rows, LANES), F32)],
    )(here, far(own), got, *tokens)


def last_kernel(slabs, here_ref, cover_ref, offset_ref, w_ref, *refs):
    v_refs, (sino_ref, r_ref, b_ref, v, s, r, b, wide) = refs[: CHUNKS * G], refs[CHUNKS * G :]
    depth, rows, cols = sino_ref.shape

    @pl.when(here_ref[0] == slabs - 1)
    def _():
        for i, v_ref in enumerate(v_refs):
            pltpu.sync_copy(v_ref.at[:depth], v.at[i])
        pltpu.sync_copy(sino_ref, s)
        block = w_ref[offset_ref[slabs - 1, 0]]
        block = jnp.where(cover_ref[slabs - 1, 0] == 1, block, jnp.zeros_like(block))
        turned = block.astype(F32).T.astype(BF16)

        def column(j, _):
            at = pl.ds(pl.multiple_of(j * LANES, LANES), LANES)
            wide[...] = s[:, :, at].astype(F32).reshape(wide.shape)
            for c in range(CHUNKS):
                for m in range(G):
                    row = CHUNKS * ((G - 1) ^ m) + c
                    seen = jnp.dot(block, v[c * G + m, :, at], preferred_element_type=F32)
                    resid = (seen - wide[pl.ds(row, depth, stride=rows), :]).astype(BF16)
                    r[row, :, at] = resid
                    b[row, :, at] = jnp.dot(turned, resid, preferred_element_type=F32)
            return 0

        lax.fori_loop(0, cols // LANES, column, 0)
        pltpu.sync_copy(r, r_ref)
        pltpu.sync_copy(b, b_ref)


def last_group(here, coverage, offsets, weights, vols, sinogram):
    slabs = coverage.shape[0]
    depth, rows, cols = sinogram.shape
    return call(
        functools.partial(last_kernel, slabs),
        0.3,
        in_specs=[SMEM, SMEM, SMEM, VMEM] + [ANY] * (CHUNKS * G + 1),
        out_specs=[ANY, ANY],
        results=[pltpu.HBM((rows, depth, cols), BF16), pltpu.HBM((rows, depth, cols), F32)],
        scratch_shapes=[
            pltpu.VMEM((CHUNKS * G, depth, cols), BF16),
            pltpu.VMEM(sinogram.shape, BF16),
            pltpu.VMEM((rows, depth, cols), BF16),
            pltpu.VMEM((rows, depth, cols), F32),
            pltpu.VMEM((depth * rows, LANES), F32),
        ],
    )(here, coverage, offsets, weights, *vols, far(sinogram))


def join_kernel(slabs, here_ref, *refs):
    in_refs, (last_ref, out_ref, wide, held) = refs[:-4], refs[-4:]
    depth, rows, cols = out_ref.shape
    place = lax.rem(here_ref[0], G)
    last = here_ref[0] == slabs - 1

    @pl.when(last)
    def _():
        at = pl.ds(pl.multiple_of(pl.program_id(0) * cols, cols), cols)
        pltpu.sync_copy(last_ref.at[:, :, at], held)
        for j in range(cols // LANES):
            for row in range(rows):
                value = held[row, :, j * LANES : (j + 1) * LANES].astype(F32)
                wide.at[j][pl.ds(row, depth, stride=rows), :] = value

    @pl.when(jnp.logical_not(last))
    def _():
        for j in range(cols // LANES):
            at = pl.ds(j * LANES, LANES)
            for c, m, ref in blocks_of(in_refs, depth):
                spot = pl.ds(row_of(place, m, c), depth, stride=rows)
                wide.at[j][spot, :] = ref[:, at].astype(F32)

    for j in range(cols // LANES):
        out_ref[:, :, j * LANES : (j + 1) * LANES] = wide[j].reshape(depth, rows, LANES).astype(out_ref.dtype)


def join_rows(here, slabs, blocks, last):
    rows, depth, cols = last.shape
    tile = 512
    return call(
        functools.partial(join_kernel, slabs),
        2.6,
        grid=(cols // tile,),
        in_specs=[SMEM] + [across(block.shape, tile) for block in blocks] + [ANY],
        out_specs=across((depth, rows, cols), tile),
        results=value((depth, rows, cols), BF16),
        scratch_shapes=[
            pltpu.VMEM((tile // LANES, depth * rows, LANES), F32),
            pltpu.VMEM((rows, depth, tile), BF16),
        ],
    )(here, *blocks, far(last))


def finish_kernel(slabs, here_ref, tv_ref, *refs):
    in_refs, (last_ref, out_ref, wide, held) = refs[:-4], refs[-4:]
    place = lax.rem(here_ref[0], G)
    depth, rows, cols = out_ref.shape
    for j in range(cols // LANES):
        at = pl.ds(j * LANES, LANES)
        for c, m, ref in blocks_of(in_refs, depth):
            spot = pl.ds(row_of(place, m, c), depth, stride=rows)
            wide.at[j][spot, :] = ref[:, at].astype(F32)

    @pl.when(here_ref[0] == slabs - 1)
    def _():
        at = pl.ds(pl.multiple_of(pl.program_id(0) * cols, cols), cols)
        pltpu.sync_copy(last_ref.at[:, :, at], held)
        for j in range(cols // LANES):
            for row in range(rows):
                spot = pl.ds(row, depth, stride=rows)
                wide.at[j][spot, :] = wide.at[j][spot, :] + held[row, :, j * LANES : (j + 1) * LANES]

    for j in range(cols // LANES):
        at = pl.ds(j * LANES, LANES)
        out_ref[:, :, at] = tv_ref[:, :, at] + wide[j].reshape(depth, rows, LANES)


def finish(here, slabs, tv, blocks, last):
    depth, rows, cols = tv.shape
    tile = 256
    whole = across(tv.shape, tile)
    return call(
        functools.partial(finish_kernel, slabs),
        5,
        grid=(cols // tile,),
        in_specs=[SMEM, whole] + [across(block.shape, tile) for block in blocks] + [ANY],
        out_specs=whole,
        results=value((depth, rows, cols), F32),
        scratch_shapes=[
            pltpu.VMEM((tile // LANES, depth * rows, LANES), F32),
            pltpu.VMEM((rows, depth, tile), F32),
        ],
    )(here, far(tv), *blocks, far(last))


def band_kernel(slabs, span, here_ref, cover_ref, offset_ref, w_ref, *refs):
    proj_ref, back_ref, turned = refs[-3:]
    side = w_ref.shape[1]
    place = lax.rem(here_ref[0], G)
    first = here_ref[0] - place
    zero = jnp.zeros((side, side), BF16)
    for i in range(w_ref.shape[0]):
        turned[i] = w_ref[i].astype(F32).T.astype(BF16)

    def block(ref, i, j):
        k = j - i
        known, step = jnp.clip(i, 0, slabs - 1), jnp.clip(k, 0, span - 1)
        inside = (i >= 0) & (i < slabs) & (j >= 0) & (j < slabs) & (k >= 0) & (k < span)
        live = inside & (cover_ref[known, step] == 1)
        return jnp.where(live, ref[offset_ref[known, step]], zero)

    def slab(m):
        return first + jnp.bitwise_xor(place, m)

    def group(m):
        to = jnp.bitwise_xor(place, m)
        return first + jnp.where(to == G - 1, -1, to)

    seen = [slab(m) for m in range(G)] + [slab(m) + G for m in range(G)] + [first - 1]
    seeing = [group(m) for m in range(G)] + [group(m) - G for m in range(G)] + [first + G - 1]
    for r in range(G):
        for s in range(2 * G + 1):
            at = (pl.ds(r * side, side), pl.ds(s * side, side))
            proj_ref[at] = block(w_ref, group(r), seen[s])
            back_ref[at] = block(turned, seeing[s], slab(r))


def bands(here, coverage, offsets, weights, *tokens):
    slabs, span = coverage.shape
    side = weights.shape[1]
    shape = (G * side, (2 * G + 1) * side)
    return call(
        functools.partial(band_kernel, slabs, span),
        1.6,
        in_specs=[SMEM, SMEM, SMEM, pl.BlockSpec(weights.shape, lambda i: (0, 0, 0))] + [ANY] * len(tokens),
        grid=(1,),
        out_specs=[pl.BlockSpec(shape, lambda i: (0, 0))] * 2,
        results=[pltpu.HBM(shape, BF16)] * 2,
        scratch_shapes=[pltpu.VMEM(weights.shape, BF16)],
    )(here, coverage, offsets, weights, *tokens)


def project_kernel(here_ref, band_ref, own_ref, high_ref, low_ref, *refs):
    (both_ref, *rest), (r_ref, down_ref) = refs[:G], refs[-2:]
    side = down_ref.shape[0]
    n = G * side
    sinos = {1: both_ref, **dict(zip(OTHERS, rest))}
    seen = jnp.concatenate([own_ref[:n], high_ref[:n], low_ref[:side]], axis=0)
    total = jnp.dot(band_ref[...], seen, preferred_element_type=F32)
    for m in range(G):
        at = pl.ds(m * side, side)
        r_ref[at, :] = (total[m * side : (m + 1) * side] - sinos[m][...].astype(F32)).astype(BF16)
    spot = jnp.bitwise_xor(lax.rem(here_ref[0], G), G - 1)
    down_ref[...] = r_ref[pl.ds(pl.multiple_of(spot * side, side), side), :]


def project(here, chunk, band, own, high, low, sinos, *tokens):
    n, side = band.shape[0], band.shape[0] // G
    cols = own.shape[1]
    tile = 512
    one = across((side, cols), tile)
    return call(
        project_kernel,
        3,
        grid=(cols // tile,),
        in_specs=[SMEM, pl.BlockSpec(band.shape, lambda i: (0, 0))]
        + [across(array.shape, tile) for array in (own, high, low)]
        + [pl.BlockSpec((side, tile), lambda i: (chunk, i))]
        + [one] * len(OTHERS)
        + [ANY] * len(tokens),
        out_specs=[across((n, cols), tile), one],
        results=[value((n, cols), BF16), value((side, cols), BF16)],
    )(here, band, own, high, low, *sinos, *tokens)


def deal_kernel(chunk, here_ref, r_ref, high_ref, *refs):
    out_refs = refs[-G:]
    side = high_ref.shape[0]
    place = lax.rem(here_ref[0], G)

    def block(m):
        last = jnp.bitwise_xor(place, m) == G - 1
        return jnp.where(last, high_ref[...], r_ref[m * side : (m + 1) * side])

    put_blocks(chunk, block, out_refs, refs[0], side)


def put_blocks(chunk, block, out_refs, before_ref, side):
    both, rest = out_refs[0], out_refs[1:]
    if chunk:
        both[:side] = before_ref[...]
        both[side:] = block(1)
    else:
        both[...] = block(1)
    for n, m in enumerate(OTHERS):
        rest[n][...] = block(m)


def block_results(chunk, side, cols, tile):
    first = (CHUNKS * side if chunk else side, cols)
    shapes = [first] + [(side, cols)] * len(OTHERS)
    return dict(out_specs=[across(s, tile) for s in shapes], results=[value(s, BF16) for s in shapes])


def deal(here, chunk, resid, high, *before):
    side, cols = high.shape
    tile = 512
    one = across((side, cols), tile)
    return call(
        functools.partial(deal_kernel, chunk),
        1,
        grid=(cols // tile,),
        in_specs=[SMEM, across(resid.shape, tile), one] + [one] * len(before),
        **block_results(chunk, side, cols, tile),
    )(here, resid, high, *before)


def back_kernel(chunk, band_ref, own_ref, low_ref, high_ref, *refs):
    side = high_ref.shape[0]
    seeing = jnp.concatenate([own_ref[...], low_ref[...], high_ref[...]], axis=0)
    total = jnp.dot(band_ref[...], seeing, preferred_element_type=F32)
    put_blocks(chunk, lambda m: total[m * side : (m + 1) * side].astype(BF16), refs[-G:], refs[0], side)


def back(chunk, band, own, low, high, before, *tokens):
    side, cols = high.shape
    tile = 512
    one = across((side, cols), tile)
    many = across(own.shape, tile)
    return call(
        functools.partial(back_kernel, chunk),
        3,
        grid=(cols // tile,),
        in_specs=[pl.BlockSpec(band.shape, lambda i: (0, 0)), many, many, one]
        + [one] * len(before)
        + [ANY] * len(tokens),
        **block_results(chunk, side, cols, tile),
    )(band, own, low, high, *before, *tokens)


def tv_kernel(here_ref, near_ref, next_level_ref, far_ref, last_level_ref, next_ref, vol_ref, *refs):
    out_ref, flux_ref = refs[-2:]
    step = pl.program_id(0)
    steps = pl.num_programs(0)
    deep, rows, cols = vol_ref.shape
    place = lax.rem(here_ref[0], G)
    row = lax.broadcasted_iota(jnp.int32, (rows, cols), 0)

    def low_slice():
        inside = jnp.where(place == 2, far_ref[...], near_ref[...])
        return jnp.where(place == 0, last_level_ref[...], inside)[rows:].astype(F32)

    def high_slice():
        inside = jnp.where(place == 1, far_ref[...], near_ref[...])
        return jnp.where(place == G - 1, next_level_ref[...], inside)[:rows].astype(F32)

    col = lax.broadcasted_iota(jnp.int32, (rows, cols), 1)

    def up_y(v):
        return jnp.where(row == rows - 1, 0.0, pltpu.roll(v, rows - 1, 0))

    def up_x(v):
        return jnp.where(col == cols - 1, 0.0, pltpu.roll(v, cols - 1, 1))

    def scale_of(cur, above):
        dz = above - cur
        dy = up_y(cur) - cur
        dx = up_x(cur) - cur
        return dz, dy, dx, 0.5 * lax.rsqrt(dz * dz + dy * dy + dx * dx + 0.25)

    def edge(v):
        return 0.5 * v * lax.rsqrt(v * v + 0.25)

    @pl.when(step == 0)
    def _():
        dz, _, _, scale = scale_of(low_slice(), vol_ref[0])
        flux_ref[...] = dz * scale

    def one(z, cur, above, below_flux):
        dz, dy, dx, scale = scale_of(cur, above)
        fz, fy, fx = dz * scale, dy * scale, dx * scale
        sides = edge(cur)
        fy_low = jnp.where(row == 0, sides, pltpu.roll(fy, 1, 0))
        fx_low = jnp.where(col == 0, sides, pltpu.roll(fx, 1, 1))
        out_ref[z] = (below_flux - fz) + (fy_low - fy) + (fx_low - fx)
        return fz

    def body(z, flux):
        return one(z, vol_ref[z], vol_ref[z + 1], flux)

    flux = lax.fori_loop(0, deep - 1, body, flux_ref[...], unroll=5)
    above = jnp.where(step == steps - 1, high_slice(), next_ref[0])
    flux_ref[...] = one(deep - 1, vol_ref[deep - 1], above, flux)


def half_tv(here, volume, ends, *tokens):
    depth, rows, cols = volume.shape
    deep = 16
    steps = depth // deep
    edges = [pl.BlockSpec((2 * rows, cols), lambda i, last=end.shape[0] // (2 * rows) - 1: (last, 0)) for end in ends]
    body = pl.BlockSpec((deep, rows, cols), lambda i: (i, 0, 0))
    after = pl.BlockSpec((1, rows, cols), lambda i: (jnp.minimum((i + 1) * deep, depth - 1), 0, 0))
    return call(
        tv_kernel,
        7,
        grid=(steps,),
        in_specs=[SMEM] + edges + [after, body] + [ANY] * len(tokens),
        out_specs=body,
        results=pltpu.HBM(volume.shape, F32),
        scratch_shapes=[pltpu.VMEM((rows, cols), F32)],
    )(here, *ends, far(volume), far(volume), *tokens)


def local(volume, sinogram, weights, coverage, offsets):
    slabs = lax.axis_size("slab")
    here = lax.axis_index("slab").astype(jnp.int32).reshape(1)

    vols = cast_rows(here, volume)
    vols0, vols1 = vols[:G], vols[G:]
    got = moved(lax.optimization_barrier((sinogram, vols0[0]))[0], G, only=G - 1)
    blocks0 = exchanged(enumerate(vols0))
    own0, edge0 = pack(here, blocks0)
    band_p, band_b = bands(here, coverage, offsets, weights, own0)
    sino = split_rows(here, sinogram, got, own0)
    own1, edge1 = pack(here, exchanged(enumerate(vols1)), sino[0])
    r_last, b_last = last_group(here, coverage, offsets, weights, vols, sinogram)
    sino_core = swapped(sino[0], 1)
    high0, high1 = moved(own0, -G), moved(own1, -G)
    low0, low1 = moved(edge0, G), moved(edge1, G)

    def residuals(c, own, high, low, *tokens):
        sinos = exchanged(zip(OTHERS, sino[1 + c * len(OTHERS) :]))
        resid, down = project(here, c, band_p, own, high, low, [sino_core] + sinos, *tokens)
        return resid, moved(resid, G), moved(down, -G)

    resid0, from_low0, from_high0 = residuals(0, own0, high0, low0, low1)
    tv = half_tv(here, volume, [blocks0[1], high0, blocks0[3], low0], resid0)
    dealt0 = deal(here, 0, resid0, from_high0)
    resid1, from_low1, from_high1 = residuals(1, own1, high1, low1, dealt0[0], tv)
    dealt1 = deal(here, 1, resid1, from_high1, dealt0[0])
    resid_blocks0 = exchanged(zip(OTHERS, dealt0[1:]))
    resid_blocks1 = exchanged(zip(OTHERS, dealt1[1:]))
    resid_blocks = [swapped(dealt1[0], 1)] + resid_blocks0 + resid_blocks1

    backs0 = back(0, band_b, resid0, from_low0, from_high0, [], dealt1[1], *resid_blocks0)
    back_blocks0 = exchanged(zip(OTHERS, backs0[1:]))
    backs1 = back(1, band_b, resid1, from_low1, from_high1, [backs0[0]], *resid_blocks1, *back_blocks0)
    back_blocks = [swapped(backs1[0], 1)] + back_blocks0 + exchanged(zip(OTHERS, backs1[1:]))

    residual = join_rows(here, slabs, resid_blocks, r_last)
    gradient = finish(here, slabs, tv, back_blocks, b_last)
    return (gradient, residual)


def solution(mesh):
    placed = (P("slab", "grp", None), P("slab", "grp", None), P(), P(), P())
    return jax.shard_map(
        local,
        mesh=mesh,
        in_specs=placed,
        out_specs=(P("slab", "grp", None), P("slab", "grp", None)),
        check_vma=False,
    )
```

time: 207 us -> 158 us (0.76)
  starting transfers between devices: 78.6 us -> 48.8 us
  blocking collectives: 16.7 us -> 0 us
  waiting for transfers between devices: 34.7 us -> 43.7 us
  local copies, waits for them, and re-layouts: 13.2 us -> 4.69 us
  Pallas kernels: 61.3 us -> 58.6 us
    all_to_all x3 -> x0, starting transfers between devices: 17.9 us -> none  [exchanged(): lax.all_to_all(array, 'slab', 0, 0, axis_index_groups=sets, tiled=True)]
    ppermute x12 -> x21, waiting for transfers between devices: 21.6 us -> 39.1 us  [swapped(): return lax.ppermute(value, 'slab', [(i, i ^ bits) for i in range(count)])]
    all_to_all x1 -> x0, blocking collectives: 16.7 us -> none  [exchanged(): lax.all_to_all(array, 'slab', 0, 0, axis_index_groups=sets, tiled=True)]
    ppermute x12 -> x21, starting transfers between devices: 34.6 us -> 24.9 us  [swapped(): return lax.ppermute(value, 'slab', [(i, i ^ bits) for i in range(count)])]
    ppermute x11 -> x9, waiting for transfers between devices: 12.1 us -> 4.63 us  [moved(): return lax.ppermute(value, 'slab', pairs)]
    unnamed x50 -> x44, local copies, waits for them, and re-layouts: 11.7 us -> 4.69 us
    pallas_call x14 -> x15, Pallas kernels: 61.3 us -> 58.6 us  [the longest x1 10.9 us: finish(): call(functools.partial(finish_kernel, slabs), 5, grid=(cols // tile,), in...]
    ppermute x11 -> x9, starting transfers between devices: 26.1 us -> 23.9 us  [moved(): return lax.ppermute(value, 'slab', pairs)]
  transfers between devices with their start and end apart: 26 -> 30, of which waited for: 7 -> 12; matrix products, arithmetic and copies ran while one was open for 1% -> 0% of each run, Pallas kernels for 23% -> 28%
where the time goes in v4:
time: 158 us; the launch traced here: 157 us
  Pallas kernels  58.6 us (37%)
  starting transfers between devices  48.8 us (31%)
  waiting for transfers between devices  43.7 us (28%)
  local copies, waits for them, and re-layouts  4.69 us (3%)
    ppermute x21, waiting for transfers between devices, swapped(): return lax.ppermute(value, 'slab', [(i, i ^ bits) for i in range(count)])  39.1 us
    ppermute x21, starting transfers between devices, swapped(): return lax.ppermute(value, 'slab', [(i, i ^ bits) for i in range(count)])  24.9 us
    ppermute x9, starting transfers between devices, moved(): return lax.ppermute(value, 'slab', pairs)  23.9 us
    pallas_call x1, Pallas kernels, finish(): call(functools.partial(finish_kernel, slabs), 5, grid=(cols // tile,), in...  10.9 us
    pallas_call x1, Pallas kernels, half_tv(): call(tv_kernel, 7, grid=(steps,), in_specs=[SMEM] + edges + [after, body]...  10.1 us
    pallas_call x1, Pallas kernels, last_group(): call(functools.partial(last_kernel, slabs), 0.3, in_specs=[SMEM, SMEM, SM...  9.45 us
    pallas_call x2, Pallas kernels, project(): call(project_kernel, 3, grid=(cols // tile,), in_specs=[SMEM, pl.BlockSpe...  5.93 us
    pallas_call x1, Pallas kernels, join_rows(): call(functools.partial(join_kernel, slabs), 2.6, grid=(cols // tile,), in...  5.51 us
  transfers between devices with their start and end apart: 30, of which 12 were waited for; matrix products, arithmetic and copies ran while one was open for 0% of the time, Pallas kernels for 28%

profile of v4, /device:TPU:29, one launch (start us, length us, event | category | flops | bytes accessed | tf_op | source)
XLA Modules:
  0.0 156.7 jit_solution(12212300139144669519)
XLA Ops:
  0.6 3.7 %shard_map.68 = (bf16[128,1024]{1,0:T(8,128)(2,1)S(1)}, bf16[144,1024]{1,0:T(8,128)(2,1)S(1)}, bf16[128,1024]{1,0:T(8,128)(2,1)S(1)}, bf16[144,1024]{1,0:T(8,128...) custom-call(s32[1]{0:T(128)} %bitcast.here_ref, ...), custom_call_target="tpu_custom_call" | custom-call | flops 4024999936 | bytes 1000 | tf_op jit(solution)/shard_map/pallas_call | solution.py:93
  4.4 1.3 collective-permute-start.5
  6.1 1.5 collective-permute-start.1
  7.6 12.8 %collective-permute-done.1.refs_2_ = bf16[128,1024]{1,0:T(8,128)(2,1)S(1)} collective-permute-done((bf16[128,1024]{1,0:T(8,128)(2,1)S(1)}, bf16[128,1024]{1,0:T(8,128)(2,1)S(1)}, u32[]{:S(2)}, u32[]{:S(2)}) %collective-permute-start.1) | collective-permute-done | bytes 262176 | tf_op jit(solution)/shard_map/ppermute | solution.py:31
  20.5 1.2 shard_map.69
  21.7 4.1 %collective-permute-start.3 = (bf16[528,1024]{1,0:T(8,128)(2,1)}, bf16[528,1024]{1,0:T(8,128)(2,1)S(1)}, u32[]{:S(2)}, u32[]{:S(2)}) collective-permute-start(bf16[528,1024]{1,0:T(8,128)(2,1)} %get-tuple-element.50.refs_0_.own_ref), channel_id=1, source_target_pairs={{4,0},{5,1},{6,2},{7,3},{8,4},{9,5},{10,6},{11,7},{12,8},{13,9},{1... | collective-permute-start | bytes 3244040 | tf_op jit(solution)/shard_map/ppermute | solution.py:26
  25.9 2.6 %collective-permute-start.11 = (bf16[128,1024]{1,0:T(8,128)(2,1)S(1)}, bf16[128,1024]{1,0:T(8,128)(2,1)S(1)}, u32[]{:S(2)}, u32[]{:S(2)}) collective-permute-start(bf16[128,1024]{1,0:T(8,128)(2,1)S(1)} %get-tuple-element.61.refs_7_), channel_id=1, source_target_pairs={{0,3},{1,2},{2,1},{3,0},{4,7},{5,6},{6,5},{7,4},{8,11},{9,10},{10,... | collective-permute-start | bytes 786440 | tf_op jit(solution)/shard_map/ppermute | solution.py:31
  28.5 3.0 %collective-permute-done.5.got_ref = bf16[128,8,1024]{2,1,0:T(8,128)(2,1)S(1)} collective-permute-done((bf16[128,8,1024]{2,1,0:T(8,128)(2,1)S(1)}, bf16[128,8,1024]{2,1,0:T(8,128)(2,1)S(1)}, u32[]{:S(2)}, u32[]{:S(2)}) %collective-permute-start.5) | collective-permute-done | bytes 2097184 | tf_op jit(solution)/shard_map/ppermute | solution.py:26
  31.4 1.3 collective-permute-start.4
  32.7 3.5 %shard_map.71 = (bf16[256,1024]{1,0:T(8,128)(2,1)}, bf16[128,1024]{1,0:T(8,128)(2,1)}, bf16[128,1024]{1,0:T(8,128)(2,1)}, bf16[128,1024]{1,0:T(8,128)(2,1)}, bf1...) custom-call(s32[1]{0:T(128)} %bitcast.here_ref, bf16[128,8,1024]{2,1,0:T(8,128)(2,1)} %refs_8_.1, ...), custom_call_target="tpu_custom_call" | custom-call | flops 4600000000 | bytes 1000 | tf_op jit(solution)/shard_map/pallas_call | solution.py:170
  36.3 3.2 %collective-permute-done.11.refs_3_ = bf16[128,1024]{1,0:T(8,128)(2,1)S(1)} collective-permute-done((bf16[128,1024]{1,0:T(8,128)(2,1)S(1)}, bf16[128,1024]{1,0:T(8,128)(2,1)S(1)}, u32[]{:S(2)}, u32[]{:S(2)}) %collective-permute-start.11) | collective-permute-done | bytes 262176 | tf_op jit(solution)/shard_map/ppermute | solution.py:31
  39.5 1.0 copy-done.3
  40.6 0.9 shard_map.72
  41.5 1.0 copy-done.1
  42.5 1.3 collective-permute-start.12
  43.9 0.7 copy-done.8
  44.6 0.8 collective-permute-start.8
  45.7 2.7 %shard_map.70 = (bf16[512,1152]{1,0:T(8,128)(2,1)}, bf16[512,1152]{1,0:T(8,128)(2,1)}) custom-call(s32[1]{0:T(128)} %bitcast.here_ref, s32[16,6]{1,0:T(8,128)S(1)} %copy.7.cover_ref, s32[16,6]{1,0:T(8,128)S(1)} %copy.8.offset_ref, bf16[8,128,128]{2,1,0:T(8,128)(2,1)S(1)} %copy-done, bf16[528,1024]{1,0:T(8,128)(2,1)} %get-tuple-element.50.refs_0_.own_ref), custom_call_target="tpu_custom_call" | custom-call | flops 1840000000 | bytes 1000 | tf_op jit(solution)/shard_map/pallas_call | solution.py:352
  48.6 4.2 %collective-permute-start.13 = (bf16[512,1024]{1,0:T(8,128)(2,1)S(1)}, bf16[512,1024]{1,0:T(8,128)(2,1)S(1)}, u32[]{:S(2)}, u32[]{:S(2)}) collective-permute-start(bf16[512,1024]{1,0:T(8,128)(2,1)S(1)} %copy-done.2), channel_id=1, source_target_pairs={{4,0},{5,1},{6,2},{7,3},{8,4},{9,5},{10,6},{11,7},{12,8},{13,9},{1... | collective-permute-start | bytes 3145736 | tf_op jit(solution)/shard_map/ppermute | solution.py:26
  52.8 0.7 collective-permute-start.14
  53.5 2.7 %collective-permute-start.15 = (bf16[128,1024]{1,0:T(8,128)(2,1)S(1)}, bf16[128,1024]{1,0:T(8,128)(2,1)S(1)}, u32[]{:S(2)}, u32[]{:S(2)}) collective-permute-start(bf16[128,1024]{1,0:T(8,128)(2,1)S(1)} %copy-done.19), channel_id=1, source_target_pairs={{0,3},{1,2},{2,1},{3,0},{4,7},{5,6},{6,5},{7,4},{8,11},{9,10},{10,... | collective-permute-start | bytes 786440 | tf_op jit(solution)/shard_map/ppermute | solution.py:31
  56.2 1.3 collective-permute-done.8.refs_3_
  57.6 1.3 copy-done.11
  58.8 3.0 %shard_map.73 = (bf16[512,1024]{1,0:T(8,128)(2,1)S(1)}, bf16[128,1024]{1,0:T(8,128)(2,1)S(1)}) custom-call(s32[1]{0:T(128)} %bitcast.here_ref, bf16[512,1152]{1,0:T(8,128)(2,1)S(1)} %copy-done.11, bf16[528,1024]{1,0:T(8,128)(2,1)} %get-tuple-element.50.refs_0_.own_ref, bf16[528,1024]{1,0:T(8,128)(2,1)S(1)} %collective-permute-done.3.high_ref.next_level_ref, ...), custom_call_target="tpu_custom_call" | custom-call | flops 3449999872 | bytes 1000 | tf_op jit(solution)/shard_map/pallas_call | solution.py:382
  61.9 4.6 %collective-permute-start.16 = (bf16[128,1024]{1,0:T(8,128)(2,1)S(1)}, bf16[128,1024]{1,0:T(8,128)(2,1)S(1)}, u32[]{:S(2)}, u32[]{:S(2)}) collective-permute-start(bf16[128,1024]{1,0:T(8,128)(2,1)S(1)} %get-tuple-element.69), channel_id=1, source_target_pairs={{4,0},{5,1},{6,2},{7,3},{8,4},{9,5},{10,6},{11,7},{12,8},{13,9},{1... | collective-permute-start | bytes 786440 | tf_op jit(solution)/shard_map/ppermute | solution.py:26
  66.4 1.3 collective-permute-start.19
  67.8 10.1 %shard_map.74.refs_5_.tv_ref = f32[128,8,1024]{2,1,0:T(8,128)} custom-call(s32[1]{0:T(128)} %bitcast.here_ref, bf16[144,1024]{1,0:T(8,128)(2,1)S(1)} %copy-done.5, bf16[528,1024]{1,0:T(8,128)(2,1)S(1)} %collective-permute-done.3.high_ref.next_level_ref, bf16[144,1024]{1,0:T(8,128)(2,1)S(1)} %copy-done.7, bf16[144,1024]{1,0:T(8,128)(2,1)S(1)} %copy-done.9, ...), custom_call_target="tpu_custom_call" | custom-call | flops 8049999872 | bytes 1000 | tf_op jit(solution)/shard_map/pallas_call | solution.py:523
  77.9 1.4 collective-permute-done.16.high_ref
  80.1 2.9 %shard_map.76 = (bf16[512,1024]{1,0:T(8,128)(2,1)S(1)}, bf16[128,1024]{1,0:T(8,128)(2,1)S(1)}) custom-call(s32[1]{0:T(128)} %bitcast.here_ref, bf16[512,1152]{1,0:T(8,128)(2,1)S(1)} %copy-done.12, bf16[512,1024]{1,0:T(8,128)(2,1)S(1)} %copy-done.2, bf16[512,1024]{1,0:T(8,128)(2,1)S(1)} %collective-permute-done.13.high_ref, ...), custom_call_target="tpu_custom_call" | custom-call | flops 3449999872 | bytes 1000 | tf_op jit(solution)/shard_map/pallas_call | solution.py:382
  83.0 1.3 collective-permute-start.17
  84.3 4.6 %collective-permute-start.18 = (bf16[128,1024]{1,0:T(8,128)(2,1)S(1)}, bf16[128,1024]{1,0:T(8,128)(2,1)S(1)}, u32[]{:S(2)}, u32[]{:S(2)}) collective-permute-start(bf16[128,1024]{1,0:T(8,128)(2,1)S(1)} %get-tuple-element.72), channel_id=1, source_target_pairs={{4,0},{5,1},{6,2},{7,3},{8,4},{9,5},{10,6},{11,7},{12,8},{13,9},{1... | collective-permute-start | bytes 786440 | tf_op jit(solution)/shard_map/ppermute | solution.py:26
  89.0 1.8 %collective-permute-start.20 = (bf16[128,1024]{1,0:T(8,128)(2,1)S(1)}, bf16[128,1024]{1,0:T(8,128)(2,1)S(1)}, u32[]{:S(2)}, u32[]{:S(2)}) collective-permute-start(bf16[128,1024]{1,0:T(8,128)(2,1)S(1)} %get-tuple-element.75), channel_id=1, source_target_pairs={{0,2},{1,3},{2,0},{3,1},{4,6},{5,7},{6,4},{7,5},{8,10},{9,11},{10,... | collective-permute-start | bytes 786440 | tf_op jit(solution)/shard_map/ppermute | solution.py:31
  90.8 2.2 %collective-permute-start.21 = (bf16[128,1024]{1,0:T(8,128)(2,1)S(1)}, bf16[128,1024]{1,0:T(8,128)(2,1)S(1)}, u32[]{:S(2)}, u32[]{:S(2)}) collective-permute-start(bf16[128,1024]{1,0:T(8,128)(2,1)S(1)} %get-tuple-element.76), channel_id=1, source_target_pairs={{0,3},{1,2},{2,1},{3,0},{4,7},{5,6},{6,5},{7,4},{8,11},{9,10},{10,... | collective-permute-start | bytes 786440 | tf_op jit(solution)/shard_map/ppermute | solution.py:31
  93.4 2.3 %collective-permute-start.22 = (bf16[128,1024]{1,0:T(8,128)(2,1)S(1)}, bf16[128,1024]{1,0:T(8,128)(2,1)S(1)}, u32[]{:S(2)}, u32[]{:S(2)}) collective-permute-start(bf16[128,1024]{1,0:T(8,128)(2,1)S(1)} %get-tuple-element.78), channel_id=1, source_target_pairs={{0,2},{1,3},{2,0},{3,1},{4,6},{5,7},{6,4},{7,5},{8,10},{9,11},{10,... | collective-permute-start | bytes 786440 | tf_op jit(solution)/shard_map/ppermute | solution.py:31
  95.7 5.4 %collective-permute-start.23 = (bf16[128,1024]{1,0:T(8,128)(2,1)S(1)}, bf16[128,1024]{1,0:T(8,128)(2,1)S(1)}, u32[]{:S(2)}, u32[]{:S(2)}) collective-permute-start(bf16[128,1024]{1,0:T(8,128)(2,1)S(1)} %get-tuple-element.79), channel_id=1, source_target_pairs={{0,3},{1,2},{2,1},{3,0},{4,7},{5,6},{6,5},{7,4},{8,11},{9,10},{10,... | collective-permute-start | bytes 786440 | tf_op jit(solution)/shard_map/ppermute | solution.py:31
  101.1 4.7 %collective-permute-done.21.refs_3_ = bf16[128,1024]{1,0:T(8,128)(2,1)S(1)} collective-permute-done((bf16[128,1024]{1,0:T(8,128)(2,1)S(1)}, bf16[128,1024]{1,0:T(8,128)(2,1)S(1)}, u32[]{:S(2)}, u32[]{:S(2)}) %collective-permute-start.21) | collective-permute-done | bytes 262176 | tf_op jit(solution)/shard_map/ppermute | solution.py:31
  105.8 2.0 %shard_map.78 = (bf16[128,1024]{1,0:T(8,128)(2,1)S(1)}, bf16[128,1024]{1,0:T(8,128)(2,1)S(1)}, bf16[128,1024]{1,0:T(8,128)(2,1)S(1)}, bf16[128,1024]{1,0:T(8,128)(2,1)S(1)}) custom-call(bf16[512,1152]{1,0:T(8,128)(2,1)S(1)} %copy-done.13, bf16[512,1024]{1,0:T(8,128)(2,1)S(1)} %get-tuple-element.63.refs_0_.r_ref.own_ref, ...), custom_call_target="tpu_custom_call" | custom-call | flops 3449999872 | bytes 1000 | tf_op jit(solution)/shard_map/pallas_call | solution.py:450
  107.8 0.7 collective-permute-start.24
  108.5 3.3 %collective-permute-start.29 = (bf16[256,1024]{1,0:T(8,128)(2,1)S(1)}, bf16[256,1024]{1,0:T(8,128)(2,1)S(1)}, u32[]{:S(2)}, u32[]{:S(2)}) collective-permute-start(bf16[256,1024]{1,0:T(8,128)(2,1)S(1)} %get-tuple-element.88), channel_id=1, source_target_pairs={{0,1},{1,0},{2,3},{3,2},{4,5},{5,4},{6,7},{7,6},{8,9},{9,8},{10,11... | collective-permute-start | bytes 1572872 | tf_op jit(solution)/shard_map/ppermute | solution.py:31
  111.9 4.9 %collective-permute-done.23.refs_3_.refs_6_ = bf16[128,1024]{1,0:T(8,128)(2,1)S(1)} collective-permute-done((bf16[128,1024]{1,0:T(8,128)(2,1)S(1)}, bf16[128,1024]{1,0:T(8,128)(2,1)S(1)}, u32[]{:S(2)}, u32[]{:S(2)}) %collective-permute-start.23) | collective-permute-done | bytes 262176 | tf_op jit(solution)/shard_map/ppermute | solution.py:31
  116.8 0.8 collective-permute-done.24.refs_5_.refs_2_
  117.6 7.8 %collective-permute-done.25.refs_6_.refs_3_ = bf16[128,1024]{1,0:T(8,128)(2,1)S(1)} collective-permute-done((bf16[128,1024]{1,0:T(8,128)(2,1)S(1)}, bf16[128,1024]{1,0:T(8,128)(2,1)S(1)}, u32[]{:S(2)}, u32[]{:S(2)}) %collective-permute-start.25) | collective-permute-done | bytes 262176 | tf_op jit(solution)/shard_map/ppermute | solution.py:31
  125.4 2.0 %shard_map.79 = (bf16[256,1024]{1,0:T(8,128)(2,1)S(1)}, bf16[128,1024]{1,0:T(8,128)(2,1)S(1)}, bf16[128,1024]{1,0:T(8,128)(2,1)S(1)}, bf16[128,1024]{1,0:T(8,128)(2,1)S(1)}) custom-call(bf16[512,1152]{1,0:T(8,128)(2,1)S(1)} %copy-done.13, bf16[512,1024]{1,0:T(8,128)(2,1)S(1)} %get-tuple-element.71.r_ref.own_ref, ...), custom_call_target="tpu_custom_call" | custom-call | flops 3449999872 | bytes 1000 | tf_op jit(solution)/shard_map/pallas_call | solution.py:450
  127.5 9.5 %shard_map.80 = (bf16[8,128,1024]{2,1,0:T(8,128)(2,1)}, f32[8,128,1024]{2,1,0:T(8,128)}) custom-call(s32[1]{0:T(128)} %bitcast.here_ref, s32[16,6]{1,0:T(8,128)S(1)} %copy.7.cover_ref, s32[16,6]{1,0:T(8,128)S(1)} %copy.8.offset_ref, bf16[8,128,128]{2,1,0:T(8,128)(2,1)S(1)} %copy-done, bf16[128,1024]{1,0:T(8,128)(2,1)S(1)} %get-tuple-element.47.refs_0_, ...), custom_call_target="tpu_custom_call" | custom-call | flops 345000000 | bytes 1000 | tf_op jit(solution)/shard_map/pallas_call | solution.py:214
  137.0 5.5 %shard_map.82 = bf16[128,8,1024]{2,1,0:T(8,128)(2,1)} custom-call(s32[1]{0:T(128)} %bitcast.here_ref, bf16[256,1024]{1,0:T(8,128)(2,1)S(1)} %collective-permute-done.29.refs_0_, bf16[128,1024]{1,0:T(8,128)(2,1)S(1)} %get-tuple-element.74.refs_1_, bf16[128,1024]{1,0:T(8,128)(2,1)S(1)} %collective-permute-done.20.refs_2_, ...), custom_call_target="tpu_custom_call" | custom-call | flops 2990000128 | bytes 1000 | tf_op jit(solution)/shard_map/pallas_call | solution.py:260
  142.5 2.0 %collective-permute-done.27.refs_5_ = bf16[128,1024]{1,0:T(8,128)(2,1)S(1)} collective-permute-done((bf16[128,1024]{1,0:T(8,128)(2,1)S(1)}, bf16[128,1024]{1,0:T(8,128)(2,1)S(1)}, u32[]{:S(2)}, u32[]{:S(2)}) %collective-permute-start.27) | collective-permute-done | bytes 262176 | tf_op jit(solution)/shard_map/ppermute | solution.py:31
  144.4 1.5 collective-permute-done.28.refs_6_
  145.9 10.9 %shard_map.81 = f32[128,8,1024]{2,1,0:T(8,128)} custom-call(s32[1]{0:T(128)} %bitcast.here_ref, f32[128,8,1024]{2,1,0:T(8,128)} %shard_map.74.refs_5_.tv_ref, bf16[256,1024]{1,0:T(8,128)(2,1)S(1)} %collective-permute-done.26.refs_0_, bf16[128,1024]{1,0:T(8,128)(2,1)S(1)} %get-tuple-element.80.refs_4_.refs_1_, ...), custom_call_target="tpu_custom_call" | custom-call | flops 5750000128 | bytes 1000 | tf_op jit(solution)/shard_map/pallas_call | solution.py:302
  (71 shorter events, 2.4 us)
Async XLA Ops:
  0.6 3.7 %copy-start.16 = (bf16[128,8,1024]{2,1,0:T(8,128)(2,1)S(1)}, bf16[128,8,1024]{2,1,0:T(8,128)(2,1)}, u32[]{:S(2)}) copy-start(bf16[128,8,1024]{2,1,0:T(8,128)(2,1)} %refs_8_.1) | copy-start | bytes 6291460
  4.4 27.1 %collective-permute-start.5 = (bf16[128,8,1024]{2,1,0:T(8,128)(2,1)S(1)}, bf16[128,8,1024]{2,1,0:T(8,128)(2,1)S(1)}, u32[]{:S(2)}, u32[]{:S(2)}) collective-permute-start(bf16[128,8,1024]{2,1,0:T(8,128)(2,1)S(1)} %copy-done.16), channel_id=1, source_target_pairs={{3,7},{7,11},{11,15},{19,23},{23,27},{27,31}} | collective-permute-start | bytes 6291464 | tf_op jit(solution)/shard_map/ppermute | solution.py:26
  5.7 14.8 %collective-permute-start = (bf16[144,1024]{1,0:T(8,128)(2,1)S(1)}, bf16[144,1024]{1,0:T(8,128)(2,1)S(1)}, u32[]{:S(2)}, u32[]{:S(2)}) collective-permute-start(bf16[144,1024]{1,0:T(8,128)(2,1)S(1)} %get-tuple-element.46.refs_1_), channel_id=1, source_target_pairs={{0,1},{1,0},{2,3},{3,2},{4,5},{5,4},{6,7},{7,6},{8,9},{9,8},{10,11... | collective-permute-start | bytes 884744 | tf_op jit(solution)/shard_map/ppermute | solution.py:31
  5.9 14.5 %collective-permute-start.2 = (bf16[144,1024]{1,0:T(8,128)(2,1)S(1)}, bf16[144,1024]{1,0:T(8,128)(2,1)S(1)}, u32[]{:S(2)}, u32[]{:S(2)}) collective-permute-start(bf16[144,1024]{1,0:T(8,128)(2,1)S(1)} %get-tuple-element.49.refs_3_), channel_id=1, source_target_pairs={{0,3},{1,2},{2,1},{3,0},{4,7},{5,6},{6,5},{7,4},{8,11},{9,10},{10,... | collective-permute-start | bytes 884744 | tf_op jit(solution)/shard_map/ppermute | solution.py:31
  6.1 14.3 %collective-permute-start.1 = (bf16[128,1024]{1,0:T(8,128)(2,1)S(1)}, bf16[128,1024]{1,0:T(8,128)(2,1)S(1)}, u32[]{:S(2)}, u32[]{:S(2)}) collective-permute-start(bf16[128,1024]{1,0:T(8,128)(2,1)S(1)} %get-tuple-element.48.refs_2_), channel_id=1, source_target_pairs={{0,2},{1,3},{2,0},{3,1},{4,6},{5,7},{6,4},{7,5},{8,10},{9,11},{10,... | collective-permute-start | bytes 786440 | tf_op jit(solution)/shard_map/ppermute | solution.py:31
  20.5 1.2 copy-start.4
  20.5 1.2 copy-start.6
  21.7 26.9 %collective-permute-start.3 = (bf16[528,1024]{1,0:T(8,128)(2,1)}, bf16[528,1024]{1,0:T(8,128)(2,1)S(1)}, u32[]{:S(2)}, u32[]{:S(2)}) collective-permute-start(bf16[528,1024]{1,0:T(8,128)(2,1)} %get-tuple-element.50.refs_0_.own_ref), channel_id=1, source_target_pairs={{4,0},{5,1},{6,2},{7,3},{8,4},{9,5},{10,6},{11,7},{12,8},{13,9},{1... | collective-permute-start | bytes 3244040 | tf_op jit(solution)/shard_map/ppermute | solution.py:26
  25.8 10.4 %collective-permute-start.10 = (bf16[128,1024]{1,0:T(8,128)(2,1)S(1)}, bf16[128,1024]{1,0:T(8,128)(2,1)S(1)}, u32[]{:S(2)}, u32[]{:S(2)}) collective-permute-start(bf16[128,1024]{1,0:T(8,128)(2,1)S(1)} %get-tuple-element.60.refs_6_), channel_id=1, source_target_pairs={{0,2},{1,3},{2,0},{3,1},{4,6},{5,7},{6,4},{7,5},{8,10},{9,11},{10,... | collective-permute-start | bytes 786440 | tf_op jit(solution)/shard_map/ppermute | solution.py:31
  25.9 13.6 %collective-permute-start.11 = (bf16[128,1024]{1,0:T(8,128)(2,1)S(1)}, bf16[128,1024]{1,0:T(8,128)(2,1)S(1)}, u32[]{:S(2)}, u32[]{:S(2)}) collective-permute-start(bf16[128,1024]{1,0:T(8,128)(2,1)S(1)} %get-tuple-element.61.refs_7_), channel_id=1, source_target_pairs={{0,3},{1,2},{2,1},{3,0},{4,7},{5,6},{6,5},{7,4},{8,11},{9,10},{10,... | collective-permute-start | bytes 786440 | tf_op jit(solution)/shard_map/ppermute | solution.py:31
  28.5 11.1 %collective-permute-start.9 = (bf16[128,1024]{1,0:T(8,128)(2,1)S(1)}, bf16[128,1024]{1,0:T(8,128)(2,1)S(1)}, u32[]{:S(2)}, u32[]{:S(2)}) collective-permute-start(bf16[128,1024]{1,0:T(8,128)(2,1)S(1)} %get-tuple-element.59.refs_5_), channel_id=1, source_target_pairs={{0,1},{1,0},{2,3},{3,2},{4,5},{5,4},{6,7},{7,6},{8,9},{9,8},{10,11... | collective-permute-start | bytes 786440 | tf_op jit(solution)/shard_map/ppermute | solution.py:31
  31.4 12.4 %collective-permute-start.4 = (bf16[144,1024]{1,0:T(8,128)(2,1)S(1)}, bf16[144,1024]{1,0:T(8,128)(2,1)S(1)}, u32[]{:S(2)}, u32[]{:S(2)}) collective-permute-start(bf16[144,1024]{1,0:T(8,128)(2,1)S(1)} %get-tuple-element.51), channel_id=1, source_target_pairs={{0,4},{1,5},{2,6},{3,7},{4,8},{5,9},{6,10},{7,11},{8,12},{9,13},{1... | collective-permute-start | bytes 884744 | tf_op jit(solution)/shard_map/ppermute | solution.py:26
  36.3 21.3 %collective-permute-start.6 = (bf16[256,1024]{1,0:T(8,128)(2,1)}, bf16[256,1024]{1,0:T(8,128)(2,1)}, u32[]{:S(2)}, u32[]{:S(2)}) collective-permute-start(bf16[256,1024]{1,0:T(8,128)(2,1)} %get-tuple-element.54.refs_4_), channel_id=1, source_target_pairs={{0,1},{1,0},{2,3},{3,2},{4,5},{5,4},{6,7},{7,6},{8,9},{9,8},{10,11... | collective-permute-start | bytes 1572872 | tf_op jit(solution)/shard_map/ppermute | solution.py:31
  40.6 4.9 %copy-start.17 = (s32[16,6]{0,1:T(8,128)S(1)}, s32[16,6]{0,1:T(8,128)}, u32[]{:S(2)}) copy-start(s32[16,6]{0,1:T(8,128)} %param.8) | copy-start | bytes 1156
  40.6 5.0 %copy-start.18 = (s32[16,6]{0,1:T(8,128)S(1)}, s32[16,6]{0,1:T(8,128)}, u32[]{:S(2)}) copy-start(s32[16,6]{0,1:T(8,128)} %param.9) | copy-start | bytes 1156
  40.6 5.1 %copy-start = (bf16[8,128,128]{2,1,0:T(8,128)(2,1)S(1)}, bf16[8,128,128]{2,1,0:T(8,128)(2,1)}, u32[]{:S(2)}) copy-start(bf16[8,128,128]{2,1,0:T(8,128)(2,1)} %w_ref.3) | copy-start | bytes 786436
  42.5 10.2 %collective-permute-start.12 = (bf16[128,1024]{1,0:T(8,128)(2,1)}, bf16[128,1024]{1,0:T(8,128)(2,1)}, u32[]{:S(2)}, u32[]{:S(2)}) collective-permute-start(bf16[128,1024]{1,0:T(8,128)(2,1)} %get-tuple-element.62), channel_id=1, source_target_pairs={{0,4},{1,5},{2,6},{3,7},{4,8},{5,9},{6,10},{7,11},{8,12},{9,13},{1... | collective-permute-start | bytes 786440 | tf_op jit(solution)/shard_map/ppermute | solution.py:26
  43.8 9.7 %collective-permute-start.7 = (bf16[128,1024]{1,0:T(8,128)(2,1)}, bf16[128,1024]{1,0:T(8,128)(2,1)}, u32[]{:S(2)}, u32[]{:S(2)}) collective-permute-start(bf16[128,1024]{1,0:T(8,128)(2,1)} %get-tuple-element.56), channel_id=1, source_target_pairs={{0,2},{1,3},{2,0},{3,1},{4,6},{5,7},{6,4},{7,5},{8,10},{9,11},{10,... | collective-permute-start | bytes 786440 | tf_op jit(solution)/shard_map/ppermute | solution.py:31
  44.6 12.9 %collective-permute-start.8 = (bf16[128,1024]{1,0:T(8,128)(2,1)}, bf16[128,1024]{1,0:T(8,128)(2,1)}, u32[]{:S(2)}, u32[]{:S(2)}) collective-permute-start(bf16[128,1024]{1,0:T(8,128)(2,1)} %get-tuple-element.57), channel_id=1, source_target_pairs={{0,3},{1,2},{2,1},{3,0},{4,7},{5,6},{6,5},{7,4},{8,11},{9,10},{10,... | collective-permute-start | bytes 786440 | tf_op jit(solution)/shard_map/ppermute | solution.py:31
  45.6 3.0 %copy-start.2 = (bf16[512,1024]{1,0:T(8,128)(2,1)S(1)}, bf16[512,1024]{1,0:T(8,128)(2,1)}, u32[]{:S(2)}) copy-start(bf16[512,1024]{1,0:T(8,128)(2,1)} %copy-done.1) | copy-start | bytes 3145732
  45.6 7.1 %copy-start.20 = (bf16[128,1024]{1,0:T(8,128)(2,1)S(1)}, bf16[128,1024]{1,0:T(8,128)(2,1)}, u32[]{:S(2)}) copy-start(bf16[128,1024]{1,0:T(8,128)(2,1)} %get-tuple-element.67) | copy-start | bytes 786436
  45.6 7.9 %copy-start.19 = (bf16[128,1024]{1,0:T(8,128)(2,1)S(1)}, bf16[128,1024]{1,0:T(8,128)(2,1)}, u32[]{:S(2)}) copy-start(bf16[128,1024]{1,0:T(8,128)(2,1)} %get-tuple-element.68) | copy-start | bytes 786436
  45.7 11.9 %copy-start.9 = (bf16[144,1024]{1,0:T(8,128)(2,1)S(1)}, bf16[144,1024]{1,0:T(8,128)(2,1)}, u32[]{:S(2)}) copy-start(bf16[144,1024]{1,0:T(8,128)(2,1)} %copy-done.8) | copy-start | bytes 884740
  45.7 11.9 %copy-start.15 = (bf16[128,1024]{1,0:T(8,128)(2,1)S(1)}, bf16[128,1024]{1,0:T(8,128)(2,1)}, u32[]{:S(2)}) copy-start(bf16[128,1024]{1,0:T(8,128)(2,1)} %get-tuple-element.55.refs_1_) | copy-start | bytes 786436
  48.6 31.1 %collective-permute-start.13 = (bf16[512,1024]{1,0:T(8,128)(2,1)S(1)}, bf16[512,1024]{1,0:T(8,128)(2,1)S(1)}, u32[]{:S(2)}, u32[]{:S(2)}) collective-permute-start(bf16[512,1024]{1,0:T(8,128)(2,1)S(1)} %copy-done.2), channel_id=1, source_target_pairs={{4,0},{5,1},{6,2},{7,3},{8,4},{9,5},{10,6},{11,7},{12,8},{13,9},{1... | collective-permute-start | bytes 3145736 | tf_op jit(solution)/shard_map/ppermute | solution.py:26
  52.8 26.9 %collective-permute-start.14 = (bf16[128,1024]{1,0:T(8,128)(2,1)S(1)}, bf16[128,1024]{1,0:T(8,128)(2,1)S(1)}, u32[]{:S(2)}, u32[]{:S(2)}) collective-permute-start(bf16[128,1024]{1,0:T(8,128)(2,1)S(1)} %copy-done.20), channel_id=1, source_target_pairs={{0,2},{1,3},{2,0},{3,1},{4,6},{5,7},{6,4},{7,5},{8,10},{9,11},{10,... | collective-permute-start | bytes 786440 | tf_op jit(solution)/shard_map/ppermute | solution.py:31
  53.5 26.1 %collective-permute-start.15 = (bf16[128,1024]{1,0:T(8,128)(2,1)S(1)}, bf16[128,1024]{1,0:T(8,128)(2,1)S(1)}, u32[]{:S(2)}, u32[]{:S(2)}) collective-permute-start(bf16[128,1024]{1,0:T(8,128)(2,1)S(1)} %copy-done.19), channel_id=1, source_target_pairs={{0,3},{1,2},{2,1},{3,0},{4,7},{5,6},{6,5},{7,4},{8,11},{9,10},{10,... | collective-permute-start | bytes 786440 | tf_op jit(solution)/shard_map/ppermute | solution.py:31
  57.5 1.3 copy-start.11
  58.8 8.9 %copy-start.5 = (bf16[144,1024]{1,0:T(8,128)(2,1)S(1)}, bf16[144,1024]{1,0:T(8,128)(2,1)}, u32[]{:S(2)}) copy-start(bf16[144,1024]{1,0:T(8,128)(2,1)} %copy-done.4) | copy-start | bytes 884740
  58.8 8.9 %copy-start.7 = (bf16[144,1024]{1,0:T(8,128)(2,1)S(1)}, bf16[144,1024]{1,0:T(8,128)(2,1)}, u32[]{:S(2)}) copy-start(bf16[144,1024]{1,0:T(8,128)(2,1)} %copy-done.6) | copy-start | bytes 884740
  61.9 17.5 %collective-permute-start.16 = (bf16[128,1024]{1,0:T(8,128)(2,1)S(1)}, bf16[128,1024]{1,0:T(8,128)(2,1)S(1)}, u32[]{:S(2)}, u32[]{:S(2)}) collective-permute-start(bf16[128,1024]{1,0:T(8,128)(2,1)S(1)} %get-tuple-element.69), channel_id=1, source_target_pairs={{4,0},{5,1},{6,2},{7,3},{8,4},{9,5},{10,6},{11,7},{12,8},{13,9},{1... | collective-permute-start | bytes 786440 | tf_op jit(solution)/shard_map/ppermute | solution.py:26
  66.4 39.4 %collective-permute-start.19 = (bf16[512,1024]{1,0:T(8,128)(2,1)S(1)}, bf16[512,1024]{1,0:T(8,128)(2,1)S(1)}, u32[]{:S(2)}, u32[]{:S(2)}) collective-permute-start(bf16[512,1024]{1,0:T(8,128)(2,1)S(1)} %get-tuple-element.63.refs_0_.r_ref.own_ref), channel_id=1, source_target_pairs={{0,4},{1,5},{2,6},{3,7},{4,8},{5,9},{6,10},{7,11},{8,12},{9,13},{1... | collective-permute-start | bytes 3145736 | tf_op jit(solution)/shard_map/ppermute | solution.py:26
  67.8 11.9 %copy-start.12 = (bf16[512,1152]{1,0:T(8,128)(2,1)S(1)}, bf16[512,1152]{1,0:T(8,128)(2,1)}, u32[]{:S(2)}) copy-start(bf16[512,1152]{1,0:T(8,128)(2,1)} %get-tuple-element.52.band_ref) | copy-start | bytes 3538948
  67.8 11.9 %copy-start.14 = (bf16[128,1024]{1,0:T(8,128)(2,1)S(1)}, bf16[128,1024]{1,0:T(8,128)(2,1)}, u32[]{:S(2)}) copy-start(bf16[128,1024]{1,0:T(8,128)(2,1)} %get-tuple-element.66.refs_1_) | copy-start | bytes 786436
  77.9 2.2 %copy-start.10 = (f32[128,8,1024]{2,1,0:T(8,128)S(1)}, f32[128,8,1024]{2,1,0:T(8,128)}, u32[]{:S(2)}) copy-start(f32[128,8,1024]{2,1,0:T(8,128)} %shard_map.74.refs_5_.tv_ref) | copy-start | bytes 12582916
  83.0 42.4 %collective-permute-start.17 = (bf16[512,1024]{1,0:T(8,128)(2,1)S(1)}, bf16[512,1024]{1,0:T(8,128)(2,1)S(1)}, u32[]{:S(2)}, u32[]{:S(2)}) collective-permute-start(bf16[512,1024]{1,0:T(8,128)(2,1)S(1)} %get-tuple-element.71.r_ref.own_ref), channel_id=1, source_target_pairs={{0,4},{1,5},{2,6},{3,7},{4,8},{5,9},{6,10},{7,11},{8,12},{9,13},{1... | collective-permute-start | bytes 3145736 | tf_op jit(solution)/shard_map/ppermute | solution.py:26
  84.3 8.7 %collective-permute-start.18 = (bf16[128,1024]{1,0:T(8,128)(2,1)S(1)}, bf16[128,1024]{1,0:T(8,128)(2,1)S(1)}, u32[]{:S(2)}, u32[]{:S(2)}) collective-permute-start(bf16[128,1024]{1,0:T(8,128)(2,1)S(1)} %get-tuple-element.72), channel_id=1, source_target_pairs={{4,0},{5,1},{6,2},{7,3},{8,4},{9,5},{10,6},{11,7},{12,8},{13,9},{1... | collective-permute-start | bytes 786440 | tf_op jit(solution)/shard_map/ppermute | solution.py:26
  89.0 6.8 %collective-permute-start.20 = (bf16[128,1024]{1,0:T(8,128)(2,1)S(1)}, bf16[128,1024]{1,0:T(8,128)(2,1)S(1)}, u32[]{:S(2)}, u32[]{:S(2)}) collective-permute-start(bf16[128,1024]{1,0:T(8,128)(2,1)S(1)} %get-tuple-element.75), channel_id=1, source_target_pairs={{0,2},{1,3},{2,0},{3,1},{4,6},{5,7},{6,4},{7,5},{8,10},{9,11},{10,... | collective-permute-start | bytes 786440 | tf_op jit(solution)/shard_map/ppermute | solution.py:31
  90.8 15.1 %copy-start.13 = (bf16[512,1152]{1,0:T(8,128)(2,1)S(1)}, bf16[512,1152]{1,0:T(8,128)(2,1)}, u32[]{:S(2)}) copy-start(bf16[512,1152]{1,0:T(8,128)(2,1)} %get-tuple-element.64.band_ref) | copy-start | bytes 3538948
  90.8 15.1 %collective-permute-start.21 = (bf16[128,1024]{1,0:T(8,128)(2,1)S(1)}, bf16[128,1024]{1,0:T(8,128)(2,1)S(1)}, u32[]{:S(2)}, u32[]{:S(2)}) collective-permute-start(bf16[128,1024]{1,0:T(8,128)(2,1)S(1)} %get-tuple-element.76), channel_id=1, source_target_pairs={{0,3},{1,2},{2,1},{3,0},{4,7},{5,6},{6,5},{7,4},{8,11},{9,10},{10,... | collective-permute-start | bytes 786440 | tf_op jit(solution)/shard_map/ppermute | solution.py:31
  93.4 15.1 %collective-permute-start.22 = (bf16[128,1024]{1,0:T(8,128)(2,1)S(1)}, bf16[128,1024]{1,0:T(8,128)(2,1)S(1)}, u32[]{:S(2)}, u32[]{:S(2)}) collective-permute-start(bf16[128,1024]{1,0:T(8,128)(2,1)S(1)} %get-tuple-element.78), channel_id=1, source_target_pairs={{0,2},{1,3},{2,0},{3,1},{4,6},{5,7},{6,4},{7,5},{8,10},{9,11},{10,... | collective-permute-start | bytes 786440 | tf_op jit(solution)/shard_map/ppermute | solution.py:31
  95.7 21.1 %collective-permute-start.23 = (bf16[128,1024]{1,0:T(8,128)(2,1)S(1)}, bf16[128,1024]{1,0:T(8,128)(2,1)S(1)}, u32[]{:S(2)}, u32[]{:S(2)}) collective-permute-start(bf16[128,1024]{1,0:T(8,128)(2,1)S(1)} %get-tuple-element.79), channel_id=1, source_target_pairs={{0,3},{1,2},{2,1},{3,0},{4,7},{5,6},{6,5},{7,4},{8,11},{9,10},{10,... | collective-permute-start | bytes 786440 | tf_op jit(solution)/shard_map/ppermute | solution.py:31
  107.8 9.8 %collective-permute-start.24 = (bf16[128,1024]{1,0:T(8,128)(2,1)S(1)}, bf16[128,1024]{1,0:T(8,128)(2,1)S(1)}, u32[]{:S(2)}, u32[]{:S(2)}) collective-permute-start(bf16[128,1024]{1,0:T(8,128)(2,1)S(1)} %get-tuple-element.81), channel_id=1, source_target_pairs={{0,2},{1,3},{2,0},{3,1},{4,6},{5,7},{6,4},{7,5},{8,10},{9,11},{10,... | collective-permute-start | bytes 786440 | tf_op jit(solution)/shard_map/ppermute | solution.py:31
  108.5 16.9 %collective-permute-start.25 = (bf16[128,1024]{1,0:T(8,128)(2,1)S(1)}, bf16[128,1024]{1,0:T(8,128)(2,1)S(1)}, u32[]{:S(2)}, u32[]{:S(2)}) collective-permute-start(bf16[128,1024]{1,0:T(8,128)(2,1)S(1)} %get-tuple-element.82), channel_id=1, source_target_pairs={{0,3},{1,2},{2,1},{3,0},{4,7},{5,6},{6,5},{7,4},{8,11},{9,10},{10,... | collective-permute-start | bytes 786440 | tf_op jit(solution)/shard_map/ppermute | solution.py:31
  108.5 28.4 %collective-permute-start.29 = (bf16[256,1024]{1,0:T(8,128)(2,1)S(1)}, bf16[256,1024]{1,0:T(8,128)(2,1)S(1)}, u32[]{:S(2)}, u32[]{:S(2)}) collective-permute-start(bf16[256,1024]{1,0:T(8,128)(2,1)S(1)} %get-tuple-element.88), channel_id=1, source_target_pairs={{0,1},{1,0},{2,3},{3,2},{4,5},{5,4},{6,7},{7,6},{8,9},{9,8},{10,11... | collective-permute-start | bytes 1572872 | tf_op jit(solution)/shard_map/ppermute | solution.py:31
  127.4 18.5 %collective-permute-start.26 = (bf16[256,1024]{1,0:T(8,128)(2,1)S(1)}, bf16[256,1024]{1,0:T(8,128)(2,1)S(1)}, u32[]{:S(2)}, u32[]{:S(2)}) collective-permute-start(bf16[256,1024]{1,0:T(8,128)(2,1)S(1)} %get-tuple-element.83), channel_id=1, source_target_pairs={{0,1},{1,0},{2,3},{3,2},{4,5},{5,4},{6,7},{7,6},{8,9},{9,8},{10,11... | collective-permute-start | bytes 1572872 | tf_op jit(solution)/shard_map/ppermute | solution.py:31
  136.9 7.5 %collective-permute-start.27 = (bf16[128,1024]{1,0:T(8,128)(2,1)S(1)}, bf16[128,1024]{1,0:T(8,128)(2,1)S(1)}, u32[]{:S(2)}, u32[]{:S(2)}) collective-permute-start(bf16[128,1024]{1,0:T(8,128)(2,1)S(1)} %get-tuple-element.85), channel_id=1, source_target_pairs={{0,2},{1,3},{2,0},{3,1},{4,6},{5,7},{6,4},{7,5},{8,10},{9,11},{10,... | collective-permute-start | bytes 786440 | tf_op jit(solution)/shard_map/ppermute | solution.py:31
  136.9 8.9 %collective-permute-start.28 = (bf16[128,1024]{1,0:T(8,128)(2,1)S(1)}, bf16[128,1024]{1,0:T(8,128)(2,1)S(1)}, u32[]{:S(2)}, u32[]{:S(2)}) collective-permute-start(bf16[128,1024]{1,0:T(8,128)(2,1)S(1)} %get-tuple-element.86), channel_id=1, source_target_pairs={{0,3},{1,2},{2,1},{3,0},{4,7},{5,6},{6,5},{7,4},{8,11},{9,10},{10,... | collective-permute-start | bytes 786440 | tf_op jit(solution)/shard_map/ppermute | solution.py:31
  (3 other events, 2.8 us)

commit v5 on v4

v5 whole, which is shorter than its diff:
```python
import functools

import jax
import jax.numpy as jnp
from jax import lax
from jax.experimental import pallas as pl
from jax.experimental.pallas import tpu as pltpu
from jax.sharding import PartitionSpec as P

G = 4
CHUNKS = 2
F32 = jnp.float32
BF16 = jnp.bfloat16
MIB = 1024 * 1024
LANES = 128
SMEM = pl.BlockSpec(memory_space=pltpu.SMEM)
VMEM = pl.BlockSpec(memory_space=pltpu.VMEM)
ANY = pl.BlockSpec(memory_space=pl.ANY)


def moved(value, steps, only=None):
    count = lax.axis_size("slab")
    first, last = max(0, -steps), min(count, count - steps)
    pairs = [(i, i + steps) for i in range(first, last) if only is None or i % G == only]
    return lax.ppermute(value, "slab", pairs)


def swapped(value, bits):
    count = lax.axis_size("slab")
    return lax.ppermute(value, "slab", [(i, i ^ bits) for i in range(count)])


def direct(chunk, groups, arrays, skip=()):
    found = []
    for group, array in zip(groups, arrays):
        (m,) = group
        if m not in skip:
            found.append((chunk, m, array if m == 0 else swapped(array, m), 0))
    return found


def in_two(chunk, pair, after=None):
    side = pair.shape[0] // 2
    over = swapped(pair, 2)
    if after is not None:
        over = lax.optimization_barrier((over, after))[0]
    return [(chunk, 2, over, 0), (chunk, 3, swapped(over[side:], 1), 0)]


def call(kernel, us, *, results, vmem=16, **how):
    return pl.pallas_call(
        kernel,
        out_shape=results,
        compiler_params=pltpu.CompilerParams(vmem_limit_bytes=vmem * MIB),
        cost_estimate=pl.CostEstimate(flops=int(us * 1.15e9), bytes_accessed=1000, transcendentals=0),
        **how,
    )


def value(shape, dtype):
    return jax.ShapeDtypeStruct(shape, dtype)


def far(array):
    return pltpu.with_memory_space_constraint(array, pltpu.HBM)


def across(shape, tile):
    block = shape[:-1] + (tile,)
    return pl.BlockSpec(block, lambda i: (0,) * (len(shape) - 1) + (i,))


def lanes(array, tile, parts):
    block = array.shape[:-1] + (tile,)
    zeros = (0,) * (len(block) - 1)
    return [pl.BlockSpec(block, lambda i, j=j: zeros + (i * parts + j,)) for j in range(parts)]


def piece_specs(pieces, side, tile):
    return [pl.BlockSpec((side, tile), lambda i, at=at: (at, i)) for _, _, _, at in pieces]


def keys_of(pieces):
    return [(chunk, m) for chunk, m, _, _ in pieces]


def arrays_of(pieces):
    return [array for _, _, array, _ in pieces]


def group_results(groups, side, cols, tile, space=None):
    shapes = [(len(group) * side, cols) for group in groups]
    results = [space(shape, BF16) if space else value(shape, BF16) for shape in shapes]
    return dict(out_specs=[across(shape, tile) for shape in shapes], results=results)


def row_of(place, m, chunk):
    return CHUNKS * jnp.bitwise_xor(place, m) + chunk


CAST_GROUPS = ((0, (0,)), (0, (1,)), (0, (2,)), (0, (3,)), (1, (0,)), (1, (1,)), (1, (2, 3)))


def cast_kernel(parts, here_ref, *refs):
    vol_refs, out_refs = refs[:parts], refs[parts:]
    rows = CHUNKS * G
    depth = vol_refs[0].shape[0] // rows
    place = lax.rem(here_ref[0], G)
    for j, vol_ref in enumerate(vol_refs):
        at = pl.ds(j * LANES, LANES)
        ends = jnp.concatenate([vol_ref[:rows, :], vol_ref[(depth - 1) * rows :, :]], axis=0).astype(BF16)
        for (c, group), out_ref in zip(CAST_GROUPS, out_refs):
            for n, m in enumerate(group):
                spot = pl.ds(row_of(place, m, c), depth, stride=rows)
                out_ref[n * depth : (n + 1) * depth, at] = vol_ref[spot, :].astype(BF16)
            if out_ref.shape[0] > len(group) * depth:
                out_ref[len(group) * depth :, at] = ends


def cast_rows(here, volume):
    depth, rows, cols = volume.shape
    flat = far(volume.reshape(depth * rows, cols))
    parts = 2
    shapes = [(len(g) * depth + (2 * rows if c == 0 and g[0] % 2 else 0), cols) for c, g in CAST_GROUPS]
    return call(
        functools.partial(cast_kernel, parts),
        3.5,
        grid=(cols // (LANES * parts),),
        in_specs=[SMEM] + lanes(flat, LANES, parts),
        out_specs=[across(shape, LANES * parts) for shape in shapes],
        results=[value(shape, BF16) for shape in shapes],
    )(here, *[flat] * parts)


def pack_kernel(here_ref, *refs):
    in_refs, (all_ref, last_ref) = refs[:G], refs[-2:]
    side = in_refs[0].shape[0]
    for m in range(G):
        all_ref[m * side : (m + 1) * side] = in_refs[m][:side]
    spot = jnp.bitwise_xor(lax.rem(here_ref[0], G), G - 1)
    last_ref[:side] = all_ref[pl.ds(pl.multiple_of(spot * side, side), side), :]
    if last_ref.shape[0] > side:
        all_ref[G * side :] = in_refs[G - 1][side:]
        last_ref[side:] = in_refs[G - 1][side:]


def pack(here, pieces, more, *tokens):
    pieces = sorted(pieces, key=lambda piece: piece[1])
    side, cols = pieces[0][2].shape
    tile = 512
    shapes = [(G * side + more, cols), (side + more, cols)]
    specs = piece_specs(pieces, side, tile)
    if more:
        specs = [across(array.shape, tile) for array in arrays_of(pieces)]
    return call(
        pack_kernel,
        1,
        grid=(cols // tile,),
        in_specs=[SMEM] + specs + [ANY] * len(tokens),
        out_specs=[across(shape, tile) for shape in shapes],
        results=[value(shape, BF16) for shape in shapes],
    )(here, *arrays_of(pieces), *tokens)


SPLIT_GROUPS = (((0, 1), (1, 1)), ((0, 0),), ((0, 2),), ((0, 3),), ((1, 0),), ((1, 2), (1, 3)))


def split_kernel(here_ref, own_ref, got_ref, *refs):
    out_refs, wide = refs[-len(SPLIT_GROUPS) - 1 : -1], refs[-1]
    depth, rows, cols = own_ref.shape
    place = lax.rem(here_ref[0], G)

    def fill(ref):
        for j in range(cols // LANES):
            wide[j] = ref[:, :, j * LANES : (j + 1) * LANES].astype(F32).reshape(wide.shape[1:])

    @pl.when(place == G - 1)
    def _():
        fill(got_ref)

    @pl.when(place != G - 1)
    def _():
        fill(own_ref)

    for j in range(cols // LANES):
        at = pl.ds(j * LANES, LANES)
        for group, out_ref in zip(SPLIT_GROUPS, out_refs):
            for n, (c, m) in enumerate(group):
                spot = pl.ds(row_of(place, m, c), depth, stride=rows)
                out_ref[n * depth : (n + 1) * depth, at] = wide.at[j][spot, :].astype(BF16)


def split_rows(here, own, got, *tokens):
    depth, rows, cols = own.shape
    tile = 512
    block = across(own.shape, tile)
    return call(
        split_kernel,
        4,
        grid=(cols // tile,),
        in_specs=[SMEM, block, block] + [ANY] * len(tokens),
        scratch_shapes=[pltpu.VMEM((tile // LANES, depth * rows, LANES), F32)],
        **group_results(SPLIT_GROUPS, depth, cols, tile, pltpu.HBM),
    )(here, far(own), got, *tokens)


def patch_kernel(slabs, here_ref, cover_ref, offset_ref, *refs):
    w_ref, *refs = refs
    end_refs, (vol_ref, sino_ref, *v_refs), (r_ref, tv_ref) = refs[:4], refs[4 : 6 + len(CAST_GROUPS)], refs[-10:-8]
    v, s, r, wide, tv, slices, fixed, sem = refs[-8:]
    depth, rows, cols = sino_ref.shape
    place = lax.rem(here_ref[0], G)
    near, next_level, far_end, last_level = (ref[...] for ref in end_refs)
    low = jnp.where(place == 0, last_level, jnp.where(place == 2, far_end, near))[rows:].astype(F32)
    high = jnp.where(place == G - 1, next_level, jnp.where(place == 1, far_end, near))[:rows].astype(F32)

    for n, z in enumerate((0, depth - 2)):
        pltpu.make_async_copy(vol_ref.at[z : z + 2], slices.at[2 * n : 2 * n + 2], sem.at[n]).start()
    for n, z in enumerate((0, depth - 2)):
        pltpu.make_async_copy(vol_ref.at[z : z + 2], slices.at[2 * n : 2 * n + 2], sem.at[n]).wait()
    fixed[0] = tv_slice(slices[0], slices[1], tv_below(low, slices[0]))[0]
    fixed[1] = tv_slice(slices[3], high, tv_below(slices[2], slices[3]))[0]
    for n, z in enumerate((0, depth - 1)):
        pltpu.make_async_copy(fixed.at[n], tv_ref.at[z], sem.at[n]).start()
    for n, z in enumerate((0, depth - 1)):
        pltpu.make_async_copy(fixed.at[n], tv_ref.at[z], sem.at[n]).wait()

    @pl.when(here_ref[0] == slabs - 1)
    def _():
        for i, (ref, (_, group)) in enumerate(zip(v_refs, CAST_GROUPS)):
            for n, m in enumerate(group):
                at = CAST_GROUPS[i][0] * G + m
                pltpu.make_async_copy(ref.at[n * depth : (n + 1) * depth], v.at[at], sem.at[5 + at]).start()
        pltpu.make_async_copy(sino_ref, s, sem.at[3]).start()
        pltpu.make_async_copy(tv_ref, tv, sem.at[4]).start()
        pltpu.make_async_copy(sino_ref, s, sem.at[3]).wait()
        pltpu.make_async_copy(tv_ref, tv, sem.at[4]).wait()
        for at in range(CHUNKS * G):
            pltpu.make_async_copy(v_refs[0].at[:depth], v.at[at], sem.at[5 + at]).wait()
        block = w_ref[offset_ref[slabs - 1, 0]]
        block = jnp.where(cover_ref[slabs - 1, 0] == 1, block, jnp.zeros_like(block))
        turned = block.astype(F32).T.astype(BF16)

        def column(j, _):
            at = pl.ds(pl.multiple_of(j * LANES, LANES), LANES)
            wide[0] = s[:, :, at].astype(F32).reshape(wide.shape[1:])
            wide[1] = tv[:, :, at].reshape(wide.shape[1:])
            for c in range(CHUNKS):
                for m in range(G):
                    spot = pl.ds(CHUNKS * ((G - 1) ^ m) + c, depth, stride=rows)
                    seen = jnp.dot(block, v[c * G + m, :, at], preferred_element_type=F32)
                    resid = (seen - wide.at[0][spot, :]).astype(BF16)
                    wide.at[0][spot, :] = resid.astype(F32)
                    wide.at[1][spot, :] += jnp.dot(turned, resid, preferred_element_type=F32)
            r[:, :, at] = wide[0].reshape(depth, rows, LANES).astype(BF16)
            tv[:, :, at] = wide[1].reshape(depth, rows, LANES)
            return 0

        lax.fori_loop(0, cols // LANES, column, 0)
        pltpu.make_async_copy(r, r_ref, sem.at[3]).start()
        pltpu.make_async_copy(tv, tv_ref, sem.at[4]).start()
        pltpu.make_async_copy(r, r_ref, sem.at[3]).wait()
        pltpu.make_async_copy(tv, tv_ref, sem.at[4]).wait()


def patch(here, coverage, offsets, weights, ends, volume, sinogram, vols, tv, *tokens):
    slabs = coverage.shape[0]
    depth, rows, cols = sinogram.shape
    edges = [pl.BlockSpec((2 * rows, cols), lambda i, last=end.shape[0] // (2 * rows) - 1: (last, 0)) for end in ends]
    return call(
        functools.partial(patch_kernel, slabs),
        3,
        vmem=32,
        grid=(1,),
        in_specs=[SMEM, SMEM, SMEM, pl.BlockSpec(weights.shape, lambda i: (0, 0, 0))]
        + edges
        + [ANY] * (3 + len(vols) + len(tokens)),
        out_specs=[ANY, ANY],
        results=[pltpu.HBM(sinogram.shape, BF16), pltpu.HBM(volume.shape, F32)],
        input_output_aliases={10 + len(vols): 1},
        scratch_shapes=[
            pltpu.VMEM((CHUNKS * G, depth, cols), BF16),
            pltpu.VMEM(sinogram.shape, BF16),
            pltpu.VMEM(sinogram.shape, BF16),
            pltpu.VMEM((2, depth * rows, LANES), F32),
            pltpu.VMEM(volume.shape, F32),
            pltpu.VMEM((4, rows, cols), F32),
            pltpu.VMEM((2, rows, cols), F32),
            pltpu.SemaphoreType.DMA((5 + CHUNKS * G,)),
        ],
    )(here, coverage, offsets, weights, *ends, far(volume), far(sinogram), *vols, far(tv), *tokens)


def join_kernel(slabs, keys, here_ref, *refs):
    in_refs, (last_ref, out_ref, wide) = refs[: len(keys)], refs[-3:]
    depth, rows, cols = out_ref.shape
    place = lax.rem(here_ref[0], G)
    last = here_ref[0] == slabs - 1

    @pl.when(last)
    def _():
        at = pl.ds(pl.multiple_of(pl.program_id(0) * cols, cols), cols)
        pltpu.sync_copy(last_ref.at[:, :, at], out_ref)

    @pl.when(jnp.logical_not(last))
    def _():
        for j in range(cols // LANES):
            at = pl.ds(j * LANES, LANES)
            for (c, m), ref in zip(keys, in_refs):
                spot = pl.ds(row_of(place, m, c), depth, stride=rows)
                wide.at[j][spot, :] = ref[:, at].astype(F32)
            out_ref[:, :, at] = wide[j].reshape(depth, rows, LANES).astype(out_ref.dtype)


def join_rows(here, slabs, pieces, last):
    depth, rows, cols = last.shape
    tile = 512
    return call(
        functools.partial(join_kernel, slabs, keys_of(pieces)),
        2.6,
        grid=(cols // tile,),
        in_specs=[SMEM] + piece_specs(pieces, depth, tile) + [ANY],
        out_specs=across((depth, rows, cols), tile),
        results=value((depth, rows, cols), BF16),
        scratch_shapes=[pltpu.VMEM((tile // LANES, depth * rows, LANES), F32)],
    )(here, *arrays_of(pieces), far(last))


def finish_kernel(keys, here_ref, tv_ref, *refs):
    in_refs, (out_ref, wide) = refs[: len(keys)], refs[-2:]
    depth, rows, cols = out_ref.shape
    place = lax.rem(here_ref[0], G)
    for j in range(cols // LANES):
        at = pl.ds(j * LANES, LANES)
        for (c, m), ref in zip(keys, in_refs):
            spot = pl.ds(row_of(place, m, c), depth, stride=rows)
            wide.at[j][spot, :] = ref[:, at].astype(F32)
        out_ref[:, :, at] = tv_ref[:, :, at] + wide[j].reshape(depth, rows, LANES)


def finish(here, tv, pieces):
    depth, rows, cols = tv.shape
    tile = 256
    whole = across(tv.shape, tile)
    return call(
        functools.partial(finish_kernel, keys_of(pieces)),
        5,
        grid=(cols // tile,),
        in_specs=[SMEM, whole] + piece_specs(pieces, depth, tile),
        out_specs=whole,
        results=value((depth, rows, cols), F32),
        scratch_shapes=[pltpu.VMEM((tile // LANES, depth * rows, LANES), F32)],
    )(here, far(tv), *arrays_of(pieces))


def band_kernel(slabs, span, here_ref, cover_ref, offset_ref, w_ref, *refs):
    proj_ref, back_ref, turned = refs[-3:]
    side = w_ref.shape[1]
    place = lax.rem(here_ref[0], G)
    first = here_ref[0] - place
    zero = jnp.zeros((side, side), BF16)
    for i in range(w_ref.shape[0]):
        turned[i] = w_ref[i].astype(F32).T.astype(BF16)

    def block(ref, i, j):
        k = j - i
        known, step = jnp.clip(i, 0, slabs - 1), jnp.clip(k, 0, span - 1)
        inside = (i >= 0) & (i < slabs) & (j >= 0) & (j < slabs) & (k >= 0) & (k < span)
        live = inside & (cover_ref[known, step] == 1)
        return jnp.where(live, ref[offset_ref[known, step]], zero)

    def slab(m):
        return first + jnp.bitwise_xor(place, m)

    def group(m):
        to = jnp.bitwise_xor(place, m)
        return first + jnp.where(to == G - 1, -1, to)

    seen = [slab(m) for m in range(G)] + [slab(m) + G for m in range(G)] + [first - 1]
    seeing = [group(m) for m in range(G)] + [group(m) - G for m in range(G)] + [first + G - 1]
    for r in range(G):
        for s in range(2 * G + 1):
            at = (pl.ds(r * side, side), pl.ds(s * side, side))
            proj_ref[at] = block(w_ref, group(r), seen[s])
            back_ref[at] = block(turned, seeing[s], slab(r))


def bands(here, coverage, offsets, weights, *tokens):
    slabs, span = coverage.shape
    side = weights.shape[1]
    shape = (G * side, (2 * G + 1) * side)
    return call(
        functools.partial(band_kernel, slabs, span),
        1.6,
        in_specs=[SMEM, SMEM, SMEM, pl.BlockSpec(weights.shape, lambda i: (0, 0, 0))] + [ANY] * len(tokens),
        grid=(1,),
        out_specs=[pl.BlockSpec(shape, lambda i: (0, 0))] * 2,
        results=[pltpu.HBM(shape, BF16)] * 2,
        scratch_shapes=[pltpu.VMEM(weights.shape, BF16)],
    )(here, coverage, offsets, weights, *tokens)


def project_kernel(keys, here_ref, band_ref, own_ref, high_ref, low_ref, *refs):
    sinos, (r_ref, down_ref) = dict(zip(keys, refs)), refs[-2:]
    side = down_ref.shape[0]
    n = G * side
    seen = jnp.concatenate([own_ref[:n], high_ref[:n], low_ref[:side]], axis=0)
    total = jnp.dot(band_ref[...], seen, preferred_element_type=F32)
    for (_, m), ref in sinos.items():
        at = slice(m * side, (m + 1) * side)
        r_ref[at, :] = (total[at] - ref[...].astype(F32)).astype(BF16)
    spot = jnp.bitwise_xor(lax.rem(here_ref[0], G), G - 1)
    down_ref[...] = r_ref[pl.ds(pl.multiple_of(spot * side, side), side), :]


def project(here, band, own, high, low, pieces, *tokens):
    n, side = band.shape[0], band.shape[0] // G
    cols = own.shape[1]
    tile = 512
    one = across((side, cols), tile)
    return call(
        functools.partial(project_kernel, keys_of(pieces)),
        3,
        grid=(cols // tile,),
        in_specs=[SMEM, pl.BlockSpec(band.shape, lambda i: (0, 0))]
        + [across(array.shape, tile) for array in (own, high, low)]
        + piece_specs(pieces, side, tile)
        + [ANY] * len(tokens),
        out_specs=[across((n, cols), tile), one],
        results=[value((n, cols), BF16), value((side, cols), BF16)],
    )(here, band, own, high, low, *arrays_of(pieces), *tokens)


def put_groups(groups, block, out_refs, before_ref, side):
    for group, out_ref in zip(groups, out_refs):
        for n, m in enumerate(group):
            out_ref[n * side : (n + 1) * side] = before_ref[...] if m is None else block(m)


def deal_kernel(groups, here_ref, r_ref, high_ref, *refs):
    side = high_ref.shape[0]
    place = lax.rem(here_ref[0], G)

    def block(m):
        last = jnp.bitwise_xor(place, m) == G - 1
        return jnp.where(last, high_ref[...], r_ref[m * side : (m + 1) * side])

    put_groups(groups, block, refs[-len(groups) :], refs[0], side)


def deal(here, groups, resid, high, before, *tokens):
    side, cols = high.shape
    tile = 512
    one = across((side, cols), tile)
    return call(
        functools.partial(deal_kernel, groups),
        1,
        grid=(cols // tile,),
        in_specs=[SMEM, across(resid.shape, tile), one] + [one] * len(before) + [ANY] * len(tokens),
        **group_results(groups, side, cols, tile),
    )(here, resid, high, *before, *tokens)


def back_kernel(groups, band_ref, own_ref, low_ref, high_ref, *refs):
    side = high_ref.shape[0]
    seeing = jnp.concatenate([own_ref[...], low_ref[...], high_ref[...]], axis=0)
    total = jnp.dot(band_ref[...], seeing, preferred_element_type=F32)
    put_groups(groups, lambda m: total[m * side : (m + 1) * side].astype(BF16), refs[-len(groups) :], refs[0], side)


def back(groups, band, own, low, high, before, *tokens):
    side, cols = high.shape
    tile = 512
    one = across((side, cols), tile)
    many = across(own.shape, tile)
    return call(
        functools.partial(back_kernel, groups),
        3,
        grid=(cols // tile,),
        in_specs=[pl.BlockSpec(band.shape, lambda i: (0, 0)), many, many, one]
        + [one] * len(before)
        + [ANY] * len(tokens),
        **group_results(groups, side, cols, tile),
    )(band, own, low, high, *before, *tokens)


def tv_flux(cur, above):
    rows, cols = cur.shape
    row = lax.broadcasted_iota(jnp.int32, (rows, cols), 0)
    col = lax.broadcasted_iota(jnp.int32, (rows, cols), 1)
    dz = above - cur
    dy = jnp.where(row == rows - 1, 0.0, pltpu.roll(cur, rows - 1, 0)) - cur
    dx = jnp.where(col == cols - 1, 0.0, pltpu.roll(cur, cols - 1, 1)) - cur
    scale = 0.5 * lax.rsqrt(dz * dz + dy * dy + dx * dx + 0.25)
    return dz * scale, dy * scale, dx * scale


def tv_below(cur, above):
    return tv_flux(cur, above)[0]


def tv_slice(cur, above, below_flux):
    rows, cols = cur.shape
    row = lax.broadcasted_iota(jnp.int32, (rows, cols), 0)
    col = lax.broadcasted_iota(jnp.int32, (rows, cols), 1)
    fz, fy, fx = tv_flux(cur, above)
    sides = 0.5 * cur * lax.rsqrt(cur * cur + 0.25)
    fy_low = jnp.where(row == 0, sides, pltpu.roll(fy, 1, 0))
    fx_low = jnp.where(col == 0, sides, pltpu.roll(fx, 1, 1))
    return (below_flux - fz) + (fy_low - fy) + (fx_low - fx), fz


def tv_kernel(next_ref, vol_ref, *refs):
    out_ref, flux_ref = refs[-2:]
    deep = vol_ref.shape[0]

    @pl.when(pl.program_id(0) == 0)
    def _():
        flux_ref[...] = jnp.zeros_like(flux_ref)

    def body(z, flux):
        out_ref[z], flux = tv_slice(vol_ref[z], vol_ref[z + 1], flux)
        return flux

    flux = lax.fori_loop(0, deep - 1, body, flux_ref[...], unroll=5)
    out_ref[deep - 1], flux_ref[...] = tv_slice(vol_ref[deep - 1], next_ref[0], flux)


def half_tv(volume, *tokens):
    depth, rows, cols = volume.shape
    deep = 16
    body = pl.BlockSpec((deep, rows, cols), lambda i: (i, 0, 0))
    after = pl.BlockSpec((1, rows, cols), lambda i: (jnp.minimum((i + 1) * deep, depth - 1), 0, 0))
    return call(
        tv_kernel,
        9,
        grid=(depth // deep,),
        in_specs=[after, body] + [ANY] * len(tokens),
        out_specs=body,
        results=pltpu.HBM(volume.shape, F32),
        scratch_shapes=[pltpu.VMEM((rows, cols), F32)],
    )(far(volume), far(volume), *tokens)


def local(volume, sinogram, weights, coverage, offsets):
    slabs = lax.axis_size("slab")
    here = lax.axis_index("slab").astype(jnp.int32).reshape(1)
    depth, rows, cols = volume.shape
    single = ((0,), (1,), (2,), (3,))

    vols = cast_rows(here, volume)
    got = moved(lax.optimization_barrier((sinogram, vols[0]))[0], G, only=G - 1)
    pieces0 = direct(0, single, vols[:G])
    tv = half_tv(volume, vols[0])
    own0, edge0 = pack(here, pieces0, 2 * rows, tv)
    high0, low0 = moved(own0, -G), moved(edge0, G)

    band_p, band_b = bands(here, coverage, offsets, weights, own0)
    sino = split_rows(here, sinogram, got, own0)
    pieces1 = direct(1, ((0,), (1,)), vols[G : G + 2]) + in_two(1, vols[G + 2], sino[0])
    own1, edge1 = pack(here, pieces1, 0, sino[0])
    high1, low1 = moved(own1, -G), moved(edge1, G)

    sino_core = swapped(sino[0], 1)
    sinos0 = [(0, 1, sino_core, 0)] + direct(0, ((0,), (2,), (3,)), sino[1:4])

    resid0, down0 = project(here, band_p, own0, high0, low0, sinos0, own1, low1)
    from_low0, from_high0 = moved(resid0, G), moved(down0, -G)
    ends = [pieces0[1][2], high0, pieces0[3][2], low0]
    r_last, tv = patch(here, coverage, offsets, weights, ends, volume, sinogram, vols, tv, resid0)
    dealt0 = deal(here, ((0,), (1,), (2, 3)), resid0, from_high0, [], r_last)
    over0 = swapped(dealt0[2], 2)

    sinos1 = [(1, 1, sino_core, 1)] + direct(1, ((0,),), sino[4:5]) + in_two(1, sino[5], dealt0[0])
    resid1, down1 = project(here, band_p, own1, high1, low1, sinos1, dealt0[0])
    from_low1, from_high1 = moved(resid1, G), moved(down1, -G)
    backs0 = back(((0,), (1,), (2, 3)), band_b, resid0, from_low0, from_high0, [], over0)
    back_pieces = direct(0, ((0,),), backs0[:1]) + in_two(0, backs0[2])
    dealt1 = deal(here, ((0,), (None, 1), (2, 3)), resid1, from_high1, [dealt0[1]], backs0[0])
    over1 = swapped(dealt1[2], 2)
    backs1 = back(((0,), (None, 1), (2,), (3,)), band_b, resid1, from_low1, from_high1, [backs0[1]], back_pieces[2][2])

    far_core = swapped(jnp.concatenate([over0[depth:], over1[depth:]], axis=0), 1)
    near_core = swapped(dealt1[1], 1)
    resid_pieces = []
    for c, (dealt, over) in enumerate(((dealt0, over0), (dealt1, over1))):
        resid_pieces += [(c, 0, dealt[0], 0), (c, 1, near_core, c), (c, 2, over, 0), (c, 3, far_core, c)]
    residual = join_rows(here, slabs, resid_pieces, r_last)

    back_core = swapped(backs1[1], 1)
    back_pieces += [(0, 1, back_core, 0), (1, 1, back_core, 1)]
    back_pieces += direct(1, ((0,), (2,), (3,)), [backs1[0], backs1[2], backs1[3]])
    gradient = finish(here, tv, back_pieces)
    return (gradient, residual)


def solution(mesh):
    placed = (P("slab", "grp", None), P("slab", "grp", None), P(), P(), P())
    return jax.shard_map(
        local,
        mesh=mesh,
        in_specs=placed,
        out_specs=(P("slab", "grp", None), P("slab", "grp", None)),
        check_vma=False,
    )
```

time: 158 us -> 153 us (0.968)
  the two profiles are of different devices: /device:TPU:29 before, /device:TPU:1 now
where the time goes in v5:
time: 153 us
  waiting for transfers between devices  51.8 us (34%)
  starting transfers between devices  48.2 us (32%)
  Pallas kernels  43.2 us (28%)
  local copies, waits for them, and re-layouts  8.35 us (5%)
    ppermute x20, waiting for transfers between devices, swapped(): return lax.ppermute(value, 'slab', [(i, i ^ bits) for i in range(count)])  35.1 us
    ppermute x20, starting transfers between devices, swapped(): return lax.ppermute(value, 'slab', [(i, i ^ bits) for i in range(count)])  26.2 us
    ppermute x9, starting transfers between devices, moved(): return lax.ppermute(value, 'slab', pairs)  22 us
    ppermute x9, waiting for transfers between devices, moved(): return lax.ppermute(value, 'slab', pairs)  16.7 us
    pallas_call x1, Pallas kernels, half_tv(): call(tv_kernel, 9, grid=(depth // deep,), in_specs=[after, body] + [ANY]...  9.9 us
    unnamed x46, local copies, waits for them, and re-layouts  8.26 us
    pallas_call x2, Pallas kernels, project(): call(functools.partial(project_kernel, keys_of(pieces)), 3, grid=(cols //...  6.07 us
    pallas_call x1, Pallas kernels, finish(): call(functools.partial(finish_kernel, keys_of(pieces)), 5, grid=(cols //...  5.32 us
  transfers between devices with their start and end apart: 29, of which 9 were waited for; matrix products, arithmetic and copies ran while one was open for 0% of the time, Pallas kernels for 22%

profile of v5, /device:TPU:1, one launch (start us, length us, event | category | flops | bytes accessed | tf_op | source)
XLA Modules:
  0.0 152.5 jit_solution(4955673073534660750)
XLA Ops:
  0.6 3.7 %shard_map.68 = (bf16[128,1024]{1,0:T(8,128)(2,1)S(1)}, bf16[144,1024]{1,0:T(8,128)(2,1)S(1)}, bf16[128,1024]{1,0:T(8,128)(2,1)S(1)}, bf16[144,1024]{1,0:T(8,128...) custom-call(s32[1]{0:T(128)} %bitcast.here_ref, ...), custom_call_target="tpu_custom_call" | custom-call | flops 4024999936 | bytes 1000 | tf_op jit(solution)/shard_map/pallas_call | solution.py:125
  4.4 0.8 collective-permute-start.5
  5.3 4.9 %collective-permute-start.2 = (bf16[144,1024]{1,0:T(8,128)(2,1)S(1)}, bf16[144,1024]{1,0:T(8,128)(2,1)S(1)}, u32[]{:S(2)}, u32[]{:S(2)}) collective-permute-start(bf16[144,1024]{1,0:T(8,128)(2,1)S(1)} %get-tuple-element.46.refs_10_), channel_id=1, source_target_pairs={{0,3},{1,2},{2,1},{3,0},{4,7},{5,6},{6,5},{7,4},{8,11},{9,10},{10,... | collective-permute-start | bytes 884744 | tf_op jit(solution)/shard_map/ppermute | solution.py:30
  10.3 1.5 collective-permute-start.10
  11.7 9.9 %shard_map.69.refs_4_.refs_14_ = f32[128,8,1024]{2,1,0:T(8,128)} custom-call(f32[128,8,1024]{2,1,0:T(8,128)} %refs_5_.1, f32[128,8,1024]{2,1,0:T(8,128)} %refs_5_.1, bf16[128,1024]{1,0:T(8,128)(2,1)S(1)} %get-tuple-element.44.refs_0_.refs_7_), custom_call_target="tpu_custom_call" | custom-call | flops 10350000128 | bytes 1000 | tf_op jit(solution)/shard_map/pallas_call | solution.py:534
  21.6 0.9 collective-permute-done.1.refs_2_
  22.6 2.2 %copy-done = f32[128,8,1024]{2,1,0:T(8,128)S(1)} copy-done((f32[128,8,1024]{2,1,0:T(8,128)S(1)}, f32[128,8,1024]{2,1,0:T(8,128)}, u32[]{:S(2)}) %copy-start) | copy-done | bytes 4194328
  24.8 1.1 shard_map.70
  25.9 1.3 collective-permute-start.3
  27.2 1.6 %collective-permute-start.9 = (bf16[128,1024]{1,0:T(8,128)(2,1)S(1)}, bf16[128,1024]{1,0:T(8,128)(2,1)S(1)}, u32[]{:S(2)}, u32[]{:S(2)}) collective-permute-start(bf16[128,1024]{1,0:T(8,128)(2,1)S(1)} %get-tuple-element.50.refs_12_), channel_id=1, source_target_pairs={{0,1},{1,0},{2,3},{3,2},{4,5},{5,4},{6,7},{7,6},{8,9},{9,8},{10,11... | collective-permute-start | bytes 786440 | tf_op jit(solution)/shard_map/ppermute | solution.py:30
  28.8 3.6 %shard_map.72 = (bf16[256,1024]{1,0:T(8,128)(2,1)}, bf16[128,1024]{1,0:T(8,128)(2,1)}, bf16[128,1024]{1,0:T(8,128)(2,1)}, bf16[128,1024]{1,0:T(8,128)(2,1)}, bf1...) custom-call(s32[1]{0:T(128)} %bitcast.here_ref, bf16[128,8,1024]{2,1,0:T(8,128)(2,1)} %refs_6_.1, ...), custom_call_target="tpu_custom_call" | custom-call | flops 4600000000 | bytes 1000 | tf_op jit(solution)/shard_map/pallas_call | solution.py:197
  32.4 1.4 collective-permute-done.10.refs_2_
  33.8 1.0 collective-permute-start.11
  34.9 3.1 %collective-permute-start.4 = (bf16[144,1024]{1,0:T(8,128)(2,1)S(1)}, bf16[144,1024]{1,0:T(8,128)(2,1)S(1)}, u32[]{:S(2)}, u32[]{:S(2)}) collective-permute-start(bf16[144,1024]{1,0:T(8,128)(2,1)S(1)} %get-tuple-element.48), channel_id=1, source_target_pairs={{0,4},{1,5},{2,6},{3,7},{4,8},{5,9},{6,10},{7,11},{8,12},{9,13},{1... | collective-permute-start | bytes 884744 | tf_op jit(solution)/shard_map/ppermute | solution.py:25
  38.3 3.0 %collective-permute-start.7 = (bf16[128,1024]{1,0:T(8,128)(2,1)}, bf16[128,1024]{1,0:T(8,128)(2,1)}, u32[]{:S(2)}, u32[]{:S(2)}) collective-permute-start(bf16[128,1024]{1,0:T(8,128)(2,1)} %get-tuple-element.56), channel_id=1, source_target_pairs={{0,2},{1,3},{2,0},{3,1},{4,6},{5,7},{6,4},{7,5},{8,10},{9,11},{10,... | collective-permute-start | bytes 786440 | tf_op jit(solution)/shard_map/ppermute | solution.py:30
  41.4 1.0 copy-done.12
  42.4 0.9 shard_map.73
  43.4 1.0 copy-done.10
  44.4 4.9 %collective-permute-start.12 = (bf16[128,1024]{1,0:T(8,128)(2,1)}, bf16[128,1024]{1,0:T(8,128)(2,1)}, u32[]{:S(2)}, u32[]{:S(2)}) collective-permute-start(bf16[128,1024]{1,0:T(8,128)(2,1)} %get-tuple-element.60), channel_id=1, source_target_pairs={{0,4},{1,5},{2,6},{3,7},{4,8},{5,9},{6,10},{7,11},{8,12},{9,13},{1... | collective-permute-start | bytes 786440 | tf_op jit(solution)/shard_map/ppermute | solution.py:25
  49.4 0.9 copy-done.1
  50.3 2.7 %shard_map.71 = (bf16[512,1152]{1,0:T(8,128)(2,1)}, bf16[512,1152]{1,0:T(8,128)(2,1)}) custom-call(s32[1]{0:T(128)} %bitcast.here_ref, s32[16,6]{1,0:T(8,128)S(1)} %copy.10.cover_ref, s32[16,6]{1,0:T(8,128)S(1)} %copy.11.offset_ref, bf16[8,128,128]{2,1,0:T(8,128)(2,1)S(1)} %copy-done.1, bf16[528,1024]{1,0:T(8,128)(2,1)} %get-tuple-element.47.refs_0_.own_ref), custom_call_target="tpu_custom_call" | custom-call | flops 1840000000 | bytes 1000 | tf_op jit(solution)/shard_map/pallas_call | solution.py:392
  53.1 2.0 %collective-permute-start.19 = (bf16[256,1024]{1,0:T(8,128)(2,1)S(1)}, bf16[256,1024]{1,0:T(8,128)(2,1)S(1)}, u32[]{:S(2)}, u32[]{:S(2)}) collective-permute-start(bf16[256,1024]{1,0:T(8,128)(2,1)S(1)} %copy-done.21), channel_id=1, source_target_pairs={{0,2},{1,3},{2,0},{3,1},{4,6},{5,7},{6,4},{7,5},{8,10},{9,11},{10,... | collective-permute-start | bytes 1572872 | tf_op jit(solution)/shard_map/ppermute | solution.py:30
  55.1 1.3 collective-permute-start.18
  56.4 1.3 copy-done.14
  57.7 3.1 %shard_map.74 = (bf16[512,1024]{1,0:T(8,128)(2,1)S(1)}, bf16[128,1024]{1,0:T(8,128)(2,1)S(1)}) custom-call(s32[1]{0:T(128)} %bitcast.here_ref, bf16[512,1152]{1,0:T(8,128)(2,1)S(1)} %copy-done.14, bf16[528,1024]{1,0:T(8,128)(2,1)} %get-tuple-element.47.refs_0_.own_ref, bf16[528,1024]{1,0:T(8,128)(2,1)S(1)} %collective-permute-done.3.high_ref.refs_2_, ...), custom_call_target="tpu_custom_call" | custom-call | flops 3449999872 | bytes 1000 | tf_op jit(solution)/shard_map/pallas_call | solution.py:421
  60.8 4.1 %collective-permute-start.13 = (bf16[512,1024]{1,0:T(8,128)(2,1)S(1)}, bf16[512,1024]{1,0:T(8,128)(2,1)S(1)}, u32[]{:S(2)}, u32[]{:S(2)}) collective-permute-start(bf16[512,1024]{1,0:T(8,128)(2,1)S(1)} %get-tuple-element.61.refs_15_.r_ref.own_ref), channel_id=1, source_target_pairs={{0,4},{1,5},{2,6},{3,7},{4,8},{5,9},{6,10},{7,11},{8,12},{9,13},{1... | collective-permute-start | bytes 3145736 | tf_op jit(solution)/shard_map/ppermute | solution.py:25
  64.8 1.3 collective-permute-start.14
  66.2 2.6 %shard_map.75 = (bf16[128,8,1024]{2,1,0:T(8,128)(2,1)}, f32[128,8,1024]{2,1,0:T(8,128)}) custom-call(s32[1]{0:T(128)} %bitcast.here_ref, s32[16,6]{1,0:T(8,128)S(1)} %copy.10.cover_ref, s32[16,6]{1,0:T(8,128)S(1)} %copy.11.offset_ref, bf16[8,128,128]{2,1,0:T(8,128)(2,1)S(1)} %copy-done.2, ...), custom_call_target="tpu_custom_call", output_to_operand_aliasing={{1}: (17, {})} | custom-call | flops 3449999872 | bytes 1000 | tf_op jit(solution)/shard_map/pallas_call | solution.py:270
  68.8 16.6 %collective-permute-done.14.high_ref = bf16[128,1024]{1,0:T(8,128)(2,1)S(1)} collective-permute-done((bf16[128,1024]{1,0:T(8,128)(2,1)S(1)}, bf16[128,1024]{1,0:T(8,128)(2,1)S(1)}, u32[]{:S(2)}, u32[]{:S(2)}) %collective-permute-start.14) | collective-permute-done | bytes 262176 | tf_op jit(solution)/shard_map/ppermute | solution.py:25
  85.4 1.6 %copy-done.9 = bf16[128,8,1024]{2,1,0:T(8,128)(2,1)S(1)} copy-done((bf16[128,8,1024]{2,1,0:T(8,128)(2,1)S(1)}, bf16[128,8,1024]{2,1,0:T(8,128)(2,1)}, u32[]{:S(2)}) %copy-start.9) | copy-done | bytes 2097176
  87.4 2.8 %collective-permute-start.20 = (bf16[128,1024]{1,0:T(8,128)(2,1)S(1)}, bf16[128,1024]{1,0:T(8,128)(2,1)S(1)}, u32[]{:S(2)}, u32[]{:S(2)}) collective-permute-start(bf16[128,1024]{1,0:T(8,128)(2,1)S(1)} %slice.17), channel_id=1, source_target_pairs={{0,1},{1,0},{2,3},{3,2},{4,5},{5,4},{6,7},{7,6},{8,9},{9,8},{10,11... | collective-permute-start | bytes 786440 | tf_op jit(solution)/shard_map/ppermute | solution.py:30
  90.2 1.1 collective-permute-done.20.refs_3_
  91.3 3.0 %shard_map.78 = (bf16[512,1024]{1,0:T(8,128)(2,1)S(1)}, bf16[128,1024]{1,0:T(8,128)(2,1)S(1)}) custom-call(s32[1]{0:T(128)} %bitcast.here_ref, bf16[512,1152]{1,0:T(8,128)(2,1)S(1)} %copy-done.15, bf16[512,1024]{1,0:T(8,128)(2,1)S(1)} %copy-done.11, bf16[512,1024]{1,0:T(8,128)(2,1)S(1)} %collective-permute-done.18.high_ref, ...), custom_call_target="tpu_custom_call" | custom-call | flops 3449999872 | bytes 1000 | tf_op jit(solution)/shard_map/pallas_call | solution.py:421
  94.3 1.3 collective-permute-start.22
  95.6 4.1 %collective-permute-start.21 = (bf16[512,1024]{1,0:T(8,128)(2,1)S(1)}, bf16[512,1024]{1,0:T(8,128)(2,1)S(1)}, u32[]{:S(2)}, u32[]{:S(2)}) collective-permute-start(bf16[512,1024]{1,0:T(8,128)(2,1)S(1)} %get-tuple-element.73.own_ref.r_ref), channel_id=1, source_target_pairs={{0,4},{1,5},{2,6},{3,7},{4,8},{5,9},{6,10},{7,11},{8,12},{9,13},{1... | collective-permute-start | bytes 3145736 | tf_op jit(solution)/shard_map/ppermute | solution.py:25
  99.7 4.0 %collective-permute-done.15.refs_0_.refs_2_ = bf16[256,1024]{1,0:T(8,128)(2,1)S(1)} collective-permute-done((bf16[256,1024]{1,0:T(8,128)(2,1)S(1)}, bf16[256,1024]{1,0:T(8,128)(2,1)S(1)}, u32[]{:S(2)}, u32[]{:S(2)}) %collective-permute-start.15) | collective-permute-done | bytes 524320 | tf_op jit(solution)/shard_map/ppermute | solution.py:30
  103.7 2.0 %shard_map.77 = (bf16[128,1024]{1,0:T(8,128)(2,1)S(1)}, bf16[128,1024]{1,0:T(8,128)(2,1)S(1)}, bf16[256,1024]{1,0:T(8,128)(2,1)S(1)}) custom-call(bf16[512,1152]{1,0:T(8,128)(2,1)S(1)} %copy-done.13, bf16[512,1024]{1,0:T(8,128)(2,1)S(1)} %get-tuple-element.61.refs_15_.r_ref.own_ref, bf16[512,1024]{1,0:T(8,128)(2,1)S(1)} %collective-permute-done.13.low_ref, ...), custom_call_target="tpu_custom_call" | custom-call | flops 3449999872 | bytes 1000 | tf_op jit(solution)/shard_map/pallas_call | solution.py:476
  106.1 1.5 collective-permute-start.27
  107.6 10.7 %collective-permute-done.16.refs_1_ = bf16[256,1024]{1,0:T(8,128)(2,1)S(1)} collective-permute-done((bf16[256,1024]{1,0:T(8,128)(2,1)S(1)}, bf16[256,1024]{1,0:T(8,128)(2,1)S(1)}, u32[]{:S(2)}, u32[]{:S(2)}) %collective-permute-start.16) | collective-permute-done | bytes 524320 | tf_op jit(solution)/shard_map/ppermute | solution.py:30
  118.3 3.2 %collective-permute-start.17 = (bf16[128,1024]{1,0:T(8,128)(2,1)S(1)}, bf16[128,1024]{1,0:T(8,128)(2,1)S(1)}, u32[]{:S(2)}, u32[]{:S(2)}) collective-permute-start(bf16[128,1024]{1,0:T(8,128)(2,1)S(1)} %slice.20), channel_id=1, source_target_pairs={{0,1},{1,0},{2,3},{3,2},{4,5},{5,4},{6,7},{7,6},{8,9},{9,8},{10,11... | collective-permute-start | bytes 786440 | tf_op jit(solution)/shard_map/ppermute | solution.py:30
  121.6 7.9 %collective-permute-done.27.refs_6_ = bf16[256,1024]{1,0:T(8,128)(2,1)S(1)} collective-permute-done((bf16[256,1024]{1,0:T(8,128)(2,1)S(1)}, bf16[256,1024]{1,0:T(8,128)(2,1)S(1)}, u32[]{:S(2)}, u32[]{:S(2)}) %collective-permute-start.27) | collective-permute-done | bytes 524320 | tf_op jit(solution)/shard_map/ppermute | solution.py:30
  129.6 1.8 %collective-permute-start.28 = (bf16[256,1024]{1,0:T(8,128)(2,1)S(1)}, bf16[256,1024]{1,0:T(8,128)(2,1)S(1)}, u32[]{:S(2)}, u32[]{:S(2)}) collective-permute-start(bf16[256,1024]{1,0:T(8,128)(2,1)S(1)} %pad_maximum_fusion), channel_id=1, source_target_pairs={{0,1},{1,0},{2,3},{3,2},{4,5},{5,4},{6,7},{7,6},{8,9},{9,8},{10,11... | collective-permute-start | bytes 1572872 | tf_op jit(solution)/shard_map/ppermute | solution.py:30
  131.4 2.0 %shard_map.79 = (bf16[128,1024]{1,0:T(8,128)(2,1)S(1)}, bf16[256,1024]{1,0:T(8,128)(2,1)S(1)}, bf16[128,1024]{1,0:T(8,128)(2,1)S(1)}, bf16[128,1024]{1,0:T(8,128)(2,1)S(1)}) custom-call(bf16[512,1152]{1,0:T(8,128)(2,1)S(1)} %copy-done.13, bf16[512,1024]{1,0:T(8,128)(2,1)S(1)} %get-tuple-element.73.own_ref.r_ref, ...), custom_call_target="tpu_custom_call" | custom-call | flops 3449999872 | bytes 1000 | tf_op jit(solution)/shard_map/pallas_call | solution.py:476
  133.6 2.0 %collective-permute-start.25 = (bf16[128,1024]{1,0:T(8,128)(2,1)S(1)}, bf16[128,1024]{1,0:T(8,128)(2,1)S(1)}, u32[]{:S(2)}, u32[]{:S(2)}) collective-permute-start(bf16[128,1024]{1,0:T(8,128)(2,1)S(1)} %get-tuple-element.79), channel_id=1, source_target_pairs={{0,3},{1,2},{2,1},{3,0},{4,7},{5,6},{6,5},{7,4},{8,11},{9,10},{10,... | collective-permute-start | bytes 786440 | tf_op jit(solution)/shard_map/ppermute | solution.py:30
  135.6 2.6 %shard_map.82 = bf16[128,8,1024]{2,1,0:T(8,128)(2,1)} custom-call(s32[1]{0:T(128)} %bitcast.here_ref, bf16[128,1024]{1,0:T(8,128)(2,1)S(1)} %get-tuple-element.71.refs_4_.refs_0_, bf16[256,1024]{1,0:T(8,128)(2,1)S(1)} %collective-permute-done.26.refs_1_.refs_5_, bf16[256,1024]{1,0:T(8,128)(2,1)S(1)} %collective-permute-done.15.refs_0_.refs_2_, ...), custom_call_target="tpu_custom_call" | custom-call | flops 2990000128 | bytes 1000 | tf_op jit(solution)/shard_map/pallas_call | solution.py:318
  138.2 2.8 %collective-permute-done.24.refs_6_ = bf16[128,1024]{1,0:T(8,128)(2,1)S(1)} collective-permute-done((bf16[128,1024]{1,0:T(8,128)(2,1)S(1)}, bf16[128,1024]{1,0:T(8,128)(2,1)S(1)}, u32[]{:S(2)}, u32[]{:S(2)}) %collective-permute-start.24) | collective-permute-done | bytes 262176 | tf_op jit(solution)/shard_map/ppermute | solution.py:30
  141.0 6.2 %collective-permute-done.25.refs_7_ = bf16[128,1024]{1,0:T(8,128)(2,1)S(1)} collective-permute-done((bf16[128,1024]{1,0:T(8,128)(2,1)S(1)}, bf16[128,1024]{1,0:T(8,128)(2,1)S(1)}, u32[]{:S(2)}, u32[]{:S(2)}) %collective-permute-start.25) | collective-permute-done | bytes 262176 | tf_op jit(solution)/shard_map/ppermute | solution.py:30
  147.2 5.3 %shard_map.80 = f32[128,8,1024]{2,1,0:T(8,128)} custom-call(s32[1]{0:T(128)} %bitcast.here_ref, f32[128,8,1024]{2,1,0:T(8,128)} %get-tuple-element.62.tv_ref, bf16[128,1024]{1,0:T(8,128)(2,1)S(1)} %get-tuple-element.67.refs_0_.refs_1_, bf16[256,1024]{1,0:T(8,128)(2,1)S(1)} %collective-permute-done.16.refs_1_, ...), custom_call_target="tpu_custom_call" | custom-call | flops 5750000128 | bytes 1000 | tf_op jit(solution)/shard_map/pallas_call | solution.py:345
  (77 shorter events, 2.0 us)
Async XLA Ops:
  0.6 3.8 %copy-start.18 = (bf16[128,8,1024]{2,1,0:T(8,128)(2,1)S(1)}, bf16[128,8,1024]{2,1,0:T(8,128)(2,1)}, u32[]{:S(2)}) copy-start(bf16[128,8,1024]{2,1,0:T(8,128)(2,1)} %refs_6_.1) | copy-start | bytes 6291460
  4.4 17.3 %copy-start.3 = (bf16[128,1024]{1,0:T(8,128)(2,1)}, bf16[128,1024]{1,0:T(8,128)(2,1)S(1)}, u32[]{:S(2)}) copy-start(bf16[128,1024]{1,0:T(8,128)(2,1)S(1)} %get-tuple-element.45.refs_9_) | copy-start | bytes 786436
  4.4 22.8 %copy-start.7 = (bf16[128,1024]{1,0:T(8,128)(2,1)}, bf16[128,1024]{1,0:T(8,128)(2,1)S(1)}, u32[]{:S(2)}) copy-start(bf16[128,1024]{1,0:T(8,128)(2,1)S(1)} %get-tuple-element.50.refs_12_) | copy-start | bytes 786436
  4.4 37.0 %copy-start.5 = (bf16[128,1024]{1,0:T(8,128)(2,1)}, bf16[128,1024]{1,0:T(8,128)(2,1)S(1)}, u32[]{:S(2)}) copy-start(bf16[128,1024]{1,0:T(8,128)(2,1)S(1)} %get-tuple-element.49.refs_0_.refs_11_) | copy-start | bytes 786436
  4.4 24.4 %collective-permute-start.5 = (bf16[128,8,1024]{2,1,0:T(8,128)(2,1)S(1)}, bf16[128,8,1024]{2,1,0:T(8,128)(2,1)S(1)}, u32[]{:S(2)}, u32[]{:S(2)}) collective-permute-start(bf16[128,8,1024]{2,1,0:T(8,128)(2,1)S(1)} %copy-done.18), channel_id=1, source_target_pairs={{3,7},{7,11},{11,15},{19,23},{23,27},{27,31}} | collective-permute-start | bytes 6291464 | tf_op jit(solution)/shard_map/ppermute | solution.py:25
  5.2 17.4 %collective-permute-start = (bf16[144,1024]{1,0:T(8,128)(2,1)S(1)}, bf16[144,1024]{1,0:T(8,128)(2,1)S(1)}, u32[]{:S(2)}, u32[]{:S(2)}) collective-permute-start(bf16[144,1024]{1,0:T(8,128)(2,1)S(1)} %get-tuple-element.43.refs_8_), channel_id=1, source_target_pairs={{0,1},{1,0},{2,3},{3,2},{4,5},{5,4},{6,7},{7,6},{8,9},{9,8},{10,11... | collective-permute-start | bytes 884744 | tf_op jit(solution)/shard_map/ppermute | solution.py:30
  5.3 17.3 %collective-permute-start.2 = (bf16[144,1024]{1,0:T(8,128)(2,1)S(1)}, bf16[144,1024]{1,0:T(8,128)(2,1)S(1)}, u32[]{:S(2)}, u32[]{:S(2)}) collective-permute-start(bf16[144,1024]{1,0:T(8,128)(2,1)S(1)} %get-tuple-element.46.refs_10_), channel_id=1, source_target_pairs={{0,3},{1,2},{2,1},{3,0},{4,7},{5,6},{6,5},{7,4},{8,11},{9,10},{10,... | collective-permute-start | bytes 884744 | tf_op jit(solution)/shard_map/ppermute | solution.py:30
  10.3 12.3 %collective-permute-start.1 = (bf16[128,1024]{1,0:T(8,128)(2,1)S(1)}, bf16[128,1024]{1,0:T(8,128)(2,1)S(1)}, u32[]{:S(2)}, u32[]{:S(2)}) collective-permute-start(bf16[128,1024]{1,0:T(8,128)(2,1)S(1)} %get-tuple-element.45.refs_9_), channel_id=1, source_target_pairs={{0,2},{1,3},{2,0},{3,1},{4,6},{5,7},{6,4},{7,5},{8,10},{9,11},{10,... | collective-permute-start | bytes 786440 | tf_op jit(solution)/shard_map/ppermute | solution.py:30
  10.3 23.5 %collective-permute-start.10 = (bf16[256,1024]{1,0:T(8,128)(2,1)S(1)}, bf16[256,1024]{1,0:T(8,128)(2,1)S(1)}, u32[]{:S(2)}, u32[]{:S(2)}) collective-permute-start(bf16[256,1024]{1,0:T(8,128)(2,1)S(1)} %get-tuple-element.51.refs_13_), channel_id=1, source_target_pairs={{0,2},{1,3},{2,0},{3,1},{4,6},{5,7},{6,4},{7,5},{8,10},{9,11},{10,... | collective-permute-start | bytes 1572872 | tf_op jit(solution)/shard_map/ppermute | solution.py:30
  22.6 2.2 %copy-start = (f32[128,8,1024]{2,1,0:T(8,128)S(1)}, f32[128,8,1024]{2,1,0:T(8,128)}, u32[]{:S(2)}) copy-start(f32[128,8,1024]{2,1,0:T(8,128)} %shard_map.69.refs_4_.refs_14_) | copy-start | bytes 12582916
  25.9 27.1 %collective-permute-start.3 = (bf16[528,1024]{1,0:T(8,128)(2,1)}, bf16[528,1024]{1,0:T(8,128)(2,1)S(1)}, u32[]{:S(2)}, u32[]{:S(2)}) collective-permute-start(bf16[528,1024]{1,0:T(8,128)(2,1)} %get-tuple-element.47.refs_0_.own_ref), channel_id=1, source_target_pairs={{4,0},{5,1},{6,2},{7,3},{8,4},{9,5},{10,6},{11,7},{12,8},{13,9},{1... | collective-permute-start | bytes 3244040 | tf_op jit(solution)/shard_map/ppermute | solution.py:25
  27.2 11.1 %collective-permute-start.9 = (bf16[128,1024]{1,0:T(8,128)(2,1)S(1)}, bf16[128,1024]{1,0:T(8,128)(2,1)S(1)}, u32[]{:S(2)}, u32[]{:S(2)}) collective-permute-start(bf16[128,1024]{1,0:T(8,128)(2,1)S(1)} %get-tuple-element.50.refs_12_), channel_id=1, source_target_pairs={{0,1},{1,0},{2,3},{3,2},{4,5},{5,4},{6,7},{7,6},{8,9},{9,8},{10,11... | collective-permute-start | bytes 786440 | tf_op jit(solution)/shard_map/ppermute | solution.py:30
  33.8 7.5 %collective-permute-start.11 = (bf16[128,1024]{1,0:T(8,128)(2,1)S(1)}, bf16[128,1024]{1,0:T(8,128)(2,1)S(1)}, u32[]{:S(2)}, u32[]{:S(2)}) collective-permute-start(bf16[128,1024]{1,0:T(8,128)(2,1)S(1)} %slice.15), channel_id=1, source_target_pairs={{0,1},{1,0},{2,3},{3,2},{4,5},{5,4},{6,7},{7,6},{8,9},{9,8},{10,11... | collective-permute-start | bytes 786440 | tf_op jit(solution)/shard_map/ppermute | solution.py:30
  34.9 9.5 %collective-permute-start.4 = (bf16[144,1024]{1,0:T(8,128)(2,1)S(1)}, bf16[144,1024]{1,0:T(8,128)(2,1)S(1)}, u32[]{:S(2)}, u32[]{:S(2)}) collective-permute-start(bf16[144,1024]{1,0:T(8,128)(2,1)S(1)} %get-tuple-element.48), channel_id=1, source_target_pairs={{0,4},{1,5},{2,6},{3,7},{4,8},{5,9},{6,10},{7,11},{8,12},{9,13},{1... | collective-permute-start | bytes 884744 | tf_op jit(solution)/shard_map/ppermute | solution.py:25
  37.9 18.4 %collective-permute-start.6 = (bf16[256,1024]{1,0:T(8,128)(2,1)}, bf16[256,1024]{1,0:T(8,128)(2,1)}, u32[]{:S(2)}, u32[]{:S(2)}) collective-permute-start(bf16[256,1024]{1,0:T(8,128)(2,1)} %get-tuple-element.54.refs_4_), channel_id=1, source_target_pairs={{0,1},{1,0},{2,3},{3,2},{4,5},{5,4},{6,7},{7,6},{8,9},{9,8},{10,11... | collective-permute-start | bytes 1572872 | tf_op jit(solution)/shard_map/ppermute | solution.py:30
  38.3 16.7 %collective-permute-start.7 = (bf16[128,1024]{1,0:T(8,128)(2,1)}, bf16[128,1024]{1,0:T(8,128)(2,1)}, u32[]{:S(2)}, u32[]{:S(2)}) collective-permute-start(bf16[128,1024]{1,0:T(8,128)(2,1)} %get-tuple-element.56), channel_id=1, source_target_pairs={{0,2},{1,3},{2,0},{3,1},{4,6},{5,7},{6,4},{7,5},{8,10},{9,11},{10,... | collective-permute-start | bytes 786440 | tf_op jit(solution)/shard_map/ppermute | solution.py:30
  41.3 15.0 %collective-permute-start.8 = (bf16[128,1024]{1,0:T(8,128)(2,1)}, bf16[128,1024]{1,0:T(8,128)(2,1)}, u32[]{:S(2)}, u32[]{:S(2)}) collective-permute-start(bf16[128,1024]{1,0:T(8,128)(2,1)} %get-tuple-element.57), channel_id=1, source_target_pairs={{0,3},{1,2},{2,1},{3,0},{4,7},{5,6},{6,5},{7,4},{8,11},{9,10},{10,... | collective-permute-start | bytes 786440 | tf_op jit(solution)/shard_map/ppermute | solution.py:30
  42.4 6.8 %copy-start.19 = (s32[16,6]{0,1:T(8,128)S(1)}, s32[16,6]{0,1:T(8,128)}, u32[]{:S(2)}) copy-start(s32[16,6]{0,1:T(8,128)} %param.8) | copy-start | bytes 1156
  42.4 6.9 %copy-start.20 = (s32[16,6]{0,1:T(8,128)S(1)}, s32[16,6]{0,1:T(8,128)}, u32[]{:S(2)}) copy-start(s32[16,6]{0,1:T(8,128)} %param.9) | copy-start | bytes 1156
  44.4 12.0 %collective-permute-start.12 = (bf16[128,1024]{1,0:T(8,128)(2,1)}, bf16[128,1024]{1,0:T(8,128)(2,1)}, u32[]{:S(2)}, u32[]{:S(2)}) collective-permute-start(bf16[128,1024]{1,0:T(8,128)(2,1)} %get-tuple-element.60), channel_id=1, source_target_pairs={{0,4},{1,5},{2,6},{3,7},{4,8},{5,9},{6,10},{7,11},{8,12},{9,13},{1... | collective-permute-start | bytes 786440 | tf_op jit(solution)/shard_map/ppermute | solution.py:25
  50.3 2.7 %copy-start.21 = (bf16[256,1024]{1,0:T(8,128)(2,1)S(1)}, bf16[256,1024]{1,0:T(8,128)(2,1)}, u32[]{:S(2)}) copy-start(bf16[256,1024]{1,0:T(8,128)(2,1)} %get-tuple-element.70) | copy-start | bytes 1572868
  50.3 4.7 %copy-start.11 = (bf16[512,1024]{1,0:T(8,128)(2,1)S(1)}, bf16[512,1024]{1,0:T(8,128)(2,1)}, u32[]{:S(2)}) copy-start(bf16[512,1024]{1,0:T(8,128)(2,1)} %copy-done.10) | copy-start | bytes 3145732
  50.3 6.0 %copy-start.16 = (bf16[128,1024]{1,0:T(8,128)(2,1)S(1)}, bf16[128,1024]{1,0:T(8,128)(2,1)}, u32[]{:S(2)}) copy-start(bf16[128,1024]{1,0:T(8,128)(2,1)} %get-tuple-element.55.refs_1_) | copy-start | bytes 786436
  53.1 34.3 %collective-permute-start.19 = (bf16[256,1024]{1,0:T(8,128)(2,1)S(1)}, bf16[256,1024]{1,0:T(8,128)(2,1)S(1)}, u32[]{:S(2)}, u32[]{:S(2)}) collective-permute-start(bf16[256,1024]{1,0:T(8,128)(2,1)S(1)} %copy-done.21), channel_id=1, source_target_pairs={{0,2},{1,3},{2,0},{3,1},{4,6},{5,7},{6,4},{7,5},{8,10},{9,11},{10,... | collective-permute-start | bytes 1572872 | tf_op jit(solution)/shard_map/ppermute | solution.py:30
  55.1 36.2 %collective-permute-start.18 = (bf16[512,1024]{1,0:T(8,128)(2,1)S(1)}, bf16[512,1024]{1,0:T(8,128)(2,1)S(1)}, u32[]{:S(2)}, u32[]{:S(2)}) collective-permute-start(bf16[512,1024]{1,0:T(8,128)(2,1)S(1)} %copy-done.11), channel_id=1, source_target_pairs={{4,0},{5,1},{6,2},{7,3},{8,4},{9,5},{10,6},{11,7},{12,8},{13,9},{1... | collective-permute-start | bytes 3145736 | tf_op jit(solution)/shard_map/ppermute | solution.py:25
  56.4 1.3 copy-start.14
  57.7 8.5 %copy-start.2 = (bf16[8,128,128]{2,1,0:T(8,128)(2,1)S(1)}, bf16[8,128,128]{2,1,0:T(8,128)(2,1)}, u32[]{:S(2)}) copy-start(bf16[8,128,128]{2,1,0:T(8,128)(2,1)} %refs_0_.1) | copy-start | bytes 786436
  57.7 8.5 %copy-start.4 = (bf16[128,1024]{1,0:T(8,128)(2,1)S(1)}, bf16[128,1024]{1,0:T(8,128)(2,1)}, u32[]{:S(2)}) copy-start(bf16[128,1024]{1,0:T(8,128)(2,1)} %copy-done.3) | copy-start | bytes 786436
  57.7 8.5 %copy-start.6 = (bf16[128,1024]{1,0:T(8,128)(2,1)S(1)}, bf16[128,1024]{1,0:T(8,128)(2,1)}, u32[]{:S(2)}) copy-start(bf16[128,1024]{1,0:T(8,128)(2,1)} %copy-done.5) | copy-start | bytes 786436
  57.7 8.5 %copy-start.8 = (bf16[128,1024]{1,0:T(8,128)(2,1)S(1)}, bf16[128,1024]{1,0:T(8,128)(2,1)}, u32[]{:S(2)}) copy-start(bf16[128,1024]{1,0:T(8,128)(2,1)} %copy-done.7) | copy-start | bytes 786436
  60.8 42.9 %collective-permute-start.13 = (bf16[512,1024]{1,0:T(8,128)(2,1)S(1)}, bf16[512,1024]{1,0:T(8,128)(2,1)S(1)}, u32[]{:S(2)}, u32[]{:S(2)}) collective-permute-start(bf16[512,1024]{1,0:T(8,128)(2,1)S(1)} %get-tuple-element.61.refs_15_.r_ref.own_ref), channel_id=1, source_target_pairs={{0,4},{1,5},{2,6},{3,7},{4,8},{5,9},{6,10},{7,11},{8,12},{9,13},{1... | collective-permute-start | bytes 3145736 | tf_op jit(solution)/shard_map/ppermute | solution.py:25
  64.8 20.6 %collective-permute-start.14 = (bf16[128,1024]{1,0:T(8,128)(2,1)S(1)}, bf16[128,1024]{1,0:T(8,128)(2,1)S(1)}, u32[]{:S(2)}, u32[]{:S(2)}) collective-permute-start(bf16[128,1024]{1,0:T(8,128)(2,1)S(1)} %get-tuple-element.64), channel_id=1, source_target_pairs={{4,0},{5,1},{6,2},{7,3},{8,4},{9,5},{10,6},{11,7},{12,8},{13,9},{1... | collective-permute-start | bytes 786440 | tf_op jit(solution)/shard_map/ppermute | solution.py:25
  85.4 1.6 %copy-start.9 = (bf16[128,8,1024]{2,1,0:T(8,128)(2,1)S(1)}, bf16[128,8,1024]{2,1,0:T(8,128)(2,1)}, u32[]{:S(2)}) copy-start(bf16[128,8,1024]{2,1,0:T(8,128)(2,1)} %get-tuple-element.65.refs_0_.refs_8_) | copy-start | bytes 6291460
  87.0 4.3 %copy-start.15 = (bf16[512,1152]{1,0:T(8,128)(2,1)S(1)}, bf16[512,1152]{1,0:T(8,128)(2,1)}, u32[]{:S(2)}) copy-start(bf16[512,1152]{1,0:T(8,128)(2,1)} %get-tuple-element.52.band_ref) | copy-start | bytes 3538948
  87.0 4.3 %copy-start.17 = (bf16[128,1024]{1,0:T(8,128)(2,1)S(1)}, bf16[128,1024]{1,0:T(8,128)(2,1)}, u32[]{:S(2)}) copy-start(bf16[128,1024]{1,0:T(8,128)(2,1)} %get-tuple-element.69.refs_1_) | copy-start | bytes 786436
  87.4 3.9 %collective-permute-start.20 = (bf16[128,1024]{1,0:T(8,128)(2,1)S(1)}, bf16[128,1024]{1,0:T(8,128)(2,1)S(1)}, u32[]{:S(2)}, u32[]{:S(2)}) collective-permute-start(bf16[128,1024]{1,0:T(8,128)(2,1)S(1)} %slice.17), channel_id=1, source_target_pairs={{0,1},{1,0},{2,3},{3,2},{4,5},{5,4},{6,7},{7,6},{8,9},{9,8},{10,11... | collective-permute-start | bytes 786440 | tf_op jit(solution)/shard_map/ppermute | solution.py:30
  90.1 13.5 %collective-permute-start.15 = (bf16[256,1024]{1,0:T(8,128)(2,1)S(1)}, bf16[256,1024]{1,0:T(8,128)(2,1)S(1)}, u32[]{:S(2)}, u32[]{:S(2)}) collective-permute-start(bf16[256,1024]{1,0:T(8,128)(2,1)S(1)} %get-tuple-element.66), channel_id=1, source_target_pairs={{0,2},{1,3},{2,0},{3,1},{4,6},{5,7},{6,4},{7,5},{8,10},{9,11},{10,... | collective-permute-start | bytes 1572872 | tf_op jit(solution)/shard_map/ppermute | solution.py:30
  91.3 12.3 %copy-start.13 = (bf16[512,1152]{1,0:T(8,128)(2,1)S(1)}, bf16[512,1152]{1,0:T(8,128)(2,1)}, u32[]{:S(2)}) copy-start(bf16[512,1152]{1,0:T(8,128)(2,1)} %get-tuple-element.63.band_ref) | copy-start | bytes 3538948
  94.3 11.4 %collective-permute-start.22 = (bf16[128,1024]{1,0:T(8,128)(2,1)S(1)}, bf16[128,1024]{1,0:T(8,128)(2,1)S(1)}, u32[]{:S(2)}, u32[]{:S(2)}) collective-permute-start(bf16[128,1024]{1,0:T(8,128)(2,1)S(1)} %get-tuple-element.74), channel_id=1, source_target_pairs={{4,0},{5,1},{6,2},{7,3},{8,4},{9,5},{10,6},{11,7},{12,8},{13,9},{1... | collective-permute-start | bytes 786440 | tf_op jit(solution)/shard_map/ppermute | solution.py:25
  95.6 35.8 %collective-permute-start.21 = (bf16[512,1024]{1,0:T(8,128)(2,1)S(1)}, bf16[512,1024]{1,0:T(8,128)(2,1)S(1)}, u32[]{:S(2)}, u32[]{:S(2)}) collective-permute-start(bf16[512,1024]{1,0:T(8,128)(2,1)S(1)} %get-tuple-element.73.own_ref.r_ref), channel_id=1, source_target_pairs={{0,4},{1,5},{2,6},{3,7},{4,8},{5,9},{6,10},{7,11},{8,12},{9,13},{1... | collective-permute-start | bytes 3145736 | tf_op jit(solution)/shard_map/ppermute | solution.py:25
  105.6 12.7 %collective-permute-start.16 = (bf16[256,1024]{1,0:T(8,128)(2,1)S(1)}, bf16[256,1024]{1,0:T(8,128)(2,1)S(1)}, u32[]{:S(2)}, u32[]{:S(2)}) collective-permute-start(bf16[256,1024]{1,0:T(8,128)(2,1)S(1)} %get-tuple-element.68), channel_id=1, source_target_pairs={{0,2},{1,3},{2,0},{3,1},{4,6},{5,7},{6,4},{7,5},{8,10},{9,11},{10,... | collective-permute-start | bytes 1572872 | tf_op jit(solution)/shard_map/ppermute | solution.py:30
  106.1 23.4 %collective-permute-start.27 = (bf16[256,1024]{1,0:T(8,128)(2,1)S(1)}, bf16[256,1024]{1,0:T(8,128)(2,1)S(1)}, u32[]{:S(2)}, u32[]{:S(2)}) collective-permute-start(bf16[256,1024]{1,0:T(8,128)(2,1)S(1)} %get-tuple-element.82), channel_id=1, source_target_pairs={{0,2},{1,3},{2,0},{3,1},{4,6},{5,7},{6,4},{7,5},{8,10},{9,11},{10,... | collective-permute-start | bytes 1572872 | tf_op jit(solution)/shard_map/ppermute | solution.py:30
  118.3 13.1 %collective-permute-start.17 = (bf16[128,1024]{1,0:T(8,128)(2,1)S(1)}, bf16[128,1024]{1,0:T(8,128)(2,1)S(1)}, u32[]{:S(2)}, u32[]{:S(2)}) collective-permute-start(bf16[128,1024]{1,0:T(8,128)(2,1)S(1)} %slice.20), channel_id=1, source_target_pairs={{0,1},{1,0},{2,3},{3,2},{4,5},{5,4},{6,7},{7,6},{8,9},{9,8},{10,11... | collective-permute-start | bytes 786440 | tf_op jit(solution)/shard_map/ppermute | solution.py:30
  121.5 14.1 %collective-permute-start.26 = (bf16[256,1024]{1,0:T(8,128)(2,1)S(1)}, bf16[256,1024]{1,0:T(8,128)(2,1)S(1)}, u32[]{:S(2)}, u32[]{:S(2)}) collective-permute-start(bf16[256,1024]{1,0:T(8,128)(2,1)S(1)} %get-tuple-element.81), channel_id=1, source_target_pairs={{0,1},{1,0},{2,3},{3,2},{4,5},{5,4},{6,7},{7,6},{8,9},{9,8},{10,11... | collective-permute-start | bytes 1572872 | tf_op jit(solution)/shard_map/ppermute | solution.py:30
  129.6 6.0 %collective-permute-start.28 = (bf16[256,1024]{1,0:T(8,128)(2,1)S(1)}, bf16[256,1024]{1,0:T(8,128)(2,1)S(1)}, u32[]{:S(2)}, u32[]{:S(2)}) collective-permute-start(bf16[256,1024]{1,0:T(8,128)(2,1)S(1)} %pad_maximum_fusion), channel_id=1, source_target_pairs={{0,1},{1,0},{2,3},{3,2},{4,5},{5,4},{6,7},{7,6},{8,9},{9,8},{10,11... | collective-permute-start | bytes 1572872 | tf_op jit(solution)/shard_map/ppermute | solution.py:30
  133.4 13.8 %collective-permute-start.23 = (bf16[256,1024]{1,0:T(8,128)(2,1)S(1)}, bf16[256,1024]{1,0:T(8,128)(2,1)S(1)}, u32[]{:S(2)}, u32[]{:S(2)}) collective-permute-start(bf16[256,1024]{1,0:T(8,128)(2,1)S(1)} %get-tuple-element.76), channel_id=1, source_target_pairs={{0,1},{1,0},{2,3},{3,2},{4,5},{5,4},{6,7},{7,6},{8,9},{9,8},{10,11... | collective-permute-start | bytes 1572872 | tf_op jit(solution)/shard_map/ppermute | solution.py:30
  133.5 7.5 %collective-permute-start.24 = (bf16[128,1024]{1,0:T(8,128)(2,1)S(1)}, bf16[128,1024]{1,0:T(8,128)(2,1)S(1)}, u32[]{:S(2)}, u32[]{:S(2)}) collective-permute-start(bf16[128,1024]{1,0:T(8,128)(2,1)S(1)} %get-tuple-element.78), channel_id=1, source_target_pairs={{0,2},{1,3},{2,0},{3,1},{4,6},{5,7},{6,4},{7,5},{8,10},{9,11},{10,... | collective-permute-start | bytes 786440 | tf_op jit(solution)/shard_map/ppermute | solution.py:30
  133.6 13.6 %collective-permute-start.25 = (bf16[128,1024]{1,0:T(8,128)(2,1)S(1)}, bf16[128,1024]{1,0:T(8,128)(2,1)S(1)}, u32[]{:S(2)}, u32[]{:S(2)}) collective-permute-start(bf16[128,1024]{1,0:T(8,128)(2,1)S(1)} %get-tuple-element.79), channel_id=1, source_target_pairs={{0,3},{1,2},{2,1},{3,0},{4,7},{5,6},{6,5},{7,4},{8,11},{9,10},{10,... | collective-permute-start | bytes 786440 | tf_op jit(solution)/shard_map/ppermute | solution.py:30
  (3 other events, 3.0 us)

commit v6 on v5

v6 whole, which is shorter than its diff:
```python
import functools

import jax
import jax.numpy as jnp
from jax import lax
from jax.experimental import pallas as pl
from jax.experimental.pallas import tpu as pltpu
from jax.sharding import PartitionSpec as P

G = 4
CHUNKS = 2
ROWS = 2
TILE = 256
F32 = jnp.float32
BF16 = jnp.bfloat16
MIB = 1024 * 1024
LANES = 128
SMEM = pl.BlockSpec(memory_space=pltpu.SMEM)
VMEM = pl.BlockSpec(memory_space=pltpu.VMEM)
ANY = pl.BlockSpec(memory_space=pl.ANY)


def moved(value, steps, only=None):
    count = lax.axis_size("slab")
    first, last = max(0, -steps), min(count, count - steps)
    pairs = [(i, i + steps) for i in range(first, last) if only is None or i % G == only]
    return lax.ppermute(value, "slab", pairs)


def swapped(value, bits):
    count = lax.axis_size("slab")
    return lax.ppermute(value, "slab", [(i, i ^ bits) for i in range(count)])


def direct(chunk, groups, arrays):
    return [(chunk, m, array if m == 0 else swapped(array, m), 0) for (m,), array in zip(groups, arrays)]


def in_two(chunk, pair, after=None):
    side = pair.shape[0] // 2
    over = swapped(pair, 2)
    if after is not None:
        over = lax.optimization_barrier((over, after))[0]
    return [(chunk, 2, over, 0), (chunk, 3, swapped(over[side:], 1), 0)]


def call(kernel, us, *, results, vmem=16, **how):
    return pl.pallas_call(
        kernel,
        out_shape=results,
        compiler_params=pltpu.CompilerParams(vmem_limit_bytes=vmem * MIB),
        cost_estimate=pl.CostEstimate(flops=int(us * 1.15e9), bytes_accessed=1000, transcendentals=0),
        **how,
    )


def value(shape, dtype):
    return jax.ShapeDtypeStruct(shape, dtype)


def far(array):
    return pltpu.with_memory_space_constraint(array, pltpu.HBM)


def across(shape, tile):
    block = shape[:-1] + (tile,)
    return pl.BlockSpec(block, lambda i: (0,) * (len(shape) - 1) + (i,))


def lanes(array, tile, parts):
    block = array.shape[:-1] + (tile,)
    zeros = (0,) * (len(block) - 1)
    return [pl.BlockSpec(block, lambda i, j=j: zeros + (i * parts + j,)) for j in range(parts)]


def piece_specs(pieces, side, tile):
    return [pl.BlockSpec((side, tile), lambda i, at=at: (at, i)) for _, _, _, at in pieces]


def keys_of(pieces):
    return [(chunk, m) for chunk, m, _, _ in pieces]


def arrays_of(pieces):
    return [array for _, _, array, _ in pieces]


def group_results(groups, side, cols, tile, space=None):
    shapes = [(len(group) * side, cols) for group in groups]
    results = [space(shape, BF16) if space else value(shape, BF16) for shape in shapes]
    return dict(out_specs=[across(shape, tile) for shape in shapes], results=results)


def rows_of(place, m):
    first = ROWS * jnp.bitwise_xor(place, m)
    return [(h * TILE, first + h) for h in range(ROWS)]


def wide_tile(rows_deep):
    return pltpu.VMEM((TILE // LANES, rows_deep, LANES), F32)


def chunk_tiles(chunk, cols):
    count = cols // CHUNKS // TILE
    return chunk * count, count


def cast_kernel(groups, sent, here_ref, *refs):
    parts = TILE // LANES
    vol_refs, refs = refs[:parts], refs[parts:]
    sem = refs[-1]
    sent_refs = refs[-1 - CHUNKS : -1] if sent else ()
    out_refs = refs[-1 - len(sent_refs) - len(groups) :]
    step = pl.program_id(0)
    rows = ROWS * G
    depth = vol_refs[0].shape[0] // rows
    place = lax.rem(here_ref[0], G)

    def copies():
        width = sent_refs[0].shape[2]
        return [
            pltpu.make_async_copy(refs[2].at[:, :, c * width : (c + 1) * width], sent_refs[c], sem.at[c])
            for c in range(CHUNKS)
        ]

    if sent:

        @pl.when(step == 0)
        def _():
            for copy in copies():
                copy.start()

    for j, vol_ref in enumerate(vol_refs):
        for group, out_ref in zip(groups, out_refs):
            for n, m in enumerate(group):
                for start, row in rows_of(place, m):
                    at = pl.ds(start + j * LANES, LANES)
                    out_ref[n * depth : (n + 1) * depth, at] = vol_ref[pl.ds(row, depth, stride=rows), :].astype(BF16)
    if sent:
        both = jnp.concatenate([refs[0][...], refs[1][...]], axis=0).astype(BF16)
        for group, out_ref in zip(groups, out_refs):
            if group[0] % 2:
                out_ref[depth:, :] = both
    if sent:

        @pl.when(step == pl.num_programs(0) - 1)
        def _():
            for copy in copies():
                copy.wait()


def cast_rows(here, volume, chunk, groups, sinogram=None, *tokens):
    depth, rows, cols = volume.shape
    flat = far(volume.reshape(depth * rows, cols))
    first, count = chunk_tiles(chunk, cols)
    parts, width = TILE // LANES, ROWS * TILE
    sent = sinogram is not None
    shapes = [(len(g) * depth + (2 * rows if sent and g[0] % 2 else 0), cols) for g in groups]
    out_specs = [across(shape, width) for shape in shapes]
    results = [value(shape, BF16) for shape in shapes]
    in_specs = [SMEM]
    in_specs += [pl.BlockSpec((depth * rows, LANES), lambda i, j=j: (0, (first + i) * parts + j)) for j in range(parts)]
    args = []
    if sent:
        args = [flat, flat, far(sinogram)]
        in_specs += [pl.BlockSpec((rows, width), lambda i, z=z: (z, i)) for z in (0, depth - 1)] + [ANY]
        out_specs += [ANY] * CHUNKS
        results += [pltpu.HBM((depth, rows, cols // CHUNKS), BF16)] * CHUNKS
    return call(
        functools.partial(cast_kernel, groups, sent),
        2,
        grid=(count,),
        in_specs=in_specs + [ANY] * len(tokens),
        out_specs=out_specs,
        results=results,
        scratch_shapes=[pltpu.SemaphoreType.DMA((CHUNKS,))],
    )(here, *[flat] * parts, *args, *tokens)


def pack_kernel(cuts, here_ref, *refs):
    in_refs, (*part_refs, last_ref) = refs[:G], refs[-len(cuts) - 1 :]
    side = in_refs[0].shape[0]
    spot = jnp.bitwise_xor(lax.rem(here_ref[0], G), G - 1)
    last = in_refs[0][...]
    for m in range(1, G):
        last = jnp.where(spot == m, in_refs[m][:side], last)
    last_ref[:side] = last
    for part, part_ref in zip(cuts, part_refs):
        for n, m in enumerate(part):
            part_ref[n * side : (n + 1) * side] = in_refs[m][:side]
    if last_ref.shape[0] > side:
        last_ref[side:] = in_refs[G - 1][side:]
        part_refs[-1][len(cuts[-1]) * side :] = in_refs[G - 1][side:]


def pack(here, pieces, cuts, more, *tokens):
    pieces = sorted(pieces, key=lambda piece: piece[1])
    side, cols = pieces[0][2].shape
    tile = 512
    shapes = [(len(part) * side, cols) for part in cuts] + [(side + more, cols)]
    shapes[-2] = (shapes[-2][0] + more, cols)
    specs = piece_specs(pieces, side, tile)
    if more:
        specs = [across(array.shape, tile) for array in arrays_of(pieces)]
    return call(
        functools.partial(pack_kernel, cuts),
        1,
        grid=(cols // tile,),
        in_specs=[SMEM] + specs + [ANY] * len(tokens),
        out_specs=[across(shape, tile) for shape in shapes],
        results=[value(shape, BF16) for shape in shapes],
    )(here, *arrays_of(pieces), *tokens)


def split_kernel(groups, here_ref, own_ref, got_ref, *refs):
    out_refs, wide = refs[-len(groups) - 1 : -1], refs[-1]
    depth, rows, cols = own_ref.shape
    place = lax.rem(here_ref[0], G)

    def fill(ref):
        for j in range(cols // LANES):
            wide[j] = ref[:, :, j * LANES : (j + 1) * LANES].astype(F32).reshape(wide.shape[1:])

    @pl.when(place == G - 1)
    def _():
        fill(got_ref)

    @pl.when(place != G - 1)
    def _():
        fill(own_ref)

    for j in range(cols // LANES):
        for group, out_ref in zip(groups, out_refs):
            for n, m in enumerate(group):
                for start, row in rows_of(place, m):
                    at = pl.ds(start + j * LANES, LANES)
                    out_ref[n * depth : (n + 1) * depth, at] = wide.at[j][pl.ds(row, depth, stride=rows), :].astype(BF16)


def split_rows(here, own, got, chunk, groups, *tokens):
    depth, rows, cols = own.shape
    first, count = chunk_tiles(chunk, cols)
    block = (depth, rows, TILE)
    return call(
        functools.partial(split_kernel, groups),
        2,
        grid=(count,),
        in_specs=[SMEM, pl.BlockSpec(block, lambda i: (0, 0, first + i)), pl.BlockSpec(block, lambda i: (0, 0, i))]
        + [ANY] * len(tokens),
        scratch_shapes=[wide_tile(depth * rows)],
        **group_results(groups, depth, cols, ROWS * TILE, pltpu.HBM),
    )(here, far(own), got, *tokens)


def patch_kernel(slabs, here_ref, cover_ref, offset_ref, *refs):
    w_ref, *refs = refs
    end_refs, (vol_ref, sino_ref), (r_ref, tv_ref) = refs[:4], refs[4:6], refs[-10:-8]
    vol, s, r, wide, tv, slices, fixed, sem = refs[-8:]
    depth, rows, cols = sino_ref.shape
    place = lax.rem(here_ref[0], G)
    near, next_level, far_end, last_level = (ref[...] for ref in end_refs)
    low = jnp.where(place == 0, last_level, jnp.where(place == 2, far_end, near))[rows:].astype(F32)
    high = jnp.where(place == G - 1, next_level, jnp.where(place == 1, far_end, near))[:rows].astype(F32)

    for n, z in enumerate((0, depth - 2)):
        pltpu.make_async_copy(vol_ref.at[z : z + 2], slices.at[2 * n : 2 * n + 2], sem.at[n]).start()
    for n, z in enumerate((0, depth - 2)):
        pltpu.make_async_copy(vol_ref.at[z : z + 2], slices.at[2 * n : 2 * n + 2], sem.at[n]).wait()
    fixed[0] = tv_slice(slices[0], slices[1], tv_below(low, slices[0]))[0]
    fixed[1] = tv_slice(slices[3], high, tv_below(slices[2], slices[3]))[0]
    for n, z in enumerate((0, depth - 1)):
        pltpu.make_async_copy(fixed.at[n], tv_ref.at[z], sem.at[n]).start()
    for n, z in enumerate((0, depth - 1)):
        pltpu.make_async_copy(fixed.at[n], tv_ref.at[z], sem.at[n]).wait()

    @pl.when(here_ref[0] == slabs - 1)
    def _():
        pltpu.make_async_copy(vol_ref, vol, sem.at[2]).start()
        pltpu.make_async_copy(sino_ref, s, sem.at[3]).start()
        pltpu.make_async_copy(tv_ref, tv, sem.at[4]).start()
        pltpu.make_async_copy(vol_ref, vol, sem.at[2]).wait()
        pltpu.make_async_copy(sino_ref, s, sem.at[3]).wait()
        pltpu.make_async_copy(tv_ref, tv, sem.at[4]).wait()
        block = w_ref[offset_ref[slabs - 1, 0]]
        block = jnp.where(cover_ref[slabs - 1, 0] == 1, block, jnp.zeros_like(block))
        turned = block.astype(F32).T.astype(BF16)

        def column(j, _):
            at = pl.ds(pl.multiple_of(j * LANES, LANES), LANES)
            for n, ref in enumerate((s, tv, vol)):
                wide[n] = ref[:, :, at].astype(F32).reshape(wide.shape[1:])
            for row in range(rows):
                spot = pl.ds(row, depth, stride=rows)
                seen = jnp.dot(block, wide.at[2][spot, :].astype(BF16), preferred_element_type=F32)
                resid = (seen - wide.at[0][spot, :]).astype(BF16)
                wide.at[0][spot, :] = resid.astype(F32)
                wide.at[1][spot, :] += jnp.dot(turned, resid, preferred_element_type=F32)
            r[:, :, at] = wide[0].reshape(depth, rows, LANES).astype(BF16)
            tv[:, :, at] = wide[1].reshape(depth, rows, LANES)
            return 0

        lax.fori_loop(0, cols // LANES, column, 0)
        pltpu.make_async_copy(r, r_ref, sem.at[3]).start()
        pltpu.make_async_copy(tv, tv_ref, sem.at[4]).start()
        pltpu.make_async_copy(r, r_ref, sem.at[3]).wait()
        pltpu.make_async_copy(tv, tv_ref, sem.at[4]).wait()


def patch(here, coverage, offsets, weights, ends, volume, sinogram, tv, *tokens):
    slabs = coverage.shape[0]
    depth, rows, cols = sinogram.shape
    edges = [pl.BlockSpec((2 * rows, cols), lambda i, last=end.shape[0] // (2 * rows) - 1: (last, 0)) for end in ends]
    return call(
        functools.partial(patch_kernel, slabs),
        3,
        vmem=32,
        grid=(1,),
        in_specs=[SMEM, SMEM, SMEM, pl.BlockSpec(weights.shape, lambda i: (0, 0, 0))]
        + edges
        + [ANY] * (3 + len(tokens)),
        out_specs=[ANY, ANY],
        results=[pltpu.HBM(sinogram.shape, BF16), pltpu.HBM(volume.shape, F32)],
        input_output_aliases={10: 1},
        scratch_shapes=[
            pltpu.VMEM(volume.shape, F32),
            pltpu.VMEM(sinogram.shape, BF16),
            pltpu.VMEM(sinogram.shape, BF16),
            pltpu.VMEM((3, depth * rows, LANES), F32),
            pltpu.VMEM(volume.shape, F32),
            pltpu.VMEM((4, rows, cols), F32),
            pltpu.VMEM((2, rows, cols), F32),
            pltpu.SemaphoreType.DMA((5,)),
        ],
    )(here, coverage, offsets, weights, *ends, far(volume), far(sinogram), far(tv), *tokens)


def join_kernel(slabs, first, keys, here_ref, *refs):
    in_refs, (base_ref, out_ref, wide) = refs[: len(keys)], refs[-3:]
    depth, rows, cols = out_ref.shape
    place = lax.rem(here_ref[0], G)
    last = here_ref[0] == slabs - 1

    @pl.when(last)
    def _():
        at = pl.ds(pl.multiple_of((first + pl.program_id(0)) * cols, cols), cols)
        pltpu.sync_copy(base_ref.at[:, :, at], out_ref)

    @pl.when(jnp.logical_not(last))
    def _():
        for j in range(cols // LANES):
            for m, ref in zip(keys, in_refs):
                for start, row in rows_of(place, m):
                    value = ref[:, start + j * LANES : start + (j + 1) * LANES].astype(F32)
                    wide.at[j][pl.ds(row, depth, stride=rows), :] = value
            out_ref[:, :, j * LANES : (j + 1) * LANES] = wide[j].reshape(depth, rows, LANES).astype(out_ref.dtype)


def join_rows(here, slabs, chunk, pieces, base, *tokens):
    depth, rows, cols = base.shape
    first, count = chunk_tiles(chunk, cols)
    return call(
        functools.partial(join_kernel, slabs, first, [m for _, m, _, _ in pieces]),
        1.5,
        grid=(count,),
        in_specs=[SMEM] + piece_specs(pieces, depth, ROWS * TILE) + [ANY] * (len(tokens) + 1),
        out_specs=pl.BlockSpec((depth, rows, TILE), lambda i: (0, 0, first + i)),
        results=pltpu.HBM(base.shape, BF16),
        input_output_aliases={1 + len(pieces) + len(tokens): 0},
        scratch_shapes=[wide_tile(depth * rows)],
    )(here, *arrays_of(pieces), *tokens, far(base))


def finish_kernel(keys, here_ref, tv_ref, *refs):
    in_refs, (out_ref, wide) = refs[: len(keys)], refs[-2:]
    depth, rows, cols = out_ref.shape
    place = lax.rem(here_ref[0], G)
    for j in range(cols // LANES):
        for m, ref in zip(keys, in_refs):
            for start, row in rows_of(place, m):
                value = ref[:, start + j * LANES : start + (j + 1) * LANES].astype(F32)
                wide.at[j][pl.ds(row, depth, stride=rows), :] = value
        at = pl.ds(j * LANES, LANES)
        out_ref[:, :, at] = tv_ref[:, :, at] + wide[j].reshape(depth, rows, LANES)


def finish(here, chunk, tv, pieces, *tokens):
    depth, rows, cols = tv.shape
    first, count = chunk_tiles(chunk, cols)
    part = pl.BlockSpec((depth, rows, TILE), lambda i: (0, 0, first + i))
    return call(
        functools.partial(finish_kernel, [m for _, m, _, _ in pieces]),
        2.6,
        grid=(count,),
        in_specs=[SMEM, part] + piece_specs(pieces, depth, ROWS * TILE) + [ANY] * len(tokens),
        out_specs=part,
        results=pltpu.HBM(tv.shape, F32),
        input_output_aliases={1: 0},
        scratch_shapes=[wide_tile(depth * rows)],
    )(here, far(tv), *arrays_of(pieces), *tokens)


def band_kernel(slabs, span, here_ref, cover_ref, offset_ref, w_ref, *refs):
    proj_ref, back_ref, turned = refs[-3:]
    side = w_ref.shape[1]
    place = lax.rem(here_ref[0], G)
    first = here_ref[0] - place
    zero = jnp.zeros((side, side), BF16)
    for i in range(w_ref.shape[0]):
        turned[i] = w_ref[i].astype(F32).T.astype(BF16)

    def block(ref, i, j):
        k = j - i
        known, step = jnp.clip(i, 0, slabs - 1), jnp.clip(k, 0, span - 1)
        inside = (i >= 0) & (i < slabs) & (j >= 0) & (j < slabs) & (k >= 0) & (k < span)
        live = inside & (cover_ref[known, step] == 1)
        return jnp.where(live, ref[offset_ref[known, step]], zero)

    def slab(m):
        return first + jnp.bitwise_xor(place, m)

    def group(m):
        to = jnp.bitwise_xor(place, m)
        return first + jnp.where(to == G - 1, -1, to)

    seen = [slab(m) for m in range(G)] + [slab(m) + G for m in range(G)] + [first - 1]
    seeing = [group(m) for m in range(G)] + [group(m) - G for m in range(G)] + [first + G - 1]
    for r in range(G):
        for s in range(2 * G + 1):
            at = (pl.ds(r * side, side), pl.ds(s * side, side))
            proj_ref[at] = block(w_ref, group(r), seen[s])
            back_ref[at] = block(turned, seeing[s], slab(r))


def bands(here, coverage, offsets, weights, *tokens):
    slabs, span = coverage.shape
    side = weights.shape[1]
    shape = (G * side, (2 * G + 1) * side)
    return call(
        functools.partial(band_kernel, slabs, span),
        1.6,
        in_specs=[SMEM, SMEM, SMEM, pl.BlockSpec(weights.shape, lambda i: (0, 0, 0))] + [ANY] * len(tokens),
        grid=(1,),
        out_specs=[pl.BlockSpec(shape, lambda i: (0, 0))] * 2,
        results=[pltpu.HBM(shape, BF16)] * 2,
        scratch_shapes=[pltpu.VMEM(weights.shape, BF16)],
    )(here, coverage, offsets, weights, *tokens)


def project_kernel(sources, keys, here_ref, band_ref, *refs):
    seen_refs, refs = refs[:sources], refs[sources:]
    sinos, (r_ref, down_ref) = dict(zip(keys, refs)), refs[-2:]
    side = down_ref.shape[0]
    seen = jnp.concatenate([ref[: ref.shape[0] // side * side] for ref in seen_refs], axis=0)
    total = jnp.dot(band_ref[...], seen, preferred_element_type=F32)
    for (_, m), ref in sinos.items():
        at = slice(m * side, (m + 1) * side)
        r_ref[at, :] = (total[at] - ref[...].astype(F32)).astype(BF16)
    spot = jnp.bitwise_xor(lax.rem(here_ref[0], G), G - 1)
    down_ref[...] = r_ref[pl.ds(pl.multiple_of(spot * side, side), side), :]


def project(here, band, sources, pieces, *tokens):
    n, side = band.shape[0], band.shape[0] // G
    cols = sources[0].shape[1]
    tile = 512
    one = across((side, cols), tile)
    return call(
        functools.partial(project_kernel, len(sources), keys_of(pieces)),
        3,
        grid=(cols // tile,),
        in_specs=[SMEM, pl.BlockSpec(band.shape, lambda i: (0, 0))]
        + [across(array.shape, tile) for array in sources]
        + piece_specs(pieces, side, tile)
        + [ANY] * len(tokens),
        out_specs=[across((n, cols), tile), one],
        results=[value((n, cols), BF16), value((side, cols), BF16)],
    )(here, band, *sources, *arrays_of(pieces), *tokens)


def put_groups(groups, block, out_refs, before_ref, side):
    for group, out_ref in zip(groups, out_refs):
        for n, m in enumerate(group):
            out_ref[n * side : (n + 1) * side] = before_ref[...] if m is None else block(m)


def deal_kernel(groups, here_ref, r_ref, high_ref, *refs):
    side = high_ref.shape[0]
    place = lax.rem(here_ref[0], G)

    def block(m):
        last = jnp.bitwise_xor(place, m) == G - 1
        return jnp.where(last, high_ref[...], r_ref[m * side : (m + 1) * side])

    put_groups(groups, block, refs[-len(groups) :], refs[0], side)


def deal(here, groups, resid, high, before, *tokens):
    side, cols = high.shape
    tile = 512
    one = across((side, cols), tile)
    return call(
        functools.partial(deal_kernel, groups),
        1,
        grid=(cols // tile,),
        in_specs=[SMEM, across(resid.shape, tile), one] + [one] * len(before) + [ANY] * len(tokens),
        **group_results(groups, side, cols, tile),
    )(here, resid, high, *before, *tokens)


def back_kernel(groups, band_ref, own_ref, low_ref, high_ref, *refs):
    side = high_ref.shape[0]
    seeing = jnp.concatenate([own_ref[...], low_ref[...], high_ref[...]], axis=0)
    total = jnp.dot(band_ref[...], seeing, preferred_element_type=F32)
    put_groups(groups, lambda m: total[m * side : (m + 1) * side].astype(BF16), refs[-len(groups) :], refs[0], side)


def back(groups, band, own, low, high, before, *tokens):
    side, cols = high.shape
    tile = 512
    one = across((side, cols), tile)
    many = across(own.shape, tile)
    return call(
        functools.partial(back_kernel, groups),
        3,
        grid=(cols // tile,),
        in_specs=[pl.BlockSpec(band.shape, lambda i: (0, 0)), many, many, one]
        + [one] * len(before)
        + [ANY] * len(tokens),
        **group_results(groups, side, cols, tile),
    )(band, own, low, high, *before, *tokens)


def tv_flux(cur, above):
    rows, cols = cur.shape
    row = lax.broadcasted_iota(jnp.int32, (rows, cols), 0)
    col = lax.broadcasted_iota(jnp.int32, (rows, cols), 1)
    dz = above - cur
    dy = jnp.where(row == rows - 1, 0.0, pltpu.roll(cur, rows - 1, 0)) - cur
    dx = jnp.where(col == cols - 1, 0.0, pltpu.roll(cur, cols - 1, 1)) - cur
    scale = 0.5 * lax.rsqrt(dz * dz + dy * dy + dx * dx + 0.25)
    return dz * scale, dy * scale, dx * scale


def tv_below(cur, above):
    return tv_flux(cur, above)[0]


def tv_slice(cur, above, below_flux):
    rows, cols = cur.shape
    row = lax.broadcasted_iota(jnp.int32, (rows, cols), 0)
    col = lax.broadcasted_iota(jnp.int32, (rows, cols), 1)
    fz, fy, fx = tv_flux(cur, above)
    sides = 0.5 * cur * lax.rsqrt(cur * cur + 0.25)
    fy_low = jnp.where(row == 0, sides, pltpu.roll(fy, 1, 0))
    fx_low = jnp.where(col == 0, sides, pltpu.roll(fx, 1, 1))
    return (below_flux - fz) + (fy_low - fy) + (fx_low - fx), fz


def tv_kernel(last_ref, next_ref, vol_ref, *refs):
    out_ref, done_ref, flux_ref = refs[-3:]
    deep = vol_ref.shape[0]

    @pl.when(pl.program_id(0) == 0)
    def _():
        flux_ref[...] = tv_below(last_ref[0], vol_ref[0])

    def body(z, flux):
        out_ref[z], flux = tv_slice(vol_ref[z], vol_ref[z + 1], flux)
        return flux

    flux = lax.fori_loop(0, deep - 1, body, flux_ref[...], unroll=5)
    out_ref[deep - 1], flux_ref[...] = tv_slice(vol_ref[deep - 1], next_ref[0], flux)
    done_ref[...] = flux_ref[:, : done_ref.shape[1]]


def half_tv(volume, half, base, *tokens):
    depth, rows, cols = volume.shape
    deep = 16
    steps = depth // deep // 2
    first = half * steps
    body = pl.BlockSpec((deep, rows, cols), lambda i: (first + i, 0, 0))
    before = pl.BlockSpec((1, rows, cols), lambda i: (max(first * deep - 1, 0), 0, 0))
    after = pl.BlockSpec((1, rows, cols), lambda i: (jnp.minimum((first + i + 1) * deep, depth - 1), 0, 0))
    bases = [] if base is None else [far(base)]
    return call(
        tv_kernel,
        5,
        grid=(steps,),
        in_specs=[before, after, body] + [ANY] * (len(bases) + len(tokens)),
        out_specs=[body, pl.BlockSpec((rows, LANES), lambda i: (0, 0))],
        results=[pltpu.HBM(volume.shape, F32), value((rows, LANES), F32)],
        input_output_aliases={3: 0} if bases else {},
        scratch_shapes=[pltpu.VMEM((rows, cols), F32)],
    )(*[far(volume)] * 3, *bases, *tokens)


def local(volume, sinogram, weights, coverage, offsets):
    slabs = lax.axis_size("slab")
    here = lax.axis_index("slab").astype(jnp.int32).reshape(1)
    rows = volume.shape[1]
    single = ((0,), (1,), (2,), (3,))
    paired = ((0,), (1,), (2, 3))

    def in_steps(chunk, blocks, after):
        return direct(chunk, paired[:2], blocks[:2]) + in_two(chunk, blocks[2], after)

    *vols0, sent0, sent1 = cast_rows(here, volume, 0, single, sinogram)
    got0 = moved(sent0, G, only=G - 1)
    pieces0 = direct(0, single, vols0)
    tv, tv_done = half_tv(volume, 0, None, vols0[0])
    vols1 = cast_rows(here, volume, 1, paired, None, tv_done)
    own0, edge0 = pack(here, pieces0, ((0, 1, 2, 3),), 2 * rows, vols1[0])
    high0, low0 = moved(own0, -G), moved(edge0, G)
    sino0 = split_rows(here, sinogram, got0, 0, single, own0)
    got1 = moved(lax.optimization_barrier((sent1, sino0[0]))[0], G, only=G - 1)
    sinos0 = direct(0, single, sino0)
    own1, own1_more, edge1 = pack(here, in_steps(1, vols1, sino0[0]), ((0, 1), (2, 3)), 0, sino0[0])
    high1, low1 = moved(own1, -G), moved(edge1, G)
    sino1 = split_rows(here, sinogram, got1, 1, paired, own1)
    band_p, band_b = bands(here, coverage, offsets, weights, own0)

    resid0, down0 = project(here, band_p, [own0, high0, low0], sinos0, low1, sino1[0])
    from_low0, from_high0 = moved(resid0, G), moved(down0, -G)
    high1_more = moved(lax.optimization_barrier((own1_more, resid0))[0], -G)
    tv, tv_done = half_tv(volume, 1, tv, resid0)
    dealt0 = deal(here, paired, resid0, from_high0, [], tv_done)
    sinos1 = in_steps(1, sino1, dealt0[0])
    resid1, down1 = project(here, band_p, [own1, own1_more, high1, high1_more, low1], sinos1, dealt0[0])
    from_low1, from_high1 = moved(resid1, G), moved(down1, -G)
    resid_pieces0 = in_steps(0, dealt0, resid1)

    backs0 = back(paired, band_b, resid0, from_low0, from_high0, [], resid_pieces0[2][2])
    dealt1 = deal(here, paired, resid1, from_high1, [], backs0[0])
    back_pieces0 = in_steps(0, backs0, dealt1[0])
    ends = [pieces0[1][2], high0, pieces0[3][2], low0]
    r_last, tv = patch(here, coverage, offsets, weights, ends, volume, sinogram, tv, dealt1[0])
    resid_pieces1 = in_steps(1, dealt1, r_last)
    settled = arrays_of(resid_pieces0[1:] + resid_pieces1[1:] + back_pieces0[1:])
    backs1 = back(single, band_b, resid1, from_low1, from_high1, [], r_last, *settled)
    back_pieces1 = direct(1, single, backs1)

    gradient = finish(here, 0, tv, back_pieces0, backs1[0])
    residual = join_rows(here, slabs, 0, resid_pieces0, r_last, backs1[0])
    residual = join_rows(here, slabs, 1, resid_pieces1, residual)
    gradient = finish(here, 1, gradient, back_pieces1)
    return (gradient, residual)


def solution(mesh):
    placed = (P("slab", "grp", None), P("slab", "grp", None), P(), P(), P())
    return jax.shard_map(
        local,
        mesh=mesh,
        in_specs=placed,
        out_specs=(P("slab", "grp", None), P("slab", "grp", None)),
        check_vma=False,
    )
```

time: 153 us -> 223 us (1.46)
  Pallas kernels: 43.2 us -> 111 us
  starting transfers between devices: 48.2 us -> 53.9 us
  local copies, waits for them, and re-layouts: 8.35 us -> 6.11 us
    pallas_call x9 -> x14, Pallas kernels: 33.3 us -> 102 us  [the longest x2 68.4 us: cast_rows(): call(functools.partial(cast_kernel, groups, sent), 2, grid=(count,), in_s...]
    ppermute x20 -> x24, starting transfers between devices: 26.2 us -> 30.8 us  [swapped(): return lax.ppermute(value, 'slab', [(i, i ^ bits) for i in range(count)])]
    ppermute x20 -> x24, waiting for transfers between devices: 35.1 us -> 31.9 us  [swapped(): return lax.ppermute(value, 'slab', [(i, i ^ bits) for i in range(count)])]
    unnamed x46 -> x30, local copies, waits for them, and re-layouts: 8.26 us -> 5.32 us
    ppermute x9 -> x11, waiting for transfers between devices: 16.7 us -> 18 us  [moved(): return lax.ppermute(value, 'slab', pairs)]
    ppermute x9 -> x11, starting transfers between devices: 22 us -> 23.1 us  [moved(): return lax.ppermute(value, 'slab', pairs)]
  transfers between devices with their start and end apart: 29 -> 35, of which waited for: 9 -> 11; matrix products, arithmetic and copies ran while one was open for 0% -> 1% of each run, Pallas kernels for 22% -> 17%
where the time goes in v6:
time: 223 us; the launch traced here: 222 us
  Pallas kernels  111 us (50%)
  starting transfers between devices  53.9 us (24%)
  waiting for transfers between devices  50 us (22%)
  local copies, waits for them, and re-layouts  6.11 us (3%)
    pallas_call x2, Pallas kernels, cast_rows(): call(functools.partial(cast_kernel, groups, sent), 2, grid=(count,), in_s...  68.4 us
    ppermute x24, waiting for transfers between devices, swapped(): return lax.ppermute(value, 'slab', [(i, i ^ bits) for i in range(count)])  31.9 us
    ppermute x24, starting transfers between devices, swapped(): return lax.ppermute(value, 'slab', [(i, i ^ bits) for i in range(count)])  30.8 us
    ppermute x11, starting transfers between devices, moved(): return lax.ppermute(value, 'slab', pairs)  23.1 us
    ppermute x11, waiting for transfers between devices, moved(): return lax.ppermute(value, 'slab', pairs)  18 us
    pallas_call x2, Pallas kernels, half_tv(): call(tv_kernel, 5, grid=(steps,), in_specs=[before, after, body] + [ANY]...  11.5 us
    pallas_call x2, Pallas kernels, finish(): call(functools.partial(finish_kernel, [m for _, m, _, _ in pieces]), 2.6,...  5.86 us
    unnamed x30, local copies, waits for them, and re-layouts  5.32 us
  transfers between devices with their start and end apart: 35, of which 11 were waited for; matrix products, arithmetic and copies ran while one was open for 1% of the time, Pallas kernels for 17%

profile of v6, /device:TPU:1, one launch (start us, length us, event | category | flops | bytes accessed | tf_op | source)
XLA Modules:
  0.0 222.4 jit_solution(6950710069177134095)
XLA Ops:
  0.6 66.0 %shard_map.68 = (bf16[128,1024]{1,0:T(8,128)(2,1)S(1)}, bf16[144,1024]{1,0:T(8,128)(2,1)S(1)}, bf16[128,1024]{1,0:T(8,128)(2,1)S(1)}, bf16[144,1024]{1,0:T(8,128...) custom-call(s32[1]{0:T(128)} %bitcast.here_ref, f32[1024,1024]{1,0:T(8,128)} %bitcast.2, ...), custom_call_target="tpu_custom_call" | custom-call | flops 2300000000 | bytes 1000 | tf_op jit(solution)/shard_map/pallas_call | solution.py:169
  67.5 4.9 %collective-permute-start.2 = (bf16[144,1024]{1,0:T(8,128)(2,1)S(1)}, bf16[144,1024]{1,0:T(8,128)(2,1)S(1)}, u32[]{:S(2)}, u32[]{:S(2)}) collective-permute-start(bf16[144,1024]{1,0:T(8,128)(2,1)S(1)} %get-tuple-element.58), channel_id=1, source_target_pairs={{0,3},{1,2},{2,1},{3,0},{4,7},{5,6},{6,5},{7,4},{8,11},{9,10},{10,... | collective-permute-start | bytes 884744 | tf_op jit(solution)/shard_map/ppermute | solution.py:32
  72.4 5.7 %shard_map.69 = (f32[128,8,1024]{2,1,0:T(8,128)}, f32[8,128]{1,0:T(8,128)S(1)}) custom-call(f32[128,8,1024]{2,1,0:T(8,128)} %refs_5_.1, f32[128,8,1024]{2,1,0:T(8,128)} %refs_5_.1, f32[128,8,1024]{2,1,0:T(8,128)} %refs_5_.1, bf16[128,1024]{1,0:T(8,128)(2,1)S(1)} %get-tuple-element.56.refs_0_), custom_call_target="tpu_custom_call" | custom-call | flops 5750000128 | bytes 1000 | tf_op jit(solution)/shard_map/pallas_call | solution.py:585
  78.2 2.5 %shard_map.70 = (bf16[128,1024]{1,0:T(8,128)(2,1)S(1)}, bf16[128,1024]{1,0:T(8,128)(2,1)}, bf16[256,1024]{1,0:T(8,128)(2,1)S(1)}) custom-call(s32[1]{0:T(128)} %bitcast.here_ref, f32[1024,1024]{1,0:T(8,128)} %bitcast.6, f32[1024,1024]{1,0:T(8,128)} %bitcast.7, f32[8,128]{1,0:T(8,128)S(1)} %get-tuple-element.59.refs_2_), custom_call_target="tpu_custom_call" | custom-call | flops 2300000000 | bytes 1000 | tf_op jit(solution)/shard_map/pallas_call | solution.py:169
  80.6 4.1 %collective-permute-done.1.refs_2_ = bf16[128,1024]{1,0:T(8,128)(2,1)S(1)} collective-permute-done((bf16[128,1024]{1,0:T(8,128)(2,1)S(1)}, bf16[128,1024]{1,0:T(8,128)(2,1)S(1)}, u32[]{:S(2)}, u32[]{:S(2)}) %collective-permute-start.1) | collective-permute-done | bytes 262176 | tf_op jit(solution)/shard_map/ppermute | solution.py:32
  84.7 1.3 shard_map.71
  86.1 2.4 %shard_map.73 = (bf16[128,1024]{1,0:T(8,128)(2,1)}, bf16[128,1024]{1,0:T(8,128)(2,1)}, bf16[128,1024]{1,0:T(8,128)(2,1)}, bf16[128,1024]{1,0:T(8,128)(2,1)}) custom-call(s32[1]{0:T(128)} %bitcast.here_ref, bf16[128,8,1024]{2,1,0:T(8,128)(2,1)} %refs_6_.1, bf16[128,8,512]{2,1,0:T(8,128)(2,1)S(1)} %collective-permute-done.5.got_ref, ...), custom_call_target="tpu_custom_call" | custom-call | flops 2300000000 | bytes 1000 | tf_op jit(solution)/shard_map/pallas_call | solution.py:244
  89.2 4.6 %collective-permute-start.10 = (bf16[256,1024]{1,0:T(8,128)(2,1)S(1)}, bf16[256,1024]{1,0:T(8,128)(2,1)S(1)}, u32[]{:S(2)}, u32[]{:S(2)}) collective-permute-start(bf16[256,1024]{1,0:T(8,128)(2,1)S(1)} %get-tuple-element.71), channel_id=1, source_target_pairs={{0,2},{1,3},{2,0},{3,1},{4,6},{5,7},{6,4},{7,5},{8,10},{9,11},{10,... | collective-permute-start | bytes 1572872 | tf_op jit(solution)/shard_map/ppermute | solution.py:32
  93.9 1.3 collective-permute-start.3
  95.2 9.5 %collective-permute-done.10.refs_2_ = bf16[256,1024]{1,0:T(8,128)(2,1)S(1)} collective-permute-done((bf16[256,1024]{1,0:T(8,128)(2,1)S(1)}, bf16[256,1024]{1,0:T(8,128)(2,1)S(1)}, u32[]{:S(2)}, u32[]{:S(2)}) %collective-permute-start.10) | collective-permute-done | bytes 524320 | tf_op jit(solution)/shard_map/ppermute | solution.py:32
  105.4 3.1 %collective-permute-start.4 = (bf16[144,1024]{1,0:T(8,128)(2,1)}, bf16[144,1024]{1,0:T(8,128)(2,1)S(1)}, u32[]{:S(2)}, u32[]{:S(2)}) collective-permute-start(bf16[144,1024]{1,0:T(8,128)(2,1)} %get-tuple-element.62), channel_id=1, source_target_pairs={{0,4},{1,5},{2,6},{3,7},{4,8},{5,9},{6,10},{7,11},{8,12},{9,13},{1... | collective-permute-start | bytes 884744 | tf_op jit(solution)/shard_map/ppermute | solution.py:27
  110.2 1.8 collective-permute-start.7
  112.0 0.9 copy-done.3
  112.9 0.9 copy-done.6
  113.9 1.3 shard_map.74
  115.2 2.5 %collective-permute-start.8 = (bf16[128,1024]{1,0:T(8,128)(2,1)S(1)}, bf16[128,1024]{1,0:T(8,128)(2,1)S(1)}, u32[]{:S(2)}, u32[]{:S(2)}) collective-permute-start(bf16[128,1024]{1,0:T(8,128)(2,1)S(1)} %copy-done.12), channel_id=1, source_target_pairs={{0,3},{1,2},{2,1},{3,0},{4,7},{5,6},{6,5},{7,4},{8,11},{9,10},{10,... | collective-permute-start | bytes 786440 | tf_op jit(solution)/shard_map/ppermute | solution.py:32
  117.7 4.0 %collective-permute-start.12 = (bf16[128,1024]{1,0:T(8,128)(2,1)S(1)}, bf16[128,1024]{1,0:T(8,128)(2,1)S(1)}, u32[]{:S(2)}, u32[]{:S(2)}) collective-permute-start(bf16[128,1024]{1,0:T(8,128)(2,1)S(1)} %get-tuple-element.73), channel_id=1, source_target_pairs={{0,4},{1,5},{2,6},{3,7},{4,8},{5,9},{6,10},{7,11},{8,12},{9,13},{1... | collective-permute-start | bytes 786440 | tf_op jit(solution)/shard_map/ppermute | solution.py:27
  121.7 2.7 %shard_map.72 = (bf16[512,1152]{1,0:T(8,128)(2,1)}, bf16[512,1152]{1,0:T(8,128)(2,1)}) custom-call(s32[1]{0:T(128)} %bitcast.here_ref, s32[16,6]{1,0:T(8,128)S(1)} %copy.15.cover_ref, s32[16,6]{1,0:T(8,128)S(1)} %copy.16.offset_ref, bf16[8,128,128]{2,1,0:T(8,128)(2,1)S(1)} %copy-done, bf16[528,1024]{1,0:T(8,128)(2,1)} %get-tuple-element.61.refs_0_), custom_call_target="tpu_custom_call" | custom-call | flops 1840000000 | bytes 1000 | tf_op jit(solution)/shard_map/pallas_call | solution.py:438
  124.4 2.6 %shard_map.75 = (bf16[128,1024]{1,0:T(8,128)(2,1)}, bf16[128,1024]{1,0:T(8,128)(2,1)}, bf16[256,1024]{1,0:T(8,128)(2,1)}) custom-call(s32[1]{0:T(128)} %bitcast.here_ref, bf16[128,8,1024]{2,1,0:T(8,128)(2,1)} %refs_6_.1, bf16[128,8,512]{2,1,0:T(8,128)(2,1)S(1)} %collective-permute-done.13.got_ref, bf16[256,1024]{1,0:T(8,128)(2,1)S(1)} %get-tuple-element.76.refs_0_), custom_call_target="tpu_custom_call" | custom-call | flops 2300000000 | bytes 1000 | tf_op jit(solution)/shard_map/pallas_call | solution.py:244
  127.1 1.3 collective-permute-start.14
  128.4 0.9 copy-done.8
  129.4 3.0 %shard_map.76 = (bf16[512,1024]{1,0:T(8,128)(2,1)S(1)}, bf16[128,1024]{1,0:T(8,128)(2,1)S(1)}) custom-call(s32[1]{0:T(128)} %bitcast.here_ref, bf16[512,1152]{1,0:T(8,128)(2,1)S(1)} %copy-done.5, bf16[528,1024]{1,0:T(8,128)(2,1)} %get-tuple-element.61.refs_0_, bf16[528,1024]{1,0:T(8,128)(2,1)S(1)} %collective-permute-done.3.refs_1_.refs_2_, ...), custom_call_target="tpu_custom_call" | custom-call | flops 3449999872 | bytes 1000 | tf_op jit(solution)/shard_map/pallas_call | solution.py:467
  132.3 1.3 collective-permute-start.18
  133.7 4.8 %collective-permute-start.21 = (bf16[512,1024]{1,0:T(8,128)(2,1)S(1)}, bf16[512,1024]{1,0:T(8,128)(2,1)S(1)}, u32[]{:S(2)}, u32[]{:S(2)}) collective-permute-start(bf16[512,1024]{1,0:T(8,128)(2,1)S(1)} %get-tuple-element.78.refs_1_.r_ref.own_ref), channel_id=1, source_target_pairs={{0,4},{1,5},{2,6},{3,7},{4,8},{5,9},{6,10},{7,11},{8,12},{9,13},{1... | collective-permute-start | bytes 3145736 | tf_op jit(solution)/shard_map/ppermute | solution.py:27
  138.5 1.3 collective-permute-start.15
  139.8 5.8 %shard_map.77 = (f32[128,8,1024]{2,1,0:T(8,128)}, f32[8,128]{1,0:T(8,128)S(1)}) custom-call(f32[128,8,1024]{2,1,0:T(8,128)} %refs_5_.1, f32[128,8,1024]{2,1,0:T(8,128)} %refs_5_.1, f32[128,8,1024]{2,1,0:T(8,128)} %refs_5_.1, f32[128,8,1024]{2,1,0:T(8,128)} %get-tuple-element.63.refs_0_, ...), custom_call_target="tpu_custom_call", output_to_operand_aliasing={{0}: (3, {})} | custom-call | flops 5750000128 | bytes 1000 | tf_op jit(solution)/shard_map/pallas_call | solution.py:585
  145.6 3.0 %collective-permute-done.18.high_ref = bf16[128,1024]{1,0:T(8,128)(2,1)S(1)} collective-permute-done((bf16[128,1024]{1,0:T(8,128)(2,1)S(1)}, bf16[128,1024]{1,0:T(8,128)(2,1)S(1)}, u32[]{:S(2)}, u32[]{:S(2)}) %collective-permute-start.18) | collective-permute-done | bytes 262176 | tf_op jit(solution)/shard_map/ppermute | solution.py:27
  150.3 9.5 %collective-permute-done.15.refs_3_ = bf16[256,1024]{1,0:T(8,128)(2,1)S(1)} collective-permute-done((bf16[256,1024]{1,0:T(8,128)(2,1)S(1)}, bf16[256,1024]{1,0:T(8,128)(2,1)S(1)}, u32[]{:S(2)}, u32[]{:S(2)}) %collective-permute-start.15) | collective-permute-done | bytes 524320 | tf_op jit(solution)/shard_map/ppermute | solution.py:27
  159.8 2.1 shard_map.79
  162.0 3.2 %collective-permute-start.26 = (bf16[512,1024]{1,0:T(8,128)(2,1)S(1)}, bf16[512,1024]{1,0:T(8,128)(2,1)S(1)}, u32[]{:S(2)}, u32[]{:S(2)}) collective-permute-start(bf16[512,1024]{1,0:T(8,128)(2,1)S(1)} %get-tuple-element.88.r_ref.own_ref), channel_id=1, source_target_pairs={{0,4},{1,5},{2,6},{3,7},{4,8},{5,9},{6,10},{7,11},{8,12},{9,13},{1... | collective-permute-start | bytes 3145736 | tf_op jit(solution)/shard_map/ppermute | solution.py:27
  165.2 1.3 collective-permute-start.20
  166.5 2.0 shard_map.80
  168.5 5.5 %collective-permute-done.20.high_ref = bf16[128,1024]{1,0:T(8,128)(2,1)S(1)} collective-permute-done((bf16[128,1024]{1,0:T(8,128)(2,1)S(1)}, bf16[128,1024]{1,0:T(8,128)(2,1)S(1)}, u32[]{:S(2)}, u32[]{:S(2)}) %collective-permute-start.20) | collective-permute-done | bytes 262176 | tf_op jit(solution)/shard_map/ppermute | solution.py:27
  174.4 1.5 collective-permute-start.24
  175.8 2.4 %collective-permute-start.27 = (bf16[128,1024]{1,0:T(8,128)(2,1)S(1)}, bf16[128,1024]{1,0:T(8,128)(2,1)S(1)}, u32[]{:S(2)}, u32[]{:S(2)}) collective-permute-start(bf16[128,1024]{1,0:T(8,128)(2,1)S(1)} %get-tuple-element.100), channel_id=1, source_target_pairs={{0,1},{1,0},{2,3},{3,2},{4,5},{5,4},{6,7},{7,6},{8,9},{9,8},{10,11... | collective-permute-start | bytes 786440 | tf_op jit(solution)/shard_map/ppermute | solution.py:32
  178.3 2.5 %shard_map.82 = (bf16[128,8,1024]{2,1,0:T(8,128)(2,1)}, f32[128,8,1024]{2,1,0:T(8,128)}) custom-call(s32[1]{0:T(128)} %bitcast.here_ref, s32[16,6]{1,0:T(8,128)S(1)} %copy.15.cover_ref, s32[16,6]{1,0:T(8,128)S(1)} %copy.16.offset_ref, bf16[8,128,128]{2,1,0:T(8,128)(2,1)S(1)} %copy-done, ...), custom_call_target="tpu_custom_call", output_to_operand_aliasing={{1}: (10, {})} | custom-call | flops 3449999872 | bytes 1000 | tf_op jit(solution)/shard_map/pallas_call | solution.py:313
  180.8 5.1 %collective-permute-done.30.refs_5_.refs_2_ = bf16[256,1024]{1,0:T(8,128)(2,1)S(1)} collective-permute-done((bf16[256,1024]{1,0:T(8,128)(2,1)S(1)}, bf16[256,1024]{1,0:T(8,128)(2,1)S(1)}, u32[]{:S(2)}, u32[]{:S(2)}) %collective-permute-start.30) | collective-permute-done | bytes 524320 | tf_op jit(solution)/shard_map/ppermute | solution.py:32
  185.9 5.1 %collective-permute-start.29 = (bf16[128,1024]{1,0:T(8,128)(2,1)S(1)}, bf16[128,1024]{1,0:T(8,128)(2,1)S(1)}, u32[]{:S(2)}, u32[]{:S(2)}) collective-permute-start(bf16[128,1024]{1,0:T(8,128)(2,1)S(1)} %get-tuple-element.101), channel_id=1, source_target_pairs={{0,1},{1,0},{2,3},{3,2},{4,5},{5,4},{6,7},{7,6},{8,9},{9,8},{10,11... | collective-permute-start | bytes 786440 | tf_op jit(solution)/shard_map/ppermute | solution.py:32
  191.1 6.1 %collective-permute-done.24.refs_8_.refs_2_ = bf16[256,1024]{1,0:T(8,128)(2,1)S(1)} collective-permute-done((bf16[256,1024]{1,0:T(8,128)(2,1)S(1)}, bf16[256,1024]{1,0:T(8,128)(2,1)S(1)}, u32[]{:S(2)}, u32[]{:S(2)}) %collective-permute-start.24) | collective-permute-done | bytes 524320 | tf_op jit(solution)/shard_map/ppermute | solution.py:32
  197.2 2.7 %collective-permute-start.23 = (bf16[128,1024]{1,0:T(8,128)(2,1)S(1)}, bf16[128,1024]{1,0:T(8,128)(2,1)S(1)}, u32[]{:S(2)}, u32[]{:S(2)}) collective-permute-start(bf16[128,1024]{1,0:T(8,128)(2,1)S(1)} %get-tuple-element.96), channel_id=1, source_target_pairs={{0,1},{1,0},{2,3},{3,2},{4,5},{5,4},{6,7},{7,6},{8,9},{9,8},{10,11... | collective-permute-start | bytes 786440 | tf_op jit(solution)/shard_map/ppermute | solution.py:32
  201.9 1.6 copy-done.1
  203.5 2.0 shard_map.83
  205.8 1.9 collective-permute-start.34
  207.7 1.6 shard_map.86.refs_4_
  209.3 1.6 shard_map.87
  210.9 2.9 %shard_map.84.tv_ref = f32[128,8,1024]{2,1,0:T(8,128)} custom-call(s32[1]{0:T(128)} %bitcast.here_ref, f32[128,8,1024]{2,1,0:T(8,128)} %get-tuple-element.95.tv_ref, bf16[128,1024]{1,0:T(8,128)(2,1)S(1)} %get-tuple-element.93.refs_0_, bf16[128,1024]{1,0:T(8,128)(2,1)S(1)} %collective-permute-done.23.refs_7_.refs_1_, ...), custom_call_target="tpu_custom_call", output_to_operand_aliasing={{}: (1, {})} | custom-call | flops 2990000128 | bytes 1000 | tf_op jit(solution)/shard_map/pallas_call | solution.py:390
  213.8 5.7 %collective-permute-done.34.refs_3_ = bf16[128,1024]{1,0:T(8,128)(2,1)S(1)} collective-permute-done((bf16[128,1024]{1,0:T(8,128)(2,1)S(1)}, bf16[128,1024]{1,0:T(8,128)(2,1)S(1)}, u32[]{:S(2)}, u32[]{:S(2)}) %collective-permute-start.34) | collective-permute-done | bytes 262176 | tf_op jit(solution)/shard_map/ppermute | solution.py:32
  219.5 2.9 %shard_map.85 = f32[128,8,1024]{2,1,0:T(8,128)} custom-call(s32[1]{0:T(128)} %bitcast.here_ref, f32[128,8,1024]{2,1,0:T(8,128)} %shard_map.84.tv_ref, bf16[128,1024]{1,0:T(8,128)(2,1)S(1)} %get-tuple-element.104.refs_4_.refs_0_, bf16[128,1024]{1,0:T(8,128)(2,1)S(1)} %collective-permute-done.32.refs_1_, ...), custom_call_target="tpu_custom_call", output_to_operand_aliasing={{}: (1, {})} | custom-call | flops 2990000128 | bytes 1000 | tf_op jit(solution)/shard_map/pallas_call | solution.py:390
  (77 shorter events, 8.6 us)
Async XLA Ops:
  66.6 19.5 %collective-permute-start.5 = (bf16[128,8,512]{2,1,0:T(8,128)(2,1)}, bf16[128,8,512]{2,1,0:T(8,128)(2,1)S(1)}, u32[]{:S(2)}, u32[]{:S(2)}) collective-permute-start(bf16[128,8,512]{2,1,0:T(8,128)(2,1)} %get-tuple-element.65), channel_id=1, source_target_pairs={{3,7},{7,11},{11,15},{19,23},{23,27},{27,31}} | collective-permute-start | bytes 3145736 | tf_op jit(solution)/shard_map/ppermute | solution.py:27
  67.3 17.4 %collective-permute-start = (bf16[144,1024]{1,0:T(8,128)(2,1)S(1)}, bf16[144,1024]{1,0:T(8,128)(2,1)S(1)}, u32[]{:S(2)}, u32[]{:S(2)}) collective-permute-start(bf16[144,1024]{1,0:T(8,128)(2,1)S(1)} %get-tuple-element.55), channel_id=1, source_target_pairs={{0,1},{1,0},{2,3},{3,2},{4,5},{5,4},{6,7},{7,6},{8,9},{9,8},{10,11... | collective-permute-start | bytes 884744 | tf_op jit(solution)/shard_map/ppermute | solution.py:32
  67.5 17.3 %collective-permute-start.2 = (bf16[144,1024]{1,0:T(8,128)(2,1)S(1)}, bf16[144,1024]{1,0:T(8,128)(2,1)S(1)}, u32[]{:S(2)}, u32[]{:S(2)}) collective-permute-start(bf16[144,1024]{1,0:T(8,128)(2,1)S(1)} %get-tuple-element.58), channel_id=1, source_target_pairs={{0,3},{1,2},{2,1},{3,0},{4,7},{5,6},{6,5},{7,4},{8,11},{9,10},{10,... | collective-permute-start | bytes 884744 | tf_op jit(solution)/shard_map/ppermute | solution.py:32
  72.4 12.3 %collective-permute-start.1 = (bf16[128,1024]{1,0:T(8,128)(2,1)S(1)}, bf16[128,1024]{1,0:T(8,128)(2,1)S(1)}, u32[]{:S(2)}, u32[]{:S(2)}) collective-permute-start(bf16[128,1024]{1,0:T(8,128)(2,1)S(1)} %get-tuple-element.57), channel_id=1, source_target_pairs={{0,2},{1,3},{2,0},{3,1},{4,6},{5,7},{6,4},{7,5},{8,10},{9,11},{10,... | collective-permute-start | bytes 786440 | tf_op jit(solution)/shard_map/ppermute | solution.py:32
  80.6 5.4 %copy-start.2 = (bf16[128,1024]{1,0:T(8,128)(2,1)}, bf16[128,1024]{1,0:T(8,128)(2,1)S(1)}, u32[]{:S(2)}) copy-start(bf16[128,1024]{1,0:T(8,128)(2,1)S(1)} %get-tuple-element.60.refs_4_.refs_0_) | copy-start | bytes 786436
  86.1 22.5 %copy-start.10 = (s32[16,6]{0,1:T(8,128)S(1)}, s32[16,6]{0,1:T(8,128)}, u32[]{:S(2)}) copy-start(s32[16,6]{0,1:T(8,128)} %param.8) | copy-start | bytes 1156
  88.5 29.2 %collective-permute-start.13 = (bf16[128,8,512]{2,1,0:T(8,128)(2,1)}, bf16[128,8,512]{2,1,0:T(8,128)(2,1)S(1)}, u32[]{:S(2)}, u32[]{:S(2)}) collective-permute-start(bf16[128,8,512]{2,1,0:T(8,128)(2,1)} %get-tuple-element.75), channel_id=1, source_target_pairs={{3,7},{7,11},{11,15},{19,23},{23,27},{27,31}} | collective-permute-start | bytes 3145736 | tf_op jit(solution)/shard_map/ppermute | solution.py:27
  89.2 15.5 %collective-permute-start.10 = (bf16[256,1024]{1,0:T(8,128)(2,1)S(1)}, bf16[256,1024]{1,0:T(8,128)(2,1)S(1)}, u32[]{:S(2)}, u32[]{:S(2)}) collective-permute-start(bf16[256,1024]{1,0:T(8,128)(2,1)S(1)} %get-tuple-element.71), channel_id=1, source_target_pairs={{0,2},{1,3},{2,0},{3,1},{4,6},{5,7},{6,4},{7,5},{8,10},{9,11},{10,... | collective-permute-start | bytes 1572872 | tf_op jit(solution)/shard_map/ppermute | solution.py:32
  93.9 34.5 %collective-permute-start.3 = (bf16[528,1024]{1,0:T(8,128)(2,1)}, bf16[528,1024]{1,0:T(8,128)(2,1)S(1)}, u32[]{:S(2)}, u32[]{:S(2)}) collective-permute-start(bf16[528,1024]{1,0:T(8,128)(2,1)} %get-tuple-element.61.refs_0_), channel_id=1, source_target_pairs={{4,0},{5,1},{6,2},{7,3},{8,4},{9,5},{10,6},{11,7},{12,8},{13,9},{1... | collective-permute-start | bytes 3244040 | tf_op jit(solution)/shard_map/ppermute | solution.py:27
  95.1 14.3 %collective-permute-start.9 = (bf16[128,1024]{1,0:T(8,128)(2,1)}, bf16[128,1024]{1,0:T(8,128)(2,1)}, u32[]{:S(2)}, u32[]{:S(2)}) collective-permute-start(bf16[128,1024]{1,0:T(8,128)(2,1)} %get-tuple-element.70), channel_id=1, source_target_pairs={{0,1},{1,0},{2,3},{3,2},{4,5},{5,4},{6,7},{7,6},{8,9},{9,8},{10,11... | collective-permute-start | bytes 786440 | tf_op jit(solution)/shard_map/ppermute | solution.py:32
  105.4 4.8 %collective-permute-start.11 = (bf16[128,1024]{1,0:T(8,128)(2,1)}, bf16[128,1024]{1,0:T(8,128)(2,1)}, u32[]{:S(2)}, u32[]{:S(2)}) collective-permute-start(bf16[128,1024]{1,0:T(8,128)(2,1)} %slice.15), channel_id=1, source_target_pairs={{0,1},{1,0},{2,3},{3,2},{4,5},{5,4},{6,7},{7,6},{8,9},{9,8},{10,11... | collective-permute-start | bytes 786440 | tf_op jit(solution)/shard_map/ppermute | solution.py:32
  105.4 9.7 %collective-permute-start.4 = (bf16[144,1024]{1,0:T(8,128)(2,1)}, bf16[144,1024]{1,0:T(8,128)(2,1)S(1)}, u32[]{:S(2)}, u32[]{:S(2)}) collective-permute-start(bf16[144,1024]{1,0:T(8,128)(2,1)} %get-tuple-element.62), channel_id=1, source_target_pairs={{0,4},{1,5},{2,6},{3,7},{4,8},{5,9},{6,10},{7,11},{8,12},{9,13},{1... | collective-permute-start | bytes 884744 | tf_op jit(solution)/shard_map/ppermute | solution.py:27
  109.4 17.6 %collective-permute-start.6 = (bf16[128,1024]{1,0:T(8,128)(2,1)}, bf16[128,1024]{1,0:T(8,128)(2,1)S(1)}, u32[]{:S(2)}, u32[]{:S(2)}) collective-permute-start(bf16[128,1024]{1,0:T(8,128)(2,1)} %get-tuple-element.67), channel_id=1, source_target_pairs={{0,1},{1,0},{2,3},{3,2},{4,5},{5,4},{6,7},{7,6},{8,9},{9,8},{10,11... | collective-permute-start | bytes 786440 | tf_op jit(solution)/shard_map/ppermute | solution.py:32
  110.2 11.5 %copy-start = (bf16[8,128,128]{2,1,0:T(8,128)(2,1)S(1)}, bf16[8,128,128]{2,1,0:T(8,128)(2,1)}, u32[]{:S(2)}) copy-start(bf16[8,128,128]{2,1,0:T(8,128)(2,1)} %refs_0_.1) | copy-start | bytes 786436
  110.2 18.1 %collective-permute-start.7 = (bf16[128,1024]{1,0:T(8,128)(2,1)}, bf16[128,1024]{1,0:T(8,128)(2,1)S(1)}, u32[]{:S(2)}, u32[]{:S(2)}) collective-permute-start(bf16[128,1024]{1,0:T(8,128)(2,1)} %get-tuple-element.68), channel_id=1, source_target_pairs={{0,2},{1,3},{2,0},{3,1},{4,6},{5,7},{6,4},{7,5},{8,10},{9,11},{10,... | collective-permute-start | bytes 786440 | tf_op jit(solution)/shard_map/ppermute | solution.py:32
  112.0 0.9 copy-start.3
  113.9 1.3 copy-start.12
  115.2 13.2 %collective-permute-start.8 = (bf16[128,1024]{1,0:T(8,128)(2,1)S(1)}, bf16[128,1024]{1,0:T(8,128)(2,1)S(1)}, u32[]{:S(2)}, u32[]{:S(2)}) collective-permute-start(bf16[128,1024]{1,0:T(8,128)(2,1)S(1)} %copy-done.12), channel_id=1, source_target_pairs={{0,3},{1,2},{2,1},{3,0},{4,7},{5,6},{6,5},{7,4},{8,11},{9,10},{10,... | collective-permute-start | bytes 786440 | tf_op jit(solution)/shard_map/ppermute | solution.py:32
  117.7 10.7 %collective-permute-start.12 = (bf16[128,1024]{1,0:T(8,128)(2,1)S(1)}, bf16[128,1024]{1,0:T(8,128)(2,1)S(1)}, u32[]{:S(2)}, u32[]{:S(2)}) collective-permute-start(bf16[128,1024]{1,0:T(8,128)(2,1)S(1)} %get-tuple-element.73), channel_id=1, source_target_pairs={{0,4},{1,5},{2,6},{3,7},{4,8},{5,9},{6,10},{7,11},{8,12},{9,13},{1... | collective-permute-start | bytes 786440 | tf_op jit(solution)/shard_map/ppermute | solution.py:27
  124.4 4.0 %copy-start.5 = (bf16[512,1152]{1,0:T(8,128)(2,1)S(1)}, bf16[512,1152]{1,0:T(8,128)(2,1)}, u32[]{:S(2)}) copy-start(bf16[512,1152]{1,0:T(8,128)(2,1)} %get-tuple-element.64.band_ref) | copy-start | bytes 3538948
  124.4 4.0 %copy-start.7 = (bf16[128,1024]{1,0:T(8,128)(2,1)S(1)}, bf16[128,1024]{1,0:T(8,128)(2,1)}, u32[]{:S(2)}) copy-start(bf16[128,1024]{1,0:T(8,128)(2,1)} %get-tuple-element.66.refs_4_.refs_3_) | copy-start | bytes 786436
  127.1 22.5 %collective-permute-start.14 = (bf16[256,1024]{1,0:T(8,128)(2,1)S(1)}, bf16[256,1024]{1,0:T(8,128)(2,1)S(1)}, u32[]{:S(2)}, u32[]{:S(2)}) collective-permute-start(bf16[256,1024]{1,0:T(8,128)(2,1)S(1)} %get-tuple-element.76.refs_0_), channel_id=1, source_target_pairs={{4,0},{5,1},{6,2},{7,3},{8,4},{9,5},{10,6},{11,7},{12,8},{13,9},{1... | collective-permute-start | bytes 1572872 | tf_op jit(solution)/shard_map/ppermute | solution.py:27
  128.4 1.0 copy-start.8
  129.4 4.3 %copy-start.11 = (bf16[256,1024]{1,0:T(8,128)(2,1)S(1)}, bf16[256,1024]{1,0:T(8,128)(2,1)}, u32[]{:S(2)}) copy-start(bf16[256,1024]{1,0:T(8,128)(2,1)} %get-tuple-element.83) | copy-start | bytes 1572868
  132.3 16.3 %collective-permute-start.18 = (bf16[128,1024]{1,0:T(8,128)(2,1)S(1)}, bf16[128,1024]{1,0:T(8,128)(2,1)S(1)}, u32[]{:S(2)}, u32[]{:S(2)}) collective-permute-start(bf16[128,1024]{1,0:T(8,128)(2,1)S(1)} %get-tuple-element.84), channel_id=1, source_target_pairs={{4,0},{5,1},{6,2},{7,3},{8,4},{9,5},{10,6},{11,7},{12,8},{13,9},{1... | collective-permute-start | bytes 786440 | tf_op jit(solution)/shard_map/ppermute | solution.py:27
  133.6 15.7 %collective-permute-start.17 = (bf16[256,1024]{1,0:T(8,128)(2,1)S(1)}, bf16[256,1024]{1,0:T(8,128)(2,1)S(1)}, u32[]{:S(2)}, u32[]{:S(2)}) collective-permute-start(bf16[256,1024]{1,0:T(8,128)(2,1)S(1)} %copy-done.11), channel_id=1, source_target_pairs={{0,2},{1,3},{2,0},{3,1},{4,6},{5,7},{6,4},{7,5},{8,10},{9,11},{10,... | collective-permute-start | bytes 1572872 | tf_op jit(solution)/shard_map/ppermute | solution.py:32
  133.7 32.8 %collective-permute-start.21 = (bf16[512,1024]{1,0:T(8,128)(2,1)S(1)}, bf16[512,1024]{1,0:T(8,128)(2,1)S(1)}, u32[]{:S(2)}, u32[]{:S(2)}) collective-permute-start(bf16[512,1024]{1,0:T(8,128)(2,1)S(1)} %get-tuple-element.78.refs_1_.r_ref.own_ref), channel_id=1, source_target_pairs={{0,4},{1,5},{2,6},{3,7},{4,8},{5,9},{6,10},{7,11},{8,12},{9,13},{1... | collective-permute-start | bytes 3145736 | tf_op jit(solution)/shard_map/ppermute | solution.py:27
  138.5 21.3 %collective-permute-start.15 = (bf16[256,1024]{1,0:T(8,128)(2,1)S(1)}, bf16[256,1024]{1,0:T(8,128)(2,1)S(1)}, u32[]{:S(2)}, u32[]{:S(2)}) collective-permute-start(bf16[256,1024]{1,0:T(8,128)(2,1)S(1)} %get-tuple-element.81.refs_1_), channel_id=1, source_target_pairs={{4,0},{5,1},{6,2},{7,3},{8,4},{9,5},{10,6},{11,7},{12,8},{13,9},{1... | collective-permute-start | bytes 1572872 | tf_op jit(solution)/shard_map/ppermute | solution.py:27
  139.8 8.8 %copy-start.13 = (bf16[128,1024]{1,0:T(8,128)(2,1)S(1)}, bf16[128,1024]{1,0:T(8,128)(2,1)}, u32[]{:S(2)}) copy-start(bf16[128,1024]{1,0:T(8,128)(2,1)} %get-tuple-element.82) | copy-start | bytes 786436
  148.6 1.7 collective-permute-start.16
  149.0 10.9 %copy-start.9 = (bf16[128,1024]{1,0:T(8,128)(2,1)S(1)}, bf16[128,1024]{1,0:T(8,128)(2,1)}, u32[]{:S(2)}) copy-start(bf16[128,1024]{1,0:T(8,128)(2,1)} %get-tuple-element.77.refs_8_.refs_5_) | copy-start | bytes 786436
  149.3 10.5 %collective-permute-start.19 = (bf16[128,1024]{1,0:T(8,128)(2,1)S(1)}, bf16[128,1024]{1,0:T(8,128)(2,1)S(1)}, u32[]{:S(2)}, u32[]{:S(2)}) collective-permute-start(bf16[128,1024]{1,0:T(8,128)(2,1)S(1)} %slice.16), channel_id=1, source_target_pairs={{0,1},{1,0},{2,3},{3,2},{4,5},{5,4},{6,7},{7,6},{8,9},{9,8},{10,11... | collective-permute-start | bytes 786440 | tf_op jit(solution)/shard_map/ppermute | solution.py:32
  149.6 16.9 %copy-start.4 = (bf16[512,1152]{1,0:T(8,128)(2,1)S(1)}, bf16[512,1152]{1,0:T(8,128)(2,1)}, u32[]{:S(2)}) copy-start(bf16[512,1152]{1,0:T(8,128)(2,1)} %get-tuple-element.90.band_ref) | copy-start | bytes 3538948
  149.6 15.6 %collective-permute-start.22 = (bf16[256,1024]{1,0:T(8,128)(2,1)S(1)}, bf16[256,1024]{1,0:T(8,128)(2,1)S(1)}, u32[]{:S(2)}, u32[]{:S(2)}) collective-permute-start(bf16[256,1024]{1,0:T(8,128)(2,1)S(1)} %get-tuple-element.91), channel_id=1, source_target_pairs={{0,2},{1,3},{2,0},{3,1},{4,6},{5,7},{6,4},{7,5},{8,10},{9,11},{10,... | collective-permute-start | bytes 1572872 | tf_op jit(solution)/shard_map/ppermute | solution.py:32
  162.0 40.0 %collective-permute-start.26 = (bf16[512,1024]{1,0:T(8,128)(2,1)S(1)}, bf16[512,1024]{1,0:T(8,128)(2,1)S(1)}, u32[]{:S(2)}, u32[]{:S(2)}) collective-permute-start(bf16[512,1024]{1,0:T(8,128)(2,1)S(1)} %get-tuple-element.88.r_ref.own_ref), channel_id=1, source_target_pairs={{0,4},{1,5},{2,6},{3,7},{4,8},{5,9},{6,10},{7,11},{8,12},{9,13},{1... | collective-permute-start | bytes 3145736 | tf_op jit(solution)/shard_map/ppermute | solution.py:27
  165.2 8.8 %collective-permute-start.20 = (bf16[128,1024]{1,0:T(8,128)(2,1)S(1)}, bf16[128,1024]{1,0:T(8,128)(2,1)S(1)}, u32[]{:S(2)}, u32[]{:S(2)}) collective-permute-start(bf16[128,1024]{1,0:T(8,128)(2,1)S(1)} %get-tuple-element.89), channel_id=1, source_target_pairs={{4,0},{5,1},{6,2},{7,3},{8,4},{9,5},{10,6},{11,7},{12,8},{13,9},{1... | collective-permute-start | bytes 786440 | tf_op jit(solution)/shard_map/ppermute | solution.py:27
  174.3 11.7 %collective-permute-start.30 = (bf16[256,1024]{1,0:T(8,128)(2,1)S(1)}, bf16[256,1024]{1,0:T(8,128)(2,1)S(1)}, u32[]{:S(2)}, u32[]{:S(2)}) collective-permute-start(bf16[256,1024]{1,0:T(8,128)(2,1)S(1)} %get-tuple-element.102), channel_id=1, source_target_pairs={{0,2},{1,3},{2,0},{3,1},{4,6},{5,7},{6,4},{7,5},{8,10},{9,11},{10,... | collective-permute-start | bytes 1572872 | tf_op jit(solution)/shard_map/ppermute | solution.py:32
  174.4 22.8 %collective-permute-start.24 = (bf16[256,1024]{1,0:T(8,128)(2,1)S(1)}, bf16[256,1024]{1,0:T(8,128)(2,1)S(1)}, u32[]{:S(2)}, u32[]{:S(2)}) collective-permute-start(bf16[256,1024]{1,0:T(8,128)(2,1)S(1)} %get-tuple-element.97), channel_id=1, source_target_pairs={{0,2},{1,3},{2,0},{3,1},{4,6},{5,7},{6,4},{7,5},{8,10},{9,11},{10,... | collective-permute-start | bytes 1572872 | tf_op jit(solution)/shard_map/ppermute | solution.py:32
  175.8 24.1 %collective-permute-start.27 = (bf16[128,1024]{1,0:T(8,128)(2,1)S(1)}, bf16[128,1024]{1,0:T(8,128)(2,1)S(1)}, u32[]{:S(2)}, u32[]{:S(2)}) collective-permute-start(bf16[128,1024]{1,0:T(8,128)(2,1)S(1)} %get-tuple-element.100), channel_id=1, source_target_pairs={{0,1},{1,0},{2,3},{3,2},{4,5},{5,4},{6,7},{7,6},{8,9},{9,8},{10,11... | collective-permute-start | bytes 786440 | tf_op jit(solution)/shard_map/ppermute | solution.py:32
  178.2 21.8 %collective-permute-start.28 = (bf16[128,1024]{1,0:T(8,128)(2,1)S(1)}, bf16[128,1024]{1,0:T(8,128)(2,1)S(1)}, u32[]{:S(2)}, u32[]{:S(2)}) collective-permute-start(bf16[128,1024]{1,0:T(8,128)(2,1)S(1)} %slice.18), channel_id=1, source_target_pairs={{0,1},{1,0},{2,3},{3,2},{4,5},{5,4},{6,7},{7,6},{8,9},{9,8},{10,11... | collective-permute-start | bytes 786440 | tf_op jit(solution)/shard_map/ppermute | solution.py:32
  185.9 14.6 %collective-permute-start.29 = (bf16[128,1024]{1,0:T(8,128)(2,1)S(1)}, bf16[128,1024]{1,0:T(8,128)(2,1)S(1)}, u32[]{:S(2)}, u32[]{:S(2)}) collective-permute-start(bf16[128,1024]{1,0:T(8,128)(2,1)S(1)} %get-tuple-element.101), channel_id=1, source_target_pairs={{0,1},{1,0},{2,3},{3,2},{4,5},{5,4},{6,7},{7,6},{8,9},{9,8},{10,11... | collective-permute-start | bytes 786440 | tf_op jit(solution)/shard_map/ppermute | solution.py:32
  197.2 3.9 %collective-permute-start.23 = (bf16[128,1024]{1,0:T(8,128)(2,1)S(1)}, bf16[128,1024]{1,0:T(8,128)(2,1)S(1)}, u32[]{:S(2)}, u32[]{:S(2)}) collective-permute-start(bf16[128,1024]{1,0:T(8,128)(2,1)S(1)} %get-tuple-element.96), channel_id=1, source_target_pairs={{0,1},{1,0},{2,3},{3,2},{4,5},{5,4},{6,7},{7,6},{8,9},{9,8},{10,11... | collective-permute-start | bytes 786440 | tf_op jit(solution)/shard_map/ppermute | solution.py:32
  200.0 1.6 collective-permute-start.31
  200.0 1.9 collective-permute-start.25
  201.9 1.6 copy-start.1
  205.5 8.3 %collective-permute-start.32 = (bf16[128,1024]{1,0:T(8,128)(2,1)S(1)}, bf16[128,1024]{1,0:T(8,128)(2,1)S(1)}, u32[]{:S(2)}, u32[]{:S(2)}) collective-permute-start(bf16[128,1024]{1,0:T(8,128)(2,1)S(1)} %get-tuple-element.105), channel_id=1, source_target_pairs={{0,1},{1,0},{2,3},{3,2},{4,5},{5,4},{6,7},{7,6},{8,9},{9,8},{10,11... | collective-permute-start | bytes 786440 | tf_op jit(solution)/shard_map/ppermute | solution.py:32
  205.8 8.0 %collective-permute-start.33 = (bf16[128,1024]{1,0:T(8,128)(2,1)S(1)}, bf16[128,1024]{1,0:T(8,128)(2,1)S(1)}, u32[]{:S(2)}, u32[]{:S(2)}) collective-permute-start(bf16[128,1024]{1,0:T(8,128)(2,1)S(1)} %get-tuple-element.106), channel_id=1, source_target_pairs={{0,2},{1,3},{2,0},{3,1},{4,6},{5,7},{6,4},{7,5},{8,10},{9,11},{10,... | collective-permute-start | bytes 786440 | tf_op jit(solution)/shard_map/ppermute | solution.py:32
  205.8 13.6 %collective-permute-start.34 = (bf16[128,1024]{1,0:T(8,128)(2,1)S(1)}, bf16[128,1024]{1,0:T(8,128)(2,1)S(1)}, u32[]{:S(2)}, u32[]{:S(2)}) collective-permute-start(bf16[128,1024]{1,0:T(8,128)(2,1)S(1)} %get-tuple-element.107), channel_id=1, source_target_pairs={{0,3},{1,2},{2,1},{3,0},{4,7},{5,6},{6,5},{7,4},{8,11},{9,10},{10,... | collective-permute-start | bytes 786440 | tf_op jit(solution)/shard_map/ppermute | solution.py:32
  (1 other events, 0.9 us)

commit v7 on v6

v7 whole, which is shorter than its diff:
```python
import functools

import jax
import jax.numpy as jnp
from jax import lax
from jax.experimental import pallas as pl
from jax.experimental.pallas import tpu as pltpu
from jax.sharding import PartitionSpec as P

G = 4
CHUNKS = 2
ROWS = 2
TILE = 256
F32 = jnp.float32
BF16 = jnp.bfloat16
MIB = 1024 * 1024
LANES = 128
SMEM = pl.BlockSpec(memory_space=pltpu.SMEM)
VMEM = pl.BlockSpec(memory_space=pltpu.VMEM)
ANY = pl.BlockSpec(memory_space=pl.ANY)


def moved(value, steps, only=None):
    count = lax.axis_size("slab")
    first, last = max(0, -steps), min(count, count - steps)
    pairs = [(i, i + steps) for i in range(first, last) if only is None or i % G == only]
    return lax.ppermute(value, "slab", pairs)


def swapped(value, bits):
    count = lax.axis_size("slab")
    return lax.ppermute(value, "slab", [(i, i ^ bits) for i in range(count)])


def direct(arrays):
    return [array if m == 0 else swapped(array, m) for m, array in enumerate(arrays)]


def call(kernel, us, *, results, vmem=16, **how):
    return pl.pallas_call(
        kernel,
        out_shape=results,
        compiler_params=pltpu.CompilerParams(vmem_limit_bytes=vmem * MIB),
        cost_estimate=pl.CostEstimate(flops=int(us * 1.15e9), bytes_accessed=1000, transcendentals=0),
        **how,
    )


def value(shape, dtype):
    return jax.ShapeDtypeStruct(shape, dtype)


def far(array):
    return pltpu.with_memory_space_constraint(array, pltpu.HBM)


def across(shape, tile):
    block = shape[:-1] + (tile,)
    return pl.BlockSpec(block, lambda i: (0,) * (len(shape) - 1) + (i,))


def piece_specs(pieces, side, tile):
    return [pl.BlockSpec((side, tile), lambda i, at=at: (at, i)) for _, at in pieces]


def arrays_of(pieces):
    return [array for array, _ in pieces]


def rows_of(place, m):
    first = ROWS * jnp.bitwise_xor(place, m)
    return [(h * TILE, first + h) for h in range(ROWS)]


def wide_tile(rows_deep):
    return pltpu.VMEM((TILE // LANES, rows_deep, LANES), F32)


def chunk_tiles(chunk, cols):
    count = cols // CHUNKS // TILE
    return chunk * count, count


CAST_GROUPS = ((0, (0,)), (0, (1,)), (0, (2,)), (0, (3,)), (1, (0,)), (1, (1,)), (1, (2, 3)))


def cast_kernel(count, here_ref, *refs):
    parts = TILE // LANES
    vol_refs, (top_ref, end_ref, sino_ref), out_refs = refs[:parts], refs[parts : parts + 3], refs[parts + 3 :]
    block_refs, sent_refs = out_refs[:-CHUNKS], out_refs[-CHUNKS:]
    step = pl.program_id(0)
    rows = ROWS * G
    depth = vol_refs[0].shape[0] // rows
    place = lax.rem(here_ref[0], G)

    for c in range(CHUNKS):

        @pl.when(step // count == c)
        def _():
            sent_refs[c][...] = sino_ref[...]
            for j, vol_ref in enumerate(vol_refs):
                for (chunk, group), out_ref in zip(CAST_GROUPS, block_refs):
                    if chunk != c:
                        continue
                    for n, m in enumerate(group):
                        for start, row in rows_of(place, m):
                            at = pl.ds(start + j * LANES, LANES)
                            block = vol_ref[pl.ds(row, depth, stride=rows), :].astype(BF16)
                            out_ref[n * depth : (n + 1) * depth, at] = block
            if c == 0:
                both = jnp.concatenate([top_ref[...], end_ref[...]], axis=0).astype(BF16)
                for (chunk, group), out_ref in zip(CAST_GROUPS, block_refs):
                    if chunk == 0 and group[0] % 2:
                        out_ref[depth:, :] = both


def cast_rows(here, volume, sinogram):
    depth, rows, cols = volume.shape
    flat = far(volume.reshape(depth * rows, cols))
    _, count = chunk_tiles(0, cols)
    parts, width = TILE // LANES, ROWS * TILE

    def step_of(chunk):
        return lambda i: jnp.clip(i - chunk * count, 0, count - 1)

    shapes = [(len(g) * depth + (2 * rows if c == 0 and g[0] % 2 else 0), cols) for c, g in CAST_GROUPS]
    out_specs = [
        pl.BlockSpec((shape[0], width), lambda i, at=step_of(c): (0, at(i))) for (c, _), shape in zip(CAST_GROUPS, shapes)
    ]
    out_specs += [pl.BlockSpec((depth, rows, TILE), lambda i, at=step_of(c): (0, 0, at(i))) for c in range(CHUNKS)]
    results = [value(shape, BF16) for shape in shapes] + [value((depth, rows, cols // CHUNKS), BF16)] * CHUNKS
    in_specs = [SMEM]
    in_specs += [pl.BlockSpec((depth * rows, LANES), lambda i, j=j: (0, i * parts + j)) for j in range(parts)]
    in_specs += [pl.BlockSpec((rows, width), lambda i, z=z, at=step_of(0): (z, at(i))) for z in (0, depth - 1)]
    in_specs += [pl.BlockSpec((depth, rows, TILE), lambda i: (0, 0, i))]
    return call(
        functools.partial(cast_kernel, count),
        4,
        grid=(CHUNKS * count,),
        in_specs=in_specs,
        out_specs=out_specs,
        results=results,
    )(here, *[flat] * parts, flat, flat, far(sinogram))


def last_block(here_ref, blocks):
    spot = jnp.bitwise_xor(lax.rem(here_ref[0], G), G - 1)
    last = blocks[0]
    for m in range(1, G):
        last = jnp.where(spot == m, blocks[m], last)
    return last


def pack_kernel(here_ref, *refs):
    in_refs, (all_ref, last_ref) = refs[:G], refs[-2:]
    side = in_refs[0].shape[0]
    for m in range(G):
        all_ref[m * side : (m + 1) * side] = in_refs[m][:side]
    last_ref[:side] = last_block(here_ref, [ref[:side] for ref in in_refs])
    all_ref[G * side :] = in_refs[G - 1][side:]
    last_ref[side:] = in_refs[G - 1][side:]


def pack(here, blocks, *tokens):
    side, cols = blocks[0].shape
    more = blocks[G - 1].shape[0] - side
    tile = 512
    shapes = [(G * side + more, cols), (side + more, cols)]
    return call(
        pack_kernel,
        1,
        grid=(cols // tile,),
        in_specs=[SMEM] + [across(block.shape, tile) for block in blocks] + [ANY] * len(tokens),
        out_specs=[across(shape, tile) for shape in shapes],
        results=[value(shape, BF16) for shape in shapes],
    )(here, *blocks, *tokens)


def split_kernel(with_resid, here_ref, own_ref, got_ref, *refs):
    out_refs, wide = refs[-G - 1 : -1], refs[-1]
    depth, rows, cols = own_ref.shape
    place = lax.rem(here_ref[0], G)

    def fill(ref):
        for j in range(cols // LANES):
            wide[j] = ref[:, :, j * LANES : (j + 1) * LANES].astype(F32).reshape(wide.shape[1:])

    @pl.when(place == G - 1)
    def _():
        fill(got_ref)

    @pl.when(place != G - 1)
    def _():
        fill(own_ref)

    for m, out_ref in enumerate(out_refs):
        for j in range(cols // LANES):
            for start, row in rows_of(place, m):
                at = pl.ds(start + j * LANES, LANES)
                out_ref[:depth, at] = wide.at[j][pl.ds(row, depth, stride=rows), :].astype(BF16)
        if with_resid:
            out_ref[depth:] = refs[0][m * depth : (m + 1) * depth]


def split_rows(here, own, got, chunk, resid, *tokens):
    depth, rows, cols = own.shape
    first, count = chunk_tiles(chunk, cols)
    block = (depth, rows, TILE)
    width = ROWS * TILE
    extra = [] if resid is None else [resid]
    shape = ((1 + len(extra)) * depth, cols)
    return call(
        functools.partial(split_kernel, resid is not None),
        2,
        grid=(count,),
        in_specs=[SMEM, pl.BlockSpec(block, lambda i: (0, 0, first + i)), pl.BlockSpec(block, lambda i: (0, 0, i))]
        + [pl.BlockSpec((G * depth, width), lambda i: (0, i))] * len(extra)
        + [ANY] * len(tokens),
        out_specs=[across(shape, width)] * G,
        results=[value(shape, BF16)] * G,
        scratch_shapes=[wide_tile(depth * rows)],
    )(here, far(own), got, *extra, *tokens)


def patch_kernel(slabs, here_ref, cover_ref, offset_ref, *refs):
    w_ref, *refs = refs
    end_refs, (vol_ref, sino_ref), (r_ref, tv_ref) = refs[:4], refs[4:6], refs[-10:-8]
    vol, s, r, wide, tv, slices, fixed, sem = refs[-8:]
    depth, rows, cols = sino_ref.shape
    place = lax.rem(here_ref[0], G)
    near, next_level, far_end, last_level = (ref[...] for ref in end_refs)
    low = jnp.where(place == 0, last_level, jnp.where(place == 2, far_end, near))[rows:].astype(F32)
    high = jnp.where(place == G - 1, next_level, jnp.where(place == 1, far_end, near))[:rows].astype(F32)

    for n, z in enumerate((0, depth - 2)):
        pltpu.make_async_copy(vol_ref.at[z : z + 2], slices.at[2 * n : 2 * n + 2], sem.at[n]).start()
    for n, z in enumerate((0, depth - 2)):
        pltpu.make_async_copy(vol_ref.at[z : z + 2], slices.at[2 * n : 2 * n + 2], sem.at[n]).wait()
    fixed[0] = tv_slice(slices[0], slices[1], tv_below(low, slices[0]))[0]
    fixed[1] = tv_slice(slices[3], high, tv_below(slices[2], slices[3]))[0]
    for n, z in enumerate((0, depth - 1)):
        pltpu.make_async_copy(fixed.at[n], tv_ref.at[z], sem.at[n]).start()
    for n, z in enumerate((0, depth - 1)):
        pltpu.make_async_copy(fixed.at[n], tv_ref.at[z], sem.at[n]).wait()

    @pl.when(here_ref[0] == slabs - 1)
    def _():
        pltpu.make_async_copy(vol_ref, vol, sem.at[2]).start()
        pltpu.make_async_copy(sino_ref, s, sem.at[3]).start()
        pltpu.make_async_copy(tv_ref, tv, sem.at[4]).start()
        pltpu.make_async_copy(vol_ref, vol, sem.at[2]).wait()
        pltpu.make_async_copy(sino_ref, s, sem.at[3]).wait()
        pltpu.make_async_copy(tv_ref, tv, sem.at[4]).wait()
        block = w_ref[offset_ref[slabs - 1, 0]]
        block = jnp.where(cover_ref[slabs - 1, 0] == 1, block, jnp.zeros_like(block))
        turned = block.astype(F32).T.astype(BF16)

        def column(j, _):
            at = pl.ds(pl.multiple_of(j * LANES, LANES), LANES)
            for n, ref in enumerate((s, tv, vol)):
                wide[n] = ref[:, :, at].astype(F32).reshape(wide.shape[1:])
            for row in range(rows):
                spot = pl.ds(row, depth, stride=rows)
                seen = jnp.dot(block, wide.at[2][spot, :].astype(BF16), preferred_element_type=F32)
                resid = (seen - wide.at[0][spot, :]).astype(BF16)
                wide.at[0][spot, :] = resid.astype(F32)
                wide.at[1][spot, :] += jnp.dot(turned, resid, preferred_element_type=F32)
            r[:, :, at] = wide[0].reshape(depth, rows, LANES).astype(BF16)
            tv[:, :, at] = wide[1].reshape(depth, rows, LANES)
            return 0

        lax.fori_loop(0, cols // LANES, column, 0)
        pltpu.make_async_copy(r, r_ref, sem.at[3]).start()
        pltpu.make_async_copy(tv, tv_ref, sem.at[4]).start()
        pltpu.make_async_copy(r, r_ref, sem.at[3]).wait()
        pltpu.make_async_copy(tv, tv_ref, sem.at[4]).wait()


def patch(here, coverage, offsets, weights, ends, volume, sinogram, tv, *tokens):
    slabs = coverage.shape[0]
    depth, rows, cols = sinogram.shape
    edges = [pl.BlockSpec((2 * rows, cols), lambda i, last=end.shape[0] // (2 * rows) - 1: (last, 0)) for end in ends]
    return call(
        functools.partial(patch_kernel, slabs),
        3,
        vmem=32,
        grid=(1,),
        in_specs=[SMEM, SMEM, SMEM, pl.BlockSpec(weights.shape, lambda i: (0, 0, 0))]
        + edges
        + [ANY] * (3 + len(tokens)),
        out_specs=[ANY, ANY],
        results=[pltpu.HBM(sinogram.shape, BF16), pltpu.HBM(volume.shape, F32)],
        input_output_aliases={10: 1},
        scratch_shapes=[
            pltpu.VMEM(volume.shape, F32),
            pltpu.VMEM(sinogram.shape, BF16),
            pltpu.VMEM(sinogram.shape, BF16),
            pltpu.VMEM((3, depth * rows, LANES), F32),
            pltpu.VMEM(volume.shape, F32),
            pltpu.VMEM((4, rows, cols), F32),
            pltpu.VMEM((2, rows, cols), F32),
            pltpu.SemaphoreType.DMA((5,)),
        ],
    )(here, coverage, offsets, weights, *ends, far(volume), far(sinogram), far(tv), *tokens)


def natural(place, in_refs, wide, j):
    depth = in_refs[0].shape[0]
    rows = ROWS * len(in_refs)
    for m, ref in enumerate(in_refs):
        for start, row in rows_of(place, m):
            value = ref[:, start + j * LANES : start + (j + 1) * LANES].astype(F32)
            wide.at[j][pl.ds(row, depth, stride=rows), :] = value
    return wide[j].reshape(depth, rows, LANES)


def join_kernel(here_ref, *refs):
    in_refs, (out_ref, wide) = refs[:G], refs[-2:]
    for j in range(out_ref.shape[2] // LANES):
        out_ref[:, :, j * LANES : (j + 1) * LANES] = natural(lax.rem(here_ref[0], G), in_refs, wide, j).astype(BF16)


def join_rows(here, pieces, shape, *tokens):
    depth, rows, cols = shape
    _, count = chunk_tiles(0, cols)
    return call(
        join_kernel,
        1.5,
        grid=(count,),
        in_specs=[SMEM] + piece_specs(pieces, depth, ROWS * TILE) + [ANY] * len(tokens),
        out_specs=pl.BlockSpec((depth, rows, TILE), lambda i: (0, 0, i)),
        results=value((depth, rows, cols // CHUNKS), BF16),
        scratch_shapes=[wide_tile(depth * rows)],
    )(here, *arrays_of(pieces), *tokens)


def settle_kernel(slabs, count, here_ref, own_ref, above_ref, *refs):
    in_refs, (base_ref, out_ref, wide) = refs[:G], refs[-3:]
    step = pl.program_id(0)
    cols = out_ref.shape[2]
    place = lax.rem(here_ref[0], G)
    last = here_ref[0] == slabs - 1

    @pl.when(last)
    def _():
        pltpu.sync_copy(base_ref.at[:, :, pl.ds(pl.multiple_of(step * cols, cols), cols)], out_ref)

    @pl.when(jnp.logical_not(last) & (step < count) & (place == G - 1))
    def _():
        out_ref[...] = above_ref[...]

    @pl.when(jnp.logical_not(last) & (step < count) & (place != G - 1))
    def _():
        out_ref[...] = own_ref[...]

    @pl.when(jnp.logical_not(last) & (step >= count))
    def _():
        for j in range(cols // LANES):
            out_ref[:, :, j * LANES : (j + 1) * LANES] = natural(place, in_refs, wide, j).astype(BF16)


def settle(here, slabs, own, above, pieces, base, *tokens):
    depth, rows, cols = base.shape
    _, count = chunk_tiles(0, cols)
    block = (depth, rows, TILE)
    early = pl.BlockSpec(block, lambda i: (0, 0, jnp.minimum(i, count - 1)))
    late = [
        pl.BlockSpec((depth, ROWS * TILE), lambda i, at=at: (at, jnp.maximum(i - count, 0))) for _, at in pieces
    ]
    return call(
        functools.partial(settle_kernel, slabs, count),
        2.6,
        grid=(CHUNKS * count,),
        in_specs=[SMEM, early, early] + late + [ANY] * (len(tokens) + 1),
        out_specs=pl.BlockSpec(block, lambda i: (0, 0, i)),
        results=value(base.shape, BF16),
        scratch_shapes=[wide_tile(depth * rows)],
    )(here, own, above, *arrays_of(pieces), *tokens, far(base))


def finish_kernel(here_ref, tv_ref, *refs):
    in_refs, (out_ref, wide) = refs[:G], refs[-2:]
    for j in range(out_ref.shape[2] // LANES):
        at = pl.ds(j * LANES, LANES)
        out_ref[:, :, at] = tv_ref[:, :, at] + natural(lax.rem(here_ref[0], G), in_refs, wide, j)


def finish(here, chunk, tv, pieces, *tokens):
    depth, rows, cols = tv.shape
    first, count = chunk_tiles(chunk, cols)
    part = pl.BlockSpec((depth, rows, TILE), lambda i: (0, 0, first + i))
    return call(
        finish_kernel,
        2.6,
        grid=(count,),
        in_specs=[SMEM, part] + piece_specs(pieces, depth, ROWS * TILE) + [ANY] * len(tokens),
        out_specs=part,
        results=pltpu.HBM(tv.shape, F32),
        input_output_aliases={1: 0},
        scratch_shapes=[wide_tile(depth * rows)],
    )(here, far(tv), *arrays_of(pieces), *tokens)


def band_kernel(slabs, span, here_ref, cover_ref, offset_ref, w_ref, *refs):
    proj_ref, back_ref, turned = refs[-3:]
    side = w_ref.shape[1]
    place = lax.rem(here_ref[0], G)
    first = here_ref[0] - place
    zero = jnp.zeros((side, side), BF16)
    for i in range(w_ref.shape[0]):
        turned[i] = w_ref[i].astype(F32).T.astype(BF16)

    def block(ref, i, j):
        k = j - i
        known, step = jnp.clip(i, 0, slabs - 1), jnp.clip(k, 0, span - 1)
        inside = (i >= 0) & (i < slabs) & (j >= 0) & (j < slabs) & (k >= 0) & (k < span)
        live = inside & (cover_ref[known, step] == 1)
        return jnp.where(live, ref[offset_ref[known, step]], zero)

    def slab(m):
        return first + jnp.bitwise_xor(place, m)

    def group(m):
        to = jnp.bitwise_xor(place, m)
        return first + jnp.where(to == G - 1, -1, to)

    seen = [slab(m) for m in range(G)] + [slab(m) + G for m in range(G)] + [first - 1]
    seeing = [group(m) for m in range(G)] + [group(m) - G for m in range(G)] + [first + G - 1]
    for r in range(G):
        for s in range(2 * G + 1):
            at = (pl.ds(r * side, side), pl.ds(s * side, side))
            proj_ref[at] = block(w_ref, group(r), seen[s])
            back_ref[at] = block(turned, seeing[s], slab(r))


def bands(here, coverage, offsets, weights, *tokens):
    slabs, span = coverage.shape
    side = weights.shape[1]
    shape = (G * side, (2 * G + 1) * side)
    return call(
        functools.partial(band_kernel, slabs, span),
        1.6,
        in_specs=[SMEM, SMEM, SMEM, pl.BlockSpec(weights.shape, lambda i: (0, 0, 0))] + [ANY] * len(tokens),
        grid=(1,),
        out_specs=[pl.BlockSpec(shape, lambda i: (0, 0))] * 2,
        results=[pltpu.HBM(shape, BF16)] * 2,
        scratch_shapes=[pltpu.VMEM(weights.shape, BF16)],
    )(here, coverage, offsets, weights, *tokens)


def residual_blocks(band, seen, sino_refs):
    side = sino_refs[0].shape[0]
    total = jnp.dot(band, jnp.concatenate(seen, axis=0), preferred_element_type=F32)
    return [(total[m * side : (m + 1) * side] - ref[...].astype(F32)).astype(BF16) for m, ref in enumerate(sino_refs)]


def first_kernel(here_ref, band_ref, own_ref, high_ref, low_ref, *refs):
    sino_refs, next_refs, (up_ref, down_ref) = refs[:G], refs[G : 2 * G], refs[-2:]
    side = sino_refs[0].shape[0]
    resid = residual_blocks(band_ref[...], [own_ref[...], high_ref[...], low_ref[...]], sino_refs)
    following = [ref[...] for ref in next_refs]
    for m in range(G):
        at = slice(m * side, (m + 1) * side)
        up_ref[at, :] = resid[m]
        down_ref[at, :] = following[m]
    up_ref[G * side :] = last_block(here_ref, following)
    down_ref[G * side :] = last_block(here_ref, resid)


def project_first(here, band, own, high, low, sinos, following, *tokens):
    n, side = band.shape[0], band.shape[0] // G
    cols = own.shape[1]
    tile = 512
    many, one = pl.BlockSpec((n, tile), lambda i: (0, i)), pl.BlockSpec((side, tile), lambda i: (0, i))
    out = (n + side, cols)
    return call(
        first_kernel,
        4,
        grid=(cols // tile,),
        in_specs=[SMEM, pl.BlockSpec(band.shape, lambda i: (0, 0)), many, many, one]
        + piece_specs(sinos + following, side, tile)
        + [ANY] * len(tokens),
        out_specs=[across(out, tile)] * 2,
        results=[value(out, BF16)] * 2,
    )(here, band, own, high, low, *arrays_of(sinos + following), *tokens)


def second_kernel(here_ref, band_ref, own_ref, high_ref, low_ref, *refs):
    sino_refs, (up_ref, down_ref) = refs[:G], refs[-2:]
    side = sino_refs[0].shape[0]
    resid = residual_blocks(band_ref[...], [own_ref[...], high_ref[...], low_ref[...]], sino_refs)
    for m in range(G):
        up_ref[m * side : (m + 1) * side] = resid[m]
    down_ref[...] = last_block(here_ref, resid)


def project_second(here, band, own, high, low, sinos, *tokens):
    n, side = band.shape[0], band.shape[0] // G
    cols = own.shape[1]
    tile = 512
    many = pl.BlockSpec((n, tile), lambda i: (0, i))
    return call(
        second_kernel,
        3,
        grid=(cols // tile,),
        in_specs=[SMEM, pl.BlockSpec(band.shape, lambda i: (0, 0)), many, many]
        + piece_specs([(low, G)] + sinos, side, tile)
        + [ANY] * len(tokens),
        out_specs=[across((n, cols), tile), across((side, cols), tile)],
        results=[value((n, cols), BF16), value((side, cols), BF16)],
    )(here, band, own, high, low, *arrays_of(sinos), *tokens)


def back_kernel(dealing, here_ref, band_ref, own_ref, low_ref, high_ref, *refs):
    out_refs = refs[-G:]
    side = high_ref.shape[0]
    seeing = jnp.concatenate([own_ref[...], low_ref[...], high_ref[...]], axis=0)
    total = jnp.dot(band_ref[...], seeing, preferred_element_type=F32)
    place = lax.rem(here_ref[0], G)
    for m, out_ref in enumerate(out_refs):
        out_ref[:side] = total[m * side : (m + 1) * side].astype(BF16)
        if dealing:
            last = jnp.bitwise_xor(place, m) == G - 1
            out_ref[side:] = jnp.where(last, refs[1][...], refs[0][m * side : (m + 1) * side])


def back(here, band, own, low, high, dealt, *tokens):
    n, side = band.shape[0], band.shape[0] // G
    cols = own.shape[1]
    tile = 512
    many = pl.BlockSpec((n, tile), lambda i: (0, i))
    one = pl.BlockSpec((side, tile), lambda i: (0, i))
    out = ((2 if dealt else 1) * side, cols)
    return call(
        functools.partial(back_kernel, bool(dealt)),
        3,
        grid=(cols // tile,),
        in_specs=[SMEM, pl.BlockSpec(band.shape, lambda i: (0, 0)), many, many]
        + piece_specs([high], side, tile)
        + ([many, one] if dealt else [])
        + [ANY] * len(tokens),
        out_specs=[across(out, tile)] * G,
        results=[value(out, BF16)] * G,
    )(here, band, own, low, high[0], *dealt, *tokens)


def tv_flux(cur, above):
    rows, cols = cur.shape
    row = lax.broadcasted_iota(jnp.int32, (rows, cols), 0)
    col = lax.broadcasted_iota(jnp.int32, (rows, cols), 1)
    dz = above - cur
    dy = jnp.where(row == rows - 1, 0.0, pltpu.roll(cur, rows - 1, 0)) - cur
    dx = jnp.where(col == cols - 1, 0.0, pltpu.roll(cur, cols - 1, 1)) - cur
    scale = 0.5 * lax.rsqrt(dz * dz + dy * dy + dx * dx + 0.25)
    return dz * scale, dy * scale, dx * scale


def tv_below(cur, above):
    return tv_flux(cur, above)[0]


def tv_slice(cur, above, below_flux):
    rows, cols = cur.shape
    row = lax.broadcasted_iota(jnp.int32, (rows, cols), 0)
    col = lax.broadcasted_iota(jnp.int32, (rows, cols), 1)
    fz, fy, fx = tv_flux(cur, above)
    sides = 0.5 * cur * lax.rsqrt(cur * cur + 0.25)
    fy_low = jnp.where(row == 0, sides, pltpu.roll(fy, 1, 0))
    fx_low = jnp.where(col == 0, sides, pltpu.roll(fx, 1, 1))
    return (below_flux - fz) + (fy_low - fy) + (fx_low - fx), fz


def tv_kernel(last_ref, next_ref, vol_ref, *refs):
    out_ref, done_ref, flux_ref = refs[-3:]
    deep = vol_ref.shape[0]

    @pl.when(pl.program_id(0) == 0)
    def _():
        flux_ref[...] = tv_below(last_ref[0], vol_ref[0])

    def body(z, flux):
        out_ref[z], flux = tv_slice(vol_ref[z], vol_ref[z + 1], flux)
        return flux

    flux = lax.fori_loop(0, deep - 1, body, flux_ref[...], unroll=5)
    out_ref[deep - 1], flux_ref[...] = tv_slice(vol_ref[deep - 1], next_ref[0], flux)
    done_ref[...] = flux_ref[:, : done_ref.shape[1]]


def half_tv(volume, half, base, *tokens):
    depth, rows, cols = volume.shape
    deep = 16
    steps = depth // deep // 2
    first = half * steps
    body = pl.BlockSpec((deep, rows, cols), lambda i: (first + i, 0, 0))
    before = pl.BlockSpec((1, rows, cols), lambda i: (max(first * deep - 1, 0), 0, 0))
    after = pl.BlockSpec((1, rows, cols), lambda i: (jnp.minimum((first + i + 1) * deep, depth - 1), 0, 0))
    bases = [] if base is None else [far(base)]
    return call(
        tv_kernel,
        5,
        grid=(steps,),
        in_specs=[before, after, body] + [ANY] * (len(bases) + len(tokens)),
        out_specs=[body, pl.BlockSpec((rows, LANES), lambda i: (0, 0))],
        results=[pltpu.HBM(volume.shape, F32), value((rows, LANES), F32)],
        input_output_aliases={3: 0} if bases else {},
        scratch_shapes=[pltpu.VMEM((rows, cols), F32)],
    )(*[far(volume)] * 3, *bases, *tokens)


def local(volume, sinogram, weights, coverage, offsets):
    slabs = lax.axis_size("slab")
    here = lax.axis_index("slab").astype(jnp.int32).reshape(1)
    depth = volume.shape[0]

    *blocks, sent0, sent1 = cast_rows(here, volume, sinogram)
    vols0, (v0, v1, v23) = blocks[:G], blocks[G:]
    got0 = moved(sent0, G, only=G - 1)
    got_vols0 = direct(vols0)
    near, over = swapped(v1, 1), swapped(v23, 2)
    tv, tv_done = half_tv(volume, 0, None, vols0[0])
    own0, edge0 = pack(here, got_vols0, tv_done, near)
    high0 = moved(own0, -G)
    sino0 = split_rows(here, sinogram, got0, 0, None, own0)
    sinos0 = [(array, 0) for array in direct(sino0)]
    edge0, sent1, over = lax.optimization_barrier((edge0, sent1, over, sinos0[1][0]))[:3]
    low0 = moved(edge0, G)
    got1 = moved(sent1, G, only=G - 1)
    vols1 = [(v0, 0), (near, 0), (over, 0), (swapped(over[depth:], 1), 0)]
    band_p, band_b = bands(here, coverage, offsets, weights, own0)

    up0, down0 = project_first(here, band_p, own0, high0, low0, sinos0, vols1)
    from_high, from_low = moved(down0, -G), moved(up0, G)
    mixed = split_rows(here, sinogram, got1, 1, up0)
    got_mixed = direct(mixed)
    tv, tv_done = half_tv(volume, 1, tv, mixed[0])
    ends = [got_vols0[1], high0, got_vols0[3], low0]
    r_last, tv = patch(here, coverage, offsets, weights, ends, volume, sinogram, tv, tv_done)
    sinos1 = [(array, 0) for array in got_mixed]
    up1, down1 = project_second(here, band_p, down0, from_high, from_low, sinos1, r_last)
    from_low1, from_high1 = moved(up1, G), moved(down1, -G)

    backs0 = back(here, band_b, up0, from_low, (from_high, G), [up1, from_high1])
    got_backs0 = direct(backs0)
    resid0 = join_rows(here, [(array, 1) for array in got_mixed], sinogram.shape, backs0[0])
    resid0_above = moved(resid0, -G, only=G - 1)
    backs1 = back(here, band_b, up1, from_low1, (from_high1, 0), [], resid0)
    got_backs1 = direct(backs1)
    residual = settle(here, slabs, resid0, resid0_above, [(array, 1) for array in got_backs0], r_last, backs1[0])
    gradient = finish(here, 0, tv, [(array, 0) for array in got_backs0], backs1[0])
    gradient = finish(here, 1, gradient, [(array, 0) for array in got_backs1])
    return (gradient, residual)


def solution(mesh):
    placed = (P("slab", "grp", None), P("slab", "grp", None), P(), P(), P())
    return jax.shard_map(
        local,
        mesh=mesh,
        in_specs=placed,
        out_specs=(P("slab", "grp", None), P("slab", "grp", None)),
        check_vma=False,
    )
```

time: 223 us -> 154 us (0.69)
  Pallas kernels: 111 us -> 45.9 us
  starting transfers between devices: 53.9 us -> 43.5 us
  waiting for transfers between devices: 50 us -> 55.8 us
    pallas_call x16 -> x12, Pallas kernels: 94.7 us -> 29.1 us  [the longest x2 5.85 us: finish(): call(finish_kernel, 2.6, grid=(count,), in_specs=[SMEM, part] + piece_spe...]
    ppermute x24 -> x18, waiting for transfers between devices: 31.9 us -> 40.3 us  [swapped(): return lax.ppermute(value, 'slab', [(i, i ^ bits) for i in range(count)])]
    ppermute x24 -> x18, starting transfers between devices: 30.8 us -> 24.1 us  [swapped(): return lax.ppermute(value, 'slab', [(i, i ^ bits) for i in range(count)])]
    ppermute x11 -> x9, starting transfers between devices: 23.1 us -> 19.4 us  [moved(): return lax.ppermute(value, 'slab', pairs)]
    ppermute x11 -> x9, waiting for transfers between devices: 18 us -> 15.5 us  [moved(): return lax.ppermute(value, 'slab', pairs)]
    unnamed x30 -> x34, local copies, waits for them, and re-layouts: 5.32 us -> 5.89 us
  transfers between devices with their start and end apart: 35 -> 27, of which waited for: 11 -> 9; matrix products, arithmetic and copies ran while one was open for 1% -> 1% of each run, Pallas kernels for 17% -> 23%
where the time goes in v7:
time: 154 us; the launch traced here: 153 us
  waiting for transfers between devices  55.8 us (36%)
  Pallas kernels  45.9 us (30%)
  starting transfers between devices  43.5 us (28%)
  local copies, waits for them, and re-layouts  6.62 us (4%)
    ppermute x18, waiting for transfers between devices, swapped(): return lax.ppermute(value, 'slab', [(i, i ^ bits) for i in range(count)])  40.3 us
    ppermute x18, starting transfers between devices, swapped(): return lax.ppermute(value, 'slab', [(i, i ^ bits) for i in range(count)])  24.1 us
    ppermute x9, starting transfers between devices, moved(): return lax.ppermute(value, 'slab', pairs)  19.4 us
    ppermute x9, waiting for transfers between devices, moved(): return lax.ppermute(value, 'slab', pairs)  15.5 us
    pallas_call x2, Pallas kernels, half_tv(): call(tv_kernel, 5, grid=(steps,), in_specs=[before, after, body] + [ANY]...  11.5 us
    unnamed x34, local copies, waits for them, and re-layouts  5.89 us
    pallas_call x2, Pallas kernels, finish(): call(finish_kernel, 2.6, grid=(count,), in_specs=[SMEM, part] + piece_spe...  5.85 us
    pallas_call x1, Pallas kernels, cast_rows(): call(functools.partial(cast_kernel, count), 4, grid=(CHUNKS * count,), in...  5.05 us
  transfers between devices with their start and end apart: 27, of which 9 were waited for; matrix products, arithmetic and copies ran while one was open for 1% of the time, Pallas kernels for 23%

profile of v7, /device:TPU:1, one launch (start us, length us, event | category | flops | bytes accessed | tf_op | source)
XLA Modules:
  0.0 152.7 jit_solution(10974972520767900299)
XLA Ops:
  0.6 5.1 %shard_map.68 = (bf16[128,1024]{1,0:T(8,128)(2,1)S(1)}, bf16[144,1024]{1,0:T(8,128)(2,1)S(1)}, bf16[128,1024]{1,0:T(8,128)(2,1)S(1)}, bf16[144,1024]{1,0:T(8,128...) custom-call(s32[1]{0:T(128)} %bitcast.here_ref, ...), custom_call_target="tpu_custom_call" | custom-call | flops 4600000000 | bytes 1000 | tf_op jit(solution)/shard_map/pallas_call | solution.py:136
  6.4 4.7 %collective-permute-start.1 = (bf16[128,1024]{1,0:T(8,128)(2,1)S(1)}, bf16[128,1024]{1,0:T(8,128)(2,1)S(1)}, u32[]{:S(2)}, u32[]{:S(2)}) collective-permute-start(bf16[128,1024]{1,0:T(8,128)(2,1)S(1)} %get-tuple-element.46), channel_id=1, source_target_pairs={{0,2},{1,3},{2,0},{3,1},{4,6},{5,7},{6,4},{7,5},{8,10},{9,11},{10,... | collective-permute-start | bytes 786440 | tf_op jit(solution)/shard_map/ppermute | solution.py:32
  11.6 5.8 %shard_map.69 = (f32[128,8,1024]{2,1,0:T(8,128)}, f32[8,128]{1,0:T(8,128)S(1)}) custom-call(f32[128,8,1024]{2,1,0:T(8,128)} %refs_5_.1, f32[128,8,1024]{2,1,0:T(8,128)} %refs_5_.1, f32[128,8,1024]{2,1,0:T(8,128)} %refs_5_.1, bf16[128,1024]{1,0:T(8,128)(2,1)S(1)} %get-tuple-element.45.refs_0_), custom_call_target="tpu_custom_call" | custom-call | flops 5750000128 | bytes 1000 | tf_op jit(solution)/shard_map/pallas_call | solution.py:599
  17.4 4.7 %collective-permute-done.2.refs_3_ = bf16[144,1024]{1,0:T(8,128)(2,1)S(1)} collective-permute-done((bf16[144,1024]{1,0:T(8,128)(2,1)S(1)}, bf16[144,1024]{1,0:T(8,128)(2,1)S(1)}, u32[]{:S(2)}, u32[]{:S(2)}) %collective-permute-start.2) | collective-permute-done | bytes 294944 | tf_op jit(solution)/shard_map/ppermute | solution.py:32
  22.1 1.0 shard_map.70
  23.1 1.3 collective-permute-start.4
  24.4 0.8 collective-permute-start.5
  25.2 2.4 %shard_map.71 = (bf16[128,1024]{1,0:T(8,128)(2,1)S(1)}, bf16[128,1024]{1,0:T(8,128)(2,1)S(1)}, bf16[128,1024]{1,0:T(8,128)(2,1)S(1)}, bf16[128,1024]{1,0:T(8,128)(2,1)}) custom-call(s32[1]{0:T(128)} %bitcast.here_ref, bf16[128,8,1024]{2,1,0:T(8,128)(2,1)} %refs_6_.1, bf16[128,8,512]{2,1,0:T(8,128)(2,1)S(1)} %collective-permute-done.6.got_ref, ...), custom_call_target="tpu_custom_call" | custom-call | flops 2300000000 | bytes 1000 | tf_op jit(solution)/shard_map/pallas_call | solution.py:212
  28.3 2.1 %collective-permute-start.7 = (bf16[128,1024]{1,0:T(8,128)(2,1)S(1)}, bf16[128,1024]{1,0:T(8,128)(2,1)S(1)}, u32[]{:S(2)}, u32[]{:S(2)}) collective-permute-start(bf16[128,1024]{1,0:T(8,128)(2,1)S(1)} %get-tuple-element.55), channel_id=1, source_target_pairs={{0,1},{1,0},{2,3},{3,2},{4,5},{5,4},{6,7},{7,6},{8,9},{9,8},{10,11... | collective-permute-start | bytes 786440 | tf_op jit(solution)/shard_map/ppermute | solution.py:32
  30.4 6.6 %collective-permute-done.5.refs_6_ = bf16[256,1024]{1,0:T(8,128)(2,1)S(1)} collective-permute-done((bf16[256,1024]{1,0:T(8,128)(2,1)S(1)}, bf16[256,1024]{1,0:T(8,128)(2,1)S(1)}, u32[]{:S(2)}, u32[]{:S(2)}) %collective-permute-start.5) | collective-permute-done | bytes 524320 | tf_op jit(solution)/shard_map/ppermute | solution.py:32
  37.1 0.7 copy-done.5
  37.8 1.6 %collective-permute-start.9 = (bf16[128,8,512]{2,1,0:T(8,128)(2,1)}, bf16[128,8,512]{2,1,0:T(8,128)(2,1)}, u32[]{:S(2)}, u32[]{:S(2)}) collective-permute-start(bf16[128,8,512]{2,1,0:T(8,128)(2,1)} %get-tuple-element.58), channel_id=1, source_target_pairs={{3,7},{7,11},{11,15},{19,23},{23,27},{27,31}} | collective-permute-start | bytes 3145736 | tf_op jit(solution)/shard_map/ppermute | solution.py:27
  39.4 4.3 %collective-permute-start.8 = (bf16[144,1024]{1,0:T(8,128)(2,1)}, bf16[144,1024]{1,0:T(8,128)(2,1)}, u32[]{:S(2)}, u32[]{:S(2)}) collective-permute-start(bf16[144,1024]{1,0:T(8,128)(2,1)} %get-tuple-element.56), channel_id=1, source_target_pairs={{0,4},{1,5},{2,6},{3,7},{4,8},{5,9},{6,10},{7,11},{8,12},{9,13},{1... | collective-permute-start | bytes 884744 | tf_op jit(solution)/shard_map/ppermute | solution.py:27
  43.8 5.7 %collective-permute-start.11 = (bf16[128,1024]{1,0:T(8,128)(2,1)}, bf16[128,1024]{1,0:T(8,128)(2,1)}, u32[]{:S(2)}, u32[]{:S(2)}) collective-permute-start(bf16[128,1024]{1,0:T(8,128)(2,1)} %get-tuple-element.62), channel_id=1, source_target_pairs={{0,3},{1,2},{2,1},{3,0},{4,7},{5,6},{6,5},{7,4},{8,11},{9,10},{10,... | collective-permute-start | bytes 786440 | tf_op jit(solution)/shard_map/ppermute | solution.py:32
  49.5 0.7 slice.3
  51.0 0.8 copy.14.offset_ref
  51.8 2.7 %shard_map.72 = (bf16[512,1152]{1,0:T(8,128)(2,1)}, bf16[512,1152]{1,0:T(8,128)(2,1)}) custom-call(s32[1]{0:T(128)} %bitcast.here_ref, s32[16,6]{1,0:T(8,128)S(1)} %copy.13.cover_ref, s32[16,6]{1,0:T(8,128)S(1)} %copy.14.offset_ref, bf16[8,128,128]{2,1,0:T(8,128)(2,1)S(1)} %copy-done, bf16[528,1024]{1,0:T(8,128)(2,1)S(1)} %get-tuple-element.50.refs_0_.own_ref), custom_call_target="tpu_custom_call" | custom-call | flops 1840000000 | bytes 1000 | tf_op jit(solution)/shard_map/pallas_call | solution.py:440
  54.5 1.7 %collective-permute-done.11.refs_3_ = bf16[128,1024]{1,0:T(8,128)(2,1)} collective-permute-done((bf16[128,1024]{1,0:T(8,128)(2,1)}, bf16[128,1024]{1,0:T(8,128)(2,1)}, u32[]{:S(2)}, u32[]{:S(2)}) %collective-permute-start.11) | collective-permute-done | bytes 262176 | tf_op jit(solution)/shard_map/ppermute | solution.py:32
  56.2 1.3 copy-done.10
  57.5 3.1 %shard_map.73 = (bf16[640,1024]{1,0:T(8,128)(2,1)S(1)}, bf16[640,1024]{1,0:T(8,128)(2,1)S(1)}) custom-call(s32[1]{0:T(128)} %bitcast.here_ref, bf16[512,1152]{1,0:T(8,128)(2,1)S(1)} %copy-done.10, bf16[528,1024]{1,0:T(8,128)(2,1)S(1)} %get-tuple-element.50.refs_0_.own_ref, bf16[528,1024]{1,0:T(8,128)(2,1)S(1)} %collective-permute-done.4.high_ref.refs_2_, ...), custom_call_target="tpu_custom_call" | custom-call | flops 4600000000 | bytes 1000 | tf_op jit(solution)/shard_map/pallas_call | solution.py:476
  60.6 1.3 collective-permute-start.14
  61.9 4.1 %collective-permute-start.13 = (bf16[640,1024]{1,0:T(8,128)(2,1)S(1)}, bf16[640,1024]{1,0:T(8,128)(2,1)S(1)}, u32[]{:S(2)}, u32[]{:S(2)}) collective-permute-start(bf16[640,1024]{1,0:T(8,128)(2,1)S(1)} %get-tuple-element.65.refs_0_.own_ref), channel_id=1, source_target_pairs={{0,4},{1,5},{2,6},{3,7},{4,8},{5,9},{6,10},{7,11},{8,12},{9,13},{1... | collective-permute-start | bytes 3932168 | tf_op jit(solution)/shard_map/ppermute | solution.py:27
  66.0 2.1 %shard_map.74 = (bf16[256,1024]{1,0:T(8,128)(2,1)S(1)}, bf16[256,1024]{1,0:T(8,128)(2,1)S(1)}, bf16[256,1024]{1,0:T(8,128)(2,1)S(1)}, bf16[256,1024]{1,0:T(8,128)(2,1)S(1)}) custom-call(s32[1]{0:T(128)} %bitcast.here_ref, bf16[128,8,1024]{2,1,0:T(8,128)(2,1)} %refs_6_.1, bf16[128,8,512]{2,1,0:T(8,128)(2,1)} %collective-permute-done.9.got_ref, ...), custom_call_target="tpu_custom_call" | custom-call | flops 2300000000 | bytes 1000 | tf_op jit(solution)/shard_map/pallas_call | solution.py:212
  68.1 0.9 collective-permute-start.15
  69.0 3.2 %collective-permute-start.16 = (bf16[256,1024]{1,0:T(8,128)(2,1)S(1)}, bf16[256,1024]{1,0:T(8,128)(2,1)S(1)}, u32[]{:S(2)}, u32[]{:S(2)}) collective-permute-start(bf16[256,1024]{1,0:T(8,128)(2,1)S(1)} %get-tuple-element.73), channel_id=1, source_target_pairs={{0,2},{1,3},{2,0},{3,1},{4,6},{5,7},{6,4},{7,5},{8,10},{9,11},{10,... | collective-permute-start | bytes 1572872 | tf_op jit(solution)/shard_map/ppermute | solution.py:32
  72.5 5.7 %shard_map.75 = (f32[128,8,1024]{2,1,0:T(8,128)}, f32[8,128]{1,0:T(8,128)S(1)}) custom-call(f32[128,8,1024]{2,1,0:T(8,128)} %refs_5_.1, f32[128,8,1024]{2,1,0:T(8,128)} %refs_5_.1, f32[128,8,1024]{2,1,0:T(8,128)} %refs_5_.1, f32[128,8,1024]{2,1,0:T(8,128)} %get-tuple-element.57.refs_0_, ...), custom_call_target="tpu_custom_call", output_to_operand_aliasing={{0}: (3, {})} | custom-call | flops 5750000128 | bytes 1000 | tf_op jit(solution)/shard_map/pallas_call | solution.py:599
  78.2 2.6 %shard_map.76 = (bf16[128,8,1024]{2,1,0:T(8,128)(2,1)}, f32[128,8,1024]{2,1,0:T(8,128)}) custom-call(s32[1]{0:T(128)} %bitcast.here_ref, s32[16,6]{1,0:T(8,128)S(1)} %copy.13.cover_ref, s32[16,6]{1,0:T(8,128)S(1)} %copy.14.offset_ref, bf16[8,128,128]{2,1,0:T(8,128)(2,1)S(1)} %copy-done, ...), custom_call_target="tpu_custom_call", output_to_operand_aliasing={{1}: (10, {})} | custom-call | flops 3449999872 | bytes 1000 | tf_op jit(solution)/shard_map/pallas_call | solution.py:283
  80.8 3.2 %collective-permute-done.16.refs_2_ = bf16[256,1024]{1,0:T(8,128)(2,1)S(1)} collective-permute-done((bf16[256,1024]{1,0:T(8,128)(2,1)S(1)}, bf16[256,1024]{1,0:T(8,128)(2,1)S(1)}, u32[]{:S(2)}, u32[]{:S(2)}) %collective-permute-start.16) | collective-permute-done | bytes 524320 | tf_op jit(solution)/shard_map/ppermute | solution.py:32
  84.1 11.5 %collective-permute-done.17.refs_3_ = bf16[256,1024]{1,0:T(8,128)(2,1)S(1)} collective-permute-done((bf16[256,1024]{1,0:T(8,128)(2,1)S(1)}, bf16[256,1024]{1,0:T(8,128)(2,1)S(1)}, u32[]{:S(2)}, u32[]{:S(2)}) %collective-permute-start.17) | collective-permute-done | bytes 524320 | tf_op jit(solution)/shard_map/ppermute | solution.py:32
  95.6 1.6 %copy-done.9 = bf16[128,8,1024]{2,1,0:T(8,128)(2,1)S(1)} copy-done((bf16[128,8,1024]{2,1,0:T(8,128)(2,1)S(1)}, bf16[128,8,1024]{2,1,0:T(8,128)(2,1)}, u32[]{:S(2)}) %copy-start.9) | copy-done | bytes 2097176
  97.2 2.1 %shard_map.77 = (bf16[512,1024]{1,0:T(8,128)(2,1)S(1)}, bf16[128,1024]{1,0:T(8,128)(2,1)S(1)}) custom-call(s32[1]{0:T(128)} %bitcast.here_ref, bf16[512,1152]{1,0:T(8,128)(2,1)S(1)} %copy-done.11, bf16[640,1024]{1,0:T(8,128)(2,1)S(1)} %get-tuple-element.71.own_ref, bf16[640,1024]{1,0:T(8,128)(2,1)S(1)} %collective-permute-done.14.high_ref, ...), custom_call_target="tpu_custom_call" | custom-call | flops 3449999872 | bytes 1000 | tf_op jit(solution)/shard_map/pallas_call | solution.py:502
  99.2 1.3 collective-permute-start.18
  100.5 4.1 %collective-permute-start.22 = (bf16[512,1024]{1,0:T(8,128)(2,1)S(1)}, bf16[512,1024]{1,0:T(8,128)(2,1)S(1)}, u32[]{:S(2)}, u32[]{:S(2)}) collective-permute-start(bf16[512,1024]{1,0:T(8,128)(2,1)S(1)} %get-tuple-element.76.refs_0_.own_ref), channel_id=1, source_target_pairs={{0,4},{1,5},{2,6},{3,7},{4,8},{5,9},{6,10},{7,11},{8,12},{9,13},{1... | collective-permute-start | bytes 3145736 | tf_op jit(solution)/shard_map/ppermute | solution.py:27
  104.6 4.3 %collective-permute-done.18.refs_1_.high_ref = bf16[128,1024]{1,0:T(8,128)(2,1)S(1)} collective-permute-done((bf16[128,1024]{1,0:T(8,128)(2,1)S(1)}, bf16[128,1024]{1,0:T(8,128)(2,1)S(1)}, u32[]{:S(2)}, u32[]{:S(2)}) %collective-permute-start.18) | collective-permute-done | bytes 262176 | tf_op jit(solution)/shard_map/ppermute | solution.py:27
  108.9 2.1 %shard_map.78 = (bf16[256,1024]{1,0:T(8,128)(2,1)S(1)}, bf16[256,1024]{1,0:T(8,128)(2,1)S(1)}, bf16[256,1024]{1,0:T(8,128)(2,1)S(1)}, bf16[256,1024]{1,0:T(8,128)(2,1)S(1)}) custom-call(s32[1]{0:T(128)} %bitcast.here_ref, bf16[512,1152]{1,0:T(8,128)(2,1)S(1)} %copy-done.12, bf16[640,1024]{1,0:T(8,128)(2,1)S(1)} %get-tuple-element.65.refs_0_.own_ref, ...), custom_call_target="tpu_custom_call" | custom-call | flops 3449999872 | bytes 1000 | tf_op jit(solution)/shard_map/pallas_call | solution.py:534
  111.0 0.9 shard_map.79.refs_0_.own_ref
  111.9 0.7 collective-permute-start.26
  112.6 1.0 collective-permute-start.19
  113.6 1.5 collective-permute-start.20
  115.4 11.2 %collective-permute-done.22.low_ref = bf16[512,1024]{1,0:T(8,128)(2,1)S(1)} collective-permute-done((bf16[512,1024]{1,0:T(8,128)(2,1)S(1)}, bf16[512,1024]{1,0:T(8,128)(2,1)S(1)}, u32[]{:S(2)}, u32[]{:S(2)}) %collective-permute-start.22) | collective-permute-done | bytes 1048608 | tf_op jit(solution)/shard_map/ppermute | solution.py:27
  126.6 2.0 %shard_map.80 = (bf16[128,1024]{1,0:T(8,128)(2,1)S(1)}, bf16[128,1024]{1,0:T(8,128)(2,1)S(1)}, bf16[128,1024]{1,0:T(8,128)(2,1)S(1)}, bf16[128,1024]{1,0:T(8,128)(2,1)S(1)}) custom-call(s32[1]{0:T(128)} %bitcast.here_ref, bf16[512,1152]{1,0:T(8,128)(2,1)S(1)} %copy-done.12, bf16[512,1024]{1,0:T(8,128)(2,1)S(1)} %get-tuple-element.76.refs_0_.own_ref, ...), custom_call_target="tpu_custom_call" | custom-call | flops 3449999872 | bytes 1000 | tf_op jit(solution)/shard_map/pallas_call | solution.py:534
  128.6 1.3 collective-permute-start.23
  129.9 1.5 collective-permute-start.24
  131.6 7.4 %collective-permute-done.21.refs_3_ = bf16[256,1024]{1,0:T(8,128)(2,1)S(1)} collective-permute-done((bf16[256,1024]{1,0:T(8,128)(2,1)S(1)}, bf16[256,1024]{1,0:T(8,128)(2,1)S(1)}, u32[]{:S(2)}, u32[]{:S(2)}) %collective-permute-start.21) | collective-permute-done | bytes 524320 | tf_op jit(solution)/shard_map/ppermute | solution.py:32
  139.1 2.9 %shard_map.81.tv_ref = f32[128,8,1024]{2,1,0:T(8,128)} custom-call(s32[1]{0:T(128)} %bitcast.here_ref, f32[128,8,1024]{2,1,0:T(8,128)} %get-tuple-element.69.tv_ref, bf16[256,1024]{1,0:T(8,128)(2,1)S(1)} %get-tuple-element.78.refs_4_.refs_0_, bf16[256,1024]{1,0:T(8,128)(2,1)S(1)} %collective-permute-done.19.refs_1_, ...), custom_call_target="tpu_custom_call", output_to_operand_aliasing={{}: (1, {})} | custom-call | flops 2990000128 | bytes 1000 | tf_op jit(solution)/shard_map/pallas_call | solution.py:392
  142.0 2.6 %shard_map.83 = bf16[128,8,1024]{2,1,0:T(8,128)(2,1)} custom-call(s32[1]{0:T(128)} %bitcast.here_ref, bf16[128,8,512]{2,1,0:T(8,128)(2,1)S(1)} %shard_map.79.refs_0_.own_ref, bf16[128,8,512]{2,1,0:T(8,128)(2,1)S(1)} %collective-permute-done.26.above_ref, bf16[256,1024]{1,0:T(8,128)(2,1)S(1)} %get-tuple-element.78.refs_4_.refs_0_, ...), custom_call_target="tpu_custom_call" | custom-call | flops 2990000128 | bytes 1000 | tf_op jit(solution)/shard_map/pallas_call | solution.py:370
  144.6 5.2 %collective-permute-done.25.refs_3_ = bf16[128,1024]{1,0:T(8,128)(2,1)S(1)} collective-permute-done((bf16[128,1024]{1,0:T(8,128)(2,1)S(1)}, bf16[128,1024]{1,0:T(8,128)(2,1)S(1)}, u32[]{:S(2)}, u32[]{:S(2)}) %collective-permute-start.25) | collective-permute-done | bytes 262176 | tf_op jit(solution)/shard_map/ppermute | solution.py:32
  149.8 2.9 %shard_map.82 = f32[128,8,1024]{2,1,0:T(8,128)} custom-call(s32[1]{0:T(128)} %bitcast.here_ref, f32[128,8,1024]{2,1,0:T(8,128)} %shard_map.81.tv_ref, bf16[128,1024]{1,0:T(8,128)(2,1)S(1)} %get-tuple-element.82.refs_4_.refs_0_, bf16[128,1024]{1,0:T(8,128)(2,1)S(1)} %collective-permute-done.23.refs_1_, ...), custom_call_target="tpu_custom_call", output_to_operand_aliasing={{}: (1, {})} | custom-call | flops 2990000128 | bytes 1000 | tf_op jit(solution)/shard_map/pallas_call | solution.py:392
  (57 shorter events, 3.8 us)
Async XLA Ops:
  5.7 11.7 %copy-start.1 = (bf16[128,1024]{1,0:T(8,128)(2,1)}, bf16[128,1024]{1,0:T(8,128)(2,1)S(1)}, u32[]{:S(2)}) copy-start(bf16[128,1024]{1,0:T(8,128)(2,1)S(1)} %get-tuple-element.63.refs_4_) | copy-start | bytes 786436
  5.7 19.5 %collective-permute-start.6 = (bf16[128,8,512]{2,1,0:T(8,128)(2,1)S(1)}, bf16[128,8,512]{2,1,0:T(8,128)(2,1)S(1)}, u32[]{:S(2)}, u32[]{:S(2)}) collective-permute-start(bf16[128,8,512]{2,1,0:T(8,128)(2,1)S(1)} %get-tuple-element.54), channel_id=1, source_target_pairs={{3,7},{7,11},{11,15},{19,23},{23,27},{27,31}} | collective-permute-start | bytes 3145736 | tf_op jit(solution)/shard_map/ppermute | solution.py:27
  6.4 11.0 %collective-permute-start.1 = (bf16[128,1024]{1,0:T(8,128)(2,1)S(1)}, bf16[128,1024]{1,0:T(8,128)(2,1)S(1)}, u32[]{:S(2)}, u32[]{:S(2)}) collective-permute-start(bf16[128,1024]{1,0:T(8,128)(2,1)S(1)} %get-tuple-element.46), channel_id=1, source_target_pairs={{0,2},{1,3},{2,0},{3,1},{4,6},{5,7},{6,4},{7,5},{8,10},{9,11},{10,... | collective-permute-start | bytes 786440 | tf_op jit(solution)/shard_map/ppermute | solution.py:32
  11.1 6.3 %collective-permute-start.3 = (bf16[128,1024]{1,0:T(8,128)(2,1)S(1)}, bf16[128,1024]{1,0:T(8,128)(2,1)S(1)}, u32[]{:S(2)}, u32[]{:S(2)}) collective-permute-start(bf16[128,1024]{1,0:T(8,128)(2,1)S(1)} %get-tuple-element.49), channel_id=1, source_target_pairs={{0,1},{1,0},{2,3},{3,2},{4,5},{5,4},{6,7},{7,6},{8,9},{9,8},{10,11... | collective-permute-start | bytes 786440 | tf_op jit(solution)/shard_map/ppermute | solution.py:32
  11.1 6.3 %collective-permute-start = (bf16[144,1024]{1,0:T(8,128)(2,1)S(1)}, bf16[144,1024]{1,0:T(8,128)(2,1)S(1)}, u32[]{:S(2)}, u32[]{:S(2)}) collective-permute-start(bf16[144,1024]{1,0:T(8,128)(2,1)S(1)} %get-tuple-element.44), channel_id=1, source_target_pairs={{0,1},{1,0},{2,3},{3,2},{4,5},{5,4},{6,7},{7,6},{8,9},{9,8},{10,11... | collective-permute-start | bytes 884744 | tf_op jit(solution)/shard_map/ppermute | solution.py:32
  11.6 10.5 %collective-permute-start.2 = (bf16[144,1024]{1,0:T(8,128)(2,1)S(1)}, bf16[144,1024]{1,0:T(8,128)(2,1)S(1)}, u32[]{:S(2)}, u32[]{:S(2)}) collective-permute-start(bf16[144,1024]{1,0:T(8,128)(2,1)S(1)} %get-tuple-element.47), channel_id=1, source_target_pairs={{0,3},{1,2},{2,1},{3,0},{4,7},{5,6},{6,5},{7,4},{8,11},{9,10},{10,... | collective-permute-start | bytes 884744 | tf_op jit(solution)/shard_map/ppermute | solution.py:32
  17.4 5.7 %copy-start.3 = (bf16[128,1024]{1,0:T(8,128)(2,1)}, bf16[128,1024]{1,0:T(8,128)(2,1)S(1)}, u32[]{:S(2)}) copy-start(bf16[128,1024]{1,0:T(8,128)(2,1)S(1)} %collective-permute-done.3.refs_5_) | copy-start | bytes 786436
  23.1 33.0 %collective-permute-start.4 = (bf16[528,1024]{1,0:T(8,128)(2,1)S(1)}, bf16[528,1024]{1,0:T(8,128)(2,1)S(1)}, u32[]{:S(2)}, u32[]{:S(2)}) collective-permute-start(bf16[528,1024]{1,0:T(8,128)(2,1)S(1)} %get-tuple-element.50.refs_0_.own_ref), channel_id=1, source_target_pairs={{4,0},{5,1},{6,2},{7,3},{8,4},{9,5},{10,6},{11,7},{12,8},{13,9},{1... | collective-permute-start | bytes 3244040 | tf_op jit(solution)/shard_map/ppermute | solution.py:27
  24.4 26.5 %copy-start.15 = (s32[16,6]{0,1:T(8,128)S(1)}, s32[16,6]{0,1:T(8,128)}, u32[]{:S(2)}) copy-start(s32[16,6]{0,1:T(8,128)} %param.8) | copy-start | bytes 1156
  24.4 27.4 %copy-start = (bf16[8,128,128]{2,1,0:T(8,128)(2,1)S(1)}, bf16[8,128,128]{2,1,0:T(8,128)(2,1)}, u32[]{:S(2)}) copy-start(bf16[8,128,128]{2,1,0:T(8,128)(2,1)} %refs_0_.1) | copy-start | bytes 786436
  24.4 12.6 %collective-permute-start.5 = (bf16[256,1024]{1,0:T(8,128)(2,1)S(1)}, bf16[256,1024]{1,0:T(8,128)(2,1)S(1)}, u32[]{:S(2)}, u32[]{:S(2)}) collective-permute-start(bf16[256,1024]{1,0:T(8,128)(2,1)S(1)} %get-tuple-element.53), channel_id=1, source_target_pairs={{0,2},{1,3},{2,0},{3,1},{4,6},{5,7},{6,4},{7,5},{8,10},{9,11},{10,... | collective-permute-start | bytes 1572872 | tf_op jit(solution)/shard_map/ppermute | solution.py:32
  27.6 0.7 copy-start.13
  28.3 8.8 %collective-permute-start.7 = (bf16[128,1024]{1,0:T(8,128)(2,1)S(1)}, bf16[128,1024]{1,0:T(8,128)(2,1)S(1)}, u32[]{:S(2)}, u32[]{:S(2)}) collective-permute-start(bf16[128,1024]{1,0:T(8,128)(2,1)S(1)} %get-tuple-element.55), channel_id=1, source_target_pairs={{0,1},{1,0},{2,3},{3,2},{4,5},{5,4},{6,7},{7,6},{8,9},{9,8},{10,11... | collective-permute-start | bytes 786440 | tf_op jit(solution)/shard_map/ppermute | solution.py:32
  30.4 19.8 %collective-permute-start.10 = (bf16[128,1024]{1,0:T(8,128)(2,1)S(1)}, bf16[128,1024]{1,0:T(8,128)(2,1)S(1)}, u32[]{:S(2)}, u32[]{:S(2)}) collective-permute-start(bf16[128,1024]{1,0:T(8,128)(2,1)S(1)} %get-tuple-element.61), channel_id=1, source_target_pairs={{0,2},{1,3},{2,0},{3,1},{4,6},{5,7},{6,4},{7,5},{8,10},{9,11},{10,... | collective-permute-start | bytes 786440 | tf_op jit(solution)/shard_map/ppermute | solution.py:32
  37.1 0.7 copy-start.5
  37.8 28.2 %collective-permute-start.9 = (bf16[128,8,512]{2,1,0:T(8,128)(2,1)}, bf16[128,8,512]{2,1,0:T(8,128)(2,1)}, u32[]{:S(2)}, u32[]{:S(2)}) collective-permute-start(bf16[128,8,512]{2,1,0:T(8,128)(2,1)} %get-tuple-element.58), channel_id=1, source_target_pairs={{3,7},{7,11},{11,15},{19,23},{23,27},{27,31}} | collective-permute-start | bytes 3145736 | tf_op jit(solution)/shard_map/ppermute | solution.py:27
  39.4 16.7 %collective-permute-start.8 = (bf16[144,1024]{1,0:T(8,128)(2,1)}, bf16[144,1024]{1,0:T(8,128)(2,1)}, u32[]{:S(2)}, u32[]{:S(2)}) collective-permute-start(bf16[144,1024]{1,0:T(8,128)(2,1)} %get-tuple-element.56), channel_id=1, source_target_pairs={{0,4},{1,5},{2,6},{3,7},{4,8},{5,9},{6,10},{7,11},{8,12},{9,13},{1... | collective-permute-start | bytes 884744 | tf_op jit(solution)/shard_map/ppermute | solution.py:27
  43.8 12.4 %collective-permute-start.11 = (bf16[128,1024]{1,0:T(8,128)(2,1)}, bf16[128,1024]{1,0:T(8,128)(2,1)}, u32[]{:S(2)}, u32[]{:S(2)}) collective-permute-start(bf16[128,1024]{1,0:T(8,128)(2,1)} %get-tuple-element.62), channel_id=1, source_target_pairs={{0,3},{1,2},{2,1},{3,0},{4,7},{5,6},{6,5},{7,4},{8,11},{9,10},{10,... | collective-permute-start | bytes 786440 | tf_op jit(solution)/shard_map/ppermute | solution.py:32
  50.2 0.7 copy-start.7
  50.9 5.2 %collective-permute-start.12 = (bf16[128,1024]{1,0:T(8,128)(2,1)}, bf16[128,1024]{1,0:T(8,128)(2,1)}, u32[]{:S(2)}, u32[]{:S(2)}) collective-permute-start(bf16[128,1024]{1,0:T(8,128)(2,1)} %slice.3), channel_id=1, source_target_pairs={{0,1},{1,0},{2,3},{3,2},{4,5},{5,4},{6,7},{7,6},{8,9},{9,8},{10,11... | collective-permute-start | bytes 786440 | tf_op jit(solution)/shard_map/ppermute | solution.py:32
  51.8 4.4 %copy-start.2 = (bf16[128,1024]{1,0:T(8,128)(2,1)S(1)}, bf16[128,1024]{1,0:T(8,128)(2,1)}, u32[]{:S(2)}) copy-start(bf16[128,1024]{1,0:T(8,128)(2,1)} %copy-done.1) | copy-start | bytes 786436
  51.8 4.4 %copy-start.4 = (bf16[128,1024]{1,0:T(8,128)(2,1)S(1)}, bf16[128,1024]{1,0:T(8,128)(2,1)}, u32[]{:S(2)}) copy-start(bf16[128,1024]{1,0:T(8,128)(2,1)} %copy-done.3) | copy-start | bytes 786436
  51.8 4.4 %copy-start.6 = (bf16[128,1024]{1,0:T(8,128)(2,1)S(1)}, bf16[128,1024]{1,0:T(8,128)(2,1)}, u32[]{:S(2)}) copy-start(bf16[128,1024]{1,0:T(8,128)(2,1)} %copy-done.5) | copy-start | bytes 786436
  51.8 4.4 %copy-start.8 = (bf16[128,1024]{1,0:T(8,128)(2,1)S(1)}, bf16[128,1024]{1,0:T(8,128)(2,1)}, u32[]{:S(2)}) copy-start(bf16[128,1024]{1,0:T(8,128)(2,1)} %copy-done.7) | copy-start | bytes 786436
  51.8 4.4 %copy-start.14 = (bf16[128,1024]{1,0:T(8,128)(2,1)S(1)}, bf16[128,1024]{1,0:T(8,128)(2,1)}, u32[]{:S(2)}) copy-start(bf16[128,1024]{1,0:T(8,128)(2,1)} %copy-done.13) | copy-start | bytes 786436
  56.2 1.3 copy-start.10
  60.6 34.9 %collective-permute-start.14 = (bf16[640,1024]{1,0:T(8,128)(2,1)S(1)}, bf16[640,1024]{1,0:T(8,128)(2,1)S(1)}, u32[]{:S(2)}, u32[]{:S(2)}) collective-permute-start(bf16[640,1024]{1,0:T(8,128)(2,1)S(1)} %get-tuple-element.71.own_ref), channel_id=1, source_target_pairs={{4,0},{5,1},{6,2},{7,3},{8,4},{9,5},{10,6},{11,7},{12,8},{13,9},{1... | collective-permute-start | bytes 3932168 | tf_op jit(solution)/shard_map/ppermute | solution.py:27
  61.9 33.6 %collective-permute-start.13 = (bf16[640,1024]{1,0:T(8,128)(2,1)S(1)}, bf16[640,1024]{1,0:T(8,128)(2,1)S(1)}, u32[]{:S(2)}, u32[]{:S(2)}) collective-permute-start(bf16[640,1024]{1,0:T(8,128)(2,1)S(1)} %get-tuple-element.65.refs_0_.own_ref), channel_id=1, source_target_pairs={{0,4},{1,5},{2,6},{3,7},{4,8},{5,9},{6,10},{7,11},{8,12},{9,13},{1... | collective-permute-start | bytes 3932168 | tf_op jit(solution)/shard_map/ppermute | solution.py:27
  68.1 12.7 %collective-permute-start.15 = (bf16[256,1024]{1,0:T(8,128)(2,1)S(1)}, bf16[256,1024]{1,0:T(8,128)(2,1)S(1)}, u32[]{:S(2)}, u32[]{:S(2)}) collective-permute-start(bf16[256,1024]{1,0:T(8,128)(2,1)S(1)} %get-tuple-element.72), channel_id=1, source_target_pairs={{0,1},{1,0},{2,3},{3,2},{4,5},{5,4},{6,7},{7,6},{8,9},{9,8},{10,11... | collective-permute-start | bytes 1572872 | tf_op jit(solution)/shard_map/ppermute | solution.py:32
  69.0 15.1 %collective-permute-start.16 = (bf16[256,1024]{1,0:T(8,128)(2,1)S(1)}, bf16[256,1024]{1,0:T(8,128)(2,1)S(1)}, u32[]{:S(2)}, u32[]{:S(2)}) collective-permute-start(bf16[256,1024]{1,0:T(8,128)(2,1)S(1)} %get-tuple-element.73), channel_id=1, source_target_pairs={{0,2},{1,3},{2,0},{3,1},{4,6},{5,7},{6,4},{7,5},{8,10},{9,11},{10,... | collective-permute-start | bytes 1572872 | tf_op jit(solution)/shard_map/ppermute | solution.py:32
  72.1 23.4 %collective-permute-start.17 = (bf16[256,1024]{1,0:T(8,128)(2,1)S(1)}, bf16[256,1024]{1,0:T(8,128)(2,1)S(1)}, u32[]{:S(2)}, u32[]{:S(2)}) collective-permute-start(bf16[256,1024]{1,0:T(8,128)(2,1)S(1)} %get-tuple-element.74), channel_id=1, source_target_pairs={{0,3},{1,2},{2,1},{3,0},{4,7},{5,6},{6,5},{7,4},{8,11},{9,10},{10,... | collective-permute-start | bytes 1572872 | tf_op jit(solution)/shard_map/ppermute | solution.py:32
  78.2 17.3 %copy-start.11 = (bf16[512,1152]{1,0:T(8,128)(2,1)S(1)}, bf16[512,1152]{1,0:T(8,128)(2,1)}, u32[]{:S(2)}) copy-start(bf16[512,1152]{1,0:T(8,128)(2,1)} %get-tuple-element.59.band_ref) | copy-start | bytes 3538948
  95.6 1.6 %copy-start.9 = (bf16[128,8,1024]{2,1,0:T(8,128)(2,1)S(1)}, bf16[128,8,1024]{2,1,0:T(8,128)(2,1)}, u32[]{:S(2)}) copy-start(bf16[128,8,1024]{2,1,0:T(8,128)(2,1)} %get-tuple-element.75.refs_4_.refs_5_) | copy-start | bytes 6291460
  97.2 11.7 %copy-start.12 = (bf16[512,1152]{1,0:T(8,128)(2,1)S(1)}, bf16[512,1152]{1,0:T(8,128)(2,1)}, u32[]{:S(2)}) copy-start(bf16[512,1152]{1,0:T(8,128)(2,1)} %get-tuple-element.70.band_ref) | copy-start | bytes 3538948
  99.2 9.7 %collective-permute-start.18 = (bf16[128,1024]{1,0:T(8,128)(2,1)S(1)}, bf16[128,1024]{1,0:T(8,128)(2,1)S(1)}, u32[]{:S(2)}, u32[]{:S(2)}) collective-permute-start(bf16[128,1024]{1,0:T(8,128)(2,1)S(1)} %get-tuple-element.77), channel_id=1, source_target_pairs={{4,0},{5,1},{6,2},{7,3},{8,4},{9,5},{10,6},{11,7},{12,8},{13,9},{1... | collective-permute-start | bytes 786440 | tf_op jit(solution)/shard_map/ppermute | solution.py:27
  100.5 26.1 %collective-permute-start.22 = (bf16[512,1024]{1,0:T(8,128)(2,1)S(1)}, bf16[512,1024]{1,0:T(8,128)(2,1)S(1)}, u32[]{:S(2)}, u32[]{:S(2)}) collective-permute-start(bf16[512,1024]{1,0:T(8,128)(2,1)S(1)} %get-tuple-element.76.refs_0_.own_ref), channel_id=1, source_target_pairs={{0,4},{1,5},{2,6},{3,7},{4,8},{5,9},{6,10},{7,11},{8,12},{9,13},{1... | collective-permute-start | bytes 3145736 | tf_op jit(solution)/shard_map/ppermute | solution.py:27
  111.9 30.1 %collective-permute-start.26 = (bf16[128,8,512]{2,1,0:T(8,128)(2,1)S(1)}, bf16[128,8,512]{2,1,0:T(8,128)(2,1)S(1)}, u32[]{:S(2)}, u32[]{:S(2)}) collective-permute-start(bf16[128,8,512]{2,1,0:T(8,128)(2,1)S(1)} %shard_map.79.refs_0_.own_ref), channel_id=1, source_target_pairs={{7,3},{11,7},{15,11},{23,19},{27,23},{31,27}} | collective-permute-start | bytes 3145736 | tf_op jit(solution)/shard_map/ppermute | solution.py:27
  112.6 17.3 %collective-permute-start.19 = (bf16[256,1024]{1,0:T(8,128)(2,1)S(1)}, bf16[256,1024]{1,0:T(8,128)(2,1)S(1)}, u32[]{:S(2)}, u32[]{:S(2)}) collective-permute-start(bf16[256,1024]{1,0:T(8,128)(2,1)S(1)} %get-tuple-element.79), channel_id=1, source_target_pairs={{0,1},{1,0},{2,3},{3,2},{4,5},{5,4},{6,7},{7,6},{8,9},{9,8},{10,11... | collective-permute-start | bytes 1572872 | tf_op jit(solution)/shard_map/ppermute | solution.py:32
  113.6 17.8 %collective-permute-start.20 = (bf16[256,1024]{1,0:T(8,128)(2,1)S(1)}, bf16[256,1024]{1,0:T(8,128)(2,1)S(1)}, u32[]{:S(2)}, u32[]{:S(2)}) collective-permute-start(bf16[256,1024]{1,0:T(8,128)(2,1)S(1)} %get-tuple-element.80), channel_id=1, source_target_pairs={{0,2},{1,3},{2,0},{3,1},{4,6},{5,7},{6,4},{7,5},{8,10},{9,11},{10,... | collective-permute-start | bytes 1572872 | tf_op jit(solution)/shard_map/ppermute | solution.py:32
  115.1 23.9 %collective-permute-start.21 = (bf16[256,1024]{1,0:T(8,128)(2,1)S(1)}, bf16[256,1024]{1,0:T(8,128)(2,1)S(1)}, u32[]{:S(2)}, u32[]{:S(2)}) collective-permute-start(bf16[256,1024]{1,0:T(8,128)(2,1)S(1)} %get-tuple-element.81), channel_id=1, source_target_pairs={{0,3},{1,2},{2,1},{3,0},{4,7},{5,6},{6,5},{7,4},{8,11},{9,10},{10,... | collective-permute-start | bytes 1572872 | tf_op jit(solution)/shard_map/ppermute | solution.py:32
  128.6 16.0 %collective-permute-start.23 = (bf16[128,1024]{1,0:T(8,128)(2,1)S(1)}, bf16[128,1024]{1,0:T(8,128)(2,1)S(1)}, u32[]{:S(2)}, u32[]{:S(2)}) collective-permute-start(bf16[128,1024]{1,0:T(8,128)(2,1)S(1)} %get-tuple-element.83), channel_id=1, source_target_pairs={{0,1},{1,0},{2,3},{3,2},{4,5},{5,4},{6,7},{7,6},{8,9},{9,8},{10,11... | collective-permute-start | bytes 786440 | tf_op jit(solution)/shard_map/ppermute | solution.py:32
  129.9 14.7 %collective-permute-start.24 = (bf16[128,1024]{1,0:T(8,128)(2,1)S(1)}, bf16[128,1024]{1,0:T(8,128)(2,1)S(1)}, u32[]{:S(2)}, u32[]{:S(2)}) collective-permute-start(bf16[128,1024]{1,0:T(8,128)(2,1)S(1)} %get-tuple-element.84), channel_id=1, source_target_pairs={{0,2},{1,3},{2,0},{3,1},{4,6},{5,7},{6,4},{7,5},{8,10},{9,11},{10,... | collective-permute-start | bytes 786440 | tf_op jit(solution)/shard_map/ppermute | solution.py:32
  131.4 18.4 %collective-permute-start.25 = (bf16[128,1024]{1,0:T(8,128)(2,1)S(1)}, bf16[128,1024]{1,0:T(8,128)(2,1)S(1)}, u32[]{:S(2)}, u32[]{:S(2)}) collective-permute-start(bf16[128,1024]{1,0:T(8,128)(2,1)S(1)} %get-tuple-element.85), channel_id=1, source_target_pairs={{0,3},{1,2},{2,1},{3,0},{4,7},{5,6},{6,5},{7,4},{8,11},{9,10},{10,... | collective-permute-start | bytes 786440 | tf_op jit(solution)/shard_map/ppermute | solution.py:32

commit v8 on v7

--- a/solution.py
+++ b/solution.py
@@ -86,8 +86,7 @@
 
 def cast_kernel(count, here_ref, *refs):
     parts = TILE // LANES
-    vol_refs, (top_ref, end_ref, sino_ref), out_refs = refs[:parts], refs[parts : parts + 3], refs[parts + 3 :]
-    block_refs, sent_refs = out_refs[:-CHUNKS], out_refs[-CHUNKS:]
+    vol_refs, (top_ref, end_ref), block_refs = refs[:parts], refs[parts : parts + 2], refs[parts + 2 :]
     step = pl.program_id(0)
     rows = ROWS * G
     depth = vol_refs[0].shape[0] // rows
@@ -97,7 +96,6 @@
 
         @pl.when(step // count == c)
         def _():
-            sent_refs[c][...] = sino_ref[...]
             for j, vol_ref in enumerate(vol_refs):
                 for (chunk, group), out_ref in zip(CAST_GROUPS, block_refs):
                     if chunk != c:
@@ -114,7 +112,7 @@
                         out_ref[depth:, :] = both
 
 
-def cast_rows(here, volume, sinogram):
+def cast_rows(here, volume):
     depth, rows, cols = volume.shape
     flat = far(volume.reshape(depth * rows, cols))
     _, count = chunk_tiles(0, cols)
@@ -127,20 +125,17 @@
     out_specs = [
         pl.BlockSpec((shape[0], width), lambda i, at=step_of(c): (0, at(i))) for (c, _), shape in zip(CAST_GROUPS, shapes)
     ]
-    out_specs += [pl.BlockSpec((depth, rows, TILE), lambda i, at=step_of(c): (0, 0, at(i))) for c in range(CHUNKS)]
-    results = [value(shape, BF16) for shape in shapes] + [value((depth, rows, cols // CHUNKS), BF16)] * CHUNKS
     in_specs = [SMEM]
     in_specs += [pl.BlockSpec((depth * rows, LANES), lambda i, j=j: (0, i * parts + j)) for j in range(parts)]
     in_specs += [pl.BlockSpec((rows, width), lambda i, z=z, at=step_of(0): (z, at(i))) for z in (0, depth - 1)]
-    in_specs += [pl.BlockSpec((depth, rows, TILE), lambda i: (0, 0, i))]
     return call(
         functools.partial(cast_kernel, count),
         4,
         grid=(CHUNKS * count,),
         in_specs=in_specs,
         out_specs=out_specs,
-        results=results,
-    )(here, *[flat] * parts, flat, flat, far(sinogram))
+        results=[value(shape, BF16) for shape in shapes],
+    )(here, *[flat] * parts, flat, flat)
 
 
 def last_block(here_ref, blocks):
@@ -157,27 +152,30 @@
     for m in range(G):
         all_ref[m * side : (m + 1) * side] = in_refs[m][:side]
     last_ref[:side] = last_block(here_ref, [ref[:side] for ref in in_refs])
-    all_ref[G * side :] = in_refs[G - 1][side:]
-    last_ref[side:] = in_refs[G - 1][side:]
-
-
-def pack(here, blocks, *tokens):
-    side, cols = blocks[0].shape
-    more = blocks[G - 1].shape[0] - side
+    if last_ref.shape[0] > side:
+        all_ref[G * side :] = in_refs[G - 1][side:]
+        last_ref[side:] = in_refs[G - 1][side:]
+
+
+def pack(here, pieces, more, *tokens):
+    side, cols = pieces[0][0].shape
     tile = 512
     shapes = [(G * side + more, cols), (side + more, cols)]
+    specs = [across(array.shape, tile) for array in arrays_of(pieces)] if more else piece_specs(pieces, side, tile)
     return call(
         pack_kernel,
         1,
         grid=(cols // tile,),
-        in_specs=[SMEM] + [across(block.shape, tile) for block in blocks] + [ANY] * len(tokens),
+        in_specs=[SMEM] + specs + [ANY] * len(tokens),
         out_specs=[across(shape, tile) for shape in shapes],
         results=[value(shape, BF16) for shape in shapes],
-    )(here, *blocks, *tokens)
-
-
-def split_kernel(with_resid, here_ref, own_ref, got_ref, *refs):
-    out_refs, wide = refs[-G - 1 : -1], refs[-1]
+    )(here, *arrays_of(pieces), *tokens)
+
+
+def split_kernel(groups, passing, here_ref, own_ref, got_ref, *refs):
+    out_refs, wide = refs[-len(groups) - passing - 1 : -1], refs[-1]
+    if passing:
+        out_refs[-1][...] = refs[0][...]
     depth, rows, cols = own_ref.shape
     place = lax.rem(here_ref[0], G)
 
@@ -193,33 +191,28 @@
     def _():
         fill(own_ref)
 
-    for m, out_ref in enumerate(out_refs):
-        for j in range(cols // LANES):
-            for start, row in rows_of(place, m):
-                at = pl.ds(start + j * LANES, LANES)
-                out_ref[:depth, at] = wide.at[j][pl.ds(row, depth, stride=rows), :].astype(BF16)
-        if with_resid:
-            out_ref[depth:] = refs[0][m * depth : (m + 1) * depth]
-
-
-def split_rows(here, own, got, chunk, resid, *tokens):
+    for group, out_ref in zip(groups, out_refs):
+        for n, m in enumerate(group):
+            for j in range(cols // LANES):
+                for start, row in rows_of(place, m):
+                    block = wide.at[j][pl.ds(row, depth, stride=rows), :].astype(BF16)
+                    out_ref[n * depth : (n + 1) * depth, start + j * LANES : start + (j + 1) * LANES] = block
+
+
+def split_rows(here, own, got, chunk, groups, passing, *tokens):
     depth, rows, cols = own.shape
     first, count = chunk_tiles(chunk, cols)
-    block = (depth, rows, TILE)
-    width = ROWS * TILE
-    extra = [] if resid is None else [resid]
-    shape = ((1 + len(extra)) * depth, cols)
-    return call(
-        functools.partial(split_kernel, resid is not None),
+    block = pl.BlockSpec((depth, rows, TILE), lambda i: (0, 0, first + i))
+    shapes = [(len(group) * depth, cols) for group in groups] + [(depth, cols)] * len(passing)
+    return call(
+        functools.partial(split_kernel, groups, len(passing)),
         2,
         grid=(count,),
-        in_specs=[SMEM, pl.BlockSpec(block, lambda i: (0, 0, first + i)), pl.BlockSpec(block, lambda i: (0, 0, i))]
-        + [pl.BlockSpec((G * depth, width), lambda i: (0, i))] * len(extra)
-        + [ANY] * len(tokens),
-        out_specs=[across(shape, width)] * G,
-        results=[value(shape, BF16)] * G,
+        in_specs=[SMEM, block, block] + piece_specs(passing, depth, ROWS * TILE) + [ANY] * len(tokens),
+        out_specs=[across(shape, ROWS * TILE) for shape in shapes],
+        results=[value(shape, BF16) for shape in shapes],
         scratch_shapes=[wide_tile(depth * rows)],
-    )(here, far(own), got, *extra, *tokens)
+    )(here, far(own), got, *arrays_of(passing), *tokens)
 
 
 def patch_kernel(slabs, here_ref, cover_ref, offset_ref, *refs):
@@ -448,66 +441,35 @@
     )(here, coverage, offsets, weights, *tokens)
 
 
-def residual_blocks(band, seen, sino_refs):
+def project_kernel(groups, here_ref, band_ref, own_ref, high_ref, low_ref, *refs):
+    sino_refs, (r_ref, down_ref, *group_refs) = refs[:G], refs[-len(groups) - 2 :]
     side = sino_refs[0].shape[0]
-    total = jnp.dot(band, jnp.concatenate(seen, axis=0), preferred_element_type=F32)
-    return [(total[m * side : (m + 1) * side] - ref[...].astype(F32)).astype(BF16) for m, ref in enumerate(sino_refs)]
-
-
-def first_kernel(here_ref, band_ref, own_ref, high_ref, low_ref, *refs):
-    sino_refs, next_refs, (up_ref, down_ref) = refs[:G], refs[G : 2 * G], refs[-2:]
-    side = sino_refs[0].shape[0]
-    resid = residual_blocks(band_ref[...], [own_ref[...], high_ref[...], low_ref[...]], sino_refs)
-    following = [ref[...] for ref in next_refs]
+    seen = jnp.concatenate([own_ref[...], high_ref[...], low_ref[...]], axis=0)
+    total = jnp.dot(band_ref[...], seen, preferred_element_type=F32)
+    resid = [(total[m * side : (m + 1) * side] - ref[...].astype(F32)).astype(BF16) for m, ref in enumerate(sino_refs)]
     for m in range(G):
-        at = slice(m * side, (m + 1) * side)
-        up_ref[at, :] = resid[m]
-        down_ref[at, :] = following[m]
-    up_ref[G * side :] = last_block(here_ref, following)
-    down_ref[G * side :] = last_block(here_ref, resid)
-
-
-def project_first(here, band, own, high, low, sinos, following, *tokens):
+        r_ref[m * side : (m + 1) * side] = resid[m]
+    for group, group_ref in zip(groups, group_refs):
+        for n, m in enumerate(group):
+            group_ref[n * side : (n + 1) * side] = resid[m]
+    down_ref[...] = last_block(here_ref, resid)
+
+
+def project(here, band, own, high, low, sinos, groups, *tokens):
     n, side = band.shape[0], band.shape[0] // G
     cols = own.shape[1]
     tile = 512
     many, one = pl.BlockSpec((n, tile), lambda i: (0, i)), pl.BlockSpec((side, tile), lambda i: (0, i))
-    out = (n + side, cols)
-    return call(
-        first_kernel,
-        4,
+    shapes = [(n, cols), (side, cols)] + [(len(group) * side, cols) for group in groups]
+    return call(
+        functools.partial(project_kernel, groups),
+        3,
         grid=(cols // tile,),
         in_specs=[SMEM, pl.BlockSpec(band.shape, lambda i: (0, 0)), many, many, one]
-        + piece_specs(sinos + following, side, tile)
+        + piece_specs(sinos, side, tile)
         + [ANY] * len(tokens),
-        out_specs=[across(out, tile)] * 2,
-        results=[value(out, BF16)] * 2,
-    )(here, band, own, high, low, *arrays_of(sinos + following), *tokens)
-
-
-def second_kernel(here_ref, band_ref, own_ref, high_ref, low_ref, *refs):
-    sino_refs, (up_ref, down_ref) = refs[:G], refs[-2:]
-    side = sino_refs[0].shape[0]
-    resid = residual_blocks(band_ref[...], [own_ref[...], high_ref[...], low_ref[...]], sino_refs)
-    for m in range(G):
-        up_ref[m * side : (m + 1) * side] = resid[m]
-    down_ref[...] = last_block(here_ref, resid)
-
-
-def project_second(here, band, own, high, low, sinos, *tokens):
-    n, side = band.shape[0], band.shape[0] // G
-    cols = own.shape[1]
-    tile = 512
-    many = pl.BlockSpec((n, tile), lambda i: (0, i))
-    return call(
-        second_kernel,
-        3,
-        grid=(cols // tile,),
-        in_specs=[SMEM, pl.BlockSpec(band.shape, lambda i: (0, 0)), many, many]
-        + piece_specs([(low, G)] + sinos, side, tile)
-        + [ANY] * len(tokens),
-        out_specs=[across((n, cols), tile), across((side, cols), tile)],
-        results=[value((n, cols), BF16), value((side, cols), BF16)],
+        out_specs=[across(shape, tile) for shape in shapes],
+        results=[value(shape, BF16) for shape in shapes],
     )(here, band, own, high, low, *arrays_of(sinos), *tokens)
 
 
@@ -570,13 +532,13 @@
     return (below_flux - fz) + (fy_low - fy) + (fx_low - fx), fz
 
 
-def tv_kernel(last_ref, next_ref, vol_ref, *refs):
+def tv_kernel(next_ref, vol_ref, *refs):
     out_ref, done_ref, flux_ref = refs[-3:]
     deep = vol_ref.shape[0]
 
     @pl.when(pl.program_id(0) == 0)
     def _():
-        flux_ref[...] = tv_below(last_ref[0], vol_ref[0])
+        flux_ref[...] = jnp.zeros_like(flux_ref)
 
     def body(z, flux):
         out_ref[z], flux = tv_slice(vol_ref[z], vol_ref[z + 1], flux)
@@ -587,68 +549,69 @@
     done_ref[...] = flux_ref[:, : done_ref.shape[1]]
 
 
-def half_tv(volume, half, base, *tokens):
+def half_tv(volume, *tokens):
     depth, rows, cols = volume.shape
     deep = 16
-    steps = depth // deep // 2
-    first = half * steps
-    body = pl.BlockSpec((deep, rows, cols), lambda i: (first + i, 0, 0))
-    before = pl.BlockSpec((1, rows, cols), lambda i: (max(first * deep - 1, 0), 0, 0))
-    after = pl.BlockSpec((1, rows, cols), lambda i: (jnp.minimum((first + i + 1) * deep, depth - 1), 0, 0))
-    bases = [] if base is None else [far(base)]
+    body = pl.BlockSpec((deep, rows, cols), lambda i: (i, 0, 0))
+    after = pl.BlockSpec((1, rows, cols), lambda i: (jnp.minimum((i + 1) * deep, depth - 1), 0, 0))
     return call(
         tv_kernel,
-        5,
-        grid=(steps,),
-        in_specs=[before, after, body] + [ANY] * (len(bases) + len(tokens)),
+        9,
+        grid=(depth // deep,),
+        in_specs=[after, body] + [ANY] * len(tokens),
         out_specs=[body, pl.BlockSpec((rows, LANES), lambda i: (0, 0))],
         results=[pltpu.HBM(volume.shape, F32), value((rows, LANES), F32)],
-        input_output_aliases={3: 0} if bases else {},
         scratch_shapes=[pltpu.VMEM((rows, cols), F32)],
-    )(*[far(volume)] * 3, *bases, *tokens)
+    )(far(volume), far(volume), *tokens)
 
 
 def local(volume, sinogram, weights, coverage, offsets):
     slabs = lax.axis_size("slab")
     here = lax.axis_index("slab").astype(jnp.int32).reshape(1)
-    depth = volume.shape[0]
-
-    *blocks, sent0, sent1 = cast_rows(here, volume, sinogram)
-    vols0, (v0, v1, v23) = blocks[:G], blocks[G:]
-    got0 = moved(sent0, G, only=G - 1)
+    depth, rows, _ = volume.shape
+    single = ((0,), (1,), (2,), (3,))
+    paired = ((0,), (1,), (2, 3))
+
+    def tied(array, *others):
+        return lax.optimization_barrier((array, *others))[0]
+
+    def beyond(over, *others):
+        return swapped(tied(over, *others)[depth:], 1)
+
+    *vols0, v0, v1, v23 = cast_rows(here, volume)
+    got = moved(tied(sinogram, vols0[0]), G, only=G - 1)
     got_vols0 = direct(vols0)
     near, over = swapped(v1, 1), swapped(v23, 2)
-    tv, tv_done = half_tv(volume, 0, None, vols0[0])
-    own0, edge0 = pack(here, got_vols0, tv_done, near)
-    high0 = moved(own0, -G)
-    sino0 = split_rows(here, sinogram, got0, 0, None, own0)
+    tv, tv_done = half_tv(volume, vols0[0])
+    own0, edge0 = pack(here, [(array, 0) for array in got_vols0], 2 * rows, tv_done)
+    high0, low0 = moved(own0, -G), moved(edge0, G)
+    band_p, band_b = bands(here, coverage, offsets, weights, own0)
+    *sino0, over_beyond = split_rows(here, sinogram, got, 0, single, [(over, 1)], band_p, near)
     sinos0 = [(array, 0) for array in direct(sino0)]
-    edge0, sent1, over = lax.optimization_barrier((edge0, sent1, over, sinos0[1][0]))[:3]
-    low0 = moved(edge0, G)
-    got1 = moved(sent1, G, only=G - 1)
-    vols1 = [(v0, 0), (near, 0), (over, 0), (swapped(over[depth:], 1), 0)]
-    band_p, band_b = bands(here, coverage, offsets, weights, own0)
-
-    up0, down0 = project_first(here, band_p, own0, high0, low0, sinos0, vols1)
-    from_high, from_low = moved(down0, -G), moved(up0, G)
-    mixed = split_rows(here, sinogram, got1, 1, up0)
-    got_mixed = direct(mixed)
-    tv, tv_done = half_tv(volume, 1, tv, mixed[0])
+    own1, edge1 = pack(here, [(v0, 0), (near, 0), (over, 0), (swapped(over_beyond, 1), 0)], 0)
+    low1, high1 = moved(edge1, G), moved(own1, -G)
+    s0, s1, s23 = split_rows(here, sinogram, got, 1, paired, [], own1)
+
+    resid0, down0, r1, r23 = project(here, band_p, own0, high0, low0, sinos0, paired[1:], low1, s0)
+    from_low0, from_high0 = moved(resid0, G), moved(down0, -G)
+    s_near, s_over = swapped(s1, 1), swapped(s23, 2)
     ends = [got_vols0[1], high0, got_vols0[3], low0]
-    r_last, tv = patch(here, coverage, offsets, weights, ends, volume, sinogram, tv, tv_done)
-    sinos1 = [(array, 0) for array in got_mixed]
-    up1, down1 = project_second(here, band_p, down0, from_high, from_low, sinos1, r_last)
-    from_low1, from_high1 = moved(up1, G), moved(down1, -G)
-
-    backs0 = back(here, band_b, up0, from_low, (from_high, G), [up1, from_high1])
+    r_last, tv = patch(here, coverage, offsets, weights, ends, volume, sinogram, tv, resid0)
+    sinos1 = [(s0, 0), (s_near, 0), (s_over, 0), (beyond(s_over, r_last), 0)]
+    r_near, r_over = swapped(tied(r1, s_over), 1), swapped(tied(r23, s_over), 2)
+    resid1, down1 = project(here, band_p, own1, high1, low1, sinos1, (), r_last)
+    from_low1, from_high1 = moved(resid1, G), moved(down1, -G)
+
+    backs0 = back(here, band_b, resid0, from_low0, (from_high0, 0), [resid1, from_high1])
     got_backs0 = direct(backs0)
-    resid0 = join_rows(here, [(array, 1) for array in got_mixed], sinogram.shape, backs0[0])
-    resid0_above = moved(resid0, -G, only=G - 1)
-    backs1 = back(here, band_b, up1, from_low1, (from_high1, 0), [], resid0)
+    r_pieces = [(resid0, 0), (r_near, 0), (r_over, 0), (beyond(r_over, backs0[0]), 0)]
+    natural0 = join_rows(here, r_pieces, sinogram.shape, backs0[0])
+    above0 = moved(natural0, -G, only=G - 1)
+    backs1 = back(here, band_b, resid1, from_low1, (from_high1, 0), [], natural0)
     got_backs1 = direct(backs1)
-    residual = settle(here, slabs, resid0, resid0_above, [(array, 1) for array in got_backs0], r_last, backs1[0])
+    residual = settle(here, slabs, natural0, above0, [(array, 1) for array in got_backs0], r_last, backs1[0])
     gradient = finish(here, 0, tv, [(array, 0) for array in got_backs0], backs1[0])
-    gradient = finish(here, 1, gradient, [(array, 0) for array in got_backs1])
+    gradient = finish(here, 1, gradient, [(array, 0) for array in got_backs1], residual)
     return (gradient, residual)
 
 

time: 154 us -> 143 us (0.929)
  waiting for transfers between devices: 55.8 us -> 40.9 us
  starting transfers between devices: 43.5 us -> 50.7 us
  Pallas kernels: 45.9 us -> 42.3 us
    ppermute x18 -> x21, waiting for transfers between devices: 40.3 us -> 20.1 us  [swapped(): return lax.ppermute(value, 'slab', [(i, i ^ bits) for i in range(count)])]
    ppermute x9 -> x10, starting transfers between devices: 19.4 us -> 24.8 us  [moved(): return lax.ppermute(value, 'slab', pairs)]
    ppermute x9 -> x10, waiting for transfers between devices: 15.5 us -> 20.9 us  [moved(): return lax.ppermute(value, 'slab', pairs)]
    pallas_call x7, Pallas kernels: 22.1 us -> 19.5 us  [the longest x1 9.87 us: half_tv(): call(tv_kernel, 9, grid=(depth // deep,), in_specs=[after, body] + [ANY]...]
    ppermute x18 -> x21, starting transfers between devices: 24.1 us -> 26 us  [swapped(): return lax.ppermute(value, 'slab', [(i, i ^ bits) for i in range(count)])]
    unnamed x34 -> x24, local copies, waits for them, and re-layouts: 5.89 us -> 6.76 us
  transfers between devices with their start and end apart: 27 -> 31, of which waited for: 9 -> 9; matrix products, arithmetic and copies ran while one was open for 1% -> 1% of each run, Pallas kernels for 23% -> 25%
where the time goes in v8:
time: 143 us; the launch traced here: 142 us
  starting transfers between devices  50.7 us (35%)
  Pallas kernels  42.3 us (30%)
  waiting for transfers between devices  40.9 us (29%)
  local copies, waits for them, and re-layouts  6.79 us (5%)
    ppermute x21, starting transfers between devices, swapped(): return lax.ppermute(value, 'slab', [(i, i ^ bits) for i in range(count)])  26 us
    ppermute x10, starting transfers between devices, moved(): return lax.ppermute(value, 'slab', pairs)  24.8 us
    ppermute x10, waiting for transfers between devices, moved(): return lax.ppermute(value, 'slab', pairs)  20.9 us
    ppermute x21, waiting for transfers between devices, swapped(): return lax.ppermute(value, 'slab', [(i, i ^ bits) for i in range(count)])  20.1 us
    pallas_call x1, Pallas kernels, half_tv(): call(tv_kernel, 9, grid=(depth // deep,), in_specs=[after, body] + [ANY]...  9.87 us
    unnamed x24, local copies, waits for them, and re-layouts  6.76 us
    pallas_call x2, Pallas kernels, finish(): call(finish_kernel, 2.6, grid=(count,), in_specs=[SMEM, part] + piece_spe...  5.85 us
    pallas_call x2, Pallas kernels, project(): call(functools.partial(project_kernel, groups), 3, grid=(cols // tile,),...  4.24 us
  transfers between devices with their start and end apart: 31, of which 9 were waited for; matrix products, arithmetic and copies ran while one was open for 1% of the time, Pallas kernels for 25%

profile of v8, /device:TPU:1, one launch (start us, length us, event | category | flops | bytes accessed | tf_op | source)
XLA Modules:
  0.0 141.7 jit_solution(9101919794019418818)
XLA Ops:
  0.6 4.2 %shard_map.68 = (bf16[128,1024]{1,0:T(8,128)(2,1)S(1)}, bf16[144,1024]{1,0:T(8,128)(2,1)S(1)}, bf16[128,1024]{1,0:T(8,128)(2,1)S(1)}, bf16[144,1024]{1,0:T(8,128...) custom-call(s32[1]{0:T(128)} %bitcast.here_ref, ...), custom_call_target="tpu_custom_call" | custom-call | flops 4600000000 | bytes 1000 | tf_op jit(solution)/shard_map/pallas_call | solution.py:131
  5.6 2.0 %collective-permute-start.5 = (bf16[128,8,1024]{2,1,0:T(8,128)(2,1)}, bf16[128,8,1024]{2,1,0:T(8,128)(2,1)}, u32[]{:S(2)}, u32[]{:S(2)}) collective-permute-start(bf16[128,8,1024]{2,1,0:T(8,128)(2,1)} %refs_6_.1), channel_id=1, source_target_pairs={{3,7},{7,11},{11,15},{19,23},{23,27},{27,31}} | collective-permute-start | bytes 6291464 | tf_op jit(solution)/shard_map/ppermute | solution.py:27
  7.6 4.6 %collective-permute-start.1 = (bf16[128,1024]{1,0:T(8,128)(2,1)S(1)}, bf16[128,1024]{1,0:T(8,128)(2,1)S(1)}, u32[]{:S(2)}, u32[]{:S(2)}) collective-permute-start(bf16[128,1024]{1,0:T(8,128)(2,1)S(1)} %get-tuple-element.48), channel_id=1, source_target_pairs={{0,2},{1,3},{2,0},{3,1},{4,6},{5,7},{6,4},{7,5},{8,10},{9,11},{10,... | collective-permute-start | bytes 786440 | tf_op jit(solution)/shard_map/ppermute | solution.py:32
  12.6 1.5 %collective-permute-start.6 = (bf16[256,1024]{1,0:T(8,128)(2,1)}, bf16[256,1024]{1,0:T(8,128)(2,1)S(1)}, u32[]{:S(2)}, u32[]{:S(2)}) collective-permute-start(bf16[256,1024]{1,0:T(8,128)(2,1)} %get-tuple-element.56), channel_id=1, source_target_pairs={{0,2},{1,3},{2,0},{3,1},{4,6},{5,7},{6,4},{7,5},{8,10},{9,11},{10,... | collective-permute-start | bytes 1572872 | tf_op jit(solution)/shard_map/ppermute | solution.py:32
  14.1 9.9 %shard_map.69 = (f32[128,8,1024]{2,1,0:T(8,128)}, f32[8,128]{1,0:T(8,128)S(1)}) custom-call(f32[128,8,1024]{2,1,0:T(8,128)} %refs_5_.1, f32[128,8,1024]{2,1,0:T(8,128)} %refs_5_.1, bf16[128,1024]{1,0:T(8,128)(2,1)S(1)} %get-tuple-element.47.refs_0_), custom_call_target="tpu_custom_call" | custom-call | flops 10350000128 | bytes 1000 | tf_op jit(solution)/shard_map/pallas_call | solution.py:557
  25.7 1.3 collective-permute-start.3
  27.0 1.2 collective-permute-start.7
  29.1 2.7 %shard_map.71 = (bf16[512,1152]{1,0:T(8,128)(2,1)}, bf16[512,1152]{1,0:T(8,128)(2,1)}) custom-call(s32[1]{0:T(128)} %bitcast.here_ref, s32[16,6]{1,0:T(8,128)S(1)} %copy.12.cover_ref, s32[16,6]{1,0:T(8,128)S(1)} %copy.13.offset_ref, bf16[8,128,128]{2,1,0:T(8,128)(2,1)S(1)} %copy-done.1, bf16[528,1024]{1,0:T(8,128)(2,1)S(1)} %get-tuple-element.51.refs_0_.own_ref), custom_call_target="tpu_custom_call" | custom-call | flops 1840000000 | bytes 1000 | tf_op jit(solution)/shard_map/pallas_call | solution.py:433
  31.8 3.1 %collective-permute-done.6.refs_0_.refs_2_ = bf16[256,1024]{1,0:T(8,128)(2,1)S(1)} collective-permute-done((bf16[256,1024]{1,0:T(8,128)(2,1)}, bf16[256,1024]{1,0:T(8,128)(2,1)S(1)}, u32[]{:S(2)}, u32[]{:S(2)}) %collective-permute-start.6) | collective-permute-done | bytes 524320 | tf_op jit(solution)/shard_map/ppermute | solution.py:32
  34.9 1.3 copy-done.7
  36.2 2.0 %shard_map.72 = (bf16[128,1024]{1,0:T(8,128)(2,1)S(1)}, bf16[128,1024]{1,0:T(8,128)(2,1)S(1)}, bf16[128,1024]{1,0:T(8,128)(2,1)S(1)}, bf16[128,1024]{1,0:T(8,128)(2,1)S(1)}, bf16[128,1024]{1,0:T(8,128)(2,1)S(1)}) custom-call(s32[1]{0:T(128)} %bitcast.here_ref, bf16[128,8,1024]{2,1,0:T(8,128)(2,1)} %refs_6_.1, ...), custom_call_target="tpu_custom_call" | custom-call | flops 2300000000 | bytes 1000 | tf_op jit(solution)/shard_map/pallas_call | solution.py:207
  38.3 4.0 %collective-permute-start.4 = (bf16[144,1024]{1,0:T(8,128)(2,1)S(1)}, bf16[144,1024]{1,0:T(8,128)(2,1)S(1)}, u32[]{:S(2)}, u32[]{:S(2)}) collective-permute-start(bf16[144,1024]{1,0:T(8,128)(2,1)S(1)} %copy-done.4), channel_id=1, source_target_pairs={{0,4},{1,5},{2,6},{3,7},{4,8},{5,9},{6,10},{7,11},{8,12},{9,13},{1... | collective-permute-start | bytes 884744 | tf_op jit(solution)/shard_map/ppermute | solution.py:27
  42.7 1.4 collective-permute-start.9
  44.5 1.1 shard_map.73
  45.7 3.0 %collective-permute-done.4.low_ref.refs_4_ = bf16[144,1024]{1,0:T(8,128)(2,1)S(1)} collective-permute-done((bf16[144,1024]{1,0:T(8,128)(2,1)S(1)}, bf16[144,1024]{1,0:T(8,128)(2,1)S(1)}, u32[]{:S(2)}, u32[]{:S(2)}) %collective-permute-start.4) | collective-permute-done | bytes 294944 | tf_op jit(solution)/shard_map/ppermute | solution.py:27
  48.7 4.1 %collective-permute-start.12 = (bf16[128,1024]{1,0:T(8,128)(2,1)S(1)}, bf16[128,1024]{1,0:T(8,128)(2,1)S(1)}, u32[]{:S(2)}, u32[]{:S(2)}) collective-permute-start(bf16[128,1024]{1,0:T(8,128)(2,1)S(1)} %get-tuple-element.64), channel_id=1, source_target_pairs={{0,4},{1,5},{2,6},{3,7},{4,8},{5,9},{6,10},{7,11},{8,12},{9,13},{1... | collective-permute-start | bytes 786440 | tf_op jit(solution)/shard_map/ppermute | solution.py:27
  52.8 1.4 %collective-permute-start.15 = (bf16[512,1024]{1,0:T(8,128)(2,1)S(1)}, bf16[512,1024]{1,0:T(8,128)(2,1)S(1)}, u32[]{:S(2)}, u32[]{:S(2)}) collective-permute-start(bf16[512,1024]{1,0:T(8,128)(2,1)S(1)} %get-tuple-element.65.refs_0_.own_ref), channel_id=1, source_target_pairs={{4,0},{5,1},{6,2},{7,3},{8,4},{9,5},{10,6},{11,7},{12,8},{13,9},{1... | collective-permute-start | bytes 3145736 | tf_op jit(solution)/shard_map/ppermute | solution.py:27
  54.2 1.9 %shard_map.74 = (bf16[128,1024]{1,0:T(8,128)(2,1)S(1)}, bf16[128,1024]{1,0:T(8,128)(2,1)S(1)}, bf16[256,1024]{1,0:T(8,128)(2,1)S(1)}) custom-call(s32[1]{0:T(128)} %bitcast.here_ref, bf16[128,8,1024]{2,1,0:T(8,128)(2,1)} %refs_6_.1, bf16[128,8,1024]{2,1,0:T(8,128)(2,1)} %collective-permute-done.5.got_ref, bf16[512,1024]{1,0:T(8,128)(2,1)S(1)} %get-tuple-element.65.refs_0_.own_ref), custom_call_target="tpu_custom_call" | custom-call | flops 2300000000 | bytes 1000 | tf_op jit(solution)/shard_map/pallas_call | solution.py:207
  56.2 1.2 collective-permute-start.16
  57.4 1.2 collective-permute-start.17
  58.5 2.2 %shard_map.75 = (bf16[512,1024]{1,0:T(8,128)(2,1)S(1)}, bf16[128,1024]{1,0:T(8,128)(2,1)S(1)}, bf16[128,1024]{1,0:T(8,128)(2,1)S(1)}, bf16[256,1024]{1,0:T(8,128)(2,1)S(1)}) custom-call(s32[1]{0:T(128)} %bitcast.here_ref, bf16[512,1152]{1,0:T(8,128)(2,1)S(1)} %copy-done.8, bf16[528,1024]{1,0:T(8,128)(2,1)S(1)} %get-tuple-element.51.refs_0_.own_ref, ...), custom_call_target="tpu_custom_call" | custom-call | flops 3449999872 | bytes 1000 | tf_op jit(solution)/shard_map/pallas_call | solution.py:464
  60.7 4.3 %collective-permute-start.13 = (bf16[512,1024]{1,0:T(8,128)(2,1)S(1)}, bf16[512,1024]{1,0:T(8,128)(2,1)S(1)}, u32[]{:S(2)}, u32[]{:S(2)}) collective-permute-start(bf16[512,1024]{1,0:T(8,128)(2,1)S(1)} %get-tuple-element.67.refs_8_.own_ref.refs_0_), channel_id=1, source_target_pairs={{0,4},{1,5},{2,6},{3,7},{4,8},{5,9},{6,10},{7,11},{8,12},{9,13},{1... | collective-permute-start | bytes 3145736 | tf_op jit(solution)/shard_map/ppermute | solution.py:27
  65.1 2.5 %shard_map.76 = (bf16[128,8,1024]{2,1,0:T(8,128)(2,1)}, f32[128,8,1024]{2,1,0:T(8,128)}) custom-call(s32[1]{0:T(128)} %bitcast.here_ref, s32[16,6]{1,0:T(8,128)S(1)} %copy.12.cover_ref, s32[16,6]{1,0:T(8,128)S(1)} %copy.13.offset_ref, bf16[8,128,128]{2,1,0:T(8,128)(2,1)S(1)} %copy-done.1, ...), custom_call_target="tpu_custom_call", output_to_operand_aliasing={{1}: (10, {})} | custom-call | flops 3449999872 | bytes 1000 | tf_op jit(solution)/shard_map/pallas_call | solution.py:276
  67.6 3.3 %collective-permute-done.17.refs_2_ = bf16[256,1024]{1,0:T(8,128)(2,1)S(1)} collective-permute-done((bf16[256,1024]{1,0:T(8,128)(2,1)S(1)}, bf16[256,1024]{1,0:T(8,128)(2,1)S(1)}, u32[]{:S(2)}, u32[]{:S(2)}) %collective-permute-start.17) | collective-permute-done | bytes 524320 | tf_op jit(solution)/shard_map/ppermute | solution.py:32
  70.9 0.9 collective-permute-start.18
  71.8 1.3 collective-permute-start.14
  73.1 5.3 %collective-permute-done.15.high_ref = bf16[512,1024]{1,0:T(8,128)(2,1)S(1)} collective-permute-done((bf16[512,1024]{1,0:T(8,128)(2,1)S(1)}, bf16[512,1024]{1,0:T(8,128)(2,1)S(1)}, u32[]{:S(2)}, u32[]{:S(2)}) %collective-permute-start.15) | collective-permute-done | bytes 1048608 | tf_op jit(solution)/shard_map/ppermute | solution.py:27
  78.4 1.6 %copy-done.2 = bf16[128,8,1024]{2,1,0:T(8,128)(2,1)S(1)} copy-done((bf16[128,8,1024]{2,1,0:T(8,128)(2,1)S(1)}, bf16[128,8,1024]{2,1,0:T(8,128)(2,1)}, u32[]{:S(2)}) %copy-start.2) | copy-done | bytes 2097176
  80.0 2.1 %shard_map.77 = (bf16[512,1024]{1,0:T(8,128)(2,1)S(1)}, bf16[128,1024]{1,0:T(8,128)(2,1)S(1)}) custom-call(s32[1]{0:T(128)} %bitcast.here_ref, bf16[512,1152]{1,0:T(8,128)(2,1)S(1)} %copy-done.8, bf16[512,1024]{1,0:T(8,128)(2,1)S(1)} %get-tuple-element.65.refs_0_.own_ref, bf16[512,1024]{1,0:T(8,128)(2,1)S(1)} %collective-permute-done.15.high_ref, ...), custom_call_target="tpu_custom_call" | custom-call | flops 3449999872 | bytes 1000 | tf_op jit(solution)/shard_map/pallas_call | solution.py:464
  82.1 1.3 collective-permute-start.19
  84.1 4.5 %collective-permute-start.24 = (bf16[128,1024]{1,0:T(8,128)(2,1)S(1)}, bf16[128,1024]{1,0:T(8,128)(2,1)S(1)}, u32[]{:S(2)}, u32[]{:S(2)}) collective-permute-start(bf16[128,1024]{1,0:T(8,128)(2,1)S(1)} %get-tuple-element.82), channel_id=1, source_target_pairs={{0,1},{1,0},{2,3},{3,2},{4,5},{5,4},{6,7},{7,6},{8,9},{9,8},{10,11... | collective-permute-start | bytes 786440 | tf_op jit(solution)/shard_map/ppermute | solution.py:32
  88.5 4.3 %collective-permute-start.23 = (bf16[512,1024]{1,0:T(8,128)(2,1)S(1)}, bf16[512,1024]{1,0:T(8,128)(2,1)S(1)}, u32[]{:S(2)}, u32[]{:S(2)}) collective-permute-start(bf16[512,1024]{1,0:T(8,128)(2,1)S(1)} %get-tuple-element.75.refs_0_.own_ref), channel_id=1, source_target_pairs={{0,4},{1,5},{2,6},{3,7},{4,8},{5,9},{6,10},{7,11},{8,12},{9,13},{1... | collective-permute-start | bytes 3145736 | tf_op jit(solution)/shard_map/ppermute | solution.py:27
  92.9 2.1 %shard_map.78 = (bf16[256,1024]{1,0:T(8,128)(2,1)S(1)}, bf16[256,1024]{1,0:T(8,128)(2,1)S(1)}, bf16[256,1024]{1,0:T(8,128)(2,1)S(1)}, bf16[256,1024]{1,0:T(8,128)(2,1)S(1)}) custom-call(s32[1]{0:T(128)} %bitcast.here_ref, bf16[512,1152]{1,0:T(8,128)(2,1)S(1)} %copy-done.9, bf16[512,1024]{1,0:T(8,128)(2,1)S(1)} %get-tuple-element.67.refs_8_.own_ref.refs_0_, ...), custom_call_target="tpu_custom_call" | custom-call | flops 3449999872 | bytes 1000 | tf_op jit(solution)/shard_map/pallas_call | solution.py:496
  95.1 2.8 %collective-permute-start.26 = (bf16[128,1024]{1,0:T(8,128)(2,1)S(1)}, bf16[128,1024]{1,0:T(8,128)(2,1)S(1)}, u32[]{:S(2)}, u32[]{:S(2)}) collective-permute-start(bf16[128,1024]{1,0:T(8,128)(2,1)S(1)} %slice.7), channel_id=1, source_target_pairs={{0,1},{1,0},{2,3},{3,2},{4,5},{5,4},{6,7},{7,6},{8,9},{9,8},{10,11... | collective-permute-start | bytes 786440 | tf_op jit(solution)/shard_map/ppermute | solution.py:32
  97.9 1.2 collective-permute-done.26.refs_3_
  99.0 0.8 shard_map.79.refs_0_.own_ref
  101.0 0.9 collective-permute-start.21
  101.9 0.9 collective-permute-start.22
  102.8 12.5 %collective-permute-done.23.low_ref = bf16[512,1024]{1,0:T(8,128)(2,1)S(1)} collective-permute-done((bf16[512,1024]{1,0:T(8,128)(2,1)S(1)}, bf16[512,1024]{1,0:T(8,128)(2,1)S(1)}, u32[]{:S(2)}, u32[]{:S(2)}) %collective-permute-start.23) | collective-permute-done | bytes 1048608 | tf_op jit(solution)/shard_map/ppermute | solution.py:27
  115.4 2.0 %shard_map.80 = (bf16[128,1024]{1,0:T(8,128)(2,1)S(1)}, bf16[128,1024]{1,0:T(8,128)(2,1)S(1)}, bf16[128,1024]{1,0:T(8,128)(2,1)S(1)}, bf16[128,1024]{1,0:T(8,128)(2,1)S(1)}) custom-call(s32[1]{0:T(128)} %bitcast.here_ref, bf16[512,1152]{1,0:T(8,128)(2,1)S(1)} %copy-done.9, bf16[512,1024]{1,0:T(8,128)(2,1)S(1)} %get-tuple-element.75.refs_0_.own_ref, ...), custom_call_target="tpu_custom_call" | custom-call | flops 3449999872 | bytes 1000 | tf_op jit(solution)/shard_map/pallas_call | solution.py:496
  117.3 0.8 collective-permute-start.27
  118.5 1.4 collective-permute-start.29
  119.9 6.6 %collective-permute-done.22.refs_3_ = bf16[256,1024]{1,0:T(8,128)(2,1)S(1)} collective-permute-done((bf16[256,1024]{1,0:T(8,128)(2,1)S(1)}, bf16[256,1024]{1,0:T(8,128)(2,1)S(1)}, u32[]{:S(2)}, u32[]{:S(2)}) %collective-permute-start.22) | collective-permute-done | bytes 524320 | tf_op jit(solution)/shard_map/ppermute | solution.py:32
  126.5 2.9 %shard_map.81.tv_ref = f32[128,8,1024]{2,1,0:T(8,128)} custom-call(s32[1]{0:T(128)} %bitcast.here_ref, f32[128,8,1024]{2,1,0:T(8,128)} %get-tuple-element.68.tv_ref, bf16[256,1024]{1,0:T(8,128)(2,1)S(1)} %get-tuple-element.77.refs_4_.refs_0_, bf16[256,1024]{1,0:T(8,128)(2,1)S(1)} %collective-permute-done.20.refs_1_, ...), custom_call_target="tpu_custom_call", output_to_operand_aliasing={{}: (1, {})} | custom-call | flops 2990000128 | bytes 1000 | tf_op jit(solution)/shard_map/pallas_call | solution.py:385
  129.4 2.6 %shard_map.82.refs_4_ = bf16[128,8,1024]{2,1,0:T(8,128)(2,1)} custom-call(s32[1]{0:T(128)} %bitcast.here_ref, bf16[128,8,512]{2,1,0:T(8,128)(2,1)S(1)} %shard_map.79.refs_0_.own_ref, bf16[128,8,512]{2,1,0:T(8,128)(2,1)S(1)} %collective-permute-done.30.above_ref, bf16[256,1024]{1,0:T(8,128)(2,1)S(1)} %get-tuple-element.77.refs_4_.refs_0_, ...), custom_call_target="tpu_custom_call" | custom-call | flops 2990000128 | bytes 1000 | tf_op jit(solution)/shard_map/pallas_call | solution.py:363
  132.0 5.1 %collective-permute-done.29.refs_3_ = bf16[128,1024]{1,0:T(8,128)(2,1)S(1)} collective-permute-done((bf16[128,1024]{1,0:T(8,128)(2,1)S(1)}, bf16[128,1024]{1,0:T(8,128)(2,1)S(1)}, u32[]{:S(2)}, u32[]{:S(2)}) %collective-permute-start.29) | collective-permute-done | bytes 262176 | tf_op jit(solution)/shard_map/ppermute | solution.py:32
  137.2 1.6 %copy-done = bf16[128,8,1024]{2,1,0:T(8,128)(2,1)S(1)} copy-done((bf16[128,8,1024]{2,1,0:T(8,128)(2,1)S(1)}, bf16[128,8,1024]{2,1,0:T(8,128)(2,1)}, u32[]{:S(2)}) %copy-start) | copy-done | bytes 2097176
  138.8 2.9 %shard_map.83 = f32[128,8,1024]{2,1,0:T(8,128)} custom-call(s32[1]{0:T(128)} %bitcast.here_ref, f32[128,8,1024]{2,1,0:T(8,128)} %shard_map.81.tv_ref, bf16[128,1024]{1,0:T(8,128)(2,1)S(1)} %get-tuple-element.86.refs_4_.refs_0_, bf16[128,1024]{1,0:T(8,128)(2,1)S(1)} %collective-permute-done.27.refs_1_, ...), custom_call_target="tpu_custom_call", output_to_operand_aliasing={{}: (1, {})} | custom-call | flops 2990000128 | bytes 1000 | tf_op jit(solution)/shard_map/pallas_call | solution.py:385
  (56 shorter events, 6.9 us)
Async XLA Ops:
  4.9 0.7 copy-start.5
  5.6 29.3 %collective-permute-start.5 = (bf16[128,8,1024]{2,1,0:T(8,128)(2,1)}, bf16[128,8,1024]{2,1,0:T(8,128)(2,1)}, u32[]{:S(2)}, u32[]{:S(2)}) collective-permute-start(bf16[128,8,1024]{2,1,0:T(8,128)(2,1)} %refs_6_.1), channel_id=1, source_target_pairs={{3,7},{7,11},{11,15},{19,23},{23,27},{27,31}} | collective-permute-start | bytes 6291464 | tf_op jit(solution)/shard_map/ppermute | solution.py:27
  7.6 16.3 %collective-permute-start.1 = (bf16[128,1024]{1,0:T(8,128)(2,1)S(1)}, bf16[128,1024]{1,0:T(8,128)(2,1)S(1)}, u32[]{:S(2)}, u32[]{:S(2)}) collective-permute-start(bf16[128,1024]{1,0:T(8,128)(2,1)S(1)} %get-tuple-element.48), channel_id=1, source_target_pairs={{0,2},{1,3},{2,0},{3,1},{4,6},{5,7},{6,4},{7,5},{8,10},{9,11},{10,... | collective-permute-start | bytes 786440 | tf_op jit(solution)/shard_map/ppermute | solution.py:32
  12.2 11.7 %collective-permute-start = (bf16[144,1024]{1,0:T(8,128)(2,1)S(1)}, bf16[144,1024]{1,0:T(8,128)(2,1)S(1)}, u32[]{:S(2)}, u32[]{:S(2)}) collective-permute-start(bf16[144,1024]{1,0:T(8,128)(2,1)S(1)} %get-tuple-element.46), channel_id=1, source_target_pairs={{0,1},{1,0},{2,3},{3,2},{4,5},{5,4},{6,7},{7,6},{8,9},{9,8},{10,11... | collective-permute-start | bytes 884744 | tf_op jit(solution)/shard_map/ppermute | solution.py:32
  12.2 12.5 %collective-permute-start.2 = (bf16[144,1024]{1,0:T(8,128)(2,1)S(1)}, bf16[144,1024]{1,0:T(8,128)(2,1)S(1)}, u32[]{:S(2)}, u32[]{:S(2)}) collective-permute-start(bf16[144,1024]{1,0:T(8,128)(2,1)S(1)} %get-tuple-element.49), channel_id=1, source_target_pairs={{0,3},{1,2},{2,1},{3,0},{4,7},{5,6},{6,5},{7,4},{8,11},{9,10},{10,... | collective-permute-start | bytes 884744 | tf_op jit(solution)/shard_map/ppermute | solution.py:32
  12.6 22.3 %collective-permute-start.6 = (bf16[256,1024]{1,0:T(8,128)(2,1)}, bf16[256,1024]{1,0:T(8,128)(2,1)S(1)}, u32[]{:S(2)}, u32[]{:S(2)}) collective-permute-start(bf16[256,1024]{1,0:T(8,128)(2,1)} %get-tuple-element.56), channel_id=1, source_target_pairs={{0,2},{1,3},{2,0},{3,1},{4,6},{5,7},{6,4},{7,5},{8,10},{9,11},{10,... | collective-permute-start | bytes 1572872 | tf_op jit(solution)/shard_map/ppermute | solution.py:32
  24.7 3.6 %copy-start.10 = (s32[16,6]{0,1:T(8,128)S(1)}, s32[16,6]{0,1:T(8,128)}, u32[]{:S(2)}) copy-start(s32[16,6]{0,1:T(8,128)} %param.8) | copy-start | bytes 1156
  24.7 4.4 %copy-start.1 = (bf16[8,128,128]{2,1,0:T(8,128)(2,1)S(1)}, bf16[8,128,128]{2,1,0:T(8,128)(2,1)}, u32[]{:S(2)}) copy-start(bf16[8,128,128]{2,1,0:T(8,128)(2,1)} %refs_0_.1) | copy-start | bytes 786436
  25.0 0.7 copy-start.3
  25.7 27.0 %collective-permute-start.3 = (bf16[528,1024]{1,0:T(8,128)(2,1)S(1)}, bf16[528,1024]{1,0:T(8,128)(2,1)S(1)}, u32[]{:S(2)}, u32[]{:S(2)}) collective-permute-start(bf16[528,1024]{1,0:T(8,128)(2,1)S(1)} %get-tuple-element.51.refs_0_.own_ref), channel_id=1, source_target_pairs={{4,0},{5,1},{6,2},{7,3},{8,4},{9,5},{10,6},{11,7},{12,8},{13,9},{1... | collective-permute-start | bytes 3244040 | tf_op jit(solution)/shard_map/ppermute | solution.py:27
  27.0 4.7 %collective-permute-start.7 = (bf16[128,1024]{1,0:T(8,128)(2,1)}, bf16[128,1024]{1,0:T(8,128)(2,1)}, u32[]{:S(2)}, u32[]{:S(2)}) collective-permute-start(bf16[128,1024]{1,0:T(8,128)(2,1)} %get-tuple-element.57), channel_id=1, source_target_pairs={{0,1},{1,0},{2,3},{3,2},{4,5},{5,4},{6,7},{7,6},{8,9},{9,8},{10,11... | collective-permute-start | bytes 786440 | tf_op jit(solution)/shard_map/ppermute | solution.py:32
  34.9 1.3 copy-start.7
  36.2 2.1 %copy-start.4 = (bf16[144,1024]{1,0:T(8,128)(2,1)S(1)}, bf16[144,1024]{1,0:T(8,128)(2,1)}, u32[]{:S(2)}) copy-start(bf16[144,1024]{1,0:T(8,128)(2,1)} %copy-done.3) | copy-start | bytes 884740
  36.2 8.3 %copy-start.6 = (bf16[128,1024]{1,0:T(8,128)(2,1)S(1)}, bf16[128,1024]{1,0:T(8,128)(2,1)}, u32[]{:S(2)}) copy-start(bf16[128,1024]{1,0:T(8,128)(2,1)} %copy-done.5) | copy-start | bytes 786436
  38.2 5.9 %collective-permute-start.11 = (bf16[128,1024]{1,0:T(8,128)(2,1)S(1)}, bf16[128,1024]{1,0:T(8,128)(2,1)S(1)}, u32[]{:S(2)}, u32[]{:S(2)}) collective-permute-start(bf16[128,1024]{1,0:T(8,128)(2,1)S(1)} %get-tuple-element.63), channel_id=1, source_target_pairs={{0,1},{1,0},{2,3},{3,2},{4,5},{5,4},{6,7},{7,6},{8,9},{9,8},{10,11... | collective-permute-start | bytes 786440 | tf_op jit(solution)/shard_map/ppermute | solution.py:32
  38.3 10.4 %collective-permute-start.4 = (bf16[144,1024]{1,0:T(8,128)(2,1)S(1)}, bf16[144,1024]{1,0:T(8,128)(2,1)S(1)}, u32[]{:S(2)}, u32[]{:S(2)}) collective-permute-start(bf16[144,1024]{1,0:T(8,128)(2,1)S(1)} %copy-done.4), channel_id=1, source_target_pairs={{0,4},{1,5},{2,6},{3,7},{4,8},{5,9},{6,10},{7,11},{8,12},{9,13},{1... | collective-permute-start | bytes 884744 | tf_op jit(solution)/shard_map/ppermute | solution.py:27
  42.3 13.9 %collective-permute-start.8 = (bf16[128,1024]{1,0:T(8,128)(2,1)S(1)}, bf16[128,1024]{1,0:T(8,128)(2,1)S(1)}, u32[]{:S(2)}, u32[]{:S(2)}) collective-permute-start(bf16[128,1024]{1,0:T(8,128)(2,1)S(1)} %get-tuple-element.59), channel_id=1, source_target_pairs={{0,1},{1,0},{2,3},{3,2},{4,5},{5,4},{6,7},{7,6},{8,9},{9,8},{10,11... | collective-permute-start | bytes 786440 | tf_op jit(solution)/shard_map/ppermute | solution.py:32
  42.7 14.7 %collective-permute-start.9 = (bf16[128,1024]{1,0:T(8,128)(2,1)S(1)}, bf16[128,1024]{1,0:T(8,128)(2,1)S(1)}, u32[]{:S(2)}, u32[]{:S(2)}) collective-permute-start(bf16[128,1024]{1,0:T(8,128)(2,1)S(1)} %get-tuple-element.60), channel_id=1, source_target_pairs={{0,2},{1,3},{2,0},{3,1},{4,6},{5,7},{6,4},{7,5},{8,10},{9,11},{10,... | collective-permute-start | bytes 786440 | tf_op jit(solution)/shard_map/ppermute | solution.py:32
  44.1 14.4 %collective-permute-start.10 = (bf16[128,1024]{1,0:T(8,128)(2,1)S(1)}, bf16[128,1024]{1,0:T(8,128)(2,1)S(1)}, u32[]{:S(2)}, u32[]{:S(2)}) collective-permute-start(bf16[128,1024]{1,0:T(8,128)(2,1)S(1)} %get-tuple-element.61), channel_id=1, source_target_pairs={{0,3},{1,2},{2,1},{3,0},{4,7},{5,6},{6,5},{7,4},{8,11},{9,10},{10,... | collective-permute-start | bytes 786440 | tf_op jit(solution)/shard_map/ppermute | solution.py:32
  48.7 9.9 %collective-permute-start.12 = (bf16[128,1024]{1,0:T(8,128)(2,1)S(1)}, bf16[128,1024]{1,0:T(8,128)(2,1)S(1)}, u32[]{:S(2)}, u32[]{:S(2)}) collective-permute-start(bf16[128,1024]{1,0:T(8,128)(2,1)S(1)} %get-tuple-element.64), channel_id=1, source_target_pairs={{0,4},{1,5},{2,6},{3,7},{4,8},{5,9},{6,10},{7,11},{8,12},{9,13},{1... | collective-permute-start | bytes 786440 | tf_op jit(solution)/shard_map/ppermute | solution.py:27
  52.8 5.7 %copy-start.8 = (bf16[512,1152]{1,0:T(8,128)(2,1)S(1)}, bf16[512,1152]{1,0:T(8,128)(2,1)}, u32[]{:S(2)}) copy-start(bf16[512,1152]{1,0:T(8,128)(2,1)} %get-tuple-element.54.refs_1_.band_ref) | copy-start | bytes 3538948
  52.8 25.6 %collective-permute-start.15 = (bf16[512,1024]{1,0:T(8,128)(2,1)S(1)}, bf16[512,1024]{1,0:T(8,128)(2,1)S(1)}, u32[]{:S(2)}, u32[]{:S(2)}) collective-permute-start(bf16[512,1024]{1,0:T(8,128)(2,1)S(1)} %get-tuple-element.65.refs_0_.own_ref), channel_id=1, source_target_pairs={{4,0},{5,1},{6,2},{7,3},{8,4},{9,5},{10,6},{11,7},{12,8},{13,9},{1... | collective-permute-start | bytes 3145736 | tf_op jit(solution)/shard_map/ppermute | solution.py:27
  56.2 16.9 %collective-permute-start.16 = (bf16[128,1024]{1,0:T(8,128)(2,1)S(1)}, bf16[128,1024]{1,0:T(8,128)(2,1)S(1)}, u32[]{:S(2)}, u32[]{:S(2)}) collective-permute-start(bf16[128,1024]{1,0:T(8,128)(2,1)S(1)} %get-tuple-element.71), channel_id=1, source_target_pairs={{0,1},{1,0},{2,3},{3,2},{4,5},{5,4},{6,7},{7,6},{8,9},{9,8},{10,11... | collective-permute-start | bytes 786440 | tf_op jit(solution)/shard_map/ppermute | solution.py:32
  57.4 13.5 %collective-permute-start.17 = (bf16[256,1024]{1,0:T(8,128)(2,1)S(1)}, bf16[256,1024]{1,0:T(8,128)(2,1)S(1)}, u32[]{:S(2)}, u32[]{:S(2)}) collective-permute-start(bf16[256,1024]{1,0:T(8,128)(2,1)S(1)} %get-tuple-element.72), channel_id=1, source_target_pairs={{0,2},{1,3},{2,0},{3,1},{4,6},{5,7},{6,4},{7,5},{8,10},{9,11},{10,... | collective-permute-start | bytes 1572872 | tf_op jit(solution)/shard_map/ppermute | solution.py:32
  60.7 32.1 %collective-permute-start.13 = (bf16[512,1024]{1,0:T(8,128)(2,1)S(1)}, bf16[512,1024]{1,0:T(8,128)(2,1)S(1)}, u32[]{:S(2)}, u32[]{:S(2)}) collective-permute-start(bf16[512,1024]{1,0:T(8,128)(2,1)S(1)} %get-tuple-element.67.refs_8_.own_ref.refs_0_), channel_id=1, source_target_pairs={{0,4},{1,5},{2,6},{3,7},{4,8},{5,9},{6,10},{7,11},{8,12},{9,13},{1... | collective-permute-start | bytes 3145736 | tf_op jit(solution)/shard_map/ppermute | solution.py:27
  70.9 2.2 %collective-permute-start.18 = (bf16[128,1024]{1,0:T(8,128)(2,1)S(1)}, bf16[128,1024]{1,0:T(8,128)(2,1)S(1)}, u32[]{:S(2)}, u32[]{:S(2)}) collective-permute-start(bf16[128,1024]{1,0:T(8,128)(2,1)S(1)} %slice.6), channel_id=1, source_target_pairs={{0,1},{1,0},{2,3},{3,2},{4,5},{5,4},{6,7},{7,6},{8,9},{9,8},{10,11... | collective-permute-start | bytes 786440 | tf_op jit(solution)/shard_map/ppermute | solution.py:32
  71.8 16.7 %collective-permute-start.14 = (bf16[128,1024]{1,0:T(8,128)(2,1)S(1)}, bf16[128,1024]{1,0:T(8,128)(2,1)S(1)}, u32[]{:S(2)}, u32[]{:S(2)}) collective-permute-start(bf16[128,1024]{1,0:T(8,128)(2,1)S(1)} %get-tuple-element.70), channel_id=1, source_target_pairs={{4,0},{5,1},{6,2},{7,3},{8,4},{9,5},{10,6},{11,7},{12,8},{13,9},{1... | collective-permute-start | bytes 786440 | tf_op jit(solution)/shard_map/ppermute | solution.py:27
  78.4 1.6 %copy-start.2 = (bf16[128,8,1024]{2,1,0:T(8,128)(2,1)S(1)}, bf16[128,8,1024]{2,1,0:T(8,128)(2,1)}, u32[]{:S(2)}) copy-start(bf16[128,8,1024]{2,1,0:T(8,128)(2,1)} %get-tuple-element.73.refs_4_.refs_5_) | copy-start | bytes 6291460
  80.0 12.9 %copy-start.9 = (bf16[512,1152]{1,0:T(8,128)(2,1)S(1)}, bf16[512,1152]{1,0:T(8,128)(2,1)}, u32[]{:S(2)}) copy-start(bf16[512,1152]{1,0:T(8,128)(2,1)} %get-tuple-element.69.band_ref) | copy-start | bytes 3538948
  82.1 10.8 %collective-permute-start.19 = (bf16[128,1024]{1,0:T(8,128)(2,1)S(1)}, bf16[128,1024]{1,0:T(8,128)(2,1)S(1)}, u32[]{:S(2)}, u32[]{:S(2)}) collective-permute-start(bf16[128,1024]{1,0:T(8,128)(2,1)S(1)} %get-tuple-element.76), channel_id=1, source_target_pairs={{4,0},{5,1},{6,2},{7,3},{8,4},{9,5},{10,6},{11,7},{12,8},{13,9},{1... | collective-permute-start | bytes 786440 | tf_op jit(solution)/shard_map/ppermute | solution.py:27
  83.4 11.7 %collective-permute-start.25 = (bf16[256,1024]{1,0:T(8,128)(2,1)S(1)}, bf16[256,1024]{1,0:T(8,128)(2,1)S(1)}, u32[]{:S(2)}, u32[]{:S(2)}) collective-permute-start(bf16[256,1024]{1,0:T(8,128)(2,1)S(1)} %get-tuple-element.84), channel_id=1, source_target_pairs={{0,2},{1,3},{2,0},{3,1},{4,6},{5,7},{6,4},{7,5},{8,10},{9,11},{10,... | collective-permute-start | bytes 1572872 | tf_op jit(solution)/shard_map/ppermute | solution.py:32
  84.1 13.8 %collective-permute-start.24 = (bf16[128,1024]{1,0:T(8,128)(2,1)S(1)}, bf16[128,1024]{1,0:T(8,128)(2,1)S(1)}, u32[]{:S(2)}, u32[]{:S(2)}) collective-permute-start(bf16[128,1024]{1,0:T(8,128)(2,1)S(1)} %get-tuple-element.82), channel_id=1, source_target_pairs={{0,1},{1,0},{2,3},{3,2},{4,5},{5,4},{6,7},{7,6},{8,9},{9,8},{10,11... | collective-permute-start | bytes 786440 | tf_op jit(solution)/shard_map/ppermute | solution.py:32
  88.5 26.8 %collective-permute-start.23 = (bf16[512,1024]{1,0:T(8,128)(2,1)S(1)}, bf16[512,1024]{1,0:T(8,128)(2,1)S(1)}, u32[]{:S(2)}, u32[]{:S(2)}) collective-permute-start(bf16[512,1024]{1,0:T(8,128)(2,1)S(1)} %get-tuple-element.75.refs_0_.own_ref), channel_id=1, source_target_pairs={{0,4},{1,5},{2,6},{3,7},{4,8},{5,9},{6,10},{7,11},{8,12},{9,13},{1... | collective-permute-start | bytes 3145736 | tf_op jit(solution)/shard_map/ppermute | solution.py:27
  95.1 3.9 %collective-permute-start.26 = (bf16[128,1024]{1,0:T(8,128)(2,1)S(1)}, bf16[128,1024]{1,0:T(8,128)(2,1)S(1)}, u32[]{:S(2)}, u32[]{:S(2)}) collective-permute-start(bf16[128,1024]{1,0:T(8,128)(2,1)S(1)} %slice.7), channel_id=1, source_target_pairs={{0,1},{1,0},{2,3},{3,2},{4,5},{5,4},{6,7},{7,6},{8,9},{9,8},{10,11... | collective-permute-start | bytes 786440 | tf_op jit(solution)/shard_map/ppermute | solution.py:32
  99.9 29.5 %collective-permute-start.30 = (bf16[128,8,512]{2,1,0:T(8,128)(2,1)S(1)}, bf16[128,8,512]{2,1,0:T(8,128)(2,1)S(1)}, u32[]{:S(2)}, u32[]{:S(2)}) collective-permute-start(bf16[128,8,512]{2,1,0:T(8,128)(2,1)S(1)} %shard_map.79.refs_0_.own_ref), channel_id=1, source_target_pairs={{7,3},{11,7},{15,11},{23,19},{27,23},{31,27}} | collective-permute-start | bytes 3145736 | tf_op jit(solution)/shard_map/ppermute | solution.py:27
  100.6 17.6 %collective-permute-start.20 = (bf16[256,1024]{1,0:T(8,128)(2,1)S(1)}, bf16[256,1024]{1,0:T(8,128)(2,1)S(1)}, u32[]{:S(2)}, u32[]{:S(2)}) collective-permute-start(bf16[256,1024]{1,0:T(8,128)(2,1)S(1)} %get-tuple-element.78), channel_id=1, source_target_pairs={{0,1},{1,0},{2,3},{3,2},{4,5},{5,4},{6,7},{7,6},{8,9},{9,8},{10,11... | collective-permute-start | bytes 1572872 | tf_op jit(solution)/shard_map/ppermute | solution.py:32
  101.0 17.5 %collective-permute-start.21 = (bf16[256,1024]{1,0:T(8,128)(2,1)S(1)}, bf16[256,1024]{1,0:T(8,128)(2,1)S(1)}, u32[]{:S(2)}, u32[]{:S(2)}) collective-permute-start(bf16[256,1024]{1,0:T(8,128)(2,1)S(1)} %get-tuple-element.79), channel_id=1, source_target_pairs={{0,2},{1,3},{2,0},{3,1},{4,6},{5,7},{6,4},{7,5},{8,10},{9,11},{10,... | collective-permute-start | bytes 1572872 | tf_op jit(solution)/shard_map/ppermute | solution.py:32
  101.9 24.5 %collective-permute-start.22 = (bf16[256,1024]{1,0:T(8,128)(2,1)S(1)}, bf16[256,1024]{1,0:T(8,128)(2,1)S(1)}, u32[]{:S(2)}, u32[]{:S(2)}) collective-permute-start(bf16[256,1024]{1,0:T(8,128)(2,1)S(1)} %get-tuple-element.80), channel_id=1, source_target_pairs={{0,3},{1,2},{2,1},{3,0},{4,7},{5,6},{6,5},{7,4},{8,11},{9,10},{10,... | collective-permute-start | bytes 1572872 | tf_op jit(solution)/shard_map/ppermute | solution.py:32
  117.3 14.7 %collective-permute-start.27 = (bf16[128,1024]{1,0:T(8,128)(2,1)S(1)}, bf16[128,1024]{1,0:T(8,128)(2,1)S(1)}, u32[]{:S(2)}, u32[]{:S(2)}) collective-permute-start(bf16[128,1024]{1,0:T(8,128)(2,1)S(1)} %get-tuple-element.87), channel_id=1, source_target_pairs={{0,1},{1,0},{2,3},{3,2},{4,5},{5,4},{6,7},{7,6},{8,9},{9,8},{10,11... | collective-permute-start | bytes 786440 | tf_op jit(solution)/shard_map/ppermute | solution.py:32
  118.2 13.9 %collective-permute-start.28 = (bf16[128,1024]{1,0:T(8,128)(2,1)S(1)}, bf16[128,1024]{1,0:T(8,128)(2,1)S(1)}, u32[]{:S(2)}, u32[]{:S(2)}) collective-permute-start(bf16[128,1024]{1,0:T(8,128)(2,1)S(1)} %get-tuple-element.88), channel_id=1, source_target_pairs={{0,2},{1,3},{2,0},{3,1},{4,6},{5,7},{6,4},{7,5},{8,10},{9,11},{10,... | collective-permute-start | bytes 786440 | tf_op jit(solution)/shard_map/ppermute | solution.py:32
  118.5 18.7 %collective-permute-start.29 = (bf16[128,1024]{1,0:T(8,128)(2,1)S(1)}, bf16[128,1024]{1,0:T(8,128)(2,1)S(1)}, u32[]{:S(2)}, u32[]{:S(2)}) collective-permute-start(bf16[128,1024]{1,0:T(8,128)(2,1)S(1)} %get-tuple-element.89), channel_id=1, source_target_pairs={{0,3},{1,2},{2,1},{3,0},{4,7},{5,6},{6,5},{7,4},{8,11},{9,10},{10,... | collective-permute-start | bytes 786440 | tf_op jit(solution)/shard_map/ppermute | solution.py:32
  137.2 1.6 %copy-start = (bf16[128,8,1024]{2,1,0:T(8,128)(2,1)S(1)}, bf16[128,8,1024]{2,1,0:T(8,128)(2,1)}, u32[]{:S(2)}) copy-start(bf16[128,8,1024]{2,1,0:T(8,128)(2,1)} %shard_map.82.refs_4_) | copy-start | bytes 6291460

commit v9 on v8

--- a/solution.py
+++ b/solution.py
@@ -81,61 +81,43 @@
     return chunk * count, count
 
 
-CAST_GROUPS = ((0, (0,)), (0, (1,)), (0, (2,)), (0, (3,)), (1, (0,)), (1, (1,)), (1, (2, 3)))
-
-
-def cast_kernel(count, here_ref, *refs):
+def cast_kernel(groups, ends, here_ref, *refs):
     parts = TILE // LANES
-    vol_refs, (top_ref, end_ref), block_refs = refs[:parts], refs[parts : parts + 2], refs[parts + 2 :]
-    step = pl.program_id(0)
+    vol_refs, end_refs, out_refs = refs[:parts], refs[parts : parts + ends], refs[-len(groups) :]
     rows = ROWS * G
     depth = vol_refs[0].shape[0] // rows
     place = lax.rem(here_ref[0], G)
-
-    for c in range(CHUNKS):
-
-        @pl.when(step // count == c)
-        def _():
-            for j, vol_ref in enumerate(vol_refs):
-                for (chunk, group), out_ref in zip(CAST_GROUPS, block_refs):
-                    if chunk != c:
-                        continue
-                    for n, m in enumerate(group):
-                        for start, row in rows_of(place, m):
-                            at = pl.ds(start + j * LANES, LANES)
-                            block = vol_ref[pl.ds(row, depth, stride=rows), :].astype(BF16)
-                            out_ref[n * depth : (n + 1) * depth, at] = block
-            if c == 0:
-                both = jnp.concatenate([top_ref[...], end_ref[...]], axis=0).astype(BF16)
-                for (chunk, group), out_ref in zip(CAST_GROUPS, block_refs):
-                    if chunk == 0 and group[0] % 2:
-                        out_ref[depth:, :] = both
-
-
-def cast_rows(here, volume):
+    for j, vol_ref in enumerate(vol_refs):
+        for group, out_ref in zip(groups, out_refs):
+            for n, m in enumerate(group):
+                for start, row in rows_of(place, m):
+                    at = pl.ds(start + j * LANES, LANES)
+                    out_ref[n * depth : (n + 1) * depth, at] = vol_ref[pl.ds(row, depth, stride=rows), :].astype(BF16)
+    if ends:
+        both = jnp.concatenate([ref[...] for ref in end_refs], axis=0).astype(BF16)
+        for group, out_ref in zip(groups, out_refs):
+            if group[0] % 2:
+                out_ref[depth:, :] = both
+
+
+def cast_rows(here, volume, chunk, groups, ends, *tokens):
     depth, rows, cols = volume.shape
     flat = far(volume.reshape(depth * rows, cols))
-    _, count = chunk_tiles(0, cols)
+    first, count = chunk_tiles(chunk, cols)
     parts, width = TILE // LANES, ROWS * TILE
-
-    def step_of(chunk):
-        return lambda i: jnp.clip(i - chunk * count, 0, count - 1)
-
-    shapes = [(len(g) * depth + (2 * rows if c == 0 and g[0] % 2 else 0), cols) for c, g in CAST_GROUPS]
-    out_specs = [
-        pl.BlockSpec((shape[0], width), lambda i, at=step_of(c): (0, at(i))) for (c, _), shape in zip(CAST_GROUPS, shapes)
-    ]
-    in_specs = [SMEM]
-    in_specs += [pl.BlockSpec((depth * rows, LANES), lambda i, j=j: (0, i * parts + j)) for j in range(parts)]
-    in_specs += [pl.BlockSpec((rows, width), lambda i, z=z, at=step_of(0): (z, at(i))) for z in (0, depth - 1)]
-    return call(
-        functools.partial(cast_kernel, count),
-        4,
-        grid=(CHUNKS * count,),
-        in_specs=in_specs,
-        out_specs=out_specs,
-        results=[value(shape, BF16) for shape in shapes],
-    )(here, *[flat] * parts, flat, flat)
+    shapes = [(len(group) * depth + (2 * rows if ends and group[0] % 2 else 0), cols) for group in groups]
+    edges = [pl.BlockSpec((rows, width), lambda i, z=z: (z, i)) for z in (0, depth - 1)] if ends else []
+    return call(
+        functools.partial(cast_kernel, groups, len(edges)),
+        2,
+        grid=(count,),
+        in_specs=[SMEM]
+        + [pl.BlockSpec((depth * rows, LANES), lambda i, j=j: (0, (first + i) * parts + j)) for j in range(parts)]
+        + edges
+        + [ANY] * len(tokens),
+        out_specs=[across(shape, width) for shape in shapes],
+        results=[(pltpu.HBM if group[0] == 0 else value)(shape, BF16) for group, shape in zip(groups, shapes)],
+    )(here, *[flat] * (parts + len(edges)), *tokens)
 
 
 def last_block(here_ref, blocks):
@@ -168,7 +150,7 @@
         grid=(cols // tile,),
         in_specs=[SMEM] + specs + [ANY] * len(tokens),
         out_specs=[across(shape, tile) for shape in shapes],
-        results=[value(shape, BF16) for shape in shapes],
+        results=[pltpu.HBM(shape, BF16) for shape in shapes],
     )(here, *arrays_of(pieces), *tokens)
 
 
@@ -318,7 +300,7 @@
     _, count = chunk_tiles(0, cols)
     return call(
         join_kernel,
-        1.5,
+        0,
         grid=(count,),
         in_specs=[SMEM] + piece_specs(pieces, depth, ROWS * TILE) + [ANY] * len(tokens),
         out_specs=pl.BlockSpec((depth, rows, TILE), lambda i: (0, 0, i)),
@@ -327,48 +309,42 @@
     )(here, *arrays_of(pieces), *tokens)
 
 
-def settle_kernel(slabs, count, here_ref, own_ref, above_ref, *refs):
-    in_refs, (base_ref, out_ref, wide) = refs[:G], refs[-3:]
+def settle_kernel(slabs, count, here_ref, *refs):
+    in_refs, (base_ref, out_ref) = refs[: 2 * CHUNKS], refs[-2:]
     step = pl.program_id(0)
     cols = out_ref.shape[2]
-    place = lax.rem(here_ref[0], G)
     last = here_ref[0] == slabs - 1
+    above = lax.rem(here_ref[0], G) == G - 1
 
     @pl.when(last)
     def _():
         pltpu.sync_copy(base_ref.at[:, :, pl.ds(pl.multiple_of(step * cols, cols), cols)], out_ref)
 
-    @pl.when(jnp.logical_not(last) & (step < count) & (place == G - 1))
-    def _():
-        out_ref[...] = above_ref[...]
-
-    @pl.when(jnp.logical_not(last) & (step < count) & (place != G - 1))
-    def _():
-        out_ref[...] = own_ref[...]
-
-    @pl.when(jnp.logical_not(last) & (step >= count))
-    def _():
-        for j in range(cols // LANES):
-            out_ref[:, :, j * LANES : (j + 1) * LANES] = natural(place, in_refs, wide, j).astype(BF16)
-
-
-def settle(here, slabs, own, above, pieces, base, *tokens):
+    for c in range(CHUNKS):
+        for n in range(2):
+
+            @pl.when(jnp.logical_not(last) & (step // count == c) & (above == (n == 1)))
+            def _():
+                out_ref[...] = in_refs[c * 2 + n][...]
+
+
+def settle(here, slabs, own_above, base, *tokens):
     depth, rows, cols = base.shape
     _, count = chunk_tiles(0, cols)
     block = (depth, rows, TILE)
-    early = pl.BlockSpec(block, lambda i: (0, 0, jnp.minimum(i, count - 1)))
-    late = [
-        pl.BlockSpec((depth, ROWS * TILE), lambda i, at=at: (at, jnp.maximum(i - count, 0))) for _, at in pieces
+    specs = [
+        pl.BlockSpec(block, lambda i, c=c: (0, 0, jnp.clip(i - c * count, 0, count - 1)))
+        for c in range(CHUNKS)
+        for _ in range(2)
     ]
     return call(
         functools.partial(settle_kernel, slabs, count),
-        2.6,
+        0,
         grid=(CHUNKS * count,),
-        in_specs=[SMEM, early, early] + late + [ANY] * (len(tokens) + 1),
+        in_specs=[SMEM] + specs + [ANY] * (len(tokens) + 1),
         out_specs=pl.BlockSpec(block, lambda i: (0, 0, i)),
-        results=value(base.shape, BF16),
-        scratch_shapes=[wide_tile(depth * rows)],
-    )(here, own, above, *arrays_of(pieces), *tokens, far(base))
+        results=pltpu.HBM(base.shape, BF16),
+    )(here, *[array for pair in own_above for array in pair], *tokens, far(base))
 
 
 def finish_kernel(here_ref, tv_ref, *refs):
@@ -384,7 +360,7 @@
     part = pl.BlockSpec((depth, rows, TILE), lambda i: (0, 0, first + i))
     return call(
         finish_kernel,
-        2.6,
+        0,
         grid=(count,),
         in_specs=[SMEM, part] + piece_specs(pieces, depth, ROWS * TILE) + [ANY] * len(tokens),
         out_specs=part,
@@ -470,23 +446,21 @@
         + [ANY] * len(tokens),
         out_specs=[across(shape, tile) for shape in shapes],
         results=[value(shape, BF16) for shape in shapes],
-    )(here, band, own, high, low, *arrays_of(sinos), *tokens)
-
-
-def back_kernel(dealing, here_ref, band_ref, own_ref, low_ref, high_ref, *refs):
+    )(here, far(band), own, high, low, *arrays_of(sinos), *tokens)
+
+
+def back_kernel(dealing, band_ref, own_ref, low_ref, high_ref, *refs):
     out_refs = refs[-G:]
     side = high_ref.shape[0]
     seeing = jnp.concatenate([own_ref[...], low_ref[...], high_ref[...]], axis=0)
     total = jnp.dot(band_ref[...], seeing, preferred_element_type=F32)
-    place = lax.rem(here_ref[0], G)
     for m, out_ref in enumerate(out_refs):
         out_ref[:side] = total[m * side : (m + 1) * side].astype(BF16)
         if dealing:
-            last = jnp.bitwise_xor(place, m) == G - 1
-            out_ref[side:] = jnp.where(last, refs[1][...], refs[0][m * side : (m + 1) * side])
-
-
-def back(here, band, own, low, high, dealt, *tokens):
+            out_ref[side:] = refs[0][m * side : (m + 1) * side]
+
+
+def back(band, own, low, high, dealt, *tokens):
     n, side = band.shape[0], band.shape[0] // G
     cols = own.shape[1]
     tile = 512
@@ -495,15 +469,14 @@
     out = ((2 if dealt else 1) * side, cols)
     return call(
         functools.partial(back_kernel, bool(dealt)),
-        3,
+        0,
         grid=(cols // tile,),
-        in_specs=[SMEM, pl.BlockSpec(band.shape, lambda i: (0, 0)), many, many]
-        + piece_specs([high], side, tile)
-        + ([many, one] if dealt else [])
+        in_specs=[pl.BlockSpec(band.shape, lambda i: (0, 0)), many, many, one]
+        + [many] * len(dealt)
         + [ANY] * len(tokens),
         out_specs=[across(out, tile)] * G,
         results=[value(out, BF16)] * G,
-    )(here, band, own, low, high[0], *dealt, *tokens)
+    )(far(band), own, low, high, *dealt, *tokens)
 
 
 def tv_flux(cur, above):
@@ -578,17 +551,19 @@
     def beyond(over, *others):
         return swapped(tied(over, *others)[depth:], 1)
 
-    *vols0, v0, v1, v23 = cast_rows(here, volume)
+    vols0 = cast_rows(here, volume, 0, single, True)
+    v0, v1, v23 = cast_rows(here, volume, 1, paired, False, vols0[1])
     got = moved(tied(sinogram, vols0[0]), G, only=G - 1)
     got_vols0 = direct(vols0)
-    near, over = swapped(v1, 1), swapped(v23, 2)
-    tv, tv_done = half_tv(volume, vols0[0])
+    over = swapped(v23, 2)
+    tv, tv_done = half_tv(volume, v1)
     own0, edge0 = pack(here, [(array, 0) for array in got_vols0], 2 * rows, tv_done)
-    high0, low0 = moved(own0, -G), moved(edge0, G)
+    high0, near = moved(own0, -G), swapped(tied(v1, own0), 1)
     band_p, band_b = bands(here, coverage, offsets, weights, own0)
-    *sino0, over_beyond = split_rows(here, sinogram, got, 0, single, [(over, 1)], band_p, near)
+    sino0 = split_rows(here, sinogram, got, 0, single, [], band_p, near)
     sinos0 = [(array, 0) for array in direct(sino0)]
-    own1, edge1 = pack(here, [(v0, 0), (near, 0), (over, 0), (swapped(over_beyond, 1), 0)], 0)
+    low0 = moved(tied(edge0, sinos0[1][0]), G)
+    own1, edge1 = pack(here, [(v0, 0), (near, 0), (over, 0), (beyond(over, sinos0[1][0]), 0)], 0)
     low1, high1 = moved(edge1, G), moved(own1, -G)
     s0, s1, s23 = split_rows(here, sinogram, got, 1, paired, [], own1)
 
@@ -598,19 +573,21 @@
     ends = [got_vols0[1], high0, got_vols0[3], low0]
     r_last, tv = patch(here, coverage, offsets, weights, ends, volume, sinogram, tv, resid0)
     sinos1 = [(s0, 0), (s_near, 0), (s_over, 0), (beyond(s_over, r_last), 0)]
-    r_near, r_over = swapped(tied(r1, s_over), 1), swapped(tied(r23, s_over), 2)
-    resid1, down1 = project(here, band_p, own1, high1, low1, sinos1, (), r_last)
+    r_near, r_over = swapped(tied(r1, s_near), 1), swapped(tied(r23, s_near), 2)
+    resid1, down1 = project(here, band_p, own1, high1, low1, sinos1, (), r_last, r_near, r_over)
     from_low1, from_high1 = moved(resid1, G), moved(down1, -G)
 
-    backs0 = back(here, band_b, resid0, from_low0, (from_high0, 0), [resid1, from_high1])
+    backs0 = back(band_b, resid0, from_low0, from_high0, [resid1])
     got_backs0 = direct(backs0)
-    r_pieces = [(resid0, 0), (r_near, 0), (r_over, 0), (beyond(r_over, backs0[0]), 0)]
+    r_pieces = [(resid0, 0), (r_near, 0), (r_over, 0), (beyond(r_over, got_backs0[1]), 0)]
     natural0 = join_rows(here, r_pieces, sinogram.shape, backs0[0])
     above0 = moved(natural0, -G, only=G - 1)
-    backs1 = back(here, band_b, resid1, from_low1, (from_high1, 0), [], natural0)
+    backs1 = back(band_b, resid1, from_low1, from_high1, [], natural0)
     got_backs1 = direct(backs1)
-    residual = settle(here, slabs, natural0, above0, [(array, 1) for array in got_backs0], r_last, backs1[0])
-    gradient = finish(here, 0, tv, [(array, 0) for array in got_backs0], backs1[0])
+    natural1 = join_rows(here, [(array, 1) for array in got_backs0], sinogram.shape, backs1[0])
+    above1 = moved(natural1, -G, only=G - 1)
+    gradient = finish(here, 0, tv, [(array, 0) for array in got_backs0], natural1)
+    residual = settle(here, slabs, [(natural0, above0), (natural1, above1)], r_last)
     gradient = finish(here, 1, gradient, [(array, 0) for array in got_backs1], residual)
     return (gradient, residual)
 

time: 143 us -> 145 us (1.014)
  the two profiles are of different devices: /device:TPU:1 before, /device:TPU:29 now
where the time goes in v9:
time: 145 us; the launch traced here: 144 us
  Pallas kernels  65.8 us (45%)
  starting transfers between devices  38.9 us (27%)
  waiting for transfers between devices  31.1 us (21%)
  local copies, waits for them, and re-layouts  7.15 us (5%)
    ppermute x11, starting transfers between devices, moved(): return lax.ppermute(value, 'slab', pairs)  23.8 us
    ppermute x11, waiting for transfers between devices, moved(): return lax.ppermute(value, 'slab', pairs)  22.9 us
    pallas_call x1, Pallas kernels, patch(): call(functools.partial(patch_kernel, slabs), 3, vmem=32, grid=(1,), in_sp...  15.5 us
    ppermute x21, starting transfers between devices, swapped(): return lax.ppermute(value, 'slab', [(i, i ^ bits) for i in range(count)])  15.1 us
    pallas_call x1, Pallas kernels, half_tv(): call(tv_kernel, 9, grid=(depth // deep,), in_specs=[after, body] + [ANY]...  9.92 us
    ppermute x21, waiting for transfers between devices, swapped(): return lax.ppermute(value, 'slab', [(i, i ^ bits) for i in range(count)])  8.18 us
    unnamed x28, local copies, waits for them, and re-layouts  7.1 us
    pallas_call x2, Pallas kernels, project(): call(functools.partial(project_kernel, groups), 3, grid=(cols // tile,),...  6.51 us
  transfers between devices with their start and end apart: 32, of which 10 were waited for; matrix products, arithmetic and copies ran while one was open for 0% of the time, Pallas kernels for 42%

profile of v9, /device:TPU:29, one launch (start us, length us, event | category | flops | bytes accessed | tf_op | source)
XLA Modules:
  0.0 144.0 jit_solution(10887171715138139834)
XLA Ops:
  0.6 2.5 %shard_map.68 = (bf16[128,1024]{1,0:T(8,128)(2,1)}, bf16[144,1024]{1,0:T(8,128)(2,1)S(1)}, bf16[128,1024]{1,0:T(8,128)(2,1)S(1)}, bf16[144,1024]{1,0:T(8,128)(2,1)S(1)}) custom-call(s32[1]{0:T(128)} %bitcast.here_ref, f32[1024,1024]{1,0:T(8,128)} %bitcast.2, f32[1024,1024]{1,0:T(8,128)} %bitcast.3, f32[1024,1024]{1,0:T(8,128)} %bitcast.4, f32[1024,1024]{1,0:T(8,128)} %bitcast.5), custom_call_target="tpu_custom_call" | custom-call | flops 2300000000 | bytes 1000 | tf_op jit(solution)/shard_map/pallas_call | solution.py:110
  3.1 1.3 collective-permute-start.4
  4.4 0.9 collective-permute-start.1
  5.3 2.1 %collective-permute-start.2 = (bf16[144,1024]{1,0:T(8,128)(2,1)S(1)}, bf16[144,1024]{1,0:T(8,128)(2,1)S(1)}, u32[]{:S(2)}, u32[]{:S(2)}) collective-permute-start(bf16[144,1024]{1,0:T(8,128)(2,1)S(1)} %get-tuple-element.51), channel_id=1, source_target_pairs={{0,3},{1,2},{2,1},{3,0},{4,7},{5,6},{6,5},{7,4},{8,11},{9,10},{10,... | collective-permute-start | bytes 884744 | tf_op jit(solution)/shard_map/ppermute | solution.py:32
  7.4 2.4 %shard_map.69 = (bf16[128,1024]{1,0:T(8,128)(2,1)}, bf16[128,1024]{1,0:T(8,128)(2,1)S(1)}, bf16[256,1024]{1,0:T(8,128)(2,1)S(1)}) custom-call(s32[1]{0:T(128)} %bitcast.here_ref, f32[1024,1024]{1,0:T(8,128)} %bitcast.6, f32[1024,1024]{1,0:T(8,128)} %bitcast.7, bf16[144,1024]{1,0:T(8,128)(2,1)S(1)} %get-tuple-element.48.refs_2_), custom_call_target="tpu_custom_call" | custom-call | flops 2300000000 | bytes 1000 | tf_op jit(solution)/shard_map/pallas_call | solution.py:110
  9.8 9.9 %shard_map.70 = (f32[128,8,1024]{2,1,0:T(8,128)}, f32[8,128]{1,0:T(8,128)S(1)}) custom-call(f32[128,8,1024]{2,1,0:T(8,128)} %refs_5_.1, f32[128,8,1024]{2,1,0:T(8,128)} %refs_5_.1, bf16[128,1024]{1,0:T(8,128)(2,1)S(1)} %get-tuple-element.58.refs_0_), custom_call_target="tpu_custom_call" | custom-call | flops 10350000128 | bytes 1000 | tf_op jit(solution)/shard_map/pallas_call | solution.py:530
  19.8 1.3 shard_map.71
  21.6 3.1 %collective-permute-start.3 = (bf16[528,1024]{1,0:T(8,128)(2,1)}, bf16[528,1024]{1,0:T(8,128)(2,1)S(1)}, u32[]{:S(2)}, u32[]{:S(2)}) collective-permute-start(bf16[528,1024]{1,0:T(8,128)(2,1)} %get-tuple-element.54.refs_0_.own_ref), channel_id=1, source_target_pairs={{4,0},{5,1},{6,2},{7,3},{8,4},{9,5},{10,6},{11,7},{12,8},{13,9},{1... | collective-permute-start | bytes 3244040 | tf_op jit(solution)/shard_map/ppermute | solution.py:27
  25.1 1.2 copy-done.3
  26.3 2.7 %shard_map.72 = (bf16[512,1152]{1,0:T(8,128)(2,1)}, bf16[512,1152]{1,0:T(8,128)(2,1)}) custom-call(s32[1]{0:T(128)} %bitcast.here_ref, s32[16,6]{1,0:T(8,128)S(1)} %copy.12.cover_ref, s32[16,6]{1,0:T(8,128)S(1)} %copy.13.offset_ref, bf16[8,128,128]{2,1,0:T(8,128)(2,1)S(1)} %copy-done.2, bf16[528,1024]{1,0:T(8,128)(2,1)S(1)} %copy-done.3), custom_call_target="tpu_custom_call" | custom-call | flops 1840000000 | bytes 1000 | tf_op jit(solution)/shard_map/pallas_call | solution.py:409
  29.0 1.4 collective-permute-done.4.got_ref
  30.4 1.3 copy-done.9
  31.7 2.0 %shard_map.73 = (bf16[128,1024]{1,0:T(8,128)(2,1)S(1)}, bf16[128,1024]{1,0:T(8,128)(2,1)S(1)}, bf16[128,1024]{1,0:T(8,128)(2,1)S(1)}, bf16[128,1024]{1,0:T(8,128)(2,1)S(1)}) custom-call(s32[1]{0:T(128)} %bitcast.here_ref, bf16[128,8,1024]{2,1,0:T(8,128)(2,1)} %refs_6_.1, bf16[128,8,1024]{2,1,0:T(8,128)(2,1)} %collective-permute-done.4.got_ref, ...), custom_call_target="tpu_custom_call" | custom-call | flops 2300000000 | bytes 1000 | tf_op jit(solution)/shard_map/pallas_call | solution.py:189
  33.7 4.4 %collective-permute-done.10.refs_2_ = bf16[256,1024]{1,0:T(8,128)(2,1)S(1)} collective-permute-done((bf16[256,1024]{1,0:T(8,128)(2,1)S(1)}, bf16[256,1024]{1,0:T(8,128)(2,1)S(1)}, u32[]{:S(2)}, u32[]{:S(2)}) %collective-permute-start.10) | collective-permute-done | bytes 524320 | tf_op jit(solution)/shard_map/ppermute | solution.py:32
  38.1 1.2 collective-permute-start.11
  39.3 1.7 %collective-permute-start.9 = (bf16[128,1024]{1,0:T(8,128)(2,1)S(1)}, bf16[128,1024]{1,0:T(8,128)(2,1)S(1)}, u32[]{:S(2)}, u32[]{:S(2)}) collective-permute-start(bf16[128,1024]{1,0:T(8,128)(2,1)S(1)} %get-tuple-element.64), channel_id=1, source_target_pairs={{0,3},{1,2},{2,1},{3,0},{4,7},{5,6},{6,5},{7,4},{8,11},{9,10},{10,... | collective-permute-start | bytes 786440 | tf_op jit(solution)/shard_map/ppermute | solution.py:32
  41.0 1.3 collective-permute-start.7
  42.3 1.3 shard_map.74
  43.6 1.3 collective-permute-start.12
  44.9 3.4 %collective-permute-done.3.high_ref.refs_2_ = bf16[528,1024]{1,0:T(8,128)(2,1)S(1)} collective-permute-done((bf16[528,1024]{1,0:T(8,128)(2,1)}, bf16[528,1024]{1,0:T(8,128)(2,1)S(1)}, u32[]{:S(2)}, u32[]{:S(2)}) %collective-permute-start.3) | collective-permute-done | bytes 1081376 | tf_op jit(solution)/shard_map/ppermute | solution.py:27
  48.3 4.2 %collective-permute-start.15 = (bf16[512,1024]{1,0:T(8,128)(2,1)}, bf16[512,1024]{1,0:T(8,128)(2,1)S(1)}, u32[]{:S(2)}, u32[]{:S(2)}) collective-permute-start(bf16[512,1024]{1,0:T(8,128)(2,1)} %get-tuple-element.69.refs_0_.own_ref), channel_id=1, source_target_pairs={{4,0},{5,1},{6,2},{7,3},{8,4},{9,5},{10,6},{11,7},{12,8},{13,9},{1... | collective-permute-start | bytes 3145736 | tf_op jit(solution)/shard_map/ppermute | solution.py:27
  52.5 1.2 copy-done.5
  53.7 1.9 %shard_map.75 = (bf16[128,1024]{1,0:T(8,128)(2,1)S(1)}, bf16[128,1024]{1,0:T(8,128)(2,1)S(1)}, bf16[256,1024]{1,0:T(8,128)(2,1)S(1)}) custom-call(s32[1]{0:T(128)} %bitcast.here_ref, bf16[128,8,1024]{2,1,0:T(8,128)(2,1)} %refs_6_.1, bf16[128,8,1024]{2,1,0:T(8,128)(2,1)} %collective-permute-done.4.got_ref, bf16[512,1024]{1,0:T(8,128)(2,1)S(1)} %copy-done.5), custom_call_target="tpu_custom_call" | custom-call | flops 2300000000 | bytes 1000 | tf_op jit(solution)/shard_map/pallas_call | solution.py:189
  55.6 1.1 collective-permute-start.16
  56.9 3.3 %shard_map.76 = (bf16[512,1024]{1,0:T(8,128)(2,1)S(1)}, bf16[128,1024]{1,0:T(8,128)(2,1)S(1)}, bf16[128,1024]{1,0:T(8,128)(2,1)S(1)}, bf16[256,1024]{1,0:T(8,128)(2,1)S(1)}) custom-call(s32[1]{0:T(128)} %bitcast.here_ref, bf16[512,1152]{1,0:T(8,128)(2,1)} %get-tuple-element.57.refs_0_.band_ref, bf16[528,1024]{1,0:T(8,128)(2,1)S(1)} %copy-done.4, ...), custom_call_target="tpu_custom_call" | custom-call | flops 3449999872 | bytes 1000 | tf_op jit(solution)/shard_map/pallas_call | solution.py:440
  60.3 1.0 collective-permute-start.19
  62.0 1.3 collective-permute-start.13
  63.3 15.5 %shard_map.77 = (bf16[128,8,1024]{2,1,0:T(8,128)(2,1)}, f32[128,8,1024]{2,1,0:T(8,128)}) custom-call(s32[1]{0:T(128)} %bitcast.here_ref, s32[16,6]{1,0:T(8,128)S(1)} %copy.12.cover_ref, s32[16,6]{1,0:T(8,128)S(1)} %copy.13.offset_ref, bf16[8,128,128]{2,1,0:T(8,128)(2,1)S(1)} %copy-done.2, ...), custom_call_target="tpu_custom_call", output_to_operand_aliasing={{1}: (10, {})} | custom-call | flops 3449999872 | bytes 1000 | tf_op jit(solution)/shard_map/pallas_call | solution.py:258
  79.0 1.3 collective-permute-start.14
  80.3 1.2 collective-permute-done.20.refs_6_.refs_2_
  81.5 1.6 %copy-done.1 = bf16[128,8,1024]{2,1,0:T(8,128)(2,1)S(1)} copy-done((bf16[128,8,1024]{2,1,0:T(8,128)(2,1)S(1)}, bf16[128,8,1024]{2,1,0:T(8,128)(2,1)}, u32[]{:S(2)}) %copy-start.1) | copy-done | bytes 2097176
  83.1 3.2 %shard_map.78 = (bf16[512,1024]{1,0:T(8,128)(2,1)S(1)}, bf16[128,1024]{1,0:T(8,128)(2,1)S(1)}) custom-call(s32[1]{0:T(128)} %bitcast.here_ref, bf16[512,1152]{1,0:T(8,128)(2,1)} %get-tuple-element.57.refs_0_.band_ref, bf16[512,1024]{1,0:T(8,128)(2,1)S(1)} %copy-done.6, bf16[512,1024]{1,0:T(8,128)(2,1)S(1)} %collective-permute-done.15.high_ref, ...), custom_call_target="tpu_custom_call" | custom-call | flops 3449999872 | bytes 1000 | tf_op jit(solution)/shard_map/pallas_call | solution.py:440
  86.3 1.3 collective-permute-start.24
  88.2 3.3 %shard_map.79 = (bf16[256,1024]{1,0:T(8,128)(2,1)S(1)}, bf16[256,1024]{1,0:T(8,128)(2,1)S(1)}, bf16[256,1024]{1,0:T(8,128)(2,1)S(1)}, bf16[256,1024]{1,0:T(8,128)(2,1)S(1)}) custom-call(bf16[512,1152]{1,0:T(8,128)(2,1)} %get-tuple-element.73.band_ref, bf16[512,1024]{1,0:T(8,128)(2,1)S(1)} %get-tuple-element.71.refs_8_.own_ref.refs_0_, ...), custom_call_target="tpu_custom_call" | custom-call | bytes 1000 | tf_op jit(solution)/shard_map/pallas_call | solution.py:470
  91.5 1.3 collective-permute-start.21
  94.8 3.3 %collective-permute-start.25 = (bf16[128,1024]{1,0:T(8,128)(2,1)S(1)}, bf16[128,1024]{1,0:T(8,128)(2,1)S(1)}, u32[]{:S(2)}, u32[]{:S(2)}) collective-permute-start(bf16[128,1024]{1,0:T(8,128)(2,1)S(1)} %get-tuple-element.88), channel_id=1, source_target_pairs={{4,0},{5,1},{6,2},{7,3},{8,4},{9,5},{10,6},{11,7},{12,8},{13,9},{1... | collective-permute-start | bytes 786440 | tf_op jit(solution)/shard_map/ppermute | solution.py:27
  99.1 2.1 %collective-permute-start.30 = (bf16[128,8,512]{2,1,0:T(8,128)(2,1)S(1)}, bf16[128,8,512]{2,1,0:T(8,128)(2,1)S(1)}, u32[]{:S(2)}, u32[]{:S(2)}) collective-permute-start(bf16[128,8,512]{2,1,0:T(8,128)(2,1)S(1)} %shard_map.80.refs_0_), channel_id=1, source_target_pairs={{7,3},{11,7},{15,11},{23,19},{27,23},{31,27}} | collective-permute-start | bytes 3145736 | tf_op jit(solution)/shard_map/ppermute | solution.py:27
  101.1 2.4 %collective-permute-done.25.high_ref = bf16[128,1024]{1,0:T(8,128)(2,1)S(1)} collective-permute-done((bf16[128,1024]{1,0:T(8,128)(2,1)S(1)}, bf16[128,1024]{1,0:T(8,128)(2,1)S(1)}, u32[]{:S(2)}, u32[]{:S(2)}) %collective-permute-start.25) | collective-permute-done | bytes 262176 | tf_op jit(solution)/shard_map/ppermute | solution.py:27
  103.5 8.5 %collective-permute-done.24.low_ref = bf16[512,1024]{1,0:T(8,128)(2,1)S(1)} collective-permute-done((bf16[512,1024]{1,0:T(8,128)(2,1)S(1)}, bf16[512,1024]{1,0:T(8,128)(2,1)S(1)}, u32[]{:S(2)}, u32[]{:S(2)}) %collective-permute-start.24) | collective-permute-done | bytes 1048608 | tf_op jit(solution)/shard_map/ppermute | solution.py:27
  112.0 3.1 %shard_map.81 = (bf16[128,1024]{1,0:T(8,128)(2,1)S(1)}, bf16[128,1024]{1,0:T(8,128)(2,1)S(1)}, bf16[128,1024]{1,0:T(8,128)(2,1)S(1)}, bf16[128,1024]{1,0:T(8,128)(2,1)S(1)}) custom-call(bf16[512,1152]{1,0:T(8,128)(2,1)} %get-tuple-element.73.band_ref, bf16[512,1024]{1,0:T(8,128)(2,1)S(1)} %get-tuple-element.83.refs_0_.own_ref, ...), custom_call_target="tpu_custom_call" | custom-call | bytes 1000 | tf_op jit(solution)/shard_map/pallas_call | solution.py:470
  115.2 2.6 %collective-permute-done.23.refs_3_ = bf16[256,1024]{1,0:T(8,128)(2,1)S(1)} collective-permute-done((bf16[256,1024]{1,0:T(8,128)(2,1)S(1)}, bf16[256,1024]{1,0:T(8,128)(2,1)S(1)}, u32[]{:S(2)}, u32[]{:S(2)}) %collective-permute-start.23) | collective-permute-done | bytes 524320 | tf_op jit(solution)/shard_map/ppermute | solution.py:32
  118.6 3.4 %collective-permute-start.31 = (bf16[128,8,512]{2,1,0:T(8,128)(2,1)S(1)}, bf16[128,8,512]{2,1,0:T(8,128)(2,1)S(1)}, u32[]{:S(2)}, u32[]{:S(2)}) collective-permute-start(bf16[128,8,512]{2,1,0:T(8,128)(2,1)S(1)} %shard_map.82.refs_4_.refs_2_), channel_id=1, source_target_pairs={{7,3},{11,7},{15,11},{23,19},{27,23},{31,27}} | collective-permute-start | bytes 3145736 | tf_op jit(solution)/shard_map/ppermute | solution.py:27
  122.2 2.0 %collective-permute-start.29 = (bf16[128,1024]{1,0:T(8,128)(2,1)S(1)}, bf16[128,1024]{1,0:T(8,128)(2,1)S(1)}, u32[]{:S(2)}, u32[]{:S(2)}) collective-permute-start(bf16[128,1024]{1,0:T(8,128)(2,1)S(1)} %get-tuple-element.93), channel_id=1, source_target_pairs={{0,3},{1,2},{2,1},{3,0},{4,7},{5,6},{6,5},{7,4},{8,11},{9,10},{10,... | collective-permute-start | bytes 786440 | tf_op jit(solution)/shard_map/ppermute | solution.py:32
  124.2 2.9 %shard_map.83.tv_ref = f32[128,8,1024]{2,1,0:T(8,128)} custom-call(s32[1]{0:T(128)} %bitcast.here_ref, f32[128,8,1024]{2,1,0:T(8,128)} %get-tuple-element.72.tv_ref, bf16[256,1024]{1,0:T(8,128)(2,1)S(1)} %get-tuple-element.84.refs_4_.refs_0_, bf16[256,1024]{1,0:T(8,128)(2,1)S(1)} %collective-permute-done.21.refs_1_, ...), custom_call_target="tpu_custom_call", output_to_operand_aliasing={{}: (1, {})} | custom-call | bytes 1000 | tf_op jit(solution)/shard_map/pallas_call | solution.py:361
  127.1 6.5 %collective-permute-done.31.refs_3_ = bf16[128,8,512]{2,1,0:T(8,128)(2,1)S(1)} collective-permute-done((bf16[128,8,512]{2,1,0:T(8,128)(2,1)S(1)}, bf16[128,8,512]{2,1,0:T(8,128)(2,1)S(1)}, u32[]{:S(2)}, u32[]{:S(2)}) %collective-permute-start.31) | collective-permute-done | bytes 1048608 | tf_op jit(solution)/shard_map/ppermute | solution.py:27
  133.7 5.8 %shard_map.84.refs_4_ = bf16[128,8,1024]{2,1,0:T(8,128)(2,1)} custom-call(s32[1]{0:T(128)} %bitcast.here_ref, bf16[128,8,512]{2,1,0:T(8,128)(2,1)S(1)} %shard_map.80.refs_0_, bf16[128,8,512]{2,1,0:T(8,128)(2,1)S(1)} %collective-permute-done.30.refs_1_, bf16[128,8,512]{2,1,0:T(8,128)(2,1)S(1)} %shard_map.82.refs_4_.refs_2_, ...), custom_call_target="tpu_custom_call" | custom-call | bytes 1000 | tf_op jit(solution)/shard_map/pallas_call | solution.py:340
  139.5 1.6 %copy-done = bf16[128,8,1024]{2,1,0:T(8,128)(2,1)S(1)} copy-done((bf16[128,8,1024]{2,1,0:T(8,128)(2,1)S(1)}, bf16[128,8,1024]{2,1,0:T(8,128)(2,1)}, u32[]{:S(2)}) %copy-start) | copy-done | bytes 2097176
  141.1 2.9 %shard_map.85 = f32[128,8,1024]{2,1,0:T(8,128)} custom-call(s32[1]{0:T(128)} %bitcast.here_ref, f32[128,8,1024]{2,1,0:T(8,128)} %shard_map.83.tv_ref, bf16[128,1024]{1,0:T(8,128)(2,1)S(1)} %get-tuple-element.90.refs_4_.refs_0_, bf16[128,1024]{1,0:T(8,128)(2,1)S(1)} %collective-permute-done.27.refs_1_, ...), custom_call_target="tpu_custom_call", output_to_operand_aliasing={{}: (1, {})} | custom-call | bytes 1000 | tf_op jit(solution)/shard_map/pallas_call | solution.py:361
  (65 shorter events, 6.4 us)
Async XLA Ops:
  3.1 27.3 %collective-permute-start.4 = (bf16[128,8,1024]{2,1,0:T(8,128)(2,1)}, bf16[128,8,1024]{2,1,0:T(8,128)(2,1)}, u32[]{:S(2)}, u32[]{:S(2)}) collective-permute-start(bf16[128,8,1024]{2,1,0:T(8,128)(2,1)} %refs_6_.1), channel_id=1, source_target_pairs={{3,7},{7,11},{11,15},{19,23},{23,27},{27,31}} | collective-permute-start | bytes 6291464 | tf_op jit(solution)/shard_map/ppermute | solution.py:27
  4.4 15.4 %collective-permute-start.1 = (bf16[128,1024]{1,0:T(8,128)(2,1)S(1)}, bf16[128,1024]{1,0:T(8,128)(2,1)S(1)}, u32[]{:S(2)}, u32[]{:S(2)}) collective-permute-start(bf16[128,1024]{1,0:T(8,128)(2,1)S(1)} %get-tuple-element.50), channel_id=1, source_target_pairs={{0,2},{1,3},{2,0},{3,1},{4,6},{5,7},{6,4},{7,5},{8,10},{9,11},{10,... | collective-permute-start | bytes 786440 | tf_op jit(solution)/shard_map/ppermute | solution.py:32
  5.3 14.4 %collective-permute-start.2 = (bf16[144,1024]{1,0:T(8,128)(2,1)S(1)}, bf16[144,1024]{1,0:T(8,128)(2,1)S(1)}, u32[]{:S(2)}, u32[]{:S(2)}) collective-permute-start(bf16[144,1024]{1,0:T(8,128)(2,1)S(1)} %get-tuple-element.51), channel_id=1, source_target_pairs={{0,3},{1,2},{2,1},{3,0},{4,7},{5,6},{6,5},{7,4},{8,11},{9,10},{10,... | collective-permute-start | bytes 884744 | tf_op jit(solution)/shard_map/ppermute | solution.py:32
  7.4 12.4 %collective-permute-start = (bf16[144,1024]{1,0:T(8,128)(2,1)S(1)}, bf16[144,1024]{1,0:T(8,128)(2,1)S(1)}, u32[]{:S(2)}, u32[]{:S(2)}) collective-permute-start(bf16[144,1024]{1,0:T(8,128)(2,1)S(1)} %get-tuple-element.48.refs_2_), channel_id=1, source_target_pairs={{0,1},{1,0},{2,3},{3,2},{4,5},{5,4},{6,7},{7,6},{8,9},{9,8},{10,11... | collective-permute-start | bytes 884744 | tf_op jit(solution)/shard_map/ppermute | solution.py:32
  9.8 9.9 %copy-start.8 = (bf16[128,1024]{1,0:T(8,128)(2,1)S(1)}, bf16[128,1024]{1,0:T(8,128)(2,1)}, u32[]{:S(2)}) copy-start(bf16[128,1024]{1,0:T(8,128)(2,1)} %get-tuple-element.49.refs_0_) | copy-start | bytes 786436
  19.8 5.1 %copy-start.10 = (s32[16,6]{0,1:T(8,128)S(1)}, s32[16,6]{0,1:T(8,128)}, u32[]{:S(2)}) copy-start(s32[16,6]{0,1:T(8,128)} %param.8) | copy-start | bytes 1156
  19.8 5.2 %copy-start.11 = (s32[16,6]{0,1:T(8,128)S(1)}, s32[16,6]{0,1:T(8,128)}, u32[]{:S(2)}) copy-start(s32[16,6]{0,1:T(8,128)} %param.9) | copy-start | bytes 1156
  19.8 5.2 %copy-start.2 = (bf16[8,128,128]{2,1,0:T(8,128)(2,1)S(1)}, bf16[8,128,128]{2,1,0:T(8,128)(2,1)}, u32[]{:S(2)}) copy-start(bf16[8,128,128]{2,1,0:T(8,128)(2,1)} %refs_0_.1) | copy-start | bytes 786436
  21.1 7.8 %collective-permute-start.5 = (bf16[128,1024]{1,0:T(8,128)(2,1)S(1)}, bf16[128,1024]{1,0:T(8,128)(2,1)S(1)}, u32[]{:S(2)}, u32[]{:S(2)}) collective-permute-start(bf16[128,1024]{1,0:T(8,128)(2,1)S(1)} %get-tuple-element.58.refs_0_), channel_id=1, source_target_pairs={{0,1},{1,0},{2,3},{3,2},{4,5},{5,4},{6,7},{7,6},{8,9},{9,8},{10,11... | collective-permute-start | bytes 786440 | tf_op jit(solution)/shard_map/ppermute | solution.py:32
  21.6 26.6 %collective-permute-start.3 = (bf16[528,1024]{1,0:T(8,128)(2,1)}, bf16[528,1024]{1,0:T(8,128)(2,1)S(1)}, u32[]{:S(2)}, u32[]{:S(2)}) collective-permute-start(bf16[528,1024]{1,0:T(8,128)(2,1)} %get-tuple-element.54.refs_0_.own_ref), channel_id=1, source_target_pairs={{4,0},{5,1},{6,2},{7,3},{8,4},{9,5},{10,6},{11,7},{12,8},{13,9},{1... | collective-permute-start | bytes 3244040 | tf_op jit(solution)/shard_map/ppermute | solution.py:27
  24.8 13.3 %collective-permute-start.10 = (bf16[256,1024]{1,0:T(8,128)(2,1)S(1)}, bf16[256,1024]{1,0:T(8,128)(2,1)S(1)}, u32[]{:S(2)}, u32[]{:S(2)}) collective-permute-start(bf16[256,1024]{1,0:T(8,128)(2,1)S(1)} %get-tuple-element.66), channel_id=1, source_target_pairs={{0,2},{1,3},{2,0},{3,1},{4,6},{5,7},{6,4},{7,5},{8,10},{9,11},{10,... | collective-permute-start | bytes 1572872 | tf_op jit(solution)/shard_map/ppermute | solution.py:32
  25.1 1.2 copy-start.3
  30.4 1.3 copy-start.9
  31.7 9.3 %copy-start.12 = (bf16[144,1024]{1,0:T(8,128)(2,1)S(1)}, bf16[144,1024]{1,0:T(8,128)(2,1)}, u32[]{:S(2)}) copy-start(bf16[144,1024]{1,0:T(8,128)(2,1)} %get-tuple-element.60) | copy-start | bytes 884740
  31.7 10.6 %copy-start.7 = (bf16[128,1024]{1,0:T(8,128)(2,1)S(1)}, bf16[128,1024]{1,0:T(8,128)(2,1)}, u32[]{:S(2)}) copy-start(bf16[128,1024]{1,0:T(8,128)(2,1)} %get-tuple-element.65.refs_0_) | copy-start | bytes 786436
  33.6 4.5 %collective-permute-start.6 = (bf16[128,1024]{1,0:T(8,128)(2,1)S(1)}, bf16[128,1024]{1,0:T(8,128)(2,1)S(1)}, u32[]{:S(2)}, u32[]{:S(2)}) collective-permute-start(bf16[128,1024]{1,0:T(8,128)(2,1)S(1)} %get-tuple-element.59), channel_id=1, source_target_pairs={{0,1},{1,0},{2,3},{3,2},{4,5},{5,4},{6,7},{7,6},{8,9},{9,8},{10,11... | collective-permute-start | bytes 786440 | tf_op jit(solution)/shard_map/ppermute | solution.py:32
  38.1 4.2 %collective-permute-start.11 = (bf16[128,1024]{1,0:T(8,128)(2,1)S(1)}, bf16[128,1024]{1,0:T(8,128)(2,1)S(1)}, u32[]{:S(2)}, u32[]{:S(2)}) collective-permute-start(bf16[128,1024]{1,0:T(8,128)(2,1)S(1)} %slice.9), channel_id=1, source_target_pairs={{0,1},{1,0},{2,3},{3,2},{4,5},{5,4},{6,7},{7,6},{8,9},{9,8},{10,11... | collective-permute-start | bytes 786440 | tf_op jit(solution)/shard_map/ppermute | solution.py:32
  39.3 16.4 %collective-permute-start.8 = (bf16[128,1024]{1,0:T(8,128)(2,1)S(1)}, bf16[128,1024]{1,0:T(8,128)(2,1)S(1)}, u32[]{:S(2)}, u32[]{:S(2)}) collective-permute-start(bf16[128,1024]{1,0:T(8,128)(2,1)S(1)} %get-tuple-element.63), channel_id=1, source_target_pairs={{0,2},{1,3},{2,0},{3,1},{4,6},{5,7},{6,4},{7,5},{8,10},{9,11},{10,... | collective-permute-start | bytes 786440 | tf_op jit(solution)/shard_map/ppermute | solution.py:32
  39.3 17.4 %collective-permute-start.9 = (bf16[128,1024]{1,0:T(8,128)(2,1)S(1)}, bf16[128,1024]{1,0:T(8,128)(2,1)S(1)}, u32[]{:S(2)}, u32[]{:S(2)}) collective-permute-start(bf16[128,1024]{1,0:T(8,128)(2,1)S(1)} %get-tuple-element.64), channel_id=1, source_target_pairs={{0,3},{1,2},{2,1},{3,0},{4,7},{5,6},{6,5},{7,4},{8,11},{9,10},{10,... | collective-permute-start | bytes 786440 | tf_op jit(solution)/shard_map/ppermute | solution.py:32
  41.0 15.8 %collective-permute-start.7 = (bf16[144,1024]{1,0:T(8,128)(2,1)S(1)}, bf16[144,1024]{1,0:T(8,128)(2,1)S(1)}, u32[]{:S(2)}, u32[]{:S(2)}) collective-permute-start(bf16[144,1024]{1,0:T(8,128)(2,1)S(1)} %copy-done.12), channel_id=1, source_target_pairs={{0,4},{1,5},{2,6},{3,7},{4,8},{5,9},{6,10},{7,11},{8,12},{9,13},{1... | collective-permute-start | bytes 884744 | tf_op jit(solution)/shard_map/ppermute | solution.py:27
  43.6 13.3 %collective-permute-start.12 = (bf16[128,1024]{1,0:T(8,128)(2,1)}, bf16[128,1024]{1,0:T(8,128)(2,1)S(1)}, u32[]{:S(2)}, u32[]{:S(2)}) collective-permute-start(bf16[128,1024]{1,0:T(8,128)(2,1)} %get-tuple-element.68), channel_id=1, source_target_pairs={{0,4},{1,5},{2,6},{3,7},{4,8},{5,9},{6,10},{7,11},{8,12},{9,13},{1... | collective-permute-start | bytes 786440 | tf_op jit(solution)/shard_map/ppermute | solution.py:27
  48.3 8.6 %copy-start.4 = (bf16[528,1024]{1,0:T(8,128)(2,1)S(1)}, bf16[528,1024]{1,0:T(8,128)(2,1)}, u32[]{:S(2)}) copy-start(bf16[528,1024]{1,0:T(8,128)(2,1)} %get-tuple-element.54.refs_0_.own_ref) | copy-start | bytes 3244036
  48.3 33.2 %collective-permute-start.15 = (bf16[512,1024]{1,0:T(8,128)(2,1)}, bf16[512,1024]{1,0:T(8,128)(2,1)S(1)}, u32[]{:S(2)}, u32[]{:S(2)}) collective-permute-start(bf16[512,1024]{1,0:T(8,128)(2,1)} %get-tuple-element.69.refs_0_.own_ref), channel_id=1, source_target_pairs={{4,0},{5,1},{6,2},{7,3},{8,4},{9,5},{10,6},{11,7},{12,8},{13,9},{1... | collective-permute-start | bytes 3145736 | tf_op jit(solution)/shard_map/ppermute | solution.py:27
  52.5 1.2 copy-start.5
  55.6 4.6 %collective-permute-start.16 = (bf16[128,1024]{1,0:T(8,128)(2,1)S(1)}, bf16[128,1024]{1,0:T(8,128)(2,1)S(1)}, u32[]{:S(2)}, u32[]{:S(2)}) collective-permute-start(bf16[128,1024]{1,0:T(8,128)(2,1)S(1)} %get-tuple-element.75), channel_id=1, source_target_pairs={{0,1},{1,0},{2,3},{3,2},{4,5},{5,4},{6,7},{7,6},{8,9},{9,8},{10,11... | collective-permute-start | bytes 786440 | tf_op jit(solution)/shard_map/ppermute | solution.py:32
  56.8 22.1 %collective-permute-start.17 = (bf16[256,1024]{1,0:T(8,128)(2,1)S(1)}, bf16[256,1024]{1,0:T(8,128)(2,1)S(1)}, u32[]{:S(2)}, u32[]{:S(2)}) collective-permute-start(bf16[256,1024]{1,0:T(8,128)(2,1)S(1)} %get-tuple-element.76), channel_id=1, source_target_pairs={{0,2},{1,3},{2,0},{3,1},{4,6},{5,7},{6,4},{7,5},{8,10},{9,11},{10,... | collective-permute-start | bytes 1572872 | tf_op jit(solution)/shard_map/ppermute | solution.py:32
  60.3 18.7 %collective-permute-start.19 = (bf16[128,1024]{1,0:T(8,128)(2,1)S(1)}, bf16[128,1024]{1,0:T(8,128)(2,1)S(1)}, u32[]{:S(2)}, u32[]{:S(2)}) collective-permute-start(bf16[128,1024]{1,0:T(8,128)(2,1)S(1)} %get-tuple-element.80), channel_id=1, source_target_pairs={{0,1},{1,0},{2,3},{3,2},{4,5},{5,4},{6,7},{7,6},{8,9},{9,8},{10,11... | collective-permute-start | bytes 786440 | tf_op jit(solution)/shard_map/ppermute | solution.py:32
  61.3 20.2 %collective-permute-start.20 = (bf16[256,1024]{1,0:T(8,128)(2,1)S(1)}, bf16[256,1024]{1,0:T(8,128)(2,1)S(1)}, u32[]{:S(2)}, u32[]{:S(2)}) collective-permute-start(bf16[256,1024]{1,0:T(8,128)(2,1)S(1)} %get-tuple-element.82), channel_id=1, source_target_pairs={{0,2},{1,3},{2,0},{3,1},{4,6},{5,7},{6,4},{7,5},{8,10},{9,11},{10,... | collective-permute-start | bytes 1572872 | tf_op jit(solution)/shard_map/ppermute | solution.py:32
  62.0 26.2 %collective-permute-start.13 = (bf16[512,1024]{1,0:T(8,128)(2,1)S(1)}, bf16[512,1024]{1,0:T(8,128)(2,1)S(1)}, u32[]{:S(2)}, u32[]{:S(2)}) collective-permute-start(bf16[512,1024]{1,0:T(8,128)(2,1)S(1)} %get-tuple-element.71.refs_8_.own_ref.refs_0_), channel_id=1, source_target_pairs={{0,4},{1,5},{2,6},{3,7},{4,8},{5,9},{6,10},{7,11},{8,12},{9,13},{1... | collective-permute-start | bytes 3145736 | tf_op jit(solution)/shard_map/ppermute | solution.py:27
  63.3 18.2 %copy-start.6 = (bf16[512,1024]{1,0:T(8,128)(2,1)S(1)}, bf16[512,1024]{1,0:T(8,128)(2,1)}, u32[]{:S(2)}) copy-start(bf16[512,1024]{1,0:T(8,128)(2,1)} %get-tuple-element.69.refs_0_.own_ref) | copy-start | bytes 3145732
  78.9 2.6 %collective-permute-start.18 = (bf16[128,1024]{1,0:T(8,128)(2,1)S(1)}, bf16[128,1024]{1,0:T(8,128)(2,1)S(1)}, u32[]{:S(2)}, u32[]{:S(2)}) collective-permute-start(bf16[128,1024]{1,0:T(8,128)(2,1)S(1)} %slice.10), channel_id=1, source_target_pairs={{0,1},{1,0},{2,3},{3,2},{4,5},{5,4},{6,7},{7,6},{8,9},{9,8},{10,11... | collective-permute-start | bytes 786440 | tf_op jit(solution)/shard_map/ppermute | solution.py:32
  79.0 8.6 %collective-permute-start.14 = (bf16[128,1024]{1,0:T(8,128)(2,1)S(1)}, bf16[128,1024]{1,0:T(8,128)(2,1)S(1)}, u32[]{:S(2)}, u32[]{:S(2)}) collective-permute-start(bf16[128,1024]{1,0:T(8,128)(2,1)S(1)} %get-tuple-element.74), channel_id=1, source_target_pairs={{4,0},{5,1},{6,2},{7,3},{8,4},{9,5},{10,6},{11,7},{12,8},{13,9},{1... | collective-permute-start | bytes 786440 | tf_op jit(solution)/shard_map/ppermute | solution.py:27
  81.5 1.6 %copy-start.1 = (bf16[128,8,1024]{2,1,0:T(8,128)(2,1)S(1)}, bf16[128,8,1024]{2,1,0:T(8,128)(2,1)}, u32[]{:S(2)}) copy-start(bf16[128,8,1024]{2,1,0:T(8,128)(2,1)} %get-tuple-element.77.refs_4_) | copy-start | bytes 6291460
  86.3 25.7 %collective-permute-start.24 = (bf16[512,1024]{1,0:T(8,128)(2,1)S(1)}, bf16[512,1024]{1,0:T(8,128)(2,1)S(1)}, u32[]{:S(2)}, u32[]{:S(2)}) collective-permute-start(bf16[512,1024]{1,0:T(8,128)(2,1)S(1)} %get-tuple-element.83.refs_0_.own_ref), channel_id=1, source_target_pairs={{0,4},{1,5},{2,6},{3,7},{4,8},{5,9},{6,10},{7,11},{8,12},{9,13},{1... | collective-permute-start | bytes 3145736 | tf_op jit(solution)/shard_map/ppermute | solution.py:27
  91.5 3.1 %collective-permute-start.21 = (bf16[256,1024]{1,0:T(8,128)(2,1)S(1)}, bf16[256,1024]{1,0:T(8,128)(2,1)S(1)}, u32[]{:S(2)}, u32[]{:S(2)}) collective-permute-start(bf16[256,1024]{1,0:T(8,128)(2,1)S(1)} %get-tuple-element.85), channel_id=1, source_target_pairs={{0,1},{1,0},{2,3},{3,2},{4,5},{5,4},{6,7},{7,6},{8,9},{9,8},{10,11... | collective-permute-start | bytes 1572872 | tf_op jit(solution)/shard_map/ppermute | solution.py:32
  92.8 22.3 %collective-permute-start.22 = (bf16[256,1024]{1,0:T(8,128)(2,1)S(1)}, bf16[256,1024]{1,0:T(8,128)(2,1)S(1)}, u32[]{:S(2)}, u32[]{:S(2)}) collective-permute-start(bf16[256,1024]{1,0:T(8,128)(2,1)S(1)} %get-tuple-element.86), channel_id=1, source_target_pairs={{0,2},{1,3},{2,0},{3,1},{4,6},{5,7},{6,4},{7,5},{8,10},{9,11},{10,... | collective-permute-start | bytes 1572872 | tf_op jit(solution)/shard_map/ppermute | solution.py:32
  93.6 24.1 %collective-permute-start.23 = (bf16[256,1024]{1,0:T(8,128)(2,1)S(1)}, bf16[256,1024]{1,0:T(8,128)(2,1)S(1)}, u32[]{:S(2)}, u32[]{:S(2)}) collective-permute-start(bf16[256,1024]{1,0:T(8,128)(2,1)S(1)} %get-tuple-element.87), channel_id=1, source_target_pairs={{0,3},{1,2},{2,1},{3,0},{4,7},{5,6},{6,5},{7,4},{8,11},{9,10},{10,... | collective-permute-start | bytes 1572872 | tf_op jit(solution)/shard_map/ppermute | solution.py:32
  94.6 3.6 %collective-permute-start.26 = (bf16[128,1024]{1,0:T(8,128)(2,1)S(1)}, bf16[128,1024]{1,0:T(8,128)(2,1)S(1)}, u32[]{:S(2)}, u32[]{:S(2)}) collective-permute-start(bf16[128,1024]{1,0:T(8,128)(2,1)S(1)} %slice.11), channel_id=1, source_target_pairs={{0,1},{1,0},{2,3},{3,2},{4,5},{5,4},{6,7},{7,6},{8,9},{9,8},{10,11... | collective-permute-start | bytes 786440 | tf_op jit(solution)/shard_map/ppermute | solution.py:32
  94.8 8.7 %collective-permute-start.25 = (bf16[128,1024]{1,0:T(8,128)(2,1)S(1)}, bf16[128,1024]{1,0:T(8,128)(2,1)S(1)}, u32[]{:S(2)}, u32[]{:S(2)}) collective-permute-start(bf16[128,1024]{1,0:T(8,128)(2,1)S(1)} %get-tuple-element.88), channel_id=1, source_target_pairs={{4,0},{5,1},{6,2},{7,3},{8,4},{9,5},{10,6},{11,7},{12,8},{13,9},{1... | collective-permute-start | bytes 786440 | tf_op jit(solution)/shard_map/ppermute | solution.py:27
  99.1 28.1 %collective-permute-start.30 = (bf16[128,8,512]{2,1,0:T(8,128)(2,1)S(1)}, bf16[128,8,512]{2,1,0:T(8,128)(2,1)S(1)}, u32[]{:S(2)}, u32[]{:S(2)}) collective-permute-start(bf16[128,8,512]{2,1,0:T(8,128)(2,1)S(1)} %shard_map.80.refs_0_), channel_id=1, source_target_pairs={{7,3},{11,7},{15,11},{23,19},{27,23},{31,27}} | collective-permute-start | bytes 3145736 | tf_op jit(solution)/shard_map/ppermute | solution.py:27
  118.6 15.1 %collective-permute-start.31 = (bf16[128,8,512]{2,1,0:T(8,128)(2,1)S(1)}, bf16[128,8,512]{2,1,0:T(8,128)(2,1)S(1)}, u32[]{:S(2)}, u32[]{:S(2)}) collective-permute-start(bf16[128,8,512]{2,1,0:T(8,128)(2,1)S(1)} %shard_map.82.refs_4_.refs_2_), channel_id=1, source_target_pairs={{7,3},{11,7},{15,11},{23,19},{27,23},{31,27}} | collective-permute-start | bytes 3145736 | tf_op jit(solution)/shard_map/ppermute | solution.py:27
  122.0 17.5 %collective-permute-start.27 = (bf16[128,1024]{1,0:T(8,128)(2,1)S(1)}, bf16[128,1024]{1,0:T(8,128)(2,1)S(1)}, u32[]{:S(2)}, u32[]{:S(2)}) collective-permute-start(bf16[128,1024]{1,0:T(8,128)(2,1)S(1)} %get-tuple-element.91), channel_id=1, source_target_pairs={{0,1},{1,0},{2,3},{3,2},{4,5},{5,4},{6,7},{7,6},{8,9},{9,8},{10,11... | collective-permute-start | bytes 786440 | tf_op jit(solution)/shard_map/ppermute | solution.py:32
  122.1 17.4 %collective-permute-start.28 = (bf16[128,1024]{1,0:T(8,128)(2,1)S(1)}, bf16[128,1024]{1,0:T(8,128)(2,1)S(1)}, u32[]{:S(2)}, u32[]{:S(2)}) collective-permute-start(bf16[128,1024]{1,0:T(8,128)(2,1)S(1)} %get-tuple-element.92), channel_id=1, source_target_pairs={{0,2},{1,3},{2,0},{3,1},{4,6},{5,7},{6,4},{7,5},{8,10},{9,11},{10,... | collective-permute-start | bytes 786440 | tf_op jit(solution)/shard_map/ppermute | solution.py:32
  122.2 17.3 %collective-permute-start.29 = (bf16[128,1024]{1,0:T(8,128)(2,1)S(1)}, bf16[128,1024]{1,0:T(8,128)(2,1)S(1)}, u32[]{:S(2)}, u32[]{:S(2)}) collective-permute-start(bf16[128,1024]{1,0:T(8,128)(2,1)S(1)} %get-tuple-element.93), channel_id=1, source_target_pairs={{0,3},{1,2},{2,1},{3,0},{4,7},{5,6},{6,5},{7,4},{8,11},{9,10},{10,... | collective-permute-start | bytes 786440 | tf_op jit(solution)/shard_map/ppermute | solution.py:32
  139.5 1.6 %copy-start = (bf16[128,8,1024]{2,1,0:T(8,128)(2,1)S(1)}, bf16[128,8,1024]{2,1,0:T(8,128)(2,1)}, u32[]{:S(2)}) copy-start(bf16[128,8,1024]{2,1,0:T(8,128)(2,1)} %shard_map.84.refs_4_) | copy-start | bytes 6291460

commit v10 on v9

--- a/solution.py
+++ b/solution.py
@@ -197,35 +197,18 @@
     )(here, far(own), got, *arrays_of(passing), *tokens)
 
 
-def patch_kernel(slabs, here_ref, cover_ref, offset_ref, *refs):
-    w_ref, *refs = refs
-    end_refs, (vol_ref, sino_ref), (r_ref, tv_ref) = refs[:4], refs[4:6], refs[-10:-8]
-    vol, s, r, wide, tv, slices, fixed, sem = refs[-8:]
+def last_kernel(slabs, here_ref, cover_ref, offset_ref, *refs):
+    w_ref, vol_ref, sino_ref, *refs = refs
+    r_ref, tv_ref, vol, s, r, wide, tv, sem = refs[-8:]
     depth, rows, cols = sino_ref.shape
-    place = lax.rem(here_ref[0], G)
-    near, next_level, far_end, last_level = (ref[...] for ref in end_refs)
-    low = jnp.where(place == 0, last_level, jnp.where(place == 2, far_end, near))[rows:].astype(F32)
-    high = jnp.where(place == G - 1, next_level, jnp.where(place == 1, far_end, near))[:rows].astype(F32)
-
-    for n, z in enumerate((0, depth - 2)):
-        pltpu.make_async_copy(vol_ref.at[z : z + 2], slices.at[2 * n : 2 * n + 2], sem.at[n]).start()
-    for n, z in enumerate((0, depth - 2)):
-        pltpu.make_async_copy(vol_ref.at[z : z + 2], slices.at[2 * n : 2 * n + 2], sem.at[n]).wait()
-    fixed[0] = tv_slice(slices[0], slices[1], tv_below(low, slices[0]))[0]
-    fixed[1] = tv_slice(slices[3], high, tv_below(slices[2], slices[3]))[0]
-    for n, z in enumerate((0, depth - 1)):
-        pltpu.make_async_copy(fixed.at[n], tv_ref.at[z], sem.at[n]).start()
-    for n, z in enumerate((0, depth - 1)):
-        pltpu.make_async_copy(fixed.at[n], tv_ref.at[z], sem.at[n]).wait()
 
     @pl.when(here_ref[0] == slabs - 1)
     def _():
-        pltpu.make_async_copy(vol_ref, vol, sem.at[2]).start()
-        pltpu.make_async_copy(sino_ref, s, sem.at[3]).start()
-        pltpu.make_async_copy(tv_ref, tv, sem.at[4]).start()
-        pltpu.make_async_copy(vol_ref, vol, sem.at[2]).wait()
-        pltpu.make_async_copy(sino_ref, s, sem.at[3]).wait()
-        pltpu.make_async_copy(tv_ref, tv, sem.at[4]).wait()
+        arrivals = [(vol_ref, vol), (sino_ref, s), (tv_ref, tv)]
+        for n, (src, dst) in enumerate(arrivals):
+            pltpu.make_async_copy(src, dst, sem.at[n]).start()
+        for n, (src, dst) in enumerate(arrivals):
+            pltpu.make_async_copy(src, dst, sem.at[n]).wait()
         block = w_ref[offset_ref[slabs - 1, 0]]
         block = jnp.where(cover_ref[slabs - 1, 0] == 1, block, jnp.zeros_like(block))
         turned = block.astype(F32).T.astype(BF16)
@@ -245,38 +228,34 @@
             return 0
 
         lax.fori_loop(0, cols // LANES, column, 0)
-        pltpu.make_async_copy(r, r_ref, sem.at[3]).start()
-        pltpu.make_async_copy(tv, tv_ref, sem.at[4]).start()
-        pltpu.make_async_copy(r, r_ref, sem.at[3]).wait()
-        pltpu.make_async_copy(tv, tv_ref, sem.at[4]).wait()
-
-
-def patch(here, coverage, offsets, weights, ends, volume, sinogram, tv, *tokens):
+        departures = [(r, r_ref), (tv, tv_ref)]
+        for n, (src, dst) in enumerate(departures):
+            pltpu.make_async_copy(src, dst, sem.at[n]).start()
+        for n, (src, dst) in enumerate(departures):
+            pltpu.make_async_copy(src, dst, sem.at[n]).wait()
+
+
+def last_group(here, coverage, offsets, weights, volume, sinogram, tv, *tokens):
     slabs = coverage.shape[0]
     depth, rows, cols = sinogram.shape
-    edges = [pl.BlockSpec((2 * rows, cols), lambda i, last=end.shape[0] // (2 * rows) - 1: (last, 0)) for end in ends]
-    return call(
-        functools.partial(patch_kernel, slabs),
-        3,
+    return call(
+        functools.partial(last_kernel, slabs),
+        0,
         vmem=32,
         grid=(1,),
-        in_specs=[SMEM, SMEM, SMEM, pl.BlockSpec(weights.shape, lambda i: (0, 0, 0))]
-        + edges
-        + [ANY] * (3 + len(tokens)),
+        in_specs=[SMEM, SMEM, SMEM, pl.BlockSpec(weights.shape, lambda i: (0, 0, 0))] + [ANY] * (3 + len(tokens)),
         out_specs=[ANY, ANY],
         results=[pltpu.HBM(sinogram.shape, BF16), pltpu.HBM(volume.shape, F32)],
-        input_output_aliases={10: 1},
+        input_output_aliases={6: 1},
         scratch_shapes=[
             pltpu.VMEM(volume.shape, F32),
             pltpu.VMEM(sinogram.shape, BF16),
             pltpu.VMEM(sinogram.shape, BF16),
             pltpu.VMEM((3, depth * rows, LANES), F32),
             pltpu.VMEM(volume.shape, F32),
-            pltpu.VMEM((4, rows, cols), F32),
-            pltpu.VMEM((2, rows, cols), F32),
-            pltpu.SemaphoreType.DMA((5,)),
+            pltpu.SemaphoreType.DMA((3,)),
         ],
-    )(here, coverage, offsets, weights, *ends, far(volume), far(sinogram), far(tv), *tokens)
+    )(here, coverage, offsets, weights, far(volume), far(sinogram), far(tv), *tokens)
 
 
 def natural(place, in_refs, wide, j):
@@ -408,7 +387,7 @@
     shape = (G * side, (2 * G + 1) * side)
     return call(
         functools.partial(band_kernel, slabs, span),
-        1.6,
+        9,
         in_specs=[SMEM, SMEM, SMEM, pl.BlockSpec(weights.shape, lambda i: (0, 0, 0))] + [ANY] * len(tokens),
         grid=(1,),
         out_specs=[pl.BlockSpec(shape, lambda i: (0, 0))] * 2,
@@ -446,7 +425,7 @@
         + [ANY] * len(tokens),
         out_specs=[across(shape, tile) for shape in shapes],
         results=[value(shape, BF16) for shape in shapes],
-    )(here, far(band), own, high, low, *arrays_of(sinos), *tokens)
+    )(here, far(band), far(own), high, low, *arrays_of(sinos), *tokens)
 
 
 def back_kernel(dealing, band_ref, own_ref, low_ref, high_ref, *refs):
@@ -505,37 +484,45 @@
     return (below_flux - fz) + (fy_low - fy) + (fx_low - fx), fz
 
 
-def tv_kernel(next_ref, vol_ref, *refs):
+def tv_kernel(here_ref, near_ref, next_level_ref, far_ref, last_level_ref, next_ref, vol_ref, *refs):
     out_ref, done_ref, flux_ref = refs[-3:]
-    deep = vol_ref.shape[0]
-
-    @pl.when(pl.program_id(0) == 0)
+    step = pl.program_id(0)
+    deep, rows, _ = vol_ref.shape
+    place = lax.rem(here_ref[0], G)
+
+    @pl.when(step == 0)
     def _():
-        flux_ref[...] = jnp.zeros_like(flux_ref)
+        inside = jnp.where(place == 2, far_ref[...], near_ref[...])
+        low = jnp.where(place == 0, last_level_ref[...], inside)[rows:].astype(F32)
+        flux_ref[...] = tv_below(low, vol_ref[0])
 
     def body(z, flux):
         out_ref[z], flux = tv_slice(vol_ref[z], vol_ref[z + 1], flux)
         return flux
 
     flux = lax.fori_loop(0, deep - 1, body, flux_ref[...], unroll=5)
-    out_ref[deep - 1], flux_ref[...] = tv_slice(vol_ref[deep - 1], next_ref[0], flux)
+    inside = jnp.where(place == 1, far_ref[...], near_ref[...])
+    high = jnp.where(place == G - 1, next_level_ref[...], inside)[:rows].astype(F32)
+    above = jnp.where(step == pl.num_programs(0) - 1, high, next_ref[0])
+    out_ref[deep - 1], flux_ref[...] = tv_slice(vol_ref[deep - 1], above, flux)
     done_ref[...] = flux_ref[:, : done_ref.shape[1]]
 
 
-def half_tv(volume, *tokens):
+def half_tv(here, volume, ends, *tokens):
     depth, rows, cols = volume.shape
     deep = 16
+    edges = [pl.BlockSpec((2 * rows, cols), lambda i, last=end.shape[0] // (2 * rows) - 1: (last, 0)) for end in ends]
     body = pl.BlockSpec((deep, rows, cols), lambda i: (i, 0, 0))
     after = pl.BlockSpec((1, rows, cols), lambda i: (jnp.minimum((i + 1) * deep, depth - 1), 0, 0))
     return call(
         tv_kernel,
-        9,
+        0,
         grid=(depth // deep,),
-        in_specs=[after, body] + [ANY] * len(tokens),
+        in_specs=[SMEM] + edges + [after, body] + [ANY] * len(tokens),
         out_specs=[body, pl.BlockSpec((rows, LANES), lambda i: (0, 0))],
         results=[pltpu.HBM(volume.shape, F32), value((rows, LANES), F32)],
         scratch_shapes=[pltpu.VMEM((rows, cols), F32)],
-    )(far(volume), far(volume), *tokens)
+    )(here, *ends, far(volume), far(volume), *tokens)
 
 
 def local(volume, sinogram, weights, coverage, offsets):
@@ -552,29 +539,28 @@
         return swapped(tied(over, *others)[depth:], 1)
 
     vols0 = cast_rows(here, volume, 0, single, True)
-    v0, v1, v23 = cast_rows(here, volume, 1, paired, False, vols0[1])
     got = moved(tied(sinogram, vols0[0]), G, only=G - 1)
     got_vols0 = direct(vols0)
+    v0, v1, v23 = cast_rows(here, volume, 1, paired, False, vols0[1])
     over = swapped(v23, 2)
-    tv, tv_done = half_tv(volume, v1)
-    own0, edge0 = pack(here, [(array, 0) for array in got_vols0], 2 * rows, tv_done)
+    band_p, band_b = bands(here, coverage, offsets, weights, v1)
+    own0, edge0 = pack(here, [(array, 0) for array in got_vols0], 2 * rows, far(band_p))
     high0, near = moved(own0, -G), swapped(tied(v1, own0), 1)
-    band_p, band_b = bands(here, coverage, offsets, weights, own0)
-    sino0 = split_rows(here, sinogram, got, 0, single, [], band_p, near)
+    *sino0, over_beyond = split_rows(here, sinogram, got, 0, single, [(over, 1)], near)
     sinos0 = [(array, 0) for array in direct(sino0)]
     low0 = moved(tied(edge0, sinos0[1][0]), G)
-    own1, edge1 = pack(here, [(v0, 0), (near, 0), (over, 0), (beyond(over, sinos0[1][0]), 0)], 0)
+    own1, edge1 = pack(here, [(v0, 0), (near, 0), (over, 0), (swapped(over_beyond, 1), 0)], 0)
     low1, high1 = moved(edge1, G), moved(own1, -G)
-    s0, s1, s23 = split_rows(here, sinogram, got, 1, paired, [], own1)
+
+    s0, s1, s23 = split_rows(here, sinogram, got, 1, paired, [], far(own1))
 
     resid0, down0, r1, r23 = project(here, band_p, own0, high0, low0, sinos0, paired[1:], low1, s0)
     from_low0, from_high0 = moved(resid0, G), moved(down0, -G)
     s_near, s_over = swapped(s1, 1), swapped(s23, 2)
-    ends = [got_vols0[1], high0, got_vols0[3], low0]
-    r_last, tv = patch(here, coverage, offsets, weights, ends, volume, sinogram, tv, resid0)
-    sinos1 = [(s0, 0), (s_near, 0), (s_over, 0), (beyond(s_over, r_last), 0)]
     r_near, r_over = swapped(tied(r1, s_near), 1), swapped(tied(r23, s_near), 2)
-    resid1, down1 = project(here, band_p, own1, high1, low1, sinos1, (), r_last, r_near, r_over)
+    tv, tv_done = half_tv(here, volume, [got_vols0[1], high0, got_vols0[3], low0], resid0)
+    sinos1 = [(s0, 0), (s_near, 0), (s_over, 0), (beyond(s_over, tv_done), 0)]
+    resid1, down1 = project(here, band_p, own1, high1, low1, sinos1, (), tv_done, r_near, r_over)
     from_low1, from_high1 = moved(resid1, G), moved(down1, -G)
 
     backs0 = back(band_b, resid0, from_low0, from_high0, [resid1])
@@ -582,13 +568,14 @@
     r_pieces = [(resid0, 0), (r_near, 0), (r_over, 0), (beyond(r_over, got_backs0[1]), 0)]
     natural0 = join_rows(here, r_pieces, sinogram.shape, backs0[0])
     above0 = moved(natural0, -G, only=G - 1)
-    backs1 = back(band_b, resid1, from_low1, from_high1, [], natural0)
+    r_last, tv = last_group(here, coverage, offsets, weights, volume, sinogram, tv, natural0)
+    backs1 = back(band_b, resid1, from_low1, from_high1, [], far(r_last))
     got_backs1 = direct(backs1)
     natural1 = join_rows(here, [(array, 1) for array in got_backs0], sinogram.shape, backs1[0])
     above1 = moved(natural1, -G, only=G - 1)
     gradient = finish(here, 0, tv, [(array, 0) for array in got_backs0], natural1)
     residual = settle(here, slabs, [(natural0, above0), (natural1, above1)], r_last)
-    gradient = finish(here, 1, gradient, [(array, 0) for array in got_backs1], residual)
+    gradient = finish(here, 1, gradient, [(array, 0) for array in got_backs1], far(residual))
     return (gradient, residual)
 
 

time: 145 us -> 153 us (1.055)
  waiting for transfers between devices: 31.1 us -> 41.4 us
  local copies, waits for them, and re-layouts: 7.15 us -> 2.54 us
  starting transfers between devices: 38.9 us -> 41.7 us
    ppermute x11, waiting for transfers between devices: 22.9 us -> 29.6 us  [moved(): return lax.ppermute(value, 'slab', pairs)]
    unnamed x28 -> x18, local copies, waits for them, and re-layouts: 7.1 us -> 2.5 us
    ppermute x21, waiting for transfers between devices: 8.18 us -> 11.8 us  [swapped(): return lax.ppermute(value, 'slab', [(i, i ^ bits) for i in range(count)])]
    pallas_call x3, Pallas kernels: 28.1 us -> 26.5 us  [the longest x1 13.8 us: last_group(): call(functools.partial(last_kernel, slabs), 0, vmem=32, grid=(1,), in_spe...]
    pallas_call x2, Pallas kernels: 2.63 us -> 4.22 us  [pack(): call(pack_kernel, 1, grid=(cols // tile,), in_specs=[SMEM] + specs + [ANY...]
  transfers between devices with their start and end apart: 32 -> 32, of which waited for: 10 -> 8; matrix products, arithmetic and copies ran while one was open for 0% -> 1% of each run, Pallas kernels for 42% -> 39%
where the time goes in v10:
time: 153 us; the launch traced here: 152 us
  Pallas kernels  65.9 us (43%)
  starting transfers between devices  41.7 us (27%)
  waiting for transfers between devices  41.4 us (27%)
  local copies, waits for them, and re-layouts  2.54 us (2%)
    ppermute x11, waiting for transfers between devices, moved(): return lax.ppermute(value, 'slab', pairs)  29.6 us
    ppermute x11, starting transfers between devices, moved(): return lax.ppermute(value, 'slab', pairs)  25.1 us
    ppermute x21, starting transfers between devices, swapped(): return lax.ppermute(value, 'slab', [(i, i ^ bits) for i in range(count)])  16.6 us
    pallas_call x1, Pallas kernels, last_group(): call(functools.partial(last_kernel, slabs), 0, vmem=32, grid=(1,), in_spe...  13.8 us
    ppermute x21, waiting for transfers between devices, swapped(): return lax.ppermute(value, 'slab', [(i, i ^ bits) for i in range(count)])  11.8 us
    pallas_call x1, Pallas kernels, half_tv(): call(tv_kernel, 0, grid=(depth // deep,), in_specs=[SMEM] + edges + [afte...  9.98 us
    pallas_call x2, Pallas kernels, project(): call(functools.partial(project_kernel, groups), 3, grid=(cols // tile,),...  6.7 us
    pallas_call x2, Pallas kernels, back(): call(functools.partial(back_kernel, bool(dealt)), 0, grid=(cols // tile,)...  6.47 us
  transfers between devices with their start and end apart: 32, of which 8 were waited for; matrix products, arithmetic and copies ran while one was open for 1% of the time, Pallas kernels for 39%

profile of v10, /device:TPU:29, one launch (start us, length us, event | category | flops | bytes accessed | tf_op | source)
XLA Modules:
  0.0 152.5 jit_solution(9446112051132616214)
XLA Ops:
  0.6 2.5 %shard_map.68 = (bf16[128,1024]{1,0:T(8,128)(2,1)}, bf16[144,1024]{1,0:T(8,128)(2,1)S(1)}, bf16[128,1024]{1,0:T(8,128)(2,1)}, bf16[144,1024]{1,0:T(8,128)(2,1)S(1)}) custom-call(s32[1]{0:T(128)} %bitcast.here_ref, f32[1024,1024]{1,0:T(8,128)} %bitcast.2, f32[1024,1024]{1,0:T(8,128)} %bitcast.3, f32[1024,1024]{1,0:T(8,128)} %bitcast.4, f32[1024,1024]{1,0:T(8,128)} %bitcast.5), custom_call_target="tpu_custom_call" | custom-call | flops 2300000000 | bytes 1000 | tf_op jit(solution)/shard_map/pallas_call | solution.py:110
  3.2 1.3 collective-permute-start.4
  4.9 1.5 collective-permute-start.1
  6.4 2.5 %shard_map.69 = (bf16[128,1024]{1,0:T(8,128)(2,1)}, bf16[128,1024]{1,0:T(8,128)(2,1)S(1)}, bf16[256,1024]{1,0:T(8,128)(2,1)}) custom-call(s32[1]{0:T(128)} %bitcast.here_ref, f32[1024,1024]{1,0:T(8,128)} %bitcast.6, f32[1024,1024]{1,0:T(8,128)} %bitcast.7, bf16[144,1024]{1,0:T(8,128)(2,1)S(1)} %get-tuple-element.48.refs_2_), custom_call_target="tpu_custom_call" | custom-call | flops 2300000000 | bytes 1000 | tf_op jit(solution)/shard_map/pallas_call | solution.py:110
  8.9 0.7 copy-done.3
  9.7 0.8 copy.13.offset_ref
  10.5 0.9 copy-done.4
  11.5 2.7 %shard_map.70 = (bf16[512,1152]{1,0:T(8,128)(2,1)}, bf16[512,1152]{1,0:T(8,128)(2,1)}) custom-call(s32[1]{0:T(128)} %bitcast.here_ref, s32[16,6]{1,0:T(8,128)S(1)} %copy.12.cover_ref, s32[16,6]{1,0:T(8,128)S(1)} %copy.13.offset_ref, bf16[8,128,128]{2,1,0:T(8,128)(2,1)S(1)} %copy-done, bf16[128,1024]{1,0:T(8,128)(2,1)S(1)} %copy-done.4), custom_call_target="tpu_custom_call" | custom-call | flops 10350000128 | bytes 1000 | tf_op jit(solution)/shard_map/pallas_call | solution.py:388
  14.1 5.2 %collective-permute-done.1.refs_2_ = bf16[128,1024]{1,0:T(8,128)(2,1)} collective-permute-done((bf16[128,1024]{1,0:T(8,128)(2,1)}, bf16[128,1024]{1,0:T(8,128)(2,1)}, u32[]{:S(2)}, u32[]{:S(2)}) %collective-permute-start.1) | collective-permute-done | bytes 262176 | tf_op jit(solution)/shard_map/ppermute | solution.py:32
  19.3 2.1 %shard_map.71 = (bf16[528,1024]{1,0:T(8,128)(2,1)}, bf16[144,1024]{1,0:T(8,128)(2,1)}) custom-call(s32[1]{0:T(128)} %bitcast.here_ref, bf16[128,1024]{1,0:T(8,128)(2,1)S(1)} %copy-done.2, bf16[144,1024]{1,0:T(8,128)(2,1)S(1)} %collective-permute-done.refs_1_.near_ref, bf16[128,1024]{1,0:T(8,128)(2,1)} %collective-permute-done.1.refs_2_, ...), custom_call_target="tpu_custom_call" | custom-call | flops 1150000000 | bytes 1000 | tf_op jit(solution)/shard_map/pallas_call | solution.py:147
  21.5 4.2 %collective-permute-start.3 = (bf16[528,1024]{1,0:T(8,128)(2,1)}, bf16[528,1024]{1,0:T(8,128)(2,1)S(1)}, u32[]{:S(2)}, u32[]{:S(2)}) collective-permute-start(bf16[528,1024]{1,0:T(8,128)(2,1)} %get-tuple-element.54.own_ref), channel_id=1, source_target_pairs={{4,0},{5,1},{6,2},{7,3},{8,4},{9,5},{10,6},{11,7},{12,8},{13,9},{1... | collective-permute-start | bytes 3244040 | tf_op jit(solution)/shard_map/ppermute | solution.py:27
  25.7 1.3 collective-permute-start.6
  27.0 3.6 %collective-permute-done.5.refs_0_.refs_2_ = bf16[256,1024]{1,0:T(8,128)(2,1)} collective-permute-done((bf16[256,1024]{1,0:T(8,128)(2,1)}, bf16[256,1024]{1,0:T(8,128)(2,1)}, u32[]{:S(2)}, u32[]{:S(2)}) %collective-permute-start.5) | collective-permute-done | bytes 524320 | tf_op jit(solution)/shard_map/ppermute | solution.py:32
  30.6 1.8 %shard_map.72 = (bf16[128,1024]{1,0:T(8,128)(2,1)S(1)}, bf16[128,1024]{1,0:T(8,128)(2,1)S(1)}, bf16[128,1024]{1,0:T(8,128)(2,1)S(1)}, bf16[128,1024]{1,0:T(8,128)(2,1)S(1)}, bf16[128,1024]{1,0:T(8,128)(2,1)S(1)}) custom-call(s32[1]{0:T(128)} %bitcast.here_ref, bf16[128,8,1024]{2,1,0:T(8,128)(2,1)} %refs_2_.1, ...), custom_call_target="tpu_custom_call" | custom-call | flops 2300000000 | bytes 1000 | tf_op jit(solution)/shard_map/pallas_call | solution.py:189
  32.4 0.8 collective-permute-start.7
  33.5 1.5 collective-permute-start.9
  35.1 1.3 collective-permute-start.8
  36.4 2.1 %shard_map.73 = (bf16[512,1024]{1,0:T(8,128)(2,1)}, bf16[128,1024]{1,0:T(8,128)(2,1)}) custom-call(s32[1]{0:T(128)} %bitcast.here_ref, bf16[128,1024]{1,0:T(8,128)(2,1)S(1)} %copy-done.1, bf16[128,1024]{1,0:T(8,128)(2,1)S(1)} %collective-permute-done.6.refs_1_, bf16[256,1024]{1,0:T(8,128)(2,1)} %collective-permute-done.5.refs_0_.refs_2_, ...), custom_call_target="tpu_custom_call" | custom-call | flops 1150000000 | bytes 1000 | tf_op jit(solution)/shard_map/pallas_call | solution.py:147
  38.5 1.3 collective-permute-start.12
  39.8 8.4 %collective-permute-done.3.high_ref.next_level_ref = bf16[528,1024]{1,0:T(8,128)(2,1)S(1)} collective-permute-done((bf16[528,1024]{1,0:T(8,128)(2,1)}, bf16[528,1024]{1,0:T(8,128)(2,1)S(1)}, u32[]{:S(2)}, u32[]{:S(2)}) %collective-permute-start.3) | collective-permute-done | bytes 1081376 | tf_op jit(solution)/shard_map/ppermute | solution.py:27
  48.2 4.1 %collective-permute-start.18 = (bf16[512,1024]{1,0:T(8,128)(2,1)}, bf16[512,1024]{1,0:T(8,128)(2,1)S(1)}, u32[]{:S(2)}, u32[]{:S(2)}) collective-permute-start(bf16[512,1024]{1,0:T(8,128)(2,1)} %get-tuple-element.67.refs_0_.own_ref), channel_id=1, source_target_pairs={{4,0},{5,1},{6,2},{7,3},{8,4},{9,5},{10,6},{11,7},{12,8},{13,9},{1... | collective-permute-start | bytes 3145736 | tf_op jit(solution)/shard_map/ppermute | solution.py:27
  52.3 1.7 %shard_map.74 = (bf16[128,1024]{1,0:T(8,128)(2,1)S(1)}, bf16[128,1024]{1,0:T(8,128)(2,1)S(1)}, bf16[256,1024]{1,0:T(8,128)(2,1)S(1)}) custom-call(s32[1]{0:T(128)} %bitcast.here_ref, bf16[128,8,1024]{2,1,0:T(8,128)(2,1)} %refs_2_.1, bf16[128,8,1024]{2,1,0:T(8,128)(2,1)S(1)} %collective-permute-done.4.got_ref, bf16[512,1024]{1,0:T(8,128)(2,1)} %get-tuple-element.67.refs_0_.own_ref), custom_call_target="tpu_custom_call" | custom-call | flops 2300000000 | bytes 1000 | tf_op jit(solution)/shard_map/pallas_call | solution.py:189
  54.1 2.2 %collective-permute-start.13 = (bf16[128,1024]{1,0:T(8,128)(2,1)S(1)}, bf16[128,1024]{1,0:T(8,128)(2,1)S(1)}, u32[]{:S(2)}, u32[]{:S(2)}) collective-permute-start(bf16[128,1024]{1,0:T(8,128)(2,1)S(1)} %get-tuple-element.72), channel_id=1, source_target_pairs={{0,1},{1,0},{2,3},{3,2},{4,5},{5,4},{6,7},{7,6},{8,9},{9,8},{10,11... | collective-permute-start | bytes 786440 | tf_op jit(solution)/shard_map/ppermute | solution.py:32
  56.3 3.4 %shard_map.75 = (bf16[512,1024]{1,0:T(8,128)(2,1)S(1)}, bf16[128,1024]{1,0:T(8,128)(2,1)S(1)}, bf16[128,1024]{1,0:T(8,128)(2,1)S(1)}, bf16[256,1024]{1,0:T(8,128)(2,1)S(1)}) custom-call(s32[1]{0:T(128)} %bitcast.here_ref, bf16[512,1152]{1,0:T(8,128)(2,1)} %get-tuple-element.53.refs_4_.band_ref, bf16[528,1024]{1,0:T(8,128)(2,1)} %get-tuple-element.54.own_ref, ...), custom_call_target="tpu_custom_call" | custom-call | flops 3449999872 | bytes 1000 | tf_op jit(solution)/shard_map/pallas_call | solution.py:419
  59.7 1.7 %collective-permute-start.15 = (bf16[256,1024]{1,0:T(8,128)(2,1)S(1)}, bf16[256,1024]{1,0:T(8,128)(2,1)S(1)}, u32[]{:S(2)}, u32[]{:S(2)}) collective-permute-start(bf16[256,1024]{1,0:T(8,128)(2,1)S(1)} %get-tuple-element.75), channel_id=1, source_target_pairs={{0,2},{1,3},{2,0},{3,1},{4,6},{5,7},{6,4},{7,5},{8,10},{9,11},{10,... | collective-permute-start | bytes 1572872 | tf_op jit(solution)/shard_map/ppermute | solution.py:32
  61.4 1.3 collective-permute-start.16
  63.1 10.0 %shard_map.76 = (f32[128,8,1024]{2,1,0:T(8,128)}, f32[8,128]{1,0:T(8,128)S(1)}) custom-call(s32[1]{0:T(128)} %bitcast.here_ref, bf16[144,1024]{1,0:T(8,128)(2,1)S(1)} %collective-permute-done.refs_1_.near_ref, bf16[528,1024]{1,0:T(8,128)(2,1)S(1)} %collective-permute-done.3.high_ref.next_level_ref, ...), custom_call_target="tpu_custom_call" | custom-call | bytes 1000 | tf_op jit(solution)/shard_map/pallas_call | solution.py:517
  73.3 4.1 %collective-permute-start.17 = (bf16[128,1024]{1,0:T(8,128)(2,1)S(1)}, bf16[128,1024]{1,0:T(8,128)(2,1)S(1)}, u32[]{:S(2)}, u32[]{:S(2)}) collective-permute-start(bf16[128,1024]{1,0:T(8,128)(2,1)S(1)} %get-tuple-element.77), channel_id=1, source_target_pairs={{4,0},{5,1},{6,2},{7,3},{8,4},{9,5},{10,6},{11,7},{12,8},{13,9},{1... | collective-permute-start | bytes 786440 | tf_op jit(solution)/shard_map/ppermute | solution.py:27
  77.5 3.3 %shard_map.77 = (bf16[512,1024]{1,0:T(8,128)(2,1)S(1)}, bf16[128,1024]{1,0:T(8,128)(2,1)S(1)}) custom-call(s32[1]{0:T(128)} %bitcast.here_ref, bf16[512,1152]{1,0:T(8,128)(2,1)} %get-tuple-element.53.refs_4_.band_ref, bf16[512,1024]{1,0:T(8,128)(2,1)} %get-tuple-element.67.refs_0_.own_ref, bf16[512,1024]{1,0:T(8,128)(2,1)S(1)} %collective-permute-done.18.high_ref, ...), custom_call_target="tpu_custom_call" | custom-call | flops 3449999872 | bytes 1000 | tf_op jit(solution)/shard_map/pallas_call | solution.py:419
  80.8 1.3 collective-permute-start.25
  82.6 5.1 %collective-permute-done.16.low_ref = bf16[512,1024]{1,0:T(8,128)(2,1)S(1)} collective-permute-done((bf16[512,1024]{1,0:T(8,128)(2,1)S(1)}, bf16[512,1024]{1,0:T(8,128)(2,1)S(1)}, u32[]{:S(2)}, u32[]{:S(2)}) %collective-permute-start.16) | collective-permute-done | bytes 1048608 | tf_op jit(solution)/shard_map/ppermute | solution.py:27
  87.7 3.3 %shard_map.78 = (bf16[256,1024]{1,0:T(8,128)(2,1)S(1)}, bf16[256,1024]{1,0:T(8,128)(2,1)S(1)}, bf16[256,1024]{1,0:T(8,128)(2,1)S(1)}, bf16[256,1024]{1,0:T(8,128)(2,1)S(1)}) custom-call(bf16[512,1152]{1,0:T(8,128)(2,1)} %get-tuple-element.76.band_ref, bf16[512,1024]{1,0:T(8,128)(2,1)S(1)} %get-tuple-element.69.refs_0_.own_ref, ...), custom_call_target="tpu_custom_call" | custom-call | bytes 1000 | tf_op jit(solution)/shard_map/pallas_call | solution.py:449
  91.1 1.9 %collective-permute-start.21 = (bf16[256,1024]{1,0:T(8,128)(2,1)S(1)}, bf16[256,1024]{1,0:T(8,128)(2,1)S(1)}, u32[]{:S(2)}, u32[]{:S(2)}) collective-permute-start(bf16[256,1024]{1,0:T(8,128)(2,1)S(1)} %get-tuple-element.82), channel_id=1, source_target_pairs={{0,1},{1,0},{2,3},{3,2},{4,5},{5,4},{6,7},{7,6},{8,9},{9,8},{10,11... | collective-permute-start | bytes 1572872 | tf_op jit(solution)/shard_map/ppermute | solution.py:32
  93.0 1.7 %collective-permute-start.24 = (bf16[256,1024]{1,0:T(8,128)(2,1)S(1)}, bf16[256,1024]{1,0:T(8,128)(2,1)S(1)}, u32[]{:S(2)}, u32[]{:S(2)}) collective-permute-start(bf16[256,1024]{1,0:T(8,128)(2,1)S(1)} %get-tuple-element.87), channel_id=1, source_target_pairs={{0,3},{1,2},{2,1},{3,0},{4,7},{5,6},{6,5},{7,4},{8,11},{9,10},{10,... | collective-permute-start | bytes 1572872 | tf_op jit(solution)/shard_map/ppermute | solution.py:32
  95.0 2.0 %collective-permute-start.26 = (bf16[128,1024]{1,0:T(8,128)(2,1)S(1)}, bf16[128,1024]{1,0:T(8,128)(2,1)S(1)}, u32[]{:S(2)}, u32[]{:S(2)}) collective-permute-start(bf16[128,1024]{1,0:T(8,128)(2,1)S(1)} %get-tuple-element.88), channel_id=1, source_target_pairs={{4,0},{5,1},{6,2},{7,3},{8,4},{9,5},{10,6},{11,7},{12,8},{13,9},{1... | collective-permute-start | bytes 786440 | tf_op jit(solution)/shard_map/ppermute | solution.py:27
  97.0 0.9 shard_map.79.refs_4_.refs_0_
  97.9 13.8 %shard_map.80 = (bf16[128,8,1024]{2,1,0:T(8,128)(2,1)}, f32[128,8,1024]{2,1,0:T(8,128)}) custom-call(s32[1]{0:T(128)} %bitcast.here_ref, s32[16,6]{1,0:T(8,128)S(1)} %copy.12.cover_ref, s32[16,6]{1,0:T(8,128)S(1)} %copy.13.offset_ref, bf16[8,128,128]{2,1,0:T(8,128)(2,1)S(1)} %copy-done, f32[128,8,1024]{2,1,0:T(8,128)} %refs_1_.1, ...), custom_call_target="tpu_custom_call", output_to_operand_aliasing={{1}: (6, {})} | custom-call | bytes 1000 | tf_op jit(solution)/shard_map/pallas_call | solution.py:241
  111.8 3.2 %shard_map.81 = (bf16[128,1024]{1,0:T(8,128)(2,1)S(1)}, bf16[128,1024]{1,0:T(8,128)(2,1)S(1)}, bf16[128,1024]{1,0:T(8,128)(2,1)S(1)}, bf16[128,1024]{1,0:T(8,128)(2,1)S(1)}) custom-call(bf16[512,1152]{1,0:T(8,128)(2,1)} %get-tuple-element.76.band_ref, bf16[512,1024]{1,0:T(8,128)(2,1)S(1)} %get-tuple-element.81.refs_0_.own_ref, ...), custom_call_target="tpu_custom_call" | custom-call | bytes 1000 | tf_op jit(solution)/shard_map/pallas_call | solution.py:449
  114.9 3.0 %collective-permute-done.24.refs_3_ = bf16[256,1024]{1,0:T(8,128)(2,1)S(1)} collective-permute-done((bf16[256,1024]{1,0:T(8,128)(2,1)S(1)}, bf16[256,1024]{1,0:T(8,128)(2,1)S(1)}, u32[]{:S(2)}, u32[]{:S(2)}) %collective-permute-start.24) | collective-permute-done | bytes 524320 | tf_op jit(solution)/shard_map/ppermute | solution.py:32
  117.9 0.8 shard_map.82.refs_4_.refs_2_
  118.7 2.1 %collective-permute-start.31 = (bf16[128,8,512]{2,1,0:T(8,128)(2,1)S(1)}, bf16[128,8,512]{2,1,0:T(8,128)(2,1)S(1)}, u32[]{:S(2)}, u32[]{:S(2)}) collective-permute-start(bf16[128,8,512]{2,1,0:T(8,128)(2,1)S(1)} %shard_map.82.refs_4_.refs_2_), channel_id=1, source_target_pairs={{7,3},{11,7},{15,11},{23,19},{27,23},{31,27}} | collective-permute-start | bytes 3145736 | tf_op jit(solution)/shard_map/ppermute | solution.py:27
  120.8 2.2 %collective-permute-start.30 = (bf16[128,8,512]{2,1,0:T(8,128)(2,1)S(1)}, bf16[128,8,512]{2,1,0:T(8,128)(2,1)S(1)}, u32[]{:S(2)}, u32[]{:S(2)}) collective-permute-start(bf16[128,8,512]{2,1,0:T(8,128)(2,1)S(1)} %shard_map.79.refs_4_.refs_0_), channel_id=1, source_target_pairs={{7,3},{11,7},{15,11},{23,19},{27,23},{31,27}} | collective-permute-start | bytes 3145736 | tf_op jit(solution)/shard_map/ppermute | solution.py:27
  123.2 2.0 %collective-permute-start.29 = (bf16[128,1024]{1,0:T(8,128)(2,1)S(1)}, bf16[128,1024]{1,0:T(8,128)(2,1)S(1)}, u32[]{:S(2)}, u32[]{:S(2)}) collective-permute-start(bf16[128,1024]{1,0:T(8,128)(2,1)S(1)} %get-tuple-element.93), channel_id=1, source_target_pairs={{0,3},{1,2},{2,1},{3,0},{4,7},{5,6},{6,5},{7,4},{8,11},{9,10},{10,... | collective-permute-start | bytes 786440 | tf_op jit(solution)/shard_map/ppermute | solution.py:32
  125.2 2.9 %shard_map.83.tv_ref = f32[128,8,1024]{2,1,0:T(8,128)} custom-call(s32[1]{0:T(128)} %bitcast.here_ref, f32[128,8,1024]{2,1,0:T(8,128)} %get-tuple-element.85.tv_ref, bf16[256,1024]{1,0:T(8,128)(2,1)S(1)} %get-tuple-element.84.refs_4_.refs_0_, bf16[256,1024]{1,0:T(8,128)(2,1)S(1)} %collective-permute-done.21.refs_1_, ...), custom_call_target="tpu_custom_call", output_to_operand_aliasing={{}: (1, {})} | custom-call | bytes 1000 | tf_op jit(solution)/shard_map/pallas_call | solution.py:340
  128.2 4.3 %collective-permute-done.31.refs_3_ = bf16[128,8,512]{2,1,0:T(8,128)(2,1)S(1)} collective-permute-done((bf16[128,8,512]{2,1,0:T(8,128)(2,1)S(1)}, bf16[128,8,512]{2,1,0:T(8,128)(2,1)S(1)}, u32[]{:S(2)}, u32[]{:S(2)}) %collective-permute-start.31) | collective-permute-done | bytes 1048608 | tf_op jit(solution)/shard_map/ppermute | solution.py:27
  132.5 11.2 %collective-permute-done.30.refs_1_ = bf16[128,8,512]{2,1,0:T(8,128)(2,1)S(1)} collective-permute-done((bf16[128,8,512]{2,1,0:T(8,128)(2,1)S(1)}, bf16[128,8,512]{2,1,0:T(8,128)(2,1)S(1)}, u32[]{:S(2)}, u32[]{:S(2)}) %collective-permute-start.30) | collective-permute-done | bytes 1048608 | tf_op jit(solution)/shard_map/ppermute | solution.py:27
  143.7 5.8 %shard_map.84.refs_4_ = bf16[128,8,1024]{2,1,0:T(8,128)(2,1)} custom-call(s32[1]{0:T(128)} %bitcast.here_ref, bf16[128,8,512]{2,1,0:T(8,128)(2,1)S(1)} %shard_map.79.refs_4_.refs_0_, bf16[128,8,512]{2,1,0:T(8,128)(2,1)S(1)} %collective-permute-done.30.refs_1_, bf16[128,8,512]{2,1,0:T(8,128)(2,1)S(1)} %shard_map.82.refs_4_.refs_2_, ...), custom_call_target="tpu_custom_call" | custom-call | bytes 1000 | tf_op jit(solution)/shard_map/pallas_call | solution.py:319
  149.5 3.0 %shard_map.85 = f32[128,8,1024]{2,1,0:T(8,128)} custom-call(s32[1]{0:T(128)} %bitcast.here_ref, f32[128,8,1024]{2,1,0:T(8,128)} %shard_map.83.tv_ref, bf16[128,1024]{1,0:T(8,128)(2,1)S(1)} %get-tuple-element.90.refs_4_.refs_0_, bf16[128,1024]{1,0:T(8,128)(2,1)S(1)} %collective-permute-done.27.refs_1_, ...), custom_call_target="tpu_custom_call", output_to_operand_aliasing={{}: (1, {})} | custom-call | bytes 1000 | tf_op jit(solution)/shard_map/pallas_call | solution.py:340
  (54 shorter events, 2.7 us)
Async XLA Ops:
  3.2 27.4 %collective-permute-start.4 = (bf16[128,8,1024]{2,1,0:T(8,128)(2,1)}, bf16[128,8,1024]{2,1,0:T(8,128)(2,1)S(1)}, u32[]{:S(2)}, u32[]{:S(2)}) collective-permute-start(bf16[128,8,1024]{2,1,0:T(8,128)(2,1)} %refs_2_.1), channel_id=1, source_target_pairs={{3,7},{7,11},{11,15},{19,23},{23,27},{27,31}} | collective-permute-start | bytes 6291464 | tf_op jit(solution)/shard_map/ppermute | solution.py:27
  4.4 14.9 %collective-permute-start = (bf16[144,1024]{1,0:T(8,128)(2,1)S(1)}, bf16[144,1024]{1,0:T(8,128)(2,1)S(1)}, u32[]{:S(2)}, u32[]{:S(2)}) collective-permute-start(bf16[144,1024]{1,0:T(8,128)(2,1)S(1)} %get-tuple-element.48.refs_2_), channel_id=1, source_target_pairs={{0,1},{1,0},{2,3},{3,2},{4,5},{5,4},{6,7},{7,6},{8,9},{9,8},{10,11... | collective-permute-start | bytes 884744 | tf_op jit(solution)/shard_map/ppermute | solution.py:32
  4.7 14.6 %collective-permute-start.2 = (bf16[144,1024]{1,0:T(8,128)(2,1)S(1)}, bf16[144,1024]{1,0:T(8,128)(2,1)S(1)}, u32[]{:S(2)}, u32[]{:S(2)}) collective-permute-start(bf16[144,1024]{1,0:T(8,128)(2,1)S(1)} %get-tuple-element.51), channel_id=1, source_target_pairs={{0,3},{1,2},{2,1},{3,0},{4,7},{5,6},{6,5},{7,4},{8,11},{9,10},{10,... | collective-permute-start | bytes 884744 | tf_op jit(solution)/shard_map/ppermute | solution.py:32
  4.9 4.8 %copy-start.6 = (s32[16,6]{0,1:T(8,128)S(1)}, s32[16,6]{0,1:T(8,128)}, u32[]{:S(2)}) copy-start(s32[16,6]{0,1:T(8,128)} %param.8) | copy-start | bytes 1156
  4.9 5.6 %copy-start = (bf16[8,128,128]{2,1,0:T(8,128)(2,1)S(1)}, bf16[8,128,128]{2,1,0:T(8,128)(2,1)}, u32[]{:S(2)}) copy-start(bf16[8,128,128]{2,1,0:T(8,128)(2,1)} %refs_0_.1) | copy-start | bytes 786436
  4.9 14.4 %collective-permute-start.1 = (bf16[128,1024]{1,0:T(8,128)(2,1)}, bf16[128,1024]{1,0:T(8,128)(2,1)}, u32[]{:S(2)}, u32[]{:S(2)}) collective-permute-start(bf16[128,1024]{1,0:T(8,128)(2,1)} %get-tuple-element.50), channel_id=1, source_target_pairs={{0,2},{1,3},{2,0},{3,1},{4,6},{5,7},{6,4},{7,5},{8,10},{9,11},{10,... | collective-permute-start | bytes 786440 | tf_op jit(solution)/shard_map/ppermute | solution.py:32
  8.9 0.7 copy-start.3
  9.6 21.0 %collective-permute-start.5 = (bf16[256,1024]{1,0:T(8,128)(2,1)}, bf16[256,1024]{1,0:T(8,128)(2,1)}, u32[]{:S(2)}, u32[]{:S(2)}) collective-permute-start(bf16[256,1024]{1,0:T(8,128)(2,1)} %get-tuple-element.57), channel_id=1, source_target_pairs={{0,2},{1,3},{2,0},{3,1},{4,6},{5,7},{6,4},{7,5},{8,10},{9,11},{10,... | collective-permute-start | bytes 1572872 | tf_op jit(solution)/shard_map/ppermute | solution.py:32
  10.5 1.0 copy-start.4
  11.5 7.9 %copy-start.2 = (bf16[128,1024]{1,0:T(8,128)(2,1)S(1)}, bf16[128,1024]{1,0:T(8,128)(2,1)}, u32[]{:S(2)}) copy-start(bf16[128,1024]{1,0:T(8,128)(2,1)} %get-tuple-element.49.refs_0_) | copy-start | bytes 786436
  19.3 6.4 %copy-start.5 = (bf16[128,1024]{1,0:T(8,128)(2,1)S(1)}, bf16[128,1024]{1,0:T(8,128)(2,1)}, u32[]{:S(2)}) copy-start(bf16[128,1024]{1,0:T(8,128)(2,1)} %copy-done.3) | copy-start | bytes 786436
  21.5 13.6 %copy-start.7 = (bf16[144,1024]{1,0:T(8,128)(2,1)S(1)}, bf16[144,1024]{1,0:T(8,128)(2,1)}, u32[]{:S(2)}) copy-start(bf16[144,1024]{1,0:T(8,128)(2,1)} %get-tuple-element.60) | copy-start | bytes 884740
  21.5 14.9 %copy-start.1 = (bf16[128,1024]{1,0:T(8,128)(2,1)S(1)}, bf16[128,1024]{1,0:T(8,128)(2,1)}, u32[]{:S(2)}) copy-start(bf16[128,1024]{1,0:T(8,128)(2,1)} %get-tuple-element.64.refs_0_) | copy-start | bytes 786436
  21.5 26.7 %collective-permute-start.3 = (bf16[528,1024]{1,0:T(8,128)(2,1)}, bf16[528,1024]{1,0:T(8,128)(2,1)S(1)}, u32[]{:S(2)}, u32[]{:S(2)}) collective-permute-start(bf16[528,1024]{1,0:T(8,128)(2,1)} %get-tuple-element.54.own_ref), channel_id=1, source_target_pairs={{4,0},{5,1},{6,2},{7,3},{8,4},{9,5},{10,6},{11,7},{12,8},{13,9},{1... | collective-permute-start | bytes 3244040 | tf_op jit(solution)/shard_map/ppermute | solution.py:27
  25.7 4.8 %collective-permute-start.6 = (bf16[128,1024]{1,0:T(8,128)(2,1)S(1)}, bf16[128,1024]{1,0:T(8,128)(2,1)S(1)}, u32[]{:S(2)}, u32[]{:S(2)}) collective-permute-start(bf16[128,1024]{1,0:T(8,128)(2,1)S(1)} %copy-done.5), channel_id=1, source_target_pairs={{0,1},{1,0},{2,3},{3,2},{4,5},{5,4},{6,7},{7,6},{8,9},{9,8},{10,11... | collective-permute-start | bytes 786440 | tf_op jit(solution)/shard_map/ppermute | solution.py:32
  32.4 2.7 %collective-permute-start.7 = (bf16[128,1024]{1,0:T(8,128)(2,1)S(1)}, bf16[128,1024]{1,0:T(8,128)(2,1)S(1)}, u32[]{:S(2)}, u32[]{:S(2)}) collective-permute-start(bf16[128,1024]{1,0:T(8,128)(2,1)S(1)} %get-tuple-element.59), channel_id=1, source_target_pairs={{0,1},{1,0},{2,3},{3,2},{4,5},{5,4},{6,7},{7,6},{8,9},{9,8},{10,11... | collective-permute-start | bytes 786440 | tf_op jit(solution)/shard_map/ppermute | solution.py:32
  33.2 3.2 %collective-permute-start.11 = (bf16[128,1024]{1,0:T(8,128)(2,1)S(1)}, bf16[128,1024]{1,0:T(8,128)(2,1)S(1)}, u32[]{:S(2)}, u32[]{:S(2)}) collective-permute-start(bf16[128,1024]{1,0:T(8,128)(2,1)S(1)} %get-tuple-element.65), channel_id=1, source_target_pairs={{0,1},{1,0},{2,3},{3,2},{4,5},{5,4},{6,7},{7,6},{8,9},{9,8},{10,11... | collective-permute-start | bytes 786440 | tf_op jit(solution)/shard_map/ppermute | solution.py:32
  33.3 20.8 %collective-permute-start.10 = (bf16[128,1024]{1,0:T(8,128)(2,1)S(1)}, bf16[128,1024]{1,0:T(8,128)(2,1)S(1)}, u32[]{:S(2)}, u32[]{:S(2)}) collective-permute-start(bf16[128,1024]{1,0:T(8,128)(2,1)S(1)} %get-tuple-element.63), channel_id=1, source_target_pairs={{0,3},{1,2},{2,1},{3,0},{4,7},{5,6},{6,5},{7,4},{8,11},{9,10},{10,... | collective-permute-start | bytes 786440 | tf_op jit(solution)/shard_map/ppermute | solution.py:32
  33.5 20.6 %collective-permute-start.9 = (bf16[128,1024]{1,0:T(8,128)(2,1)S(1)}, bf16[128,1024]{1,0:T(8,128)(2,1)S(1)}, u32[]{:S(2)}, u32[]{:S(2)}) collective-permute-start(bf16[128,1024]{1,0:T(8,128)(2,1)S(1)} %get-tuple-element.62), channel_id=1, source_target_pairs={{0,2},{1,3},{2,0},{3,1},{4,6},{5,7},{6,4},{7,5},{8,10},{9,11},{10,... | collective-permute-start | bytes 786440 | tf_op jit(solution)/shard_map/ppermute | solution.py:32
  35.1 21.2 %collective-permute-start.8 = (bf16[144,1024]{1,0:T(8,128)(2,1)S(1)}, bf16[144,1024]{1,0:T(8,128)(2,1)S(1)}, u32[]{:S(2)}, u32[]{:S(2)}) collective-permute-start(bf16[144,1024]{1,0:T(8,128)(2,1)S(1)} %copy-done.7), channel_id=1, source_target_pairs={{0,4},{1,5},{2,6},{3,7},{4,8},{5,9},{6,10},{7,11},{8,12},{9,13},{1... | collective-permute-start | bytes 884744 | tf_op jit(solution)/shard_map/ppermute | solution.py:27
  38.5 17.8 %collective-permute-start.12 = (bf16[128,1024]{1,0:T(8,128)(2,1)}, bf16[128,1024]{1,0:T(8,128)(2,1)S(1)}, u32[]{:S(2)}, u32[]{:S(2)}) collective-permute-start(bf16[128,1024]{1,0:T(8,128)(2,1)} %get-tuple-element.66), channel_id=1, source_target_pairs={{0,4},{1,5},{2,6},{3,7},{4,8},{5,9},{6,10},{7,11},{8,12},{9,13},{1... | collective-permute-start | bytes 786440 | tf_op jit(solution)/shard_map/ppermute | solution.py:27
  48.2 29.3 %collective-permute-start.18 = (bf16[512,1024]{1,0:T(8,128)(2,1)}, bf16[512,1024]{1,0:T(8,128)(2,1)S(1)}, u32[]{:S(2)}, u32[]{:S(2)}) collective-permute-start(bf16[512,1024]{1,0:T(8,128)(2,1)} %get-tuple-element.67.refs_0_.own_ref), channel_id=1, source_target_pairs={{4,0},{5,1},{6,2},{7,3},{8,4},{9,5},{10,6},{11,7},{12,8},{13,9},{1... | collective-permute-start | bytes 3145736 | tf_op jit(solution)/shard_map/ppermute | solution.py:27
  54.0 19.0 %collective-permute-start.19 = (bf16[256,1024]{1,0:T(8,128)(2,1)S(1)}, bf16[256,1024]{1,0:T(8,128)(2,1)S(1)}, u32[]{:S(2)}, u32[]{:S(2)}) collective-permute-start(bf16[256,1024]{1,0:T(8,128)(2,1)S(1)} %get-tuple-element.78), channel_id=1, source_target_pairs={{0,2},{1,3},{2,0},{3,1},{4,6},{5,7},{6,4},{7,5},{8,10},{9,11},{10,... | collective-permute-start | bytes 1572872 | tf_op jit(solution)/shard_map/ppermute | solution.py:32
  54.1 5.6 %collective-permute-start.13 = (bf16[128,1024]{1,0:T(8,128)(2,1)S(1)}, bf16[128,1024]{1,0:T(8,128)(2,1)S(1)}, u32[]{:S(2)}, u32[]{:S(2)}) collective-permute-start(bf16[128,1024]{1,0:T(8,128)(2,1)S(1)} %get-tuple-element.72), channel_id=1, source_target_pairs={{0,1},{1,0},{2,3},{3,2},{4,5},{5,4},{6,7},{7,6},{8,9},{9,8},{10,11... | collective-permute-start | bytes 786440 | tf_op jit(solution)/shard_map/ppermute | solution.py:32
  59.7 17.8 %collective-permute-start.15 = (bf16[256,1024]{1,0:T(8,128)(2,1)S(1)}, bf16[256,1024]{1,0:T(8,128)(2,1)S(1)}, u32[]{:S(2)}, u32[]{:S(2)}) collective-permute-start(bf16[256,1024]{1,0:T(8,128)(2,1)S(1)} %get-tuple-element.75), channel_id=1, source_target_pairs={{0,2},{1,3},{2,0},{3,1},{4,6},{5,7},{6,4},{7,5},{8,10},{9,11},{10,... | collective-permute-start | bytes 1572872 | tf_op jit(solution)/shard_map/ppermute | solution.py:32
  61.4 26.3 %collective-permute-start.16 = (bf16[512,1024]{1,0:T(8,128)(2,1)S(1)}, bf16[512,1024]{1,0:T(8,128)(2,1)S(1)}, u32[]{:S(2)}, u32[]{:S(2)}) collective-permute-start(bf16[512,1024]{1,0:T(8,128)(2,1)S(1)} %get-tuple-element.69.refs_0_.own_ref), channel_id=1, source_target_pairs={{0,4},{1,5},{2,6},{3,7},{4,8},{5,9},{6,10},{7,11},{8,12},{9,13},{1... | collective-permute-start | bytes 3145736 | tf_op jit(solution)/shard_map/ppermute | solution.py:27
  62.7 10.6 %collective-permute-start.14 = (bf16[128,1024]{1,0:T(8,128)(2,1)S(1)}, bf16[128,1024]{1,0:T(8,128)(2,1)S(1)}, u32[]{:S(2)}, u32[]{:S(2)}) collective-permute-start(bf16[128,1024]{1,0:T(8,128)(2,1)S(1)} %get-tuple-element.73), channel_id=1, source_target_pairs={{0,1},{1,0},{2,3},{3,2},{4,5},{5,4},{6,7},{7,6},{8,9},{9,8},{10,11... | collective-permute-start | bytes 786440 | tf_op jit(solution)/shard_map/ppermute | solution.py:32
  73.1 4.4 %collective-permute-start.20 = (bf16[128,1024]{1,0:T(8,128)(2,1)S(1)}, bf16[128,1024]{1,0:T(8,128)(2,1)S(1)}, u32[]{:S(2)}, u32[]{:S(2)}) collective-permute-start(bf16[128,1024]{1,0:T(8,128)(2,1)S(1)} %slice.6), channel_id=1, source_target_pairs={{0,1},{1,0},{2,3},{3,2},{4,5},{5,4},{6,7},{7,6},{8,9},{9,8},{10,11... | collective-permute-start | bytes 786440 | tf_op jit(solution)/shard_map/ppermute | solution.py:32
  73.3 9.3 %collective-permute-start.17 = (bf16[128,1024]{1,0:T(8,128)(2,1)S(1)}, bf16[128,1024]{1,0:T(8,128)(2,1)S(1)}, u32[]{:S(2)}, u32[]{:S(2)}) collective-permute-start(bf16[128,1024]{1,0:T(8,128)(2,1)S(1)} %get-tuple-element.77), channel_id=1, source_target_pairs={{4,0},{5,1},{6,2},{7,3},{8,4},{9,5},{10,6},{11,7},{12,8},{13,9},{1... | collective-permute-start | bytes 786440 | tf_op jit(solution)/shard_map/ppermute | solution.py:27
  80.8 30.9 %collective-permute-start.25 = (bf16[512,1024]{1,0:T(8,128)(2,1)S(1)}, bf16[512,1024]{1,0:T(8,128)(2,1)S(1)}, u32[]{:S(2)}, u32[]{:S(2)}) collective-permute-start(bf16[512,1024]{1,0:T(8,128)(2,1)S(1)} %get-tuple-element.81.refs_0_.own_ref), channel_id=1, source_target_pairs={{0,4},{1,5},{2,6},{3,7},{4,8},{5,9},{6,10},{7,11},{8,12},{9,13},{1... | collective-permute-start | bytes 3145736 | tf_op jit(solution)/shard_map/ppermute | solution.py:27
  91.1 3.6 %collective-permute-start.21 = (bf16[256,1024]{1,0:T(8,128)(2,1)S(1)}, bf16[256,1024]{1,0:T(8,128)(2,1)S(1)}, u32[]{:S(2)}, u32[]{:S(2)}) collective-permute-start(bf16[256,1024]{1,0:T(8,128)(2,1)S(1)} %get-tuple-element.82), channel_id=1, source_target_pairs={{0,1},{1,0},{2,3},{3,2},{4,5},{5,4},{6,7},{7,6},{8,9},{9,8},{10,11... | collective-permute-start | bytes 1572872 | tf_op jit(solution)/shard_map/ppermute | solution.py:32
  93.0 21.9 %collective-permute-start.23 = (bf16[256,1024]{1,0:T(8,128)(2,1)S(1)}, bf16[256,1024]{1,0:T(8,128)(2,1)S(1)}, u32[]{:S(2)}, u32[]{:S(2)}) collective-permute-start(bf16[256,1024]{1,0:T(8,128)(2,1)S(1)} %get-tuple-element.86), channel_id=1, source_target_pairs={{0,2},{1,3},{2,0},{3,1},{4,6},{5,7},{6,4},{7,5},{8,10},{9,11},{10,... | collective-permute-start | bytes 1572872 | tf_op jit(solution)/shard_map/ppermute | solution.py:32
  93.0 24.9 %collective-permute-start.24 = (bf16[256,1024]{1,0:T(8,128)(2,1)S(1)}, bf16[256,1024]{1,0:T(8,128)(2,1)S(1)}, u32[]{:S(2)}, u32[]{:S(2)}) collective-permute-start(bf16[256,1024]{1,0:T(8,128)(2,1)S(1)} %get-tuple-element.87), channel_id=1, source_target_pairs={{0,3},{1,2},{2,1},{3,0},{4,7},{5,6},{6,5},{7,4},{8,11},{9,10},{10,... | collective-permute-start | bytes 1572872 | tf_op jit(solution)/shard_map/ppermute | solution.py:32
  94.7 2.3 %collective-permute-start.22 = (bf16[128,1024]{1,0:T(8,128)(2,1)S(1)}, bf16[128,1024]{1,0:T(8,128)(2,1)S(1)}, u32[]{:S(2)}, u32[]{:S(2)}) collective-permute-start(bf16[128,1024]{1,0:T(8,128)(2,1)S(1)} %slice.7), channel_id=1, source_target_pairs={{0,1},{1,0},{2,3},{3,2},{4,5},{5,4},{6,7},{7,6},{8,9},{9,8},{10,11... | collective-permute-start | bytes 786440 | tf_op jit(solution)/shard_map/ppermute | solution.py:32
  95.0 16.8 %collective-permute-start.26 = (bf16[128,1024]{1,0:T(8,128)(2,1)S(1)}, bf16[128,1024]{1,0:T(8,128)(2,1)S(1)}, u32[]{:S(2)}, u32[]{:S(2)}) collective-permute-start(bf16[128,1024]{1,0:T(8,128)(2,1)S(1)} %get-tuple-element.88), channel_id=1, source_target_pairs={{4,0},{5,1},{6,2},{7,3},{8,4},{9,5},{10,6},{11,7},{12,8},{13,9},{1... | collective-permute-start | bytes 786440 | tf_op jit(solution)/shard_map/ppermute | solution.py:27
  118.7 13.7 %collective-permute-start.31 = (bf16[128,8,512]{2,1,0:T(8,128)(2,1)S(1)}, bf16[128,8,512]{2,1,0:T(8,128)(2,1)S(1)}, u32[]{:S(2)}, u32[]{:S(2)}) collective-permute-start(bf16[128,8,512]{2,1,0:T(8,128)(2,1)S(1)} %shard_map.82.refs_4_.refs_2_), channel_id=1, source_target_pairs={{7,3},{11,7},{15,11},{23,19},{27,23},{31,27}} | collective-permute-start | bytes 3145736 | tf_op jit(solution)/shard_map/ppermute | solution.py:27
  120.8 22.9 %collective-permute-start.30 = (bf16[128,8,512]{2,1,0:T(8,128)(2,1)S(1)}, bf16[128,8,512]{2,1,0:T(8,128)(2,1)S(1)}, u32[]{:S(2)}, u32[]{:S(2)}) collective-permute-start(bf16[128,8,512]{2,1,0:T(8,128)(2,1)S(1)} %shard_map.79.refs_4_.refs_0_), channel_id=1, source_target_pairs={{7,3},{11,7},{15,11},{23,19},{27,23},{31,27}} | collective-permute-start | bytes 3145736 | tf_op jit(solution)/shard_map/ppermute | solution.py:27
  123.0 26.5 %collective-permute-start.27 = (bf16[128,1024]{1,0:T(8,128)(2,1)S(1)}, bf16[128,1024]{1,0:T(8,128)(2,1)S(1)}, u32[]{:S(2)}, u32[]{:S(2)}) collective-permute-start(bf16[128,1024]{1,0:T(8,128)(2,1)S(1)} %get-tuple-element.91), channel_id=1, source_target_pairs={{0,1},{1,0},{2,3},{3,2},{4,5},{5,4},{6,7},{7,6},{8,9},{9,8},{10,11... | collective-permute-start | bytes 786440 | tf_op jit(solution)/shard_map/ppermute | solution.py:32
  123.1 26.4 %collective-permute-start.28 = (bf16[128,1024]{1,0:T(8,128)(2,1)S(1)}, bf16[128,1024]{1,0:T(8,128)(2,1)S(1)}, u32[]{:S(2)}, u32[]{:S(2)}) collective-permute-start(bf16[128,1024]{1,0:T(8,128)(2,1)S(1)} %get-tuple-element.92), channel_id=1, source_target_pairs={{0,2},{1,3},{2,0},{3,1},{4,6},{5,7},{6,4},{7,5},{8,10},{9,11},{10,... | collective-permute-start | bytes 786440 | tf_op jit(solution)/shard_map/ppermute | solution.py:32
  123.2 26.3 %collective-permute-start.29 = (bf16[128,1024]{1,0:T(8,128)(2,1)S(1)}, bf16[128,1024]{1,0:T(8,128)(2,1)S(1)}, u32[]{:S(2)}, u32[]{:S(2)}) collective-permute-start(bf16[128,1024]{1,0:T(8,128)(2,1)S(1)} %get-tuple-element.93), channel_id=1, source_target_pairs={{0,3},{1,2},{2,1},{3,0},{4,7},{5,6},{6,5},{7,4},{8,11},{9,10},{10,... | collective-permute-start | bytes 786440 | tf_op jit(solution)/shard_map/ppermute | solution.py:32

commit v11 on v10

--- a/solution.py
+++ b/solution.py
@@ -288,42 +288,48 @@
     )(here, *arrays_of(pieces), *tokens)
 
 
-def settle_kernel(slabs, count, here_ref, *refs):
-    in_refs, (base_ref, out_ref) = refs[: 2 * CHUNKS], refs[-2:]
+def settle_kernel(slabs, count, here_ref, own_ref, above_ref, *refs):
+    in_refs, (base_ref, out_ref, wide) = refs[:G], refs[-3:]
     step = pl.program_id(0)
     cols = out_ref.shape[2]
+    place = lax.rem(here_ref[0], G)
     last = here_ref[0] == slabs - 1
-    above = lax.rem(here_ref[0], G) == G - 1
 
     @pl.when(last)
     def _():
         pltpu.sync_copy(base_ref.at[:, :, pl.ds(pl.multiple_of(step * cols, cols), cols)], out_ref)
 
-    for c in range(CHUNKS):
-        for n in range(2):
-
-            @pl.when(jnp.logical_not(last) & (step // count == c) & (above == (n == 1)))
-            def _():
-                out_ref[...] = in_refs[c * 2 + n][...]
-
-
-def settle(here, slabs, own_above, base, *tokens):
+    @pl.when(jnp.logical_not(last) & (step < count) & (place == G - 1))
+    def _():
+        out_ref[...] = above_ref[...]
+
+    @pl.when(jnp.logical_not(last) & (step < count) & (place != G - 1))
+    def _():
+        out_ref[...] = own_ref[...]
+
+    @pl.when(jnp.logical_not(last) & (step >= count))
+    def _():
+        for j in range(cols // LANES):
+            out_ref[:, :, j * LANES : (j + 1) * LANES] = natural(place, in_refs, wide, j).astype(BF16)
+
+
+def settle(here, slabs, own, above, pieces, base, *tokens):
     depth, rows, cols = base.shape
     _, count = chunk_tiles(0, cols)
     block = (depth, rows, TILE)
-    specs = [
-        pl.BlockSpec(block, lambda i, c=c: (0, 0, jnp.clip(i - c * count, 0, count - 1)))
-        for c in range(CHUNKS)
-        for _ in range(2)
+    early = pl.BlockSpec(block, lambda i: (0, 0, jnp.minimum(i, count - 1)))
+    late = [
+        pl.BlockSpec((depth, ROWS * TILE), lambda i, at=at: (at, jnp.maximum(i - count, 0))) for _, at in pieces
     ]
     return call(
         functools.partial(settle_kernel, slabs, count),
         0,
         grid=(CHUNKS * count,),
-        in_specs=[SMEM] + specs + [ANY] * (len(tokens) + 1),
+        in_specs=[SMEM, early, early] + late + [ANY] * (len(tokens) + 1),
         out_specs=pl.BlockSpec(block, lambda i: (0, 0, i)),
         results=pltpu.HBM(base.shape, BF16),
-    )(here, *[array for pair in own_above for array in pair], *tokens, far(base))
+        scratch_shapes=[wide_tile(depth * rows)],
+    )(here, own, above, *arrays_of(pieces), *tokens, far(base))
 
 
 def finish_kernel(here_ref, tv_ref, *refs):
@@ -428,18 +434,20 @@
     )(here, far(band), far(own), high, low, *arrays_of(sinos), *tokens)
 
 
-def back_kernel(dealing, band_ref, own_ref, low_ref, high_ref, *refs):
+def back_kernel(dealing, here_ref, band_ref, own_ref, low_ref, high_ref, *refs):
     out_refs = refs[-G:]
     side = high_ref.shape[0]
     seeing = jnp.concatenate([own_ref[...], low_ref[...], high_ref[...]], axis=0)
     total = jnp.dot(band_ref[...], seeing, preferred_element_type=F32)
+    place = lax.rem(here_ref[0], G)
     for m, out_ref in enumerate(out_refs):
         out_ref[:side] = total[m * side : (m + 1) * side].astype(BF16)
         if dealing:
-            out_ref[side:] = refs[0][m * side : (m + 1) * side]
-
-
-def back(band, own, low, high, dealt, *tokens):
+            last = jnp.bitwise_xor(place, m) == G - 1
+            out_ref[side:] = jnp.where(last, refs[1][...], refs[0][m * side : (m + 1) * side])
+
+
+def back(here, band, own, low, high, dealt, *tokens):
     n, side = band.shape[0], band.shape[0] // G
     cols = own.shape[1]
     tile = 512
@@ -450,12 +458,12 @@
         functools.partial(back_kernel, bool(dealt)),
         0,
         grid=(cols // tile,),
-        in_specs=[pl.BlockSpec(band.shape, lambda i: (0, 0)), many, many, one]
-        + [many] * len(dealt)
+        in_specs=[SMEM, pl.BlockSpec(band.shape, lambda i: (0, 0)), many, many, one]
+        + ([many, one] if dealt else [])
         + [ANY] * len(tokens),
         out_specs=[across(out, tile)] * G,
         results=[value(out, BF16)] * G,
-    )(far(band), own, low, high, *dealt, *tokens)
+    )(here, far(band), own, low, high, *dealt, *tokens)
 
 
 def tv_flux(cur, above):
@@ -546,11 +554,12 @@
     band_p, band_b = bands(here, coverage, offsets, weights, v1)
     own0, edge0 = pack(here, [(array, 0) for array in got_vols0], 2 * rows, far(band_p))
     high0, near = moved(own0, -G), swapped(tied(v1, own0), 1)
-    *sino0, over_beyond = split_rows(here, sinogram, got, 0, single, [(over, 1)], near)
-    sinos0 = [(array, 0) for array in direct(sino0)]
-    low0 = moved(tied(edge0, sinos0[1][0]), G)
+    s0, s1, s23, over_beyond = split_rows(here, sinogram, got, 0, paired, [(over, 1)], near)
+    s_near, s_over = swapped(s1, 1), swapped(s23, 2)
+    low0 = moved(tied(edge0, s_near), G)
     own1, edge1 = pack(here, [(v0, 0), (near, 0), (over, 0), (swapped(over_beyond, 1), 0)], 0)
     low1, high1 = moved(edge1, G), moved(own1, -G)
+    sinos0 = [(s0, 0), (s_near, 0), (s_over, 0), (beyond(s_over, own1), 0)]
 
     s0, s1, s23 = split_rows(here, sinogram, got, 1, paired, [], far(own1))
 
@@ -563,18 +572,16 @@
     resid1, down1 = project(here, band_p, own1, high1, low1, sinos1, (), tv_done, r_near, r_over)
     from_low1, from_high1 = moved(resid1, G), moved(down1, -G)
 
-    backs0 = back(band_b, resid0, from_low0, from_high0, [resid1])
+    backs0 = back(here, band_b, resid0, from_low0, from_high0, [resid1, from_high1])
     got_backs0 = direct(backs0)
-    r_pieces = [(resid0, 0), (r_near, 0), (r_over, 0), (beyond(r_over, got_backs0[1]), 0)]
+    r_pieces = [(resid0, 0), (r_near, 0), (r_over, 0), (beyond(r_over, resid1), 0)]
     natural0 = join_rows(here, r_pieces, sinogram.shape, backs0[0])
     above0 = moved(natural0, -G, only=G - 1)
-    r_last, tv = last_group(here, coverage, offsets, weights, volume, sinogram, tv, natural0)
-    backs1 = back(band_b, resid1, from_low1, from_high1, [], far(r_last))
+    r_last, tv = last_group(here, coverage, offsets, weights, volume, sinogram, tv, backs0[0])
+    backs1 = back(here, band_b, resid1, from_low1, from_high1, [], far(r_last), natural0)
     got_backs1 = direct(backs1)
-    natural1 = join_rows(here, [(array, 1) for array in got_backs0], sinogram.shape, backs1[0])
-    above1 = moved(natural1, -G, only=G - 1)
-    gradient = finish(here, 0, tv, [(array, 0) for array in got_backs0], natural1)
-    residual = settle(here, slabs, [(natural0, above0), (natural1, above1)], r_last)
+    gradient = finish(here, 0, tv, [(array, 0) for array in got_backs0], backs1[0])
+    residual = settle(here, slabs, natural0, above0, [(array, 1) for array in got_backs0], r_last, backs1[0])
     gradient = finish(here, 1, gradient, [(array, 0) for array in got_backs1], far(residual))
     return (gradient, residual)
 

time: 153 us -> 137 us (0.90)
  the two profiles are of different devices: /device:TPU:29 before, /device:TPU:1 now
where the time goes in v11:
time: 137 us; the launch traced here: 136 us
  starting transfers between devices  49.1 us (36%)
  Pallas kernels  48.7 us (36%)
  waiting for transfers between devices  34.8 us (25%)
  local copies, waits for them, and re-layouts  2.56 us (2%)
    ppermute x21, starting transfers between devices, swapped(): return lax.ppermute(value, 'slab', [(i, i ^ bits) for i in range(count)])  27.8 us
    ppermute x21, waiting for transfers between devices, swapped(): return lax.ppermute(value, 'slab', [(i, i ^ bits) for i in range(count)])  26.3 us
    ppermute x10, starting transfers between devices, moved(): return lax.ppermute(value, 'slab', pairs)  21.3 us
    pallas_call x1, Pallas kernels, half_tv(): call(tv_kernel, 0, grid=(depth // deep,), in_specs=[SMEM] + edges + [afte...  10 us
    ppermute x10, waiting for transfers between devices, moved(): return lax.ppermute(value, 'slab', pairs)  8.49 us
    pallas_call x2, Pallas kernels, project(): call(functools.partial(project_kernel, groups), 3, grid=(cols // tile,),...  6.68 us
    pallas_call x2, Pallas kernels, back(): call(functools.partial(back_kernel, bool(dealt)), 0, grid=(cols // tile,)...  6.41 us
    pallas_call x2, Pallas kernels, finish(): call(finish_kernel, 0, grid=(count,), in_specs=[SMEM, part] + piece_specs...  5.85 us
  transfers between devices with their start and end apart: 31, of which 11 were waited for; matrix products, arithmetic and copies ran while one was open for 1% of the time, Pallas kernels for 32%

profile of v11, /device:TPU:1, one launch (start us, length us, event | category | flops | bytes accessed | tf_op | source)
XLA Modules:
  0.0 136.1 jit_solution(1056332186062289659)
XLA Ops:
  0.6 2.5 %shard_map.68 = (bf16[128,1024]{1,0:T(8,128)(2,1)}, bf16[144,1024]{1,0:T(8,128)(2,1)S(1)}, bf16[128,1024]{1,0:T(8,128)(2,1)}, bf16[144,1024]{1,0:T(8,128)(2,1)S(1)}) custom-call(s32[1]{0:T(128)} %bitcast.here_ref, f32[1024,1024]{1,0:T(8,128)} %bitcast.2, f32[1024,1024]{1,0:T(8,128)} %bitcast.3, f32[1024,1024]{1,0:T(8,128)} %bitcast.4, f32[1024,1024]{1,0:T(8,128)} %bitcast.5), custom_call_target="tpu_custom_call" | custom-call | flops 2300000000 | bytes 1000 | tf_op jit(solution)/shard_map/pallas_call | solution.py:110
  3.1 0.8 collective-permute-start.4
  4.1 4.6 %collective-permute-start.1 = (bf16[128,1024]{1,0:T(8,128)(2,1)}, bf16[128,1024]{1,0:T(8,128)(2,1)}, u32[]{:S(2)}, u32[]{:S(2)}) collective-permute-start(bf16[128,1024]{1,0:T(8,128)(2,1)} %get-tuple-element.50), channel_id=1, source_target_pairs={{0,2},{1,3},{2,0},{3,1},{4,6},{5,7},{6,4},{7,5},{8,10},{9,11},{10,... | collective-permute-start | bytes 786440 | tf_op jit(solution)/shard_map/ppermute | solution.py:32
  9.0 2.5 %shard_map.69 = (bf16[128,1024]{1,0:T(8,128)(2,1)}, bf16[128,1024]{1,0:T(8,128)(2,1)S(1)}, bf16[256,1024]{1,0:T(8,128)(2,1)}) custom-call(s32[1]{0:T(128)} %bitcast.here_ref, f32[1024,1024]{1,0:T(8,128)} %bitcast.6, f32[1024,1024]{1,0:T(8,128)} %bitcast.7, bf16[144,1024]{1,0:T(8,128)(2,1)S(1)} %get-tuple-element.48.refs_2_), custom_call_target="tpu_custom_call" | custom-call | flops 2300000000 | bytes 1000 | tf_op jit(solution)/shard_map/pallas_call | solution.py:110
  12.3 1.7 %collective-permute-start.5 = (bf16[256,1024]{1,0:T(8,128)(2,1)}, bf16[256,1024]{1,0:T(8,128)(2,1)}, u32[]{:S(2)}, u32[]{:S(2)}) collective-permute-start(bf16[256,1024]{1,0:T(8,128)(2,1)} %get-tuple-element.57), channel_id=1, source_target_pairs={{0,2},{1,3},{2,0},{3,1},{4,6},{5,7},{6,4},{7,5},{8,10},{9,11},{10,... | collective-permute-start | bytes 1572872 | tf_op jit(solution)/shard_map/ppermute | solution.py:32
  14.1 0.8 copy.13.offset_ref
  14.8 0.9 copy-done.4
  15.8 2.7 %shard_map.70 = (bf16[512,1152]{1,0:T(8,128)(2,1)}, bf16[512,1152]{1,0:T(8,128)(2,1)}) custom-call(s32[1]{0:T(128)} %bitcast.here_ref, s32[16,6]{1,0:T(8,128)S(1)} %copy.12.cover_ref, s32[16,6]{1,0:T(8,128)S(1)} %copy.13.offset_ref, bf16[8,128,128]{2,1,0:T(8,128)(2,1)S(1)} %copy-done, bf16[128,1024]{1,0:T(8,128)(2,1)S(1)} %copy-done.4), custom_call_target="tpu_custom_call" | custom-call | flops 10350000128 | bytes 1000 | tf_op jit(solution)/shard_map/pallas_call | solution.py:394
  18.5 3.9 %collective-permute-done.2.refs_3_.far_ref = bf16[144,1024]{1,0:T(8,128)(2,1)S(1)} collective-permute-done((bf16[144,1024]{1,0:T(8,128)(2,1)S(1)}, bf16[144,1024]{1,0:T(8,128)(2,1)S(1)}, u32[]{:S(2)}, u32[]{:S(2)}) %collective-permute-start.2) | collective-permute-done | bytes 294944 | tf_op jit(solution)/shard_map/ppermute | solution.py:32
  22.3 2.1 %shard_map.71 = (bf16[528,1024]{1,0:T(8,128)(2,1)}, bf16[144,1024]{1,0:T(8,128)(2,1)}) custom-call(s32[1]{0:T(128)} %bitcast.here_ref, bf16[128,1024]{1,0:T(8,128)(2,1)S(1)} %copy-done.2, bf16[144,1024]{1,0:T(8,128)(2,1)S(1)} %collective-permute-done.refs_1_.near_ref, bf16[128,1024]{1,0:T(8,128)(2,1)} %collective-permute-done.1.refs_2_, ...), custom_call_target="tpu_custom_call" | custom-call | flops 1150000000 | bytes 1000 | tf_op jit(solution)/shard_map/pallas_call | solution.py:147
  24.8 1.3 collective-permute-start.3
  26.1 6.8 %collective-permute-done.5.refs_0_.refs_2_ = bf16[256,1024]{1,0:T(8,128)(2,1)} collective-permute-done((bf16[256,1024]{1,0:T(8,128)(2,1)}, bf16[256,1024]{1,0:T(8,128)(2,1)}, u32[]{:S(2)}, u32[]{:S(2)}) %collective-permute-start.5) | collective-permute-done | bytes 524320 | tf_op jit(solution)/shard_map/ppermute | solution.py:32
  32.9 1.8 %shard_map.72 = (bf16[128,1024]{1,0:T(8,128)(2,1)S(1)}, bf16[128,1024]{1,0:T(8,128)(2,1)S(1)}, bf16[256,1024]{1,0:T(8,128)(2,1)S(1)}, bf16[128,1024]{1,0:T(8,128)(2,1)S(1)}) custom-call(s32[1]{0:T(128)} %bitcast.here_ref, bf16[128,8,1024]{2,1,0:T(8,128)(2,1)} %refs_2_.1, bf16[128,8,1024]{2,1,0:T(8,128)(2,1)S(1)} %collective-permute-done.4.got_ref, ...), custom_call_target="tpu_custom_call" | custom-call | flops 2300000000 | bytes 1000 | tf_op jit(solution)/shard_map/pallas_call | solution.py:189
  34.7 1.2 collective-permute-start.9
  35.9 1.5 %collective-permute-start.7 = (bf16[128,1024]{1,0:T(8,128)(2,1)S(1)}, bf16[128,1024]{1,0:T(8,128)(2,1)S(1)}, u32[]{:S(2)}, u32[]{:S(2)}) collective-permute-start(bf16[128,1024]{1,0:T(8,128)(2,1)S(1)} %get-tuple-element.59), channel_id=1, source_target_pairs={{0,1},{1,0},{2,3},{3,2},{4,5},{5,4},{6,7},{7,6},{8,9},{9,8},{10,11... | collective-permute-start | bytes 786440 | tf_op jit(solution)/shard_map/ppermute | solution.py:32
  37.4 1.2 collective-permute-done.7.refs_1_
  38.6 3.1 %collective-permute-start.8 = (bf16[144,1024]{1,0:T(8,128)(2,1)S(1)}, bf16[144,1024]{1,0:T(8,128)(2,1)S(1)}, u32[]{:S(2)}, u32[]{:S(2)}) collective-permute-start(bf16[144,1024]{1,0:T(8,128)(2,1)S(1)} %copy-done.7), channel_id=1, source_target_pairs={{0,4},{1,5},{2,6},{3,7},{4,8},{5,9},{6,10},{7,11},{8,12},{9,13},{1... | collective-permute-start | bytes 884744 | tf_op jit(solution)/shard_map/ppermute | solution.py:27
  41.7 2.1 %shard_map.73 = (bf16[512,1024]{1,0:T(8,128)(2,1)}, bf16[128,1024]{1,0:T(8,128)(2,1)}) custom-call(s32[1]{0:T(128)} %bitcast.here_ref, bf16[128,1024]{1,0:T(8,128)(2,1)S(1)} %copy-done.1, bf16[128,1024]{1,0:T(8,128)(2,1)S(1)} %collective-permute-done.6.refs_1_, bf16[256,1024]{1,0:T(8,128)(2,1)} %collective-permute-done.5.refs_0_.refs_2_, ...), custom_call_target="tpu_custom_call" | custom-call | flops 1150000000 | bytes 1000 | tf_op jit(solution)/shard_map/pallas_call | solution.py:147
  43.8 3.2 %collective-permute-start.12 = (bf16[128,1024]{1,0:T(8,128)(2,1)}, bf16[128,1024]{1,0:T(8,128)(2,1)S(1)}, u32[]{:S(2)}, u32[]{:S(2)}) collective-permute-start(bf16[128,1024]{1,0:T(8,128)(2,1)} %get-tuple-element.67), channel_id=1, source_target_pairs={{0,4},{1,5},{2,6},{3,7},{4,8},{5,9},{6,10},{7,11},{8,12},{9,13},{1... | collective-permute-start | bytes 786440 | tf_op jit(solution)/shard_map/ppermute | solution.py:27
  47.3 1.9 %collective-permute-start.11 = (bf16[128,1024]{1,0:T(8,128)(2,1)S(1)}, bf16[128,1024]{1,0:T(8,128)(2,1)S(1)}, u32[]{:S(2)}, u32[]{:S(2)}) collective-permute-start(bf16[128,1024]{1,0:T(8,128)(2,1)S(1)} %slice.9), channel_id=1, source_target_pairs={{0,1},{1,0},{2,3},{3,2},{4,5},{5,4},{6,7},{7,6},{8,9},{9,8},{10,11... | collective-permute-start | bytes 786440 | tf_op jit(solution)/shard_map/ppermute | solution.py:32
  49.2 1.3 collective-permute-start.15
  50.5 1.7 %shard_map.74 = (bf16[128,1024]{1,0:T(8,128)(2,1)S(1)}, bf16[128,1024]{1,0:T(8,128)(2,1)S(1)}, bf16[256,1024]{1,0:T(8,128)(2,1)S(1)}) custom-call(s32[1]{0:T(128)} %bitcast.here_ref, bf16[128,8,1024]{2,1,0:T(8,128)(2,1)} %refs_2_.1, bf16[128,8,1024]{2,1,0:T(8,128)(2,1)S(1)} %collective-permute-done.4.got_ref, bf16[512,1024]{1,0:T(8,128)(2,1)} %get-tuple-element.65.refs_0_.own_ref), custom_call_target="tpu_custom_call" | custom-call | flops 2300000000 | bytes 1000 | tf_op jit(solution)/shard_map/pallas_call | solution.py:189
  52.2 0.9 collective-permute-start.16
  53.5 1.3 collective-permute-start.17
  54.8 3.4 %shard_map.75 = (bf16[512,1024]{1,0:T(8,128)(2,1)S(1)}, bf16[128,1024]{1,0:T(8,128)(2,1)S(1)}, bf16[128,1024]{1,0:T(8,128)(2,1)S(1)}, bf16[256,1024]{1,0:T(8,128)(2,1)S(1)}) custom-call(s32[1]{0:T(128)} %bitcast.here_ref, bf16[512,1152]{1,0:T(8,128)(2,1)} %get-tuple-element.53.refs_4_.band_ref, bf16[528,1024]{1,0:T(8,128)(2,1)} %get-tuple-element.54.own_ref, ...), custom_call_target="tpu_custom_call" | custom-call | flops 3449999872 | bytes 1000 | tf_op jit(solution)/shard_map/pallas_call | solution.py:425
  58.5 4.1 %collective-permute-start.13 = (bf16[512,1024]{1,0:T(8,128)(2,1)S(1)}, bf16[512,1024]{1,0:T(8,128)(2,1)S(1)}, u32[]{:S(2)}, u32[]{:S(2)}) collective-permute-start(bf16[512,1024]{1,0:T(8,128)(2,1)S(1)} %get-tuple-element.69.refs_0_.own_ref), channel_id=1, source_target_pairs={{0,4},{1,5},{2,6},{3,7},{4,8},{5,9},{6,10},{7,11},{8,12},{9,13},{1... | collective-permute-start | bytes 3145736 | tf_op jit(solution)/shard_map/ppermute | solution.py:27
  62.5 10.0 %shard_map.76 = (f32[128,8,1024]{2,1,0:T(8,128)}, f32[8,128]{1,0:T(8,128)S(1)}) custom-call(s32[1]{0:T(128)} %bitcast.here_ref, bf16[144,1024]{1,0:T(8,128)(2,1)S(1)} %collective-permute-done.refs_1_.near_ref, bf16[528,1024]{1,0:T(8,128)(2,1)S(1)} %collective-permute-done.3.high_ref.next_level_ref, ...), custom_call_target="tpu_custom_call" | custom-call | bytes 1000 | tf_op jit(solution)/shard_map/pallas_call | solution.py:525
  72.5 2.0 %collective-permute-start.18 = (bf16[128,1024]{1,0:T(8,128)(2,1)S(1)}, bf16[128,1024]{1,0:T(8,128)(2,1)S(1)}, u32[]{:S(2)}, u32[]{:S(2)}) collective-permute-start(bf16[128,1024]{1,0:T(8,128)(2,1)S(1)} %slice.10), channel_id=1, source_target_pairs={{0,1},{1,0},{2,3},{3,2},{4,5},{5,4},{6,7},{7,6},{8,9},{9,8},{10,11... | collective-permute-start | bytes 786440 | tf_op jit(solution)/shard_map/ppermute | solution.py:32
  74.6 1.1 collective-permute-done.18.refs_3_
  75.7 1.3 collective-permute-start.14
  77.4 3.3 %shard_map.77 = (bf16[512,1024]{1,0:T(8,128)(2,1)S(1)}, bf16[128,1024]{1,0:T(8,128)(2,1)S(1)}) custom-call(s32[1]{0:T(128)} %bitcast.here_ref, bf16[512,1152]{1,0:T(8,128)(2,1)} %get-tuple-element.53.refs_4_.band_ref, bf16[512,1024]{1,0:T(8,128)(2,1)} %get-tuple-element.65.refs_0_.own_ref, bf16[512,1024]{1,0:T(8,128)(2,1)S(1)} %collective-permute-done.15.high_ref, ...), custom_call_target="tpu_custom_call" | custom-call | flops 3449999872 | bytes 1000 | tf_op jit(solution)/shard_map/pallas_call | solution.py:425
  80.7 1.3 collective-permute-start.21
  82.0 4.4 %collective-permute-start.25 = (bf16[512,1024]{1,0:T(8,128)(2,1)S(1)}, bf16[512,1024]{1,0:T(8,128)(2,1)S(1)}, u32[]{:S(2)}, u32[]{:S(2)}) collective-permute-start(bf16[512,1024]{1,0:T(8,128)(2,1)S(1)} %get-tuple-element.81.refs_0_.own_ref), channel_id=1, source_target_pairs={{0,4},{1,5},{2,6},{3,7},{4,8},{5,9},{6,10},{7,11},{8,12},{9,13},{1... | collective-permute-start | bytes 3145736 | tf_op jit(solution)/shard_map/ppermute | solution.py:27
  86.4 2.4 %collective-permute-start.26 = (bf16[128,1024]{1,0:T(8,128)(2,1)S(1)}, bf16[128,1024]{1,0:T(8,128)(2,1)S(1)}, u32[]{:S(2)}, u32[]{:S(2)}) collective-permute-start(bf16[128,1024]{1,0:T(8,128)(2,1)S(1)} %slice.11), channel_id=1, source_target_pairs={{0,1},{1,0},{2,3},{3,2},{4,5},{5,4},{6,7},{7,6},{8,9},{9,8},{10,11... | collective-permute-start | bytes 786440 | tf_op jit(solution)/shard_map/ppermute | solution.py:32
  89.5 3.3 %shard_map.78 = (bf16[256,1024]{1,0:T(8,128)(2,1)S(1)}, bf16[256,1024]{1,0:T(8,128)(2,1)S(1)}, bf16[256,1024]{1,0:T(8,128)(2,1)S(1)}, bf16[256,1024]{1,0:T(8,128)(2,1)S(1)}) custom-call(s32[1]{0:T(128)} %bitcast.here_ref, bf16[512,1152]{1,0:T(8,128)(2,1)} %get-tuple-element.71.band_ref, bf16[512,1024]{1,0:T(8,128)(2,1)S(1)} %get-tuple-element.69.refs_0_.own_ref, ...), custom_call_target="tpu_custom_call" | custom-call | bytes 1000 | tf_op jit(solution)/shard_map/pallas_call | solution.py:457
  92.8 0.9 shard_map.80.refs_1_.own_ref
  94.4 2.4 %collective-permute-start.22 = (bf16[256,1024]{1,0:T(8,128)(2,1)S(1)}, bf16[256,1024]{1,0:T(8,128)(2,1)S(1)}, u32[]{:S(2)}, u32[]{:S(2)}) collective-permute-start(bf16[256,1024]{1,0:T(8,128)(2,1)S(1)} %get-tuple-element.85), channel_id=1, source_target_pairs={{0,1},{1,0},{2,3},{3,2},{4,5},{5,4},{6,7},{7,6},{8,9},{9,8},{10,11... | collective-permute-start | bytes 1572872 | tf_op jit(solution)/shard_map/ppermute | solution.py:32
  96.9 1.6 %collective-permute-start.23 = (bf16[256,1024]{1,0:T(8,128)(2,1)S(1)}, bf16[256,1024]{1,0:T(8,128)(2,1)S(1)}, u32[]{:S(2)}, u32[]{:S(2)}) collective-permute-start(bf16[256,1024]{1,0:T(8,128)(2,1)S(1)} %get-tuple-element.86), channel_id=1, source_target_pairs={{0,2},{1,3},{2,0},{3,1},{4,6},{5,7},{6,4},{7,5},{8,10},{9,11},{10,... | collective-permute-start | bytes 1572872 | tf_op jit(solution)/shard_map/ppermute | solution.py:32
  98.6 0.8 shard_map.79
  99.4 7.3 %collective-permute-done.25.low_ref = bf16[512,1024]{1,0:T(8,128)(2,1)S(1)} collective-permute-done((bf16[512,1024]{1,0:T(8,128)(2,1)S(1)}, bf16[512,1024]{1,0:T(8,128)(2,1)S(1)}, u32[]{:S(2)}, u32[]{:S(2)}) %collective-permute-start.25) | collective-permute-done | bytes 1048608 | tf_op jit(solution)/shard_map/ppermute | solution.py:27
  106.8 3.1 %shard_map.81 = (bf16[128,1024]{1,0:T(8,128)(2,1)S(1)}, bf16[128,1024]{1,0:T(8,128)(2,1)S(1)}, bf16[128,1024]{1,0:T(8,128)(2,1)S(1)}, bf16[128,1024]{1,0:T(8,128)(2,1)S(1)}) custom-call(s32[1]{0:T(128)} %bitcast.here_ref, bf16[512,1152]{1,0:T(8,128)(2,1)} %get-tuple-element.71.band_ref, bf16[512,1024]{1,0:T(8,128)(2,1)S(1)} %get-tuple-element.81.refs_0_.own_ref, ...), custom_call_target="tpu_custom_call" | custom-call | bytes 1000 | tf_op jit(solution)/shard_map/pallas_call | solution.py:457
  109.9 3.0 %collective-permute-start.27 = (bf16[128,1024]{1,0:T(8,128)(2,1)S(1)}, bf16[128,1024]{1,0:T(8,128)(2,1)S(1)}, u32[]{:S(2)}, u32[]{:S(2)}) collective-permute-start(bf16[128,1024]{1,0:T(8,128)(2,1)S(1)} %get-tuple-element.91), channel_id=1, source_target_pairs={{0,1},{1,0},{2,3},{3,2},{4,5},{5,4},{6,7},{7,6},{8,9},{9,8},{10,11... | collective-permute-start | bytes 786440 | tf_op jit(solution)/shard_map/ppermute | solution.py:32
  112.9 1.9 %collective-permute-start.28 = (bf16[128,1024]{1,0:T(8,128)(2,1)S(1)}, bf16[128,1024]{1,0:T(8,128)(2,1)S(1)}, u32[]{:S(2)}, u32[]{:S(2)}) collective-permute-start(bf16[128,1024]{1,0:T(8,128)(2,1)S(1)} %get-tuple-element.92), channel_id=1, source_target_pairs={{0,2},{1,3},{2,0},{3,1},{4,6},{5,7},{6,4},{7,5},{8,10},{9,11},{10,... | collective-permute-start | bytes 786440 | tf_op jit(solution)/shard_map/ppermute | solution.py:32
  114.9 7.3 %collective-permute-done.24.refs_3_ = bf16[256,1024]{1,0:T(8,128)(2,1)S(1)} collective-permute-done((bf16[256,1024]{1,0:T(8,128)(2,1)S(1)}, bf16[256,1024]{1,0:T(8,128)(2,1)S(1)}, u32[]{:S(2)}, u32[]{:S(2)}) %collective-permute-start.24) | collective-permute-done | bytes 524320 | tf_op jit(solution)/shard_map/ppermute | solution.py:32
  122.2 2.9 %shard_map.82.tv_ref = f32[128,8,1024]{2,1,0:T(8,128)} custom-call(s32[1]{0:T(128)} %bitcast.here_ref, f32[128,8,1024]{2,1,0:T(8,128)} %get-tuple-element.84.tv_ref, bf16[256,1024]{1,0:T(8,128)(2,1)S(1)} %get-tuple-element.83.refs_4_.refs_0_, bf16[256,1024]{1,0:T(8,128)(2,1)S(1)} %collective-permute-done.22.refs_1_, ...), custom_call_target="tpu_custom_call", output_to_operand_aliasing={{}: (1, {})} | custom-call | bytes 1000 | tf_op jit(solution)/shard_map/pallas_call | solution.py:346
  125.1 2.6 %shard_map.83.refs_4_ = bf16[128,8,1024]{2,1,0:T(8,128)(2,1)} custom-call(s32[1]{0:T(128)} %bitcast.here_ref, bf16[128,8,512]{2,1,0:T(8,128)(2,1)S(1)} %shard_map.80.refs_1_.own_ref, bf16[128,8,512]{2,1,0:T(8,128)(2,1)S(1)} %collective-permute-done.30.above_ref, bf16[256,1024]{1,0:T(8,128)(2,1)S(1)} %get-tuple-element.83.refs_4_.refs_0_, ...), custom_call_target="tpu_custom_call" | custom-call | bytes 1000 | tf_op jit(solution)/shard_map/pallas_call | solution.py:324
  127.8 5.4 %collective-permute-done.29.refs_3_ = bf16[128,1024]{1,0:T(8,128)(2,1)S(1)} collective-permute-done((bf16[128,1024]{1,0:T(8,128)(2,1)S(1)}, bf16[128,1024]{1,0:T(8,128)(2,1)S(1)}, u32[]{:S(2)}, u32[]{:S(2)}) %collective-permute-start.29) | collective-permute-done | bytes 262176 | tf_op jit(solution)/shard_map/ppermute | solution.py:32
  133.2 2.9 %shard_map.84 = f32[128,8,1024]{2,1,0:T(8,128)} custom-call(s32[1]{0:T(128)} %bitcast.here_ref, f32[128,8,1024]{2,1,0:T(8,128)} %shard_map.82.tv_ref, bf16[128,1024]{1,0:T(8,128)(2,1)S(1)} %get-tuple-element.90.refs_4_.refs_0_, bf16[128,1024]{1,0:T(8,128)(2,1)S(1)} %collective-permute-done.27.refs_1_, ...), custom_call_target="tpu_custom_call", output_to_operand_aliasing={{}: (1, {})} | custom-call | bytes 1000 | tf_op jit(solution)/shard_map/pallas_call | solution.py:346
  (52 shorter events, 4.6 us)
Async XLA Ops:
  3.1 29.7 %collective-permute-start.4 = (bf16[128,8,1024]{2,1,0:T(8,128)(2,1)}, bf16[128,8,1024]{2,1,0:T(8,128)(2,1)S(1)}, u32[]{:S(2)}, u32[]{:S(2)}) collective-permute-start(bf16[128,8,1024]{2,1,0:T(8,128)(2,1)} %refs_2_.1), channel_id=1, source_target_pairs={{3,7},{7,11},{11,15},{19,23},{23,27},{27,31}} | collective-permute-start | bytes 6291464 | tf_op jit(solution)/shard_map/ppermute | solution.py:27
  3.9 14.5 %collective-permute-start = (bf16[144,1024]{1,0:T(8,128)(2,1)S(1)}, bf16[144,1024]{1,0:T(8,128)(2,1)S(1)}, u32[]{:S(2)}, u32[]{:S(2)}) collective-permute-start(bf16[144,1024]{1,0:T(8,128)(2,1)S(1)} %get-tuple-element.48.refs_2_), channel_id=1, source_target_pairs={{0,1},{1,0},{2,3},{3,2},{4,5},{5,4},{6,7},{7,6},{8,9},{9,8},{10,11... | collective-permute-start | bytes 884744 | tf_op jit(solution)/shard_map/ppermute | solution.py:32
  4.1 14.4 %collective-permute-start.1 = (bf16[128,1024]{1,0:T(8,128)(2,1)}, bf16[128,1024]{1,0:T(8,128)(2,1)}, u32[]{:S(2)}, u32[]{:S(2)}) collective-permute-start(bf16[128,1024]{1,0:T(8,128)(2,1)} %get-tuple-element.50), channel_id=1, source_target_pairs={{0,2},{1,3},{2,0},{3,1},{4,6},{5,7},{6,4},{7,5},{8,10},{9,11},{10,... | collective-permute-start | bytes 786440 | tf_op jit(solution)/shard_map/ppermute | solution.py:32
  8.7 5.3 %copy-start.6 = (s32[16,6]{0,1:T(8,128)S(1)}, s32[16,6]{0,1:T(8,128)}, u32[]{:S(2)}) copy-start(s32[16,6]{0,1:T(8,128)} %param.8) | copy-start | bytes 1156
  8.7 6.1 %copy-start = (bf16[8,128,128]{2,1,0:T(8,128)(2,1)S(1)}, bf16[8,128,128]{2,1,0:T(8,128)(2,1)}, u32[]{:S(2)}) copy-start(bf16[8,128,128]{2,1,0:T(8,128)(2,1)} %refs_0_.1) | copy-start | bytes 786436
  8.7 13.6 %collective-permute-start.2 = (bf16[144,1024]{1,0:T(8,128)(2,1)S(1)}, bf16[144,1024]{1,0:T(8,128)(2,1)S(1)}, u32[]{:S(2)}, u32[]{:S(2)}) collective-permute-start(bf16[144,1024]{1,0:T(8,128)(2,1)S(1)} %get-tuple-element.51), channel_id=1, source_target_pairs={{0,3},{1,2},{2,1},{3,0},{4,7},{5,6},{6,5},{7,4},{8,11},{9,10},{10,... | collective-permute-start | bytes 884744 | tf_op jit(solution)/shard_map/ppermute | solution.py:32
  11.6 0.7 copy-start.3
  12.3 20.6 %collective-permute-start.5 = (bf16[256,1024]{1,0:T(8,128)(2,1)}, bf16[256,1024]{1,0:T(8,128)(2,1)}, u32[]{:S(2)}, u32[]{:S(2)}) collective-permute-start(bf16[256,1024]{1,0:T(8,128)(2,1)} %get-tuple-element.57), channel_id=1, source_target_pairs={{0,2},{1,3},{2,0},{3,1},{4,6},{5,7},{6,4},{7,5},{8,10},{9,11},{10,... | collective-permute-start | bytes 1572872 | tf_op jit(solution)/shard_map/ppermute | solution.py:32
  14.8 1.0 copy-start.4
  15.8 6.6 %copy-start.2 = (bf16[128,1024]{1,0:T(8,128)(2,1)S(1)}, bf16[128,1024]{1,0:T(8,128)(2,1)}, u32[]{:S(2)}) copy-start(bf16[128,1024]{1,0:T(8,128)(2,1)} %get-tuple-element.49.refs_0_) | copy-start | bytes 786436
  22.3 2.1 %copy-start.5 = (bf16[128,1024]{1,0:T(8,128)(2,1)S(1)}, bf16[128,1024]{1,0:T(8,128)(2,1)}, u32[]{:S(2)}) copy-start(bf16[128,1024]{1,0:T(8,128)(2,1)} %copy-done.3) | copy-start | bytes 786436
  24.4 14.2 %copy-start.7 = (bf16[144,1024]{1,0:T(8,128)(2,1)S(1)}, bf16[144,1024]{1,0:T(8,128)(2,1)}, u32[]{:S(2)}) copy-start(bf16[144,1024]{1,0:T(8,128)(2,1)} %get-tuple-element.60) | copy-start | bytes 884740
  24.4 17.3 %copy-start.1 = (bf16[128,1024]{1,0:T(8,128)(2,1)S(1)}, bf16[128,1024]{1,0:T(8,128)(2,1)}, u32[]{:S(2)}) copy-start(bf16[128,1024]{1,0:T(8,128)(2,1)} %get-tuple-element.63.refs_0_) | copy-start | bytes 786436
  24.5 8.4 %collective-permute-start.6 = (bf16[128,1024]{1,0:T(8,128)(2,1)S(1)}, bf16[128,1024]{1,0:T(8,128)(2,1)S(1)}, u32[]{:S(2)}, u32[]{:S(2)}) collective-permute-start(bf16[128,1024]{1,0:T(8,128)(2,1)S(1)} %copy-done.5), channel_id=1, source_target_pairs={{0,1},{1,0},{2,3},{3,2},{4,5},{5,4},{6,7},{7,6},{8,9},{9,8},{10,11... | collective-permute-start | bytes 786440 | tf_op jit(solution)/shard_map/ppermute | solution.py:32
  24.8 27.4 %collective-permute-start.3 = (bf16[528,1024]{1,0:T(8,128)(2,1)}, bf16[528,1024]{1,0:T(8,128)(2,1)S(1)}, u32[]{:S(2)}, u32[]{:S(2)}) collective-permute-start(bf16[528,1024]{1,0:T(8,128)(2,1)} %get-tuple-element.54.own_ref), channel_id=1, source_target_pairs={{4,0},{5,1},{6,2},{7,3},{8,4},{9,5},{10,6},{11,7},{12,8},{13,9},{1... | collective-permute-start | bytes 3244040 | tf_op jit(solution)/shard_map/ppermute | solution.py:27
  34.7 12.5 %collective-permute-start.9 = (bf16[256,1024]{1,0:T(8,128)(2,1)S(1)}, bf16[256,1024]{1,0:T(8,128)(2,1)S(1)}, u32[]{:S(2)}, u32[]{:S(2)}) collective-permute-start(bf16[256,1024]{1,0:T(8,128)(2,1)S(1)} %get-tuple-element.62), channel_id=1, source_target_pairs={{0,2},{1,3},{2,0},{3,1},{4,6},{5,7},{6,4},{7,5},{8,10},{9,11},{10,... | collective-permute-start | bytes 1572872 | tf_op jit(solution)/shard_map/ppermute | solution.py:32
  35.9 2.7 %collective-permute-start.7 = (bf16[128,1024]{1,0:T(8,128)(2,1)S(1)}, bf16[128,1024]{1,0:T(8,128)(2,1)S(1)}, u32[]{:S(2)}, u32[]{:S(2)}) collective-permute-start(bf16[128,1024]{1,0:T(8,128)(2,1)S(1)} %get-tuple-element.59), channel_id=1, source_target_pairs={{0,1},{1,0},{2,3},{3,2},{4,5},{5,4},{6,7},{7,6},{8,9},{9,8},{10,11... | collective-permute-start | bytes 786440 | tf_op jit(solution)/shard_map/ppermute | solution.py:32
  37.4 4.3 %collective-permute-start.10 = (bf16[128,1024]{1,0:T(8,128)(2,1)S(1)}, bf16[128,1024]{1,0:T(8,128)(2,1)S(1)}, u32[]{:S(2)}, u32[]{:S(2)}) collective-permute-start(bf16[128,1024]{1,0:T(8,128)(2,1)S(1)} %get-tuple-element.64), channel_id=1, source_target_pairs={{0,1},{1,0},{2,3},{3,2},{4,5},{5,4},{6,7},{7,6},{8,9},{9,8},{10,11... | collective-permute-start | bytes 786440 | tf_op jit(solution)/shard_map/ppermute | solution.py:32
  38.6 16.2 %collective-permute-start.8 = (bf16[144,1024]{1,0:T(8,128)(2,1)S(1)}, bf16[144,1024]{1,0:T(8,128)(2,1)S(1)}, u32[]{:S(2)}, u32[]{:S(2)}) collective-permute-start(bf16[144,1024]{1,0:T(8,128)(2,1)S(1)} %copy-done.7), channel_id=1, source_target_pairs={{0,4},{1,5},{2,6},{3,7},{4,8},{5,9},{6,10},{7,11},{8,12},{9,13},{1... | collective-permute-start | bytes 884744 | tf_op jit(solution)/shard_map/ppermute | solution.py:27
  43.8 9.7 %collective-permute-start.12 = (bf16[128,1024]{1,0:T(8,128)(2,1)}, bf16[128,1024]{1,0:T(8,128)(2,1)S(1)}, u32[]{:S(2)}, u32[]{:S(2)}) collective-permute-start(bf16[128,1024]{1,0:T(8,128)(2,1)} %get-tuple-element.67), channel_id=1, source_target_pairs={{0,4},{1,5},{2,6},{3,7},{4,8},{5,9},{6,10},{7,11},{8,12},{9,13},{1... | collective-permute-start | bytes 786440 | tf_op jit(solution)/shard_map/ppermute | solution.py:27
  47.3 7.6 %collective-permute-start.11 = (bf16[128,1024]{1,0:T(8,128)(2,1)S(1)}, bf16[128,1024]{1,0:T(8,128)(2,1)S(1)}, u32[]{:S(2)}, u32[]{:S(2)}) collective-permute-start(bf16[128,1024]{1,0:T(8,128)(2,1)S(1)} %slice.9), channel_id=1, source_target_pairs={{0,1},{1,0},{2,3},{3,2},{4,5},{5,4},{6,7},{7,6},{8,9},{9,8},{10,11... | collective-permute-start | bytes 786440 | tf_op jit(solution)/shard_map/ppermute | solution.py:32
  49.2 27.8 %collective-permute-start.15 = (bf16[512,1024]{1,0:T(8,128)(2,1)}, bf16[512,1024]{1,0:T(8,128)(2,1)S(1)}, u32[]{:S(2)}, u32[]{:S(2)}) collective-permute-start(bf16[512,1024]{1,0:T(8,128)(2,1)} %get-tuple-element.65.refs_0_.own_ref), channel_id=1, source_target_pairs={{4,0},{5,1},{6,2},{7,3},{8,4},{9,5},{10,6},{11,7},{12,8},{13,9},{1... | collective-permute-start | bytes 3145736 | tf_op jit(solution)/shard_map/ppermute | solution.py:27
  52.2 6.0 %collective-permute-start.16 = (bf16[128,1024]{1,0:T(8,128)(2,1)S(1)}, bf16[128,1024]{1,0:T(8,128)(2,1)S(1)}, u32[]{:S(2)}, u32[]{:S(2)}) collective-permute-start(bf16[128,1024]{1,0:T(8,128)(2,1)S(1)} %get-tuple-element.73), channel_id=1, source_target_pairs={{0,1},{1,0},{2,3},{3,2},{4,5},{5,4},{6,7},{7,6},{8,9},{9,8},{10,11... | collective-permute-start | bytes 786440 | tf_op jit(solution)/shard_map/ppermute | solution.py:32
  53.5 19.0 %collective-permute-start.17 = (bf16[256,1024]{1,0:T(8,128)(2,1)S(1)}, bf16[256,1024]{1,0:T(8,128)(2,1)S(1)}, u32[]{:S(2)}, u32[]{:S(2)}) collective-permute-start(bf16[256,1024]{1,0:T(8,128)(2,1)S(1)} %get-tuple-element.74), channel_id=1, source_target_pairs={{0,2},{1,3},{2,0},{3,1},{4,6},{5,7},{6,4},{7,5},{8,10},{9,11},{10,... | collective-permute-start | bytes 1572872 | tf_op jit(solution)/shard_map/ppermute | solution.py:32
  58.2 19.2 %collective-permute-start.20 = (bf16[256,1024]{1,0:T(8,128)(2,1)S(1)}, bf16[256,1024]{1,0:T(8,128)(2,1)S(1)}, u32[]{:S(2)}, u32[]{:S(2)}) collective-permute-start(bf16[256,1024]{1,0:T(8,128)(2,1)S(1)} %get-tuple-element.80), channel_id=1, source_target_pairs={{0,2},{1,3},{2,0},{3,1},{4,6},{5,7},{6,4},{7,5},{8,10},{9,11},{10,... | collective-permute-start | bytes 1572872 | tf_op jit(solution)/shard_map/ppermute | solution.py:32
  58.5 31.1 %collective-permute-start.13 = (bf16[512,1024]{1,0:T(8,128)(2,1)S(1)}, bf16[512,1024]{1,0:T(8,128)(2,1)S(1)}, u32[]{:S(2)}, u32[]{:S(2)}) collective-permute-start(bf16[512,1024]{1,0:T(8,128)(2,1)S(1)} %get-tuple-element.69.refs_0_.own_ref), channel_id=1, source_target_pairs={{0,4},{1,5},{2,6},{3,7},{4,8},{5,9},{6,10},{7,11},{8,12},{9,13},{1... | collective-permute-start | bytes 3145736 | tf_op jit(solution)/shard_map/ppermute | solution.py:27
  72.5 3.2 %collective-permute-start.18 = (bf16[128,1024]{1,0:T(8,128)(2,1)S(1)}, bf16[128,1024]{1,0:T(8,128)(2,1)S(1)}, u32[]{:S(2)}, u32[]{:S(2)}) collective-permute-start(bf16[128,1024]{1,0:T(8,128)(2,1)S(1)} %slice.10), channel_id=1, source_target_pairs={{0,1},{1,0},{2,3},{3,2},{4,5},{5,4},{6,7},{7,6},{8,9},{9,8},{10,11... | collective-permute-start | bytes 786440 | tf_op jit(solution)/shard_map/ppermute | solution.py:32
  74.5 2.5 %collective-permute-start.19 = (bf16[128,1024]{1,0:T(8,128)(2,1)S(1)}, bf16[128,1024]{1,0:T(8,128)(2,1)S(1)}, u32[]{:S(2)}, u32[]{:S(2)}) collective-permute-start(bf16[128,1024]{1,0:T(8,128)(2,1)S(1)} %get-tuple-element.78), channel_id=1, source_target_pairs={{0,1},{1,0},{2,3},{3,2},{4,5},{5,4},{6,7},{7,6},{8,9},{9,8},{10,11... | collective-permute-start | bytes 786440 | tf_op jit(solution)/shard_map/ppermute | solution.py:32
  75.7 13.1 %collective-permute-start.14 = (bf16[128,1024]{1,0:T(8,128)(2,1)S(1)}, bf16[128,1024]{1,0:T(8,128)(2,1)S(1)}, u32[]{:S(2)}, u32[]{:S(2)}) collective-permute-start(bf16[128,1024]{1,0:T(8,128)(2,1)S(1)} %get-tuple-element.72), channel_id=1, source_target_pairs={{4,0},{5,1},{6,2},{7,3},{8,4},{9,5},{10,6},{11,7},{12,8},{13,9},{1... | collective-permute-start | bytes 786440 | tf_op jit(solution)/shard_map/ppermute | solution.py:27
  80.7 8.8 %collective-permute-start.21 = (bf16[128,1024]{1,0:T(8,128)(2,1)S(1)}, bf16[128,1024]{1,0:T(8,128)(2,1)S(1)}, u32[]{:S(2)}, u32[]{:S(2)}) collective-permute-start(bf16[128,1024]{1,0:T(8,128)(2,1)S(1)} %get-tuple-element.82), channel_id=1, source_target_pairs={{4,0},{5,1},{6,2},{7,3},{8,4},{9,5},{10,6},{11,7},{12,8},{13,9},{1... | collective-permute-start | bytes 786440 | tf_op jit(solution)/shard_map/ppermute | solution.py:27
  82.0 24.7 %collective-permute-start.25 = (bf16[512,1024]{1,0:T(8,128)(2,1)S(1)}, bf16[512,1024]{1,0:T(8,128)(2,1)S(1)}, u32[]{:S(2)}, u32[]{:S(2)}) collective-permute-start(bf16[512,1024]{1,0:T(8,128)(2,1)S(1)} %get-tuple-element.81.refs_0_.own_ref), channel_id=1, source_target_pairs={{0,4},{1,5},{2,6},{3,7},{4,8},{5,9},{6,10},{7,11},{8,12},{9,13},{1... | collective-permute-start | bytes 3145736 | tf_op jit(solution)/shard_map/ppermute | solution.py:27
  86.4 6.4 %collective-permute-start.26 = (bf16[128,1024]{1,0:T(8,128)(2,1)S(1)}, bf16[128,1024]{1,0:T(8,128)(2,1)S(1)}, u32[]{:S(2)}, u32[]{:S(2)}) collective-permute-start(bf16[128,1024]{1,0:T(8,128)(2,1)S(1)} %slice.11), channel_id=1, source_target_pairs={{0,1},{1,0},{2,3},{3,2},{4,5},{5,4},{6,7},{7,6},{8,9},{9,8},{10,11... | collective-permute-start | bytes 786440 | tf_op jit(solution)/shard_map/ppermute | solution.py:32
  93.7 31.4 %collective-permute-start.30 = (bf16[128,8,512]{2,1,0:T(8,128)(2,1)S(1)}, bf16[128,8,512]{2,1,0:T(8,128)(2,1)S(1)}, u32[]{:S(2)}, u32[]{:S(2)}) collective-permute-start(bf16[128,8,512]{2,1,0:T(8,128)(2,1)S(1)} %shard_map.80.refs_1_.own_ref), channel_id=1, source_target_pairs={{7,3},{11,7},{15,11},{23,19},{27,23},{31,27}} | collective-permute-start | bytes 3145736 | tf_op jit(solution)/shard_map/ppermute | solution.py:27
  94.4 18.5 %collective-permute-start.22 = (bf16[256,1024]{1,0:T(8,128)(2,1)S(1)}, bf16[256,1024]{1,0:T(8,128)(2,1)S(1)}, u32[]{:S(2)}, u32[]{:S(2)}) collective-permute-start(bf16[256,1024]{1,0:T(8,128)(2,1)S(1)} %get-tuple-element.85), channel_id=1, source_target_pairs={{0,1},{1,0},{2,3},{3,2},{4,5},{5,4},{6,7},{7,6},{8,9},{9,8},{10,11... | collective-permute-start | bytes 1572872 | tf_op jit(solution)/shard_map/ppermute | solution.py:32
  96.9 17.9 %collective-permute-start.23 = (bf16[256,1024]{1,0:T(8,128)(2,1)S(1)}, bf16[256,1024]{1,0:T(8,128)(2,1)S(1)}, u32[]{:S(2)}, u32[]{:S(2)}) collective-permute-start(bf16[256,1024]{1,0:T(8,128)(2,1)S(1)} %get-tuple-element.86), channel_id=1, source_target_pairs={{0,2},{1,3},{2,0},{3,1},{4,6},{5,7},{6,4},{7,5},{8,10},{9,11},{10,... | collective-permute-start | bytes 1572872 | tf_op jit(solution)/shard_map/ppermute | solution.py:32
  98.5 23.7 %collective-permute-start.24 = (bf16[256,1024]{1,0:T(8,128)(2,1)S(1)}, bf16[256,1024]{1,0:T(8,128)(2,1)S(1)}, u32[]{:S(2)}, u32[]{:S(2)}) collective-permute-start(bf16[256,1024]{1,0:T(8,128)(2,1)S(1)} %get-tuple-element.87), channel_id=1, source_target_pairs={{0,3},{1,2},{2,1},{3,0},{4,7},{5,6},{6,5},{7,4},{8,11},{9,10},{10,... | collective-permute-start | bytes 1572872 | tf_op jit(solution)/shard_map/ppermute | solution.py:32
  109.9 17.9 %collective-permute-start.27 = (bf16[128,1024]{1,0:T(8,128)(2,1)S(1)}, bf16[128,1024]{1,0:T(8,128)(2,1)S(1)}, u32[]{:S(2)}, u32[]{:S(2)}) collective-permute-start(bf16[128,1024]{1,0:T(8,128)(2,1)S(1)} %get-tuple-element.91), channel_id=1, source_target_pairs={{0,1},{1,0},{2,3},{3,2},{4,5},{5,4},{6,7},{7,6},{8,9},{9,8},{10,11... | collective-permute-start | bytes 786440 | tf_op jit(solution)/shard_map/ppermute | solution.py:32
  112.9 14.9 %collective-permute-start.28 = (bf16[128,1024]{1,0:T(8,128)(2,1)S(1)}, bf16[128,1024]{1,0:T(8,128)(2,1)S(1)}, u32[]{:S(2)}, u32[]{:S(2)}) collective-permute-start(bf16[128,1024]{1,0:T(8,128)(2,1)S(1)} %get-tuple-element.92), channel_id=1, source_target_pairs={{0,2},{1,3},{2,0},{3,1},{4,6},{5,7},{6,4},{7,5},{8,10},{9,11},{10,... | collective-permute-start | bytes 786440 | tf_op jit(solution)/shard_map/ppermute | solution.py:32
  114.8 18.3 %collective-permute-start.29 = (bf16[128,1024]{1,0:T(8,128)(2,1)S(1)}, bf16[128,1024]{1,0:T(8,128)(2,1)S(1)}, u32[]{:S(2)}, u32[]{:S(2)}) collective-permute-start(bf16[128,1024]{1,0:T(8,128)(2,1)S(1)} %get-tuple-element.93), channel_id=1, source_target_pairs={{0,3},{1,2},{2,1},{3,0},{4,7},{5,6},{6,5},{7,4},{8,11},{9,10},{10,... | collective-permute-start | bytes 786440 | tf_op jit(solution)/shard_map/ppermute | solution.py:32

commit v12 on v11

--- a/solution.py
+++ b/solution.py
@@ -150,7 +150,7 @@
         grid=(cols // tile,),
         in_specs=[SMEM] + specs + [ANY] * len(tokens),
         out_specs=[across(shape, tile) for shape in shapes],
-        results=[pltpu.HBM(shape, BF16) for shape in shapes],
+        results=[value(shape, BF16) for shape in shapes],
     )(here, *arrays_of(pieces), *tokens)
 
 
@@ -202,19 +202,32 @@
     r_ref, tv_ref, vol, s, r, wide, tv, sem = refs[-8:]
     depth, rows, cols = sino_ref.shape
 
+    count = cols // LANES
+
+    def columns(j):
+        return pl.ds(pl.multiple_of(j * LANES, LANES), LANES)
+
+    def arrival(n, j):
+        src, dst = ((vol_ref, vol), (sino_ref, s), (tv_ref, tv))[n]
+        return pltpu.make_async_copy(src.at[:, :, columns(j)], dst.at[:, :, columns(j)], sem.at[n, j])
+
+    def departure(n, j):
+        src, dst = ((r, r_ref), (tv, tv_ref))[n]
+        return pltpu.make_async_copy(src.at[:, :, columns(j)], dst.at[:, :, columns(j)], sem.at[3 + n, j])
+
     @pl.when(here_ref[0] == slabs - 1)
     def _():
-        arrivals = [(vol_ref, vol), (sino_ref, s), (tv_ref, tv)]
-        for n, (src, dst) in enumerate(arrivals):
-            pltpu.make_async_copy(src, dst, sem.at[n]).start()
-        for n, (src, dst) in enumerate(arrivals):
-            pltpu.make_async_copy(src, dst, sem.at[n]).wait()
+        for j in range(count):
+            for n in range(3):
+                arrival(n, j).start()
         block = w_ref[offset_ref[slabs - 1, 0]]
         block = jnp.where(cover_ref[slabs - 1, 0] == 1, block, jnp.zeros_like(block))
         turned = block.astype(F32).T.astype(BF16)
 
         def column(j, _):
-            at = pl.ds(pl.multiple_of(j * LANES, LANES), LANES)
+            at = columns(j)
+            for n in range(3):
+                arrival(n, j).wait()
             for n, ref in enumerate((s, tv, vol)):
                 wide[n] = ref[:, :, at].astype(F32).reshape(wide.shape[1:])
             for row in range(rows):
@@ -225,14 +238,14 @@
                 wide.at[1][spot, :] += jnp.dot(turned, resid, preferred_element_type=F32)
             r[:, :, at] = wide[0].reshape(depth, rows, LANES).astype(BF16)
             tv[:, :, at] = wide[1].reshape(depth, rows, LANES)
+            for n in range(2):
+                departure(n, j).start()
             return 0
 
-        lax.fori_loop(0, cols // LANES, column, 0)
-        departures = [(r, r_ref), (tv, tv_ref)]
-        for n, (src, dst) in enumerate(departures):
-            pltpu.make_async_copy(src, dst, sem.at[n]).start()
-        for n, (src, dst) in enumerate(departures):
-            pltpu.make_async_copy(src, dst, sem.at[n]).wait()
+        lax.fori_loop(0, count, column, 0)
+        for j in range(count):
+            for n in range(2):
+                departure(n, j).wait()
 
 
 def last_group(here, coverage, offsets, weights, volume, sinogram, tv, *tokens):
@@ -253,7 +266,7 @@
             pltpu.VMEM(sinogram.shape, BF16),
             pltpu.VMEM((3, depth * rows, LANES), F32),
             pltpu.VMEM(volume.shape, F32),
-            pltpu.SemaphoreType.DMA((3,)),
+            pltpu.SemaphoreType.DMA((5, cols // LANES)),
         ],
     )(here, coverage, offsets, weights, far(volume), far(sinogram), far(tv), *tokens)
 
@@ -397,7 +410,7 @@
         in_specs=[SMEM, SMEM, SMEM, pl.BlockSpec(weights.shape, lambda i: (0, 0, 0))] + [ANY] * len(tokens),
         grid=(1,),
         out_specs=[pl.BlockSpec(shape, lambda i: (0, 0))] * 2,
-        results=[pltpu.HBM(shape, BF16)] * 2,
+        results=[value(shape, BF16)] * 2,
         scratch_shapes=[pltpu.VMEM(weights.shape, BF16)],
     )(here, coverage, offsets, weights, *tokens)
 
@@ -431,7 +444,7 @@
         + [ANY] * len(tokens),
         out_specs=[across(shape, tile) for shape in shapes],
         results=[value(shape, BF16) for shape in shapes],
-    )(here, far(band), far(own), high, low, *arrays_of(sinos), *tokens)
+    )(here, band, own, high, low, *arrays_of(sinos), *tokens)
 
 
 def back_kernel(dealing, here_ref, band_ref, own_ref, low_ref, high_ref, *refs):
@@ -463,7 +476,7 @@
         + [ANY] * len(tokens),
         out_specs=[across(out, tile)] * G,
         results=[value(out, BF16)] * G,
-    )(here, far(band), own, low, high, *dealt, *tokens)
+    )(here, band, own, low, high, *dealt, *tokens)
 
 
 def tv_flux(cur, above):
@@ -552,7 +565,7 @@
     v0, v1, v23 = cast_rows(here, volume, 1, paired, False, vols0[1])
     over = swapped(v23, 2)
     band_p, band_b = bands(here, coverage, offsets, weights, v1)
-    own0, edge0 = pack(here, [(array, 0) for array in got_vols0], 2 * rows, far(band_p))
+    own0, edge0 = pack(here, [(array, 0) for array in got_vols0], 2 * rows, band_p)
     high0, near = moved(own0, -G), swapped(tied(v1, own0), 1)
     s0, s1, s23, over_beyond = split_rows(here, sinogram, got, 0, paired, [(over, 1)], near)
     s_near, s_over = swapped(s1, 1), swapped(s23, 2)
@@ -561,7 +574,7 @@
     low1, high1 = moved(edge1, G), moved(own1, -G)
     sinos0 = [(s0, 0), (s_near, 0), (s_over, 0), (beyond(s_over, own1), 0)]
 
-    s0, s1, s23 = split_rows(here, sinogram, got, 1, paired, [], far(own1))
+    s0, s1, s23 = split_rows(here, sinogram, got, 1, paired, [], own1)
 
     resid0, down0, r1, r23 = project(here, band_p, own0, high0, low0, sinos0, paired[1:], low1, s0)
     from_low0, from_high0 = moved(resid0, G), moved(down0, -G)

time: 137 us -> 135 us (0.985)
  Pallas kernels: 48.7 us -> 41.3 us
  waiting for transfers between devices: 34.8 us -> 39.8 us
    ppermute x21, waiting for transfers between devices: 26.3 us -> 30 us  [swapped(): return lax.ppermute(value, 'slab', [(i, i ^ bits) for i in range(count)])]
    pallas_call x2, Pallas kernels: 6.68 us -> 4.22 us  [project(): call(functools.partial(project_kernel, groups), 3, grid=(cols // tile,),...]
    pallas_call x2, Pallas kernels: 6.41 us -> 4.08 us  [back(): call(functools.partial(back_kernel, bool(dealt)), 0, grid=(cols // tile,)...]
    pallas_call x2, Pallas kernels: 4.22 us -> 2.37 us  [pack(): call(pack_kernel, 1, grid=(cols // tile,), in_specs=[SMEM] + specs + [ANY...]
  transfers between devices with their start and end apart: 31 -> 31, of which waited for: 11 -> 12; matrix products, arithmetic and copies ran while one was open for 1% -> 1% of each run, Pallas kernels for 32% -> 27%
where the time goes in v12:
time: 135 us; the launch traced here: 134 us
  starting transfers between devices  48.9 us (36%)
  Pallas kernels  41.3 us (31%)
  waiting for transfers between devices  39.8 us (29%)
  local copies, waits for them, and re-layouts  2.59 us (2%)
    ppermute x21, waiting for transfers between devices, swapped(): return lax.ppermute(value, 'slab', [(i, i ^ bits) for i in range(count)])  30 us
    ppermute x21, starting transfers between devices, swapped(): return lax.ppermute(value, 'slab', [(i, i ^ bits) for i in range(count)])  27 us
    ppermute x10, starting transfers between devices, moved(): return lax.ppermute(value, 'slab', pairs)  21.9 us
    pallas_call x1, Pallas kernels, half_tv(): call(tv_kernel, 0, grid=(depth // deep,), in_specs=[SMEM] + edges + [afte...  10 us
    ppermute x10, waiting for transfers between devices, moved(): return lax.ppermute(value, 'slab', pairs)  9.85 us
    pallas_call x2, Pallas kernels, finish(): call(finish_kernel, 0, grid=(count,), in_specs=[SMEM, part] + piece_specs...  5.85 us
    pallas_call x2, Pallas kernels, cast_rows(): call(functools.partial(cast_kernel, groups, len(edges)), 2, grid=(count,)...  5.02 us
    pallas_call x2, Pallas kernels, project(): call(functools.partial(project_kernel, groups), 3, grid=(cols // tile,),...  4.22 us
  transfers between devices with their start and end apart: 31, of which 12 were waited for; matrix products, arithmetic and copies ran while one was open for 1% of the time, Pallas kernels for 27%

profile of v12, /device:TPU:1, one launch (start us, length us, event | category | flops | bytes accessed | tf_op | source)
XLA Modules:
  0.0 133.6 jit_solution(3858886944091105498)
XLA Ops:
  0.6 2.5 %shard_map.68 = (bf16[128,1024]{1,0:T(8,128)(2,1)}, bf16[144,1024]{1,0:T(8,128)(2,1)S(1)}, bf16[128,1024]{1,0:T(8,128)(2,1)}, bf16[144,1024]{1,0:T(8,128)(2,1)S(1)}) custom-call(s32[1]{0:T(128)} %bitcast.here_ref, f32[1024,1024]{1,0:T(8,128)} %bitcast.2, f32[1024,1024]{1,0:T(8,128)} %bitcast.3, f32[1024,1024]{1,0:T(8,128)} %bitcast.4, f32[1024,1024]{1,0:T(8,128)} %bitcast.5), custom_call_target="tpu_custom_call" | custom-call | flops 2300000000 | bytes 1000 | tf_op jit(solution)/shard_map/pallas_call | solution.py:110
  4.1 4.6 %collective-permute-start.1 = (bf16[128,1024]{1,0:T(8,128)(2,1)}, bf16[128,1024]{1,0:T(8,128)(2,1)}, u32[]{:S(2)}, u32[]{:S(2)}) collective-permute-start(bf16[128,1024]{1,0:T(8,128)(2,1)} %get-tuple-element.50), channel_id=1, source_target_pairs={{0,2},{1,3},{2,0},{3,1},{4,6},{5,7},{6,4},{7,5},{8,10},{9,11},{10,... | collective-permute-start | bytes 786440 | tf_op jit(solution)/shard_map/ppermute | solution.py:32
  9.1 2.5 %shard_map.69 = (bf16[128,1024]{1,0:T(8,128)(2,1)}, bf16[128,1024]{1,0:T(8,128)(2,1)S(1)}, bf16[256,1024]{1,0:T(8,128)(2,1)}) custom-call(s32[1]{0:T(128)} %bitcast.here_ref, f32[1024,1024]{1,0:T(8,128)} %bitcast.6, f32[1024,1024]{1,0:T(8,128)} %bitcast.7, bf16[144,1024]{1,0:T(8,128)(2,1)S(1)} %get-tuple-element.48.refs_2_), custom_call_target="tpu_custom_call" | custom-call | flops 2300000000 | bytes 1000 | tf_op jit(solution)/shard_map/pallas_call | solution.py:110
  12.3 1.7 %collective-permute-start.5 = (bf16[256,1024]{1,0:T(8,128)(2,1)}, bf16[256,1024]{1,0:T(8,128)(2,1)}, u32[]{:S(2)}, u32[]{:S(2)}) collective-permute-start(bf16[256,1024]{1,0:T(8,128)(2,1)} %get-tuple-element.57), channel_id=1, source_target_pairs={{0,2},{1,3},{2,0},{3,1},{4,6},{5,7},{6,4},{7,5},{8,10},{9,11},{10,... | collective-permute-start | bytes 1572872 | tf_op jit(solution)/shard_map/ppermute | solution.py:32
  14.8 0.9 copy-done.4
  15.8 1.6 %shard_map.70 = (bf16[512,1152]{1,0:T(8,128)(2,1)S(1)}, bf16[512,1152]{1,0:T(8,128)(2,1)S(1)}) custom-call(s32[1]{0:T(128)} %bitcast.here_ref, s32[16,6]{1,0:T(8,128)S(1)} %copy.12.cover_ref, s32[16,6]{1,0:T(8,128)S(1)} %copy.13.offset_ref, bf16[8,128,128]{2,1,0:T(8,128)(2,1)S(1)} %copy-done, bf16[128,1024]{1,0:T(8,128)(2,1)S(1)} %copy-done.4), custom_call_target="tpu_custom_call" | custom-call | flops 10350000128 | bytes 1000 | tf_op jit(solution)/shard_map/pallas_call | solution.py:407
  17.4 4.9 %collective-permute-done.2.refs_3_.far_ref = bf16[144,1024]{1,0:T(8,128)(2,1)S(1)} collective-permute-done((bf16[144,1024]{1,0:T(8,128)(2,1)S(1)}, bf16[144,1024]{1,0:T(8,128)(2,1)S(1)}, u32[]{:S(2)}, u32[]{:S(2)}) %collective-permute-start.2) | collective-permute-done | bytes 294944 | tf_op jit(solution)/shard_map/ppermute | solution.py:32
  22.4 1.2 shard_map.71
  23.9 1.3 collective-permute-start.3
  25.2 7.7 %collective-permute-done.5.refs_0_.refs_2_ = bf16[256,1024]{1,0:T(8,128)(2,1)} collective-permute-done((bf16[256,1024]{1,0:T(8,128)(2,1)}, bf16[256,1024]{1,0:T(8,128)(2,1)}, u32[]{:S(2)}, u32[]{:S(2)}) %collective-permute-start.5) | collective-permute-done | bytes 524320 | tf_op jit(solution)/shard_map/ppermute | solution.py:32
  32.9 1.8 %shard_map.72 = (bf16[128,1024]{1,0:T(8,128)(2,1)S(1)}, bf16[128,1024]{1,0:T(8,128)(2,1)S(1)}, bf16[256,1024]{1,0:T(8,128)(2,1)S(1)}, bf16[128,1024]{1,0:T(8,128)(2,1)S(1)}) custom-call(s32[1]{0:T(128)} %bitcast.here_ref, bf16[128,8,1024]{2,1,0:T(8,128)(2,1)} %refs_2_.1, bf16[128,8,1024]{2,1,0:T(8,128)(2,1)S(1)} %collective-permute-done.4.got_ref, ...), custom_call_target="tpu_custom_call" | custom-call | flops 2300000000 | bytes 1000 | tf_op jit(solution)/shard_map/pallas_call | solution.py:189
  34.7 1.2 collective-permute-start.9
  35.9 1.5 %collective-permute-start.7 = (bf16[128,1024]{1,0:T(8,128)(2,1)S(1)}, bf16[128,1024]{1,0:T(8,128)(2,1)S(1)}, u32[]{:S(2)}, u32[]{:S(2)}) collective-permute-start(bf16[128,1024]{1,0:T(8,128)(2,1)S(1)} %get-tuple-element.59), channel_id=1, source_target_pairs={{0,1},{1,0},{2,3},{3,2},{4,5},{5,4},{6,7},{7,6},{8,9},{9,8},{10,11... | collective-permute-start | bytes 786440 | tf_op jit(solution)/shard_map/ppermute | solution.py:32
  37.5 1.2 collective-permute-done.7.refs_1_
  38.6 3.1 %collective-permute-start.8 = (bf16[144,1024]{1,0:T(8,128)(2,1)S(1)}, bf16[144,1024]{1,0:T(8,128)(2,1)S(1)}, u32[]{:S(2)}, u32[]{:S(2)}) collective-permute-start(bf16[144,1024]{1,0:T(8,128)(2,1)S(1)} %get-tuple-element.60), channel_id=1, source_target_pairs={{0,4},{1,5},{2,6},{3,7},{4,8},{5,9},{6,10},{7,11},{8,12},{9,13},{1... | collective-permute-start | bytes 884744 | tf_op jit(solution)/shard_map/ppermute | solution.py:27
  41.7 1.2 shard_map.73
  42.9 3.2 %collective-permute-start.12 = (bf16[128,1024]{1,0:T(8,128)(2,1)S(1)}, bf16[128,1024]{1,0:T(8,128)(2,1)S(1)}, u32[]{:S(2)}, u32[]{:S(2)}) collective-permute-start(bf16[128,1024]{1,0:T(8,128)(2,1)S(1)} %get-tuple-element.67), channel_id=1, source_target_pairs={{0,4},{1,5},{2,6},{3,7},{4,8},{5,9},{6,10},{7,11},{8,12},{9,13},{1... | collective-permute-start | bytes 786440 | tf_op jit(solution)/shard_map/ppermute | solution.py:27
  46.1 1.1 collective-permute-done.9.refs_2_
  47.3 1.9 %collective-permute-start.11 = (bf16[128,1024]{1,0:T(8,128)(2,1)S(1)}, bf16[128,1024]{1,0:T(8,128)(2,1)S(1)}, u32[]{:S(2)}, u32[]{:S(2)}) collective-permute-start(bf16[128,1024]{1,0:T(8,128)(2,1)S(1)} %slice.9), channel_id=1, source_target_pairs={{0,1},{1,0},{2,3},{3,2},{4,5},{5,4},{6,7},{7,6},{8,9},{9,8},{10,11... | collective-permute-start | bytes 786440 | tf_op jit(solution)/shard_map/ppermute | solution.py:32
  49.2 1.3 collective-permute-start.15
  50.5 1.7 %shard_map.74 = (bf16[128,1024]{1,0:T(8,128)(2,1)S(1)}, bf16[128,1024]{1,0:T(8,128)(2,1)S(1)}, bf16[256,1024]{1,0:T(8,128)(2,1)S(1)}) custom-call(s32[1]{0:T(128)} %bitcast.here_ref, bf16[128,8,1024]{2,1,0:T(8,128)(2,1)} %refs_2_.1, bf16[128,8,1024]{2,1,0:T(8,128)(2,1)S(1)} %collective-permute-done.4.got_ref, ...), custom_call_target="tpu_custom_call" | custom-call | flops 2300000000 | bytes 1000 | tf_op jit(solution)/shard_map/pallas_call | solution.py:189
  52.3 1.0 collective-permute-done.12.refs_4_.low_ref
  53.6 2.1 %shard_map.75 = (bf16[512,1024]{1,0:T(8,128)(2,1)S(1)}, bf16[128,1024]{1,0:T(8,128)(2,1)S(1)}, bf16[128,1024]{1,0:T(8,128)(2,1)S(1)}, bf16[256,1024]{1,0:T(8,128)(2,1)S(1)}) custom-call(s32[1]{0:T(128)} %bitcast.here_ref, bf16[512,1152]{1,0:T(8,128)(2,1)S(1)} %get-tuple-element.53.refs_4_.band_ref, bf16[528,1024]{1,0:T(8,128)(2,1)S(1)} %get-tuple-element.54.own_ref, ...), custom_call_target="tpu_custom_call" | custom-call | flops 3449999872 | bytes 1000 | tf_op jit(solution)/shard_map/pallas_call | solution.py:438
  55.8 1.2 collective-permute-start.20
  57.0 4.2 %collective-permute-start.13 = (bf16[512,1024]{1,0:T(8,128)(2,1)S(1)}, bf16[512,1024]{1,0:T(8,128)(2,1)S(1)}, u32[]{:S(2)}, u32[]{:S(2)}) collective-permute-start(bf16[512,1024]{1,0:T(8,128)(2,1)S(1)} %get-tuple-element.69.refs_0_.own_ref), channel_id=1, source_target_pairs={{0,4},{1,5},{2,6},{3,7},{4,8},{5,9},{6,10},{7,11},{8,12},{9,13},{1... | collective-permute-start | bytes 3145736 | tf_op jit(solution)/shard_map/ppermute | solution.py:27
  61.2 10.0 %shard_map.76 = (f32[128,8,1024]{2,1,0:T(8,128)}, f32[8,128]{1,0:T(8,128)S(1)}) custom-call(s32[1]{0:T(128)} %bitcast.here_ref, bf16[144,1024]{1,0:T(8,128)(2,1)S(1)} %collective-permute-done.refs_1_.near_ref, bf16[528,1024]{1,0:T(8,128)(2,1)S(1)} %collective-permute-done.3.high_ref.next_level_ref, ...), custom_call_target="tpu_custom_call" | custom-call | bytes 1000 | tf_op jit(solution)/shard_map/pallas_call | solution.py:538
  71.2 2.1 %collective-permute-start.18 = (bf16[128,1024]{1,0:T(8,128)(2,1)S(1)}, bf16[128,1024]{1,0:T(8,128)(2,1)S(1)}, u32[]{:S(2)}, u32[]{:S(2)}) collective-permute-start(bf16[128,1024]{1,0:T(8,128)(2,1)S(1)} %slice.10), channel_id=1, source_target_pairs={{0,1},{1,0},{2,3},{3,2},{4,5},{5,4},{6,7},{7,6},{8,9},{9,8},{10,11... | collective-permute-start | bytes 786440 | tf_op jit(solution)/shard_map/ppermute | solution.py:32
  73.4 1.1 collective-permute-done.18.refs_3_
  74.5 1.3 collective-permute-start.14
  75.8 0.9 collective-permute-done.20.refs_6_.refs_2_
  76.8 2.1 %shard_map.77 = (bf16[512,1024]{1,0:T(8,128)(2,1)S(1)}, bf16[128,1024]{1,0:T(8,128)(2,1)S(1)}) custom-call(s32[1]{0:T(128)} %bitcast.here_ref, bf16[512,1152]{1,0:T(8,128)(2,1)S(1)} %get-tuple-element.53.refs_4_.band_ref, bf16[512,1024]{1,0:T(8,128)(2,1)S(1)} %get-tuple-element.65.refs_0_.own_ref, bf16[512,1024]{1,0:T(8,128)(2,1)S(1)} %collective-permute-done.15.high_ref, ...), custom_call_target="tpu_custom_call" | custom-call | flops 3449999872 | bytes 1000 | tf_op jit(solution)/shard_map/pallas_call | solution.py:438
  78.8 1.3 collective-permute-start.21
  80.1 4.8 %collective-permute-start.25 = (bf16[512,1024]{1,0:T(8,128)(2,1)S(1)}, bf16[512,1024]{1,0:T(8,128)(2,1)S(1)}, u32[]{:S(2)}, u32[]{:S(2)}) collective-permute-start(bf16[512,1024]{1,0:T(8,128)(2,1)S(1)} %get-tuple-element.81.refs_0_.own_ref), channel_id=1, source_target_pairs={{0,4},{1,5},{2,6},{3,7},{4,8},{5,9},{6,10},{7,11},{8,12},{9,13},{1... | collective-permute-start | bytes 3145736 | tf_op jit(solution)/shard_map/ppermute | solution.py:27
  85.0 2.5 %collective-permute-start.26 = (bf16[128,1024]{1,0:T(8,128)(2,1)S(1)}, bf16[128,1024]{1,0:T(8,128)(2,1)S(1)}, u32[]{:S(2)}, u32[]{:S(2)}) collective-permute-start(bf16[128,1024]{1,0:T(8,128)(2,1)S(1)} %slice.11), channel_id=1, source_target_pairs={{0,1},{1,0},{2,3},{3,2},{4,5},{5,4},{6,7},{7,6},{8,9},{9,8},{10,11... | collective-permute-start | bytes 786440 | tf_op jit(solution)/shard_map/ppermute | solution.py:32
  87.5 1.0 collective-permute-done.21.refs_1_.high_ref
  88.4 2.1 %shard_map.78 = (bf16[256,1024]{1,0:T(8,128)(2,1)S(1)}, bf16[256,1024]{1,0:T(8,128)(2,1)S(1)}, bf16[256,1024]{1,0:T(8,128)(2,1)S(1)}, bf16[256,1024]{1,0:T(8,128)(2,1)S(1)}) custom-call(s32[1]{0:T(128)} %bitcast.here_ref, bf16[512,1152]{1,0:T(8,128)(2,1)S(1)} %get-tuple-element.71.band_ref, bf16[512,1024]{1,0:T(8,128)(2,1)S(1)} %get-tuple-element.69.refs_0_.own_ref, ...), custom_call_target="tpu_custom_call" | custom-call | bytes 1000 | tf_op jit(solution)/shard_map/pallas_call | solution.py:470
  92.2 2.3 %collective-permute-start.22 = (bf16[256,1024]{1,0:T(8,128)(2,1)S(1)}, bf16[256,1024]{1,0:T(8,128)(2,1)S(1)}, u32[]{:S(2)}, u32[]{:S(2)}) collective-permute-start(bf16[256,1024]{1,0:T(8,128)(2,1)S(1)} %get-tuple-element.85), channel_id=1, source_target_pairs={{0,1},{1,0},{2,3},{3,2},{4,5},{5,4},{6,7},{7,6},{8,9},{9,8},{10,11... | collective-permute-start | bytes 1572872 | tf_op jit(solution)/shard_map/ppermute | solution.py:32
  94.7 1.5 %collective-permute-start.24 = (bf16[256,1024]{1,0:T(8,128)(2,1)S(1)}, bf16[256,1024]{1,0:T(8,128)(2,1)S(1)}, u32[]{:S(2)}, u32[]{:S(2)}) collective-permute-start(bf16[256,1024]{1,0:T(8,128)(2,1)S(1)} %get-tuple-element.87), channel_id=1, source_target_pairs={{0,3},{1,2},{2,1},{3,0},{4,7},{5,6},{6,5},{7,4},{8,11},{9,10},{10,... | collective-permute-start | bytes 1572872 | tf_op jit(solution)/shard_map/ppermute | solution.py:32
  96.2 1.2 shard_map.79
  97.4 7.8 %collective-permute-done.25.low_ref = bf16[512,1024]{1,0:T(8,128)(2,1)S(1)} collective-permute-done((bf16[512,1024]{1,0:T(8,128)(2,1)S(1)}, bf16[512,1024]{1,0:T(8,128)(2,1)S(1)}, u32[]{:S(2)}, u32[]{:S(2)}) %collective-permute-start.25) | collective-permute-done | bytes 1048608 | tf_op jit(solution)/shard_map/ppermute | solution.py:27
  105.2 2.0 %shard_map.81 = (bf16[128,1024]{1,0:T(8,128)(2,1)S(1)}, bf16[128,1024]{1,0:T(8,128)(2,1)S(1)}, bf16[128,1024]{1,0:T(8,128)(2,1)S(1)}, bf16[128,1024]{1,0:T(8,128)(2,1)S(1)}) custom-call(s32[1]{0:T(128)} %bitcast.here_ref, bf16[512,1152]{1,0:T(8,128)(2,1)S(1)} %get-tuple-element.71.band_ref, bf16[512,1024]{1,0:T(8,128)(2,1)S(1)} %get-tuple-element.81.refs_0_.own_ref, ...), custom_call_target="tpu_custom_call" | custom-call | bytes 1000 | tf_op jit(solution)/shard_map/pallas_call | solution.py:470
  107.2 3.1 %collective-permute-start.27 = (bf16[128,1024]{1,0:T(8,128)(2,1)S(1)}, bf16[128,1024]{1,0:T(8,128)(2,1)S(1)}, u32[]{:S(2)}, u32[]{:S(2)}) collective-permute-start(bf16[128,1024]{1,0:T(8,128)(2,1)S(1)} %get-tuple-element.91), channel_id=1, source_target_pairs={{0,1},{1,0},{2,3},{3,2},{4,5},{5,4},{6,7},{7,6},{8,9},{9,8},{10,11... | collective-permute-start | bytes 786440 | tf_op jit(solution)/shard_map/ppermute | solution.py:32
  111.0 1.0 collective-permute-start.29
  112.0 7.9 %collective-permute-done.24.refs_3_ = bf16[256,1024]{1,0:T(8,128)(2,1)S(1)} collective-permute-done((bf16[256,1024]{1,0:T(8,128)(2,1)S(1)}, bf16[256,1024]{1,0:T(8,128)(2,1)S(1)}, u32[]{:S(2)}, u32[]{:S(2)}) %collective-permute-start.24) | collective-permute-done | bytes 524320 | tf_op jit(solution)/shard_map/ppermute | solution.py:32
  119.9 2.9 %shard_map.82.tv_ref = f32[128,8,1024]{2,1,0:T(8,128)} custom-call(s32[1]{0:T(128)} %bitcast.here_ref, f32[128,8,1024]{2,1,0:T(8,128)} %get-tuple-element.84.tv_ref, bf16[256,1024]{1,0:T(8,128)(2,1)S(1)} %get-tuple-element.83.refs_4_.refs_0_, bf16[256,1024]{1,0:T(8,128)(2,1)S(1)} %collective-permute-done.22.refs_1_, ...), custom_call_target="tpu_custom_call", output_to_operand_aliasing={{}: (1, {})} | custom-call | bytes 1000 | tf_op jit(solution)/shard_map/pallas_call | solution.py:359
  122.8 2.6 %shard_map.83.refs_4_ = bf16[128,8,1024]{2,1,0:T(8,128)(2,1)} custom-call(s32[1]{0:T(128)} %bitcast.here_ref, bf16[128,8,512]{2,1,0:T(8,128)(2,1)S(1)} %shard_map.80.refs_1_.own_ref, bf16[128,8,512]{2,1,0:T(8,128)(2,1)S(1)} %collective-permute-done.30.above_ref, bf16[256,1024]{1,0:T(8,128)(2,1)S(1)} %get-tuple-element.83.refs_4_.refs_0_, ...), custom_call_target="tpu_custom_call" | custom-call | bytes 1000 | tf_op jit(solution)/shard_map/pallas_call | solution.py:337
  125.4 5.2 %collective-permute-done.29.refs_3_ = bf16[128,1024]{1,0:T(8,128)(2,1)S(1)} collective-permute-done((bf16[128,1024]{1,0:T(8,128)(2,1)S(1)}, bf16[128,1024]{1,0:T(8,128)(2,1)S(1)}, u32[]{:S(2)}, u32[]{:S(2)}) %collective-permute-start.29) | collective-permute-done | bytes 262176 | tf_op jit(solution)/shard_map/ppermute | solution.py:32
  130.6 2.9 %shard_map.84 = f32[128,8,1024]{2,1,0:T(8,128)} custom-call(s32[1]{0:T(128)} %bitcast.here_ref, f32[128,8,1024]{2,1,0:T(8,128)} %shard_map.82.tv_ref, bf16[128,1024]{1,0:T(8,128)(2,1)S(1)} %get-tuple-element.90.refs_4_.refs_0_, bf16[128,1024]{1,0:T(8,128)(2,1)S(1)} %collective-permute-done.27.refs_1_, ...), custom_call_target="tpu_custom_call", output_to_operand_aliasing={{}: (1, {})} | custom-call | bytes 1000 | tf_op jit(solution)/shard_map/pallas_call | solution.py:359
  (50 shorter events, 6.3 us)
Async XLA Ops:
  3.2 29.7 %collective-permute-start.4 = (bf16[128,8,1024]{2,1,0:T(8,128)(2,1)}, bf16[128,8,1024]{2,1,0:T(8,128)(2,1)S(1)}, u32[]{:S(2)}, u32[]{:S(2)}) collective-permute-start(bf16[128,8,1024]{2,1,0:T(8,128)(2,1)} %refs_2_.1), channel_id=1, source_target_pairs={{3,7},{7,11},{11,15},{19,23},{23,27},{27,31}} | collective-permute-start | bytes 6291464 | tf_op jit(solution)/shard_map/ppermute | solution.py:27
  4.0 13.5 %collective-permute-start = (bf16[144,1024]{1,0:T(8,128)(2,1)S(1)}, bf16[144,1024]{1,0:T(8,128)(2,1)S(1)}, u32[]{:S(2)}, u32[]{:S(2)}) collective-permute-start(bf16[144,1024]{1,0:T(8,128)(2,1)S(1)} %get-tuple-element.48.refs_2_), channel_id=1, source_target_pairs={{0,1},{1,0},{2,3},{3,2},{4,5},{5,4},{6,7},{7,6},{8,9},{9,8},{10,11... | collective-permute-start | bytes 884744 | tf_op jit(solution)/shard_map/ppermute | solution.py:32
  4.1 13.4 %collective-permute-start.1 = (bf16[128,1024]{1,0:T(8,128)(2,1)}, bf16[128,1024]{1,0:T(8,128)(2,1)}, u32[]{:S(2)}, u32[]{:S(2)}) collective-permute-start(bf16[128,1024]{1,0:T(8,128)(2,1)} %get-tuple-element.50), channel_id=1, source_target_pairs={{0,2},{1,3},{2,0},{3,1},{4,6},{5,7},{6,4},{7,5},{8,10},{9,11},{10,... | collective-permute-start | bytes 786440 | tf_op jit(solution)/shard_map/ppermute | solution.py:32
  8.7 5.3 %copy-start.6 = (s32[16,6]{0,1:T(8,128)S(1)}, s32[16,6]{0,1:T(8,128)}, u32[]{:S(2)}) copy-start(s32[16,6]{0,1:T(8,128)} %param.8) | copy-start | bytes 1156
  8.7 6.1 %copy-start = (bf16[8,128,128]{2,1,0:T(8,128)(2,1)S(1)}, bf16[8,128,128]{2,1,0:T(8,128)(2,1)}, u32[]{:S(2)}) copy-start(bf16[8,128,128]{2,1,0:T(8,128)(2,1)} %refs_0_.1) | copy-start | bytes 786436
  8.7 13.6 %collective-permute-start.2 = (bf16[144,1024]{1,0:T(8,128)(2,1)S(1)}, bf16[144,1024]{1,0:T(8,128)(2,1)S(1)}, u32[]{:S(2)}, u32[]{:S(2)}) collective-permute-start(bf16[144,1024]{1,0:T(8,128)(2,1)S(1)} %get-tuple-element.51), channel_id=1, source_target_pairs={{0,3},{1,2},{2,1},{3,0},{4,7},{5,6},{6,5},{7,4},{8,11},{9,10},{10,... | collective-permute-start | bytes 884744 | tf_op jit(solution)/shard_map/ppermute | solution.py:32
  11.6 0.7 copy-start.3
  12.3 20.6 %collective-permute-start.5 = (bf16[256,1024]{1,0:T(8,128)(2,1)}, bf16[256,1024]{1,0:T(8,128)(2,1)}, u32[]{:S(2)}, u32[]{:S(2)}) collective-permute-start(bf16[256,1024]{1,0:T(8,128)(2,1)} %get-tuple-element.57), channel_id=1, source_target_pairs={{0,2},{1,3},{2,0},{3,1},{4,6},{5,7},{6,4},{7,5},{8,10},{9,11},{10,... | collective-permute-start | bytes 1572872 | tf_op jit(solution)/shard_map/ppermute | solution.py:32
  14.8 1.0 copy-start.4
  15.8 6.6 %copy-start.2 = (bf16[128,1024]{1,0:T(8,128)(2,1)S(1)}, bf16[128,1024]{1,0:T(8,128)(2,1)}, u32[]{:S(2)}) copy-start(bf16[128,1024]{1,0:T(8,128)(2,1)} %get-tuple-element.49.refs_0_) | copy-start | bytes 786436
  22.4 1.2 copy-start.5
  23.6 18.1 %copy-start.1 = (bf16[128,1024]{1,0:T(8,128)(2,1)S(1)}, bf16[128,1024]{1,0:T(8,128)(2,1)}, u32[]{:S(2)}) copy-start(bf16[128,1024]{1,0:T(8,128)(2,1)} %get-tuple-element.63.refs_0_) | copy-start | bytes 786436
  23.6 9.3 %collective-permute-start.6 = (bf16[128,1024]{1,0:T(8,128)(2,1)S(1)}, bf16[128,1024]{1,0:T(8,128)(2,1)S(1)}, u32[]{:S(2)}, u32[]{:S(2)}) collective-permute-start(bf16[128,1024]{1,0:T(8,128)(2,1)S(1)} %copy-done.5), channel_id=1, source_target_pairs={{0,1},{1,0},{2,3},{3,2},{4,5},{5,4},{6,7},{7,6},{8,9},{9,8},{10,11... | collective-permute-start | bytes 786440 | tf_op jit(solution)/shard_map/ppermute | solution.py:32
  23.9 28.3 %collective-permute-start.3 = (bf16[528,1024]{1,0:T(8,128)(2,1)S(1)}, bf16[528,1024]{1,0:T(8,128)(2,1)S(1)}, u32[]{:S(2)}, u32[]{:S(2)}) collective-permute-start(bf16[528,1024]{1,0:T(8,128)(2,1)S(1)} %get-tuple-element.54.own_ref), channel_id=1, source_target_pairs={{4,0},{5,1},{6,2},{7,3},{8,4},{9,5},{10,6},{11,7},{12,8},{13,9},{1... | collective-permute-start | bytes 3244040 | tf_op jit(solution)/shard_map/ppermute | solution.py:27
  34.7 12.5 %collective-permute-start.9 = (bf16[256,1024]{1,0:T(8,128)(2,1)S(1)}, bf16[256,1024]{1,0:T(8,128)(2,1)S(1)}, u32[]{:S(2)}, u32[]{:S(2)}) collective-permute-start(bf16[256,1024]{1,0:T(8,128)(2,1)S(1)} %get-tuple-element.62), channel_id=1, source_target_pairs={{0,2},{1,3},{2,0},{3,1},{4,6},{5,7},{6,4},{7,5},{8,10},{9,11},{10,... | collective-permute-start | bytes 1572872 | tf_op jit(solution)/shard_map/ppermute | solution.py:32
  35.9 2.7 %collective-permute-start.7 = (bf16[128,1024]{1,0:T(8,128)(2,1)S(1)}, bf16[128,1024]{1,0:T(8,128)(2,1)S(1)}, u32[]{:S(2)}, u32[]{:S(2)}) collective-permute-start(bf16[128,1024]{1,0:T(8,128)(2,1)S(1)} %get-tuple-element.59), channel_id=1, source_target_pairs={{0,1},{1,0},{2,3},{3,2},{4,5},{5,4},{6,7},{7,6},{8,9},{9,8},{10,11... | collective-permute-start | bytes 786440 | tf_op jit(solution)/shard_map/ppermute | solution.py:32
  37.5 4.2 %collective-permute-start.10 = (bf16[128,1024]{1,0:T(8,128)(2,1)S(1)}, bf16[128,1024]{1,0:T(8,128)(2,1)S(1)}, u32[]{:S(2)}, u32[]{:S(2)}) collective-permute-start(bf16[128,1024]{1,0:T(8,128)(2,1)S(1)} %get-tuple-element.64), channel_id=1, source_target_pairs={{0,1},{1,0},{2,3},{3,2},{4,5},{5,4},{6,7},{7,6},{8,9},{9,8},{10,11... | collective-permute-start | bytes 786440 | tf_op jit(solution)/shard_map/ppermute | solution.py:32
  38.6 15.0 %collective-permute-start.8 = (bf16[144,1024]{1,0:T(8,128)(2,1)S(1)}, bf16[144,1024]{1,0:T(8,128)(2,1)S(1)}, u32[]{:S(2)}, u32[]{:S(2)}) collective-permute-start(bf16[144,1024]{1,0:T(8,128)(2,1)S(1)} %get-tuple-element.60), channel_id=1, source_target_pairs={{0,4},{1,5},{2,6},{3,7},{4,8},{5,9},{6,10},{7,11},{8,12},{9,13},{1... | collective-permute-start | bytes 884744 | tf_op jit(solution)/shard_map/ppermute | solution.py:27
  42.9 10.4 %collective-permute-start.12 = (bf16[128,1024]{1,0:T(8,128)(2,1)S(1)}, bf16[128,1024]{1,0:T(8,128)(2,1)S(1)}, u32[]{:S(2)}, u32[]{:S(2)}) collective-permute-start(bf16[128,1024]{1,0:T(8,128)(2,1)S(1)} %get-tuple-element.67), channel_id=1, source_target_pairs={{0,4},{1,5},{2,6},{3,7},{4,8},{5,9},{6,10},{7,11},{8,12},{9,13},{1... | collective-permute-start | bytes 786440 | tf_op jit(solution)/shard_map/ppermute | solution.py:27
  47.3 6.4 %collective-permute-start.11 = (bf16[128,1024]{1,0:T(8,128)(2,1)S(1)}, bf16[128,1024]{1,0:T(8,128)(2,1)S(1)}, u32[]{:S(2)}, u32[]{:S(2)}) collective-permute-start(bf16[128,1024]{1,0:T(8,128)(2,1)S(1)} %slice.9), channel_id=1, source_target_pairs={{0,1},{1,0},{2,3},{3,2},{4,5},{5,4},{6,7},{7,6},{8,9},{9,8},{10,11... | collective-permute-start | bytes 786440 | tf_op jit(solution)/shard_map/ppermute | solution.py:32
  49.2 26.6 %collective-permute-start.15 = (bf16[512,1024]{1,0:T(8,128)(2,1)S(1)}, bf16[512,1024]{1,0:T(8,128)(2,1)S(1)}, u32[]{:S(2)}, u32[]{:S(2)}) collective-permute-start(bf16[512,1024]{1,0:T(8,128)(2,1)S(1)} %get-tuple-element.65.refs_0_.own_ref), channel_id=1, source_target_pairs={{4,0},{5,1},{6,2},{7,3},{8,4},{9,5},{10,6},{11,7},{12,8},{13,9},{1... | collective-permute-start | bytes 3145736 | tf_op jit(solution)/shard_map/ppermute | solution.py:27
  52.2 3.6 %collective-permute-start.16 = (bf16[128,1024]{1,0:T(8,128)(2,1)S(1)}, bf16[128,1024]{1,0:T(8,128)(2,1)S(1)}, u32[]{:S(2)}, u32[]{:S(2)}) collective-permute-start(bf16[128,1024]{1,0:T(8,128)(2,1)S(1)} %get-tuple-element.73), channel_id=1, source_target_pairs={{0,1},{1,0},{2,3},{3,2},{4,5},{5,4},{6,7},{7,6},{8,9},{9,8},{10,11... | collective-permute-start | bytes 786440 | tf_op jit(solution)/shard_map/ppermute | solution.py:32
  53.3 17.9 %collective-permute-start.17 = (bf16[256,1024]{1,0:T(8,128)(2,1)S(1)}, bf16[256,1024]{1,0:T(8,128)(2,1)S(1)}, u32[]{:S(2)}, u32[]{:S(2)}) collective-permute-start(bf16[256,1024]{1,0:T(8,128)(2,1)S(1)} %get-tuple-element.74), channel_id=1, source_target_pairs={{0,2},{1,3},{2,0},{3,1},{4,6},{5,7},{6,4},{7,5},{8,10},{9,11},{10,... | collective-permute-start | bytes 1572872 | tf_op jit(solution)/shard_map/ppermute | solution.py:32
  55.8 21.0 %collective-permute-start.20 = (bf16[256,1024]{1,0:T(8,128)(2,1)S(1)}, bf16[256,1024]{1,0:T(8,128)(2,1)S(1)}, u32[]{:S(2)}, u32[]{:S(2)}) collective-permute-start(bf16[256,1024]{1,0:T(8,128)(2,1)S(1)} %get-tuple-element.80), channel_id=1, source_target_pairs={{0,2},{1,3},{2,0},{3,1},{4,6},{5,7},{6,4},{7,5},{8,10},{9,11},{10,... | collective-permute-start | bytes 1572872 | tf_op jit(solution)/shard_map/ppermute | solution.py:32
  57.0 31.4 %collective-permute-start.13 = (bf16[512,1024]{1,0:T(8,128)(2,1)S(1)}, bf16[512,1024]{1,0:T(8,128)(2,1)S(1)}, u32[]{:S(2)}, u32[]{:S(2)}) collective-permute-start(bf16[512,1024]{1,0:T(8,128)(2,1)S(1)} %get-tuple-element.69.refs_0_.own_ref), channel_id=1, source_target_pairs={{0,4},{1,5},{2,6},{3,7},{4,8},{5,9},{6,10},{7,11},{8,12},{9,13},{1... | collective-permute-start | bytes 3145736 | tf_op jit(solution)/shard_map/ppermute | solution.py:27
  71.2 3.3 %collective-permute-start.18 = (bf16[128,1024]{1,0:T(8,128)(2,1)S(1)}, bf16[128,1024]{1,0:T(8,128)(2,1)S(1)}, u32[]{:S(2)}, u32[]{:S(2)}) collective-permute-start(bf16[128,1024]{1,0:T(8,128)(2,1)S(1)} %slice.10), channel_id=1, source_target_pairs={{0,1},{1,0},{2,3},{3,2},{4,5},{5,4},{6,7},{7,6},{8,9},{9,8},{10,11... | collective-permute-start | bytes 786440 | tf_op jit(solution)/shard_map/ppermute | solution.py:32
  73.3 2.5 %collective-permute-start.19 = (bf16[128,1024]{1,0:T(8,128)(2,1)S(1)}, bf16[128,1024]{1,0:T(8,128)(2,1)S(1)}, u32[]{:S(2)}, u32[]{:S(2)}) collective-permute-start(bf16[128,1024]{1,0:T(8,128)(2,1)S(1)} %get-tuple-element.78), channel_id=1, source_target_pairs={{0,1},{1,0},{2,3},{3,2},{4,5},{5,4},{6,7},{7,6},{8,9},{9,8},{10,11... | collective-permute-start | bytes 786440 | tf_op jit(solution)/shard_map/ppermute | solution.py:32
  74.5 13.0 %collective-permute-start.14 = (bf16[128,1024]{1,0:T(8,128)(2,1)S(1)}, bf16[128,1024]{1,0:T(8,128)(2,1)S(1)}, u32[]{:S(2)}, u32[]{:S(2)}) collective-permute-start(bf16[128,1024]{1,0:T(8,128)(2,1)S(1)} %get-tuple-element.72), channel_id=1, source_target_pairs={{4,0},{5,1},{6,2},{7,3},{8,4},{9,5},{10,6},{11,7},{12,8},{13,9},{1... | collective-permute-start | bytes 786440 | tf_op jit(solution)/shard_map/ppermute | solution.py:27
  78.8 9.6 %collective-permute-start.21 = (bf16[128,1024]{1,0:T(8,128)(2,1)S(1)}, bf16[128,1024]{1,0:T(8,128)(2,1)S(1)}, u32[]{:S(2)}, u32[]{:S(2)}) collective-permute-start(bf16[128,1024]{1,0:T(8,128)(2,1)S(1)} %get-tuple-element.82), channel_id=1, source_target_pairs={{4,0},{5,1},{6,2},{7,3},{8,4},{9,5},{10,6},{11,7},{12,8},{13,9},{1... | collective-permute-start | bytes 786440 | tf_op jit(solution)/shard_map/ppermute | solution.py:27
  80.1 25.1 %collective-permute-start.25 = (bf16[512,1024]{1,0:T(8,128)(2,1)S(1)}, bf16[512,1024]{1,0:T(8,128)(2,1)S(1)}, u32[]{:S(2)}, u32[]{:S(2)}) collective-permute-start(bf16[512,1024]{1,0:T(8,128)(2,1)S(1)} %get-tuple-element.81.refs_0_.own_ref), channel_id=1, source_target_pairs={{0,4},{1,5},{2,6},{3,7},{4,8},{5,9},{6,10},{7,11},{8,12},{9,13},{1... | collective-permute-start | bytes 3145736 | tf_op jit(solution)/shard_map/ppermute | solution.py:27
  85.0 5.6 %collective-permute-start.26 = (bf16[128,1024]{1,0:T(8,128)(2,1)S(1)}, bf16[128,1024]{1,0:T(8,128)(2,1)S(1)}, u32[]{:S(2)}, u32[]{:S(2)}) collective-permute-start(bf16[128,1024]{1,0:T(8,128)(2,1)S(1)} %slice.11), channel_id=1, source_target_pairs={{0,1},{1,0},{2,3},{3,2},{4,5},{5,4},{6,7},{7,6},{8,9},{9,8},{10,11... | collective-permute-start | bytes 786440 | tf_op jit(solution)/shard_map/ppermute | solution.py:32
  91.4 31.3 %collective-permute-start.30 = (bf16[128,8,512]{2,1,0:T(8,128)(2,1)S(1)}, bf16[128,8,512]{2,1,0:T(8,128)(2,1)S(1)}, u32[]{:S(2)}, u32[]{:S(2)}) collective-permute-start(bf16[128,8,512]{2,1,0:T(8,128)(2,1)S(1)} %shard_map.80.refs_1_.own_ref), channel_id=1, source_target_pairs={{7,3},{11,7},{15,11},{23,19},{27,23},{31,27}} | collective-permute-start | bytes 3145736 | tf_op jit(solution)/shard_map/ppermute | solution.py:27
  92.2 18.1 %collective-permute-start.22 = (bf16[256,1024]{1,0:T(8,128)(2,1)S(1)}, bf16[256,1024]{1,0:T(8,128)(2,1)S(1)}, u32[]{:S(2)}, u32[]{:S(2)}) collective-permute-start(bf16[256,1024]{1,0:T(8,128)(2,1)S(1)} %get-tuple-element.85), channel_id=1, source_target_pairs={{0,1},{1,0},{2,3},{3,2},{4,5},{5,4},{6,7},{7,6},{8,9},{9,8},{10,11... | collective-permute-start | bytes 1572872 | tf_op jit(solution)/shard_map/ppermute | solution.py:32
  94.5 16.5 %collective-permute-start.23 = (bf16[256,1024]{1,0:T(8,128)(2,1)S(1)}, bf16[256,1024]{1,0:T(8,128)(2,1)S(1)}, u32[]{:S(2)}, u32[]{:S(2)}) collective-permute-start(bf16[256,1024]{1,0:T(8,128)(2,1)S(1)} %get-tuple-element.86), channel_id=1, source_target_pairs={{0,2},{1,3},{2,0},{3,1},{4,6},{5,7},{6,4},{7,5},{8,10},{9,11},{10,... | collective-permute-start | bytes 1572872 | tf_op jit(solution)/shard_map/ppermute | solution.py:32
  94.7 25.1 %collective-permute-start.24 = (bf16[256,1024]{1,0:T(8,128)(2,1)S(1)}, bf16[256,1024]{1,0:T(8,128)(2,1)S(1)}, u32[]{:S(2)}, u32[]{:S(2)}) collective-permute-start(bf16[256,1024]{1,0:T(8,128)(2,1)S(1)} %get-tuple-element.87), channel_id=1, source_target_pairs={{0,3},{1,2},{2,1},{3,0},{4,7},{5,6},{6,5},{7,4},{8,11},{9,10},{10,... | collective-permute-start | bytes 1572872 | tf_op jit(solution)/shard_map/ppermute | solution.py:32
  107.2 18.3 %collective-permute-start.27 = (bf16[128,1024]{1,0:T(8,128)(2,1)S(1)}, bf16[128,1024]{1,0:T(8,128)(2,1)S(1)}, u32[]{:S(2)}, u32[]{:S(2)}) collective-permute-start(bf16[128,1024]{1,0:T(8,128)(2,1)S(1)} %get-tuple-element.91), channel_id=1, source_target_pairs={{0,1},{1,0},{2,3},{3,2},{4,5},{5,4},{6,7},{7,6},{8,9},{9,8},{10,11... | collective-permute-start | bytes 786440 | tf_op jit(solution)/shard_map/ppermute | solution.py:32
  110.3 15.1 %collective-permute-start.28 = (bf16[128,1024]{1,0:T(8,128)(2,1)S(1)}, bf16[128,1024]{1,0:T(8,128)(2,1)S(1)}, u32[]{:S(2)}, u32[]{:S(2)}) collective-permute-start(bf16[128,1024]{1,0:T(8,128)(2,1)S(1)} %get-tuple-element.92), channel_id=1, source_target_pairs={{0,2},{1,3},{2,0},{3,1},{4,6},{5,7},{6,4},{7,5},{8,10},{9,11},{10,... | collective-permute-start | bytes 786440 | tf_op jit(solution)/shard_map/ppermute | solution.py:32
  111.0 19.7 %collective-permute-start.29 = (bf16[128,1024]{1,0:T(8,128)(2,1)S(1)}, bf16[128,1024]{1,0:T(8,128)(2,1)S(1)}, u32[]{:S(2)}, u32[]{:S(2)}) collective-permute-start(bf16[128,1024]{1,0:T(8,128)(2,1)S(1)} %get-tuple-element.93), channel_id=1, source_target_pairs={{0,3},{1,2},{2,1},{3,0},{4,7},{5,6},{6,5},{7,4},{8,11},{9,10},{10,... | collective-permute-start | bytes 786440 | tf_op jit(solution)/shard_map/ppermute | solution.py:32

commit v13 on v12

--- a/solution.py
+++ b/solution.py
@@ -560,7 +560,7 @@
         return swapped(tied(over, *others)[depth:], 1)
 
     vols0 = cast_rows(here, volume, 0, single, True)
-    got = moved(tied(sinogram, vols0[0]), G, only=G - 1)
+    got = moved(sinogram, G, only=G - 1)
     got_vols0 = direct(vols0)
     v0, v1, v23 = cast_rows(here, volume, 1, paired, False, vols0[1])
     over = swapped(v23, 2)
@@ -576,18 +576,18 @@
 
     s0, s1, s23 = split_rows(here, sinogram, got, 1, paired, [], own1)
 
-    resid0, down0, r1, r23 = project(here, band_p, own0, high0, low0, sinos0, paired[1:], low1, s0)
+    resid0, down0, *r = project(here, band_p, own0, high0, low0, sinos0, single[1:], low1, s0)
     from_low0, from_high0 = moved(resid0, G), moved(down0, -G)
     s_near, s_over = swapped(s1, 1), swapped(s23, 2)
-    r_near, r_over = swapped(tied(r1, s_near), 1), swapped(tied(r23, s_near), 2)
+    got_r = [swapped(tied(array, s_near), m + 1) for m, array in enumerate(r)]
     tv, tv_done = half_tv(here, volume, [got_vols0[1], high0, got_vols0[3], low0], resid0)
     sinos1 = [(s0, 0), (s_near, 0), (s_over, 0), (beyond(s_over, tv_done), 0)]
-    resid1, down1 = project(here, band_p, own1, high1, low1, sinos1, (), tv_done, r_near, r_over)
+    resid1, down1 = project(here, band_p, own1, high1, low1, sinos1, (), tv_done, *got_r)
     from_low1, from_high1 = moved(resid1, G), moved(down1, -G)
 
     backs0 = back(here, band_b, resid0, from_low0, from_high0, [resid1, from_high1])
     got_backs0 = direct(backs0)
-    r_pieces = [(resid0, 0), (r_near, 0), (r_over, 0), (beyond(r_over, resid1), 0)]
+    r_pieces = [(array, 0) for array in [resid0] + got_r]
     natural0 = join_rows(here, r_pieces, sinogram.shape, backs0[0])
     above0 = moved(natural0, -G, only=G - 1)
     r_last, tv = last_group(here, coverage, offsets, weights, volume, sinogram, tv, backs0[0])

time: 135 us -> 142 us (1.052)
  waiting for transfers between devices: 39.8 us -> 52.9 us
  starting transfers between devices: 48.9 us -> 43.3 us
    ppermute x21, waiting for transfers between devices: 30 us -> 37.6 us  [swapped(): return lax.ppermute(value, 'slab', [(i, i ^ bits) for i in range(count)])]
    ppermute x10, waiting for transfers between devices: 9.85 us -> 15.3 us  [moved(): return lax.ppermute(value, 'slab', pairs)]
    ppermute x21, starting transfers between devices: 27 us -> 22.1 us  [swapped(): return lax.ppermute(value, 'slab', [(i, i ^ bits) for i in range(count)])]
  transfers between devices with their start and end apart: 31 -> 31, of which waited for: 12 -> 10; matrix products, arithmetic and copies ran while one was open for 1% -> 1% of each run, Pallas kernels for 27% -> 27%
where the time goes in v13:
time: 142 us; the launch traced here: 141 us
  waiting for transfers between devices  52.9 us (37%)
  starting transfers between devices  43.3 us (30%)
  Pallas kernels  41.3 us (29%)
  local copies, waits for them, and re-layouts  2.57 us (2%)
    ppermute x21, waiting for transfers between devices, swapped(): return lax.ppermute(value, 'slab', [(i, i ^ bits) for i in range(count)])  37.6 us
    ppermute x21, starting transfers between devices, swapped(): return lax.ppermute(value, 'slab', [(i, i ^ bits) for i in range(count)])  22.1 us
    ppermute x10, starting transfers between devices, moved(): return lax.ppermute(value, 'slab', pairs)  21.2 us
    ppermute x10, waiting for transfers between devices, moved(): return lax.ppermute(value, 'slab', pairs)  15.3 us
    pallas_call x1, Pallas kernels, half_tv(): call(tv_kernel, 0, grid=(depth // deep,), in_specs=[SMEM] + edges + [afte...  10 us
    pallas_call x2, Pallas kernels, finish(): call(finish_kernel, 0, grid=(count,), in_specs=[SMEM, part] + piece_specs...  5.85 us
    pallas_call x2, Pallas kernels, cast_rows(): call(functools.partial(cast_kernel, groups, len(edges)), 2, grid=(count,)...  5.02 us
    pallas_call x2, Pallas kernels, project(): call(functools.partial(project_kernel, groups), 3, grid=(cols // tile,),...  4.22 us
  transfers between devices with their start and end apart: 31, of which 10 were waited for; matrix products, arithmetic and copies ran while one was open for 1% of the time, Pallas kernels for 27%

profile of v13, /device:TPU:1, one launch (start us, length us, event | category | flops | bytes accessed | tf_op | source)
XLA Modules:
  0.0 141.0 jit_solution(5254841038942688796)
XLA Ops:
  1.4 2.5 %shard_map.68 = (bf16[128,1024]{1,0:T(8,128)(2,1)}, bf16[144,1024]{1,0:T(8,128)(2,1)S(1)}, bf16[128,1024]{1,0:T(8,128)(2,1)}, bf16[144,1024]{1,0:T(8,128)(2,1)S(1)}) custom-call(s32[1]{0:T(128)} %bitcast.here_ref, f32[1024,1024]{1,0:T(8,128)} %bitcast.2, f32[1024,1024]{1,0:T(8,128)} %bitcast.3, f32[1024,1024]{1,0:T(8,128)} %bitcast.4, f32[1024,1024]{1,0:T(8,128)} %bitcast.5), custom_call_target="tpu_custom_call" | custom-call | flops 2300000000 | bytes 1000 | tf_op jit(solution)/shard_map/pallas_call | solution.py:110
  4.0 4.6 %collective-permute-start.1 = (bf16[128,1024]{1,0:T(8,128)(2,1)}, bf16[128,1024]{1,0:T(8,128)(2,1)}, u32[]{:S(2)}, u32[]{:S(2)}) collective-permute-start(bf16[128,1024]{1,0:T(8,128)(2,1)} %get-tuple-element.50), channel_id=1, source_target_pairs={{0,2},{1,3},{2,0},{3,1},{4,6},{5,7},{6,4},{7,5},{8,10},{9,11},{10,... | collective-permute-start | bytes 786440 | tf_op jit(solution)/shard_map/ppermute | solution.py:32
  9.0 2.5 %shard_map.69 = (bf16[128,1024]{1,0:T(8,128)(2,1)}, bf16[128,1024]{1,0:T(8,128)(2,1)S(1)}, bf16[256,1024]{1,0:T(8,128)(2,1)}) custom-call(s32[1]{0:T(128)} %bitcast.here_ref, f32[1024,1024]{1,0:T(8,128)} %bitcast.6, f32[1024,1024]{1,0:T(8,128)} %bitcast.7, bf16[144,1024]{1,0:T(8,128)(2,1)S(1)} %get-tuple-element.48.refs_2_), custom_call_target="tpu_custom_call" | custom-call | flops 2300000000 | bytes 1000 | tf_op jit(solution)/shard_map/pallas_call | solution.py:110
  12.2 1.7 %collective-permute-start.5 = (bf16[256,1024]{1,0:T(8,128)(2,1)}, bf16[256,1024]{1,0:T(8,128)(2,1)}, u32[]{:S(2)}, u32[]{:S(2)}) collective-permute-start(bf16[256,1024]{1,0:T(8,128)(2,1)} %get-tuple-element.56), channel_id=1, source_target_pairs={{0,2},{1,3},{2,0},{3,1},{4,6},{5,7},{6,4},{7,5},{8,10},{9,11},{10,... | collective-permute-start | bytes 1572872 | tf_op jit(solution)/shard_map/ppermute | solution.py:32
  14.8 0.9 copy-done.4
  15.7 1.6 %shard_map.70 = (bf16[512,1152]{1,0:T(8,128)(2,1)S(1)}, bf16[512,1152]{1,0:T(8,128)(2,1)S(1)}) custom-call(s32[1]{0:T(128)} %bitcast.here_ref, s32[16,6]{1,0:T(8,128)S(1)} %copy.12.cover_ref, s32[16,6]{1,0:T(8,128)S(1)} %copy.13.offset_ref, bf16[8,128,128]{2,1,0:T(8,128)(2,1)S(1)} %copy-done, bf16[128,1024]{1,0:T(8,128)(2,1)S(1)} %copy-done.4), custom_call_target="tpu_custom_call" | custom-call | flops 10350000128 | bytes 1000 | tf_op jit(solution)/shard_map/pallas_call | solution.py:407
  17.4 4.9 %collective-permute-done.2.refs_3_.far_ref = bf16[144,1024]{1,0:T(8,128)(2,1)S(1)} collective-permute-done((bf16[144,1024]{1,0:T(8,128)(2,1)S(1)}, bf16[144,1024]{1,0:T(8,128)(2,1)S(1)}, u32[]{:S(2)}, u32[]{:S(2)}) %collective-permute-start.2) | collective-permute-done | bytes 294944 | tf_op jit(solution)/shard_map/ppermute | solution.py:32
  22.3 1.2 shard_map.71
  23.9 1.3 collective-permute-start.3
  25.2 7.6 %collective-permute-done.5.refs_0_.refs_2_ = bf16[256,1024]{1,0:T(8,128)(2,1)} collective-permute-done((bf16[256,1024]{1,0:T(8,128)(2,1)}, bf16[256,1024]{1,0:T(8,128)(2,1)}, u32[]{:S(2)}, u32[]{:S(2)}) %collective-permute-start.5) | collective-permute-done | bytes 524320 | tf_op jit(solution)/shard_map/ppermute | solution.py:32
  32.8 1.8 %shard_map.72 = (bf16[128,1024]{1,0:T(8,128)(2,1)S(1)}, bf16[128,1024]{1,0:T(8,128)(2,1)S(1)}, bf16[256,1024]{1,0:T(8,128)(2,1)S(1)}, bf16[128,1024]{1,0:T(8,128)(2,1)S(1)}) custom-call(s32[1]{0:T(128)} %bitcast.here_ref, bf16[128,8,1024]{2,1,0:T(8,128)(2,1)} %refs_2_.1, bf16[128,8,1024]{2,1,0:T(8,128)(2,1)S(1)} %collective-permute-done.4.got_ref, ...), custom_call_target="tpu_custom_call" | custom-call | flops 2300000000 | bytes 1000 | tf_op jit(solution)/shard_map/pallas_call | solution.py:189
  34.6 1.2 collective-permute-start.9
  35.8 1.6 %collective-permute-start.7 = (bf16[128,1024]{1,0:T(8,128)(2,1)S(1)}, bf16[128,1024]{1,0:T(8,128)(2,1)S(1)}, u32[]{:S(2)}, u32[]{:S(2)}) collective-permute-start(bf16[128,1024]{1,0:T(8,128)(2,1)S(1)} %get-tuple-element.58), channel_id=1, source_target_pairs={{0,1},{1,0},{2,3},{3,2},{4,5},{5,4},{6,7},{7,6},{8,9},{9,8},{10,11... | collective-permute-start | bytes 786440 | tf_op jit(solution)/shard_map/ppermute | solution.py:32
  37.4 1.2 collective-permute-done.7.refs_1_
  38.6 3.1 %collective-permute-start.8 = (bf16[144,1024]{1,0:T(8,128)(2,1)S(1)}, bf16[144,1024]{1,0:T(8,128)(2,1)S(1)}, u32[]{:S(2)}, u32[]{:S(2)}) collective-permute-start(bf16[144,1024]{1,0:T(8,128)(2,1)S(1)} %get-tuple-element.59), channel_id=1, source_target_pairs={{0,4},{1,5},{2,6},{3,7},{4,8},{5,9},{6,10},{7,11},{8,12},{9,13},{1... | collective-permute-start | bytes 884744 | tf_op jit(solution)/shard_map/ppermute | solution.py:27
  41.7 1.2 shard_map.73
  42.8 3.2 %collective-permute-start.12 = (bf16[128,1024]{1,0:T(8,128)(2,1)S(1)}, bf16[128,1024]{1,0:T(8,128)(2,1)S(1)}, u32[]{:S(2)}, u32[]{:S(2)}) collective-permute-start(bf16[128,1024]{1,0:T(8,128)(2,1)S(1)} %get-tuple-element.66), channel_id=1, source_target_pairs={{0,4},{1,5},{2,6},{3,7},{4,8},{5,9},{6,10},{7,11},{8,12},{9,13},{1... | collective-permute-start | bytes 786440 | tf_op jit(solution)/shard_map/ppermute | solution.py:27
  46.0 1.1 collective-permute-done.9.refs_2_
  47.2 1.9 %collective-permute-start.11 = (bf16[128,1024]{1,0:T(8,128)(2,1)S(1)}, bf16[128,1024]{1,0:T(8,128)(2,1)S(1)}, u32[]{:S(2)}, u32[]{:S(2)}) collective-permute-start(bf16[128,1024]{1,0:T(8,128)(2,1)S(1)} %slice.6), channel_id=1, source_target_pairs={{0,1},{1,0},{2,3},{3,2},{4,5},{5,4},{6,7},{7,6},{8,9},{9,8},{10,11... | collective-permute-start | bytes 786440 | tf_op jit(solution)/shard_map/ppermute | solution.py:32
  49.1 1.7 %shard_map.74 = (bf16[128,1024]{1,0:T(8,128)(2,1)S(1)}, bf16[128,1024]{1,0:T(8,128)(2,1)S(1)}, bf16[256,1024]{1,0:T(8,128)(2,1)S(1)}) custom-call(s32[1]{0:T(128)} %bitcast.here_ref, bf16[128,8,1024]{2,1,0:T(8,128)(2,1)} %refs_2_.1, bf16[128,8,1024]{2,1,0:T(8,128)(2,1)S(1)} %collective-permute-done.4.got_ref, ...), custom_call_target="tpu_custom_call" | custom-call | flops 2300000000 | bytes 1000 | tf_op jit(solution)/shard_map/pallas_call | solution.py:189
  50.8 1.2 collective-permute-start.17
  52.1 1.3 collective-permute-start.15
  53.4 1.1 collective-permute-start.16
  54.4 2.1 %shard_map.75 = (bf16[512,1024]{1,0:T(8,128)(2,1)S(1)}, bf16[128,1024]{1,0:T(8,128)(2,1)S(1)}, bf16[128,1024]{1,0:T(8,128)(2,1)S(1)}, bf16[128,1024]{1,0:T(8,128)(2,1)S(1)}, bf16[128,1024]{1,0:T(8,128)(2,1)S(1)}) custom-call(s32[1]{0:T(128)} %bitcast.here_ref, bf16[512,1152]{1,0:T(8,128)(2,1)S(1)} %get-tuple-element.53.refs_4_.band_ref, ...), custom_call_target="tpu_custom_call" | custom-call | flops 3449999872 | bytes 1000 | tf_op jit(solution)/shard_map/pallas_call | solution.py:438
  56.6 10.0 %shard_map.76 = (f32[128,8,1024]{2,1,0:T(8,128)}, f32[8,128]{1,0:T(8,128)S(1)}) custom-call(s32[1]{0:T(128)} %bitcast.here_ref, bf16[144,1024]{1,0:T(8,128)(2,1)S(1)} %collective-permute-done.refs_1_.near_ref, bf16[528,1024]{1,0:T(8,128)(2,1)S(1)} %collective-permute-done.3.high_ref.next_level_ref, ...), custom_call_target="tpu_custom_call" | custom-call | bytes 1000 | tf_op jit(solution)/shard_map/pallas_call | solution.py:538
  66.7 4.2 %collective-permute-start.13 = (bf16[512,1024]{1,0:T(8,128)(2,1)S(1)}, bf16[512,1024]{1,0:T(8,128)(2,1)S(1)}, u32[]{:S(2)}, u32[]{:S(2)}) collective-permute-start(bf16[512,1024]{1,0:T(8,128)(2,1)S(1)} %get-tuple-element.68.refs_0_.own_ref), channel_id=1, source_target_pairs={{0,4},{1,5},{2,6},{3,7},{4,8},{5,9},{6,10},{7,11},{8,12},{9,13},{1... | collective-permute-start | bytes 3145736 | tf_op jit(solution)/shard_map/ppermute | solution.py:27
  72.4 1.0 collective-permute-start.21
  73.4 1.3 collective-permute-start.14
  74.7 4.9 %collective-permute-done.20.refs_6_.refs_2_ = bf16[128,1024]{1,0:T(8,128)(2,1)S(1)} collective-permute-done((bf16[128,1024]{1,0:T(8,128)(2,1)S(1)}, bf16[128,1024]{1,0:T(8,128)(2,1)S(1)}, u32[]{:S(2)}, u32[]{:S(2)}) %collective-permute-start.20) | collective-permute-done | bytes 262176 | tf_op jit(solution)/shard_map/ppermute | solution.py:32
  79.6 5.8 %collective-permute-done.21.refs_7_.refs_3_ = bf16[128,1024]{1,0:T(8,128)(2,1)S(1)} collective-permute-done((bf16[128,1024]{1,0:T(8,128)(2,1)S(1)}, bf16[128,1024]{1,0:T(8,128)(2,1)S(1)}, u32[]{:S(2)}, u32[]{:S(2)}) %collective-permute-start.21) | collective-permute-done | bytes 262176 | tf_op jit(solution)/shard_map/ppermute | solution.py:32
  85.4 2.1 %shard_map.77 = (bf16[512,1024]{1,0:T(8,128)(2,1)S(1)}, bf16[128,1024]{1,0:T(8,128)(2,1)S(1)}) custom-call(s32[1]{0:T(128)} %bitcast.here_ref, bf16[512,1152]{1,0:T(8,128)(2,1)S(1)} %get-tuple-element.53.refs_4_.band_ref, bf16[512,1024]{1,0:T(8,128)(2,1)S(1)} %get-tuple-element.64.refs_0_.own_ref, bf16[512,1024]{1,0:T(8,128)(2,1)S(1)} %collective-permute-done.15.high_ref, ...), custom_call_target="tpu_custom_call" | custom-call | flops 3449999872 | bytes 1000 | tf_op jit(solution)/shard_map/pallas_call | solution.py:438
  87.5 1.3 collective-permute-start.22
  88.8 4.1 %collective-permute-start.26 = (bf16[512,1024]{1,0:T(8,128)(2,1)S(1)}, bf16[512,1024]{1,0:T(8,128)(2,1)S(1)}, u32[]{:S(2)}, u32[]{:S(2)}) collective-permute-start(bf16[512,1024]{1,0:T(8,128)(2,1)S(1)} %get-tuple-element.82.refs_0_.own_ref), channel_id=1, source_target_pairs={{0,4},{1,5},{2,6},{3,7},{4,8},{5,9},{6,10},{7,11},{8,12},{9,13},{1... | collective-permute-start | bytes 3145736 | tf_op jit(solution)/shard_map/ppermute | solution.py:27
  92.9 4.3 %collective-permute-done.22.refs_1_.high_ref = bf16[128,1024]{1,0:T(8,128)(2,1)S(1)} collective-permute-done((bf16[128,1024]{1,0:T(8,128)(2,1)S(1)}, bf16[128,1024]{1,0:T(8,128)(2,1)S(1)}, u32[]{:S(2)}, u32[]{:S(2)}) %collective-permute-start.22) | collective-permute-done | bytes 262176 | tf_op jit(solution)/shard_map/ppermute | solution.py:27
  97.2 2.1 %shard_map.78 = (bf16[256,1024]{1,0:T(8,128)(2,1)S(1)}, bf16[256,1024]{1,0:T(8,128)(2,1)S(1)}, bf16[256,1024]{1,0:T(8,128)(2,1)S(1)}, bf16[256,1024]{1,0:T(8,128)(2,1)S(1)}) custom-call(s32[1]{0:T(128)} %bitcast.here_ref, bf16[512,1152]{1,0:T(8,128)(2,1)S(1)} %get-tuple-element.70.band_ref, bf16[512,1024]{1,0:T(8,128)(2,1)S(1)} %get-tuple-element.68.refs_0_.own_ref, ...), custom_call_target="tpu_custom_call" | custom-call | bytes 1000 | tf_op jit(solution)/shard_map/pallas_call | solution.py:470
  99.3 0.9 shard_map.80.refs_1_.own_ref
  100.9 1.0 collective-permute-start.23
  102.6 1.1 collective-permute-start.25
  103.7 1.2 shard_map.79
  104.8 11.0 %collective-permute-done.26.low_ref = bf16[512,1024]{1,0:T(8,128)(2,1)S(1)} collective-permute-done((bf16[512,1024]{1,0:T(8,128)(2,1)S(1)}, bf16[512,1024]{1,0:T(8,128)(2,1)S(1)}, u32[]{:S(2)}, u32[]{:S(2)}) %collective-permute-start.26) | collective-permute-done | bytes 1048608 | tf_op jit(solution)/shard_map/ppermute | solution.py:27
  115.8 2.0 %shard_map.81 = (bf16[128,1024]{1,0:T(8,128)(2,1)S(1)}, bf16[128,1024]{1,0:T(8,128)(2,1)S(1)}, bf16[128,1024]{1,0:T(8,128)(2,1)S(1)}, bf16[128,1024]{1,0:T(8,128)(2,1)S(1)}) custom-call(s32[1]{0:T(128)} %bitcast.here_ref, bf16[512,1152]{1,0:T(8,128)(2,1)S(1)} %get-tuple-element.70.band_ref, bf16[512,1024]{1,0:T(8,128)(2,1)S(1)} %get-tuple-element.82.refs_0_.own_ref, ...), custom_call_target="tpu_custom_call" | custom-call | bytes 1000 | tf_op jit(solution)/shard_map/pallas_call | solution.py:470
  117.8 0.9 collective-permute-start.27
  119.4 1.0 collective-permute-start.29
  120.4 6.9 %collective-permute-done.25.refs_3_ = bf16[256,1024]{1,0:T(8,128)(2,1)S(1)} collective-permute-done((bf16[256,1024]{1,0:T(8,128)(2,1)S(1)}, bf16[256,1024]{1,0:T(8,128)(2,1)S(1)}, u32[]{:S(2)}, u32[]{:S(2)}) %collective-permute-start.25) | collective-permute-done | bytes 524320 | tf_op jit(solution)/shard_map/ppermute | solution.py:32
  127.3 2.9 %shard_map.82.tv_ref = f32[128,8,1024]{2,1,0:T(8,128)} custom-call(s32[1]{0:T(128)} %bitcast.here_ref, f32[128,8,1024]{2,1,0:T(8,128)} %get-tuple-element.85.tv_ref, bf16[256,1024]{1,0:T(8,128)(2,1)S(1)} %get-tuple-element.84.refs_4_.refs_0_, bf16[256,1024]{1,0:T(8,128)(2,1)S(1)} %collective-permute-done.23.refs_1_, ...), custom_call_target="tpu_custom_call", output_to_operand_aliasing={{}: (1, {})} | custom-call | bytes 1000 | tf_op jit(solution)/shard_map/pallas_call | solution.py:359
  130.2 2.6 %shard_map.83.refs_4_ = bf16[128,8,1024]{2,1,0:T(8,128)(2,1)} custom-call(s32[1]{0:T(128)} %bitcast.here_ref, bf16[128,8,512]{2,1,0:T(8,128)(2,1)S(1)} %shard_map.80.refs_1_.own_ref, bf16[128,8,512]{2,1,0:T(8,128)(2,1)S(1)} %collective-permute-done.30.above_ref, bf16[256,1024]{1,0:T(8,128)(2,1)S(1)} %get-tuple-element.84.refs_4_.refs_0_, ...), custom_call_target="tpu_custom_call" | custom-call | bytes 1000 | tf_op jit(solution)/shard_map/pallas_call | solution.py:337
  132.9 5.2 %collective-permute-done.29.refs_3_ = bf16[128,1024]{1,0:T(8,128)(2,1)S(1)} collective-permute-done((bf16[128,1024]{1,0:T(8,128)(2,1)S(1)}, bf16[128,1024]{1,0:T(8,128)(2,1)S(1)}, u32[]{:S(2)}, u32[]{:S(2)}) %collective-permute-start.29) | collective-permute-done | bytes 262176 | tf_op jit(solution)/shard_map/ppermute | solution.py:32
  138.1 2.9 %shard_map.84 = f32[128,8,1024]{2,1,0:T(8,128)} custom-call(s32[1]{0:T(128)} %bitcast.here_ref, f32[128,8,1024]{2,1,0:T(8,128)} %shard_map.82.tv_ref, bf16[128,1024]{1,0:T(8,128)(2,1)S(1)} %get-tuple-element.90.refs_4_.refs_0_, bf16[128,1024]{1,0:T(8,128)(2,1)S(1)} %collective-permute-done.27.refs_1_, ...), custom_call_target="tpu_custom_call", output_to_operand_aliasing={{}: (1, {})} | custom-call | bytes 1000 | tf_op jit(solution)/shard_map/pallas_call | solution.py:359
  (49 shorter events, 6.8 us)
Async XLA Ops:
  0.6 32.2 %collective-permute-start.4 = (bf16[128,8,1024]{2,1,0:T(8,128)(2,1)}, bf16[128,8,1024]{2,1,0:T(8,128)(2,1)S(1)}, u32[]{:S(2)}, u32[]{:S(2)}) collective-permute-start(bf16[128,8,1024]{2,1,0:T(8,128)(2,1)} %refs_2_.1), channel_id=1, source_target_pairs={{3,7},{7,11},{11,15},{19,23},{23,27},{27,31}} | collective-permute-start | bytes 6291464 | tf_op jit(solution)/shard_map/ppermute | solution.py:27
  4.0 13.4 %collective-permute-start = (bf16[144,1024]{1,0:T(8,128)(2,1)S(1)}, bf16[144,1024]{1,0:T(8,128)(2,1)S(1)}, u32[]{:S(2)}, u32[]{:S(2)}) collective-permute-start(bf16[144,1024]{1,0:T(8,128)(2,1)S(1)} %get-tuple-element.48.refs_2_), channel_id=1, source_target_pairs={{0,1},{1,0},{2,3},{3,2},{4,5},{5,4},{6,7},{7,6},{8,9},{9,8},{10,11... | collective-permute-start | bytes 884744 | tf_op jit(solution)/shard_map/ppermute | solution.py:32
  4.0 13.4 %collective-permute-start.1 = (bf16[128,1024]{1,0:T(8,128)(2,1)}, bf16[128,1024]{1,0:T(8,128)(2,1)}, u32[]{:S(2)}, u32[]{:S(2)}) collective-permute-start(bf16[128,1024]{1,0:T(8,128)(2,1)} %get-tuple-element.50), channel_id=1, source_target_pairs={{0,2},{1,3},{2,0},{3,1},{4,6},{5,7},{6,4},{7,5},{8,10},{9,11},{10,... | collective-permute-start | bytes 786440 | tf_op jit(solution)/shard_map/ppermute | solution.py:32
  8.6 5.3 %copy-start.6 = (s32[16,6]{0,1:T(8,128)S(1)}, s32[16,6]{0,1:T(8,128)}, u32[]{:S(2)}) copy-start(s32[16,6]{0,1:T(8,128)} %param.8) | copy-start | bytes 1156
  8.6 6.1 %copy-start = (bf16[8,128,128]{2,1,0:T(8,128)(2,1)S(1)}, bf16[8,128,128]{2,1,0:T(8,128)(2,1)}, u32[]{:S(2)}) copy-start(bf16[8,128,128]{2,1,0:T(8,128)(2,1)} %refs_0_.1) | copy-start | bytes 786436
  8.6 13.7 %collective-permute-start.2 = (bf16[144,1024]{1,0:T(8,128)(2,1)S(1)}, bf16[144,1024]{1,0:T(8,128)(2,1)S(1)}, u32[]{:S(2)}, u32[]{:S(2)}) collective-permute-start(bf16[144,1024]{1,0:T(8,128)(2,1)S(1)} %get-tuple-element.51), channel_id=1, source_target_pairs={{0,3},{1,2},{2,1},{3,0},{4,7},{5,6},{6,5},{7,4},{8,11},{9,10},{10,... | collective-permute-start | bytes 884744 | tf_op jit(solution)/shard_map/ppermute | solution.py:32
  11.5 0.7 copy-start.3
  12.2 20.6 %collective-permute-start.5 = (bf16[256,1024]{1,0:T(8,128)(2,1)}, bf16[256,1024]{1,0:T(8,128)(2,1)}, u32[]{:S(2)}, u32[]{:S(2)}) collective-permute-start(bf16[256,1024]{1,0:T(8,128)(2,1)} %get-tuple-element.56), channel_id=1, source_target_pairs={{0,2},{1,3},{2,0},{3,1},{4,6},{5,7},{6,4},{7,5},{8,10},{9,11},{10,... | collective-permute-start | bytes 1572872 | tf_op jit(solution)/shard_map/ppermute | solution.py:32
  14.8 1.0 copy-start.4
  15.7 6.6 %copy-start.2 = (bf16[128,1024]{1,0:T(8,128)(2,1)S(1)}, bf16[128,1024]{1,0:T(8,128)(2,1)}, u32[]{:S(2)}) copy-start(bf16[128,1024]{1,0:T(8,128)(2,1)} %get-tuple-element.49.refs_0_) | copy-start | bytes 786436
  22.3 1.2 copy-start.5
  23.5 18.1 %copy-start.1 = (bf16[128,1024]{1,0:T(8,128)(2,1)S(1)}, bf16[128,1024]{1,0:T(8,128)(2,1)}, u32[]{:S(2)}) copy-start(bf16[128,1024]{1,0:T(8,128)(2,1)} %get-tuple-element.62.refs_0_) | copy-start | bytes 786436
  23.5 9.3 %collective-permute-start.6 = (bf16[128,1024]{1,0:T(8,128)(2,1)S(1)}, bf16[128,1024]{1,0:T(8,128)(2,1)S(1)}, u32[]{:S(2)}, u32[]{:S(2)}) collective-permute-start(bf16[128,1024]{1,0:T(8,128)(2,1)S(1)} %copy-done.5), channel_id=1, source_target_pairs={{0,1},{1,0},{2,3},{3,2},{4,5},{5,4},{6,7},{7,6},{8,9},{9,8},{10,11... | collective-permute-start | bytes 786440 | tf_op jit(solution)/shard_map/ppermute | solution.py:32
  23.9 28.2 %collective-permute-start.3 = (bf16[528,1024]{1,0:T(8,128)(2,1)S(1)}, bf16[528,1024]{1,0:T(8,128)(2,1)S(1)}, u32[]{:S(2)}, u32[]{:S(2)}) collective-permute-start(bf16[528,1024]{1,0:T(8,128)(2,1)S(1)} %get-tuple-element.54.own_ref), channel_id=1, source_target_pairs={{4,0},{5,1},{6,2},{7,3},{8,4},{9,5},{10,6},{11,7},{12,8},{13,9},{1... | collective-permute-start | bytes 3244040 | tf_op jit(solution)/shard_map/ppermute | solution.py:27
  34.6 12.5 %collective-permute-start.9 = (bf16[256,1024]{1,0:T(8,128)(2,1)S(1)}, bf16[256,1024]{1,0:T(8,128)(2,1)S(1)}, u32[]{:S(2)}, u32[]{:S(2)}) collective-permute-start(bf16[256,1024]{1,0:T(8,128)(2,1)S(1)} %get-tuple-element.61), channel_id=1, source_target_pairs={{0,2},{1,3},{2,0},{3,1},{4,6},{5,7},{6,4},{7,5},{8,10},{9,11},{10,... | collective-permute-start | bytes 1572872 | tf_op jit(solution)/shard_map/ppermute | solution.py:32
  35.8 2.7 %collective-permute-start.7 = (bf16[128,1024]{1,0:T(8,128)(2,1)S(1)}, bf16[128,1024]{1,0:T(8,128)(2,1)S(1)}, u32[]{:S(2)}, u32[]{:S(2)}) collective-permute-start(bf16[128,1024]{1,0:T(8,128)(2,1)S(1)} %get-tuple-element.58), channel_id=1, source_target_pairs={{0,1},{1,0},{2,3},{3,2},{4,5},{5,4},{6,7},{7,6},{8,9},{9,8},{10,11... | collective-permute-start | bytes 786440 | tf_op jit(solution)/shard_map/ppermute | solution.py:32
  37.4 4.2 %collective-permute-start.10 = (bf16[128,1024]{1,0:T(8,128)(2,1)S(1)}, bf16[128,1024]{1,0:T(8,128)(2,1)S(1)}, u32[]{:S(2)}, u32[]{:S(2)}) collective-permute-start(bf16[128,1024]{1,0:T(8,128)(2,1)S(1)} %get-tuple-element.63), channel_id=1, source_target_pairs={{0,1},{1,0},{2,3},{3,2},{4,5},{5,4},{6,7},{7,6},{8,9},{9,8},{10,11... | collective-permute-start | bytes 786440 | tf_op jit(solution)/shard_map/ppermute | solution.py:32
  38.6 15.9 %collective-permute-start.8 = (bf16[144,1024]{1,0:T(8,128)(2,1)S(1)}, bf16[144,1024]{1,0:T(8,128)(2,1)S(1)}, u32[]{:S(2)}, u32[]{:S(2)}) collective-permute-start(bf16[144,1024]{1,0:T(8,128)(2,1)S(1)} %get-tuple-element.59), channel_id=1, source_target_pairs={{0,4},{1,5},{2,6},{3,7},{4,8},{5,9},{6,10},{7,11},{8,12},{9,13},{1... | collective-permute-start | bytes 884744 | tf_op jit(solution)/shard_map/ppermute | solution.py:27
  42.8 10.5 %collective-permute-start.12 = (bf16[128,1024]{1,0:T(8,128)(2,1)S(1)}, bf16[128,1024]{1,0:T(8,128)(2,1)S(1)}, u32[]{:S(2)}, u32[]{:S(2)}) collective-permute-start(bf16[128,1024]{1,0:T(8,128)(2,1)S(1)} %get-tuple-element.66), channel_id=1, source_target_pairs={{0,4},{1,5},{2,6},{3,7},{4,8},{5,9},{6,10},{7,11},{8,12},{9,13},{1... | collective-permute-start | bytes 786440 | tf_op jit(solution)/shard_map/ppermute | solution.py:27
  47.2 7.3 %collective-permute-start.11 = (bf16[128,1024]{1,0:T(8,128)(2,1)S(1)}, bf16[128,1024]{1,0:T(8,128)(2,1)S(1)}, u32[]{:S(2)}, u32[]{:S(2)}) collective-permute-start(bf16[128,1024]{1,0:T(8,128)(2,1)S(1)} %slice.6), channel_id=1, source_target_pairs={{0,1},{1,0},{2,3},{3,2},{4,5},{5,4},{6,7},{7,6},{8,9},{9,8},{10,11... | collective-permute-start | bytes 786440 | tf_op jit(solution)/shard_map/ppermute | solution.py:32
  50.8 15.8 %collective-permute-start.17 = (bf16[256,1024]{1,0:T(8,128)(2,1)S(1)}, bf16[256,1024]{1,0:T(8,128)(2,1)S(1)}, u32[]{:S(2)}, u32[]{:S(2)}) collective-permute-start(bf16[256,1024]{1,0:T(8,128)(2,1)S(1)} %get-tuple-element.73), channel_id=1, source_target_pairs={{0,2},{1,3},{2,0},{3,1},{4,6},{5,7},{6,4},{7,5},{8,10},{9,11},{10,... | collective-permute-start | bytes 1572872 | tf_op jit(solution)/shard_map/ppermute | solution.py:32
  52.1 33.3 %collective-permute-start.15 = (bf16[512,1024]{1,0:T(8,128)(2,1)S(1)}, bf16[512,1024]{1,0:T(8,128)(2,1)S(1)}, u32[]{:S(2)}, u32[]{:S(2)}) collective-permute-start(bf16[512,1024]{1,0:T(8,128)(2,1)S(1)} %get-tuple-element.64.refs_0_.own_ref), channel_id=1, source_target_pairs={{4,0},{5,1},{6,2},{7,3},{8,4},{9,5},{10,6},{11,7},{12,8},{13,9},{1... | collective-permute-start | bytes 3145736 | tf_op jit(solution)/shard_map/ppermute | solution.py:27
  53.4 17.5 %collective-permute-start.16 = (bf16[128,1024]{1,0:T(8,128)(2,1)S(1)}, bf16[128,1024]{1,0:T(8,128)(2,1)S(1)}, u32[]{:S(2)}, u32[]{:S(2)}) collective-permute-start(bf16[128,1024]{1,0:T(8,128)(2,1)S(1)} %get-tuple-element.72), channel_id=1, source_target_pairs={{0,1},{1,0},{2,3},{3,2},{4,5},{5,4},{6,7},{7,6},{8,9},{9,8},{10,11... | collective-permute-start | bytes 786440 | tf_op jit(solution)/shard_map/ppermute | solution.py:32
  66.6 5.8 %collective-permute-start.18 = (bf16[128,1024]{1,0:T(8,128)(2,1)S(1)}, bf16[128,1024]{1,0:T(8,128)(2,1)S(1)}, u32[]{:S(2)}, u32[]{:S(2)}) collective-permute-start(bf16[128,1024]{1,0:T(8,128)(2,1)S(1)} %slice.7), channel_id=1, source_target_pairs={{0,1},{1,0},{2,3},{3,2},{4,5},{5,4},{6,7},{7,6},{8,9},{9,8},{10,11... | collective-permute-start | bytes 786440 | tf_op jit(solution)/shard_map/ppermute | solution.py:32
  66.7 30.5 %collective-permute-start.13 = (bf16[512,1024]{1,0:T(8,128)(2,1)S(1)}, bf16[512,1024]{1,0:T(8,128)(2,1)S(1)}, u32[]{:S(2)}, u32[]{:S(2)}) collective-permute-start(bf16[512,1024]{1,0:T(8,128)(2,1)S(1)} %get-tuple-element.68.refs_0_.own_ref), channel_id=1, source_target_pairs={{0,4},{1,5},{2,6},{3,7},{4,8},{5,9},{6,10},{7,11},{8,12},{9,13},{1... | collective-permute-start | bytes 3145736 | tf_op jit(solution)/shard_map/ppermute | solution.py:27
  70.9 2.5 %collective-permute-start.19 = (bf16[128,1024]{1,0:T(8,128)(2,1)S(1)}, bf16[128,1024]{1,0:T(8,128)(2,1)S(1)}, u32[]{:S(2)}, u32[]{:S(2)}) collective-permute-start(bf16[128,1024]{1,0:T(8,128)(2,1)S(1)} %get-tuple-element.77), channel_id=1, source_target_pairs={{0,1},{1,0},{2,3},{3,2},{4,5},{5,4},{6,7},{7,6},{8,9},{9,8},{10,11... | collective-permute-start | bytes 786440 | tf_op jit(solution)/shard_map/ppermute | solution.py:32
  71.7 7.9 %collective-permute-start.20 = (bf16[128,1024]{1,0:T(8,128)(2,1)S(1)}, bf16[128,1024]{1,0:T(8,128)(2,1)S(1)}, u32[]{:S(2)}, u32[]{:S(2)}) collective-permute-start(bf16[128,1024]{1,0:T(8,128)(2,1)S(1)} %get-tuple-element.79), channel_id=1, source_target_pairs={{0,2},{1,3},{2,0},{3,1},{4,6},{5,7},{6,4},{7,5},{8,10},{9,11},{10,... | collective-permute-start | bytes 786440 | tf_op jit(solution)/shard_map/ppermute | solution.py:32
  72.4 13.0 %collective-permute-start.21 = (bf16[128,1024]{1,0:T(8,128)(2,1)S(1)}, bf16[128,1024]{1,0:T(8,128)(2,1)S(1)}, u32[]{:S(2)}, u32[]{:S(2)}) collective-permute-start(bf16[128,1024]{1,0:T(8,128)(2,1)S(1)} %get-tuple-element.81), channel_id=1, source_target_pairs={{0,3},{1,2},{2,1},{3,0},{4,7},{5,6},{6,5},{7,4},{8,11},{9,10},{10,... | collective-permute-start | bytes 786440 | tf_op jit(solution)/shard_map/ppermute | solution.py:32
  73.4 19.5 %collective-permute-start.14 = (bf16[128,1024]{1,0:T(8,128)(2,1)S(1)}, bf16[128,1024]{1,0:T(8,128)(2,1)S(1)}, u32[]{:S(2)}, u32[]{:S(2)}) collective-permute-start(bf16[128,1024]{1,0:T(8,128)(2,1)S(1)} %get-tuple-element.71), channel_id=1, source_target_pairs={{4,0},{5,1},{6,2},{7,3},{8,4},{9,5},{10,6},{11,7},{12,8},{13,9},{1... | collective-permute-start | bytes 786440 | tf_op jit(solution)/shard_map/ppermute | solution.py:27
  87.5 9.7 %collective-permute-start.22 = (bf16[128,1024]{1,0:T(8,128)(2,1)S(1)}, bf16[128,1024]{1,0:T(8,128)(2,1)S(1)}, u32[]{:S(2)}, u32[]{:S(2)}) collective-permute-start(bf16[128,1024]{1,0:T(8,128)(2,1)S(1)} %get-tuple-element.83), channel_id=1, source_target_pairs={{4,0},{5,1},{6,2},{7,3},{8,4},{9,5},{10,6},{11,7},{12,8},{13,9},{1... | collective-permute-start | bytes 786440 | tf_op jit(solution)/shard_map/ppermute | solution.py:27
  88.8 27.0 %collective-permute-start.26 = (bf16[512,1024]{1,0:T(8,128)(2,1)S(1)}, bf16[512,1024]{1,0:T(8,128)(2,1)S(1)}, u32[]{:S(2)}, u32[]{:S(2)}) collective-permute-start(bf16[512,1024]{1,0:T(8,128)(2,1)S(1)} %get-tuple-element.82.refs_0_.own_ref), channel_id=1, source_target_pairs={{0,4},{1,5},{2,6},{3,7},{4,8},{5,9},{6,10},{7,11},{8,12},{9,13},{1... | collective-permute-start | bytes 3145736 | tf_op jit(solution)/shard_map/ppermute | solution.py:27
  100.2 30.0 %collective-permute-start.30 = (bf16[128,8,512]{2,1,0:T(8,128)(2,1)S(1)}, bf16[128,8,512]{2,1,0:T(8,128)(2,1)S(1)}, u32[]{:S(2)}, u32[]{:S(2)}) collective-permute-start(bf16[128,8,512]{2,1,0:T(8,128)(2,1)S(1)} %shard_map.80.refs_1_.own_ref), channel_id=1, source_target_pairs={{7,3},{11,7},{15,11},{23,19},{27,23},{31,27}} | collective-permute-start | bytes 3145736 | tf_op jit(solution)/shard_map/ppermute | solution.py:27
  100.9 17.7 %collective-permute-start.23 = (bf16[256,1024]{1,0:T(8,128)(2,1)S(1)}, bf16[256,1024]{1,0:T(8,128)(2,1)S(1)}, u32[]{:S(2)}, u32[]{:S(2)}) collective-permute-start(bf16[256,1024]{1,0:T(8,128)(2,1)S(1)} %get-tuple-element.86), channel_id=1, source_target_pairs={{0,1},{1,0},{2,3},{3,2},{4,5},{5,4},{6,7},{7,6},{8,9},{9,8},{10,11... | collective-permute-start | bytes 1572872 | tf_op jit(solution)/shard_map/ppermute | solution.py:32
  102.0 17.4 %collective-permute-start.24 = (bf16[256,1024]{1,0:T(8,128)(2,1)S(1)}, bf16[256,1024]{1,0:T(8,128)(2,1)S(1)}, u32[]{:S(2)}, u32[]{:S(2)}) collective-permute-start(bf16[256,1024]{1,0:T(8,128)(2,1)S(1)} %get-tuple-element.87), channel_id=1, source_target_pairs={{0,2},{1,3},{2,0},{3,1},{4,6},{5,7},{6,4},{7,5},{8,10},{9,11},{10,... | collective-permute-start | bytes 1572872 | tf_op jit(solution)/shard_map/ppermute | solution.py:32
  102.6 24.8 %collective-permute-start.25 = (bf16[256,1024]{1,0:T(8,128)(2,1)S(1)}, bf16[256,1024]{1,0:T(8,128)(2,1)S(1)}, u32[]{:S(2)}, u32[]{:S(2)}) collective-permute-start(bf16[256,1024]{1,0:T(8,128)(2,1)S(1)} %get-tuple-element.88), channel_id=1, source_target_pairs={{0,3},{1,2},{2,1},{3,0},{4,7},{5,6},{6,5},{7,4},{8,11},{9,10},{10,... | collective-permute-start | bytes 1572872 | tf_op jit(solution)/shard_map/ppermute | solution.py:32
  117.8 15.1 %collective-permute-start.27 = (bf16[128,1024]{1,0:T(8,128)(2,1)S(1)}, bf16[128,1024]{1,0:T(8,128)(2,1)S(1)}, u32[]{:S(2)}, u32[]{:S(2)}) collective-permute-start(bf16[128,1024]{1,0:T(8,128)(2,1)S(1)} %get-tuple-element.91), channel_id=1, source_target_pairs={{0,1},{1,0},{2,3},{3,2},{4,5},{5,4},{6,7},{7,6},{8,9},{9,8},{10,11... | collective-permute-start | bytes 786440 | tf_op jit(solution)/shard_map/ppermute | solution.py:32
  118.7 14.2 %collective-permute-start.28 = (bf16[128,1024]{1,0:T(8,128)(2,1)S(1)}, bf16[128,1024]{1,0:T(8,128)(2,1)S(1)}, u32[]{:S(2)}, u32[]{:S(2)}) collective-permute-start(bf16[128,1024]{1,0:T(8,128)(2,1)S(1)} %get-tuple-element.92), channel_id=1, source_target_pairs={{0,2},{1,3},{2,0},{3,1},{4,6},{5,7},{6,4},{7,5},{8,10},{9,11},{10,... | collective-permute-start | bytes 786440 | tf_op jit(solution)/shard_map/ppermute | solution.py:32
  119.4 18.7 %collective-permute-start.29 = (bf16[128,1024]{1,0:T(8,128)(2,1)S(1)}, bf16[128,1024]{1,0:T(8,128)(2,1)S(1)}, u32[]{:S(2)}, u32[]{:S(2)}) collective-permute-start(bf16[128,1024]{1,0:T(8,128)(2,1)S(1)} %get-tuple-element.93), channel_id=1, source_target_pairs={{0,3},{1,2},{2,1},{3,0},{4,7},{5,6},{6,5},{7,4},{8,11},{9,10},{10,... | collective-permute-start | bytes 786440 | tf_op jit(solution)/shard_map/ppermute | solution.py:32

commit v14 on v12

--- a/solution.py
+++ b/solution.py
@@ -81,9 +81,12 @@
     return chunk * count, count
 
 
-def cast_kernel(groups, ends, here_ref, *refs):
+def cast_kernel(groups, ends, halves, here_ref, *refs):
     parts = TILE // LANES
-    vol_refs, end_refs, out_refs = refs[:parts], refs[parts : parts + ends], refs[-len(groups) :]
+    vol_refs, end_refs = refs[:parts], refs[parts : parts + ends]
+    for half_ref, sent_ref in zip(refs[parts + ends : parts + ends + halves], refs[len(refs) - halves :]):
+        sent_ref[...] = half_ref[...]
+    out_refs = refs[len(refs) - halves - len(groups) : len(refs) - halves]
     rows = ROWS * G
     depth = vol_refs[0].shape[0] // rows
     place = lax.rem(here_ref[0], G)
@@ -100,24 +103,28 @@
                 out_ref[depth:, :] = both
 
 
-def cast_rows(here, volume, chunk, groups, ends, *tokens):
+def cast_rows(here, volume, chunk, groups, ends, sinogram, *tokens):
     depth, rows, cols = volume.shape
     flat = far(volume.reshape(depth * rows, cols))
     first, count = chunk_tiles(chunk, cols)
     parts, width = TILE // LANES, ROWS * TILE
     shapes = [(len(group) * depth + (2 * rows if ends and group[0] % 2 else 0), cols) for group in groups]
     edges = [pl.BlockSpec((rows, width), lambda i, z=z: (z, i)) for z in (0, depth - 1)] if ends else []
-    return call(
-        functools.partial(cast_kernel, groups, len(edges)),
+    halves = 0 if sinogram is None else CHUNKS
+    block = (depth, rows, TILE)
+    return call(
+        functools.partial(cast_kernel, groups, len(edges), halves),
         2,
         grid=(count,),
         in_specs=[SMEM]
         + [pl.BlockSpec((depth * rows, LANES), lambda i, j=j: (0, (first + i) * parts + j)) for j in range(parts)]
         + edges
+        + [pl.BlockSpec(block, lambda i, c=c: (0, 0, c * count + i)) for c in range(halves)]
         + [ANY] * len(tokens),
-        out_specs=[across(shape, width) for shape in shapes],
-        results=[(pltpu.HBM if group[0] == 0 else value)(shape, BF16) for group, shape in zip(groups, shapes)],
-    )(here, *[flat] * (parts + len(edges)), *tokens)
+        out_specs=[across(shape, width) for shape in shapes] + [pl.BlockSpec(block, lambda i: (0, 0, i))] * halves,
+        results=[(pltpu.HBM if group[0] == 0 else value)(shape, BF16) for group, shape in zip(groups, shapes)]
+        + [value((depth, rows, cols // CHUNKS), BF16)] * halves,
+    )(here, *[flat] * (parts + len(edges)), *[sinogram if halves == 0 else far(sinogram)] * halves, *tokens)
 
 
 def last_block(here_ref, blocks):
@@ -190,7 +197,8 @@
         functools.partial(split_kernel, groups, len(passing)),
         2,
         grid=(count,),
-        in_specs=[SMEM, block, block] + piece_specs(passing, depth, ROWS * TILE) + [ANY] * len(tokens),
+        in_specs=[SMEM, block, pl.BlockSpec((depth, rows, TILE), lambda i: (0, 0, i))]
+        + piece_specs(passing, depth, ROWS * TILE) + [ANY] * len(tokens),
         out_specs=[across(shape, ROWS * TILE) for shape in shapes],
         results=[value(shape, BF16) for shape in shapes],
         scratch_shapes=[wide_tile(depth * rows)],
@@ -559,22 +567,23 @@
     def beyond(over, *others):
         return swapped(tied(over, *others)[depth:], 1)
 
-    vols0 = cast_rows(here, volume, 0, single, True)
-    got = moved(tied(sinogram, vols0[0]), G, only=G - 1)
+    vols0 = cast_rows(here, volume, 0, single, True, None)
     got_vols0 = direct(vols0)
-    v0, v1, v23 = cast_rows(here, volume, 1, paired, False, vols0[1])
+    v0, v1, v23, sent0, sent1 = cast_rows(here, volume, 1, paired, False, sinogram, vols0[1])
+    got0 = moved(sent0, G, only=G - 1)
     over = swapped(v23, 2)
     band_p, band_b = bands(here, coverage, offsets, weights, v1)
     own0, edge0 = pack(here, [(array, 0) for array in got_vols0], 2 * rows, band_p)
     high0, near = moved(own0, -G), swapped(tied(v1, own0), 1)
-    s0, s1, s23, over_beyond = split_rows(here, sinogram, got, 0, paired, [(over, 1)], near)
+    got1 = moved(tied(sent1, own0), G, only=G - 1)
+    s0, s1, s23, over_beyond = split_rows(here, sinogram, got0, 0, paired, [(over, 1)], near)
     s_near, s_over = swapped(s1, 1), swapped(s23, 2)
     low0 = moved(tied(edge0, s_near), G)
     own1, edge1 = pack(here, [(v0, 0), (near, 0), (over, 0), (swapped(over_beyond, 1), 0)], 0)
     low1, high1 = moved(edge1, G), moved(own1, -G)
     sinos0 = [(s0, 0), (s_near, 0), (s_over, 0), (beyond(s_over, own1), 0)]
 
-    s0, s1, s23 = split_rows(here, sinogram, got, 1, paired, [], own1)
+    s0, s1, s23 = split_rows(here, sinogram, got1, 1, paired, [], own1)
 
     resid0, down0, r1, r23 = project(here, band_p, own0, high0, low0, sinos0, paired[1:], low1, s0)
     from_low0, from_high0 = moved(resid0, G), moved(down0, -G)

time: 135 us -> 131 us (0.970)
  waiting for transfers between devices: 39.8 us -> 34.8 us
    ppermute x21, waiting for transfers between devices: 30 us -> 24.7 us  [swapped(): return lax.ppermute(value, 'slab', [(i, i ^ bits) for i in range(count)])]
    ppermute x10 -> x11, starting transfers between devices: 21.9 us -> 22.8 us  [moved(): return lax.ppermute(value, 'slab', pairs)]
    ppermute x10 -> x11, waiting for transfers between devices: 9.85 us -> 10.2 us  [moved(): return lax.ppermute(value, 'slab', pairs)]
  transfers between devices with their start and end apart: 31 -> 32, of which waited for: 12 -> 11; matrix products, arithmetic and copies ran while one was open for 1% -> 1% of each run, Pallas kernels for 27% -> 28%
where the time goes in v14:
time: 131 us; the launch traced here: 130 us
  starting transfers between devices  49.8 us (38%)
  Pallas kernels  42.3 us (32%)
  waiting for transfers between devices  34.8 us (27%)
  local copies, waits for them, and re-layouts  2.57 us (2%)
    ppermute x21, starting transfers between devices, swapped(): return lax.ppermute(value, 'slab', [(i, i ^ bits) for i in range(count)])  27 us
    ppermute x21, waiting for transfers between devices, swapped(): return lax.ppermute(value, 'slab', [(i, i ^ bits) for i in range(count)])  24.7 us
    ppermute x11, starting transfers between devices, moved(): return lax.ppermute(value, 'slab', pairs)  22.8 us
    ppermute x11, waiting for transfers between devices, moved(): return lax.ppermute(value, 'slab', pairs)  10.2 us
    pallas_call x1, Pallas kernels, half_tv(): call(tv_kernel, 0, grid=(depth // deep,), in_specs=[SMEM] + edges + [afte...  9.99 us
    pallas_call x2, Pallas kernels, cast_rows(): call(functools.partial(cast_kernel, groups, len(edges), halves), 2, grid=...  5.97 us
    pallas_call x2, Pallas kernels, finish(): call(finish_kernel, 0, grid=(count,), in_specs=[SMEM, part] + piece_specs...  5.85 us
    pallas_call x2, Pallas kernels, project(): call(functools.partial(project_kernel, groups), 3, grid=(cols // tile,),...  4.22 us
  transfers between devices with their start and end apart: 32, of which 11 were waited for; matrix products, arithmetic and copies ran while one was open for 1% of the time, Pallas kernels for 28%

profile of v14, /device:TPU:1, one launch (start us, length us, event | category | flops | bytes accessed | tf_op | source)
XLA Modules:
  0.0 130.4 jit_solution(3176315010230616734)
XLA Ops:
  0.6 2.5 %shard_map.68 = (bf16[128,1024]{1,0:T(8,128)(2,1)}, bf16[144,1024]{1,0:T(8,128)(2,1)S(1)}, bf16[128,1024]{1,0:T(8,128)(2,1)}, bf16[144,1024]{1,0:T(8,128)(2,1)S(1)}) custom-call(s32[1]{0:T(128)} %bitcast.here_ref, f32[1024,1024]{1,0:T(8,128)} %bitcast.2, f32[1024,1024]{1,0:T(8,128)} %bitcast.3, f32[1024,1024]{1,0:T(8,128)} %bitcast.4, f32[1024,1024]{1,0:T(8,128)} %bitcast.5), custom_call_target="tpu_custom_call" | custom-call | flops 2300000000 | bytes 1000 | tf_op jit(solution)/shard_map/pallas_call | solution.py:115
  3.2 2.7 %collective-permute-start.1 = (bf16[128,1024]{1,0:T(8,128)(2,1)}, bf16[128,1024]{1,0:T(8,128)(2,1)}, u32[]{:S(2)}, u32[]{:S(2)}) collective-permute-start(bf16[128,1024]{1,0:T(8,128)(2,1)} %get-tuple-element.52), channel_id=1, source_target_pairs={{0,2},{1,3},{2,0},{3,1},{4,6},{5,7},{6,4},{7,5},{8,10},{9,11},{10,... | collective-permute-start | bytes 786440 | tf_op jit(solution)/shard_map/ppermute | solution.py:32
  6.0 3.4 %shard_map.69 = (bf16[128,1024]{1,0:T(8,128)(2,1)}, bf16[128,1024]{1,0:T(8,128)(2,1)S(1)}, bf16[256,1024]{1,0:T(8,128)(2,1)}, bf16[128,8,512]{2,1,0:T(8,128)(2,1)}, bf16[128,8,512]{2,1,0:T(8,128)(2,1)S(1)}) custom-call(s32[1]{0:T(128)} %bitcast.here_ref, f32[1024,1024]{1,0:T(8,128)} %bitcast.6, f32[1024,1024]{1,0:T(8,128)} %bitcast.7, ...), custom_call_target="tpu_custom_call" | custom-call | flops 2300000000 | bytes 1000 | tf_op jit(solution)/shard_map/pallas_call | solution.py:115
  10.8 4.2 %collective-permute-start.5 = (bf16[256,1024]{1,0:T(8,128)(2,1)}, bf16[256,1024]{1,0:T(8,128)(2,1)}, u32[]{:S(2)}, u32[]{:S(2)}) collective-permute-start(bf16[256,1024]{1,0:T(8,128)(2,1)} %get-tuple-element.59), channel_id=1, source_target_pairs={{0,2},{1,3},{2,0},{3,1},{4,6},{5,7},{6,4},{7,5},{8,10},{9,11},{10,... | collective-permute-start | bytes 1572872 | tf_op jit(solution)/shard_map/ppermute | solution.py:32
  15.1 0.8 copy.13.offset_ref
  15.9 0.9 copy-done.3
  16.8 1.6 %shard_map.70 = (bf16[512,1152]{1,0:T(8,128)(2,1)S(1)}, bf16[512,1152]{1,0:T(8,128)(2,1)S(1)}) custom-call(s32[1]{0:T(128)} %bitcast.here_ref, s32[16,6]{1,0:T(8,128)S(1)} %copy.12.cover_ref, s32[16,6]{1,0:T(8,128)S(1)} %copy.13.offset_ref, bf16[8,128,128]{2,1,0:T(8,128)(2,1)S(1)} %copy-done, bf16[128,1024]{1,0:T(8,128)(2,1)S(1)} %copy-done.3), custom_call_target="tpu_custom_call" | custom-call | flops 10350000128 | bytes 1000 | tf_op jit(solution)/shard_map/pallas_call | solution.py:415
  18.5 0.8 collective-permute-done.2.refs_3_.far_ref
  19.3 1.2 shard_map.71
  20.7 0.8 collective-permute-start.13
  21.6 1.3 collective-permute-start.3
  22.9 7.5 %collective-permute-done.5.refs_0_.refs_2_ = bf16[256,1024]{1,0:T(8,128)(2,1)} collective-permute-done((bf16[256,1024]{1,0:T(8,128)(2,1)}, bf16[256,1024]{1,0:T(8,128)(2,1)}, u32[]{:S(2)}, u32[]{:S(2)}) %collective-permute-start.5) | collective-permute-done | bytes 524320 | tf_op jit(solution)/shard_map/ppermute | solution.py:32
  30.4 1.8 %shard_map.72 = (bf16[128,1024]{1,0:T(8,128)(2,1)S(1)}, bf16[128,1024]{1,0:T(8,128)(2,1)S(1)}, bf16[256,1024]{1,0:T(8,128)(2,1)S(1)}, bf16[128,1024]{1,0:T(8,128)(2,1)S(1)}) custom-call(s32[1]{0:T(128)} %bitcast.here_ref, bf16[128,8,1024]{2,1,0:T(8,128)(2,1)} %refs_2_.3, bf16[128,8,512]{2,1,0:T(8,128)(2,1)S(1)} %collective-permute-done.4.got_ref, ...), custom_call_target="tpu_custom_call" | custom-call | flops 2300000000 | bytes 1000 | tf_op jit(solution)/shard_map/pallas_call | solution.py:196
  32.2 1.3 %collective-permute-start.9 = (bf16[256,1024]{1,0:T(8,128)(2,1)S(1)}, bf16[256,1024]{1,0:T(8,128)(2,1)S(1)}, u32[]{:S(2)}, u32[]{:S(2)}) collective-permute-start(bf16[256,1024]{1,0:T(8,128)(2,1)S(1)} %get-tuple-element.64), channel_id=1, source_target_pairs={{0,2},{1,3},{2,0},{3,1},{4,6},{5,7},{6,4},{7,5},{8,10},{9,11},{10,... | collective-permute-start | bytes 1572872 | tf_op jit(solution)/shard_map/ppermute | solution.py:32
  33.5 1.1 collective-permute-start.7
  34.7 1.2 collective-permute-done.7.refs_1_
  35.8 3.2 %collective-permute-start.8 = (bf16[144,1024]{1,0:T(8,128)(2,1)S(1)}, bf16[144,1024]{1,0:T(8,128)(2,1)S(1)}, u32[]{:S(2)}, u32[]{:S(2)}) collective-permute-start(bf16[144,1024]{1,0:T(8,128)(2,1)S(1)} %get-tuple-element.62), channel_id=1, source_target_pairs={{0,4},{1,5},{2,6},{3,7},{4,8},{5,9},{6,10},{7,11},{8,12},{9,13},{1... | collective-permute-start | bytes 884744 | tf_op jit(solution)/shard_map/ppermute | solution.py:27
  39.0 1.2 shard_map.73
  40.2 3.2 %collective-permute-start.12 = (bf16[128,1024]{1,0:T(8,128)(2,1)S(1)}, bf16[128,1024]{1,0:T(8,128)(2,1)S(1)}, u32[]{:S(2)}, u32[]{:S(2)}) collective-permute-start(bf16[128,1024]{1,0:T(8,128)(2,1)S(1)} %get-tuple-element.69), channel_id=1, source_target_pairs={{0,4},{1,5},{2,6},{3,7},{4,8},{5,9},{6,10},{7,11},{8,12},{9,13},{1... | collective-permute-start | bytes 786440 | tf_op jit(solution)/shard_map/ppermute | solution.py:27
  43.4 1.6 %collective-permute-done.9.refs_2_ = bf16[256,1024]{1,0:T(8,128)(2,1)S(1)} collective-permute-done((bf16[256,1024]{1,0:T(8,128)(2,1)S(1)}, bf16[256,1024]{1,0:T(8,128)(2,1)S(1)}, u32[]{:S(2)}, u32[]{:S(2)}) %collective-permute-start.9) | collective-permute-done | bytes 524320 | tf_op jit(solution)/shard_map/ppermute | solution.py:32
  45.1 1.6 %collective-permute-start.11 = (bf16[128,1024]{1,0:T(8,128)(2,1)S(1)}, bf16[128,1024]{1,0:T(8,128)(2,1)S(1)}, u32[]{:S(2)}, u32[]{:S(2)}) collective-permute-start(bf16[128,1024]{1,0:T(8,128)(2,1)S(1)} %slice.9), channel_id=1, source_target_pairs={{0,1},{1,0},{2,3},{3,2},{4,5},{5,4},{6,7},{7,6},{8,9},{9,8},{10,11... | collective-permute-start | bytes 786440 | tf_op jit(solution)/shard_map/ppermute | solution.py:32
  46.7 1.3 collective-permute-start.16
  48.0 1.7 %shard_map.74 = (bf16[128,1024]{1,0:T(8,128)(2,1)S(1)}, bf16[128,1024]{1,0:T(8,128)(2,1)S(1)}, bf16[256,1024]{1,0:T(8,128)(2,1)S(1)}) custom-call(s32[1]{0:T(128)} %bitcast.here_ref, bf16[128,8,1024]{2,1,0:T(8,128)(2,1)} %refs_2_.3, bf16[128,8,512]{2,1,0:T(8,128)(2,1)S(1)} %collective-permute-done.13.got_ref, ...), custom_call_target="tpu_custom_call" | custom-call | flops 2300000000 | bytes 1000 | tf_op jit(solution)/shard_map/pallas_call | solution.py:196
  50.6 0.9 collective-permute-start.18
  51.5 2.1 %shard_map.75 = (bf16[512,1024]{1,0:T(8,128)(2,1)S(1)}, bf16[128,1024]{1,0:T(8,128)(2,1)S(1)}, bf16[128,1024]{1,0:T(8,128)(2,1)S(1)}, bf16[256,1024]{1,0:T(8,128)(2,1)S(1)}) custom-call(s32[1]{0:T(128)} %bitcast.here_ref, bf16[512,1152]{1,0:T(8,128)(2,1)S(1)} %get-tuple-element.55.refs_4_.band_ref, bf16[528,1024]{1,0:T(8,128)(2,1)S(1)} %get-tuple-element.56.own_ref, ...), custom_call_target="tpu_custom_call" | custom-call | flops 3449999872 | bytes 1000 | tf_op jit(solution)/shard_map/pallas_call | solution.py:446
  54.3 4.2 %collective-permute-start.14 = (bf16[512,1024]{1,0:T(8,128)(2,1)S(1)}, bf16[512,1024]{1,0:T(8,128)(2,1)S(1)}, u32[]{:S(2)}, u32[]{:S(2)}) collective-permute-start(bf16[512,1024]{1,0:T(8,128)(2,1)S(1)} %get-tuple-element.73.refs_0_.own_ref), channel_id=1, source_target_pairs={{0,4},{1,5},{2,6},{3,7},{4,8},{5,9},{6,10},{7,11},{8,12},{9,13},{1... | collective-permute-start | bytes 3145736 | tf_op jit(solution)/shard_map/ppermute | solution.py:27
  58.5 2.1 %collective-permute-start.20 = (bf16[128,1024]{1,0:T(8,128)(2,1)S(1)}, bf16[128,1024]{1,0:T(8,128)(2,1)S(1)}, u32[]{:S(2)}, u32[]{:S(2)}) collective-permute-start(bf16[128,1024]{1,0:T(8,128)(2,1)S(1)} %get-tuple-element.82), channel_id=1, source_target_pairs={{0,1},{1,0},{2,3},{3,2},{4,5},{5,4},{6,7},{7,6},{8,9},{9,8},{10,11... | collective-permute-start | bytes 786440 | tf_op jit(solution)/shard_map/ppermute | solution.py:32
  60.6 10.0 %shard_map.76 = (f32[128,8,1024]{2,1,0:T(8,128)}, f32[8,128]{1,0:T(8,128)S(1)}) custom-call(s32[1]{0:T(128)} %bitcast.here_ref, bf16[144,1024]{1,0:T(8,128)(2,1)S(1)} %collective-permute-done.refs_1_.near_ref, bf16[528,1024]{1,0:T(8,128)(2,1)S(1)} %collective-permute-done.3.high_ref.next_level_ref, ...), custom_call_target="tpu_custom_call" | custom-call | bytes 1000 | tf_op jit(solution)/shard_map/pallas_call | solution.py:546
  70.7 1.3 collective-permute-start.15
  72.2 1.1 collective-permute-done.16.high_ref
  74.1 2.1 %shard_map.77 = (bf16[512,1024]{1,0:T(8,128)(2,1)S(1)}, bf16[128,1024]{1,0:T(8,128)(2,1)S(1)}) custom-call(s32[1]{0:T(128)} %bitcast.here_ref, bf16[512,1152]{1,0:T(8,128)(2,1)S(1)} %get-tuple-element.55.refs_4_.band_ref, bf16[512,1024]{1,0:T(8,128)(2,1)S(1)} %get-tuple-element.67.refs_0_.own_ref, bf16[512,1024]{1,0:T(8,128)(2,1)S(1)} %collective-permute-done.16.high_ref, ...), custom_call_target="tpu_custom_call" | custom-call | flops 3449999872 | bytes 1000 | tf_op jit(solution)/shard_map/pallas_call | solution.py:446
  76.2 1.3 collective-permute-start.22
  77.5 4.8 %collective-permute-start.26 = (bf16[512,1024]{1,0:T(8,128)(2,1)S(1)}, bf16[512,1024]{1,0:T(8,128)(2,1)S(1)}, u32[]{:S(2)}, u32[]{:S(2)}) collective-permute-start(bf16[512,1024]{1,0:T(8,128)(2,1)S(1)} %get-tuple-element.85.refs_0_.own_ref), channel_id=1, source_target_pairs={{0,4},{1,5},{2,6},{3,7},{4,8},{5,9},{6,10},{7,11},{8,12},{9,13},{1... | collective-permute-start | bytes 3145736 | tf_op jit(solution)/shard_map/ppermute | solution.py:27
  82.3 2.5 %collective-permute-start.27 = (bf16[128,1024]{1,0:T(8,128)(2,1)S(1)}, bf16[128,1024]{1,0:T(8,128)(2,1)S(1)}, u32[]{:S(2)}, u32[]{:S(2)}) collective-permute-start(bf16[128,1024]{1,0:T(8,128)(2,1)S(1)} %slice.11), channel_id=1, source_target_pairs={{0,1},{1,0},{2,3},{3,2},{4,5},{5,4},{6,7},{7,6},{8,9},{9,8},{10,11... | collective-permute-start | bytes 786440 | tf_op jit(solution)/shard_map/ppermute | solution.py:32
  84.8 2.1 %shard_map.78 = (bf16[256,1024]{1,0:T(8,128)(2,1)S(1)}, bf16[256,1024]{1,0:T(8,128)(2,1)S(1)}, bf16[256,1024]{1,0:T(8,128)(2,1)S(1)}, bf16[256,1024]{1,0:T(8,128)(2,1)S(1)}) custom-call(s32[1]{0:T(128)} %bitcast.here_ref, bf16[512,1152]{1,0:T(8,128)(2,1)S(1)} %get-tuple-element.75.band_ref, bf16[512,1024]{1,0:T(8,128)(2,1)S(1)} %get-tuple-element.73.refs_0_.own_ref, ...), custom_call_target="tpu_custom_call" | custom-call | bytes 1000 | tf_op jit(solution)/shard_map/pallas_call | solution.py:478
  87.0 0.9 shard_map.80.refs_1_.own_ref
  88.5 2.8 %collective-permute-start.23 = (bf16[256,1024]{1,0:T(8,128)(2,1)S(1)}, bf16[256,1024]{1,0:T(8,128)(2,1)S(1)}, u32[]{:S(2)}, u32[]{:S(2)}) collective-permute-start(bf16[256,1024]{1,0:T(8,128)(2,1)S(1)} %get-tuple-element.89), channel_id=1, source_target_pairs={{0,1},{1,0},{2,3},{3,2},{4,5},{5,4},{6,7},{7,6},{8,9},{9,8},{10,11... | collective-permute-start | bytes 1572872 | tf_op jit(solution)/shard_map/ppermute | solution.py:32
  91.3 1.1 collective-permute-start.24
  93.1 1.2 shard_map.79
  94.2 8.3 %collective-permute-done.26.low_ref = bf16[512,1024]{1,0:T(8,128)(2,1)S(1)} collective-permute-done((bf16[512,1024]{1,0:T(8,128)(2,1)S(1)}, bf16[512,1024]{1,0:T(8,128)(2,1)S(1)}, u32[]{:S(2)}, u32[]{:S(2)}) %collective-permute-start.26) | collective-permute-done | bytes 1048608 | tf_op jit(solution)/shard_map/ppermute | solution.py:27
  102.5 1.9 %shard_map.81 = (bf16[128,1024]{1,0:T(8,128)(2,1)S(1)}, bf16[128,1024]{1,0:T(8,128)(2,1)S(1)}, bf16[128,1024]{1,0:T(8,128)(2,1)S(1)}, bf16[128,1024]{1,0:T(8,128)(2,1)S(1)}) custom-call(s32[1]{0:T(128)} %bitcast.here_ref, bf16[512,1152]{1,0:T(8,128)(2,1)S(1)} %get-tuple-element.75.band_ref, bf16[512,1024]{1,0:T(8,128)(2,1)S(1)} %get-tuple-element.85.refs_0_.own_ref, ...), custom_call_target="tpu_custom_call" | custom-call | bytes 1000 | tf_op jit(solution)/shard_map/pallas_call | solution.py:478
  104.5 3.1 %collective-permute-start.28 = (bf16[128,1024]{1,0:T(8,128)(2,1)S(1)}, bf16[128,1024]{1,0:T(8,128)(2,1)S(1)}, u32[]{:S(2)}, u32[]{:S(2)}) collective-permute-start(bf16[128,1024]{1,0:T(8,128)(2,1)S(1)} %get-tuple-element.95), channel_id=1, source_target_pairs={{0,1},{1,0},{2,3},{3,2},{4,5},{5,4},{6,7},{7,6},{8,9},{9,8},{10,11... | collective-permute-start | bytes 786440 | tf_op jit(solution)/shard_map/ppermute | solution.py:32
  107.6 1.1 collective-permute-start.29
  109.3 7.4 %collective-permute-done.25.refs_3_ = bf16[256,1024]{1,0:T(8,128)(2,1)S(1)} collective-permute-done((bf16[256,1024]{1,0:T(8,128)(2,1)S(1)}, bf16[256,1024]{1,0:T(8,128)(2,1)S(1)}, u32[]{:S(2)}, u32[]{:S(2)}) %collective-permute-start.25) | collective-permute-done | bytes 524320 | tf_op jit(solution)/shard_map/ppermute | solution.py:32
  116.7 2.9 %shard_map.82.tv_ref = f32[128,8,1024]{2,1,0:T(8,128)} custom-call(s32[1]{0:T(128)} %bitcast.here_ref, f32[128,8,1024]{2,1,0:T(8,128)} %get-tuple-element.88.tv_ref, bf16[256,1024]{1,0:T(8,128)(2,1)S(1)} %get-tuple-element.87.refs_4_.refs_0_, bf16[256,1024]{1,0:T(8,128)(2,1)S(1)} %collective-permute-done.23.refs_1_, ...), custom_call_target="tpu_custom_call", output_to_operand_aliasing={{}: (1, {})} | custom-call | bytes 1000 | tf_op jit(solution)/shard_map/pallas_call | solution.py:367
  119.6 2.6 %shard_map.83.refs_4_ = bf16[128,8,1024]{2,1,0:T(8,128)(2,1)} custom-call(s32[1]{0:T(128)} %bitcast.here_ref, bf16[128,8,512]{2,1,0:T(8,128)(2,1)S(1)} %shard_map.80.refs_1_.own_ref, bf16[128,8,512]{2,1,0:T(8,128)(2,1)S(1)} %collective-permute-done.31.above_ref, bf16[256,1024]{1,0:T(8,128)(2,1)S(1)} %get-tuple-element.87.refs_4_.refs_0_, ...), custom_call_target="tpu_custom_call" | custom-call | bytes 1000 | tf_op jit(solution)/shard_map/pallas_call | solution.py:345
  122.3 5.2 %collective-permute-done.30.refs_3_ = bf16[128,1024]{1,0:T(8,128)(2,1)S(1)} collective-permute-done((bf16[128,1024]{1,0:T(8,128)(2,1)S(1)}, bf16[128,1024]{1,0:T(8,128)(2,1)S(1)}, u32[]{:S(2)}, u32[]{:S(2)}) %collective-permute-start.30) | collective-permute-done | bytes 262176 | tf_op jit(solution)/shard_map/ppermute | solution.py:32
  127.5 2.9 %shard_map.84 = f32[128,8,1024]{2,1,0:T(8,128)} custom-call(s32[1]{0:T(128)} %bitcast.here_ref, f32[128,8,1024]{2,1,0:T(8,128)} %shard_map.82.tv_ref, bf16[128,1024]{1,0:T(8,128)(2,1)S(1)} %get-tuple-element.94.refs_4_.refs_0_, bf16[128,1024]{1,0:T(8,128)(2,1)S(1)} %collective-permute-done.28.refs_1_, ...), custom_call_target="tpu_custom_call", output_to_operand_aliasing={{}: (1, {})} | custom-call | bytes 1000 | tf_op jit(solution)/shard_map/pallas_call | solution.py:367
  (52 shorter events, 6.6 us)
Async XLA Ops:
  3.2 15.3 %collective-permute-start = (bf16[144,1024]{1,0:T(8,128)(2,1)S(1)}, bf16[144,1024]{1,0:T(8,128)(2,1)S(1)}, u32[]{:S(2)}, u32[]{:S(2)}) collective-permute-start(bf16[144,1024]{1,0:T(8,128)(2,1)S(1)} %get-tuple-element.50.refs_4_), channel_id=1, source_target_pairs={{0,1},{1,0},{2,3},{3,2},{4,5},{5,4},{6,7},{7,6},{8,9},{9,8},{10,11... | collective-permute-start | bytes 884744 | tf_op jit(solution)/shard_map/ppermute | solution.py:32
  3.2 15.3 %collective-permute-start.1 = (bf16[128,1024]{1,0:T(8,128)(2,1)}, bf16[128,1024]{1,0:T(8,128)(2,1)}, u32[]{:S(2)}, u32[]{:S(2)}) collective-permute-start(bf16[128,1024]{1,0:T(8,128)(2,1)} %get-tuple-element.52), channel_id=1, source_target_pairs={{0,2},{1,3},{2,0},{3,1},{4,6},{5,7},{6,4},{7,5},{8,10},{9,11},{10,... | collective-permute-start | bytes 786440 | tf_op jit(solution)/shard_map/ppermute | solution.py:32
  5.9 9.1 %copy-start.6 = (s32[16,6]{0,1:T(8,128)S(1)}, s32[16,6]{0,1:T(8,128)}, u32[]{:S(2)}) copy-start(s32[16,6]{0,1:T(8,128)} %param.8) | copy-start | bytes 1156
  5.9 10.0 %copy-start = (bf16[8,128,128]{2,1,0:T(8,128)(2,1)S(1)}, bf16[8,128,128]{2,1,0:T(8,128)(2,1)}, u32[]{:S(2)}) copy-start(bf16[8,128,128]{2,1,0:T(8,128)(2,1)} %refs_0_.1) | copy-start | bytes 786436
  5.9 13.3 %collective-permute-start.2 = (bf16[144,1024]{1,0:T(8,128)(2,1)S(1)}, bf16[144,1024]{1,0:T(8,128)(2,1)S(1)}, u32[]{:S(2)}, u32[]{:S(2)}) collective-permute-start(bf16[144,1024]{1,0:T(8,128)(2,1)S(1)} %get-tuple-element.53), channel_id=1, source_target_pairs={{0,3},{1,2},{2,1},{3,0},{4,7},{5,6},{6,5},{7,4},{8,11},{9,10},{10,... | collective-permute-start | bytes 884744 | tf_op jit(solution)/shard_map/ppermute | solution.py:32
  9.4 0.7 copy-start.2
  10.1 20.3 %collective-permute-start.4 = (bf16[128,8,512]{2,1,0:T(8,128)(2,1)}, bf16[128,8,512]{2,1,0:T(8,128)(2,1)S(1)}, u32[]{:S(2)}, u32[]{:S(2)}) collective-permute-start(bf16[128,8,512]{2,1,0:T(8,128)(2,1)} %get-tuple-element.58), channel_id=1, source_target_pairs={{3,7},{7,11},{11,15},{19,23},{23,27},{27,31}} | collective-permute-start | bytes 3145736 | tf_op jit(solution)/shard_map/ppermute | solution.py:27
  10.8 19.6 %collective-permute-start.5 = (bf16[256,1024]{1,0:T(8,128)(2,1)}, bf16[256,1024]{1,0:T(8,128)(2,1)}, u32[]{:S(2)}, u32[]{:S(2)}) collective-permute-start(bf16[256,1024]{1,0:T(8,128)(2,1)} %get-tuple-element.59), channel_id=1, source_target_pairs={{0,2},{1,3},{2,0},{3,1},{4,6},{5,7},{6,4},{7,5},{8,10},{9,11},{10,... | collective-permute-start | bytes 1572872 | tf_op jit(solution)/shard_map/ppermute | solution.py:32
  15.9 1.0 copy-start.3
  16.8 2.4 %copy-start.5 = (bf16[128,1024]{1,0:T(8,128)(2,1)S(1)}, bf16[128,1024]{1,0:T(8,128)(2,1)}, u32[]{:S(2)}) copy-start(bf16[128,1024]{1,0:T(8,128)(2,1)} %get-tuple-element.51.refs_0_) | copy-start | bytes 786436
  19.3 1.2 copy-start.4
  20.5 9.9 %collective-permute-start.6 = (bf16[128,1024]{1,0:T(8,128)(2,1)S(1)}, bf16[128,1024]{1,0:T(8,128)(2,1)S(1)}, u32[]{:S(2)}, u32[]{:S(2)}) collective-permute-start(bf16[128,1024]{1,0:T(8,128)(2,1)S(1)} %copy-done.4), channel_id=1, source_target_pairs={{0,1},{1,0},{2,3},{3,2},{4,5},{5,4},{6,7},{7,6},{8,9},{9,8},{10,11... | collective-permute-start | bytes 786440 | tf_op jit(solution)/shard_map/ppermute | solution.py:32
  20.7 18.3 %copy-start.1 = (bf16[128,1024]{1,0:T(8,128)(2,1)S(1)}, bf16[128,1024]{1,0:T(8,128)(2,1)}, u32[]{:S(2)}) copy-start(bf16[128,1024]{1,0:T(8,128)(2,1)} %get-tuple-element.65.refs_0_) | copy-start | bytes 786436
  20.7 26.0 %collective-permute-start.13 = (bf16[128,8,512]{2,1,0:T(8,128)(2,1)S(1)}, bf16[128,8,512]{2,1,0:T(8,128)(2,1)S(1)}, u32[]{:S(2)}, u32[]{:S(2)}) collective-permute-start(bf16[128,8,512]{2,1,0:T(8,128)(2,1)S(1)} %get-tuple-element.71), channel_id=1, source_target_pairs={{3,7},{7,11},{11,15},{19,23},{23,27},{27,31}} | collective-permute-start | bytes 3145736 | tf_op jit(solution)/shard_map/ppermute | solution.py:27
  21.6 28.1 %collective-permute-start.3 = (bf16[528,1024]{1,0:T(8,128)(2,1)S(1)}, bf16[528,1024]{1,0:T(8,128)(2,1)S(1)}, u32[]{:S(2)}, u32[]{:S(2)}) collective-permute-start(bf16[528,1024]{1,0:T(8,128)(2,1)S(1)} %get-tuple-element.56.own_ref), channel_id=1, source_target_pairs={{4,0},{5,1},{6,2},{7,3},{8,4},{9,5},{10,6},{11,7},{12,8},{13,9},{1... | collective-permute-start | bytes 3244040 | tf_op jit(solution)/shard_map/ppermute | solution.py:27
  32.2 12.9 %collective-permute-start.9 = (bf16[256,1024]{1,0:T(8,128)(2,1)S(1)}, bf16[256,1024]{1,0:T(8,128)(2,1)S(1)}, u32[]{:S(2)}, u32[]{:S(2)}) collective-permute-start(bf16[256,1024]{1,0:T(8,128)(2,1)S(1)} %get-tuple-element.64), channel_id=1, source_target_pairs={{0,2},{1,3},{2,0},{3,1},{4,6},{5,7},{6,4},{7,5},{8,10},{9,11},{10,... | collective-permute-start | bytes 1572872 | tf_op jit(solution)/shard_map/ppermute | solution.py:32
  33.5 2.3 %collective-permute-start.7 = (bf16[128,1024]{1,0:T(8,128)(2,1)S(1)}, bf16[128,1024]{1,0:T(8,128)(2,1)S(1)}, u32[]{:S(2)}, u32[]{:S(2)}) collective-permute-start(bf16[128,1024]{1,0:T(8,128)(2,1)S(1)} %get-tuple-element.61), channel_id=1, source_target_pairs={{0,1},{1,0},{2,3},{3,2},{4,5},{5,4},{6,7},{7,6},{8,9},{9,8},{10,11... | collective-permute-start | bytes 786440 | tf_op jit(solution)/shard_map/ppermute | solution.py:32
  34.7 4.4 %collective-permute-start.10 = (bf16[128,1024]{1,0:T(8,128)(2,1)S(1)}, bf16[128,1024]{1,0:T(8,128)(2,1)S(1)}, u32[]{:S(2)}, u32[]{:S(2)}) collective-permute-start(bf16[128,1024]{1,0:T(8,128)(2,1)S(1)} %get-tuple-element.66), channel_id=1, source_target_pairs={{0,1},{1,0},{2,3},{3,2},{4,5},{5,4},{6,7},{7,6},{8,9},{9,8},{10,11... | collective-permute-start | bytes 786440 | tf_op jit(solution)/shard_map/ppermute | solution.py:32
  35.8 15.7 %collective-permute-start.8 = (bf16[144,1024]{1,0:T(8,128)(2,1)S(1)}, bf16[144,1024]{1,0:T(8,128)(2,1)S(1)}, u32[]{:S(2)}, u32[]{:S(2)}) collective-permute-start(bf16[144,1024]{1,0:T(8,128)(2,1)S(1)} %get-tuple-element.62), channel_id=1, source_target_pairs={{0,4},{1,5},{2,6},{3,7},{4,8},{5,9},{6,10},{7,11},{8,12},{9,13},{1... | collective-permute-start | bytes 884744 | tf_op jit(solution)/shard_map/ppermute | solution.py:27
  40.2 10.4 %collective-permute-start.12 = (bf16[128,1024]{1,0:T(8,128)(2,1)S(1)}, bf16[128,1024]{1,0:T(8,128)(2,1)S(1)}, u32[]{:S(2)}, u32[]{:S(2)}) collective-permute-start(bf16[128,1024]{1,0:T(8,128)(2,1)S(1)} %get-tuple-element.69), channel_id=1, source_target_pairs={{0,4},{1,5},{2,6},{3,7},{4,8},{5,9},{6,10},{7,11},{8,12},{9,13},{1... | collective-permute-start | bytes 786440 | tf_op jit(solution)/shard_map/ppermute | solution.py:27
  45.1 6.4 %collective-permute-start.11 = (bf16[128,1024]{1,0:T(8,128)(2,1)S(1)}, bf16[128,1024]{1,0:T(8,128)(2,1)S(1)}, u32[]{:S(2)}, u32[]{:S(2)}) collective-permute-start(bf16[128,1024]{1,0:T(8,128)(2,1)S(1)} %slice.9), channel_id=1, source_target_pairs={{0,1},{1,0},{2,3},{3,2},{4,5},{5,4},{6,7},{7,6},{8,9},{9,8},{10,11... | collective-permute-start | bytes 786440 | tf_op jit(solution)/shard_map/ppermute | solution.py:32
  46.7 26.6 %collective-permute-start.16 = (bf16[512,1024]{1,0:T(8,128)(2,1)S(1)}, bf16[512,1024]{1,0:T(8,128)(2,1)S(1)}, u32[]{:S(2)}, u32[]{:S(2)}) collective-permute-start(bf16[512,1024]{1,0:T(8,128)(2,1)S(1)} %get-tuple-element.67.refs_0_.own_ref), channel_id=1, source_target_pairs={{4,0},{5,1},{6,2},{7,3},{8,4},{9,5},{10,6},{11,7},{12,8},{13,9},{1... | collective-permute-start | bytes 3145736 | tf_op jit(solution)/shard_map/ppermute | solution.py:27
  49.7 4.0 %collective-permute-start.17 = (bf16[128,1024]{1,0:T(8,128)(2,1)S(1)}, bf16[128,1024]{1,0:T(8,128)(2,1)S(1)}, u32[]{:S(2)}, u32[]{:S(2)}) collective-permute-start(bf16[128,1024]{1,0:T(8,128)(2,1)S(1)} %get-tuple-element.77), channel_id=1, source_target_pairs={{0,1},{1,0},{2,3},{3,2},{4,5},{5,4},{6,7},{7,6},{8,9},{9,8},{10,11... | collective-permute-start | bytes 786440 | tf_op jit(solution)/shard_map/ppermute | solution.py:32
  50.6 20.0 %collective-permute-start.18 = (bf16[256,1024]{1,0:T(8,128)(2,1)S(1)}, bf16[256,1024]{1,0:T(8,128)(2,1)S(1)}, u32[]{:S(2)}, u32[]{:S(2)}) collective-permute-start(bf16[256,1024]{1,0:T(8,128)(2,1)S(1)} %get-tuple-element.78), channel_id=1, source_target_pairs={{0,2},{1,3},{2,0},{3,1},{4,6},{5,7},{6,4},{7,5},{8,10},{9,11},{10,... | collective-permute-start | bytes 1572872 | tf_op jit(solution)/shard_map/ppermute | solution.py:32
  53.7 20.4 %collective-permute-start.21 = (bf16[256,1024]{1,0:T(8,128)(2,1)S(1)}, bf16[256,1024]{1,0:T(8,128)(2,1)S(1)}, u32[]{:S(2)}, u32[]{:S(2)}) collective-permute-start(bf16[256,1024]{1,0:T(8,128)(2,1)S(1)} %get-tuple-element.84), channel_id=1, source_target_pairs={{0,2},{1,3},{2,0},{3,1},{4,6},{5,7},{6,4},{7,5},{8,10},{9,11},{10,... | collective-permute-start | bytes 1572872 | tf_op jit(solution)/shard_map/ppermute | solution.py:32
  54.3 30.4 %collective-permute-start.14 = (bf16[512,1024]{1,0:T(8,128)(2,1)S(1)}, bf16[512,1024]{1,0:T(8,128)(2,1)S(1)}, u32[]{:S(2)}, u32[]{:S(2)}) collective-permute-start(bf16[512,1024]{1,0:T(8,128)(2,1)S(1)} %get-tuple-element.73.refs_0_.own_ref), channel_id=1, source_target_pairs={{0,4},{1,5},{2,6},{3,7},{4,8},{5,9},{6,10},{7,11},{8,12},{9,13},{1... | collective-permute-start | bytes 3145736 | tf_op jit(solution)/shard_map/ppermute | solution.py:27
  58.5 12.2 %collective-permute-start.20 = (bf16[128,1024]{1,0:T(8,128)(2,1)S(1)}, bf16[128,1024]{1,0:T(8,128)(2,1)S(1)}, u32[]{:S(2)}, u32[]{:S(2)}) collective-permute-start(bf16[128,1024]{1,0:T(8,128)(2,1)S(1)} %get-tuple-element.82), channel_id=1, source_target_pairs={{0,1},{1,0},{2,3},{3,2},{4,5},{5,4},{6,7},{7,6},{8,9},{9,8},{10,11... | collective-permute-start | bytes 786440 | tf_op jit(solution)/shard_map/ppermute | solution.py:32
  70.6 1.6 %collective-permute-start.19 = (bf16[128,1024]{1,0:T(8,128)(2,1)S(1)}, bf16[128,1024]{1,0:T(8,128)(2,1)S(1)}, u32[]{:S(2)}, u32[]{:S(2)}) collective-permute-start(bf16[128,1024]{1,0:T(8,128)(2,1)S(1)} %slice.10), channel_id=1, source_target_pairs={{0,1},{1,0},{2,3},{3,2},{4,5},{5,4},{6,7},{7,6},{8,9},{9,8},{10,11... | collective-permute-start | bytes 786440 | tf_op jit(solution)/shard_map/ppermute | solution.py:32
  70.7 14.1 %collective-permute-start.15 = (bf16[128,1024]{1,0:T(8,128)(2,1)S(1)}, bf16[128,1024]{1,0:T(8,128)(2,1)S(1)}, u32[]{:S(2)}, u32[]{:S(2)}) collective-permute-start(bf16[128,1024]{1,0:T(8,128)(2,1)S(1)} %get-tuple-element.76), channel_id=1, source_target_pairs={{4,0},{5,1},{6,2},{7,3},{8,4},{9,5},{10,6},{11,7},{12,8},{13,9},{1... | collective-permute-start | bytes 786440 | tf_op jit(solution)/shard_map/ppermute | solution.py:27
  76.2 8.6 %collective-permute-start.22 = (bf16[128,1024]{1,0:T(8,128)(2,1)S(1)}, bf16[128,1024]{1,0:T(8,128)(2,1)S(1)}, u32[]{:S(2)}, u32[]{:S(2)}) collective-permute-start(bf16[128,1024]{1,0:T(8,128)(2,1)S(1)} %get-tuple-element.86), channel_id=1, source_target_pairs={{4,0},{5,1},{6,2},{7,3},{8,4},{9,5},{10,6},{11,7},{12,8},{13,9},{1... | collective-permute-start | bytes 786440 | tf_op jit(solution)/shard_map/ppermute | solution.py:27
  77.5 25.0 %collective-permute-start.26 = (bf16[512,1024]{1,0:T(8,128)(2,1)S(1)}, bf16[512,1024]{1,0:T(8,128)(2,1)S(1)}, u32[]{:S(2)}, u32[]{:S(2)}) collective-permute-start(bf16[512,1024]{1,0:T(8,128)(2,1)S(1)} %get-tuple-element.85.refs_0_.own_ref), channel_id=1, source_target_pairs={{0,4},{1,5},{2,6},{3,7},{4,8},{5,9},{6,10},{7,11},{8,12},{9,13},{1... | collective-permute-start | bytes 3145736 | tf_op jit(solution)/shard_map/ppermute | solution.py:27
  82.3 4.6 %collective-permute-start.27 = (bf16[128,1024]{1,0:T(8,128)(2,1)S(1)}, bf16[128,1024]{1,0:T(8,128)(2,1)S(1)}, u32[]{:S(2)}, u32[]{:S(2)}) collective-permute-start(bf16[128,1024]{1,0:T(8,128)(2,1)S(1)} %slice.11), channel_id=1, source_target_pairs={{0,1},{1,0},{2,3},{3,2},{4,5},{5,4},{6,7},{7,6},{8,9},{9,8},{10,11... | collective-permute-start | bytes 786440 | tf_op jit(solution)/shard_map/ppermute | solution.py:32
  87.8 31.8 %collective-permute-start.31 = (bf16[128,8,512]{2,1,0:T(8,128)(2,1)S(1)}, bf16[128,8,512]{2,1,0:T(8,128)(2,1)S(1)}, u32[]{:S(2)}, u32[]{:S(2)}) collective-permute-start(bf16[128,8,512]{2,1,0:T(8,128)(2,1)S(1)} %shard_map.80.refs_1_.own_ref), channel_id=1, source_target_pairs={{7,3},{11,7},{15,11},{23,19},{27,23},{31,27}} | collective-permute-start | bytes 3145736 | tf_op jit(solution)/shard_map/ppermute | solution.py:27
  88.5 19.0 %collective-permute-start.23 = (bf16[256,1024]{1,0:T(8,128)(2,1)S(1)}, bf16[256,1024]{1,0:T(8,128)(2,1)S(1)}, u32[]{:S(2)}, u32[]{:S(2)}) collective-permute-start(bf16[256,1024]{1,0:T(8,128)(2,1)S(1)} %get-tuple-element.89), channel_id=1, source_target_pairs={{0,1},{1,0},{2,3},{3,2},{4,5},{5,4},{6,7},{7,6},{8,9},{9,8},{10,11... | collective-permute-start | bytes 1572872 | tf_op jit(solution)/shard_map/ppermute | solution.py:32
  91.3 17.3 %collective-permute-start.24 = (bf16[256,1024]{1,0:T(8,128)(2,1)S(1)}, bf16[256,1024]{1,0:T(8,128)(2,1)S(1)}, u32[]{:S(2)}, u32[]{:S(2)}) collective-permute-start(bf16[256,1024]{1,0:T(8,128)(2,1)S(1)} %get-tuple-element.90), channel_id=1, source_target_pairs={{0,2},{1,3},{2,0},{3,1},{4,6},{5,7},{6,4},{7,5},{8,10},{9,11},{10,... | collective-permute-start | bytes 1572872 | tf_op jit(solution)/shard_map/ppermute | solution.py:32
  92.4 24.3 %collective-permute-start.25 = (bf16[256,1024]{1,0:T(8,128)(2,1)S(1)}, bf16[256,1024]{1,0:T(8,128)(2,1)S(1)}, u32[]{:S(2)}, u32[]{:S(2)}) collective-permute-start(bf16[256,1024]{1,0:T(8,128)(2,1)S(1)} %get-tuple-element.91), channel_id=1, source_target_pairs={{0,3},{1,2},{2,1},{3,0},{4,7},{5,6},{6,5},{7,4},{8,11},{9,10},{10,... | collective-permute-start | bytes 1572872 | tf_op jit(solution)/shard_map/ppermute | solution.py:32
  104.5 17.8 %collective-permute-start.28 = (bf16[128,1024]{1,0:T(8,128)(2,1)S(1)}, bf16[128,1024]{1,0:T(8,128)(2,1)S(1)}, u32[]{:S(2)}, u32[]{:S(2)}) collective-permute-start(bf16[128,1024]{1,0:T(8,128)(2,1)S(1)} %get-tuple-element.95), channel_id=1, source_target_pairs={{0,1},{1,0},{2,3},{3,2},{4,5},{5,4},{6,7},{7,6},{8,9},{9,8},{10,11... | collective-permute-start | bytes 786440 | tf_op jit(solution)/shard_map/ppermute | solution.py:32
  107.6 14.7 %collective-permute-start.29 = (bf16[128,1024]{1,0:T(8,128)(2,1)S(1)}, bf16[128,1024]{1,0:T(8,128)(2,1)S(1)}, u32[]{:S(2)}, u32[]{:S(2)}) collective-permute-start(bf16[128,1024]{1,0:T(8,128)(2,1)S(1)} %get-tuple-element.96), channel_id=1, source_target_pairs={{0,2},{1,3},{2,0},{3,1},{4,6},{5,7},{6,4},{7,5},{8,10},{9,11},{10,... | collective-permute-start | bytes 786440 | tf_op jit(solution)/shard_map/ppermute | solution.py:32
  108.7 18.8 %collective-permute-start.30 = (bf16[128,1024]{1,0:T(8,128)(2,1)S(1)}, bf16[128,1024]{1,0:T(8,128)(2,1)S(1)}, u32[]{:S(2)}, u32[]{:S(2)}) collective-permute-start(bf16[128,1024]{1,0:T(8,128)(2,1)S(1)} %get-tuple-element.97), channel_id=1, source_target_pairs={{0,3},{1,2},{2,1},{3,0},{4,7},{5,6},{6,5},{7,4},{8,11},{9,10},{10,... | collective-permute-start | bytes 786440 | tf_op jit(solution)/shard_map/ppermute | solution.py:32

commit v15 on v14

--- a/solution.py
+++ b/solution.py
@@ -585,18 +585,18 @@
 
     s0, s1, s23 = split_rows(here, sinogram, got1, 1, paired, [], own1)
 
-    resid0, down0, r1, r23 = project(here, band_p, own0, high0, low0, sinos0, paired[1:], low1, s0)
+    resid0, down0, *r = project(here, band_p, own0, high0, low0, sinos0, single[1:], low1, s0)
     from_low0, from_high0 = moved(resid0, G), moved(down0, -G)
     s_near, s_over = swapped(s1, 1), swapped(s23, 2)
-    r_near, r_over = swapped(tied(r1, s_near), 1), swapped(tied(r23, s_near), 2)
+    got_r = [swapped(tied(array, s_near), m + 1) for m, array in enumerate(r)]
     tv, tv_done = half_tv(here, volume, [got_vols0[1], high0, got_vols0[3], low0], resid0)
     sinos1 = [(s0, 0), (s_near, 0), (s_over, 0), (beyond(s_over, tv_done), 0)]
-    resid1, down1 = project(here, band_p, own1, high1, low1, sinos1, (), tv_done, r_near, r_over)
+    resid1, down1 = project(here, band_p, own1, high1, low1, sinos1, (), tv_done, *got_r)
     from_low1, from_high1 = moved(resid1, G), moved(down1, -G)
 
     backs0 = back(here, band_b, resid0, from_low0, from_high0, [resid1, from_high1])
     got_backs0 = direct(backs0)
-    r_pieces = [(resid0, 0), (r_near, 0), (r_over, 0), (beyond(r_over, resid1), 0)]
+    r_pieces = [(array, 0) for array in [resid0] + got_r]
     natural0 = join_rows(here, r_pieces, sinogram.shape, backs0[0])
     above0 = moved(natural0, -G, only=G - 1)
     r_last, tv = last_group(here, coverage, offsets, weights, volume, sinogram, tv, backs0[0])

time: 131 us -> 135 us (1.031)
  waiting for transfers between devices: 34.8 us -> 45.2 us
  starting transfers between devices: 49.8 us -> 43.5 us
    ppermute x21, waiting for transfers between devices: 24.7 us -> 30.4 us  [swapped(): return lax.ppermute(value, 'slab', [(i, i ^ bits) for i in range(count)])]
    ppermute x21, starting transfers between devices: 27 us -> 21.4 us  [swapped(): return lax.ppermute(value, 'slab', [(i, i ^ bits) for i in range(count)])]
    ppermute x11, waiting for transfers between devices: 10.2 us -> 14.8 us  [moved(): return lax.ppermute(value, 'slab', pairs)]
  transfers between devices with their start and end apart: 32 -> 32, of which waited for: 11 -> 10; matrix products, arithmetic and copies ran while one was open for 1% -> 1% of each run, Pallas kernels for 28% -> 27%
where the time goes in v15:
time: 135 us; the launch traced here: 134 us
  waiting for transfers between devices  45.2 us (33%)
  starting transfers between devices  43.5 us (32%)
  Pallas kernels  42.3 us (31%)
  local copies, waits for them, and re-layouts  2.55 us (2%)
    ppermute x21, waiting for transfers between devices, swapped(): return lax.ppermute(value, 'slab', [(i, i ^ bits) for i in range(count)])  30.4 us
    ppermute x11, starting transfers between devices, moved(): return lax.ppermute(value, 'slab', pairs)  22.1 us
    ppermute x21, starting transfers between devices, swapped(): return lax.ppermute(value, 'slab', [(i, i ^ bits) for i in range(count)])  21.4 us
    ppermute x11, waiting for transfers between devices, moved(): return lax.ppermute(value, 'slab', pairs)  14.8 us
    pallas_call x1, Pallas kernels, half_tv(): call(tv_kernel, 0, grid=(depth // deep,), in_specs=[SMEM] + edges + [afte...  9.99 us
    pallas_call x2, Pallas kernels, cast_rows(): call(functools.partial(cast_kernel, groups, len(edges), halves), 2, grid=...  5.97 us
    pallas_call x2, Pallas kernels, finish(): call(finish_kernel, 0, grid=(count,), in_specs=[SMEM, part] + piece_specs...  5.85 us
    pallas_call x2, Pallas kernels, project(): call(functools.partial(project_kernel, groups), 3, grid=(cols // tile,),...  4.23 us
  transfers between devices with their start and end apart: 32, of which 10 were waited for; matrix products, arithmetic and copies ran while one was open for 1% of the time, Pallas kernels for 27%

profile of v15, /device:TPU:1, one launch (start us, length us, event | category | flops | bytes accessed | tf_op | source)
XLA Modules:
  0.0 134.4 jit_solution(12755770966754975138)
XLA Ops:
  0.6 2.5 %shard_map.68 = (bf16[128,1024]{1,0:T(8,128)(2,1)}, bf16[144,1024]{1,0:T(8,128)(2,1)S(1)}, bf16[128,1024]{1,0:T(8,128)(2,1)}, bf16[144,1024]{1,0:T(8,128)(2,1)S(1)}) custom-call(s32[1]{0:T(128)} %bitcast.here_ref, f32[1024,1024]{1,0:T(8,128)} %bitcast.2, f32[1024,1024]{1,0:T(8,128)} %bitcast.3, f32[1024,1024]{1,0:T(8,128)} %bitcast.4, f32[1024,1024]{1,0:T(8,128)} %bitcast.5), custom_call_target="tpu_custom_call" | custom-call | flops 2300000000 | bytes 1000 | tf_op jit(solution)/shard_map/pallas_call | solution.py:115
  3.2 2.7 %collective-permute-start.1 = (bf16[128,1024]{1,0:T(8,128)(2,1)}, bf16[128,1024]{1,0:T(8,128)(2,1)}, u32[]{:S(2)}, u32[]{:S(2)}) collective-permute-start(bf16[128,1024]{1,0:T(8,128)(2,1)} %get-tuple-element.53), channel_id=1, source_target_pairs={{0,2},{1,3},{2,0},{3,1},{4,6},{5,7},{6,4},{7,5},{8,10},{9,11},{10,... | collective-permute-start | bytes 786440 | tf_op jit(solution)/shard_map/ppermute | solution.py:32
  6.0 3.4 %shard_map.69 = (bf16[128,1024]{1,0:T(8,128)(2,1)}, bf16[128,1024]{1,0:T(8,128)(2,1)S(1)}, bf16[256,1024]{1,0:T(8,128)(2,1)}, bf16[128,8,512]{2,1,0:T(8,128)(2,1)}, bf16[128,8,512]{2,1,0:T(8,128)(2,1)S(1)}) custom-call(s32[1]{0:T(128)} %bitcast.here_ref, f32[1024,1024]{1,0:T(8,128)} %bitcast.6, f32[1024,1024]{1,0:T(8,128)} %bitcast.7, ...), custom_call_target="tpu_custom_call" | custom-call | flops 2300000000 | bytes 1000 | tf_op jit(solution)/shard_map/pallas_call | solution.py:115
  10.8 4.2 %collective-permute-start.5 = (bf16[256,1024]{1,0:T(8,128)(2,1)}, bf16[256,1024]{1,0:T(8,128)(2,1)}, u32[]{:S(2)}, u32[]{:S(2)}) collective-permute-start(bf16[256,1024]{1,0:T(8,128)(2,1)} %get-tuple-element.60), channel_id=1, source_target_pairs={{0,2},{1,3},{2,0},{3,1},{4,6},{5,7},{6,4},{7,5},{8,10},{9,11},{10,... | collective-permute-start | bytes 1572872 | tf_op jit(solution)/shard_map/ppermute | solution.py:32
  15.1 0.8 copy.13.offset_ref
  15.9 0.9 copy-done.3
  16.8 1.6 %shard_map.70 = (bf16[512,1152]{1,0:T(8,128)(2,1)S(1)}, bf16[512,1152]{1,0:T(8,128)(2,1)S(1)}) custom-call(s32[1]{0:T(128)} %bitcast.here_ref, s32[16,6]{1,0:T(8,128)S(1)} %copy.12.cover_ref, s32[16,6]{1,0:T(8,128)S(1)} %copy.13.offset_ref, bf16[8,128,128]{2,1,0:T(8,128)(2,1)S(1)} %copy-done, bf16[128,1024]{1,0:T(8,128)(2,1)S(1)} %copy-done.3), custom_call_target="tpu_custom_call" | custom-call | flops 10350000128 | bytes 1000 | tf_op jit(solution)/shard_map/pallas_call | solution.py:415
  19.3 1.2 shard_map.71
  20.7 0.8 collective-permute-start.13
  21.6 1.3 collective-permute-start.3
  22.9 7.5 %collective-permute-done.5.refs_0_.refs_2_ = bf16[256,1024]{1,0:T(8,128)(2,1)} collective-permute-done((bf16[256,1024]{1,0:T(8,128)(2,1)}, bf16[256,1024]{1,0:T(8,128)(2,1)}, u32[]{:S(2)}, u32[]{:S(2)}) %collective-permute-start.5) | collective-permute-done | bytes 524320 | tf_op jit(solution)/shard_map/ppermute | solution.py:32
  30.4 1.8 %shard_map.72 = (bf16[128,1024]{1,0:T(8,128)(2,1)S(1)}, bf16[128,1024]{1,0:T(8,128)(2,1)S(1)}, bf16[256,1024]{1,0:T(8,128)(2,1)S(1)}, bf16[128,1024]{1,0:T(8,128)(2,1)S(1)}) custom-call(s32[1]{0:T(128)} %bitcast.here_ref, bf16[128,8,1024]{2,1,0:T(8,128)(2,1)} %refs_2_.3, bf16[128,8,512]{2,1,0:T(8,128)(2,1)S(1)} %collective-permute-done.4.got_ref, ...), custom_call_target="tpu_custom_call" | custom-call | flops 2300000000 | bytes 1000 | tf_op jit(solution)/shard_map/pallas_call | solution.py:196
  32.2 1.3 collective-permute-start.9
  33.5 1.1 collective-permute-start.7
  34.7 1.2 collective-permute-done.7.refs_1_
  35.8 3.2 %collective-permute-start.8 = (bf16[144,1024]{1,0:T(8,128)(2,1)S(1)}, bf16[144,1024]{1,0:T(8,128)(2,1)S(1)}, u32[]{:S(2)}, u32[]{:S(2)}) collective-permute-start(bf16[144,1024]{1,0:T(8,128)(2,1)S(1)} %get-tuple-element.63), channel_id=1, source_target_pairs={{0,4},{1,5},{2,6},{3,7},{4,8},{5,9},{6,10},{7,11},{8,12},{9,13},{1... | collective-permute-start | bytes 884744 | tf_op jit(solution)/shard_map/ppermute | solution.py:27
  39.0 1.2 shard_map.73
  40.2 3.2 %collective-permute-start.12 = (bf16[128,1024]{1,0:T(8,128)(2,1)S(1)}, bf16[128,1024]{1,0:T(8,128)(2,1)S(1)}, u32[]{:S(2)}, u32[]{:S(2)}) collective-permute-start(bf16[128,1024]{1,0:T(8,128)(2,1)S(1)} %get-tuple-element.70), channel_id=1, source_target_pairs={{0,4},{1,5},{2,6},{3,7},{4,8},{5,9},{6,10},{7,11},{8,12},{9,13},{1... | collective-permute-start | bytes 786440 | tf_op jit(solution)/shard_map/ppermute | solution.py:27
  43.4 1.6 %collective-permute-done.9.refs_2_ = bf16[256,1024]{1,0:T(8,128)(2,1)S(1)} collective-permute-done((bf16[256,1024]{1,0:T(8,128)(2,1)S(1)}, bf16[256,1024]{1,0:T(8,128)(2,1)S(1)}, u32[]{:S(2)}, u32[]{:S(2)}) %collective-permute-start.9) | collective-permute-done | bytes 524320 | tf_op jit(solution)/shard_map/ppermute | solution.py:32
  45.1 1.6 %collective-permute-start.11 = (bf16[128,1024]{1,0:T(8,128)(2,1)S(1)}, bf16[128,1024]{1,0:T(8,128)(2,1)S(1)}, u32[]{:S(2)}, u32[]{:S(2)}) collective-permute-start(bf16[128,1024]{1,0:T(8,128)(2,1)S(1)} %slice.6), channel_id=1, source_target_pairs={{0,1},{1,0},{2,3},{3,2},{4,5},{5,4},{6,7},{7,6},{8,9},{9,8},{10,11... | collective-permute-start | bytes 786440 | tf_op jit(solution)/shard_map/ppermute | solution.py:32
  46.7 1.3 collective-permute-start.16
  48.0 1.7 %shard_map.74 = (bf16[128,1024]{1,0:T(8,128)(2,1)S(1)}, bf16[128,1024]{1,0:T(8,128)(2,1)S(1)}, bf16[256,1024]{1,0:T(8,128)(2,1)S(1)}) custom-call(s32[1]{0:T(128)} %bitcast.here_ref, bf16[128,8,1024]{2,1,0:T(8,128)(2,1)} %refs_2_.3, bf16[128,8,512]{2,1,0:T(8,128)(2,1)S(1)} %collective-permute-done.13.got_ref, ...), custom_call_target="tpu_custom_call" | custom-call | flops 2300000000 | bytes 1000 | tf_op jit(solution)/shard_map/pallas_call | solution.py:196
  50.6 0.9 collective-permute-start.18
  51.5 2.2 %shard_map.75 = (bf16[512,1024]{1,0:T(8,128)(2,1)S(1)}, bf16[128,1024]{1,0:T(8,128)(2,1)S(1)}, bf16[128,1024]{1,0:T(8,128)(2,1)S(1)}, bf16[128,1024]{1,0:T(8,128)(2,1)S(1)}, bf16[128,1024]{1,0:T(8,128)(2,1)S(1)}) custom-call(s32[1]{0:T(128)} %bitcast.here_ref, bf16[512,1152]{1,0:T(8,128)(2,1)S(1)} %get-tuple-element.56.refs_4_.band_ref, ...), custom_call_target="tpu_custom_call" | custom-call | flops 3449999872 | bytes 1000 | tf_op jit(solution)/shard_map/pallas_call | solution.py:446
  53.7 0.9 collective-permute-start.20
  54.6 4.1 %collective-permute-start.14 = (bf16[512,1024]{1,0:T(8,128)(2,1)S(1)}, bf16[512,1024]{1,0:T(8,128)(2,1)S(1)}, u32[]{:S(2)}, u32[]{:S(2)}) collective-permute-start(bf16[512,1024]{1,0:T(8,128)(2,1)S(1)} %get-tuple-element.74.refs_0_.own_ref), channel_id=1, source_target_pairs={{0,4},{1,5},{2,6},{3,7},{4,8},{5,9},{6,10},{7,11},{8,12},{9,13},{1... | collective-permute-start | bytes 3145736 | tf_op jit(solution)/shard_map/ppermute | solution.py:27
  58.7 1.3 collective-permute-start.21
  60.0 10.0 %shard_map.76 = (f32[128,8,1024]{2,1,0:T(8,128)}, f32[8,128]{1,0:T(8,128)S(1)}) custom-call(s32[1]{0:T(128)} %bitcast.here_ref, bf16[144,1024]{1,0:T(8,128)(2,1)S(1)} %collective-permute-done.refs_1_.near_ref, bf16[528,1024]{1,0:T(8,128)(2,1)S(1)} %collective-permute-done.3.high_ref.next_level_ref, ...), custom_call_target="tpu_custom_call" | custom-call | bytes 1000 | tf_op jit(solution)/shard_map/pallas_call | solution.py:546
  70.9 1.3 collective-permute-start.15
  72.2 6.7 %collective-permute-done.22.refs_7_.refs_3_ = bf16[128,1024]{1,0:T(8,128)(2,1)S(1)} collective-permute-done((bf16[128,1024]{1,0:T(8,128)(2,1)S(1)}, bf16[128,1024]{1,0:T(8,128)(2,1)S(1)}, u32[]{:S(2)}, u32[]{:S(2)}) %collective-permute-start.22) | collective-permute-done | bytes 262176 | tf_op jit(solution)/shard_map/ppermute | solution.py:32
  78.8 2.1 %shard_map.77 = (bf16[512,1024]{1,0:T(8,128)(2,1)S(1)}, bf16[128,1024]{1,0:T(8,128)(2,1)S(1)}) custom-call(s32[1]{0:T(128)} %bitcast.here_ref, bf16[512,1152]{1,0:T(8,128)(2,1)S(1)} %get-tuple-element.56.refs_4_.band_ref, bf16[512,1024]{1,0:T(8,128)(2,1)S(1)} %get-tuple-element.68.refs_0_.own_ref, bf16[512,1024]{1,0:T(8,128)(2,1)S(1)} %collective-permute-done.16.high_ref, ...), custom_call_target="tpu_custom_call" | custom-call | flops 3449999872 | bytes 1000 | tf_op jit(solution)/shard_map/pallas_call | solution.py:446
  80.9 1.3 collective-permute-start.23
  82.2 4.1 %collective-permute-start.27 = (bf16[512,1024]{1,0:T(8,128)(2,1)S(1)}, bf16[512,1024]{1,0:T(8,128)(2,1)S(1)}, u32[]{:S(2)}, u32[]{:S(2)}) collective-permute-start(bf16[512,1024]{1,0:T(8,128)(2,1)S(1)} %get-tuple-element.88.refs_0_.own_ref), channel_id=1, source_target_pairs={{0,4},{1,5},{2,6},{3,7},{4,8},{5,9},{6,10},{7,11},{8,12},{9,13},{1... | collective-permute-start | bytes 3145736 | tf_op jit(solution)/shard_map/ppermute | solution.py:27
  86.3 4.1 %collective-permute-done.23.refs_1_.high_ref = bf16[128,1024]{1,0:T(8,128)(2,1)S(1)} collective-permute-done((bf16[128,1024]{1,0:T(8,128)(2,1)S(1)}, bf16[128,1024]{1,0:T(8,128)(2,1)S(1)}, u32[]{:S(2)}, u32[]{:S(2)}) %collective-permute-start.23) | collective-permute-done | bytes 262176 | tf_op jit(solution)/shard_map/ppermute | solution.py:27
  90.4 2.1 %shard_map.78 = (bf16[256,1024]{1,0:T(8,128)(2,1)S(1)}, bf16[256,1024]{1,0:T(8,128)(2,1)S(1)}, bf16[256,1024]{1,0:T(8,128)(2,1)S(1)}, bf16[256,1024]{1,0:T(8,128)(2,1)S(1)}) custom-call(s32[1]{0:T(128)} %bitcast.here_ref, bf16[512,1152]{1,0:T(8,128)(2,1)S(1)} %get-tuple-element.76.band_ref, bf16[512,1024]{1,0:T(8,128)(2,1)S(1)} %get-tuple-element.74.refs_0_.own_ref, ...), custom_call_target="tpu_custom_call" | custom-call | bytes 1000 | tf_op jit(solution)/shard_map/pallas_call | solution.py:478
  92.6 0.9 shard_map.80.refs_1_.own_ref
  94.2 1.2 collective-permute-start.24
  95.6 1.5 %collective-permute-start.26 = (bf16[256,1024]{1,0:T(8,128)(2,1)S(1)}, bf16[256,1024]{1,0:T(8,128)(2,1)S(1)}, u32[]{:S(2)}, u32[]{:S(2)}) collective-permute-start(bf16[256,1024]{1,0:T(8,128)(2,1)S(1)} %get-tuple-element.94), channel_id=1, source_target_pairs={{0,3},{1,2},{2,1},{3,0},{4,7},{5,6},{6,5},{7,4},{8,11},{9,10},{10,... | collective-permute-start | bytes 1572872 | tf_op jit(solution)/shard_map/ppermute | solution.py:32
  97.1 1.2 shard_map.79
  98.2 9.9 %collective-permute-done.27.low_ref = bf16[512,1024]{1,0:T(8,128)(2,1)S(1)} collective-permute-done((bf16[512,1024]{1,0:T(8,128)(2,1)S(1)}, bf16[512,1024]{1,0:T(8,128)(2,1)S(1)}, u32[]{:S(2)}, u32[]{:S(2)}) %collective-permute-start.27) | collective-permute-done | bytes 1048608 | tf_op jit(solution)/shard_map/ppermute | solution.py:27
  108.1 1.9 %shard_map.81 = (bf16[128,1024]{1,0:T(8,128)(2,1)S(1)}, bf16[128,1024]{1,0:T(8,128)(2,1)S(1)}, bf16[128,1024]{1,0:T(8,128)(2,1)S(1)}, bf16[128,1024]{1,0:T(8,128)(2,1)S(1)}) custom-call(s32[1]{0:T(128)} %bitcast.here_ref, bf16[512,1152]{1,0:T(8,128)(2,1)S(1)} %get-tuple-element.76.band_ref, bf16[512,1024]{1,0:T(8,128)(2,1)S(1)} %get-tuple-element.88.refs_0_.own_ref, ...), custom_call_target="tpu_custom_call" | custom-call | bytes 1000 | tf_op jit(solution)/shard_map/pallas_call | solution.py:478
  110.1 1.5 %collective-permute-start.28 = (bf16[128,1024]{1,0:T(8,128)(2,1)S(1)}, bf16[128,1024]{1,0:T(8,128)(2,1)S(1)}, u32[]{:S(2)}, u32[]{:S(2)}) collective-permute-start(bf16[128,1024]{1,0:T(8,128)(2,1)S(1)} %get-tuple-element.97), channel_id=1, source_target_pairs={{0,1},{1,0},{2,3},{3,2},{4,5},{5,4},{6,7},{7,6},{8,9},{9,8},{10,11... | collective-permute-start | bytes 786440 | tf_op jit(solution)/shard_map/ppermute | solution.py:32
  111.8 1.5 %collective-permute-start.30 = (bf16[128,1024]{1,0:T(8,128)(2,1)S(1)}, bf16[128,1024]{1,0:T(8,128)(2,1)S(1)}, u32[]{:S(2)}, u32[]{:S(2)}) collective-permute-start(bf16[128,1024]{1,0:T(8,128)(2,1)S(1)} %get-tuple-element.99), channel_id=1, source_target_pairs={{0,3},{1,2},{2,1},{3,0},{4,7},{5,6},{6,5},{7,4},{8,11},{9,10},{10,... | collective-permute-start | bytes 786440 | tf_op jit(solution)/shard_map/ppermute | solution.py:32
  113.3 7.4 %collective-permute-done.26.refs_3_ = bf16[256,1024]{1,0:T(8,128)(2,1)S(1)} collective-permute-done((bf16[256,1024]{1,0:T(8,128)(2,1)S(1)}, bf16[256,1024]{1,0:T(8,128)(2,1)S(1)}, u32[]{:S(2)}, u32[]{:S(2)}) %collective-permute-start.26) | collective-permute-done | bytes 524320 | tf_op jit(solution)/shard_map/ppermute | solution.py:32
  120.7 2.9 %shard_map.82.tv_ref = f32[128,8,1024]{2,1,0:T(8,128)} custom-call(s32[1]{0:T(128)} %bitcast.here_ref, f32[128,8,1024]{2,1,0:T(8,128)} %get-tuple-element.91.tv_ref, bf16[256,1024]{1,0:T(8,128)(2,1)S(1)} %get-tuple-element.90.refs_4_.refs_0_, bf16[256,1024]{1,0:T(8,128)(2,1)S(1)} %collective-permute-done.24.refs_1_, ...), custom_call_target="tpu_custom_call", output_to_operand_aliasing={{}: (1, {})} | custom-call | bytes 1000 | tf_op jit(solution)/shard_map/pallas_call | solution.py:367
  123.6 2.6 %shard_map.83.refs_4_ = bf16[128,8,1024]{2,1,0:T(8,128)(2,1)} custom-call(s32[1]{0:T(128)} %bitcast.here_ref, bf16[128,8,512]{2,1,0:T(8,128)(2,1)S(1)} %shard_map.80.refs_1_.own_ref, bf16[128,8,512]{2,1,0:T(8,128)(2,1)S(1)} %collective-permute-done.31.above_ref, bf16[256,1024]{1,0:T(8,128)(2,1)S(1)} %get-tuple-element.90.refs_4_.refs_0_, ...), custom_call_target="tpu_custom_call" | custom-call | bytes 1000 | tf_op jit(solution)/shard_map/pallas_call | solution.py:345
  126.3 5.2 %collective-permute-done.30.refs_3_ = bf16[128,1024]{1,0:T(8,128)(2,1)S(1)} collective-permute-done((bf16[128,1024]{1,0:T(8,128)(2,1)S(1)}, bf16[128,1024]{1,0:T(8,128)(2,1)S(1)}, u32[]{:S(2)}, u32[]{:S(2)}) %collective-permute-start.30) | collective-permute-done | bytes 262176 | tf_op jit(solution)/shard_map/ppermute | solution.py:32
  131.5 2.9 %shard_map.84 = f32[128,8,1024]{2,1,0:T(8,128)} custom-call(s32[1]{0:T(128)} %bitcast.here_ref, f32[128,8,1024]{2,1,0:T(8,128)} %shard_map.82.tv_ref, bf16[128,1024]{1,0:T(8,128)(2,1)S(1)} %get-tuple-element.96.refs_4_.refs_0_, bf16[128,1024]{1,0:T(8,128)(2,1)S(1)} %collective-permute-done.28.refs_1_, ...), custom_call_target="tpu_custom_call", output_to_operand_aliasing={{}: (1, {})} | custom-call | bytes 1000 | tf_op jit(solution)/shard_map/pallas_call | solution.py:367
  (51 shorter events, 5.6 us)
Async XLA Ops:
  3.2 15.3 %collective-permute-start = (bf16[144,1024]{1,0:T(8,128)(2,1)S(1)}, bf16[144,1024]{1,0:T(8,128)(2,1)S(1)}, u32[]{:S(2)}, u32[]{:S(2)}) collective-permute-start(bf16[144,1024]{1,0:T(8,128)(2,1)S(1)} %get-tuple-element.51.refs_4_), channel_id=1, source_target_pairs={{0,1},{1,0},{2,3},{3,2},{4,5},{5,4},{6,7},{7,6},{8,9},{9,8},{10,11... | collective-permute-start | bytes 884744 | tf_op jit(solution)/shard_map/ppermute | solution.py:32
  3.2 15.3 %collective-permute-start.1 = (bf16[128,1024]{1,0:T(8,128)(2,1)}, bf16[128,1024]{1,0:T(8,128)(2,1)}, u32[]{:S(2)}, u32[]{:S(2)}) collective-permute-start(bf16[128,1024]{1,0:T(8,128)(2,1)} %get-tuple-element.53), channel_id=1, source_target_pairs={{0,2},{1,3},{2,0},{3,1},{4,6},{5,7},{6,4},{7,5},{8,10},{9,11},{10,... | collective-permute-start | bytes 786440 | tf_op jit(solution)/shard_map/ppermute | solution.py:32
  5.9 9.1 %copy-start.6 = (s32[16,6]{0,1:T(8,128)S(1)}, s32[16,6]{0,1:T(8,128)}, u32[]{:S(2)}) copy-start(s32[16,6]{0,1:T(8,128)} %param.8) | copy-start | bytes 1156
  5.9 10.0 %copy-start = (bf16[8,128,128]{2,1,0:T(8,128)(2,1)S(1)}, bf16[8,128,128]{2,1,0:T(8,128)(2,1)}, u32[]{:S(2)}) copy-start(bf16[8,128,128]{2,1,0:T(8,128)(2,1)} %refs_0_.1) | copy-start | bytes 786436
  5.9 13.3 %collective-permute-start.2 = (bf16[144,1024]{1,0:T(8,128)(2,1)S(1)}, bf16[144,1024]{1,0:T(8,128)(2,1)S(1)}, u32[]{:S(2)}, u32[]{:S(2)}) collective-permute-start(bf16[144,1024]{1,0:T(8,128)(2,1)S(1)} %get-tuple-element.54), channel_id=1, source_target_pairs={{0,3},{1,2},{2,1},{3,0},{4,7},{5,6},{6,5},{7,4},{8,11},{9,10},{10,... | collective-permute-start | bytes 884744 | tf_op jit(solution)/shard_map/ppermute | solution.py:32
  9.4 0.7 copy-start.2
  10.1 20.3 %collective-permute-start.4 = (bf16[128,8,512]{2,1,0:T(8,128)(2,1)}, bf16[128,8,512]{2,1,0:T(8,128)(2,1)S(1)}, u32[]{:S(2)}, u32[]{:S(2)}) collective-permute-start(bf16[128,8,512]{2,1,0:T(8,128)(2,1)} %get-tuple-element.59), channel_id=1, source_target_pairs={{3,7},{7,11},{11,15},{19,23},{23,27},{27,31}} | collective-permute-start | bytes 3145736 | tf_op jit(solution)/shard_map/ppermute | solution.py:27
  10.8 19.6 %collective-permute-start.5 = (bf16[256,1024]{1,0:T(8,128)(2,1)}, bf16[256,1024]{1,0:T(8,128)(2,1)}, u32[]{:S(2)}, u32[]{:S(2)}) collective-permute-start(bf16[256,1024]{1,0:T(8,128)(2,1)} %get-tuple-element.60), channel_id=1, source_target_pairs={{0,2},{1,3},{2,0},{3,1},{4,6},{5,7},{6,4},{7,5},{8,10},{9,11},{10,... | collective-permute-start | bytes 1572872 | tf_op jit(solution)/shard_map/ppermute | solution.py:32
  15.9 1.0 copy-start.3
  16.8 2.4 %copy-start.5 = (bf16[128,1024]{1,0:T(8,128)(2,1)S(1)}, bf16[128,1024]{1,0:T(8,128)(2,1)}, u32[]{:S(2)}) copy-start(bf16[128,1024]{1,0:T(8,128)(2,1)} %get-tuple-element.52.refs_0_) | copy-start | bytes 786436
  19.3 1.2 copy-start.4
  20.5 9.9 %collective-permute-start.6 = (bf16[128,1024]{1,0:T(8,128)(2,1)S(1)}, bf16[128,1024]{1,0:T(8,128)(2,1)S(1)}, u32[]{:S(2)}, u32[]{:S(2)}) collective-permute-start(bf16[128,1024]{1,0:T(8,128)(2,1)S(1)} %copy-done.4), channel_id=1, source_target_pairs={{0,1},{1,0},{2,3},{3,2},{4,5},{5,4},{6,7},{7,6},{8,9},{9,8},{10,11... | collective-permute-start | bytes 786440 | tf_op jit(solution)/shard_map/ppermute | solution.py:32
  20.7 18.3 %copy-start.1 = (bf16[128,1024]{1,0:T(8,128)(2,1)S(1)}, bf16[128,1024]{1,0:T(8,128)(2,1)}, u32[]{:S(2)}) copy-start(bf16[128,1024]{1,0:T(8,128)(2,1)} %get-tuple-element.66.refs_0_) | copy-start | bytes 786436
  20.7 26.0 %collective-permute-start.13 = (bf16[128,8,512]{2,1,0:T(8,128)(2,1)S(1)}, bf16[128,8,512]{2,1,0:T(8,128)(2,1)S(1)}, u32[]{:S(2)}, u32[]{:S(2)}) collective-permute-start(bf16[128,8,512]{2,1,0:T(8,128)(2,1)S(1)} %get-tuple-element.72), channel_id=1, source_target_pairs={{3,7},{7,11},{11,15},{19,23},{23,27},{27,31}} | collective-permute-start | bytes 3145736 | tf_op jit(solution)/shard_map/ppermute | solution.py:27
  21.6 28.1 %collective-permute-start.3 = (bf16[528,1024]{1,0:T(8,128)(2,1)S(1)}, bf16[528,1024]{1,0:T(8,128)(2,1)S(1)}, u32[]{:S(2)}, u32[]{:S(2)}) collective-permute-start(bf16[528,1024]{1,0:T(8,128)(2,1)S(1)} %get-tuple-element.57.own_ref), channel_id=1, source_target_pairs={{4,0},{5,1},{6,2},{7,3},{8,4},{9,5},{10,6},{11,7},{12,8},{13,9},{1... | collective-permute-start | bytes 3244040 | tf_op jit(solution)/shard_map/ppermute | solution.py:27
  32.2 12.9 %collective-permute-start.9 = (bf16[256,1024]{1,0:T(8,128)(2,1)S(1)}, bf16[256,1024]{1,0:T(8,128)(2,1)S(1)}, u32[]{:S(2)}, u32[]{:S(2)}) collective-permute-start(bf16[256,1024]{1,0:T(8,128)(2,1)S(1)} %get-tuple-element.65), channel_id=1, source_target_pairs={{0,2},{1,3},{2,0},{3,1},{4,6},{5,7},{6,4},{7,5},{8,10},{9,11},{10,... | collective-permute-start | bytes 1572872 | tf_op jit(solution)/shard_map/ppermute | solution.py:32
  33.5 2.3 %collective-permute-start.7 = (bf16[128,1024]{1,0:T(8,128)(2,1)S(1)}, bf16[128,1024]{1,0:T(8,128)(2,1)S(1)}, u32[]{:S(2)}, u32[]{:S(2)}) collective-permute-start(bf16[128,1024]{1,0:T(8,128)(2,1)S(1)} %get-tuple-element.62), channel_id=1, source_target_pairs={{0,1},{1,0},{2,3},{3,2},{4,5},{5,4},{6,7},{7,6},{8,9},{9,8},{10,11... | collective-permute-start | bytes 786440 | tf_op jit(solution)/shard_map/ppermute | solution.py:32
  34.7 4.4 %collective-permute-start.10 = (bf16[128,1024]{1,0:T(8,128)(2,1)S(1)}, bf16[128,1024]{1,0:T(8,128)(2,1)S(1)}, u32[]{:S(2)}, u32[]{:S(2)}) collective-permute-start(bf16[128,1024]{1,0:T(8,128)(2,1)S(1)} %get-tuple-element.67), channel_id=1, source_target_pairs={{0,1},{1,0},{2,3},{3,2},{4,5},{5,4},{6,7},{7,6},{8,9},{9,8},{10,11... | collective-permute-start | bytes 786440 | tf_op jit(solution)/shard_map/ppermute | solution.py:32
  35.8 15.7 %collective-permute-start.8 = (bf16[144,1024]{1,0:T(8,128)(2,1)S(1)}, bf16[144,1024]{1,0:T(8,128)(2,1)S(1)}, u32[]{:S(2)}, u32[]{:S(2)}) collective-permute-start(bf16[144,1024]{1,0:T(8,128)(2,1)S(1)} %get-tuple-element.63), channel_id=1, source_target_pairs={{0,4},{1,5},{2,6},{3,7},{4,8},{5,9},{6,10},{7,11},{8,12},{9,13},{1... | collective-permute-start | bytes 884744 | tf_op jit(solution)/shard_map/ppermute | solution.py:27
  40.2 10.4 %collective-permute-start.12 = (bf16[128,1024]{1,0:T(8,128)(2,1)S(1)}, bf16[128,1024]{1,0:T(8,128)(2,1)S(1)}, u32[]{:S(2)}, u32[]{:S(2)}) collective-permute-start(bf16[128,1024]{1,0:T(8,128)(2,1)S(1)} %get-tuple-element.70), channel_id=1, source_target_pairs={{0,4},{1,5},{2,6},{3,7},{4,8},{5,9},{6,10},{7,11},{8,12},{9,13},{1... | collective-permute-start | bytes 786440 | tf_op jit(solution)/shard_map/ppermute | solution.py:27
  45.1 6.4 %collective-permute-start.11 = (bf16[128,1024]{1,0:T(8,128)(2,1)S(1)}, bf16[128,1024]{1,0:T(8,128)(2,1)S(1)}, u32[]{:S(2)}, u32[]{:S(2)}) collective-permute-start(bf16[128,1024]{1,0:T(8,128)(2,1)S(1)} %slice.6), channel_id=1, source_target_pairs={{0,1},{1,0},{2,3},{3,2},{4,5},{5,4},{6,7},{7,6},{8,9},{9,8},{10,11... | collective-permute-start | bytes 786440 | tf_op jit(solution)/shard_map/ppermute | solution.py:32
  46.7 32.1 %collective-permute-start.16 = (bf16[512,1024]{1,0:T(8,128)(2,1)S(1)}, bf16[512,1024]{1,0:T(8,128)(2,1)S(1)}, u32[]{:S(2)}, u32[]{:S(2)}) collective-permute-start(bf16[512,1024]{1,0:T(8,128)(2,1)S(1)} %get-tuple-element.68.refs_0_.own_ref), channel_id=1, source_target_pairs={{4,0},{5,1},{6,2},{7,3},{8,4},{9,5},{10,6},{11,7},{12,8},{13,9},{1... | collective-permute-start | bytes 3145736 | tf_op jit(solution)/shard_map/ppermute | solution.py:27
  49.7 4.0 %collective-permute-start.17 = (bf16[128,1024]{1,0:T(8,128)(2,1)S(1)}, bf16[128,1024]{1,0:T(8,128)(2,1)S(1)}, u32[]{:S(2)}, u32[]{:S(2)}) collective-permute-start(bf16[128,1024]{1,0:T(8,128)(2,1)S(1)} %get-tuple-element.78), channel_id=1, source_target_pairs={{0,1},{1,0},{2,3},{3,2},{4,5},{5,4},{6,7},{7,6},{8,9},{9,8},{10,11... | collective-permute-start | bytes 786440 | tf_op jit(solution)/shard_map/ppermute | solution.py:32
  50.6 19.4 %collective-permute-start.18 = (bf16[256,1024]{1,0:T(8,128)(2,1)S(1)}, bf16[256,1024]{1,0:T(8,128)(2,1)S(1)}, u32[]{:S(2)}, u32[]{:S(2)}) collective-permute-start(bf16[256,1024]{1,0:T(8,128)(2,1)S(1)} %get-tuple-element.79), channel_id=1, source_target_pairs={{0,2},{1,3},{2,0},{3,1},{4,6},{5,7},{6,4},{7,5},{8,10},{9,11},{10,... | collective-permute-start | bytes 1572872 | tf_op jit(solution)/shard_map/ppermute | solution.py:32
  53.7 17.0 %collective-permute-start.20 = (bf16[128,1024]{1,0:T(8,128)(2,1)S(1)}, bf16[128,1024]{1,0:T(8,128)(2,1)S(1)}, u32[]{:S(2)}, u32[]{:S(2)}) collective-permute-start(bf16[128,1024]{1,0:T(8,128)(2,1)S(1)} %get-tuple-element.83), channel_id=1, source_target_pairs={{0,1},{1,0},{2,3},{3,2},{4,5},{5,4},{6,7},{7,6},{8,9},{9,8},{10,11... | collective-permute-start | bytes 786440 | tf_op jit(solution)/shard_map/ppermute | solution.py:32
  54.6 35.8 %collective-permute-start.14 = (bf16[512,1024]{1,0:T(8,128)(2,1)S(1)}, bf16[512,1024]{1,0:T(8,128)(2,1)S(1)}, u32[]{:S(2)}, u32[]{:S(2)}) collective-permute-start(bf16[512,1024]{1,0:T(8,128)(2,1)S(1)} %get-tuple-element.74.refs_0_.own_ref), channel_id=1, source_target_pairs={{0,4},{1,5},{2,6},{3,7},{4,8},{5,9},{6,10},{7,11},{8,12},{9,13},{1... | collective-permute-start | bytes 3145736 | tf_op jit(solution)/shard_map/ppermute | solution.py:27
  58.7 12.1 %collective-permute-start.21 = (bf16[128,1024]{1,0:T(8,128)(2,1)S(1)}, bf16[128,1024]{1,0:T(8,128)(2,1)S(1)}, u32[]{:S(2)}, u32[]{:S(2)}) collective-permute-start(bf16[128,1024]{1,0:T(8,128)(2,1)S(1)} %get-tuple-element.85), channel_id=1, source_target_pairs={{0,2},{1,3},{2,0},{3,1},{4,6},{5,7},{6,4},{7,5},{8,10},{9,11},{10,... | collective-permute-start | bytes 786440 | tf_op jit(solution)/shard_map/ppermute | solution.py:32
  70.0 8.8 %collective-permute-start.22 = (bf16[128,1024]{1,0:T(8,128)(2,1)S(1)}, bf16[128,1024]{1,0:T(8,128)(2,1)S(1)}, u32[]{:S(2)}, u32[]{:S(2)}) collective-permute-start(bf16[128,1024]{1,0:T(8,128)(2,1)S(1)} %get-tuple-element.87), channel_id=1, source_target_pairs={{0,3},{1,2},{2,1},{3,0},{4,7},{5,6},{6,5},{7,4},{8,11},{9,10},{10,... | collective-permute-start | bytes 786440 | tf_op jit(solution)/shard_map/ppermute | solution.py:32
  70.8 8.1 %collective-permute-start.19 = (bf16[128,1024]{1,0:T(8,128)(2,1)S(1)}, bf16[128,1024]{1,0:T(8,128)(2,1)S(1)}, u32[]{:S(2)}, u32[]{:S(2)}) collective-permute-start(bf16[128,1024]{1,0:T(8,128)(2,1)S(1)} %slice.7), channel_id=1, source_target_pairs={{0,1},{1,0},{2,3},{3,2},{4,5},{5,4},{6,7},{7,6},{8,9},{9,8},{10,11... | collective-permute-start | bytes 786440 | tf_op jit(solution)/shard_map/ppermute | solution.py:32
  70.9 15.4 %collective-permute-start.15 = (bf16[128,1024]{1,0:T(8,128)(2,1)S(1)}, bf16[128,1024]{1,0:T(8,128)(2,1)S(1)}, u32[]{:S(2)}, u32[]{:S(2)}) collective-permute-start(bf16[128,1024]{1,0:T(8,128)(2,1)S(1)} %get-tuple-element.77), channel_id=1, source_target_pairs={{4,0},{5,1},{6,2},{7,3},{8,4},{9,5},{10,6},{11,7},{12,8},{13,9},{1... | collective-permute-start | bytes 786440 | tf_op jit(solution)/shard_map/ppermute | solution.py:27
  80.9 9.5 %collective-permute-start.23 = (bf16[128,1024]{1,0:T(8,128)(2,1)S(1)}, bf16[128,1024]{1,0:T(8,128)(2,1)S(1)}, u32[]{:S(2)}, u32[]{:S(2)}) collective-permute-start(bf16[128,1024]{1,0:T(8,128)(2,1)S(1)} %get-tuple-element.89), channel_id=1, source_target_pairs={{4,0},{5,1},{6,2},{7,3},{8,4},{9,5},{10,6},{11,7},{12,8},{13,9},{1... | collective-permute-start | bytes 786440 | tf_op jit(solution)/shard_map/ppermute | solution.py:27
  82.2 25.9 %collective-permute-start.27 = (bf16[512,1024]{1,0:T(8,128)(2,1)S(1)}, bf16[512,1024]{1,0:T(8,128)(2,1)S(1)}, u32[]{:S(2)}, u32[]{:S(2)}) collective-permute-start(bf16[512,1024]{1,0:T(8,128)(2,1)S(1)} %get-tuple-element.88.refs_0_.own_ref), channel_id=1, source_target_pairs={{0,4},{1,5},{2,6},{3,7},{4,8},{5,9},{6,10},{7,11},{8,12},{9,13},{1... | collective-permute-start | bytes 3145736 | tf_op jit(solution)/shard_map/ppermute | solution.py:27
  93.4 30.2 %collective-permute-start.31 = (bf16[128,8,512]{2,1,0:T(8,128)(2,1)S(1)}, bf16[128,8,512]{2,1,0:T(8,128)(2,1)S(1)}, u32[]{:S(2)}, u32[]{:S(2)}) collective-permute-start(bf16[128,8,512]{2,1,0:T(8,128)(2,1)S(1)} %shard_map.80.refs_1_.own_ref), channel_id=1, source_target_pairs={{7,3},{11,7},{15,11},{23,19},{27,23},{31,27}} | collective-permute-start | bytes 3145736 | tf_op jit(solution)/shard_map/ppermute | solution.py:27
  94.2 17.4 %collective-permute-start.24 = (bf16[256,1024]{1,0:T(8,128)(2,1)S(1)}, bf16[256,1024]{1,0:T(8,128)(2,1)S(1)}, u32[]{:S(2)}, u32[]{:S(2)}) collective-permute-start(bf16[256,1024]{1,0:T(8,128)(2,1)S(1)} %get-tuple-element.92), channel_id=1, source_target_pairs={{0,1},{1,0},{2,3},{3,2},{4,5},{5,4},{6,7},{7,6},{8,9},{9,8},{10,11... | collective-permute-start | bytes 1572872 | tf_op jit(solution)/shard_map/ppermute | solution.py:32
  95.3 16.5 %collective-permute-start.25 = (bf16[256,1024]{1,0:T(8,128)(2,1)S(1)}, bf16[256,1024]{1,0:T(8,128)(2,1)S(1)}, u32[]{:S(2)}, u32[]{:S(2)}) collective-permute-start(bf16[256,1024]{1,0:T(8,128)(2,1)S(1)} %get-tuple-element.93), channel_id=1, source_target_pairs={{0,2},{1,3},{2,0},{3,1},{4,6},{5,7},{6,4},{7,5},{8,10},{9,11},{10,... | collective-permute-start | bytes 1572872 | tf_op jit(solution)/shard_map/ppermute | solution.py:32
  95.6 25.1 %collective-permute-start.26 = (bf16[256,1024]{1,0:T(8,128)(2,1)S(1)}, bf16[256,1024]{1,0:T(8,128)(2,1)S(1)}, u32[]{:S(2)}, u32[]{:S(2)}) collective-permute-start(bf16[256,1024]{1,0:T(8,128)(2,1)S(1)} %get-tuple-element.94), channel_id=1, source_target_pairs={{0,3},{1,2},{2,1},{3,0},{4,7},{5,6},{6,5},{7,4},{8,11},{9,10},{10,... | collective-permute-start | bytes 1572872 | tf_op jit(solution)/shard_map/ppermute | solution.py:32
  110.1 16.2 %collective-permute-start.28 = (bf16[128,1024]{1,0:T(8,128)(2,1)S(1)}, bf16[128,1024]{1,0:T(8,128)(2,1)S(1)}, u32[]{:S(2)}, u32[]{:S(2)}) collective-permute-start(bf16[128,1024]{1,0:T(8,128)(2,1)S(1)} %get-tuple-element.97), channel_id=1, source_target_pairs={{0,1},{1,0},{2,3},{3,2},{4,5},{5,4},{6,7},{7,6},{8,9},{9,8},{10,11... | collective-permute-start | bytes 786440 | tf_op jit(solution)/shard_map/ppermute | solution.py:32
  111.6 14.7 %collective-permute-start.29 = (bf16[128,1024]{1,0:T(8,128)(2,1)S(1)}, bf16[128,1024]{1,0:T(8,128)(2,1)S(1)}, u32[]{:S(2)}, u32[]{:S(2)}) collective-permute-start(bf16[128,1024]{1,0:T(8,128)(2,1)S(1)} %get-tuple-element.98), channel_id=1, source_target_pairs={{0,2},{1,3},{2,0},{3,1},{4,6},{5,7},{6,4},{7,5},{8,10},{9,11},{10,... | collective-permute-start | bytes 786440 | tf_op jit(solution)/shard_map/ppermute | solution.py:32
  111.8 19.6 %collective-permute-start.30 = (bf16[128,1024]{1,0:T(8,128)(2,1)S(1)}, bf16[128,1024]{1,0:T(8,128)(2,1)S(1)}, u32[]{:S(2)}, u32[]{:S(2)}) collective-permute-start(bf16[128,1024]{1,0:T(8,128)(2,1)S(1)} %get-tuple-element.99), channel_id=1, source_target_pairs={{0,3},{1,2},{2,1},{3,0},{4,7},{5,6},{6,5},{7,4},{8,11},{9,10},{10,... | collective-permute-start | bytes 786440 | tf_op jit(solution)/shard_map/ppermute | solution.py:32

commit v16 on v14

--- a/solution.py
+++ b/solution.py
@@ -363,16 +363,19 @@
 def finish(here, chunk, tv, pieces, *tokens):
     depth, rows, cols = tv.shape
     first, count = chunk_tiles(chunk, cols)
-    part = pl.BlockSpec((depth, rows, TILE), lambda i: (0, 0, first + i))
+    cuts = 2
+    deep = depth // cuts
+    part = pl.BlockSpec((deep, rows, TILE), lambda i, z: (z, 0, first + i))
+    blocks = [pl.BlockSpec((deep, ROWS * TILE), lambda i, z, at=at: (at * cuts + z, i)) for _, at in pieces]
     return call(
         finish_kernel,
         0,
-        grid=(count,),
-        in_specs=[SMEM, part] + piece_specs(pieces, depth, ROWS * TILE) + [ANY] * len(tokens),
+        grid=(count, cuts),
+        in_specs=[SMEM, part] + blocks + [ANY] * len(tokens),
         out_specs=part,
         results=pltpu.HBM(tv.shape, F32),
         input_output_aliases={1: 0},
-        scratch_shapes=[wide_tile(depth * rows)],
+        scratch_shapes=[wide_tile(deep * rows)],
     )(here, far(tv), *arrays_of(pieces), *tokens)
 
 
@@ -581,16 +584,16 @@
     low0 = moved(tied(edge0, s_near), G)
     own1, edge1 = pack(here, [(v0, 0), (near, 0), (over, 0), (swapped(over_beyond, 1), 0)], 0)
     low1, high1 = moved(edge1, G), moved(own1, -G)
-    sinos0 = [(s0, 0), (s_near, 0), (s_over, 0), (beyond(s_over, own1), 0)]
-
-    s0, s1, s23 = split_rows(here, sinogram, got1, 1, paired, [], own1)
-
-    resid0, down0, r1, r23 = project(here, band_p, own0, high0, low0, sinos0, paired[1:], low1, s0)
+    t0, t1, t23 = split_rows(here, sinogram, got1, 1, paired, [], own1)
+    sinos0 = [(s0, 0), (s_near, 0), (s_over, 0), (beyond(s_over, t0), 0)]
+
+
+    resid0, down0, r1, r23 = project(here, band_p, own0, high0, low0, sinos0, paired[1:], low1)
     from_low0, from_high0 = moved(resid0, G), moved(down0, -G)
-    s_near, s_over = swapped(s1, 1), swapped(s23, 2)
-    r_near, r_over = swapped(tied(r1, s_near), 1), swapped(tied(r23, s_near), 2)
+    t_near, t_over = swapped(t1, 1), swapped(t23, 2)
+    r_near, r_over = swapped(tied(r1, t_near), 1), swapped(tied(r23, t_near), 2)
     tv, tv_done = half_tv(here, volume, [got_vols0[1], high0, got_vols0[3], low0], resid0)
-    sinos1 = [(s0, 0), (s_near, 0), (s_over, 0), (beyond(s_over, tv_done), 0)]
+    sinos1 = [(t0, 0), (t_near, 0), (t_over, 0), (beyond(t_over, tv_done), 0)]
     resid1, down1 = project(here, band_p, own1, high1, low1, sinos1, (), tv_done, r_near, r_over)
     from_low1, from_high1 = moved(resid1, G), moved(down1, -G)
 

time: 131 us -> 135 us (1.031)
  waiting for transfers between devices: 34.8 us -> 40.3 us
  starting transfers between devices: 49.8 us -> 45.7 us
  Pallas kernels: 42.3 us -> 44.5 us
    ppermute x11, waiting for transfers between devices: 10.2 us -> 15 us  [moved(): return lax.ppermute(value, 'slab', pairs)]
    ppermute x21, starting transfers between devices: 27 us -> 24.6 us  [swapped(): return lax.ppermute(value, 'slab', [(i, i ^ bits) for i in range(count)])]
    pallas_call x2, Pallas kernels: 5.85 us -> 8.07 us  [finish(): call(finish_kernel, 0, grid=(count, cuts), in_specs=[SMEM, part] + blocks...]
    ppermute x11, starting transfers between devices: 22.8 us -> 21.1 us  [moved(): return lax.ppermute(value, 'slab', pairs)]
where the time goes in v16:
time: 135 us; the launch traced here: 134 us
  starting transfers between devices  45.7 us (34%)
  Pallas kernels  44.5 us (33%)
  waiting for transfers between devices  40.3 us (30%)
  local copies, waits for them, and re-layouts  2.57 us (2%)
    ppermute x21, waiting for transfers between devices, swapped(): return lax.ppermute(value, 'slab', [(i, i ^ bits) for i in range(count)])  25.3 us
    ppermute x21, starting transfers between devices, swapped(): return lax.ppermute(value, 'slab', [(i, i ^ bits) for i in range(count)])  24.6 us
    ppermute x11, starting transfers between devices, moved(): return lax.ppermute(value, 'slab', pairs)  21.1 us
    ppermute x11, waiting for transfers between devices, moved(): return lax.ppermute(value, 'slab', pairs)  15 us
    pallas_call x1, Pallas kernels, half_tv(): call(tv_kernel, 0, grid=(depth // deep,), in_specs=[SMEM] + edges + [afte...  9.99 us
    pallas_call x2, Pallas kernels, finish(): call(finish_kernel, 0, grid=(count, cuts), in_specs=[SMEM, part] + blocks...  8.07 us
    pallas_call x2, Pallas kernels, cast_rows(): call(functools.partial(cast_kernel, groups, len(edges), halves), 2, grid=...  5.97 us
    pallas_call x2, Pallas kernels, project(): call(functools.partial(project_kernel, groups), 3, grid=(cols // tile,),...  4.22 us
  transfers between devices with their start and end apart: 32, of which 11 were waited for; matrix products, arithmetic and copies ran while one was open for 1% of the time, Pallas kernels for 28%

profile of v16, /device:TPU:1, one launch (start us, length us, event | category | flops | bytes accessed | tf_op | source)
XLA Modules:
  0.0 134.0 jit_solution(3994473352029702734)
XLA Ops:
  0.6 2.5 %shard_map.68 = (bf16[128,1024]{1,0:T(8,128)(2,1)}, bf16[144,1024]{1,0:T(8,128)(2,1)S(1)}, bf16[128,1024]{1,0:T(8,128)(2,1)}, bf16[144,1024]{1,0:T(8,128)(2,1)S(1)}) custom-call(s32[1]{0:T(128)} %bitcast.here_ref, f32[1024,1024]{1,0:T(8,128)} %bitcast.2, f32[1024,1024]{1,0:T(8,128)} %bitcast.3, f32[1024,1024]{1,0:T(8,128)} %bitcast.4, f32[1024,1024]{1,0:T(8,128)} %bitcast.5), custom_call_target="tpu_custom_call" | custom-call | flops 2300000000 | bytes 1000 | tf_op jit(solution)/shard_map/pallas_call | solution.py:115
  3.2 2.7 %collective-permute-start.1 = (bf16[128,1024]{1,0:T(8,128)(2,1)}, bf16[128,1024]{1,0:T(8,128)(2,1)}, u32[]{:S(2)}, u32[]{:S(2)}) collective-permute-start(bf16[128,1024]{1,0:T(8,128)(2,1)} %get-tuple-element.52), channel_id=1, source_target_pairs={{0,2},{1,3},{2,0},{3,1},{4,6},{5,7},{6,4},{7,5},{8,10},{9,11},{10,... | collective-permute-start | bytes 786440 | tf_op jit(solution)/shard_map/ppermute | solution.py:32
  6.0 3.4 %shard_map.69 = (bf16[128,1024]{1,0:T(8,128)(2,1)}, bf16[128,1024]{1,0:T(8,128)(2,1)S(1)}, bf16[256,1024]{1,0:T(8,128)(2,1)}, bf16[128,8,512]{2,1,0:T(8,128)(2,1)}, bf16[128,8,512]{2,1,0:T(8,128)(2,1)S(1)}) custom-call(s32[1]{0:T(128)} %bitcast.here_ref, f32[1024,1024]{1,0:T(8,128)} %bitcast.6, f32[1024,1024]{1,0:T(8,128)} %bitcast.7, ...), custom_call_target="tpu_custom_call" | custom-call | flops 2300000000 | bytes 1000 | tf_op jit(solution)/shard_map/pallas_call | solution.py:115
  10.8 4.2 %collective-permute-start.5 = (bf16[256,1024]{1,0:T(8,128)(2,1)}, bf16[256,1024]{1,0:T(8,128)(2,1)}, u32[]{:S(2)}, u32[]{:S(2)}) collective-permute-start(bf16[256,1024]{1,0:T(8,128)(2,1)} %get-tuple-element.59), channel_id=1, source_target_pairs={{0,2},{1,3},{2,0},{3,1},{4,6},{5,7},{6,4},{7,5},{8,10},{9,11},{10,... | collective-permute-start | bytes 1572872 | tf_op jit(solution)/shard_map/ppermute | solution.py:32
  15.1 0.8 copy.13.offset_ref
  15.9 0.9 copy-done.3
  16.8 1.6 %shard_map.70 = (bf16[512,1152]{1,0:T(8,128)(2,1)S(1)}, bf16[512,1152]{1,0:T(8,128)(2,1)S(1)}) custom-call(s32[1]{0:T(128)} %bitcast.here_ref, s32[16,6]{1,0:T(8,128)S(1)} %copy.12.cover_ref, s32[16,6]{1,0:T(8,128)S(1)} %copy.13.offset_ref, bf16[8,128,128]{2,1,0:T(8,128)(2,1)S(1)} %copy-done, bf16[128,1024]{1,0:T(8,128)(2,1)S(1)} %copy-done.3), custom_call_target="tpu_custom_call" | custom-call | flops 10350000128 | bytes 1000 | tf_op jit(solution)/shard_map/pallas_call | solution.py:418
  18.5 0.8 collective-permute-done.2.refs_3_.far_ref
  19.3 1.2 shard_map.71
  20.5 0.9 collective-permute-start.10
  21.6 1.3 collective-permute-start.3
  22.9 7.5 %collective-permute-done.5.refs_0_.refs_2_ = bf16[256,1024]{1,0:T(8,128)(2,1)} collective-permute-done((bf16[256,1024]{1,0:T(8,128)(2,1)}, bf16[256,1024]{1,0:T(8,128)(2,1)}, u32[]{:S(2)}, u32[]{:S(2)}) %collective-permute-start.5) | collective-permute-done | bytes 524320 | tf_op jit(solution)/shard_map/ppermute | solution.py:32
  30.4 1.8 %shard_map.72 = (bf16[128,1024]{1,0:T(8,128)(2,1)S(1)}, bf16[128,1024]{1,0:T(8,128)(2,1)S(1)}, bf16[256,1024]{1,0:T(8,128)(2,1)S(1)}, bf16[128,1024]{1,0:T(8,128)(2,1)S(1)}) custom-call(s32[1]{0:T(128)} %bitcast.here_ref, bf16[128,8,1024]{2,1,0:T(8,128)(2,1)} %refs_2_.3, bf16[128,8,512]{2,1,0:T(8,128)(2,1)S(1)} %collective-permute-done.4.got_ref, ...), custom_call_target="tpu_custom_call" | custom-call | flops 2300000000 | bytes 1000 | tf_op jit(solution)/shard_map/pallas_call | solution.py:196
  33.0 1.5 %collective-permute-start.9 = (bf16[256,1024]{1,0:T(8,128)(2,1)S(1)}, bf16[256,1024]{1,0:T(8,128)(2,1)S(1)}, u32[]{:S(2)}, u32[]{:S(2)}) collective-permute-start(bf16[256,1024]{1,0:T(8,128)(2,1)S(1)} %get-tuple-element.64), channel_id=1, source_target_pairs={{0,2},{1,3},{2,0},{3,1},{4,6},{5,7},{6,4},{7,5},{8,10},{9,11},{10,... | collective-permute-start | bytes 1572872 | tf_op jit(solution)/shard_map/ppermute | solution.py:32
  34.5 3.2 %collective-permute-start.8 = (bf16[144,1024]{1,0:T(8,128)(2,1)S(1)}, bf16[144,1024]{1,0:T(8,128)(2,1)S(1)}, u32[]{:S(2)}, u32[]{:S(2)}) collective-permute-start(bf16[144,1024]{1,0:T(8,128)(2,1)S(1)} %get-tuple-element.62), channel_id=1, source_target_pairs={{0,4},{1,5},{2,6},{3,7},{4,8},{5,9},{6,10},{7,11},{8,12},{9,13},{1... | collective-permute-start | bytes 884744 | tf_op jit(solution)/shard_map/ppermute | solution.py:27
  37.7 1.2 shard_map.73
  38.9 3.2 %collective-permute-start.13 = (bf16[128,1024]{1,0:T(8,128)(2,1)S(1)}, bf16[128,1024]{1,0:T(8,128)(2,1)S(1)}, u32[]{:S(2)}, u32[]{:S(2)}) collective-permute-start(bf16[128,1024]{1,0:T(8,128)(2,1)S(1)} %get-tuple-element.72), channel_id=1, source_target_pairs={{0,4},{1,5},{2,6},{3,7},{4,8},{5,9},{6,10},{7,11},{8,12},{9,13},{1... | collective-permute-start | bytes 786440 | tf_op jit(solution)/shard_map/ppermute | solution.py:27
  42.1 1.7 %shard_map.74 = (bf16[128,1024]{1,0:T(8,128)(2,1)S(1)}, bf16[128,1024]{1,0:T(8,128)(2,1)S(1)}, bf16[256,1024]{1,0:T(8,128)(2,1)S(1)}) custom-call(s32[1]{0:T(128)} %bitcast.here_ref, bf16[128,8,1024]{2,1,0:T(8,128)(2,1)} %refs_2_.3, bf16[128,8,512]{2,1,0:T(8,128)(2,1)S(1)} %collective-permute-done.10.got_ref, ...), custom_call_target="tpu_custom_call" | custom-call | flops 2300000000 | bytes 1000 | tf_op jit(solution)/shard_map/pallas_call | solution.py:196
  43.8 2.2 %collective-permute-done.9.refs_2_ = bf16[256,1024]{1,0:T(8,128)(2,1)S(1)} collective-permute-done((bf16[256,1024]{1,0:T(8,128)(2,1)S(1)}, bf16[256,1024]{1,0:T(8,128)(2,1)S(1)}, u32[]{:S(2)}, u32[]{:S(2)}) %collective-permute-start.9) | collective-permute-done | bytes 524320 | tf_op jit(solution)/shard_map/ppermute | solution.py:32
  46.1 1.3 collective-permute-start.12
  47.4 1.3 collective-permute-start.16
  48.9 1.0 collective-permute-start.17
  49.9 3.9 %collective-permute-start.18 = (bf16[256,1024]{1,0:T(8,128)(2,1)S(1)}, bf16[256,1024]{1,0:T(8,128)(2,1)S(1)}, u32[]{:S(2)}, u32[]{:S(2)}) collective-permute-start(bf16[256,1024]{1,0:T(8,128)(2,1)S(1)} %get-tuple-element.78), channel_id=1, source_target_pairs={{0,2},{1,3},{2,0},{3,1},{4,6},{5,7},{6,4},{7,5},{8,10},{9,11},{10,... | collective-permute-start | bytes 1572872 | tf_op jit(solution)/shard_map/ppermute | solution.py:32
  53.8 2.1 %shard_map.75 = (bf16[512,1024]{1,0:T(8,128)(2,1)S(1)}, bf16[128,1024]{1,0:T(8,128)(2,1)S(1)}, bf16[128,1024]{1,0:T(8,128)(2,1)S(1)}, bf16[256,1024]{1,0:T(8,128)(2,1)S(1)}) custom-call(s32[1]{0:T(128)} %bitcast.here_ref, bf16[512,1152]{1,0:T(8,128)(2,1)S(1)} %get-tuple-element.55.refs_4_.band_ref, bf16[528,1024]{1,0:T(8,128)(2,1)S(1)} %get-tuple-element.56.own_ref, ...), custom_call_target="tpu_custom_call" | custom-call | flops 3449999872 | bytes 1000 | tf_op jit(solution)/shard_map/pallas_call | solution.py:449
  56.1 3.2 %collective-permute-start.14 = (bf16[512,1024]{1,0:T(8,128)(2,1)S(1)}, bf16[512,1024]{1,0:T(8,128)(2,1)S(1)}, u32[]{:S(2)}, u32[]{:S(2)}) collective-permute-start(bf16[512,1024]{1,0:T(8,128)(2,1)S(1)} %get-tuple-element.73.refs_0_.own_ref), channel_id=1, source_target_pairs={{0,4},{1,5},{2,6},{3,7},{4,8},{5,9},{6,10},{7,11},{8,12},{9,13},{1... | collective-permute-start | bytes 3145736 | tf_op jit(solution)/shard_map/ppermute | solution.py:27
  59.9 10.0 %shard_map.76 = (f32[128,8,1024]{2,1,0:T(8,128)}, f32[8,128]{1,0:T(8,128)S(1)}) custom-call(s32[1]{0:T(128)} %bitcast.here_ref, bf16[144,1024]{1,0:T(8,128)(2,1)S(1)} %collective-permute-done.refs_1_.near_ref, bf16[528,1024]{1,0:T(8,128)(2,1)S(1)} %collective-permute-done.3.high_ref.next_level_ref, ...), custom_call_target="tpu_custom_call" | custom-call | bytes 1000 | tf_op jit(solution)/shard_map/pallas_call | solution.py:549
  70.0 1.3 collective-permute-start.15
  71.5 2.7 %collective-permute-done.16.high_ref = bf16[512,1024]{1,0:T(8,128)(2,1)S(1)} collective-permute-done((bf16[512,1024]{1,0:T(8,128)(2,1)S(1)}, bf16[512,1024]{1,0:T(8,128)(2,1)S(1)}, u32[]{:S(2)}, u32[]{:S(2)}) %collective-permute-start.16) | collective-permute-done | bytes 1048608 | tf_op jit(solution)/shard_map/ppermute | solution.py:27
  74.2 3.1 %collective-permute-done.21.refs_6_.refs_2_ = bf16[256,1024]{1,0:T(8,128)(2,1)S(1)} collective-permute-done((bf16[256,1024]{1,0:T(8,128)(2,1)S(1)}, bf16[256,1024]{1,0:T(8,128)(2,1)S(1)}, u32[]{:S(2)}, u32[]{:S(2)}) %collective-permute-start.21) | collective-permute-done | bytes 524320 | tf_op jit(solution)/shard_map/ppermute | solution.py:32
  77.3 2.1 %shard_map.77 = (bf16[512,1024]{1,0:T(8,128)(2,1)S(1)}, bf16[128,1024]{1,0:T(8,128)(2,1)S(1)}) custom-call(s32[1]{0:T(128)} %bitcast.here_ref, bf16[512,1152]{1,0:T(8,128)(2,1)S(1)} %get-tuple-element.55.refs_4_.band_ref, bf16[512,1024]{1,0:T(8,128)(2,1)S(1)} %get-tuple-element.69.refs_0_.own_ref, bf16[512,1024]{1,0:T(8,128)(2,1)S(1)} %collective-permute-done.16.high_ref, ...), custom_call_target="tpu_custom_call" | custom-call | flops 3449999872 | bytes 1000 | tf_op jit(solution)/shard_map/pallas_call | solution.py:449
  79.4 1.3 collective-permute-start.22
  80.7 4.1 %collective-permute-start.26 = (bf16[512,1024]{1,0:T(8,128)(2,1)S(1)}, bf16[512,1024]{1,0:T(8,128)(2,1)S(1)}, u32[]{:S(2)}, u32[]{:S(2)}) collective-permute-start(bf16[512,1024]{1,0:T(8,128)(2,1)S(1)} %get-tuple-element.85.refs_0_.own_ref), channel_id=1, source_target_pairs={{0,4},{1,5},{2,6},{3,7},{4,8},{5,9},{6,10},{7,11},{8,12},{9,13},{1... | collective-permute-start | bytes 3145736 | tf_op jit(solution)/shard_map/ppermute | solution.py:27
  84.8 1.2 collective-permute-start.27
  86.0 2.6 %collective-permute-done.22.refs_1_.high_ref = bf16[128,1024]{1,0:T(8,128)(2,1)S(1)} collective-permute-done((bf16[128,1024]{1,0:T(8,128)(2,1)S(1)}, bf16[128,1024]{1,0:T(8,128)(2,1)S(1)}, u32[]{:S(2)}, u32[]{:S(2)}) %collective-permute-start.22) | collective-permute-done | bytes 262176 | tf_op jit(solution)/shard_map/ppermute | solution.py:27
  88.6 2.1 %shard_map.78 = (bf16[256,1024]{1,0:T(8,128)(2,1)S(1)}, bf16[256,1024]{1,0:T(8,128)(2,1)S(1)}, bf16[256,1024]{1,0:T(8,128)(2,1)S(1)}, bf16[256,1024]{1,0:T(8,128)(2,1)S(1)}) custom-call(s32[1]{0:T(128)} %bitcast.here_ref, bf16[512,1152]{1,0:T(8,128)(2,1)S(1)} %get-tuple-element.75.band_ref, bf16[512,1024]{1,0:T(8,128)(2,1)S(1)} %get-tuple-element.73.refs_0_.own_ref, ...), custom_call_target="tpu_custom_call" | custom-call | bytes 1000 | tf_op jit(solution)/shard_map/pallas_call | solution.py:481
  90.8 0.9 shard_map.80.refs_1_.own_ref
  92.4 1.5 %collective-permute-start.23 = (bf16[256,1024]{1,0:T(8,128)(2,1)S(1)}, bf16[256,1024]{1,0:T(8,128)(2,1)S(1)}, u32[]{:S(2)}, u32[]{:S(2)}) collective-permute-start(bf16[256,1024]{1,0:T(8,128)(2,1)S(1)} %get-tuple-element.89), channel_id=1, source_target_pairs={{0,1},{1,0},{2,3},{3,2},{4,5},{5,4},{6,7},{7,6},{8,9},{9,8},{10,11... | collective-permute-start | bytes 1572872 | tf_op jit(solution)/shard_map/ppermute | solution.py:32
  93.9 1.3 collective-permute-start.24
  95.6 1.2 shard_map.79
  96.7 9.6 %collective-permute-done.26.low_ref = bf16[512,1024]{1,0:T(8,128)(2,1)S(1)} collective-permute-done((bf16[512,1024]{1,0:T(8,128)(2,1)S(1)}, bf16[512,1024]{1,0:T(8,128)(2,1)S(1)}, u32[]{:S(2)}, u32[]{:S(2)}) %collective-permute-start.26) | collective-permute-done | bytes 1048608 | tf_op jit(solution)/shard_map/ppermute | solution.py:27
  106.3 1.9 %shard_map.81 = (bf16[128,1024]{1,0:T(8,128)(2,1)S(1)}, bf16[128,1024]{1,0:T(8,128)(2,1)S(1)}, bf16[128,1024]{1,0:T(8,128)(2,1)S(1)}, bf16[128,1024]{1,0:T(8,128)(2,1)S(1)}) custom-call(s32[1]{0:T(128)} %bitcast.here_ref, bf16[512,1152]{1,0:T(8,128)(2,1)S(1)} %get-tuple-element.75.band_ref, bf16[512,1024]{1,0:T(8,128)(2,1)S(1)} %get-tuple-element.85.refs_0_.own_ref, ...), custom_call_target="tpu_custom_call" | custom-call | bytes 1000 | tf_op jit(solution)/shard_map/pallas_call | solution.py:481
  108.3 1.8 %collective-permute-start.28 = (bf16[128,1024]{1,0:T(8,128)(2,1)S(1)}, bf16[128,1024]{1,0:T(8,128)(2,1)S(1)}, u32[]{:S(2)}, u32[]{:S(2)}) collective-permute-start(bf16[128,1024]{1,0:T(8,128)(2,1)S(1)} %get-tuple-element.95), channel_id=1, source_target_pairs={{0,1},{1,0},{2,3},{3,2},{4,5},{5,4},{6,7},{7,6},{8,9},{9,8},{10,11... | collective-permute-start | bytes 786440 | tf_op jit(solution)/shard_map/ppermute | solution.py:32
  110.1 1.3 collective-permute-start.29
  111.8 7.4 %collective-permute-done.25.refs_3_ = bf16[256,1024]{1,0:T(8,128)(2,1)S(1)} collective-permute-done((bf16[256,1024]{1,0:T(8,128)(2,1)S(1)}, bf16[256,1024]{1,0:T(8,128)(2,1)S(1)}, u32[]{:S(2)}, u32[]{:S(2)}) %collective-permute-start.25) | collective-permute-done | bytes 524320 | tf_op jit(solution)/shard_map/ppermute | solution.py:32
  119.2 4.0 %shard_map.82.tv_ref = f32[128,8,1024]{2,1,0:T(8,128)} custom-call(s32[1]{0:T(128)} %bitcast.here_ref, f32[128,8,1024]{2,1,0:T(8,128)} %get-tuple-element.88.tv_ref, bf16[256,1024]{1,0:T(8,128)(2,1)S(1)} %get-tuple-element.87.refs_4_.refs_0_, bf16[256,1024]{1,0:T(8,128)(2,1)S(1)} %collective-permute-done.23.refs_1_, ...), custom_call_target="tpu_custom_call", output_to_operand_aliasing={{}: (1, {})} | custom-call | bytes 1000 | tf_op jit(solution)/shard_map/pallas_call | solution.py:370
  123.3 2.6 %shard_map.83.refs_4_ = bf16[128,8,1024]{2,1,0:T(8,128)(2,1)} custom-call(s32[1]{0:T(128)} %bitcast.here_ref, bf16[128,8,512]{2,1,0:T(8,128)(2,1)S(1)} %shard_map.80.refs_1_.own_ref, bf16[128,8,512]{2,1,0:T(8,128)(2,1)S(1)} %collective-permute-done.31.above_ref, bf16[256,1024]{1,0:T(8,128)(2,1)S(1)} %get-tuple-element.87.refs_4_.refs_0_, ...), custom_call_target="tpu_custom_call" | custom-call | bytes 1000 | tf_op jit(solution)/shard_map/pallas_call | solution.py:345
  125.9 4.1 %collective-permute-done.30.refs_3_ = bf16[128,1024]{1,0:T(8,128)(2,1)S(1)} collective-permute-done((bf16[128,1024]{1,0:T(8,128)(2,1)S(1)}, bf16[128,1024]{1,0:T(8,128)(2,1)S(1)}, u32[]{:S(2)}, u32[]{:S(2)}) %collective-permute-start.30) | collective-permute-done | bytes 262176 | tf_op jit(solution)/shard_map/ppermute | solution.py:32
  130.0 4.0 %shard_map.84 = f32[128,8,1024]{2,1,0:T(8,128)} custom-call(s32[1]{0:T(128)} %bitcast.here_ref, f32[128,8,1024]{2,1,0:T(8,128)} %shard_map.82.tv_ref, bf16[128,1024]{1,0:T(8,128)(2,1)S(1)} %get-tuple-element.94.refs_4_.refs_0_, bf16[128,1024]{1,0:T(8,128)(2,1)S(1)} %collective-permute-done.28.refs_1_, ...), custom_call_target="tpu_custom_call", output_to_operand_aliasing={{}: (1, {})} | custom-call | bytes 1000 | tf_op jit(solution)/shard_map/pallas_call | solution.py:370
  (52 shorter events, 5.6 us)
Async XLA Ops:
  3.2 15.3 %collective-permute-start = (bf16[144,1024]{1,0:T(8,128)(2,1)S(1)}, bf16[144,1024]{1,0:T(8,128)(2,1)S(1)}, u32[]{:S(2)}, u32[]{:S(2)}) collective-permute-start(bf16[144,1024]{1,0:T(8,128)(2,1)S(1)} %get-tuple-element.50.refs_4_), channel_id=1, source_target_pairs={{0,1},{1,0},{2,3},{3,2},{4,5},{5,4},{6,7},{7,6},{8,9},{9,8},{10,11... | collective-permute-start | bytes 884744 | tf_op jit(solution)/shard_map/ppermute | solution.py:32
  3.2 15.3 %collective-permute-start.1 = (bf16[128,1024]{1,0:T(8,128)(2,1)}, bf16[128,1024]{1,0:T(8,128)(2,1)}, u32[]{:S(2)}, u32[]{:S(2)}) collective-permute-start(bf16[128,1024]{1,0:T(8,128)(2,1)} %get-tuple-element.52), channel_id=1, source_target_pairs={{0,2},{1,3},{2,0},{3,1},{4,6},{5,7},{6,4},{7,5},{8,10},{9,11},{10,... | collective-permute-start | bytes 786440 | tf_op jit(solution)/shard_map/ppermute | solution.py:32
  5.9 9.1 %copy-start.6 = (s32[16,6]{0,1:T(8,128)S(1)}, s32[16,6]{0,1:T(8,128)}, u32[]{:S(2)}) copy-start(s32[16,6]{0,1:T(8,128)} %param.8) | copy-start | bytes 1156
  5.9 10.0 %copy-start = (bf16[8,128,128]{2,1,0:T(8,128)(2,1)S(1)}, bf16[8,128,128]{2,1,0:T(8,128)(2,1)}, u32[]{:S(2)}) copy-start(bf16[8,128,128]{2,1,0:T(8,128)(2,1)} %refs_0_.1) | copy-start | bytes 786436
  5.9 13.3 %collective-permute-start.2 = (bf16[144,1024]{1,0:T(8,128)(2,1)S(1)}, bf16[144,1024]{1,0:T(8,128)(2,1)S(1)}, u32[]{:S(2)}, u32[]{:S(2)}) collective-permute-start(bf16[144,1024]{1,0:T(8,128)(2,1)S(1)} %get-tuple-element.53), channel_id=1, source_target_pairs={{0,3},{1,2},{2,1},{3,0},{4,7},{5,6},{6,5},{7,4},{8,11},{9,10},{10,... | collective-permute-start | bytes 884744 | tf_op jit(solution)/shard_map/ppermute | solution.py:32
  9.4 0.7 copy-start.2
  10.1 20.3 %collective-permute-start.4 = (bf16[128,8,512]{2,1,0:T(8,128)(2,1)}, bf16[128,8,512]{2,1,0:T(8,128)(2,1)S(1)}, u32[]{:S(2)}, u32[]{:S(2)}) collective-permute-start(bf16[128,8,512]{2,1,0:T(8,128)(2,1)} %get-tuple-element.58), channel_id=1, source_target_pairs={{3,7},{7,11},{11,15},{19,23},{23,27},{27,31}} | collective-permute-start | bytes 3145736 | tf_op jit(solution)/shard_map/ppermute | solution.py:27
  10.8 19.6 %collective-permute-start.5 = (bf16[256,1024]{1,0:T(8,128)(2,1)}, bf16[256,1024]{1,0:T(8,128)(2,1)}, u32[]{:S(2)}, u32[]{:S(2)}) collective-permute-start(bf16[256,1024]{1,0:T(8,128)(2,1)} %get-tuple-element.59), channel_id=1, source_target_pairs={{0,2},{1,3},{2,0},{3,1},{4,6},{5,7},{6,4},{7,5},{8,10},{9,11},{10,... | collective-permute-start | bytes 1572872 | tf_op jit(solution)/shard_map/ppermute | solution.py:32
  15.9 1.0 copy-start.3
  16.8 2.4 %copy-start.5 = (bf16[128,1024]{1,0:T(8,128)(2,1)S(1)}, bf16[128,1024]{1,0:T(8,128)(2,1)}, u32[]{:S(2)}) copy-start(bf16[128,1024]{1,0:T(8,128)(2,1)} %get-tuple-element.51.refs_0_) | copy-start | bytes 786436
  19.3 2.1 %copy-start.4 = (bf16[128,1024]{1,0:T(8,128)(2,1)S(1)}, bf16[128,1024]{1,0:T(8,128)(2,1)}, u32[]{:S(2)}) copy-start(bf16[128,1024]{1,0:T(8,128)(2,1)} %copy-done.2) | copy-start | bytes 786436
  20.5 17.2 %copy-start.1 = (bf16[128,1024]{1,0:T(8,128)(2,1)S(1)}, bf16[128,1024]{1,0:T(8,128)(2,1)}, u32[]{:S(2)}) copy-start(bf16[128,1024]{1,0:T(8,128)(2,1)} %get-tuple-element.67.refs_0_) | copy-start | bytes 786436
  20.5 21.6 %collective-permute-start.10 = (bf16[128,8,512]{2,1,0:T(8,128)(2,1)S(1)}, bf16[128,8,512]{2,1,0:T(8,128)(2,1)S(1)}, u32[]{:S(2)}, u32[]{:S(2)}) collective-permute-start(bf16[128,8,512]{2,1,0:T(8,128)(2,1)S(1)} %get-tuple-element.66), channel_id=1, source_target_pairs={{3,7},{7,11},{11,15},{19,23},{23,27},{27,31}} | collective-permute-start | bytes 3145736 | tf_op jit(solution)/shard_map/ppermute | solution.py:27
  21.4 9.0 %collective-permute-start.6 = (bf16[128,1024]{1,0:T(8,128)(2,1)S(1)}, bf16[128,1024]{1,0:T(8,128)(2,1)S(1)}, u32[]{:S(2)}, u32[]{:S(2)}) collective-permute-start(bf16[128,1024]{1,0:T(8,128)(2,1)S(1)} %copy-done.4), channel_id=1, source_target_pairs={{0,1},{1,0},{2,3},{3,2},{4,5},{5,4},{6,7},{7,6},{8,9},{9,8},{10,11... | collective-permute-start | bytes 786440 | tf_op jit(solution)/shard_map/ppermute | solution.py:32
  21.6 27.2 %collective-permute-start.3 = (bf16[528,1024]{1,0:T(8,128)(2,1)S(1)}, bf16[528,1024]{1,0:T(8,128)(2,1)S(1)}, u32[]{:S(2)}, u32[]{:S(2)}) collective-permute-start(bf16[528,1024]{1,0:T(8,128)(2,1)S(1)} %get-tuple-element.56.own_ref), channel_id=1, source_target_pairs={{4,0},{5,1},{6,2},{7,3},{8,4},{9,5},{10,6},{11,7},{12,8},{13,9},{1... | collective-permute-start | bytes 3244040 | tf_op jit(solution)/shard_map/ppermute | solution.py:27
  32.2 2.3 %collective-permute-start.7 = (bf16[128,1024]{1,0:T(8,128)(2,1)S(1)}, bf16[128,1024]{1,0:T(8,128)(2,1)S(1)}, u32[]{:S(2)}, u32[]{:S(2)}) collective-permute-start(bf16[128,1024]{1,0:T(8,128)(2,1)S(1)} %get-tuple-element.61), channel_id=1, source_target_pairs={{0,1},{1,0},{2,3},{3,2},{4,5},{5,4},{6,7},{7,6},{8,9},{9,8},{10,11... | collective-permute-start | bytes 786440 | tf_op jit(solution)/shard_map/ppermute | solution.py:32
  32.9 4.8 %collective-permute-start.11 = (bf16[128,1024]{1,0:T(8,128)(2,1)S(1)}, bf16[128,1024]{1,0:T(8,128)(2,1)S(1)}, u32[]{:S(2)}, u32[]{:S(2)}) collective-permute-start(bf16[128,1024]{1,0:T(8,128)(2,1)S(1)} %get-tuple-element.68), channel_id=1, source_target_pairs={{0,1},{1,0},{2,3},{3,2},{4,5},{5,4},{6,7},{7,6},{8,9},{9,8},{10,11... | collective-permute-start | bytes 786440 | tf_op jit(solution)/shard_map/ppermute | solution.py:32
  33.0 13.1 %collective-permute-start.9 = (bf16[256,1024]{1,0:T(8,128)(2,1)S(1)}, bf16[256,1024]{1,0:T(8,128)(2,1)S(1)}, u32[]{:S(2)}, u32[]{:S(2)}) collective-permute-start(bf16[256,1024]{1,0:T(8,128)(2,1)S(1)} %get-tuple-element.64), channel_id=1, source_target_pairs={{0,2},{1,3},{2,0},{3,1},{4,6},{5,7},{6,4},{7,5},{8,10},{9,11},{10,... | collective-permute-start | bytes 1572872 | tf_op jit(solution)/shard_map/ppermute | solution.py:32
  34.5 19.4 %collective-permute-start.8 = (bf16[144,1024]{1,0:T(8,128)(2,1)S(1)}, bf16[144,1024]{1,0:T(8,128)(2,1)S(1)}, u32[]{:S(2)}, u32[]{:S(2)}) collective-permute-start(bf16[144,1024]{1,0:T(8,128)(2,1)S(1)} %get-tuple-element.62), channel_id=1, source_target_pairs={{0,4},{1,5},{2,6},{3,7},{4,8},{5,9},{6,10},{7,11},{8,12},{9,13},{1... | collective-permute-start | bytes 884744 | tf_op jit(solution)/shard_map/ppermute | solution.py:27
  38.9 11.0 %collective-permute-start.13 = (bf16[128,1024]{1,0:T(8,128)(2,1)S(1)}, bf16[128,1024]{1,0:T(8,128)(2,1)S(1)}, u32[]{:S(2)}, u32[]{:S(2)}) collective-permute-start(bf16[128,1024]{1,0:T(8,128)(2,1)S(1)} %get-tuple-element.72), channel_id=1, source_target_pairs={{0,4},{1,5},{2,6},{3,7},{4,8},{5,9},{6,10},{7,11},{8,12},{9,13},{1... | collective-permute-start | bytes 786440 | tf_op jit(solution)/shard_map/ppermute | solution.py:27
  46.1 7.7 %collective-permute-start.12 = (bf16[128,1024]{1,0:T(8,128)(2,1)S(1)}, bf16[128,1024]{1,0:T(8,128)(2,1)S(1)}, u32[]{:S(2)}, u32[]{:S(2)}) collective-permute-start(bf16[128,1024]{1,0:T(8,128)(2,1)S(1)} %slice.9), channel_id=1, source_target_pairs={{0,1},{1,0},{2,3},{3,2},{4,5},{5,4},{6,7},{7,6},{8,9},{9,8},{10,11... | collective-permute-start | bytes 786440 | tf_op jit(solution)/shard_map/ppermute | solution.py:32
  47.4 26.8 %collective-permute-start.16 = (bf16[512,1024]{1,0:T(8,128)(2,1)S(1)}, bf16[512,1024]{1,0:T(8,128)(2,1)S(1)}, u32[]{:S(2)}, u32[]{:S(2)}) collective-permute-start(bf16[512,1024]{1,0:T(8,128)(2,1)S(1)} %get-tuple-element.69.refs_0_.own_ref), channel_id=1, source_target_pairs={{4,0},{5,1},{6,2},{7,3},{8,4},{9,5},{10,6},{11,7},{12,8},{13,9},{1... | collective-permute-start | bytes 3145736 | tf_op jit(solution)/shard_map/ppermute | solution.py:27
  48.9 7.1 %collective-permute-start.17 = (bf16[128,1024]{1,0:T(8,128)(2,1)S(1)}, bf16[128,1024]{1,0:T(8,128)(2,1)S(1)}, u32[]{:S(2)}, u32[]{:S(2)}) collective-permute-start(bf16[128,1024]{1,0:T(8,128)(2,1)S(1)} %get-tuple-element.77), channel_id=1, source_target_pairs={{0,1},{1,0},{2,3},{3,2},{4,5},{5,4},{6,7},{7,6},{8,9},{9,8},{10,11... | collective-permute-start | bytes 786440 | tf_op jit(solution)/shard_map/ppermute | solution.py:32
  49.9 20.0 %collective-permute-start.18 = (bf16[256,1024]{1,0:T(8,128)(2,1)S(1)}, bf16[256,1024]{1,0:T(8,128)(2,1)S(1)}, u32[]{:S(2)}, u32[]{:S(2)}) collective-permute-start(bf16[256,1024]{1,0:T(8,128)(2,1)S(1)} %get-tuple-element.78), channel_id=1, source_target_pairs={{0,2},{1,3},{2,0},{3,1},{4,6},{5,7},{6,4},{7,5},{8,10},{9,11},{10,... | collective-permute-start | bytes 1572872 | tf_op jit(solution)/shard_map/ppermute | solution.py:32
  56.0 21.4 %collective-permute-start.21 = (bf16[256,1024]{1,0:T(8,128)(2,1)S(1)}, bf16[256,1024]{1,0:T(8,128)(2,1)S(1)}, u32[]{:S(2)}, u32[]{:S(2)}) collective-permute-start(bf16[256,1024]{1,0:T(8,128)(2,1)S(1)} %get-tuple-element.84), channel_id=1, source_target_pairs={{0,2},{1,3},{2,0},{3,1},{4,6},{5,7},{6,4},{7,5},{8,10},{9,11},{10,... | collective-permute-start | bytes 1572872 | tf_op jit(solution)/shard_map/ppermute | solution.py:32
  56.1 32.5 %collective-permute-start.14 = (bf16[512,1024]{1,0:T(8,128)(2,1)S(1)}, bf16[512,1024]{1,0:T(8,128)(2,1)S(1)}, u32[]{:S(2)}, u32[]{:S(2)}) collective-permute-start(bf16[512,1024]{1,0:T(8,128)(2,1)S(1)} %get-tuple-element.73.refs_0_.own_ref), channel_id=1, source_target_pairs={{0,4},{1,5},{2,6},{3,7},{4,8},{5,9},{6,10},{7,11},{8,12},{9,13},{1... | collective-permute-start | bytes 3145736 | tf_op jit(solution)/shard_map/ppermute | solution.py:27
  59.3 10.8 %collective-permute-start.20 = (bf16[128,1024]{1,0:T(8,128)(2,1)S(1)}, bf16[128,1024]{1,0:T(8,128)(2,1)S(1)}, u32[]{:S(2)}, u32[]{:S(2)}) collective-permute-start(bf16[128,1024]{1,0:T(8,128)(2,1)S(1)} %get-tuple-element.82), channel_id=1, source_target_pairs={{0,1},{1,0},{2,3},{3,2},{4,5},{5,4},{6,7},{7,6},{8,9},{9,8},{10,11... | collective-permute-start | bytes 786440 | tf_op jit(solution)/shard_map/ppermute | solution.py:32
  69.9 1.6 %collective-permute-start.19 = (bf16[128,1024]{1,0:T(8,128)(2,1)S(1)}, bf16[128,1024]{1,0:T(8,128)(2,1)S(1)}, u32[]{:S(2)}, u32[]{:S(2)}) collective-permute-start(bf16[128,1024]{1,0:T(8,128)(2,1)S(1)} %slice.10), channel_id=1, source_target_pairs={{0,1},{1,0},{2,3},{3,2},{4,5},{5,4},{6,7},{7,6},{8,9},{9,8},{10,11... | collective-permute-start | bytes 786440 | tf_op jit(solution)/shard_map/ppermute | solution.py:32
  70.0 16.0 %collective-permute-start.15 = (bf16[128,1024]{1,0:T(8,128)(2,1)S(1)}, bf16[128,1024]{1,0:T(8,128)(2,1)S(1)}, u32[]{:S(2)}, u32[]{:S(2)}) collective-permute-start(bf16[128,1024]{1,0:T(8,128)(2,1)S(1)} %get-tuple-element.76), channel_id=1, source_target_pairs={{4,0},{5,1},{6,2},{7,3},{8,4},{9,5},{10,6},{11,7},{12,8},{13,9},{1... | collective-permute-start | bytes 786440 | tf_op jit(solution)/shard_map/ppermute | solution.py:27
  79.4 9.2 %collective-permute-start.22 = (bf16[128,1024]{1,0:T(8,128)(2,1)S(1)}, bf16[128,1024]{1,0:T(8,128)(2,1)S(1)}, u32[]{:S(2)}, u32[]{:S(2)}) collective-permute-start(bf16[128,1024]{1,0:T(8,128)(2,1)S(1)} %get-tuple-element.86), channel_id=1, source_target_pairs={{4,0},{5,1},{6,2},{7,3},{8,4},{9,5},{10,6},{11,7},{12,8},{13,9},{1... | collective-permute-start | bytes 786440 | tf_op jit(solution)/shard_map/ppermute | solution.py:27
  80.7 25.6 %collective-permute-start.26 = (bf16[512,1024]{1,0:T(8,128)(2,1)S(1)}, bf16[512,1024]{1,0:T(8,128)(2,1)S(1)}, u32[]{:S(2)}, u32[]{:S(2)}) collective-permute-start(bf16[512,1024]{1,0:T(8,128)(2,1)S(1)} %get-tuple-element.85.refs_0_.own_ref), channel_id=1, source_target_pairs={{0,4},{1,5},{2,6},{3,7},{4,8},{5,9},{6,10},{7,11},{8,12},{9,13},{1... | collective-permute-start | bytes 3145736 | tf_op jit(solution)/shard_map/ppermute | solution.py:27
  84.8 5.9 %collective-permute-start.27 = (bf16[128,1024]{1,0:T(8,128)(2,1)S(1)}, bf16[128,1024]{1,0:T(8,128)(2,1)S(1)}, u32[]{:S(2)}, u32[]{:S(2)}) collective-permute-start(bf16[128,1024]{1,0:T(8,128)(2,1)S(1)} %slice.11), channel_id=1, source_target_pairs={{0,1},{1,0},{2,3},{3,2},{4,5},{5,4},{6,7},{7,6},{8,9},{9,8},{10,11... | collective-permute-start | bytes 786440 | tf_op jit(solution)/shard_map/ppermute | solution.py:32
  91.6 31.6 %collective-permute-start.31 = (bf16[128,8,512]{2,1,0:T(8,128)(2,1)S(1)}, bf16[128,8,512]{2,1,0:T(8,128)(2,1)S(1)}, u32[]{:S(2)}, u32[]{:S(2)}) collective-permute-start(bf16[128,8,512]{2,1,0:T(8,128)(2,1)S(1)} %shard_map.80.refs_1_.own_ref), channel_id=1, source_target_pairs={{7,3},{11,7},{15,11},{23,19},{27,23},{31,27}} | collective-permute-start | bytes 3145736 | tf_op jit(solution)/shard_map/ppermute | solution.py:27
  92.4 17.7 %collective-permute-start.23 = (bf16[256,1024]{1,0:T(8,128)(2,1)S(1)}, bf16[256,1024]{1,0:T(8,128)(2,1)S(1)}, u32[]{:S(2)}, u32[]{:S(2)}) collective-permute-start(bf16[256,1024]{1,0:T(8,128)(2,1)S(1)} %get-tuple-element.89), channel_id=1, source_target_pairs={{0,1},{1,0},{2,3},{3,2},{4,5},{5,4},{6,7},{7,6},{8,9},{9,8},{10,11... | collective-permute-start | bytes 1572872 | tf_op jit(solution)/shard_map/ppermute | solution.py:32
  93.9 17.5 %collective-permute-start.24 = (bf16[256,1024]{1,0:T(8,128)(2,1)S(1)}, bf16[256,1024]{1,0:T(8,128)(2,1)S(1)}, u32[]{:S(2)}, u32[]{:S(2)}) collective-permute-start(bf16[256,1024]{1,0:T(8,128)(2,1)S(1)} %get-tuple-element.90), channel_id=1, source_target_pairs={{0,2},{1,3},{2,0},{3,1},{4,6},{5,7},{6,4},{7,5},{8,10},{9,11},{10,... | collective-permute-start | bytes 1572872 | tf_op jit(solution)/shard_map/ppermute | solution.py:32
  95.1 24.1 %collective-permute-start.25 = (bf16[256,1024]{1,0:T(8,128)(2,1)S(1)}, bf16[256,1024]{1,0:T(8,128)(2,1)S(1)}, u32[]{:S(2)}, u32[]{:S(2)}) collective-permute-start(bf16[256,1024]{1,0:T(8,128)(2,1)S(1)} %get-tuple-element.91), channel_id=1, source_target_pairs={{0,3},{1,2},{2,1},{3,0},{4,7},{5,6},{6,5},{7,4},{8,11},{9,10},{10,... | collective-permute-start | bytes 1572872 | tf_op jit(solution)/shard_map/ppermute | solution.py:32
  108.3 17.6 %collective-permute-start.28 = (bf16[128,1024]{1,0:T(8,128)(2,1)S(1)}, bf16[128,1024]{1,0:T(8,128)(2,1)S(1)}, u32[]{:S(2)}, u32[]{:S(2)}) collective-permute-start(bf16[128,1024]{1,0:T(8,128)(2,1)S(1)} %get-tuple-element.95), channel_id=1, source_target_pairs={{0,1},{1,0},{2,3},{3,2},{4,5},{5,4},{6,7},{7,6},{8,9},{9,8},{10,11... | collective-permute-start | bytes 786440 | tf_op jit(solution)/shard_map/ppermute | solution.py:32
  110.1 15.8 %collective-permute-start.29 = (bf16[128,1024]{1,0:T(8,128)(2,1)S(1)}, bf16[128,1024]{1,0:T(8,128)(2,1)S(1)}, u32[]{:S(2)}, u32[]{:S(2)}) collective-permute-start(bf16[128,1024]{1,0:T(8,128)(2,1)S(1)} %get-tuple-element.96), channel_id=1, source_target_pairs={{0,2},{1,3},{2,0},{3,1},{4,6},{5,7},{6,4},{7,5},{8,10},{9,11},{10,... | collective-permute-start | bytes 786440 | tf_op jit(solution)/shard_map/ppermute | solution.py:32
  111.4 18.6 %collective-permute-start.30 = (bf16[128,1024]{1,0:T(8,128)(2,1)S(1)}, bf16[128,1024]{1,0:T(8,128)(2,1)S(1)}, u32[]{:S(2)}, u32[]{:S(2)}) collective-permute-start(bf16[128,1024]{1,0:T(8,128)(2,1)S(1)} %get-tuple-element.97), channel_id=1, source_target_pairs={{0,3},{1,2},{2,1},{3,0},{4,7},{5,6},{6,5},{7,4},{8,11},{9,10},{10,... | collective-permute-start | bytes 786440 | tf_op jit(solution)/shard_map/ppermute | solution.py:32

commit v17 on v14

--- a/solution.py
+++ b/solution.py
@@ -573,9 +573,9 @@
     got0 = moved(sent0, G, only=G - 1)
     over = swapped(v23, 2)
     band_p, band_b = bands(here, coverage, offsets, weights, v1)
+    got1 = moved(tied(sent1, band_p), G, only=G - 1)
     own0, edge0 = pack(here, [(array, 0) for array in got_vols0], 2 * rows, band_p)
     high0, near = moved(own0, -G), swapped(tied(v1, own0), 1)
-    got1 = moved(tied(sent1, own0), G, only=G - 1)
     s0, s1, s23, over_beyond = split_rows(here, sinogram, got0, 0, paired, [(over, 1)], near)
     s_near, s_over = swapped(s1, 1), swapped(s23, 2)
     low0 = moved(tied(edge0, s_near), G)

time: 131 us -> 131 us (level)
  transfers between devices with their start and end apart: 32 -> 32, of which waited for: 11 -> 10; matrix products, arithmetic and copies ran while one was open for 1% -> 1% of each run, Pallas kernels for 28% -> 28%
where the time goes in v17:
time: 131 us; the launch traced here: 130 us
  starting transfers between devices  49.6 us (38%)
  Pallas kernels  42.3 us (32%)
  waiting for transfers between devices  35 us (27%)
  local copies, waits for them, and re-layouts  2.57 us (2%)
    ppermute x21, starting transfers between devices, swapped(): return lax.ppermute(value, 'slab', [(i, i ^ bits) for i in range(count)])  26.9 us
    ppermute x21, waiting for transfers between devices, swapped(): return lax.ppermute(value, 'slab', [(i, i ^ bits) for i in range(count)])  24.8 us
    ppermute x11, starting transfers between devices, moved(): return lax.ppermute(value, 'slab', pairs)  22.7 us
    ppermute x11, waiting for transfers between devices, moved(): return lax.ppermute(value, 'slab', pairs)  10.2 us
    pallas_call x1, Pallas kernels, half_tv(): call(tv_kernel, 0, grid=(depth // deep,), in_specs=[SMEM] + edges + [afte...  9.99 us
    pallas_call x2, Pallas kernels, cast_rows(): call(functools.partial(cast_kernel, groups, len(edges), halves), 2, grid=...  5.97 us
    pallas_call x2, Pallas kernels, finish(): call(finish_kernel, 0, grid=(count,), in_specs=[SMEM, part] + piece_specs...  5.85 us
    pallas_call x2, Pallas kernels, project(): call(functools.partial(project_kernel, groups), 3, grid=(cols // tile,),...  4.23 us
  transfers between devices with their start and end apart: 32, of which 10 were waited for; matrix products, arithmetic and copies ran while one was open for 1% of the time, Pallas kernels for 28%

profile of v17, /device:TPU:1, one launch (start us, length us, event | category | flops | bytes accessed | tf_op | source)
XLA Modules:
  0.0 130.4 jit_solution(14938525649489257823)
XLA Ops:
  0.6 2.5 %shard_map.68 = (bf16[128,1024]{1,0:T(8,128)(2,1)}, bf16[144,1024]{1,0:T(8,128)(2,1)S(1)}, bf16[128,1024]{1,0:T(8,128)(2,1)}, bf16[144,1024]{1,0:T(8,128)(2,1)S(1)}) custom-call(s32[1]{0:T(128)} %bitcast.here_ref, f32[1024,1024]{1,0:T(8,128)} %bitcast.2, f32[1024,1024]{1,0:T(8,128)} %bitcast.3, f32[1024,1024]{1,0:T(8,128)} %bitcast.4, f32[1024,1024]{1,0:T(8,128)} %bitcast.5), custom_call_target="tpu_custom_call" | custom-call | flops 2300000000 | bytes 1000 | tf_op jit(solution)/shard_map/pallas_call | solution.py:115
  3.2 2.7 %collective-permute-start.1 = (bf16[128,1024]{1,0:T(8,128)(2,1)}, bf16[128,1024]{1,0:T(8,128)(2,1)}, u32[]{:S(2)}, u32[]{:S(2)}) collective-permute-start(bf16[128,1024]{1,0:T(8,128)(2,1)} %get-tuple-element.52), channel_id=1, source_target_pairs={{0,2},{1,3},{2,0},{3,1},{4,6},{5,7},{6,4},{7,5},{8,10},{9,11},{10,... | collective-permute-start | bytes 786440 | tf_op jit(solution)/shard_map/ppermute | solution.py:32
  6.0 3.4 %shard_map.69 = (bf16[128,1024]{1,0:T(8,128)(2,1)}, bf16[128,1024]{1,0:T(8,128)(2,1)S(1)}, bf16[256,1024]{1,0:T(8,128)(2,1)}, bf16[128,8,512]{2,1,0:T(8,128)(2,1)}, bf16[128,8,512]{2,1,0:T(8,128)(2,1)S(1)}) custom-call(s32[1]{0:T(128)} %bitcast.here_ref, f32[1024,1024]{1,0:T(8,128)} %bitcast.6, f32[1024,1024]{1,0:T(8,128)} %bitcast.7, ...), custom_call_target="tpu_custom_call" | custom-call | flops 2300000000 | bytes 1000 | tf_op jit(solution)/shard_map/pallas_call | solution.py:115
  10.8 4.2 %collective-permute-start.5 = (bf16[256,1024]{1,0:T(8,128)(2,1)}, bf16[256,1024]{1,0:T(8,128)(2,1)}, u32[]{:S(2)}, u32[]{:S(2)}) collective-permute-start(bf16[256,1024]{1,0:T(8,128)(2,1)} %get-tuple-element.59), channel_id=1, source_target_pairs={{0,2},{1,3},{2,0},{3,1},{4,6},{5,7},{6,4},{7,5},{8,10},{9,11},{10,... | collective-permute-start | bytes 1572872 | tf_op jit(solution)/shard_map/ppermute | solution.py:32
  15.1 0.8 copy.13.offset_ref
  15.9 0.9 copy-done.4
  16.8 1.6 %shard_map.70 = (bf16[512,1152]{1,0:T(8,128)(2,1)S(1)}, bf16[512,1152]{1,0:T(8,128)(2,1)S(1)}) custom-call(s32[1]{0:T(128)} %bitcast.here_ref, s32[16,6]{1,0:T(8,128)S(1)} %copy.12.cover_ref, s32[16,6]{1,0:T(8,128)S(1)} %copy.13.offset_ref, bf16[8,128,128]{2,1,0:T(8,128)(2,1)S(1)} %copy-done, bf16[128,1024]{1,0:T(8,128)(2,1)S(1)} %copy-done.4), custom_call_target="tpu_custom_call" | custom-call | flops 10350000128 | bytes 1000 | tf_op jit(solution)/shard_map/pallas_call | solution.py:415
  19.3 1.2 shard_map.71
  20.7 1.3 collective-permute-start.3
  22.0 8.4 %collective-permute-done.5.refs_0_.refs_2_ = bf16[256,1024]{1,0:T(8,128)(2,1)} collective-permute-done((bf16[256,1024]{1,0:T(8,128)(2,1)}, bf16[256,1024]{1,0:T(8,128)(2,1)}, u32[]{:S(2)}, u32[]{:S(2)}) %collective-permute-start.5) | collective-permute-done | bytes 524320 | tf_op jit(solution)/shard_map/ppermute | solution.py:32
  30.4 1.8 %shard_map.72 = (bf16[128,1024]{1,0:T(8,128)(2,1)S(1)}, bf16[128,1024]{1,0:T(8,128)(2,1)S(1)}, bf16[256,1024]{1,0:T(8,128)(2,1)S(1)}, bf16[128,1024]{1,0:T(8,128)(2,1)S(1)}) custom-call(s32[1]{0:T(128)} %bitcast.here_ref, bf16[128,8,1024]{2,1,0:T(8,128)(2,1)} %refs_2_.3, bf16[128,8,512]{2,1,0:T(8,128)(2,1)S(1)} %collective-permute-done.4.got_ref, ...), custom_call_target="tpu_custom_call" | custom-call | flops 2300000000 | bytes 1000 | tf_op jit(solution)/shard_map/pallas_call | solution.py:196
  32.2 1.3 %collective-permute-start.9 = (bf16[256,1024]{1,0:T(8,128)(2,1)S(1)}, bf16[256,1024]{1,0:T(8,128)(2,1)S(1)}, u32[]{:S(2)}, u32[]{:S(2)}) collective-permute-start(bf16[256,1024]{1,0:T(8,128)(2,1)S(1)} %get-tuple-element.64), channel_id=1, source_target_pairs={{0,2},{1,3},{2,0},{3,1},{4,6},{5,7},{6,4},{7,5},{8,10},{9,11},{10,... | collective-permute-start | bytes 1572872 | tf_op jit(solution)/shard_map/ppermute | solution.py:32
  33.5 1.1 collective-permute-start.7
  34.7 1.2 collective-permute-done.7.refs_1_
  35.8 3.2 %collective-permute-start.8 = (bf16[144,1024]{1,0:T(8,128)(2,1)S(1)}, bf16[144,1024]{1,0:T(8,128)(2,1)S(1)}, u32[]{:S(2)}, u32[]{:S(2)}) collective-permute-start(bf16[144,1024]{1,0:T(8,128)(2,1)S(1)} %get-tuple-element.62), channel_id=1, source_target_pairs={{0,4},{1,5},{2,6},{3,7},{4,8},{5,9},{6,10},{7,11},{8,12},{9,13},{1... | collective-permute-start | bytes 884744 | tf_op jit(solution)/shard_map/ppermute | solution.py:27
  39.0 1.2 shard_map.73
  40.2 3.2 %collective-permute-start.12 = (bf16[128,1024]{1,0:T(8,128)(2,1)S(1)}, bf16[128,1024]{1,0:T(8,128)(2,1)S(1)}, u32[]{:S(2)}, u32[]{:S(2)}) collective-permute-start(bf16[128,1024]{1,0:T(8,128)(2,1)S(1)} %get-tuple-element.69), channel_id=1, source_target_pairs={{0,4},{1,5},{2,6},{3,7},{4,8},{5,9},{6,10},{7,11},{8,12},{9,13},{1... | collective-permute-start | bytes 786440 | tf_op jit(solution)/shard_map/ppermute | solution.py:27
  43.4 1.6 %collective-permute-done.9.refs_2_ = bf16[256,1024]{1,0:T(8,128)(2,1)S(1)} collective-permute-done((bf16[256,1024]{1,0:T(8,128)(2,1)S(1)}, bf16[256,1024]{1,0:T(8,128)(2,1)S(1)}, u32[]{:S(2)}, u32[]{:S(2)}) %collective-permute-start.9) | collective-permute-done | bytes 524320 | tf_op jit(solution)/shard_map/ppermute | solution.py:32
  45.1 1.6 %collective-permute-start.11 = (bf16[128,1024]{1,0:T(8,128)(2,1)S(1)}, bf16[128,1024]{1,0:T(8,128)(2,1)S(1)}, u32[]{:S(2)}, u32[]{:S(2)}) collective-permute-start(bf16[128,1024]{1,0:T(8,128)(2,1)S(1)} %slice.9), channel_id=1, source_target_pairs={{0,1},{1,0},{2,3},{3,2},{4,5},{5,4},{6,7},{7,6},{8,9},{9,8},{10,11... | collective-permute-start | bytes 786440 | tf_op jit(solution)/shard_map/ppermute | solution.py:32
  46.7 1.3 collective-permute-start.16
  48.0 1.7 %shard_map.74 = (bf16[128,1024]{1,0:T(8,128)(2,1)S(1)}, bf16[128,1024]{1,0:T(8,128)(2,1)S(1)}, bf16[256,1024]{1,0:T(8,128)(2,1)S(1)}) custom-call(s32[1]{0:T(128)} %bitcast.here_ref, bf16[128,8,1024]{2,1,0:T(8,128)(2,1)} %refs_2_.3, bf16[128,8,512]{2,1,0:T(8,128)(2,1)S(1)} %collective-permute-done.13.got_ref, ...), custom_call_target="tpu_custom_call" | custom-call | flops 2300000000 | bytes 1000 | tf_op jit(solution)/shard_map/pallas_call | solution.py:196
  49.8 0.8 collective-permute-done.12.refs_4_.low_ref
  51.3 2.1 %shard_map.75 = (bf16[512,1024]{1,0:T(8,128)(2,1)S(1)}, bf16[128,1024]{1,0:T(8,128)(2,1)S(1)}, bf16[128,1024]{1,0:T(8,128)(2,1)S(1)}, bf16[256,1024]{1,0:T(8,128)(2,1)S(1)}) custom-call(s32[1]{0:T(128)} %bitcast.here_ref, bf16[512,1152]{1,0:T(8,128)(2,1)S(1)} %get-tuple-element.55.refs_4_.band_ref, bf16[528,1024]{1,0:T(8,128)(2,1)S(1)} %get-tuple-element.56.own_ref, ...), custom_call_target="tpu_custom_call" | custom-call | flops 3449999872 | bytes 1000 | tf_op jit(solution)/shard_map/pallas_call | solution.py:446
  53.4 0.9 collective-permute-start.21
  54.3 4.2 %collective-permute-start.14 = (bf16[512,1024]{1,0:T(8,128)(2,1)S(1)}, bf16[512,1024]{1,0:T(8,128)(2,1)S(1)}, u32[]{:S(2)}, u32[]{:S(2)}) collective-permute-start(bf16[512,1024]{1,0:T(8,128)(2,1)S(1)} %get-tuple-element.73.refs_0_.own_ref), channel_id=1, source_target_pairs={{0,4},{1,5},{2,6},{3,7},{4,8},{5,9},{6,10},{7,11},{8,12},{9,13},{1... | collective-permute-start | bytes 3145736 | tf_op jit(solution)/shard_map/ppermute | solution.py:27
  58.5 2.1 %collective-permute-start.20 = (bf16[128,1024]{1,0:T(8,128)(2,1)S(1)}, bf16[128,1024]{1,0:T(8,128)(2,1)S(1)}, u32[]{:S(2)}, u32[]{:S(2)}) collective-permute-start(bf16[128,1024]{1,0:T(8,128)(2,1)S(1)} %get-tuple-element.82), channel_id=1, source_target_pairs={{0,1},{1,0},{2,3},{3,2},{4,5},{5,4},{6,7},{7,6},{8,9},{9,8},{10,11... | collective-permute-start | bytes 786440 | tf_op jit(solution)/shard_map/ppermute | solution.py:32
  60.6 10.0 %shard_map.76 = (f32[128,8,1024]{2,1,0:T(8,128)}, f32[8,128]{1,0:T(8,128)S(1)}) custom-call(s32[1]{0:T(128)} %bitcast.here_ref, bf16[144,1024]{1,0:T(8,128)(2,1)S(1)} %collective-permute-done.refs_1_.near_ref, bf16[528,1024]{1,0:T(8,128)(2,1)S(1)} %collective-permute-done.3.high_ref.next_level_ref, ...), custom_call_target="tpu_custom_call" | custom-call | bytes 1000 | tf_op jit(solution)/shard_map/pallas_call | solution.py:546
  70.7 1.3 collective-permute-start.15
  72.2 1.1 collective-permute-done.16.high_ref
  73.3 0.8 collective-permute-done.21.refs_6_.refs_2_
  74.1 2.1 %shard_map.77 = (bf16[512,1024]{1,0:T(8,128)(2,1)S(1)}, bf16[128,1024]{1,0:T(8,128)(2,1)S(1)}) custom-call(s32[1]{0:T(128)} %bitcast.here_ref, bf16[512,1152]{1,0:T(8,128)(2,1)S(1)} %get-tuple-element.55.refs_4_.band_ref, bf16[512,1024]{1,0:T(8,128)(2,1)S(1)} %get-tuple-element.67.refs_0_.own_ref, bf16[512,1024]{1,0:T(8,128)(2,1)S(1)} %collective-permute-done.16.high_ref, ...), custom_call_target="tpu_custom_call" | custom-call | flops 3449999872 | bytes 1000 | tf_op jit(solution)/shard_map/pallas_call | solution.py:446
  76.2 1.3 collective-permute-start.22
  77.5 4.8 %collective-permute-start.26 = (bf16[512,1024]{1,0:T(8,128)(2,1)S(1)}, bf16[512,1024]{1,0:T(8,128)(2,1)S(1)}, u32[]{:S(2)}, u32[]{:S(2)}) collective-permute-start(bf16[512,1024]{1,0:T(8,128)(2,1)S(1)} %get-tuple-element.85.refs_0_.own_ref), channel_id=1, source_target_pairs={{0,4},{1,5},{2,6},{3,7},{4,8},{5,9},{6,10},{7,11},{8,12},{9,13},{1... | collective-permute-start | bytes 3145736 | tf_op jit(solution)/shard_map/ppermute | solution.py:27
  82.3 2.5 %collective-permute-start.27 = (bf16[128,1024]{1,0:T(8,128)(2,1)S(1)}, bf16[128,1024]{1,0:T(8,128)(2,1)S(1)}, u32[]{:S(2)}, u32[]{:S(2)}) collective-permute-start(bf16[128,1024]{1,0:T(8,128)(2,1)S(1)} %slice.11), channel_id=1, source_target_pairs={{0,1},{1,0},{2,3},{3,2},{4,5},{5,4},{6,7},{7,6},{8,9},{9,8},{10,11... | collective-permute-start | bytes 786440 | tf_op jit(solution)/shard_map/ppermute | solution.py:32
  84.8 2.1 %shard_map.78 = (bf16[256,1024]{1,0:T(8,128)(2,1)S(1)}, bf16[256,1024]{1,0:T(8,128)(2,1)S(1)}, bf16[256,1024]{1,0:T(8,128)(2,1)S(1)}, bf16[256,1024]{1,0:T(8,128)(2,1)S(1)}) custom-call(s32[1]{0:T(128)} %bitcast.here_ref, bf16[512,1152]{1,0:T(8,128)(2,1)S(1)} %get-tuple-element.75.band_ref, bf16[512,1024]{1,0:T(8,128)(2,1)S(1)} %get-tuple-element.73.refs_0_.own_ref, ...), custom_call_target="tpu_custom_call" | custom-call | bytes 1000 | tf_op jit(solution)/shard_map/pallas_call | solution.py:478
  87.0 0.9 shard_map.80.refs_1_.own_ref
  88.5 2.8 %collective-permute-start.23 = (bf16[256,1024]{1,0:T(8,128)(2,1)S(1)}, bf16[256,1024]{1,0:T(8,128)(2,1)S(1)}, u32[]{:S(2)}, u32[]{:S(2)}) collective-permute-start(bf16[256,1024]{1,0:T(8,128)(2,1)S(1)} %get-tuple-element.89), channel_id=1, source_target_pairs={{0,1},{1,0},{2,3},{3,2},{4,5},{5,4},{6,7},{7,6},{8,9},{9,8},{10,11... | collective-permute-start | bytes 1572872 | tf_op jit(solution)/shard_map/ppermute | solution.py:32
  91.3 1.1 collective-permute-start.24
  93.1 1.2 shard_map.79
  94.2 8.3 %collective-permute-done.26.low_ref = bf16[512,1024]{1,0:T(8,128)(2,1)S(1)} collective-permute-done((bf16[512,1024]{1,0:T(8,128)(2,1)S(1)}, bf16[512,1024]{1,0:T(8,128)(2,1)S(1)}, u32[]{:S(2)}, u32[]{:S(2)}) %collective-permute-start.26) | collective-permute-done | bytes 1048608 | tf_op jit(solution)/shard_map/ppermute | solution.py:27
  102.5 1.9 %shard_map.81 = (bf16[128,1024]{1,0:T(8,128)(2,1)S(1)}, bf16[128,1024]{1,0:T(8,128)(2,1)S(1)}, bf16[128,1024]{1,0:T(8,128)(2,1)S(1)}, bf16[128,1024]{1,0:T(8,128)(2,1)S(1)}) custom-call(s32[1]{0:T(128)} %bitcast.here_ref, bf16[512,1152]{1,0:T(8,128)(2,1)S(1)} %get-tuple-element.75.band_ref, bf16[512,1024]{1,0:T(8,128)(2,1)S(1)} %get-tuple-element.85.refs_0_.own_ref, ...), custom_call_target="tpu_custom_call" | custom-call | bytes 1000 | tf_op jit(solution)/shard_map/pallas_call | solution.py:478
  104.5 3.1 %collective-permute-start.28 = (bf16[128,1024]{1,0:T(8,128)(2,1)S(1)}, bf16[128,1024]{1,0:T(8,128)(2,1)S(1)}, u32[]{:S(2)}, u32[]{:S(2)}) collective-permute-start(bf16[128,1024]{1,0:T(8,128)(2,1)S(1)} %get-tuple-element.95), channel_id=1, source_target_pairs={{0,1},{1,0},{2,3},{3,2},{4,5},{5,4},{6,7},{7,6},{8,9},{9,8},{10,11... | collective-permute-start | bytes 786440 | tf_op jit(solution)/shard_map/ppermute | solution.py:32
  107.6 1.1 collective-permute-start.29
  109.3 7.4 %collective-permute-done.25.refs_3_ = bf16[256,1024]{1,0:T(8,128)(2,1)S(1)} collective-permute-done((bf16[256,1024]{1,0:T(8,128)(2,1)S(1)}, bf16[256,1024]{1,0:T(8,128)(2,1)S(1)}, u32[]{:S(2)}, u32[]{:S(2)}) %collective-permute-start.25) | collective-permute-done | bytes 524320 | tf_op jit(solution)/shard_map/ppermute | solution.py:32
  116.7 2.9 %shard_map.82.tv_ref = f32[128,8,1024]{2,1,0:T(8,128)} custom-call(s32[1]{0:T(128)} %bitcast.here_ref, f32[128,8,1024]{2,1,0:T(8,128)} %get-tuple-element.88.tv_ref, bf16[256,1024]{1,0:T(8,128)(2,1)S(1)} %get-tuple-element.87.refs_4_.refs_0_, bf16[256,1024]{1,0:T(8,128)(2,1)S(1)} %collective-permute-done.23.refs_1_, ...), custom_call_target="tpu_custom_call", output_to_operand_aliasing={{}: (1, {})} | custom-call | bytes 1000 | tf_op jit(solution)/shard_map/pallas_call | solution.py:367
  119.6 2.6 %shard_map.83.refs_4_ = bf16[128,8,1024]{2,1,0:T(8,128)(2,1)} custom-call(s32[1]{0:T(128)} %bitcast.here_ref, bf16[128,8,512]{2,1,0:T(8,128)(2,1)S(1)} %shard_map.80.refs_1_.own_ref, bf16[128,8,512]{2,1,0:T(8,128)(2,1)S(1)} %collective-permute-done.31.above_ref, bf16[256,1024]{1,0:T(8,128)(2,1)S(1)} %get-tuple-element.87.refs_4_.refs_0_, ...), custom_call_target="tpu_custom_call" | custom-call | bytes 1000 | tf_op jit(solution)/shard_map/pallas_call | solution.py:345
  122.3 5.2 %collective-permute-done.30.refs_3_ = bf16[128,1024]{1,0:T(8,128)(2,1)S(1)} collective-permute-done((bf16[128,1024]{1,0:T(8,128)(2,1)S(1)}, bf16[128,1024]{1,0:T(8,128)(2,1)S(1)}, u32[]{:S(2)}, u32[]{:S(2)}) %collective-permute-start.30) | collective-permute-done | bytes 262176 | tf_op jit(solution)/shard_map/ppermute | solution.py:32
  127.5 2.9 %shard_map.84 = f32[128,8,1024]{2,1,0:T(8,128)} custom-call(s32[1]{0:T(128)} %bitcast.here_ref, f32[128,8,1024]{2,1,0:T(8,128)} %shard_map.82.tv_ref, bf16[128,1024]{1,0:T(8,128)(2,1)S(1)} %get-tuple-element.94.refs_4_.refs_0_, bf16[128,1024]{1,0:T(8,128)(2,1)S(1)} %collective-permute-done.28.refs_1_, ...), custom_call_target="tpu_custom_call", output_to_operand_aliasing={{}: (1, {})} | custom-call | bytes 1000 | tf_op jit(solution)/shard_map/pallas_call | solution.py:367
  (52 shorter events, 5.7 us)
Async XLA Ops:
  3.2 16.1 %collective-permute-start = (bf16[144,1024]{1,0:T(8,128)(2,1)S(1)}, bf16[144,1024]{1,0:T(8,128)(2,1)S(1)}, u32[]{:S(2)}, u32[]{:S(2)}) collective-permute-start(bf16[144,1024]{1,0:T(8,128)(2,1)S(1)} %get-tuple-element.50.refs_4_), channel_id=1, source_target_pairs={{0,1},{1,0},{2,3},{3,2},{4,5},{5,4},{6,7},{7,6},{8,9},{9,8},{10,11... | collective-permute-start | bytes 884744 | tf_op jit(solution)/shard_map/ppermute | solution.py:32
  3.2 15.3 %collective-permute-start.1 = (bf16[128,1024]{1,0:T(8,128)(2,1)}, bf16[128,1024]{1,0:T(8,128)(2,1)}, u32[]{:S(2)}, u32[]{:S(2)}) collective-permute-start(bf16[128,1024]{1,0:T(8,128)(2,1)} %get-tuple-element.52), channel_id=1, source_target_pairs={{0,2},{1,3},{2,0},{3,1},{4,6},{5,7},{6,4},{7,5},{8,10},{9,11},{10,... | collective-permute-start | bytes 786440 | tf_op jit(solution)/shard_map/ppermute | solution.py:32
  5.9 9.1 %copy-start.6 = (s32[16,6]{0,1:T(8,128)S(1)}, s32[16,6]{0,1:T(8,128)}, u32[]{:S(2)}) copy-start(s32[16,6]{0,1:T(8,128)} %param.8) | copy-start | bytes 1156
  5.9 10.0 %copy-start = (bf16[8,128,128]{2,1,0:T(8,128)(2,1)S(1)}, bf16[8,128,128]{2,1,0:T(8,128)(2,1)}, u32[]{:S(2)}) copy-start(bf16[8,128,128]{2,1,0:T(8,128)(2,1)} %refs_0_.1) | copy-start | bytes 786436
  5.9 13.3 %collective-permute-start.2 = (bf16[144,1024]{1,0:T(8,128)(2,1)S(1)}, bf16[144,1024]{1,0:T(8,128)(2,1)S(1)}, u32[]{:S(2)}, u32[]{:S(2)}) collective-permute-start(bf16[144,1024]{1,0:T(8,128)(2,1)S(1)} %get-tuple-element.53), channel_id=1, source_target_pairs={{0,3},{1,2},{2,1},{3,0},{4,7},{5,6},{6,5},{7,4},{8,11},{9,10},{10,... | collective-permute-start | bytes 884744 | tf_op jit(solution)/shard_map/ppermute | solution.py:32
  9.4 0.7 copy-start.3
  10.1 20.3 %collective-permute-start.4 = (bf16[128,8,512]{2,1,0:T(8,128)(2,1)}, bf16[128,8,512]{2,1,0:T(8,128)(2,1)S(1)}, u32[]{:S(2)}, u32[]{:S(2)}) collective-permute-start(bf16[128,8,512]{2,1,0:T(8,128)(2,1)} %get-tuple-element.58), channel_id=1, source_target_pairs={{3,7},{7,11},{11,15},{19,23},{23,27},{27,31}} | collective-permute-start | bytes 3145736 | tf_op jit(solution)/shard_map/ppermute | solution.py:27
  10.8 19.6 %collective-permute-start.5 = (bf16[256,1024]{1,0:T(8,128)(2,1)}, bf16[256,1024]{1,0:T(8,128)(2,1)}, u32[]{:S(2)}, u32[]{:S(2)}) collective-permute-start(bf16[256,1024]{1,0:T(8,128)(2,1)} %get-tuple-element.59), channel_id=1, source_target_pairs={{0,2},{1,3},{2,0},{3,1},{4,6},{5,7},{6,4},{7,5},{8,10},{9,11},{10,... | collective-permute-start | bytes 1572872 | tf_op jit(solution)/shard_map/ppermute | solution.py:32
  15.9 1.0 copy-start.4
  16.8 2.4 %copy-start.2 = (bf16[128,1024]{1,0:T(8,128)(2,1)S(1)}, bf16[128,1024]{1,0:T(8,128)(2,1)}, u32[]{:S(2)}) copy-start(bf16[128,1024]{1,0:T(8,128)(2,1)} %get-tuple-element.51.refs_0_) | copy-start | bytes 786436
  18.5 28.2 %collective-permute-start.13 = (bf16[128,8,512]{2,1,0:T(8,128)(2,1)S(1)}, bf16[128,8,512]{2,1,0:T(8,128)(2,1)S(1)}, u32[]{:S(2)}, u32[]{:S(2)}) collective-permute-start(bf16[128,8,512]{2,1,0:T(8,128)(2,1)S(1)} %get-tuple-element.71), channel_id=1, source_target_pairs={{3,7},{7,11},{11,15},{19,23},{23,27},{27,31}} | collective-permute-start | bytes 3145736 | tf_op jit(solution)/shard_map/ppermute | solution.py:27
  19.3 1.2 copy-start.5
  20.5 18.5 %copy-start.1 = (bf16[128,1024]{1,0:T(8,128)(2,1)S(1)}, bf16[128,1024]{1,0:T(8,128)(2,1)}, u32[]{:S(2)}) copy-start(bf16[128,1024]{1,0:T(8,128)(2,1)} %get-tuple-element.65.refs_0_) | copy-start | bytes 786436
  20.5 9.9 %collective-permute-start.6 = (bf16[128,1024]{1,0:T(8,128)(2,1)S(1)}, bf16[128,1024]{1,0:T(8,128)(2,1)S(1)}, u32[]{:S(2)}, u32[]{:S(2)}) collective-permute-start(bf16[128,1024]{1,0:T(8,128)(2,1)S(1)} %copy-done.5), channel_id=1, source_target_pairs={{0,1},{1,0},{2,3},{3,2},{4,5},{5,4},{6,7},{7,6},{8,9},{9,8},{10,11... | collective-permute-start | bytes 786440 | tf_op jit(solution)/shard_map/ppermute | solution.py:32
  20.7 29.0 %collective-permute-start.3 = (bf16[528,1024]{1,0:T(8,128)(2,1)S(1)}, bf16[528,1024]{1,0:T(8,128)(2,1)S(1)}, u32[]{:S(2)}, u32[]{:S(2)}) collective-permute-start(bf16[528,1024]{1,0:T(8,128)(2,1)S(1)} %get-tuple-element.56.own_ref), channel_id=1, source_target_pairs={{4,0},{5,1},{6,2},{7,3},{8,4},{9,5},{10,6},{11,7},{12,8},{13,9},{1... | collective-permute-start | bytes 3244040 | tf_op jit(solution)/shard_map/ppermute | solution.py:27
  32.2 12.9 %collective-permute-start.9 = (bf16[256,1024]{1,0:T(8,128)(2,1)S(1)}, bf16[256,1024]{1,0:T(8,128)(2,1)S(1)}, u32[]{:S(2)}, u32[]{:S(2)}) collective-permute-start(bf16[256,1024]{1,0:T(8,128)(2,1)S(1)} %get-tuple-element.64), channel_id=1, source_target_pairs={{0,2},{1,3},{2,0},{3,1},{4,6},{5,7},{6,4},{7,5},{8,10},{9,11},{10,... | collective-permute-start | bytes 1572872 | tf_op jit(solution)/shard_map/ppermute | solution.py:32
  33.5 2.3 %collective-permute-start.7 = (bf16[128,1024]{1,0:T(8,128)(2,1)S(1)}, bf16[128,1024]{1,0:T(8,128)(2,1)S(1)}, u32[]{:S(2)}, u32[]{:S(2)}) collective-permute-start(bf16[128,1024]{1,0:T(8,128)(2,1)S(1)} %get-tuple-element.61), channel_id=1, source_target_pairs={{0,1},{1,0},{2,3},{3,2},{4,5},{5,4},{6,7},{7,6},{8,9},{9,8},{10,11... | collective-permute-start | bytes 786440 | tf_op jit(solution)/shard_map/ppermute | solution.py:32
  34.7 4.4 %collective-permute-start.10 = (bf16[128,1024]{1,0:T(8,128)(2,1)S(1)}, bf16[128,1024]{1,0:T(8,128)(2,1)S(1)}, u32[]{:S(2)}, u32[]{:S(2)}) collective-permute-start(bf16[128,1024]{1,0:T(8,128)(2,1)S(1)} %get-tuple-element.66), channel_id=1, source_target_pairs={{0,1},{1,0},{2,3},{3,2},{4,5},{5,4},{6,7},{7,6},{8,9},{9,8},{10,11... | collective-permute-start | bytes 786440 | tf_op jit(solution)/shard_map/ppermute | solution.py:32
  35.8 15.4 %collective-permute-start.8 = (bf16[144,1024]{1,0:T(8,128)(2,1)S(1)}, bf16[144,1024]{1,0:T(8,128)(2,1)S(1)}, u32[]{:S(2)}, u32[]{:S(2)}) collective-permute-start(bf16[144,1024]{1,0:T(8,128)(2,1)S(1)} %get-tuple-element.62), channel_id=1, source_target_pairs={{0,4},{1,5},{2,6},{3,7},{4,8},{5,9},{6,10},{7,11},{8,12},{9,13},{1... | collective-permute-start | bytes 884744 | tf_op jit(solution)/shard_map/ppermute | solution.py:27
  40.2 10.4 %collective-permute-start.12 = (bf16[128,1024]{1,0:T(8,128)(2,1)S(1)}, bf16[128,1024]{1,0:T(8,128)(2,1)S(1)}, u32[]{:S(2)}, u32[]{:S(2)}) collective-permute-start(bf16[128,1024]{1,0:T(8,128)(2,1)S(1)} %get-tuple-element.69), channel_id=1, source_target_pairs={{0,4},{1,5},{2,6},{3,7},{4,8},{5,9},{6,10},{7,11},{8,12},{9,13},{1... | collective-permute-start | bytes 786440 | tf_op jit(solution)/shard_map/ppermute | solution.py:27
  45.1 6.2 %collective-permute-start.11 = (bf16[128,1024]{1,0:T(8,128)(2,1)S(1)}, bf16[128,1024]{1,0:T(8,128)(2,1)S(1)}, u32[]{:S(2)}, u32[]{:S(2)}) collective-permute-start(bf16[128,1024]{1,0:T(8,128)(2,1)S(1)} %slice.9), channel_id=1, source_target_pairs={{0,1},{1,0},{2,3},{3,2},{4,5},{5,4},{6,7},{7,6},{8,9},{9,8},{10,11... | collective-permute-start | bytes 786440 | tf_op jit(solution)/shard_map/ppermute | solution.py:32
  46.7 26.6 %collective-permute-start.16 = (bf16[512,1024]{1,0:T(8,128)(2,1)S(1)}, bf16[512,1024]{1,0:T(8,128)(2,1)S(1)}, u32[]{:S(2)}, u32[]{:S(2)}) collective-permute-start(bf16[512,1024]{1,0:T(8,128)(2,1)S(1)} %get-tuple-element.67.refs_0_.own_ref), channel_id=1, source_target_pairs={{4,0},{5,1},{6,2},{7,3},{8,4},{9,5},{10,6},{11,7},{12,8},{13,9},{1... | collective-permute-start | bytes 3145736 | tf_op jit(solution)/shard_map/ppermute | solution.py:27
  49.7 3.7 %collective-permute-start.17 = (bf16[128,1024]{1,0:T(8,128)(2,1)S(1)}, bf16[128,1024]{1,0:T(8,128)(2,1)S(1)}, u32[]{:S(2)}, u32[]{:S(2)}) collective-permute-start(bf16[128,1024]{1,0:T(8,128)(2,1)S(1)} %get-tuple-element.77), channel_id=1, source_target_pairs={{0,1},{1,0},{2,3},{3,2},{4,5},{5,4},{6,7},{7,6},{8,9},{9,8},{10,11... | collective-permute-start | bytes 786440 | tf_op jit(solution)/shard_map/ppermute | solution.py:32
  50.6 20.0 %collective-permute-start.18 = (bf16[256,1024]{1,0:T(8,128)(2,1)S(1)}, bf16[256,1024]{1,0:T(8,128)(2,1)S(1)}, u32[]{:S(2)}, u32[]{:S(2)}) collective-permute-start(bf16[256,1024]{1,0:T(8,128)(2,1)S(1)} %get-tuple-element.78), channel_id=1, source_target_pairs={{0,2},{1,3},{2,0},{3,1},{4,6},{5,7},{6,4},{7,5},{8,10},{9,11},{10,... | collective-permute-start | bytes 1572872 | tf_op jit(solution)/shard_map/ppermute | solution.py:32
  53.4 20.7 %collective-permute-start.21 = (bf16[256,1024]{1,0:T(8,128)(2,1)S(1)}, bf16[256,1024]{1,0:T(8,128)(2,1)S(1)}, u32[]{:S(2)}, u32[]{:S(2)}) collective-permute-start(bf16[256,1024]{1,0:T(8,128)(2,1)S(1)} %get-tuple-element.84), channel_id=1, source_target_pairs={{0,2},{1,3},{2,0},{3,1},{4,6},{5,7},{6,4},{7,5},{8,10},{9,11},{10,... | collective-permute-start | bytes 1572872 | tf_op jit(solution)/shard_map/ppermute | solution.py:32
  54.3 30.4 %collective-permute-start.14 = (bf16[512,1024]{1,0:T(8,128)(2,1)S(1)}, bf16[512,1024]{1,0:T(8,128)(2,1)S(1)}, u32[]{:S(2)}, u32[]{:S(2)}) collective-permute-start(bf16[512,1024]{1,0:T(8,128)(2,1)S(1)} %get-tuple-element.73.refs_0_.own_ref), channel_id=1, source_target_pairs={{0,4},{1,5},{2,6},{3,7},{4,8},{5,9},{6,10},{7,11},{8,12},{9,13},{1... | collective-permute-start | bytes 3145736 | tf_op jit(solution)/shard_map/ppermute | solution.py:27
  58.5 12.2 %collective-permute-start.20 = (bf16[128,1024]{1,0:T(8,128)(2,1)S(1)}, bf16[128,1024]{1,0:T(8,128)(2,1)S(1)}, u32[]{:S(2)}, u32[]{:S(2)}) collective-permute-start(bf16[128,1024]{1,0:T(8,128)(2,1)S(1)} %get-tuple-element.82), channel_id=1, source_target_pairs={{0,1},{1,0},{2,3},{3,2},{4,5},{5,4},{6,7},{7,6},{8,9},{9,8},{10,11... | collective-permute-start | bytes 786440 | tf_op jit(solution)/shard_map/ppermute | solution.py:32
  70.6 1.6 %collective-permute-start.19 = (bf16[128,1024]{1,0:T(8,128)(2,1)S(1)}, bf16[128,1024]{1,0:T(8,128)(2,1)S(1)}, u32[]{:S(2)}, u32[]{:S(2)}) collective-permute-start(bf16[128,1024]{1,0:T(8,128)(2,1)S(1)} %slice.10), channel_id=1, source_target_pairs={{0,1},{1,0},{2,3},{3,2},{4,5},{5,4},{6,7},{7,6},{8,9},{9,8},{10,11... | collective-permute-start | bytes 786440 | tf_op jit(solution)/shard_map/ppermute | solution.py:32
  70.7 14.1 %collective-permute-start.15 = (bf16[128,1024]{1,0:T(8,128)(2,1)S(1)}, bf16[128,1024]{1,0:T(8,128)(2,1)S(1)}, u32[]{:S(2)}, u32[]{:S(2)}) collective-permute-start(bf16[128,1024]{1,0:T(8,128)(2,1)S(1)} %get-tuple-element.76), channel_id=1, source_target_pairs={{4,0},{5,1},{6,2},{7,3},{8,4},{9,5},{10,6},{11,7},{12,8},{13,9},{1... | collective-permute-start | bytes 786440 | tf_op jit(solution)/shard_map/ppermute | solution.py:27
  76.2 8.6 %collective-permute-start.22 = (bf16[128,1024]{1,0:T(8,128)(2,1)S(1)}, bf16[128,1024]{1,0:T(8,128)(2,1)S(1)}, u32[]{:S(2)}, u32[]{:S(2)}) collective-permute-start(bf16[128,1024]{1,0:T(8,128)(2,1)S(1)} %get-tuple-element.86), channel_id=1, source_target_pairs={{4,0},{5,1},{6,2},{7,3},{8,4},{9,5},{10,6},{11,7},{12,8},{13,9},{1... | collective-permute-start | bytes 786440 | tf_op jit(solution)/shard_map/ppermute | solution.py:27
  77.5 25.0 %collective-permute-start.26 = (bf16[512,1024]{1,0:T(8,128)(2,1)S(1)}, bf16[512,1024]{1,0:T(8,128)(2,1)S(1)}, u32[]{:S(2)}, u32[]{:S(2)}) collective-permute-start(bf16[512,1024]{1,0:T(8,128)(2,1)S(1)} %get-tuple-element.85.refs_0_.own_ref), channel_id=1, source_target_pairs={{0,4},{1,5},{2,6},{3,7},{4,8},{5,9},{6,10},{7,11},{8,12},{9,13},{1... | collective-permute-start | bytes 3145736 | tf_op jit(solution)/shard_map/ppermute | solution.py:27
  82.3 4.6 %collective-permute-start.27 = (bf16[128,1024]{1,0:T(8,128)(2,1)S(1)}, bf16[128,1024]{1,0:T(8,128)(2,1)S(1)}, u32[]{:S(2)}, u32[]{:S(2)}) collective-permute-start(bf16[128,1024]{1,0:T(8,128)(2,1)S(1)} %slice.11), channel_id=1, source_target_pairs={{0,1},{1,0},{2,3},{3,2},{4,5},{5,4},{6,7},{7,6},{8,9},{9,8},{10,11... | collective-permute-start | bytes 786440 | tf_op jit(solution)/shard_map/ppermute | solution.py:32
  87.8 31.8 %collective-permute-start.31 = (bf16[128,8,512]{2,1,0:T(8,128)(2,1)S(1)}, bf16[128,8,512]{2,1,0:T(8,128)(2,1)S(1)}, u32[]{:S(2)}, u32[]{:S(2)}) collective-permute-start(bf16[128,8,512]{2,1,0:T(8,128)(2,1)S(1)} %shard_map.80.refs_1_.own_ref), channel_id=1, source_target_pairs={{7,3},{11,7},{15,11},{23,19},{27,23},{31,27}} | collective-permute-start | bytes 3145736 | tf_op jit(solution)/shard_map/ppermute | solution.py:27
  88.5 19.0 %collective-permute-start.23 = (bf16[256,1024]{1,0:T(8,128)(2,1)S(1)}, bf16[256,1024]{1,0:T(8,128)(2,1)S(1)}, u32[]{:S(2)}, u32[]{:S(2)}) collective-permute-start(bf16[256,1024]{1,0:T(8,128)(2,1)S(1)} %get-tuple-element.89), channel_id=1, source_target_pairs={{0,1},{1,0},{2,3},{3,2},{4,5},{5,4},{6,7},{7,6},{8,9},{9,8},{10,11... | collective-permute-start | bytes 1572872 | tf_op jit(solution)/shard_map/ppermute | solution.py:32
  91.3 17.3 %collective-permute-start.24 = (bf16[256,1024]{1,0:T(8,128)(2,1)S(1)}, bf16[256,1024]{1,0:T(8,128)(2,1)S(1)}, u32[]{:S(2)}, u32[]{:S(2)}) collective-permute-start(bf16[256,1024]{1,0:T(8,128)(2,1)S(1)} %get-tuple-element.90), channel_id=1, source_target_pairs={{0,2},{1,3},{2,0},{3,1},{4,6},{5,7},{6,4},{7,5},{8,10},{9,11},{10,... | collective-permute-start | bytes 1572872 | tf_op jit(solution)/shard_map/ppermute | solution.py:32
  92.4 24.3 %collective-permute-start.25 = (bf16[256,1024]{1,0:T(8,128)(2,1)S(1)}, bf16[256,1024]{1,0:T(8,128)(2,1)S(1)}, u32[]{:S(2)}, u32[]{:S(2)}) collective-permute-start(bf16[256,1024]{1,0:T(8,128)(2,1)S(1)} %get-tuple-element.91), channel_id=1, source_target_pairs={{0,3},{1,2},{2,1},{3,0},{4,7},{5,6},{6,5},{7,4},{8,11},{9,10},{10,... | collective-permute-start | bytes 1572872 | tf_op jit(solution)/shard_map/ppermute | solution.py:32
  104.5 17.8 %collective-permute-start.28 = (bf16[128,1024]{1,0:T(8,128)(2,1)S(1)}, bf16[128,1024]{1,0:T(8,128)(2,1)S(1)}, u32[]{:S(2)}, u32[]{:S(2)}) collective-permute-start(bf16[128,1024]{1,0:T(8,128)(2,1)S(1)} %get-tuple-element.95), channel_id=1, source_target_pairs={{0,1},{1,0},{2,3},{3,2},{4,5},{5,4},{6,7},{7,6},{8,9},{9,8},{10,11... | collective-permute-start | bytes 786440 | tf_op jit(solution)/shard_map/ppermute | solution.py:32
  107.6 14.7 %collective-permute-start.29 = (bf16[128,1024]{1,0:T(8,128)(2,1)S(1)}, bf16[128,1024]{1,0:T(8,128)(2,1)S(1)}, u32[]{:S(2)}, u32[]{:S(2)}) collective-permute-start(bf16[128,1024]{1,0:T(8,128)(2,1)S(1)} %get-tuple-element.96), channel_id=1, source_target_pairs={{0,2},{1,3},{2,0},{3,1},{4,6},{5,7},{6,4},{7,5},{8,10},{9,11},{10,... | collective-permute-start | bytes 786440 | tf_op jit(solution)/shard_map/ppermute | solution.py:32
  108.7 18.8 %collective-permute-start.30 = (bf16[128,1024]{1,0:T(8,128)(2,1)S(1)}, bf16[128,1024]{1,0:T(8,128)(2,1)S(1)}, u32[]{:S(2)}, u32[]{:S(2)}) collective-permute-start(bf16[128,1024]{1,0:T(8,128)(2,1)S(1)} %get-tuple-element.97), channel_id=1, source_target_pairs={{0,3},{1,2},{2,1},{3,0},{4,7},{5,6},{6,5},{7,4},{8,11},{9,10},{10,... | collective-permute-start | bytes 786440 | tf_op jit(solution)/shard_map/ppermute | solution.py:32

commit v18 on v17

--- a/solution.py
+++ b/solution.py
@@ -581,16 +581,16 @@
     low0 = moved(tied(edge0, s_near), G)
     own1, edge1 = pack(here, [(v0, 0), (near, 0), (over, 0), (swapped(over_beyond, 1), 0)], 0)
     low1, high1 = moved(edge1, G), moved(own1, -G)
-    sinos0 = [(s0, 0), (s_near, 0), (s_over, 0), (beyond(s_over, own1), 0)]
-
-    s0, s1, s23 = split_rows(here, sinogram, got1, 1, paired, [], own1)
-
-    resid0, down0, r1, r23 = project(here, band_p, own0, high0, low0, sinos0, paired[1:], low1, s0)
+    t0, t1, t23 = split_rows(here, sinogram, got1, 1, paired, [], own1)
+    sinos0 = [(s0, 0), (s_near, 0), (s_over, 0), (beyond(s_over, t0), 0)]
+
+
+    resid0, down0, r1, r23 = project(here, band_p, own0, high0, low0, sinos0, paired[1:], low1)
     from_low0, from_high0 = moved(resid0, G), moved(down0, -G)
-    s_near, s_over = swapped(s1, 1), swapped(s23, 2)
-    r_near, r_over = swapped(tied(r1, s_near), 1), swapped(tied(r23, s_near), 2)
+    t_near, t_over = swapped(t1, 1), swapped(t23, 2)
+    r_near, r_over = swapped(tied(r1, t_near), 1), swapped(tied(r23, t_near), 2)
     tv, tv_done = half_tv(here, volume, [got_vols0[1], high0, got_vols0[3], low0], resid0)
-    sinos1 = [(s0, 0), (s_near, 0), (s_over, 0), (beyond(s_over, tv_done), 0)]
+    sinos1 = [(t0, 0), (t_near, 0), (t_over, 0), (beyond(t_over, tv_done), 0)]
     resid1, down1 = project(here, band_p, own1, high1, low1, sinos1, (), tv_done, r_near, r_over)
     from_low1, from_high1 = moved(resid1, G), moved(down1, -G)
 

time: 131 us -> 131 us (level)
  starting transfers between devices: 49.6 us -> 46.9 us
  waiting for transfers between devices: 35 us -> 37.2 us
    ppermute x11, waiting for transfers between devices: 10.2 us -> 13.7 us  [moved(): return lax.ppermute(value, 'slab', pairs)]
    ppermute x11, starting transfers between devices: 22.7 us -> 21.1 us  [moved(): return lax.ppermute(value, 'slab', pairs)]
    ppermute x21, waiting for transfers between devices: 24.8 us -> 23.5 us  [swapped(): return lax.ppermute(value, 'slab', [(i, i ^ bits) for i in range(count)])]
  transfers between devices with their start and end apart: 32 -> 32, of which waited for: 10 -> 8; matrix products, arithmetic and copies ran while one was open for 1% -> 1% of each run, Pallas kernels for 28% -> 28%
where the time goes in v18:
time: 131 us; the launch traced here: 130 us
  starting transfers between devices  46.9 us (36%)
  Pallas kernels  42.3 us (32%)
  waiting for transfers between devices  37.2 us (28%)
  local copies, waits for them, and re-layouts  2.57 us (2%)
    ppermute x21, starting transfers between devices, swapped(): return lax.ppermute(value, 'slab', [(i, i ^ bits) for i in range(count)])  25.8 us
    ppermute x21, waiting for transfers between devices, swapped(): return lax.ppermute(value, 'slab', [(i, i ^ bits) for i in range(count)])  23.5 us
    ppermute x11, starting transfers between devices, moved(): return lax.ppermute(value, 'slab', pairs)  21.1 us
    ppermute x11, waiting for transfers between devices, moved(): return lax.ppermute(value, 'slab', pairs)  13.7 us
    pallas_call x1, Pallas kernels, half_tv(): call(tv_kernel, 0, grid=(depth // deep,), in_specs=[SMEM] + edges + [afte...  9.99 us
    pallas_call x2, Pallas kernels, cast_rows(): call(functools.partial(cast_kernel, groups, len(edges), halves), 2, grid=...  5.97 us
    pallas_call x2, Pallas kernels, finish(): call(finish_kernel, 0, grid=(count,), in_specs=[SMEM, part] + piece_specs...  5.85 us
    pallas_call x2, Pallas kernels, project(): call(functools.partial(project_kernel, groups), 3, grid=(cols // tile,),...  4.22 us
  transfers between devices with their start and end apart: 32, of which 8 were waited for; matrix products, arithmetic and copies ran while one was open for 1% of the time, Pallas kernels for 28%

profile of v18, /device:TPU:1, one launch (start us, length us, event | category | flops | bytes accessed | tf_op | source)
XLA Modules:
  0.0 129.8 jit_solution(7908748928510703378)
XLA Ops:
  0.6 2.5 %shard_map.68 = (bf16[128,1024]{1,0:T(8,128)(2,1)}, bf16[144,1024]{1,0:T(8,128)(2,1)S(1)}, bf16[128,1024]{1,0:T(8,128)(2,1)}, bf16[144,1024]{1,0:T(8,128)(2,1)S(1)}) custom-call(s32[1]{0:T(128)} %bitcast.here_ref, f32[1024,1024]{1,0:T(8,128)} %bitcast.2, f32[1024,1024]{1,0:T(8,128)} %bitcast.3, f32[1024,1024]{1,0:T(8,128)} %bitcast.4, f32[1024,1024]{1,0:T(8,128)} %bitcast.5), custom_call_target="tpu_custom_call" | custom-call | flops 2300000000 | bytes 1000 | tf_op jit(solution)/shard_map/pallas_call | solution.py:115
  3.2 2.7 %collective-permute-start.1 = (bf16[128,1024]{1,0:T(8,128)(2,1)}, bf16[128,1024]{1,0:T(8,128)(2,1)}, u32[]{:S(2)}, u32[]{:S(2)}) collective-permute-start(bf16[128,1024]{1,0:T(8,128)(2,1)} %get-tuple-element.52), channel_id=1, source_target_pairs={{0,2},{1,3},{2,0},{3,1},{4,6},{5,7},{6,4},{7,5},{8,10},{9,11},{10,... | collective-permute-start | bytes 786440 | tf_op jit(solution)/shard_map/ppermute | solution.py:32
  6.0 3.4 %shard_map.69 = (bf16[128,1024]{1,0:T(8,128)(2,1)}, bf16[128,1024]{1,0:T(8,128)(2,1)S(1)}, bf16[256,1024]{1,0:T(8,128)(2,1)}, bf16[128,8,512]{2,1,0:T(8,128)(2,1)}, bf16[128,8,512]{2,1,0:T(8,128)(2,1)S(1)}) custom-call(s32[1]{0:T(128)} %bitcast.here_ref, f32[1024,1024]{1,0:T(8,128)} %bitcast.6, f32[1024,1024]{1,0:T(8,128)} %bitcast.7, ...), custom_call_target="tpu_custom_call" | custom-call | flops 2300000000 | bytes 1000 | tf_op jit(solution)/shard_map/pallas_call | solution.py:115
  10.1 0.7 collective-permute-start.4
  10.8 4.2 %collective-permute-start.5 = (bf16[256,1024]{1,0:T(8,128)(2,1)}, bf16[256,1024]{1,0:T(8,128)(2,1)}, u32[]{:S(2)}, u32[]{:S(2)}) collective-permute-start(bf16[256,1024]{1,0:T(8,128)(2,1)} %get-tuple-element.59), channel_id=1, source_target_pairs={{0,2},{1,3},{2,0},{3,1},{4,6},{5,7},{6,4},{7,5},{8,10},{9,11},{10,... | collective-permute-start | bytes 1572872 | tf_op jit(solution)/shard_map/ppermute | solution.py:32
  15.1 0.8 copy.13.offset_ref
  15.9 0.9 copy-done.4
  16.8 1.6 %shard_map.70 = (bf16[512,1152]{1,0:T(8,128)(2,1)S(1)}, bf16[512,1152]{1,0:T(8,128)(2,1)S(1)}) custom-call(s32[1]{0:T(128)} %bitcast.here_ref, s32[16,6]{1,0:T(8,128)S(1)} %copy.12.cover_ref, s32[16,6]{1,0:T(8,128)S(1)} %copy.13.offset_ref, bf16[8,128,128]{2,1,0:T(8,128)(2,1)S(1)} %copy-done, bf16[128,1024]{1,0:T(8,128)(2,1)S(1)} %copy-done.4), custom_call_target="tpu_custom_call" | custom-call | flops 10350000128 | bytes 1000 | tf_op jit(solution)/shard_map/pallas_call | solution.py:415
  18.5 0.7 collective-permute-start.10
  19.3 1.2 shard_map.71
  20.7 1.3 collective-permute-start.3
  22.0 8.4 %collective-permute-done.5.refs_0_.refs_2_ = bf16[256,1024]{1,0:T(8,128)(2,1)} collective-permute-done((bf16[256,1024]{1,0:T(8,128)(2,1)}, bf16[256,1024]{1,0:T(8,128)(2,1)}, u32[]{:S(2)}, u32[]{:S(2)}) %collective-permute-start.5) | collective-permute-done | bytes 524320 | tf_op jit(solution)/shard_map/ppermute | solution.py:32
  30.4 1.8 %shard_map.72 = (bf16[128,1024]{1,0:T(8,128)(2,1)S(1)}, bf16[128,1024]{1,0:T(8,128)(2,1)S(1)}, bf16[256,1024]{1,0:T(8,128)(2,1)S(1)}, bf16[128,1024]{1,0:T(8,128)(2,1)S(1)}) custom-call(s32[1]{0:T(128)} %bitcast.here_ref, bf16[128,8,1024]{2,1,0:T(8,128)(2,1)} %refs_2_.3, bf16[128,8,512]{2,1,0:T(8,128)(2,1)S(1)} %collective-permute-done.4.got_ref, ...), custom_call_target="tpu_custom_call" | custom-call | flops 2300000000 | bytes 1000 | tf_op jit(solution)/shard_map/pallas_call | solution.py:196
  33.0 1.5 %collective-permute-start.9 = (bf16[256,1024]{1,0:T(8,128)(2,1)S(1)}, bf16[256,1024]{1,0:T(8,128)(2,1)S(1)}, u32[]{:S(2)}, u32[]{:S(2)}) collective-permute-start(bf16[256,1024]{1,0:T(8,128)(2,1)S(1)} %get-tuple-element.64), channel_id=1, source_target_pairs={{0,2},{1,3},{2,0},{3,1},{4,6},{5,7},{6,4},{7,5},{8,10},{9,11},{10,... | collective-permute-start | bytes 1572872 | tf_op jit(solution)/shard_map/ppermute | solution.py:32
  34.5 3.2 %collective-permute-start.8 = (bf16[144,1024]{1,0:T(8,128)(2,1)S(1)}, bf16[144,1024]{1,0:T(8,128)(2,1)S(1)}, u32[]{:S(2)}, u32[]{:S(2)}) collective-permute-start(bf16[144,1024]{1,0:T(8,128)(2,1)S(1)} %get-tuple-element.62), channel_id=1, source_target_pairs={{0,4},{1,5},{2,6},{3,7},{4,8},{5,9},{6,10},{7,11},{8,12},{9,13},{1... | collective-permute-start | bytes 884744 | tf_op jit(solution)/shard_map/ppermute | solution.py:27
  37.7 1.2 shard_map.73
  38.9 3.2 %collective-permute-start.13 = (bf16[128,1024]{1,0:T(8,128)(2,1)S(1)}, bf16[128,1024]{1,0:T(8,128)(2,1)S(1)}, u32[]{:S(2)}, u32[]{:S(2)}) collective-permute-start(bf16[128,1024]{1,0:T(8,128)(2,1)S(1)} %get-tuple-element.72), channel_id=1, source_target_pairs={{0,4},{1,5},{2,6},{3,7},{4,8},{5,9},{6,10},{7,11},{8,12},{9,13},{1... | collective-permute-start | bytes 786440 | tf_op jit(solution)/shard_map/ppermute | solution.py:27
  42.1 1.7 %shard_map.74 = (bf16[128,1024]{1,0:T(8,128)(2,1)S(1)}, bf16[128,1024]{1,0:T(8,128)(2,1)S(1)}, bf16[256,1024]{1,0:T(8,128)(2,1)S(1)}) custom-call(s32[1]{0:T(128)} %bitcast.here_ref, bf16[128,8,1024]{2,1,0:T(8,128)(2,1)} %refs_2_.3, bf16[128,8,512]{2,1,0:T(8,128)(2,1)S(1)} %collective-permute-done.10.got_ref, ...), custom_call_target="tpu_custom_call" | custom-call | flops 2300000000 | bytes 1000 | tf_op jit(solution)/shard_map/pallas_call | solution.py:196
  43.8 2.2 %collective-permute-done.9.refs_2_ = bf16[256,1024]{1,0:T(8,128)(2,1)S(1)} collective-permute-done((bf16[256,1024]{1,0:T(8,128)(2,1)S(1)}, bf16[256,1024]{1,0:T(8,128)(2,1)S(1)}, u32[]{:S(2)}, u32[]{:S(2)}) %collective-permute-start.9) | collective-permute-done | bytes 524320 | tf_op jit(solution)/shard_map/ppermute | solution.py:32
  46.1 1.3 %collective-permute-start.12 = (bf16[128,1024]{1,0:T(8,128)(2,1)S(1)}, bf16[128,1024]{1,0:T(8,128)(2,1)S(1)}, u32[]{:S(2)}, u32[]{:S(2)}) collective-permute-start(bf16[128,1024]{1,0:T(8,128)(2,1)S(1)} %slice.9), channel_id=1, source_target_pairs={{0,1},{1,0},{2,3},{3,2},{4,5},{5,4},{6,7},{7,6},{8,9},{9,8},{10,11... | collective-permute-start | bytes 786440 | tf_op jit(solution)/shard_map/ppermute | solution.py:32
  47.4 1.3 collective-permute-start.16
  49.0 2.2 %collective-permute-start.18 = (bf16[256,1024]{1,0:T(8,128)(2,1)S(1)}, bf16[256,1024]{1,0:T(8,128)(2,1)S(1)}, u32[]{:S(2)}, u32[]{:S(2)}) collective-permute-start(bf16[256,1024]{1,0:T(8,128)(2,1)S(1)} %get-tuple-element.78), channel_id=1, source_target_pairs={{0,2},{1,3},{2,0},{3,1},{4,6},{5,7},{6,4},{7,5},{8,10},{9,11},{10,... | collective-permute-start | bytes 1572872 | tf_op jit(solution)/shard_map/ppermute | solution.py:32
  51.3 2.1 %shard_map.75 = (bf16[512,1024]{1,0:T(8,128)(2,1)S(1)}, bf16[128,1024]{1,0:T(8,128)(2,1)S(1)}, bf16[128,1024]{1,0:T(8,128)(2,1)S(1)}, bf16[256,1024]{1,0:T(8,128)(2,1)S(1)}) custom-call(s32[1]{0:T(128)} %bitcast.here_ref, bf16[512,1152]{1,0:T(8,128)(2,1)S(1)} %get-tuple-element.55.refs_4_.band_ref, bf16[528,1024]{1,0:T(8,128)(2,1)S(1)} %get-tuple-element.56.own_ref, ...), custom_call_target="tpu_custom_call" | custom-call | flops 3449999872 | bytes 1000 | tf_op jit(solution)/shard_map/pallas_call | solution.py:446
  53.5 3.3 %collective-permute-start.14 = (bf16[512,1024]{1,0:T(8,128)(2,1)S(1)}, bf16[512,1024]{1,0:T(8,128)(2,1)S(1)}, u32[]{:S(2)}, u32[]{:S(2)}) collective-permute-start(bf16[512,1024]{1,0:T(8,128)(2,1)S(1)} %get-tuple-element.73.refs_0_.own_ref), channel_id=1, source_target_pairs={{0,4},{1,5},{2,6},{3,7},{4,8},{5,9},{6,10},{7,11},{8,12},{9,13},{1... | collective-permute-start | bytes 3145736 | tf_op jit(solution)/shard_map/ppermute | solution.py:27
  56.9 2.4 %collective-permute-start.20 = (bf16[128,1024]{1,0:T(8,128)(2,1)S(1)}, bf16[128,1024]{1,0:T(8,128)(2,1)S(1)}, u32[]{:S(2)}, u32[]{:S(2)}) collective-permute-start(bf16[128,1024]{1,0:T(8,128)(2,1)S(1)} %get-tuple-element.82), channel_id=1, source_target_pairs={{0,1},{1,0},{2,3},{3,2},{4,5},{5,4},{6,7},{7,6},{8,9},{9,8},{10,11... | collective-permute-start | bytes 786440 | tf_op jit(solution)/shard_map/ppermute | solution.py:32
  59.3 10.0 %shard_map.76 = (f32[128,8,1024]{2,1,0:T(8,128)}, f32[8,128]{1,0:T(8,128)S(1)}) custom-call(s32[1]{0:T(128)} %bitcast.here_ref, bf16[144,1024]{1,0:T(8,128)(2,1)S(1)} %collective-permute-done.refs_1_.near_ref, bf16[528,1024]{1,0:T(8,128)(2,1)S(1)} %collective-permute-done.3.high_ref.next_level_ref, ...), custom_call_target="tpu_custom_call" | custom-call | bytes 1000 | tf_op jit(solution)/shard_map/pallas_call | solution.py:546
  69.4 1.3 collective-permute-start.15
  70.9 3.3 %collective-permute-done.16.high_ref = bf16[512,1024]{1,0:T(8,128)(2,1)S(1)} collective-permute-done((bf16[512,1024]{1,0:T(8,128)(2,1)S(1)}, bf16[512,1024]{1,0:T(8,128)(2,1)S(1)}, u32[]{:S(2)}, u32[]{:S(2)}) %collective-permute-start.16) | collective-permute-done | bytes 1048608 | tf_op jit(solution)/shard_map/ppermute | solution.py:27
  74.2 2.1 %shard_map.77 = (bf16[512,1024]{1,0:T(8,128)(2,1)S(1)}, bf16[128,1024]{1,0:T(8,128)(2,1)S(1)}) custom-call(s32[1]{0:T(128)} %bitcast.here_ref, bf16[512,1152]{1,0:T(8,128)(2,1)S(1)} %get-tuple-element.55.refs_4_.band_ref, bf16[512,1024]{1,0:T(8,128)(2,1)S(1)} %get-tuple-element.69.refs_0_.own_ref, bf16[512,1024]{1,0:T(8,128)(2,1)S(1)} %collective-permute-done.16.high_ref, ...), custom_call_target="tpu_custom_call" | custom-call | flops 3449999872 | bytes 1000 | tf_op jit(solution)/shard_map/pallas_call | solution.py:446
  76.3 1.3 collective-permute-start.22
  77.6 4.1 %collective-permute-start.26 = (bf16[512,1024]{1,0:T(8,128)(2,1)S(1)}, bf16[512,1024]{1,0:T(8,128)(2,1)S(1)}, u32[]{:S(2)}, u32[]{:S(2)}) collective-permute-start(bf16[512,1024]{1,0:T(8,128)(2,1)S(1)} %get-tuple-element.85.refs_0_.own_ref), channel_id=1, source_target_pairs={{0,4},{1,5},{2,6},{3,7},{4,8},{5,9},{6,10},{7,11},{8,12},{9,13},{1... | collective-permute-start | bytes 3145736 | tf_op jit(solution)/shard_map/ppermute | solution.py:27
  81.7 1.8 %collective-permute-start.27 = (bf16[128,1024]{1,0:T(8,128)(2,1)S(1)}, bf16[128,1024]{1,0:T(8,128)(2,1)S(1)}, u32[]{:S(2)}, u32[]{:S(2)}) collective-permute-start(bf16[128,1024]{1,0:T(8,128)(2,1)S(1)} %slice.11), channel_id=1, source_target_pairs={{0,1},{1,0},{2,3},{3,2},{4,5},{5,4},{6,7},{7,6},{8,9},{9,8},{10,11... | collective-permute-start | bytes 786440 | tf_op jit(solution)/shard_map/ppermute | solution.py:32
  83.5 1.4 %collective-permute-done.22.refs_1_.high_ref = bf16[128,1024]{1,0:T(8,128)(2,1)S(1)} collective-permute-done((bf16[128,1024]{1,0:T(8,128)(2,1)S(1)}, bf16[128,1024]{1,0:T(8,128)(2,1)S(1)}, u32[]{:S(2)}, u32[]{:S(2)}) %collective-permute-start.22) | collective-permute-done | bytes 262176 | tf_op jit(solution)/shard_map/ppermute | solution.py:27
  84.8 2.1 %shard_map.78 = (bf16[256,1024]{1,0:T(8,128)(2,1)S(1)}, bf16[256,1024]{1,0:T(8,128)(2,1)S(1)}, bf16[256,1024]{1,0:T(8,128)(2,1)S(1)}, bf16[256,1024]{1,0:T(8,128)(2,1)S(1)}) custom-call(s32[1]{0:T(128)} %bitcast.here_ref, bf16[512,1152]{1,0:T(8,128)(2,1)S(1)} %get-tuple-element.75.band_ref, bf16[512,1024]{1,0:T(8,128)(2,1)S(1)} %get-tuple-element.73.refs_0_.own_ref, ...), custom_call_target="tpu_custom_call" | custom-call | bytes 1000 | tf_op jit(solution)/shard_map/pallas_call | solution.py:478
  87.0 0.9 shard_map.80.refs_1_.own_ref
  87.8 0.7 collective-permute-start.31
  88.6 2.1 %collective-permute-start.23 = (bf16[256,1024]{1,0:T(8,128)(2,1)S(1)}, bf16[256,1024]{1,0:T(8,128)(2,1)S(1)}, u32[]{:S(2)}, u32[]{:S(2)}) collective-permute-start(bf16[256,1024]{1,0:T(8,128)(2,1)S(1)} %get-tuple-element.89), channel_id=1, source_target_pairs={{0,1},{1,0},{2,3},{3,2},{4,5},{5,4},{6,7},{7,6},{8,9},{9,8},{10,11... | collective-permute-start | bytes 1572872 | tf_op jit(solution)/shard_map/ppermute | solution.py:32
  90.7 1.5 %collective-permute-start.24 = (bf16[256,1024]{1,0:T(8,128)(2,1)S(1)}, bf16[256,1024]{1,0:T(8,128)(2,1)S(1)}, u32[]{:S(2)}, u32[]{:S(2)}) collective-permute-start(bf16[256,1024]{1,0:T(8,128)(2,1)S(1)} %get-tuple-element.90), channel_id=1, source_target_pairs={{0,2},{1,3},{2,0},{3,1},{4,6},{5,7},{6,4},{7,5},{8,10},{9,11},{10,... | collective-permute-start | bytes 1572872 | tf_op jit(solution)/shard_map/ppermute | solution.py:32
  92.4 1.2 shard_map.79
  93.6 9.0 %collective-permute-done.26.low_ref = bf16[512,1024]{1,0:T(8,128)(2,1)S(1)} collective-permute-done((bf16[512,1024]{1,0:T(8,128)(2,1)S(1)}, bf16[512,1024]{1,0:T(8,128)(2,1)S(1)}, u32[]{:S(2)}, u32[]{:S(2)}) %collective-permute-start.26) | collective-permute-done | bytes 1048608 | tf_op jit(solution)/shard_map/ppermute | solution.py:27
  102.6 2.0 %shard_map.81 = (bf16[128,1024]{1,0:T(8,128)(2,1)S(1)}, bf16[128,1024]{1,0:T(8,128)(2,1)S(1)}, bf16[128,1024]{1,0:T(8,128)(2,1)S(1)}, bf16[128,1024]{1,0:T(8,128)(2,1)S(1)}) custom-call(s32[1]{0:T(128)} %bitcast.here_ref, bf16[512,1152]{1,0:T(8,128)(2,1)S(1)} %get-tuple-element.75.band_ref, bf16[512,1024]{1,0:T(8,128)(2,1)S(1)} %get-tuple-element.85.refs_0_.own_ref, ...), custom_call_target="tpu_custom_call" | custom-call | bytes 1000 | tf_op jit(solution)/shard_map/pallas_call | solution.py:478
  104.5 2.4 %collective-permute-start.28 = (bf16[128,1024]{1,0:T(8,128)(2,1)S(1)}, bf16[128,1024]{1,0:T(8,128)(2,1)S(1)}, u32[]{:S(2)}, u32[]{:S(2)}) collective-permute-start(bf16[128,1024]{1,0:T(8,128)(2,1)S(1)} %get-tuple-element.95), channel_id=1, source_target_pairs={{0,1},{1,0},{2,3},{3,2},{4,5},{5,4},{6,7},{7,6},{8,9},{9,8},{10,11... | collective-permute-start | bytes 786440 | tf_op jit(solution)/shard_map/ppermute | solution.py:32
  107.0 1.5 %collective-permute-start.29 = (bf16[128,1024]{1,0:T(8,128)(2,1)S(1)}, bf16[128,1024]{1,0:T(8,128)(2,1)S(1)}, u32[]{:S(2)}, u32[]{:S(2)}) collective-permute-start(bf16[128,1024]{1,0:T(8,128)(2,1)S(1)} %get-tuple-element.96), channel_id=1, source_target_pairs={{0,2},{1,3},{2,0},{3,1},{4,6},{5,7},{6,4},{7,5},{8,10},{9,11},{10,... | collective-permute-start | bytes 786440 | tf_op jit(solution)/shard_map/ppermute | solution.py:32
  108.7 7.4 %collective-permute-done.25.refs_3_ = bf16[256,1024]{1,0:T(8,128)(2,1)S(1)} collective-permute-done((bf16[256,1024]{1,0:T(8,128)(2,1)S(1)}, bf16[256,1024]{1,0:T(8,128)(2,1)S(1)}, u32[]{:S(2)}, u32[]{:S(2)}) %collective-permute-start.25) | collective-permute-done | bytes 524320 | tf_op jit(solution)/shard_map/ppermute | solution.py:32
  116.1 2.9 %shard_map.82.tv_ref = f32[128,8,1024]{2,1,0:T(8,128)} custom-call(s32[1]{0:T(128)} %bitcast.here_ref, f32[128,8,1024]{2,1,0:T(8,128)} %get-tuple-element.88.tv_ref, bf16[256,1024]{1,0:T(8,128)(2,1)S(1)} %get-tuple-element.87.refs_4_.refs_0_, bf16[256,1024]{1,0:T(8,128)(2,1)S(1)} %collective-permute-done.23.refs_1_, ...), custom_call_target="tpu_custom_call", output_to_operand_aliasing={{}: (1, {})} | custom-call | bytes 1000 | tf_op jit(solution)/shard_map/pallas_call | solution.py:367
  119.0 2.6 %shard_map.83.refs_4_ = bf16[128,8,1024]{2,1,0:T(8,128)(2,1)} custom-call(s32[1]{0:T(128)} %bitcast.here_ref, bf16[128,8,512]{2,1,0:T(8,128)(2,1)S(1)} %shard_map.80.refs_1_.own_ref, bf16[128,8,512]{2,1,0:T(8,128)(2,1)S(1)} %collective-permute-done.31.above_ref, bf16[256,1024]{1,0:T(8,128)(2,1)S(1)} %get-tuple-element.87.refs_4_.refs_0_, ...), custom_call_target="tpu_custom_call" | custom-call | bytes 1000 | tf_op jit(solution)/shard_map/pallas_call | solution.py:345
  121.6 5.3 %collective-permute-done.30.refs_3_ = bf16[128,1024]{1,0:T(8,128)(2,1)S(1)} collective-permute-done((bf16[128,1024]{1,0:T(8,128)(2,1)S(1)}, bf16[128,1024]{1,0:T(8,128)(2,1)S(1)}, u32[]{:S(2)}, u32[]{:S(2)}) %collective-permute-start.30) | collective-permute-done | bytes 262176 | tf_op jit(solution)/shard_map/ppermute | solution.py:32
  126.9 2.9 %shard_map.84 = f32[128,8,1024]{2,1,0:T(8,128)} custom-call(s32[1]{0:T(128)} %bitcast.here_ref, f32[128,8,1024]{2,1,0:T(8,128)} %shard_map.82.tv_ref, bf16[128,1024]{1,0:T(8,128)(2,1)S(1)} %get-tuple-element.94.refs_4_.refs_0_, bf16[128,1024]{1,0:T(8,128)(2,1)S(1)} %collective-permute-done.28.refs_1_, ...), custom_call_target="tpu_custom_call", output_to_operand_aliasing={{}: (1, {})} | custom-call | bytes 1000 | tf_op jit(solution)/shard_map/pallas_call | solution.py:367
  (52 shorter events, 3.2 us)
Async XLA Ops:
  3.2 16.1 %collective-permute-start = (bf16[144,1024]{1,0:T(8,128)(2,1)S(1)}, bf16[144,1024]{1,0:T(8,128)(2,1)S(1)}, u32[]{:S(2)}, u32[]{:S(2)}) collective-permute-start(bf16[144,1024]{1,0:T(8,128)(2,1)S(1)} %get-tuple-element.50.refs_4_), channel_id=1, source_target_pairs={{0,1},{1,0},{2,3},{3,2},{4,5},{5,4},{6,7},{7,6},{8,9},{9,8},{10,11... | collective-permute-start | bytes 884744 | tf_op jit(solution)/shard_map/ppermute | solution.py:32
  3.2 15.3 %collective-permute-start.1 = (bf16[128,1024]{1,0:T(8,128)(2,1)}, bf16[128,1024]{1,0:T(8,128)(2,1)}, u32[]{:S(2)}, u32[]{:S(2)}) collective-permute-start(bf16[128,1024]{1,0:T(8,128)(2,1)} %get-tuple-element.52), channel_id=1, source_target_pairs={{0,2},{1,3},{2,0},{3,1},{4,6},{5,7},{6,4},{7,5},{8,10},{9,11},{10,... | collective-permute-start | bytes 786440 | tf_op jit(solution)/shard_map/ppermute | solution.py:32
  5.9 9.1 %copy-start.6 = (s32[16,6]{0,1:T(8,128)S(1)}, s32[16,6]{0,1:T(8,128)}, u32[]{:S(2)}) copy-start(s32[16,6]{0,1:T(8,128)} %param.8) | copy-start | bytes 1156
  5.9 10.0 %copy-start = (bf16[8,128,128]{2,1,0:T(8,128)(2,1)S(1)}, bf16[8,128,128]{2,1,0:T(8,128)(2,1)}, u32[]{:S(2)}) copy-start(bf16[8,128,128]{2,1,0:T(8,128)(2,1)} %refs_0_.1) | copy-start | bytes 786436
  5.9 13.3 %collective-permute-start.2 = (bf16[144,1024]{1,0:T(8,128)(2,1)S(1)}, bf16[144,1024]{1,0:T(8,128)(2,1)S(1)}, u32[]{:S(2)}, u32[]{:S(2)}) collective-permute-start(bf16[144,1024]{1,0:T(8,128)(2,1)S(1)} %get-tuple-element.53), channel_id=1, source_target_pairs={{0,3},{1,2},{2,1},{3,0},{4,7},{5,6},{6,5},{7,4},{8,11},{9,10},{10,... | collective-permute-start | bytes 884744 | tf_op jit(solution)/shard_map/ppermute | solution.py:32
  9.4 0.7 copy-start.3
  10.1 20.3 %collective-permute-start.4 = (bf16[128,8,512]{2,1,0:T(8,128)(2,1)}, bf16[128,8,512]{2,1,0:T(8,128)(2,1)S(1)}, u32[]{:S(2)}, u32[]{:S(2)}) collective-permute-start(bf16[128,8,512]{2,1,0:T(8,128)(2,1)} %get-tuple-element.58), channel_id=1, source_target_pairs={{3,7},{7,11},{11,15},{19,23},{23,27},{27,31}} | collective-permute-start | bytes 3145736 | tf_op jit(solution)/shard_map/ppermute | solution.py:27
  10.8 19.6 %collective-permute-start.5 = (bf16[256,1024]{1,0:T(8,128)(2,1)}, bf16[256,1024]{1,0:T(8,128)(2,1)}, u32[]{:S(2)}, u32[]{:S(2)}) collective-permute-start(bf16[256,1024]{1,0:T(8,128)(2,1)} %get-tuple-element.59), channel_id=1, source_target_pairs={{0,2},{1,3},{2,0},{3,1},{4,6},{5,7},{6,4},{7,5},{8,10},{9,11},{10,... | collective-permute-start | bytes 1572872 | tf_op jit(solution)/shard_map/ppermute | solution.py:32
  15.9 1.0 copy-start.4
  16.8 2.4 %copy-start.2 = (bf16[128,1024]{1,0:T(8,128)(2,1)S(1)}, bf16[128,1024]{1,0:T(8,128)(2,1)}, u32[]{:S(2)}) copy-start(bf16[128,1024]{1,0:T(8,128)(2,1)} %get-tuple-element.51.refs_0_) | copy-start | bytes 786436
  18.5 23.6 %collective-permute-start.10 = (bf16[128,8,512]{2,1,0:T(8,128)(2,1)S(1)}, bf16[128,8,512]{2,1,0:T(8,128)(2,1)S(1)}, u32[]{:S(2)}, u32[]{:S(2)}) collective-permute-start(bf16[128,8,512]{2,1,0:T(8,128)(2,1)S(1)} %get-tuple-element.66), channel_id=1, source_target_pairs={{3,7},{7,11},{11,15},{19,23},{23,27},{27,31}} | collective-permute-start | bytes 3145736 | tf_op jit(solution)/shard_map/ppermute | solution.py:27
  19.3 1.2 copy-start.5
  20.5 17.2 %copy-start.1 = (bf16[128,1024]{1,0:T(8,128)(2,1)S(1)}, bf16[128,1024]{1,0:T(8,128)(2,1)}, u32[]{:S(2)}) copy-start(bf16[128,1024]{1,0:T(8,128)(2,1)} %get-tuple-element.67.refs_0_) | copy-start | bytes 786436
  20.5 9.9 %collective-permute-start.6 = (bf16[128,1024]{1,0:T(8,128)(2,1)S(1)}, bf16[128,1024]{1,0:T(8,128)(2,1)S(1)}, u32[]{:S(2)}, u32[]{:S(2)}) collective-permute-start(bf16[128,1024]{1,0:T(8,128)(2,1)S(1)} %copy-done.5), channel_id=1, source_target_pairs={{0,1},{1,0},{2,3},{3,2},{4,5},{5,4},{6,7},{7,6},{8,9},{9,8},{10,11... | collective-permute-start | bytes 786440 | tf_op jit(solution)/shard_map/ppermute | solution.py:32
  20.7 28.0 %collective-permute-start.3 = (bf16[528,1024]{1,0:T(8,128)(2,1)S(1)}, bf16[528,1024]{1,0:T(8,128)(2,1)S(1)}, u32[]{:S(2)}, u32[]{:S(2)}) collective-permute-start(bf16[528,1024]{1,0:T(8,128)(2,1)S(1)} %get-tuple-element.56.own_ref), channel_id=1, source_target_pairs={{4,0},{5,1},{6,2},{7,3},{8,4},{9,5},{10,6},{11,7},{12,8},{13,9},{1... | collective-permute-start | bytes 3244040 | tf_op jit(solution)/shard_map/ppermute | solution.py:27
  32.2 2.3 %collective-permute-start.7 = (bf16[128,1024]{1,0:T(8,128)(2,1)S(1)}, bf16[128,1024]{1,0:T(8,128)(2,1)S(1)}, u32[]{:S(2)}, u32[]{:S(2)}) collective-permute-start(bf16[128,1024]{1,0:T(8,128)(2,1)S(1)} %get-tuple-element.61), channel_id=1, source_target_pairs={{0,1},{1,0},{2,3},{3,2},{4,5},{5,4},{6,7},{7,6},{8,9},{9,8},{10,11... | collective-permute-start | bytes 786440 | tf_op jit(solution)/shard_map/ppermute | solution.py:32
  32.9 4.8 %collective-permute-start.11 = (bf16[128,1024]{1,0:T(8,128)(2,1)S(1)}, bf16[128,1024]{1,0:T(8,128)(2,1)S(1)}, u32[]{:S(2)}, u32[]{:S(2)}) collective-permute-start(bf16[128,1024]{1,0:T(8,128)(2,1)S(1)} %get-tuple-element.68), channel_id=1, source_target_pairs={{0,1},{1,0},{2,3},{3,2},{4,5},{5,4},{6,7},{7,6},{8,9},{9,8},{10,11... | collective-permute-start | bytes 786440 | tf_op jit(solution)/shard_map/ppermute | solution.py:32
  33.0 13.1 %collective-permute-start.9 = (bf16[256,1024]{1,0:T(8,128)(2,1)S(1)}, bf16[256,1024]{1,0:T(8,128)(2,1)S(1)}, u32[]{:S(2)}, u32[]{:S(2)}) collective-permute-start(bf16[256,1024]{1,0:T(8,128)(2,1)S(1)} %get-tuple-element.64), channel_id=1, source_target_pairs={{0,2},{1,3},{2,0},{3,1},{4,6},{5,7},{6,4},{7,5},{8,10},{9,11},{10,... | collective-permute-start | bytes 1572872 | tf_op jit(solution)/shard_map/ppermute | solution.py:32
  34.5 16.8 %collective-permute-start.8 = (bf16[144,1024]{1,0:T(8,128)(2,1)S(1)}, bf16[144,1024]{1,0:T(8,128)(2,1)S(1)}, u32[]{:S(2)}, u32[]{:S(2)}) collective-permute-start(bf16[144,1024]{1,0:T(8,128)(2,1)S(1)} %get-tuple-element.62), channel_id=1, source_target_pairs={{0,4},{1,5},{2,6},{3,7},{4,8},{5,9},{6,10},{7,11},{8,12},{9,13},{1... | collective-permute-start | bytes 884744 | tf_op jit(solution)/shard_map/ppermute | solution.py:27
  38.9 10.1 %collective-permute-start.13 = (bf16[128,1024]{1,0:T(8,128)(2,1)S(1)}, bf16[128,1024]{1,0:T(8,128)(2,1)S(1)}, u32[]{:S(2)}, u32[]{:S(2)}) collective-permute-start(bf16[128,1024]{1,0:T(8,128)(2,1)S(1)} %get-tuple-element.72), channel_id=1, source_target_pairs={{0,4},{1,5},{2,6},{3,7},{4,8},{5,9},{6,10},{7,11},{8,12},{9,13},{1... | collective-permute-start | bytes 786440 | tf_op jit(solution)/shard_map/ppermute | solution.py:27
  46.1 5.2 %collective-permute-start.12 = (bf16[128,1024]{1,0:T(8,128)(2,1)S(1)}, bf16[128,1024]{1,0:T(8,128)(2,1)S(1)}, u32[]{:S(2)}, u32[]{:S(2)}) collective-permute-start(bf16[128,1024]{1,0:T(8,128)(2,1)S(1)} %slice.9), channel_id=1, source_target_pairs={{0,1},{1,0},{2,3},{3,2},{4,5},{5,4},{6,7},{7,6},{8,9},{9,8},{10,11... | collective-permute-start | bytes 786440 | tf_op jit(solution)/shard_map/ppermute | solution.py:32
  47.4 26.8 %collective-permute-start.16 = (bf16[512,1024]{1,0:T(8,128)(2,1)S(1)}, bf16[512,1024]{1,0:T(8,128)(2,1)S(1)}, u32[]{:S(2)}, u32[]{:S(2)}) collective-permute-start(bf16[512,1024]{1,0:T(8,128)(2,1)S(1)} %get-tuple-element.69.refs_0_.own_ref), channel_id=1, source_target_pairs={{4,0},{5,1},{6,2},{7,3},{8,4},{9,5},{10,6},{11,7},{12,8},{13,9},{1... | collective-permute-start | bytes 3145736 | tf_op jit(solution)/shard_map/ppermute | solution.py:27
  48.7 4.7 %collective-permute-start.17 = (bf16[128,1024]{1,0:T(8,128)(2,1)S(1)}, bf16[128,1024]{1,0:T(8,128)(2,1)S(1)}, u32[]{:S(2)}, u32[]{:S(2)}) collective-permute-start(bf16[128,1024]{1,0:T(8,128)(2,1)S(1)} %get-tuple-element.77), channel_id=1, source_target_pairs={{0,1},{1,0},{2,3},{3,2},{4,5},{5,4},{6,7},{7,6},{8,9},{9,8},{10,11... | collective-permute-start | bytes 786440 | tf_op jit(solution)/shard_map/ppermute | solution.py:32
  49.0 20.2 %collective-permute-start.18 = (bf16[256,1024]{1,0:T(8,128)(2,1)S(1)}, bf16[256,1024]{1,0:T(8,128)(2,1)S(1)}, u32[]{:S(2)}, u32[]{:S(2)}) collective-permute-start(bf16[256,1024]{1,0:T(8,128)(2,1)S(1)} %get-tuple-element.78), channel_id=1, source_target_pairs={{0,2},{1,3},{2,0},{3,1},{4,6},{5,7},{6,4},{7,5},{8,10},{9,11},{10,... | collective-permute-start | bytes 1572872 | tf_op jit(solution)/shard_map/ppermute | solution.py:32
  53.4 20.8 %collective-permute-start.21 = (bf16[256,1024]{1,0:T(8,128)(2,1)S(1)}, bf16[256,1024]{1,0:T(8,128)(2,1)S(1)}, u32[]{:S(2)}, u32[]{:S(2)}) collective-permute-start(bf16[256,1024]{1,0:T(8,128)(2,1)S(1)} %get-tuple-element.84), channel_id=1, source_target_pairs={{0,2},{1,3},{2,0},{3,1},{4,6},{5,7},{6,4},{7,5},{8,10},{9,11},{10,... | collective-permute-start | bytes 1572872 | tf_op jit(solution)/shard_map/ppermute | solution.py:32
  53.5 31.3 %collective-permute-start.14 = (bf16[512,1024]{1,0:T(8,128)(2,1)S(1)}, bf16[512,1024]{1,0:T(8,128)(2,1)S(1)}, u32[]{:S(2)}, u32[]{:S(2)}) collective-permute-start(bf16[512,1024]{1,0:T(8,128)(2,1)S(1)} %get-tuple-element.73.refs_0_.own_ref), channel_id=1, source_target_pairs={{0,4},{1,5},{2,6},{3,7},{4,8},{5,9},{6,10},{7,11},{8,12},{9,13},{1... | collective-permute-start | bytes 3145736 | tf_op jit(solution)/shard_map/ppermute | solution.py:27
  56.9 12.5 %collective-permute-start.20 = (bf16[128,1024]{1,0:T(8,128)(2,1)S(1)}, bf16[128,1024]{1,0:T(8,128)(2,1)S(1)}, u32[]{:S(2)}, u32[]{:S(2)}) collective-permute-start(bf16[128,1024]{1,0:T(8,128)(2,1)S(1)} %get-tuple-element.82), channel_id=1, source_target_pairs={{0,1},{1,0},{2,3},{3,2},{4,5},{5,4},{6,7},{7,6},{8,9},{9,8},{10,11... | collective-permute-start | bytes 786440 | tf_op jit(solution)/shard_map/ppermute | solution.py:32
  69.3 1.6 %collective-permute-start.19 = (bf16[128,1024]{1,0:T(8,128)(2,1)S(1)}, bf16[128,1024]{1,0:T(8,128)(2,1)S(1)}, u32[]{:S(2)}, u32[]{:S(2)}) collective-permute-start(bf16[128,1024]{1,0:T(8,128)(2,1)S(1)} %slice.10), channel_id=1, source_target_pairs={{0,1},{1,0},{2,3},{3,2},{4,5},{5,4},{6,7},{7,6},{8,9},{9,8},{10,11... | collective-permute-start | bytes 786440 | tf_op jit(solution)/shard_map/ppermute | solution.py:32
  69.4 14.1 %collective-permute-start.15 = (bf16[128,1024]{1,0:T(8,128)(2,1)S(1)}, bf16[128,1024]{1,0:T(8,128)(2,1)S(1)}, u32[]{:S(2)}, u32[]{:S(2)}) collective-permute-start(bf16[128,1024]{1,0:T(8,128)(2,1)S(1)} %get-tuple-element.76), channel_id=1, source_target_pairs={{4,0},{5,1},{6,2},{7,3},{8,4},{9,5},{10,6},{11,7},{12,8},{13,9},{1... | collective-permute-start | bytes 786440 | tf_op jit(solution)/shard_map/ppermute | solution.py:27
  76.3 8.5 %collective-permute-start.22 = (bf16[128,1024]{1,0:T(8,128)(2,1)S(1)}, bf16[128,1024]{1,0:T(8,128)(2,1)S(1)}, u32[]{:S(2)}, u32[]{:S(2)}) collective-permute-start(bf16[128,1024]{1,0:T(8,128)(2,1)S(1)} %get-tuple-element.86), channel_id=1, source_target_pairs={{4,0},{5,1},{6,2},{7,3},{8,4},{9,5},{10,6},{11,7},{12,8},{13,9},{1... | collective-permute-start | bytes 786440 | tf_op jit(solution)/shard_map/ppermute | solution.py:27
  77.6 25.0 %collective-permute-start.26 = (bf16[512,1024]{1,0:T(8,128)(2,1)S(1)}, bf16[512,1024]{1,0:T(8,128)(2,1)S(1)}, u32[]{:S(2)}, u32[]{:S(2)}) collective-permute-start(bf16[512,1024]{1,0:T(8,128)(2,1)S(1)} %get-tuple-element.85.refs_0_.own_ref), channel_id=1, source_target_pairs={{0,4},{1,5},{2,6},{3,7},{4,8},{5,9},{6,10},{7,11},{8,12},{9,13},{1... | collective-permute-start | bytes 3145736 | tf_op jit(solution)/shard_map/ppermute | solution.py:27
  81.7 5.3 %collective-permute-start.27 = (bf16[128,1024]{1,0:T(8,128)(2,1)S(1)}, bf16[128,1024]{1,0:T(8,128)(2,1)S(1)}, u32[]{:S(2)}, u32[]{:S(2)}) collective-permute-start(bf16[128,1024]{1,0:T(8,128)(2,1)S(1)} %slice.11), channel_id=1, source_target_pairs={{0,1},{1,0},{2,3},{3,2},{4,5},{5,4},{6,7},{7,6},{8,9},{9,8},{10,11... | collective-permute-start | bytes 786440 | tf_op jit(solution)/shard_map/ppermute | solution.py:32
  87.8 31.1 %collective-permute-start.31 = (bf16[128,8,512]{2,1,0:T(8,128)(2,1)S(1)}, bf16[128,8,512]{2,1,0:T(8,128)(2,1)S(1)}, u32[]{:S(2)}, u32[]{:S(2)}) collective-permute-start(bf16[128,8,512]{2,1,0:T(8,128)(2,1)S(1)} %shard_map.80.refs_1_.own_ref), channel_id=1, source_target_pairs={{7,3},{11,7},{15,11},{23,19},{27,23},{31,27}} | collective-permute-start | bytes 3145736 | tf_op jit(solution)/shard_map/ppermute | solution.py:27
  88.6 18.4 %collective-permute-start.23 = (bf16[256,1024]{1,0:T(8,128)(2,1)S(1)}, bf16[256,1024]{1,0:T(8,128)(2,1)S(1)}, u32[]{:S(2)}, u32[]{:S(2)}) collective-permute-start(bf16[256,1024]{1,0:T(8,128)(2,1)S(1)} %get-tuple-element.89), channel_id=1, source_target_pairs={{0,1},{1,0},{2,3},{3,2},{4,5},{5,4},{6,7},{7,6},{8,9},{9,8},{10,11... | collective-permute-start | bytes 1572872 | tf_op jit(solution)/shard_map/ppermute | solution.py:32
  90.7 17.8 %collective-permute-start.24 = (bf16[256,1024]{1,0:T(8,128)(2,1)S(1)}, bf16[256,1024]{1,0:T(8,128)(2,1)S(1)}, u32[]{:S(2)}, u32[]{:S(2)}) collective-permute-start(bf16[256,1024]{1,0:T(8,128)(2,1)S(1)} %get-tuple-element.90), channel_id=1, source_target_pairs={{0,2},{1,3},{2,0},{3,1},{4,6},{5,7},{6,4},{7,5},{8,10},{9,11},{10,... | collective-permute-start | bytes 1572872 | tf_op jit(solution)/shard_map/ppermute | solution.py:32
  92.2 23.8 %collective-permute-start.25 = (bf16[256,1024]{1,0:T(8,128)(2,1)S(1)}, bf16[256,1024]{1,0:T(8,128)(2,1)S(1)}, u32[]{:S(2)}, u32[]{:S(2)}) collective-permute-start(bf16[256,1024]{1,0:T(8,128)(2,1)S(1)} %get-tuple-element.91), channel_id=1, source_target_pairs={{0,3},{1,2},{2,1},{3,0},{4,7},{5,6},{6,5},{7,4},{8,11},{9,10},{10,... | collective-permute-start | bytes 1572872 | tf_op jit(solution)/shard_map/ppermute | solution.py:32
  104.5 17.1 %collective-permute-start.28 = (bf16[128,1024]{1,0:T(8,128)(2,1)S(1)}, bf16[128,1024]{1,0:T(8,128)(2,1)S(1)}, u32[]{:S(2)}, u32[]{:S(2)}) collective-permute-start(bf16[128,1024]{1,0:T(8,128)(2,1)S(1)} %get-tuple-element.95), channel_id=1, source_target_pairs={{0,1},{1,0},{2,3},{3,2},{4,5},{5,4},{6,7},{7,6},{8,9},{9,8},{10,11... | collective-permute-start | bytes 786440 | tf_op jit(solution)/shard_map/ppermute | solution.py:32
  107.0 14.6 %collective-permute-start.29 = (bf16[128,1024]{1,0:T(8,128)(2,1)S(1)}, bf16[128,1024]{1,0:T(8,128)(2,1)S(1)}, u32[]{:S(2)}, u32[]{:S(2)}) collective-permute-start(bf16[128,1024]{1,0:T(8,128)(2,1)S(1)} %get-tuple-element.96), channel_id=1, source_target_pairs={{0,2},{1,3},{2,0},{3,1},{4,6},{5,7},{6,4},{7,5},{8,10},{9,11},{10,... | collective-permute-start | bytes 786440 | tf_op jit(solution)/shard_map/ppermute | solution.py:32
  108.5 18.4 %collective-permute-start.30 = (bf16[128,1024]{1,0:T(8,128)(2,1)S(1)}, bf16[128,1024]{1,0:T(8,128)(2,1)S(1)}, u32[]{:S(2)}, u32[]{:S(2)}) collective-permute-start(bf16[128,1024]{1,0:T(8,128)(2,1)S(1)} %get-tuple-element.97), channel_id=1, source_target_pairs={{0,3},{1,2},{2,1},{3,0},{4,7},{5,6},{6,5},{7,4},{8,11},{9,10},{10,... | collective-permute-start | bytes 786440 | tf_op jit(solution)/shard_map/ppermute | solution.py:32

commit v19 on v18

--- a/solution.py
+++ b/solution.py
@@ -440,7 +440,7 @@
 def project(here, band, own, high, low, sinos, groups, *tokens):
     n, side = band.shape[0], band.shape[0] // G
     cols = own.shape[1]
-    tile = 512
+    tile = 256
     many, one = pl.BlockSpec((n, tile), lambda i: (0, i)), pl.BlockSpec((side, tile), lambda i: (0, i))
     shapes = [(n, cols), (side, cols)] + [(len(group) * side, cols) for group in groups]
     return call(
@@ -471,7 +471,7 @@
 def back(here, band, own, low, high, dealt, *tokens):
     n, side = band.shape[0], band.shape[0] // G
     cols = own.shape[1]
-    tile = 512
+    tile = 256
     many = pl.BlockSpec((n, tile), lambda i: (0, i))
     one = pl.BlockSpec((side, tile), lambda i: (0, i))
     out = ((2 if dealt else 1) * side, cols)

time: 131 us -> 132 us (level)
  Pallas kernels: 42.3 us -> 44.9 us
    ppermute x11, waiting for transfers between devices: 13.7 us -> 12.3 us  [moved(): return lax.ppermute(value, 'slab', pairs)]
    pallas_call x2, Pallas kernels: 4.22 us -> 5.55 us  [project(): call(functools.partial(project_kernel, groups), 3, grid=(cols // tile,),...]
  transfers between devices with their start and end apart: 32 -> 32, of which waited for: 8 -> 8; matrix products, arithmetic and copies ran while one was open for 1% -> 1% of each run, Pallas kernels for 28% -> 30%
where the time goes in v19:
time: 132 us; the launch traced here: 131 us
  starting transfers between devices  46.9 us (36%)
  Pallas kernels  44.9 us (34%)
  waiting for transfers between devices  35.9 us (27%)
  local copies, waits for them, and re-layouts  2.57 us (2%)
    ppermute x21, starting transfers between devices, swapped(): return lax.ppermute(value, 'slab', [(i, i ^ bits) for i in range(count)])  25.8 us
    ppermute x21, waiting for transfers between devices, swapped(): return lax.ppermute(value, 'slab', [(i, i ^ bits) for i in range(count)])  23.6 us
    ppermute x11, starting transfers between devices, moved(): return lax.ppermute(value, 'slab', pairs)  21.1 us
    ppermute x11, waiting for transfers between devices, moved(): return lax.ppermute(value, 'slab', pairs)  12.3 us
    pallas_call x1, Pallas kernels, half_tv(): call(tv_kernel, 0, grid=(depth // deep,), in_specs=[SMEM] + edges + [afte...  9.99 us
    pallas_call x2, Pallas kernels, cast_rows(): call(functools.partial(cast_kernel, groups, len(edges), halves), 2, grid=...  5.97 us
    pallas_call x2, Pallas kernels, finish(): call(finish_kernel, 0, grid=(count,), in_specs=[SMEM, part] + piece_specs...  5.85 us
    pallas_call x2, Pallas kernels, project(): call(functools.partial(project_kernel, groups), 3, grid=(cols // tile,),...  5.55 us
  transfers between devices with their start and end apart: 32, of which 8 were waited for; matrix products, arithmetic and copies ran while one was open for 1% of the time, Pallas kernels for 30%

profile of v19, /device:TPU:1, one launch (start us, length us, event | category | flops | bytes accessed | tf_op | source)
XLA Modules:
  0.0 131.2 jit_solution(44713525735881412)
XLA Ops:
  0.6 2.5 %shard_map.68 = (bf16[128,1024]{1,0:T(8,128)(2,1)}, bf16[144,1024]{1,0:T(8,128)(2,1)S(1)}, bf16[128,1024]{1,0:T(8,128)(2,1)}, bf16[144,1024]{1,0:T(8,128)(2,1)S(1)}) custom-call(s32[1]{0:T(128)} %bitcast.here_ref, f32[1024,1024]{1,0:T(8,128)} %bitcast.2, f32[1024,1024]{1,0:T(8,128)} %bitcast.3, f32[1024,1024]{1,0:T(8,128)} %bitcast.4, f32[1024,1024]{1,0:T(8,128)} %bitcast.5), custom_call_target="tpu_custom_call" | custom-call | flops 2300000000 | bytes 1000 | tf_op jit(solution)/shard_map/pallas_call | solution.py:115
  3.2 2.7 %collective-permute-start.1 = (bf16[128,1024]{1,0:T(8,128)(2,1)}, bf16[128,1024]{1,0:T(8,128)(2,1)}, u32[]{:S(2)}, u32[]{:S(2)}) collective-permute-start(bf16[128,1024]{1,0:T(8,128)(2,1)} %get-tuple-element.52), channel_id=1, source_target_pairs={{0,2},{1,3},{2,0},{3,1},{4,6},{5,7},{6,4},{7,5},{8,10},{9,11},{10,... | collective-permute-start | bytes 786440 | tf_op jit(solution)/shard_map/ppermute | solution.py:32
  6.0 3.4 %shard_map.69 = (bf16[128,1024]{1,0:T(8,128)(2,1)}, bf16[128,1024]{1,0:T(8,128)(2,1)S(1)}, bf16[256,1024]{1,0:T(8,128)(2,1)}, bf16[128,8,512]{2,1,0:T(8,128)(2,1)}, bf16[128,8,512]{2,1,0:T(8,128)(2,1)S(1)}) custom-call(s32[1]{0:T(128)} %bitcast.here_ref, f32[1024,1024]{1,0:T(8,128)} %bitcast.6, f32[1024,1024]{1,0:T(8,128)} %bitcast.7, ...), custom_call_target="tpu_custom_call" | custom-call | flops 2300000000 | bytes 1000 | tf_op jit(solution)/shard_map/pallas_call | solution.py:115
  10.1 0.7 collective-permute-start.4
  10.8 4.2 %collective-permute-start.5 = (bf16[256,1024]{1,0:T(8,128)(2,1)}, bf16[256,1024]{1,0:T(8,128)(2,1)}, u32[]{:S(2)}, u32[]{:S(2)}) collective-permute-start(bf16[256,1024]{1,0:T(8,128)(2,1)} %get-tuple-element.59), channel_id=1, source_target_pairs={{0,2},{1,3},{2,0},{3,1},{4,6},{5,7},{6,4},{7,5},{8,10},{9,11},{10,... | collective-permute-start | bytes 1572872 | tf_op jit(solution)/shard_map/ppermute | solution.py:32
  15.1 0.8 copy.13.offset_ref
  15.9 0.9 copy-done.4
  16.8 1.6 %shard_map.70 = (bf16[512,1152]{1,0:T(8,128)(2,1)S(1)}, bf16[512,1152]{1,0:T(8,128)(2,1)S(1)}) custom-call(s32[1]{0:T(128)} %bitcast.here_ref, s32[16,6]{1,0:T(8,128)S(1)} %copy.12.cover_ref, s32[16,6]{1,0:T(8,128)S(1)} %copy.13.offset_ref, bf16[8,128,128]{2,1,0:T(8,128)(2,1)S(1)} %copy-done, bf16[128,1024]{1,0:T(8,128)(2,1)S(1)} %copy-done.4), custom_call_target="tpu_custom_call" | custom-call | flops 10350000128 | bytes 1000 | tf_op jit(solution)/shard_map/pallas_call | solution.py:415
  18.5 0.7 collective-permute-start.10
  19.3 1.2 shard_map.71
  20.7 1.3 collective-permute-start.3
  22.0 8.4 %collective-permute-done.5.refs_0_.refs_2_ = bf16[256,1024]{1,0:T(8,128)(2,1)} collective-permute-done((bf16[256,1024]{1,0:T(8,128)(2,1)}, bf16[256,1024]{1,0:T(8,128)(2,1)}, u32[]{:S(2)}, u32[]{:S(2)}) %collective-permute-start.5) | collective-permute-done | bytes 524320 | tf_op jit(solution)/shard_map/ppermute | solution.py:32
  30.4 1.8 %shard_map.72 = (bf16[128,1024]{1,0:T(8,128)(2,1)S(1)}, bf16[128,1024]{1,0:T(8,128)(2,1)S(1)}, bf16[256,1024]{1,0:T(8,128)(2,1)S(1)}, bf16[128,1024]{1,0:T(8,128)(2,1)S(1)}) custom-call(s32[1]{0:T(128)} %bitcast.here_ref, bf16[128,8,1024]{2,1,0:T(8,128)(2,1)} %refs_2_.3, bf16[128,8,512]{2,1,0:T(8,128)(2,1)S(1)} %collective-permute-done.4.got_ref, ...), custom_call_target="tpu_custom_call" | custom-call | flops 2300000000 | bytes 1000 | tf_op jit(solution)/shard_map/pallas_call | solution.py:196
  33.0 1.5 %collective-permute-start.9 = (bf16[256,1024]{1,0:T(8,128)(2,1)S(1)}, bf16[256,1024]{1,0:T(8,128)(2,1)S(1)}, u32[]{:S(2)}, u32[]{:S(2)}) collective-permute-start(bf16[256,1024]{1,0:T(8,128)(2,1)S(1)} %get-tuple-element.64), channel_id=1, source_target_pairs={{0,2},{1,3},{2,0},{3,1},{4,6},{5,7},{6,4},{7,5},{8,10},{9,11},{10,... | collective-permute-start | bytes 1572872 | tf_op jit(solution)/shard_map/ppermute | solution.py:32
  34.5 3.2 %collective-permute-start.8 = (bf16[144,1024]{1,0:T(8,128)(2,1)S(1)}, bf16[144,1024]{1,0:T(8,128)(2,1)S(1)}, u32[]{:S(2)}, u32[]{:S(2)}) collective-permute-start(bf16[144,1024]{1,0:T(8,128)(2,1)S(1)} %get-tuple-element.62), channel_id=1, source_target_pairs={{0,4},{1,5},{2,6},{3,7},{4,8},{5,9},{6,10},{7,11},{8,12},{9,13},{1... | collective-permute-start | bytes 884744 | tf_op jit(solution)/shard_map/ppermute | solution.py:27
  37.7 1.2 shard_map.73
  38.9 3.2 %collective-permute-start.13 = (bf16[128,1024]{1,0:T(8,128)(2,1)S(1)}, bf16[128,1024]{1,0:T(8,128)(2,1)S(1)}, u32[]{:S(2)}, u32[]{:S(2)}) collective-permute-start(bf16[128,1024]{1,0:T(8,128)(2,1)S(1)} %get-tuple-element.72), channel_id=1, source_target_pairs={{0,4},{1,5},{2,6},{3,7},{4,8},{5,9},{6,10},{7,11},{8,12},{9,13},{1... | collective-permute-start | bytes 786440 | tf_op jit(solution)/shard_map/ppermute | solution.py:27
  42.1 1.7 %shard_map.74 = (bf16[128,1024]{1,0:T(8,128)(2,1)S(1)}, bf16[128,1024]{1,0:T(8,128)(2,1)S(1)}, bf16[256,1024]{1,0:T(8,128)(2,1)S(1)}) custom-call(s32[1]{0:T(128)} %bitcast.here_ref, bf16[128,8,1024]{2,1,0:T(8,128)(2,1)} %refs_2_.3, bf16[128,8,512]{2,1,0:T(8,128)(2,1)S(1)} %collective-permute-done.10.got_ref, ...), custom_call_target="tpu_custom_call" | custom-call | flops 2300000000 | bytes 1000 | tf_op jit(solution)/shard_map/pallas_call | solution.py:196
  43.8 2.2 %collective-permute-done.9.refs_2_ = bf16[256,1024]{1,0:T(8,128)(2,1)S(1)} collective-permute-done((bf16[256,1024]{1,0:T(8,128)(2,1)S(1)}, bf16[256,1024]{1,0:T(8,128)(2,1)S(1)}, u32[]{:S(2)}, u32[]{:S(2)}) %collective-permute-start.9) | collective-permute-done | bytes 524320 | tf_op jit(solution)/shard_map/ppermute | solution.py:32
  46.1 1.3 %collective-permute-start.12 = (bf16[128,1024]{1,0:T(8,128)(2,1)S(1)}, bf16[128,1024]{1,0:T(8,128)(2,1)S(1)}, u32[]{:S(2)}, u32[]{:S(2)}) collective-permute-start(bf16[128,1024]{1,0:T(8,128)(2,1)S(1)} %slice.9), channel_id=1, source_target_pairs={{0,1},{1,0},{2,3},{3,2},{4,5},{5,4},{6,7},{7,6},{8,9},{9,8},{10,11... | collective-permute-start | bytes 786440 | tf_op jit(solution)/shard_map/ppermute | solution.py:32
  47.4 1.3 collective-permute-start.16
  49.0 2.2 %collective-permute-start.18 = (bf16[256,1024]{1,0:T(8,128)(2,1)S(1)}, bf16[256,1024]{1,0:T(8,128)(2,1)S(1)}, u32[]{:S(2)}, u32[]{:S(2)}) collective-permute-start(bf16[256,1024]{1,0:T(8,128)(2,1)S(1)} %get-tuple-element.78), channel_id=1, source_target_pairs={{0,2},{1,3},{2,0},{3,1},{4,6},{5,7},{6,4},{7,5},{8,10},{9,11},{10,... | collective-permute-start | bytes 1572872 | tf_op jit(solution)/shard_map/ppermute | solution.py:32
  51.3 2.8 %shard_map.75 = (bf16[512,1024]{1,0:T(8,128)(2,1)S(1)}, bf16[128,1024]{1,0:T(8,128)(2,1)S(1)}, bf16[128,1024]{1,0:T(8,128)(2,1)S(1)}, bf16[256,1024]{1,0:T(8,128)(2,1)S(1)}) custom-call(s32[1]{0:T(128)} %bitcast.here_ref, bf16[512,1152]{1,0:T(8,128)(2,1)S(1)} %get-tuple-element.55.refs_4_.band_ref, bf16[528,1024]{1,0:T(8,128)(2,1)S(1)} %get-tuple-element.56.own_ref, ...), custom_call_target="tpu_custom_call" | custom-call | flops 3449999872 | bytes 1000 | tf_op jit(solution)/shard_map/pallas_call | solution.py:446
  54.2 3.3 %collective-permute-start.14 = (bf16[512,1024]{1,0:T(8,128)(2,1)S(1)}, bf16[512,1024]{1,0:T(8,128)(2,1)S(1)}, u32[]{:S(2)}, u32[]{:S(2)}) collective-permute-start(bf16[512,1024]{1,0:T(8,128)(2,1)S(1)} %get-tuple-element.73.refs_0_.own_ref), channel_id=1, source_target_pairs={{0,4},{1,5},{2,6},{3,7},{4,8},{5,9},{6,10},{7,11},{8,12},{9,13},{1... | collective-permute-start | bytes 3145736 | tf_op jit(solution)/shard_map/ppermute | solution.py:27
  57.6 2.4 %collective-permute-start.20 = (bf16[128,1024]{1,0:T(8,128)(2,1)S(1)}, bf16[128,1024]{1,0:T(8,128)(2,1)S(1)}, u32[]{:S(2)}, u32[]{:S(2)}) collective-permute-start(bf16[128,1024]{1,0:T(8,128)(2,1)S(1)} %get-tuple-element.82), channel_id=1, source_target_pairs={{0,1},{1,0},{2,3},{3,2},{4,5},{5,4},{6,7},{7,6},{8,9},{9,8},{10,11... | collective-permute-start | bytes 786440 | tf_op jit(solution)/shard_map/ppermute | solution.py:32
  59.9 10.0 %shard_map.76 = (f32[128,8,1024]{2,1,0:T(8,128)}, f32[8,128]{1,0:T(8,128)S(1)}) custom-call(s32[1]{0:T(128)} %bitcast.here_ref, bf16[144,1024]{1,0:T(8,128)(2,1)S(1)} %collective-permute-done.refs_1_.near_ref, bf16[528,1024]{1,0:T(8,128)(2,1)S(1)} %collective-permute-done.3.high_ref.next_level_ref, ...), custom_call_target="tpu_custom_call" | custom-call | bytes 1000 | tf_op jit(solution)/shard_map/pallas_call | solution.py:546
  70.1 1.3 collective-permute-start.15
  71.6 2.6 %collective-permute-done.16.high_ref = bf16[512,1024]{1,0:T(8,128)(2,1)S(1)} collective-permute-done((bf16[512,1024]{1,0:T(8,128)(2,1)S(1)}, bf16[512,1024]{1,0:T(8,128)(2,1)S(1)}, u32[]{:S(2)}, u32[]{:S(2)}) %collective-permute-start.16) | collective-permute-done | bytes 1048608 | tf_op jit(solution)/shard_map/ppermute | solution.py:27
  74.2 2.7 %shard_map.77 = (bf16[512,1024]{1,0:T(8,128)(2,1)S(1)}, bf16[128,1024]{1,0:T(8,128)(2,1)S(1)}) custom-call(s32[1]{0:T(128)} %bitcast.here_ref, bf16[512,1152]{1,0:T(8,128)(2,1)S(1)} %get-tuple-element.55.refs_4_.band_ref, bf16[512,1024]{1,0:T(8,128)(2,1)S(1)} %get-tuple-element.69.refs_0_.own_ref, bf16[512,1024]{1,0:T(8,128)(2,1)S(1)} %collective-permute-done.16.high_ref, ...), custom_call_target="tpu_custom_call" | custom-call | flops 3449999872 | bytes 1000 | tf_op jit(solution)/shard_map/pallas_call | solution.py:446
  76.9 1.3 collective-permute-start.22
  78.2 4.1 %collective-permute-start.26 = (bf16[512,1024]{1,0:T(8,128)(2,1)S(1)}, bf16[512,1024]{1,0:T(8,128)(2,1)S(1)}, u32[]{:S(2)}, u32[]{:S(2)}) collective-permute-start(bf16[512,1024]{1,0:T(8,128)(2,1)S(1)} %get-tuple-element.85.refs_0_.own_ref), channel_id=1, source_target_pairs={{0,4},{1,5},{2,6},{3,7},{4,8},{5,9},{6,10},{7,11},{8,12},{9,13},{1... | collective-permute-start | bytes 3145736 | tf_op jit(solution)/shard_map/ppermute | solution.py:27
  82.3 1.8 %collective-permute-start.27 = (bf16[128,1024]{1,0:T(8,128)(2,1)S(1)}, bf16[128,1024]{1,0:T(8,128)(2,1)S(1)}, u32[]{:S(2)}, u32[]{:S(2)}) collective-permute-start(bf16[128,1024]{1,0:T(8,128)(2,1)S(1)} %slice.11), channel_id=1, source_target_pairs={{0,1},{1,0},{2,3},{3,2},{4,5},{5,4},{6,7},{7,6},{8,9},{9,8},{10,11... | collective-permute-start | bytes 786440 | tf_op jit(solution)/shard_map/ppermute | solution.py:32
  84.1 1.3 %collective-permute-done.22.refs_1_.high_ref = bf16[128,1024]{1,0:T(8,128)(2,1)S(1)} collective-permute-done((bf16[128,1024]{1,0:T(8,128)(2,1)S(1)}, bf16[128,1024]{1,0:T(8,128)(2,1)S(1)}, u32[]{:S(2)}, u32[]{:S(2)}) %collective-permute-start.22) | collective-permute-done | bytes 262176 | tf_op jit(solution)/shard_map/ppermute | solution.py:27
  85.5 2.8 %shard_map.78 = (bf16[256,1024]{1,0:T(8,128)(2,1)S(1)}, bf16[256,1024]{1,0:T(8,128)(2,1)S(1)}, bf16[256,1024]{1,0:T(8,128)(2,1)S(1)}, bf16[256,1024]{1,0:T(8,128)(2,1)S(1)}) custom-call(s32[1]{0:T(128)} %bitcast.here_ref, bf16[512,1152]{1,0:T(8,128)(2,1)S(1)} %get-tuple-element.75.band_ref, bf16[512,1024]{1,0:T(8,128)(2,1)S(1)} %get-tuple-element.73.refs_0_.own_ref, ...), custom_call_target="tpu_custom_call" | custom-call | bytes 1000 | tf_op jit(solution)/shard_map/pallas_call | solution.py:478
  88.3 0.9 shard_map.80.refs_1_.own_ref
  89.2 0.7 collective-permute-start.31
  89.9 2.1 %collective-permute-start.23 = (bf16[256,1024]{1,0:T(8,128)(2,1)S(1)}, bf16[256,1024]{1,0:T(8,128)(2,1)S(1)}, u32[]{:S(2)}, u32[]{:S(2)}) collective-permute-start(bf16[256,1024]{1,0:T(8,128)(2,1)S(1)} %get-tuple-element.89), channel_id=1, source_target_pairs={{0,1},{1,0},{2,3},{3,2},{4,5},{5,4},{6,7},{7,6},{8,9},{9,8},{10,11... | collective-permute-start | bytes 1572872 | tf_op jit(solution)/shard_map/ppermute | solution.py:32
  92.0 1.5 %collective-permute-start.24 = (bf16[256,1024]{1,0:T(8,128)(2,1)S(1)}, bf16[256,1024]{1,0:T(8,128)(2,1)S(1)}, u32[]{:S(2)}, u32[]{:S(2)}) collective-permute-start(bf16[256,1024]{1,0:T(8,128)(2,1)S(1)} %get-tuple-element.90), channel_id=1, source_target_pairs={{0,2},{1,3},{2,0},{3,1},{4,6},{5,7},{6,4},{7,5},{8,10},{9,11},{10,... | collective-permute-start | bytes 1572872 | tf_op jit(solution)/shard_map/ppermute | solution.py:32
  93.8 1.2 shard_map.79
  94.9 8.3 %collective-permute-done.26.low_ref = bf16[512,1024]{1,0:T(8,128)(2,1)S(1)} collective-permute-done((bf16[512,1024]{1,0:T(8,128)(2,1)S(1)}, bf16[512,1024]{1,0:T(8,128)(2,1)S(1)}, u32[]{:S(2)}, u32[]{:S(2)}) %collective-permute-start.26) | collective-permute-done | bytes 1048608 | tf_op jit(solution)/shard_map/ppermute | solution.py:27
  103.2 2.5 %shard_map.81 = (bf16[128,1024]{1,0:T(8,128)(2,1)S(1)}, bf16[128,1024]{1,0:T(8,128)(2,1)S(1)}, bf16[128,1024]{1,0:T(8,128)(2,1)S(1)}, bf16[128,1024]{1,0:T(8,128)(2,1)S(1)}) custom-call(s32[1]{0:T(128)} %bitcast.here_ref, bf16[512,1152]{1,0:T(8,128)(2,1)S(1)} %get-tuple-element.75.band_ref, bf16[512,1024]{1,0:T(8,128)(2,1)S(1)} %get-tuple-element.85.refs_0_.own_ref, ...), custom_call_target="tpu_custom_call" | custom-call | bytes 1000 | tf_op jit(solution)/shard_map/pallas_call | solution.py:478
  105.7 2.4 %collective-permute-start.28 = (bf16[128,1024]{1,0:T(8,128)(2,1)S(1)}, bf16[128,1024]{1,0:T(8,128)(2,1)S(1)}, u32[]{:S(2)}, u32[]{:S(2)}) collective-permute-start(bf16[128,1024]{1,0:T(8,128)(2,1)S(1)} %get-tuple-element.95), channel_id=1, source_target_pairs={{0,1},{1,0},{2,3},{3,2},{4,5},{5,4},{6,7},{7,6},{8,9},{9,8},{10,11... | collective-permute-start | bytes 786440 | tf_op jit(solution)/shard_map/ppermute | solution.py:32
  108.2 1.5 %collective-permute-start.29 = (bf16[128,1024]{1,0:T(8,128)(2,1)S(1)}, bf16[128,1024]{1,0:T(8,128)(2,1)S(1)}, u32[]{:S(2)}, u32[]{:S(2)}) collective-permute-start(bf16[128,1024]{1,0:T(8,128)(2,1)S(1)} %get-tuple-element.96), channel_id=1, source_target_pairs={{0,2},{1,3},{2,0},{3,1},{4,6},{5,7},{6,4},{7,5},{8,10},{9,11},{10,... | collective-permute-start | bytes 786440 | tf_op jit(solution)/shard_map/ppermute | solution.py:32
  109.9 7.5 %collective-permute-done.25.refs_3_ = bf16[256,1024]{1,0:T(8,128)(2,1)S(1)} collective-permute-done((bf16[256,1024]{1,0:T(8,128)(2,1)S(1)}, bf16[256,1024]{1,0:T(8,128)(2,1)S(1)}, u32[]{:S(2)}, u32[]{:S(2)}) %collective-permute-start.25) | collective-permute-done | bytes 524320 | tf_op jit(solution)/shard_map/ppermute | solution.py:32
  117.4 2.9 %shard_map.82.tv_ref = f32[128,8,1024]{2,1,0:T(8,128)} custom-call(s32[1]{0:T(128)} %bitcast.here_ref, f32[128,8,1024]{2,1,0:T(8,128)} %get-tuple-element.88.tv_ref, bf16[256,1024]{1,0:T(8,128)(2,1)S(1)} %get-tuple-element.87.refs_4_.refs_0_, bf16[256,1024]{1,0:T(8,128)(2,1)S(1)} %collective-permute-done.23.refs_1_, ...), custom_call_target="tpu_custom_call", output_to_operand_aliasing={{}: (1, {})} | custom-call | bytes 1000 | tf_op jit(solution)/shard_map/pallas_call | solution.py:367
  120.3 2.6 %shard_map.83.refs_4_ = bf16[128,8,1024]{2,1,0:T(8,128)(2,1)} custom-call(s32[1]{0:T(128)} %bitcast.here_ref, bf16[128,8,512]{2,1,0:T(8,128)(2,1)S(1)} %shard_map.80.refs_1_.own_ref, bf16[128,8,512]{2,1,0:T(8,128)(2,1)S(1)} %collective-permute-done.31.above_ref, bf16[256,1024]{1,0:T(8,128)(2,1)S(1)} %get-tuple-element.87.refs_4_.refs_0_, ...), custom_call_target="tpu_custom_call" | custom-call | bytes 1000 | tf_op jit(solution)/shard_map/pallas_call | solution.py:345
  123.0 5.3 %collective-permute-done.30.refs_3_ = bf16[128,1024]{1,0:T(8,128)(2,1)S(1)} collective-permute-done((bf16[128,1024]{1,0:T(8,128)(2,1)S(1)}, bf16[128,1024]{1,0:T(8,128)(2,1)S(1)}, u32[]{:S(2)}, u32[]{:S(2)}) %collective-permute-start.30) | collective-permute-done | bytes 262176 | tf_op jit(solution)/shard_map/ppermute | solution.py:32
  128.2 2.9 %shard_map.84 = f32[128,8,1024]{2,1,0:T(8,128)} custom-call(s32[1]{0:T(128)} %bitcast.here_ref, f32[128,8,1024]{2,1,0:T(8,128)} %shard_map.82.tv_ref, bf16[128,1024]{1,0:T(8,128)(2,1)S(1)} %get-tuple-element.94.refs_4_.refs_0_, bf16[128,1024]{1,0:T(8,128)(2,1)S(1)} %collective-permute-done.28.refs_1_, ...), custom_call_target="tpu_custom_call", output_to_operand_aliasing={{}: (1, {})} | custom-call | bytes 1000 | tf_op jit(solution)/shard_map/pallas_call | solution.py:367
  (52 shorter events, 3.2 us)
Async XLA Ops:
  3.2 16.1 %collective-permute-start = (bf16[144,1024]{1,0:T(8,128)(2,1)S(1)}, bf16[144,1024]{1,0:T(8,128)(2,1)S(1)}, u32[]{:S(2)}, u32[]{:S(2)}) collective-permute-start(bf16[144,1024]{1,0:T(8,128)(2,1)S(1)} %get-tuple-element.50.refs_4_), channel_id=1, source_target_pairs={{0,1},{1,0},{2,3},{3,2},{4,5},{5,4},{6,7},{7,6},{8,9},{9,8},{10,11... | collective-permute-start | bytes 884744 | tf_op jit(solution)/shard_map/ppermute | solution.py:32
  3.2 15.3 %collective-permute-start.1 = (bf16[128,1024]{1,0:T(8,128)(2,1)}, bf16[128,1024]{1,0:T(8,128)(2,1)}, u32[]{:S(2)}, u32[]{:S(2)}) collective-permute-start(bf16[128,1024]{1,0:T(8,128)(2,1)} %get-tuple-element.52), channel_id=1, source_target_pairs={{0,2},{1,3},{2,0},{3,1},{4,6},{5,7},{6,4},{7,5},{8,10},{9,11},{10,... | collective-permute-start | bytes 786440 | tf_op jit(solution)/shard_map/ppermute | solution.py:32
  5.9 9.1 %copy-start.6 = (s32[16,6]{0,1:T(8,128)S(1)}, s32[16,6]{0,1:T(8,128)}, u32[]{:S(2)}) copy-start(s32[16,6]{0,1:T(8,128)} %param.8) | copy-start | bytes 1156
  5.9 10.0 %copy-start = (bf16[8,128,128]{2,1,0:T(8,128)(2,1)S(1)}, bf16[8,128,128]{2,1,0:T(8,128)(2,1)}, u32[]{:S(2)}) copy-start(bf16[8,128,128]{2,1,0:T(8,128)(2,1)} %refs_0_.1) | copy-start | bytes 786436
  5.9 13.3 %collective-permute-start.2 = (bf16[144,1024]{1,0:T(8,128)(2,1)S(1)}, bf16[144,1024]{1,0:T(8,128)(2,1)S(1)}, u32[]{:S(2)}, u32[]{:S(2)}) collective-permute-start(bf16[144,1024]{1,0:T(8,128)(2,1)S(1)} %get-tuple-element.53), channel_id=1, source_target_pairs={{0,3},{1,2},{2,1},{3,0},{4,7},{5,6},{6,5},{7,4},{8,11},{9,10},{10,... | collective-permute-start | bytes 884744 | tf_op jit(solution)/shard_map/ppermute | solution.py:32
  9.4 0.7 copy-start.3
  10.1 20.3 %collective-permute-start.4 = (bf16[128,8,512]{2,1,0:T(8,128)(2,1)}, bf16[128,8,512]{2,1,0:T(8,128)(2,1)S(1)}, u32[]{:S(2)}, u32[]{:S(2)}) collective-permute-start(bf16[128,8,512]{2,1,0:T(8,128)(2,1)} %get-tuple-element.58), channel_id=1, source_target_pairs={{3,7},{7,11},{11,15},{19,23},{23,27},{27,31}} | collective-permute-start | bytes 3145736 | tf_op jit(solution)/shard_map/ppermute | solution.py:27
  10.8 19.6 %collective-permute-start.5 = (bf16[256,1024]{1,0:T(8,128)(2,1)}, bf16[256,1024]{1,0:T(8,128)(2,1)}, u32[]{:S(2)}, u32[]{:S(2)}) collective-permute-start(bf16[256,1024]{1,0:T(8,128)(2,1)} %get-tuple-element.59), channel_id=1, source_target_pairs={{0,2},{1,3},{2,0},{3,1},{4,6},{5,7},{6,4},{7,5},{8,10},{9,11},{10,... | collective-permute-start | bytes 1572872 | tf_op jit(solution)/shard_map/ppermute | solution.py:32
  15.9 1.0 copy-start.4
  16.8 2.4 %copy-start.2 = (bf16[128,1024]{1,0:T(8,128)(2,1)S(1)}, bf16[128,1024]{1,0:T(8,128)(2,1)}, u32[]{:S(2)}) copy-start(bf16[128,1024]{1,0:T(8,128)(2,1)} %get-tuple-element.51.refs_0_) | copy-start | bytes 786436
  18.5 23.6 %collective-permute-start.10 = (bf16[128,8,512]{2,1,0:T(8,128)(2,1)S(1)}, bf16[128,8,512]{2,1,0:T(8,128)(2,1)S(1)}, u32[]{:S(2)}, u32[]{:S(2)}) collective-permute-start(bf16[128,8,512]{2,1,0:T(8,128)(2,1)S(1)} %get-tuple-element.66), channel_id=1, source_target_pairs={{3,7},{7,11},{11,15},{19,23},{23,27},{27,31}} | collective-permute-start | bytes 3145736 | tf_op jit(solution)/shard_map/ppermute | solution.py:27
  19.3 1.2 copy-start.5
  20.5 17.2 %copy-start.1 = (bf16[128,1024]{1,0:T(8,128)(2,1)S(1)}, bf16[128,1024]{1,0:T(8,128)(2,1)}, u32[]{:S(2)}) copy-start(bf16[128,1024]{1,0:T(8,128)(2,1)} %get-tuple-element.67.refs_0_) | copy-start | bytes 786436
  20.5 9.9 %collective-permute-start.6 = (bf16[128,1024]{1,0:T(8,128)(2,1)S(1)}, bf16[128,1024]{1,0:T(8,128)(2,1)S(1)}, u32[]{:S(2)}, u32[]{:S(2)}) collective-permute-start(bf16[128,1024]{1,0:T(8,128)(2,1)S(1)} %copy-done.5), channel_id=1, source_target_pairs={{0,1},{1,0},{2,3},{3,2},{4,5},{5,4},{6,7},{7,6},{8,9},{9,8},{10,11... | collective-permute-start | bytes 786440 | tf_op jit(solution)/shard_map/ppermute | solution.py:32
  20.7 28.0 %collective-permute-start.3 = (bf16[528,1024]{1,0:T(8,128)(2,1)S(1)}, bf16[528,1024]{1,0:T(8,128)(2,1)S(1)}, u32[]{:S(2)}, u32[]{:S(2)}) collective-permute-start(bf16[528,1024]{1,0:T(8,128)(2,1)S(1)} %get-tuple-element.56.own_ref), channel_id=1, source_target_pairs={{4,0},{5,1},{6,2},{7,3},{8,4},{9,5},{10,6},{11,7},{12,8},{13,9},{1... | collective-permute-start | bytes 3244040 | tf_op jit(solution)/shard_map/ppermute | solution.py:27
  32.2 2.3 %collective-permute-start.7 = (bf16[128,1024]{1,0:T(8,128)(2,1)S(1)}, bf16[128,1024]{1,0:T(8,128)(2,1)S(1)}, u32[]{:S(2)}, u32[]{:S(2)}) collective-permute-start(bf16[128,1024]{1,0:T(8,128)(2,1)S(1)} %get-tuple-element.61), channel_id=1, source_target_pairs={{0,1},{1,0},{2,3},{3,2},{4,5},{5,4},{6,7},{7,6},{8,9},{9,8},{10,11... | collective-permute-start | bytes 786440 | tf_op jit(solution)/shard_map/ppermute | solution.py:32
  32.9 4.8 %collective-permute-start.11 = (bf16[128,1024]{1,0:T(8,128)(2,1)S(1)}, bf16[128,1024]{1,0:T(8,128)(2,1)S(1)}, u32[]{:S(2)}, u32[]{:S(2)}) collective-permute-start(bf16[128,1024]{1,0:T(8,128)(2,1)S(1)} %get-tuple-element.68), channel_id=1, source_target_pairs={{0,1},{1,0},{2,3},{3,2},{4,5},{5,4},{6,7},{7,6},{8,9},{9,8},{10,11... | collective-permute-start | bytes 786440 | tf_op jit(solution)/shard_map/ppermute | solution.py:32
  33.0 13.1 %collective-permute-start.9 = (bf16[256,1024]{1,0:T(8,128)(2,1)S(1)}, bf16[256,1024]{1,0:T(8,128)(2,1)S(1)}, u32[]{:S(2)}, u32[]{:S(2)}) collective-permute-start(bf16[256,1024]{1,0:T(8,128)(2,1)S(1)} %get-tuple-element.64), channel_id=1, source_target_pairs={{0,2},{1,3},{2,0},{3,1},{4,6},{5,7},{6,4},{7,5},{8,10},{9,11},{10,... | collective-permute-start | bytes 1572872 | tf_op jit(solution)/shard_map/ppermute | solution.py:32
  34.5 16.8 %collective-permute-start.8 = (bf16[144,1024]{1,0:T(8,128)(2,1)S(1)}, bf16[144,1024]{1,0:T(8,128)(2,1)S(1)}, u32[]{:S(2)}, u32[]{:S(2)}) collective-permute-start(bf16[144,1024]{1,0:T(8,128)(2,1)S(1)} %get-tuple-element.62), channel_id=1, source_target_pairs={{0,4},{1,5},{2,6},{3,7},{4,8},{5,9},{6,10},{7,11},{8,12},{9,13},{1... | collective-permute-start | bytes 884744 | tf_op jit(solution)/shard_map/ppermute | solution.py:27
  38.9 10.1 %collective-permute-start.13 = (bf16[128,1024]{1,0:T(8,128)(2,1)S(1)}, bf16[128,1024]{1,0:T(8,128)(2,1)S(1)}, u32[]{:S(2)}, u32[]{:S(2)}) collective-permute-start(bf16[128,1024]{1,0:T(8,128)(2,1)S(1)} %get-tuple-element.72), channel_id=1, source_target_pairs={{0,4},{1,5},{2,6},{3,7},{4,8},{5,9},{6,10},{7,11},{8,12},{9,13},{1... | collective-permute-start | bytes 786440 | tf_op jit(solution)/shard_map/ppermute | solution.py:27
  46.1 5.2 %collective-permute-start.12 = (bf16[128,1024]{1,0:T(8,128)(2,1)S(1)}, bf16[128,1024]{1,0:T(8,128)(2,1)S(1)}, u32[]{:S(2)}, u32[]{:S(2)}) collective-permute-start(bf16[128,1024]{1,0:T(8,128)(2,1)S(1)} %slice.9), channel_id=1, source_target_pairs={{0,1},{1,0},{2,3},{3,2},{4,5},{5,4},{6,7},{7,6},{8,9},{9,8},{10,11... | collective-permute-start | bytes 786440 | tf_op jit(solution)/shard_map/ppermute | solution.py:32
  47.4 26.8 %collective-permute-start.16 = (bf16[512,1024]{1,0:T(8,128)(2,1)S(1)}, bf16[512,1024]{1,0:T(8,128)(2,1)S(1)}, u32[]{:S(2)}, u32[]{:S(2)}) collective-permute-start(bf16[512,1024]{1,0:T(8,128)(2,1)S(1)} %get-tuple-element.69.refs_0_.own_ref), channel_id=1, source_target_pairs={{4,0},{5,1},{6,2},{7,3},{8,4},{9,5},{10,6},{11,7},{12,8},{13,9},{1... | collective-permute-start | bytes 3145736 | tf_op jit(solution)/shard_map/ppermute | solution.py:27
  48.7 5.4 %collective-permute-start.17 = (bf16[128,1024]{1,0:T(8,128)(2,1)S(1)}, bf16[128,1024]{1,0:T(8,128)(2,1)S(1)}, u32[]{:S(2)}, u32[]{:S(2)}) collective-permute-start(bf16[128,1024]{1,0:T(8,128)(2,1)S(1)} %get-tuple-element.77), channel_id=1, source_target_pairs={{0,1},{1,0},{2,3},{3,2},{4,5},{5,4},{6,7},{7,6},{8,9},{9,8},{10,11... | collective-permute-start | bytes 786440 | tf_op jit(solution)/shard_map/ppermute | solution.py:32
  49.0 20.9 %collective-permute-start.18 = (bf16[256,1024]{1,0:T(8,128)(2,1)S(1)}, bf16[256,1024]{1,0:T(8,128)(2,1)S(1)}, u32[]{:S(2)}, u32[]{:S(2)}) collective-permute-start(bf16[256,1024]{1,0:T(8,128)(2,1)S(1)} %get-tuple-element.78), channel_id=1, source_target_pairs={{0,2},{1,3},{2,0},{3,1},{4,6},{5,7},{6,4},{7,5},{8,10},{9,11},{10,... | collective-permute-start | bytes 1572872 | tf_op jit(solution)/shard_map/ppermute | solution.py:32
  54.1 20.1 %collective-permute-start.21 = (bf16[256,1024]{1,0:T(8,128)(2,1)S(1)}, bf16[256,1024]{1,0:T(8,128)(2,1)S(1)}, u32[]{:S(2)}, u32[]{:S(2)}) collective-permute-start(bf16[256,1024]{1,0:T(8,128)(2,1)S(1)} %get-tuple-element.84), channel_id=1, source_target_pairs={{0,2},{1,3},{2,0},{3,1},{4,6},{5,7},{6,4},{7,5},{8,10},{9,11},{10,... | collective-permute-start | bytes 1572872 | tf_op jit(solution)/shard_map/ppermute | solution.py:32
  54.2 31.2 %collective-permute-start.14 = (bf16[512,1024]{1,0:T(8,128)(2,1)S(1)}, bf16[512,1024]{1,0:T(8,128)(2,1)S(1)}, u32[]{:S(2)}, u32[]{:S(2)}) collective-permute-start(bf16[512,1024]{1,0:T(8,128)(2,1)S(1)} %get-tuple-element.73.refs_0_.own_ref), channel_id=1, source_target_pairs={{0,4},{1,5},{2,6},{3,7},{4,8},{5,9},{6,10},{7,11},{8,12},{9,13},{1... | collective-permute-start | bytes 3145736 | tf_op jit(solution)/shard_map/ppermute | solution.py:27
  57.6 12.5 %collective-permute-start.20 = (bf16[128,1024]{1,0:T(8,128)(2,1)S(1)}, bf16[128,1024]{1,0:T(8,128)(2,1)S(1)}, u32[]{:S(2)}, u32[]{:S(2)}) collective-permute-start(bf16[128,1024]{1,0:T(8,128)(2,1)S(1)} %get-tuple-element.82), channel_id=1, source_target_pairs={{0,1},{1,0},{2,3},{3,2},{4,5},{5,4},{6,7},{7,6},{8,9},{9,8},{10,11... | collective-permute-start | bytes 786440 | tf_op jit(solution)/shard_map/ppermute | solution.py:32
  70.0 1.6 %collective-permute-start.19 = (bf16[128,1024]{1,0:T(8,128)(2,1)S(1)}, bf16[128,1024]{1,0:T(8,128)(2,1)S(1)}, u32[]{:S(2)}, u32[]{:S(2)}) collective-permute-start(bf16[128,1024]{1,0:T(8,128)(2,1)S(1)} %slice.10), channel_id=1, source_target_pairs={{0,1},{1,0},{2,3},{3,2},{4,5},{5,4},{6,7},{7,6},{8,9},{9,8},{10,11... | collective-permute-start | bytes 786440 | tf_op jit(solution)/shard_map/ppermute | solution.py:32
  70.1 14.0 %collective-permute-start.15 = (bf16[128,1024]{1,0:T(8,128)(2,1)S(1)}, bf16[128,1024]{1,0:T(8,128)(2,1)S(1)}, u32[]{:S(2)}, u32[]{:S(2)}) collective-permute-start(bf16[128,1024]{1,0:T(8,128)(2,1)S(1)} %get-tuple-element.76), channel_id=1, source_target_pairs={{4,0},{5,1},{6,2},{7,3},{8,4},{9,5},{10,6},{11,7},{12,8},{13,9},{1... | collective-permute-start | bytes 786440 | tf_op jit(solution)/shard_map/ppermute | solution.py:27
  76.9 8.5 %collective-permute-start.22 = (bf16[128,1024]{1,0:T(8,128)(2,1)S(1)}, bf16[128,1024]{1,0:T(8,128)(2,1)S(1)}, u32[]{:S(2)}, u32[]{:S(2)}) collective-permute-start(bf16[128,1024]{1,0:T(8,128)(2,1)S(1)} %get-tuple-element.86), channel_id=1, source_target_pairs={{4,0},{5,1},{6,2},{7,3},{8,4},{9,5},{10,6},{11,7},{12,8},{13,9},{1... | collective-permute-start | bytes 786440 | tf_op jit(solution)/shard_map/ppermute | solution.py:27
  78.2 25.0 %collective-permute-start.26 = (bf16[512,1024]{1,0:T(8,128)(2,1)S(1)}, bf16[512,1024]{1,0:T(8,128)(2,1)S(1)}, u32[]{:S(2)}, u32[]{:S(2)}) collective-permute-start(bf16[512,1024]{1,0:T(8,128)(2,1)S(1)} %get-tuple-element.85.refs_0_.own_ref), channel_id=1, source_target_pairs={{0,4},{1,5},{2,6},{3,7},{4,8},{5,9},{6,10},{7,11},{8,12},{9,13},{1... | collective-permute-start | bytes 3145736 | tf_op jit(solution)/shard_map/ppermute | solution.py:27
  82.3 6.0 %collective-permute-start.27 = (bf16[128,1024]{1,0:T(8,128)(2,1)S(1)}, bf16[128,1024]{1,0:T(8,128)(2,1)S(1)}, u32[]{:S(2)}, u32[]{:S(2)}) collective-permute-start(bf16[128,1024]{1,0:T(8,128)(2,1)S(1)} %slice.11), channel_id=1, source_target_pairs={{0,1},{1,0},{2,3},{3,2},{4,5},{5,4},{6,7},{7,6},{8,9},{9,8},{10,11... | collective-permute-start | bytes 786440 | tf_op jit(solution)/shard_map/ppermute | solution.py:32
  89.2 31.1 %collective-permute-start.31 = (bf16[128,8,512]{2,1,0:T(8,128)(2,1)S(1)}, bf16[128,8,512]{2,1,0:T(8,128)(2,1)S(1)}, u32[]{:S(2)}, u32[]{:S(2)}) collective-permute-start(bf16[128,8,512]{2,1,0:T(8,128)(2,1)S(1)} %shard_map.80.refs_1_.own_ref), channel_id=1, source_target_pairs={{7,3},{11,7},{15,11},{23,19},{27,23},{31,27}} | collective-permute-start | bytes 3145736 | tf_op jit(solution)/shard_map/ppermute | solution.py:27
  89.9 18.3 %collective-permute-start.23 = (bf16[256,1024]{1,0:T(8,128)(2,1)S(1)}, bf16[256,1024]{1,0:T(8,128)(2,1)S(1)}, u32[]{:S(2)}, u32[]{:S(2)}) collective-permute-start(bf16[256,1024]{1,0:T(8,128)(2,1)S(1)} %get-tuple-element.89), channel_id=1, source_target_pairs={{0,1},{1,0},{2,3},{3,2},{4,5},{5,4},{6,7},{7,6},{8,9},{9,8},{10,11... | collective-permute-start | bytes 1572872 | tf_op jit(solution)/shard_map/ppermute | solution.py:32
  92.0 17.6 %collective-permute-start.24 = (bf16[256,1024]{1,0:T(8,128)(2,1)S(1)}, bf16[256,1024]{1,0:T(8,128)(2,1)S(1)}, u32[]{:S(2)}, u32[]{:S(2)}) collective-permute-start(bf16[256,1024]{1,0:T(8,128)(2,1)S(1)} %get-tuple-element.90), channel_id=1, source_target_pairs={{0,2},{1,3},{2,0},{3,1},{4,6},{5,7},{6,4},{7,5},{8,10},{9,11},{10,... | collective-permute-start | bytes 1572872 | tf_op jit(solution)/shard_map/ppermute | solution.py:32
  93.6 23.8 %collective-permute-start.25 = (bf16[256,1024]{1,0:T(8,128)(2,1)S(1)}, bf16[256,1024]{1,0:T(8,128)(2,1)S(1)}, u32[]{:S(2)}, u32[]{:S(2)}) collective-permute-start(bf16[256,1024]{1,0:T(8,128)(2,1)S(1)} %get-tuple-element.91), channel_id=1, source_target_pairs={{0,3},{1,2},{2,1},{3,0},{4,7},{5,6},{6,5},{7,4},{8,11},{9,10},{10,... | collective-permute-start | bytes 1572872 | tf_op jit(solution)/shard_map/ppermute | solution.py:32
  105.7 17.2 %collective-permute-start.28 = (bf16[128,1024]{1,0:T(8,128)(2,1)S(1)}, bf16[128,1024]{1,0:T(8,128)(2,1)S(1)}, u32[]{:S(2)}, u32[]{:S(2)}) collective-permute-start(bf16[128,1024]{1,0:T(8,128)(2,1)S(1)} %get-tuple-element.95), channel_id=1, source_target_pairs={{0,1},{1,0},{2,3},{3,2},{4,5},{5,4},{6,7},{7,6},{8,9},{9,8},{10,11... | collective-permute-start | bytes 786440 | tf_op jit(solution)/shard_map/ppermute | solution.py:32
  108.2 14.8 %collective-permute-start.29 = (bf16[128,1024]{1,0:T(8,128)(2,1)S(1)}, bf16[128,1024]{1,0:T(8,128)(2,1)S(1)}, u32[]{:S(2)}, u32[]{:S(2)}) collective-permute-start(bf16[128,1024]{1,0:T(8,128)(2,1)S(1)} %get-tuple-element.96), channel_id=1, source_target_pairs={{0,2},{1,3},{2,0},{3,1},{4,6},{5,7},{6,4},{7,5},{8,10},{9,11},{10,... | collective-permute-start | bytes 786440 | tf_op jit(solution)/shard_map/ppermute | solution.py:32
  109.7 18.5 %collective-permute-start.30 = (bf16[128,1024]{1,0:T(8,128)(2,1)S(1)}, bf16[128,1024]{1,0:T(8,128)(2,1)S(1)}, u32[]{:S(2)}, u32[]{:S(2)}) collective-permute-start(bf16[128,1024]{1,0:T(8,128)(2,1)S(1)} %get-tuple-element.97), channel_id=1, source_target_pairs={{0,3},{1,2},{2,1},{3,0},{4,7},{5,6},{6,5},{7,4},{8,11},{9,10},{10,... | collective-permute-start | bytes 786440 | tf_op jit(solution)/shard_map/ppermute | solution.py:32

commit v20 on v19

--- a/solution.py
+++ b/solution.py
@@ -440,7 +440,7 @@
 def project(here, band, own, high, low, sinos, groups, *tokens):
     n, side = band.shape[0], band.shape[0] // G
     cols = own.shape[1]
-    tile = 256
+    tile = cols
     many, one = pl.BlockSpec((n, tile), lambda i: (0, i)), pl.BlockSpec((side, tile), lambda i: (0, i))
     shapes = [(n, cols), (side, cols)] + [(len(group) * side, cols) for group in groups]
     return call(
@@ -471,7 +471,7 @@
 def back(here, band, own, low, high, dealt, *tokens):
     n, side = band.shape[0], band.shape[0] // G
     cols = own.shape[1]
-    tile = 256
+    tile = cols
     many = pl.BlockSpec((n, tile), lambda i: (0, i))
     one = pl.BlockSpec((side, tile), lambda i: (0, i))
     out = ((2 if dealt else 1) * side, cols)

time: 132 us -> 130 us (0.985)
  Pallas kernels: 44.9 us -> 40.1 us
  waiting for transfers between devices: 35.9 us -> 38.2 us
    ppermute x11, waiting for transfers between devices: 12.3 us -> 14.9 us  [moved(): return lax.ppermute(value, 'slab', pairs)]
    pallas_call x2, Pallas kernels: 5.55 us -> 3.06 us  [project(): call(functools.partial(project_kernel, groups), 3, grid=(cols // tile,),...]
    pallas_call x2, Pallas kernels: 5.35 us -> 3.08 us  [back(): call(functools.partial(back_kernel, bool(dealt)), 0, grid=(cols // tile,)...]
  transfers between devices with their start and end apart: 32 -> 32, of which waited for: 8 -> 8; matrix products, arithmetic and copies ran while one was open for 1% -> 1% of each run, Pallas kernels for 30% -> 27%
where the time goes in v20:
time: 130 us; the launch traced here: 129 us
  starting transfers between devices  46.9 us (36%)
  Pallas kernels  40.1 us (31%)
  waiting for transfers between devices  38.2 us (29%)
  local copies, waits for them, and re-layouts  2.57 us (2%)
    ppermute x21, starting transfers between devices, swapped(): return lax.ppermute(value, 'slab', [(i, i ^ bits) for i in range(count)])  25.8 us
    ppermute x21, waiting for transfers between devices, swapped(): return lax.ppermute(value, 'slab', [(i, i ^ bits) for i in range(count)])  23.3 us
    ppermute x11, starting transfers between devices, moved(): return lax.ppermute(value, 'slab', pairs)  21.1 us
    ppermute x11, waiting for transfers between devices, moved(): return lax.ppermute(value, 'slab', pairs)  14.9 us
    pallas_call x1, Pallas kernels, half_tv(): call(tv_kernel, 0, grid=(depth // deep,), in_specs=[SMEM] + edges + [afte...  9.99 us
    pallas_call x2, Pallas kernels, cast_rows(): call(functools.partial(cast_kernel, groups, len(edges), halves), 2, grid=...  5.97 us
    pallas_call x2, Pallas kernels, finish(): call(finish_kernel, 0, grid=(count,), in_specs=[SMEM, part] + piece_specs...  5.85 us
    pallas_call x2, Pallas kernels, split_rows(): call(functools.partial(split_kernel, groups, len(passing)), 2, grid=(coun...  3.53 us
  transfers between devices with their start and end apart: 32, of which 8 were waited for; matrix products, arithmetic and copies ran while one was open for 1% of the time, Pallas kernels for 27%

profile of v20, /device:TPU:1, one launch (start us, length us, event | category | flops | bytes accessed | tf_op | source)
XLA Modules:
  0.0 128.7 jit_solution(8701721928445581716)
XLA Ops:
  0.6 2.5 %shard_map.68 = (bf16[128,1024]{1,0:T(8,128)(2,1)}, bf16[144,1024]{1,0:T(8,128)(2,1)S(1)}, bf16[128,1024]{1,0:T(8,128)(2,1)}, bf16[144,1024]{1,0:T(8,128)(2,1)S(1)}) custom-call(s32[1]{0:T(128)} %bitcast.here_ref, f32[1024,1024]{1,0:T(8,128)} %bitcast.2, f32[1024,1024]{1,0:T(8,128)} %bitcast.3, f32[1024,1024]{1,0:T(8,128)} %bitcast.4, f32[1024,1024]{1,0:T(8,128)} %bitcast.5), custom_call_target="tpu_custom_call" | custom-call | flops 2300000000 | bytes 1000 | tf_op jit(solution)/shard_map/pallas_call | solution.py:115
  3.2 2.7 %collective-permute-start.1 = (bf16[128,1024]{1,0:T(8,128)(2,1)}, bf16[128,1024]{1,0:T(8,128)(2,1)}, u32[]{:S(2)}, u32[]{:S(2)}) collective-permute-start(bf16[128,1024]{1,0:T(8,128)(2,1)} %get-tuple-element.52), channel_id=1, source_target_pairs={{0,2},{1,3},{2,0},{3,1},{4,6},{5,7},{6,4},{7,5},{8,10},{9,11},{10,... | collective-permute-start | bytes 786440 | tf_op jit(solution)/shard_map/ppermute | solution.py:32
  6.0 3.4 %shard_map.69 = (bf16[128,1024]{1,0:T(8,128)(2,1)}, bf16[128,1024]{1,0:T(8,128)(2,1)S(1)}, bf16[256,1024]{1,0:T(8,128)(2,1)}, bf16[128,8,512]{2,1,0:T(8,128)(2,1)}, bf16[128,8,512]{2,1,0:T(8,128)(2,1)S(1)}) custom-call(s32[1]{0:T(128)} %bitcast.here_ref, f32[1024,1024]{1,0:T(8,128)} %bitcast.6, f32[1024,1024]{1,0:T(8,128)} %bitcast.7, ...), custom_call_target="tpu_custom_call" | custom-call | flops 2300000000 | bytes 1000 | tf_op jit(solution)/shard_map/pallas_call | solution.py:115
  10.1 0.7 collective-permute-start.4
  10.8 4.2 %collective-permute-start.5 = (bf16[256,1024]{1,0:T(8,128)(2,1)}, bf16[256,1024]{1,0:T(8,128)(2,1)}, u32[]{:S(2)}, u32[]{:S(2)}) collective-permute-start(bf16[256,1024]{1,0:T(8,128)(2,1)} %get-tuple-element.59), channel_id=1, source_target_pairs={{0,2},{1,3},{2,0},{3,1},{4,6},{5,7},{6,4},{7,5},{8,10},{9,11},{10,... | collective-permute-start | bytes 1572872 | tf_op jit(solution)/shard_map/ppermute | solution.py:32
  15.1 0.8 copy.13.offset_ref
  15.9 0.9 copy-done.4
  16.8 1.6 %shard_map.70 = (bf16[512,1152]{1,0:T(8,128)(2,1)S(1)}, bf16[512,1152]{1,0:T(8,128)(2,1)S(1)}) custom-call(s32[1]{0:T(128)} %bitcast.here_ref, s32[16,6]{1,0:T(8,128)S(1)} %copy.12.cover_ref, s32[16,6]{1,0:T(8,128)S(1)} %copy.13.offset_ref, bf16[8,128,128]{2,1,0:T(8,128)(2,1)S(1)} %copy-done, bf16[128,1024]{1,0:T(8,128)(2,1)S(1)} %copy-done.4), custom_call_target="tpu_custom_call" | custom-call | flops 10350000128 | bytes 1000 | tf_op jit(solution)/shard_map/pallas_call | solution.py:415
  18.5 0.7 collective-permute-start.10
  19.3 1.2 shard_map.71
  20.7 1.3 collective-permute-start.3
  22.0 8.4 %collective-permute-done.5.refs_0_.refs_2_ = bf16[256,1024]{1,0:T(8,128)(2,1)} collective-permute-done((bf16[256,1024]{1,0:T(8,128)(2,1)}, bf16[256,1024]{1,0:T(8,128)(2,1)}, u32[]{:S(2)}, u32[]{:S(2)}) %collective-permute-start.5) | collective-permute-done | bytes 524320 | tf_op jit(solution)/shard_map/ppermute | solution.py:32
  30.4 1.8 %shard_map.72 = (bf16[128,1024]{1,0:T(8,128)(2,1)S(1)}, bf16[128,1024]{1,0:T(8,128)(2,1)S(1)}, bf16[256,1024]{1,0:T(8,128)(2,1)S(1)}, bf16[128,1024]{1,0:T(8,128)(2,1)S(1)}) custom-call(s32[1]{0:T(128)} %bitcast.here_ref, bf16[128,8,1024]{2,1,0:T(8,128)(2,1)} %refs_2_.3, bf16[128,8,512]{2,1,0:T(8,128)(2,1)S(1)} %collective-permute-done.4.got_ref, ...), custom_call_target="tpu_custom_call" | custom-call | flops 2300000000 | bytes 1000 | tf_op jit(solution)/shard_map/pallas_call | solution.py:196
  33.0 1.5 %collective-permute-start.9 = (bf16[256,1024]{1,0:T(8,128)(2,1)S(1)}, bf16[256,1024]{1,0:T(8,128)(2,1)S(1)}, u32[]{:S(2)}, u32[]{:S(2)}) collective-permute-start(bf16[256,1024]{1,0:T(8,128)(2,1)S(1)} %get-tuple-element.64), channel_id=1, source_target_pairs={{0,2},{1,3},{2,0},{3,1},{4,6},{5,7},{6,4},{7,5},{8,10},{9,11},{10,... | collective-permute-start | bytes 1572872 | tf_op jit(solution)/shard_map/ppermute | solution.py:32
  34.5 3.2 %collective-permute-start.8 = (bf16[144,1024]{1,0:T(8,128)(2,1)S(1)}, bf16[144,1024]{1,0:T(8,128)(2,1)S(1)}, u32[]{:S(2)}, u32[]{:S(2)}) collective-permute-start(bf16[144,1024]{1,0:T(8,128)(2,1)S(1)} %get-tuple-element.62), channel_id=1, source_target_pairs={{0,4},{1,5},{2,6},{3,7},{4,8},{5,9},{6,10},{7,11},{8,12},{9,13},{1... | collective-permute-start | bytes 884744 | tf_op jit(solution)/shard_map/ppermute | solution.py:27
  37.7 1.2 shard_map.73
  38.9 3.2 %collective-permute-start.13 = (bf16[128,1024]{1,0:T(8,128)(2,1)S(1)}, bf16[128,1024]{1,0:T(8,128)(2,1)S(1)}, u32[]{:S(2)}, u32[]{:S(2)}) collective-permute-start(bf16[128,1024]{1,0:T(8,128)(2,1)S(1)} %get-tuple-element.72), channel_id=1, source_target_pairs={{0,4},{1,5},{2,6},{3,7},{4,8},{5,9},{6,10},{7,11},{8,12},{9,13},{1... | collective-permute-start | bytes 786440 | tf_op jit(solution)/shard_map/ppermute | solution.py:27
  42.1 1.7 %shard_map.74 = (bf16[128,1024]{1,0:T(8,128)(2,1)S(1)}, bf16[128,1024]{1,0:T(8,128)(2,1)S(1)}, bf16[256,1024]{1,0:T(8,128)(2,1)S(1)}) custom-call(s32[1]{0:T(128)} %bitcast.here_ref, bf16[128,8,1024]{2,1,0:T(8,128)(2,1)} %refs_2_.3, bf16[128,8,512]{2,1,0:T(8,128)(2,1)S(1)} %collective-permute-done.10.got_ref, ...), custom_call_target="tpu_custom_call" | custom-call | flops 2300000000 | bytes 1000 | tf_op jit(solution)/shard_map/pallas_call | solution.py:196
  43.8 2.2 %collective-permute-done.9.refs_2_ = bf16[256,1024]{1,0:T(8,128)(2,1)S(1)} collective-permute-done((bf16[256,1024]{1,0:T(8,128)(2,1)S(1)}, bf16[256,1024]{1,0:T(8,128)(2,1)S(1)}, u32[]{:S(2)}, u32[]{:S(2)}) %collective-permute-start.9) | collective-permute-done | bytes 524320 | tf_op jit(solution)/shard_map/ppermute | solution.py:32
  46.1 1.3 %collective-permute-start.12 = (bf16[128,1024]{1,0:T(8,128)(2,1)S(1)}, bf16[128,1024]{1,0:T(8,128)(2,1)S(1)}, u32[]{:S(2)}, u32[]{:S(2)}) collective-permute-start(bf16[128,1024]{1,0:T(8,128)(2,1)S(1)} %slice.9), channel_id=1, source_target_pairs={{0,1},{1,0},{2,3},{3,2},{4,5},{5,4},{6,7},{7,6},{8,9},{9,8},{10,11... | collective-permute-start | bytes 786440 | tf_op jit(solution)/shard_map/ppermute | solution.py:32
  47.4 1.3 collective-permute-start.16
  49.0 2.2 %collective-permute-start.18 = (bf16[256,1024]{1,0:T(8,128)(2,1)S(1)}, bf16[256,1024]{1,0:T(8,128)(2,1)S(1)}, u32[]{:S(2)}, u32[]{:S(2)}) collective-permute-start(bf16[256,1024]{1,0:T(8,128)(2,1)S(1)} %get-tuple-element.78), channel_id=1, source_target_pairs={{0,2},{1,3},{2,0},{3,1},{4,6},{5,7},{6,4},{7,5},{8,10},{9,11},{10,... | collective-permute-start | bytes 1572872 | tf_op jit(solution)/shard_map/ppermute | solution.py:32
  51.3 1.5 %shard_map.75 = (bf16[512,1024]{1,0:T(8,128)(2,1)S(1)}, bf16[128,1024]{1,0:T(8,128)(2,1)S(1)}, bf16[128,1024]{1,0:T(8,128)(2,1)S(1)}, bf16[256,1024]{1,0:T(8,128)(2,1)S(1)}) custom-call(s32[1]{0:T(128)} %bitcast.here_ref, bf16[512,1152]{1,0:T(8,128)(2,1)S(1)} %get-tuple-element.55.refs_4_.band_ref, bf16[528,1024]{1,0:T(8,128)(2,1)S(1)} %get-tuple-element.56.own_ref, ...), custom_call_target="tpu_custom_call" | custom-call | flops 3449999872 | bytes 1000 | tf_op jit(solution)/shard_map/pallas_call | solution.py:446
  52.9 3.3 %collective-permute-start.14 = (bf16[512,1024]{1,0:T(8,128)(2,1)S(1)}, bf16[512,1024]{1,0:T(8,128)(2,1)S(1)}, u32[]{:S(2)}, u32[]{:S(2)}) collective-permute-start(bf16[512,1024]{1,0:T(8,128)(2,1)S(1)} %get-tuple-element.73.refs_0_.own_ref), channel_id=1, source_target_pairs={{0,4},{1,5},{2,6},{3,7},{4,8},{5,9},{6,10},{7,11},{8,12},{9,13},{1... | collective-permute-start | bytes 3145736 | tf_op jit(solution)/shard_map/ppermute | solution.py:27
  56.2 2.4 %collective-permute-start.20 = (bf16[128,1024]{1,0:T(8,128)(2,1)S(1)}, bf16[128,1024]{1,0:T(8,128)(2,1)S(1)}, u32[]{:S(2)}, u32[]{:S(2)}) collective-permute-start(bf16[128,1024]{1,0:T(8,128)(2,1)S(1)} %get-tuple-element.82), channel_id=1, source_target_pairs={{0,1},{1,0},{2,3},{3,2},{4,5},{5,4},{6,7},{7,6},{8,9},{9,8},{10,11... | collective-permute-start | bytes 786440 | tf_op jit(solution)/shard_map/ppermute | solution.py:32
  58.6 10.0 %shard_map.76 = (f32[128,8,1024]{2,1,0:T(8,128)}, f32[8,128]{1,0:T(8,128)S(1)}) custom-call(s32[1]{0:T(128)} %bitcast.here_ref, bf16[144,1024]{1,0:T(8,128)(2,1)S(1)} %collective-permute-done.refs_1_.near_ref, bf16[528,1024]{1,0:T(8,128)(2,1)S(1)} %collective-permute-done.3.high_ref.next_level_ref, ...), custom_call_target="tpu_custom_call" | custom-call | bytes 1000 | tf_op jit(solution)/shard_map/pallas_call | solution.py:546
  68.8 1.3 collective-permute-start.15
  70.2 4.0 %collective-permute-done.16.high_ref = bf16[512,1024]{1,0:T(8,128)(2,1)S(1)} collective-permute-done((bf16[512,1024]{1,0:T(8,128)(2,1)S(1)}, bf16[512,1024]{1,0:T(8,128)(2,1)S(1)}, u32[]{:S(2)}, u32[]{:S(2)}) %collective-permute-start.16) | collective-permute-done | bytes 1048608 | tf_op jit(solution)/shard_map/ppermute | solution.py:27
  74.2 1.5 %shard_map.77 = (bf16[512,1024]{1,0:T(8,128)(2,1)S(1)}, bf16[128,1024]{1,0:T(8,128)(2,1)S(1)}) custom-call(s32[1]{0:T(128)} %bitcast.here_ref, bf16[512,1152]{1,0:T(8,128)(2,1)S(1)} %get-tuple-element.55.refs_4_.band_ref, bf16[512,1024]{1,0:T(8,128)(2,1)S(1)} %get-tuple-element.69.refs_0_.own_ref, bf16[512,1024]{1,0:T(8,128)(2,1)S(1)} %collective-permute-done.16.high_ref, ...), custom_call_target="tpu_custom_call" | custom-call | flops 3449999872 | bytes 1000 | tf_op jit(solution)/shard_map/pallas_call | solution.py:446
  75.7 1.3 %collective-permute-start.22 = (bf16[128,1024]{1,0:T(8,128)(2,1)S(1)}, bf16[128,1024]{1,0:T(8,128)(2,1)S(1)}, u32[]{:S(2)}, u32[]{:S(2)}) collective-permute-start(bf16[128,1024]{1,0:T(8,128)(2,1)S(1)} %get-tuple-element.86), channel_id=1, source_target_pairs={{4,0},{5,1},{6,2},{7,3},{8,4},{9,5},{10,6},{11,7},{12,8},{13,9},{1... | collective-permute-start | bytes 786440 | tf_op jit(solution)/shard_map/ppermute | solution.py:27
  77.0 4.1 %collective-permute-start.26 = (bf16[512,1024]{1,0:T(8,128)(2,1)S(1)}, bf16[512,1024]{1,0:T(8,128)(2,1)S(1)}, u32[]{:S(2)}, u32[]{:S(2)}) collective-permute-start(bf16[512,1024]{1,0:T(8,128)(2,1)S(1)} %get-tuple-element.85.refs_0_.own_ref), channel_id=1, source_target_pairs={{0,4},{1,5},{2,6},{3,7},{4,8},{5,9},{6,10},{7,11},{8,12},{9,13},{1... | collective-permute-start | bytes 3145736 | tf_op jit(solution)/shard_map/ppermute | solution.py:27
  81.1 1.8 %collective-permute-start.27 = (bf16[128,1024]{1,0:T(8,128)(2,1)S(1)}, bf16[128,1024]{1,0:T(8,128)(2,1)S(1)}, u32[]{:S(2)}, u32[]{:S(2)}) collective-permute-start(bf16[128,1024]{1,0:T(8,128)(2,1)S(1)} %slice.11), channel_id=1, source_target_pairs={{0,1},{1,0},{2,3},{3,2},{4,5},{5,4},{6,7},{7,6},{8,9},{9,8},{10,11... | collective-permute-start | bytes 786440 | tf_op jit(solution)/shard_map/ppermute | solution.py:32
  82.9 1.4 %collective-permute-done.22.refs_1_.high_ref = bf16[128,1024]{1,0:T(8,128)(2,1)S(1)} collective-permute-done((bf16[128,1024]{1,0:T(8,128)(2,1)S(1)}, bf16[128,1024]{1,0:T(8,128)(2,1)S(1)}, u32[]{:S(2)}, u32[]{:S(2)}) %collective-permute-start.22) | collective-permute-done | bytes 262176 | tf_op jit(solution)/shard_map/ppermute | solution.py:27
  84.3 1.6 %shard_map.78 = (bf16[256,1024]{1,0:T(8,128)(2,1)S(1)}, bf16[256,1024]{1,0:T(8,128)(2,1)S(1)}, bf16[256,1024]{1,0:T(8,128)(2,1)S(1)}, bf16[256,1024]{1,0:T(8,128)(2,1)S(1)}) custom-call(s32[1]{0:T(128)} %bitcast.here_ref, bf16[512,1152]{1,0:T(8,128)(2,1)S(1)} %get-tuple-element.75.band_ref, bf16[512,1024]{1,0:T(8,128)(2,1)S(1)} %get-tuple-element.73.refs_0_.own_ref, ...), custom_call_target="tpu_custom_call" | custom-call | bytes 1000 | tf_op jit(solution)/shard_map/pallas_call | solution.py:478
  85.9 0.9 shard_map.80.refs_1_.own_ref
  86.7 0.7 collective-permute-start.31
  87.5 2.1 %collective-permute-start.23 = (bf16[256,1024]{1,0:T(8,128)(2,1)S(1)}, bf16[256,1024]{1,0:T(8,128)(2,1)S(1)}, u32[]{:S(2)}, u32[]{:S(2)}) collective-permute-start(bf16[256,1024]{1,0:T(8,128)(2,1)S(1)} %get-tuple-element.89), channel_id=1, source_target_pairs={{0,1},{1,0},{2,3},{3,2},{4,5},{5,4},{6,7},{7,6},{8,9},{9,8},{10,11... | collective-permute-start | bytes 1572872 | tf_op jit(solution)/shard_map/ppermute | solution.py:32
  89.6 1.5 %collective-permute-start.24 = (bf16[256,1024]{1,0:T(8,128)(2,1)S(1)}, bf16[256,1024]{1,0:T(8,128)(2,1)S(1)}, u32[]{:S(2)}, u32[]{:S(2)}) collective-permute-start(bf16[256,1024]{1,0:T(8,128)(2,1)S(1)} %get-tuple-element.90), channel_id=1, source_target_pairs={{0,2},{1,3},{2,0},{3,1},{4,6},{5,7},{6,4},{7,5},{8,10},{9,11},{10,... | collective-permute-start | bytes 1572872 | tf_op jit(solution)/shard_map/ppermute | solution.py:32
  91.3 1.2 shard_map.79
  92.5 9.5 %collective-permute-done.26.low_ref = bf16[512,1024]{1,0:T(8,128)(2,1)S(1)} collective-permute-done((bf16[512,1024]{1,0:T(8,128)(2,1)S(1)}, bf16[512,1024]{1,0:T(8,128)(2,1)S(1)}, u32[]{:S(2)}, u32[]{:S(2)}) %collective-permute-start.26) | collective-permute-done | bytes 1048608 | tf_op jit(solution)/shard_map/ppermute | solution.py:27
  102.0 1.5 %shard_map.81 = (bf16[128,1024]{1,0:T(8,128)(2,1)S(1)}, bf16[128,1024]{1,0:T(8,128)(2,1)S(1)}, bf16[128,1024]{1,0:T(8,128)(2,1)S(1)}, bf16[128,1024]{1,0:T(8,128)(2,1)S(1)}) custom-call(s32[1]{0:T(128)} %bitcast.here_ref, bf16[512,1152]{1,0:T(8,128)(2,1)S(1)} %get-tuple-element.75.band_ref, bf16[512,1024]{1,0:T(8,128)(2,1)S(1)} %get-tuple-element.85.refs_0_.own_ref, ...), custom_call_target="tpu_custom_call" | custom-call | bytes 1000 | tf_op jit(solution)/shard_map/pallas_call | solution.py:478
  103.5 2.4 %collective-permute-start.28 = (bf16[128,1024]{1,0:T(8,128)(2,1)S(1)}, bf16[128,1024]{1,0:T(8,128)(2,1)S(1)}, u32[]{:S(2)}, u32[]{:S(2)}) collective-permute-start(bf16[128,1024]{1,0:T(8,128)(2,1)S(1)} %get-tuple-element.95), channel_id=1, source_target_pairs={{0,1},{1,0},{2,3},{3,2},{4,5},{5,4},{6,7},{7,6},{8,9},{9,8},{10,11... | collective-permute-start | bytes 786440 | tf_op jit(solution)/shard_map/ppermute | solution.py:32
  106.0 1.5 %collective-permute-start.29 = (bf16[128,1024]{1,0:T(8,128)(2,1)S(1)}, bf16[128,1024]{1,0:T(8,128)(2,1)S(1)}, u32[]{:S(2)}, u32[]{:S(2)}) collective-permute-start(bf16[128,1024]{1,0:T(8,128)(2,1)S(1)} %get-tuple-element.96), channel_id=1, source_target_pairs={{0,2},{1,3},{2,0},{3,1},{4,6},{5,7},{6,4},{7,5},{8,10},{9,11},{10,... | collective-permute-start | bytes 786440 | tf_op jit(solution)/shard_map/ppermute | solution.py:32
  107.7 7.2 %collective-permute-done.25.refs_3_ = bf16[256,1024]{1,0:T(8,128)(2,1)S(1)} collective-permute-done((bf16[256,1024]{1,0:T(8,128)(2,1)S(1)}, bf16[256,1024]{1,0:T(8,128)(2,1)S(1)}, u32[]{:S(2)}, u32[]{:S(2)}) %collective-permute-start.25) | collective-permute-done | bytes 524320 | tf_op jit(solution)/shard_map/ppermute | solution.py:32
  115.0 2.9 %shard_map.82.tv_ref = f32[128,8,1024]{2,1,0:T(8,128)} custom-call(s32[1]{0:T(128)} %bitcast.here_ref, f32[128,8,1024]{2,1,0:T(8,128)} %get-tuple-element.88.tv_ref, bf16[256,1024]{1,0:T(8,128)(2,1)S(1)} %get-tuple-element.87.refs_4_.refs_0_, bf16[256,1024]{1,0:T(8,128)(2,1)S(1)} %collective-permute-done.23.refs_1_, ...), custom_call_target="tpu_custom_call", output_to_operand_aliasing={{}: (1, {})} | custom-call | bytes 1000 | tf_op jit(solution)/shard_map/pallas_call | solution.py:367
  117.9 2.6 %shard_map.83.refs_4_ = bf16[128,8,1024]{2,1,0:T(8,128)(2,1)} custom-call(s32[1]{0:T(128)} %bitcast.here_ref, bf16[128,8,512]{2,1,0:T(8,128)(2,1)S(1)} %shard_map.80.refs_1_.own_ref, bf16[128,8,512]{2,1,0:T(8,128)(2,1)S(1)} %collective-permute-done.31.above_ref, bf16[256,1024]{1,0:T(8,128)(2,1)S(1)} %get-tuple-element.87.refs_4_.refs_0_, ...), custom_call_target="tpu_custom_call" | custom-call | bytes 1000 | tf_op jit(solution)/shard_map/pallas_call | solution.py:345
  120.5 5.3 %collective-permute-done.30.refs_3_ = bf16[128,1024]{1,0:T(8,128)(2,1)S(1)} collective-permute-done((bf16[128,1024]{1,0:T(8,128)(2,1)S(1)}, bf16[128,1024]{1,0:T(8,128)(2,1)S(1)}, u32[]{:S(2)}, u32[]{:S(2)}) %collective-permute-start.30) | collective-permute-done | bytes 262176 | tf_op jit(solution)/shard_map/ppermute | solution.py:32
  125.8 2.9 %shard_map.84 = f32[128,8,1024]{2,1,0:T(8,128)} custom-call(s32[1]{0:T(128)} %bitcast.here_ref, f32[128,8,1024]{2,1,0:T(8,128)} %shard_map.82.tv_ref, bf16[128,1024]{1,0:T(8,128)(2,1)S(1)} %get-tuple-element.94.refs_4_.refs_0_, bf16[128,1024]{1,0:T(8,128)(2,1)S(1)} %collective-permute-done.28.refs_1_, ...), custom_call_target="tpu_custom_call", output_to_operand_aliasing={{}: (1, {})} | custom-call | bytes 1000 | tf_op jit(solution)/shard_map/pallas_call | solution.py:367
  (52 shorter events, 3.2 us)
Async XLA Ops:
  3.2 16.1 %collective-permute-start = (bf16[144,1024]{1,0:T(8,128)(2,1)S(1)}, bf16[144,1024]{1,0:T(8,128)(2,1)S(1)}, u32[]{:S(2)}, u32[]{:S(2)}) collective-permute-start(bf16[144,1024]{1,0:T(8,128)(2,1)S(1)} %get-tuple-element.50.refs_4_), channel_id=1, source_target_pairs={{0,1},{1,0},{2,3},{3,2},{4,5},{5,4},{6,7},{7,6},{8,9},{9,8},{10,11... | collective-permute-start | bytes 884744 | tf_op jit(solution)/shard_map/ppermute | solution.py:32
  3.2 15.3 %collective-permute-start.1 = (bf16[128,1024]{1,0:T(8,128)(2,1)}, bf16[128,1024]{1,0:T(8,128)(2,1)}, u32[]{:S(2)}, u32[]{:S(2)}) collective-permute-start(bf16[128,1024]{1,0:T(8,128)(2,1)} %get-tuple-element.52), channel_id=1, source_target_pairs={{0,2},{1,3},{2,0},{3,1},{4,6},{5,7},{6,4},{7,5},{8,10},{9,11},{10,... | collective-permute-start | bytes 786440 | tf_op jit(solution)/shard_map/ppermute | solution.py:32
  5.9 9.1 %copy-start.6 = (s32[16,6]{0,1:T(8,128)S(1)}, s32[16,6]{0,1:T(8,128)}, u32[]{:S(2)}) copy-start(s32[16,6]{0,1:T(8,128)} %param.8) | copy-start | bytes 1156
  5.9 10.0 %copy-start = (bf16[8,128,128]{2,1,0:T(8,128)(2,1)S(1)}, bf16[8,128,128]{2,1,0:T(8,128)(2,1)}, u32[]{:S(2)}) copy-start(bf16[8,128,128]{2,1,0:T(8,128)(2,1)} %refs_0_.1) | copy-start | bytes 786436
  5.9 13.3 %collective-permute-start.2 = (bf16[144,1024]{1,0:T(8,128)(2,1)S(1)}, bf16[144,1024]{1,0:T(8,128)(2,1)S(1)}, u32[]{:S(2)}, u32[]{:S(2)}) collective-permute-start(bf16[144,1024]{1,0:T(8,128)(2,1)S(1)} %get-tuple-element.53), channel_id=1, source_target_pairs={{0,3},{1,2},{2,1},{3,0},{4,7},{5,6},{6,5},{7,4},{8,11},{9,10},{10,... | collective-permute-start | bytes 884744 | tf_op jit(solution)/shard_map/ppermute | solution.py:32
  9.4 0.7 copy-start.3
  10.1 20.3 %collective-permute-start.4 = (bf16[128,8,512]{2,1,0:T(8,128)(2,1)}, bf16[128,8,512]{2,1,0:T(8,128)(2,1)S(1)}, u32[]{:S(2)}, u32[]{:S(2)}) collective-permute-start(bf16[128,8,512]{2,1,0:T(8,128)(2,1)} %get-tuple-element.58), channel_id=1, source_target_pairs={{3,7},{7,11},{11,15},{19,23},{23,27},{27,31}} | collective-permute-start | bytes 3145736 | tf_op jit(solution)/shard_map/ppermute | solution.py:27
  10.8 19.6 %collective-permute-start.5 = (bf16[256,1024]{1,0:T(8,128)(2,1)}, bf16[256,1024]{1,0:T(8,128)(2,1)}, u32[]{:S(2)}, u32[]{:S(2)}) collective-permute-start(bf16[256,1024]{1,0:T(8,128)(2,1)} %get-tuple-element.59), channel_id=1, source_target_pairs={{0,2},{1,3},{2,0},{3,1},{4,6},{5,7},{6,4},{7,5},{8,10},{9,11},{10,... | collective-permute-start | bytes 1572872 | tf_op jit(solution)/shard_map/ppermute | solution.py:32
  15.9 1.0 copy-start.4
  16.8 2.4 %copy-start.2 = (bf16[128,1024]{1,0:T(8,128)(2,1)S(1)}, bf16[128,1024]{1,0:T(8,128)(2,1)}, u32[]{:S(2)}) copy-start(bf16[128,1024]{1,0:T(8,128)(2,1)} %get-tuple-element.51.refs_0_) | copy-start | bytes 786436
  18.5 23.6 %collective-permute-start.10 = (bf16[128,8,512]{2,1,0:T(8,128)(2,1)S(1)}, bf16[128,8,512]{2,1,0:T(8,128)(2,1)S(1)}, u32[]{:S(2)}, u32[]{:S(2)}) collective-permute-start(bf16[128,8,512]{2,1,0:T(8,128)(2,1)S(1)} %get-tuple-element.66), channel_id=1, source_target_pairs={{3,7},{7,11},{11,15},{19,23},{23,27},{27,31}} | collective-permute-start | bytes 3145736 | tf_op jit(solution)/shard_map/ppermute | solution.py:27
  19.3 1.2 copy-start.5
  20.5 17.2 %copy-start.1 = (bf16[128,1024]{1,0:T(8,128)(2,1)S(1)}, bf16[128,1024]{1,0:T(8,128)(2,1)}, u32[]{:S(2)}) copy-start(bf16[128,1024]{1,0:T(8,128)(2,1)} %get-tuple-element.67.refs_0_) | copy-start | bytes 786436
  20.5 9.9 %collective-permute-start.6 = (bf16[128,1024]{1,0:T(8,128)(2,1)S(1)}, bf16[128,1024]{1,0:T(8,128)(2,1)S(1)}, u32[]{:S(2)}, u32[]{:S(2)}) collective-permute-start(bf16[128,1024]{1,0:T(8,128)(2,1)S(1)} %copy-done.5), channel_id=1, source_target_pairs={{0,1},{1,0},{2,3},{3,2},{4,5},{5,4},{6,7},{7,6},{8,9},{9,8},{10,11... | collective-permute-start | bytes 786440 | tf_op jit(solution)/shard_map/ppermute | solution.py:32
  20.7 28.0 %collective-permute-start.3 = (bf16[528,1024]{1,0:T(8,128)(2,1)S(1)}, bf16[528,1024]{1,0:T(8,128)(2,1)S(1)}, u32[]{:S(2)}, u32[]{:S(2)}) collective-permute-start(bf16[528,1024]{1,0:T(8,128)(2,1)S(1)} %get-tuple-element.56.own_ref), channel_id=1, source_target_pairs={{4,0},{5,1},{6,2},{7,3},{8,4},{9,5},{10,6},{11,7},{12,8},{13,9},{1... | collective-permute-start | bytes 3244040 | tf_op jit(solution)/shard_map/ppermute | solution.py:27
  32.2 2.3 %collective-permute-start.7 = (bf16[128,1024]{1,0:T(8,128)(2,1)S(1)}, bf16[128,1024]{1,0:T(8,128)(2,1)S(1)}, u32[]{:S(2)}, u32[]{:S(2)}) collective-permute-start(bf16[128,1024]{1,0:T(8,128)(2,1)S(1)} %get-tuple-element.61), channel_id=1, source_target_pairs={{0,1},{1,0},{2,3},{3,2},{4,5},{5,4},{6,7},{7,6},{8,9},{9,8},{10,11... | collective-permute-start | bytes 786440 | tf_op jit(solution)/shard_map/ppermute | solution.py:32
  32.9 4.8 %collective-permute-start.11 = (bf16[128,1024]{1,0:T(8,128)(2,1)S(1)}, bf16[128,1024]{1,0:T(8,128)(2,1)S(1)}, u32[]{:S(2)}, u32[]{:S(2)}) collective-permute-start(bf16[128,1024]{1,0:T(8,128)(2,1)S(1)} %get-tuple-element.68), channel_id=1, source_target_pairs={{0,1},{1,0},{2,3},{3,2},{4,5},{5,4},{6,7},{7,6},{8,9},{9,8},{10,11... | collective-permute-start | bytes 786440 | tf_op jit(solution)/shard_map/ppermute | solution.py:32
  33.0 13.1 %collective-permute-start.9 = (bf16[256,1024]{1,0:T(8,128)(2,1)S(1)}, bf16[256,1024]{1,0:T(8,128)(2,1)S(1)}, u32[]{:S(2)}, u32[]{:S(2)}) collective-permute-start(bf16[256,1024]{1,0:T(8,128)(2,1)S(1)} %get-tuple-element.64), channel_id=1, source_target_pairs={{0,2},{1,3},{2,0},{3,1},{4,6},{5,7},{6,4},{7,5},{8,10},{9,11},{10,... | collective-permute-start | bytes 1572872 | tf_op jit(solution)/shard_map/ppermute | solution.py:32
  34.5 16.8 %collective-permute-start.8 = (bf16[144,1024]{1,0:T(8,128)(2,1)S(1)}, bf16[144,1024]{1,0:T(8,128)(2,1)S(1)}, u32[]{:S(2)}, u32[]{:S(2)}) collective-permute-start(bf16[144,1024]{1,0:T(8,128)(2,1)S(1)} %get-tuple-element.62), channel_id=1, source_target_pairs={{0,4},{1,5},{2,6},{3,7},{4,8},{5,9},{6,10},{7,11},{8,12},{9,13},{1... | collective-permute-start | bytes 884744 | tf_op jit(solution)/shard_map/ppermute | solution.py:27
  38.9 10.1 %collective-permute-start.13 = (bf16[128,1024]{1,0:T(8,128)(2,1)S(1)}, bf16[128,1024]{1,0:T(8,128)(2,1)S(1)}, u32[]{:S(2)}, u32[]{:S(2)}) collective-permute-start(bf16[128,1024]{1,0:T(8,128)(2,1)S(1)} %get-tuple-element.72), channel_id=1, source_target_pairs={{0,4},{1,5},{2,6},{3,7},{4,8},{5,9},{6,10},{7,11},{8,12},{9,13},{1... | collective-permute-start | bytes 786440 | tf_op jit(solution)/shard_map/ppermute | solution.py:27
  46.1 5.2 %collective-permute-start.12 = (bf16[128,1024]{1,0:T(8,128)(2,1)S(1)}, bf16[128,1024]{1,0:T(8,128)(2,1)S(1)}, u32[]{:S(2)}, u32[]{:S(2)}) collective-permute-start(bf16[128,1024]{1,0:T(8,128)(2,1)S(1)} %slice.9), channel_id=1, source_target_pairs={{0,1},{1,0},{2,3},{3,2},{4,5},{5,4},{6,7},{7,6},{8,9},{9,8},{10,11... | collective-permute-start | bytes 786440 | tf_op jit(solution)/shard_map/ppermute | solution.py:32
  47.4 26.8 %collective-permute-start.16 = (bf16[512,1024]{1,0:T(8,128)(2,1)S(1)}, bf16[512,1024]{1,0:T(8,128)(2,1)S(1)}, u32[]{:S(2)}, u32[]{:S(2)}) collective-permute-start(bf16[512,1024]{1,0:T(8,128)(2,1)S(1)} %get-tuple-element.69.refs_0_.own_ref), channel_id=1, source_target_pairs={{4,0},{5,1},{6,2},{7,3},{8,4},{9,5},{10,6},{11,7},{12,8},{13,9},{1... | collective-permute-start | bytes 3145736 | tf_op jit(solution)/shard_map/ppermute | solution.py:27
  48.7 4.1 %collective-permute-start.17 = (bf16[128,1024]{1,0:T(8,128)(2,1)S(1)}, bf16[128,1024]{1,0:T(8,128)(2,1)S(1)}, u32[]{:S(2)}, u32[]{:S(2)}) collective-permute-start(bf16[128,1024]{1,0:T(8,128)(2,1)S(1)} %get-tuple-element.77), channel_id=1, source_target_pairs={{0,1},{1,0},{2,3},{3,2},{4,5},{5,4},{6,7},{7,6},{8,9},{9,8},{10,11... | collective-permute-start | bytes 786440 | tf_op jit(solution)/shard_map/ppermute | solution.py:32
  49.0 19.6 %collective-permute-start.18 = (bf16[256,1024]{1,0:T(8,128)(2,1)S(1)}, bf16[256,1024]{1,0:T(8,128)(2,1)S(1)}, u32[]{:S(2)}, u32[]{:S(2)}) collective-permute-start(bf16[256,1024]{1,0:T(8,128)(2,1)S(1)} %get-tuple-element.78), channel_id=1, source_target_pairs={{0,2},{1,3},{2,0},{3,1},{4,6},{5,7},{6,4},{7,5},{8,10},{9,11},{10,... | collective-permute-start | bytes 1572872 | tf_op jit(solution)/shard_map/ppermute | solution.py:32
  52.8 21.4 %collective-permute-start.21 = (bf16[256,1024]{1,0:T(8,128)(2,1)S(1)}, bf16[256,1024]{1,0:T(8,128)(2,1)S(1)}, u32[]{:S(2)}, u32[]{:S(2)}) collective-permute-start(bf16[256,1024]{1,0:T(8,128)(2,1)S(1)} %get-tuple-element.84), channel_id=1, source_target_pairs={{0,2},{1,3},{2,0},{3,1},{4,6},{5,7},{6,4},{7,5},{8,10},{9,11},{10,... | collective-permute-start | bytes 1572872 | tf_op jit(solution)/shard_map/ppermute | solution.py:32
  52.9 31.4 %collective-permute-start.14 = (bf16[512,1024]{1,0:T(8,128)(2,1)S(1)}, bf16[512,1024]{1,0:T(8,128)(2,1)S(1)}, u32[]{:S(2)}, u32[]{:S(2)}) collective-permute-start(bf16[512,1024]{1,0:T(8,128)(2,1)S(1)} %get-tuple-element.73.refs_0_.own_ref), channel_id=1, source_target_pairs={{0,4},{1,5},{2,6},{3,7},{4,8},{5,9},{6,10},{7,11},{8,12},{9,13},{1... | collective-permute-start | bytes 3145736 | tf_op jit(solution)/shard_map/ppermute | solution.py:27
  56.2 12.5 %collective-permute-start.20 = (bf16[128,1024]{1,0:T(8,128)(2,1)S(1)}, bf16[128,1024]{1,0:T(8,128)(2,1)S(1)}, u32[]{:S(2)}, u32[]{:S(2)}) collective-permute-start(bf16[128,1024]{1,0:T(8,128)(2,1)S(1)} %get-tuple-element.82), channel_id=1, source_target_pairs={{0,1},{1,0},{2,3},{3,2},{4,5},{5,4},{6,7},{7,6},{8,9},{9,8},{10,11... | collective-permute-start | bytes 786440 | tf_op jit(solution)/shard_map/ppermute | solution.py:32
  68.6 1.6 %collective-permute-start.19 = (bf16[128,1024]{1,0:T(8,128)(2,1)S(1)}, bf16[128,1024]{1,0:T(8,128)(2,1)S(1)}, u32[]{:S(2)}, u32[]{:S(2)}) collective-permute-start(bf16[128,1024]{1,0:T(8,128)(2,1)S(1)} %slice.10), channel_id=1, source_target_pairs={{0,1},{1,0},{2,3},{3,2},{4,5},{5,4},{6,7},{7,6},{8,9},{9,8},{10,11... | collective-permute-start | bytes 786440 | tf_op jit(solution)/shard_map/ppermute | solution.py:32
  68.8 14.2 %collective-permute-start.15 = (bf16[128,1024]{1,0:T(8,128)(2,1)S(1)}, bf16[128,1024]{1,0:T(8,128)(2,1)S(1)}, u32[]{:S(2)}, u32[]{:S(2)}) collective-permute-start(bf16[128,1024]{1,0:T(8,128)(2,1)S(1)} %get-tuple-element.76), channel_id=1, source_target_pairs={{4,0},{5,1},{6,2},{7,3},{8,4},{9,5},{10,6},{11,7},{12,8},{13,9},{1... | collective-permute-start | bytes 786440 | tf_op jit(solution)/shard_map/ppermute | solution.py:27
  75.7 8.5 %collective-permute-start.22 = (bf16[128,1024]{1,0:T(8,128)(2,1)S(1)}, bf16[128,1024]{1,0:T(8,128)(2,1)S(1)}, u32[]{:S(2)}, u32[]{:S(2)}) collective-permute-start(bf16[128,1024]{1,0:T(8,128)(2,1)S(1)} %get-tuple-element.86), channel_id=1, source_target_pairs={{4,0},{5,1},{6,2},{7,3},{8,4},{9,5},{10,6},{11,7},{12,8},{13,9},{1... | collective-permute-start | bytes 786440 | tf_op jit(solution)/shard_map/ppermute | solution.py:27
  77.0 25.0 %collective-permute-start.26 = (bf16[512,1024]{1,0:T(8,128)(2,1)S(1)}, bf16[512,1024]{1,0:T(8,128)(2,1)S(1)}, u32[]{:S(2)}, u32[]{:S(2)}) collective-permute-start(bf16[512,1024]{1,0:T(8,128)(2,1)S(1)} %get-tuple-element.85.refs_0_.own_ref), channel_id=1, source_target_pairs={{0,4},{1,5},{2,6},{3,7},{4,8},{5,9},{6,10},{7,11},{8,12},{9,13},{1... | collective-permute-start | bytes 3145736 | tf_op jit(solution)/shard_map/ppermute | solution.py:27
  81.1 4.7 %collective-permute-start.27 = (bf16[128,1024]{1,0:T(8,128)(2,1)S(1)}, bf16[128,1024]{1,0:T(8,128)(2,1)S(1)}, u32[]{:S(2)}, u32[]{:S(2)}) collective-permute-start(bf16[128,1024]{1,0:T(8,128)(2,1)S(1)} %slice.11), channel_id=1, source_target_pairs={{0,1},{1,0},{2,3},{3,2},{4,5},{5,4},{6,7},{7,6},{8,9},{9,8},{10,11... | collective-permute-start | bytes 786440 | tf_op jit(solution)/shard_map/ppermute | solution.py:32
  86.7 31.2 %collective-permute-start.31 = (bf16[128,8,512]{2,1,0:T(8,128)(2,1)S(1)}, bf16[128,8,512]{2,1,0:T(8,128)(2,1)S(1)}, u32[]{:S(2)}, u32[]{:S(2)}) collective-permute-start(bf16[128,8,512]{2,1,0:T(8,128)(2,1)S(1)} %shard_map.80.refs_1_.own_ref), channel_id=1, source_target_pairs={{7,3},{11,7},{15,11},{23,19},{27,23},{31,27}} | collective-permute-start | bytes 3145736 | tf_op jit(solution)/shard_map/ppermute | solution.py:27
  87.5 18.5 %collective-permute-start.23 = (bf16[256,1024]{1,0:T(8,128)(2,1)S(1)}, bf16[256,1024]{1,0:T(8,128)(2,1)S(1)}, u32[]{:S(2)}, u32[]{:S(2)}) collective-permute-start(bf16[256,1024]{1,0:T(8,128)(2,1)S(1)} %get-tuple-element.89), channel_id=1, source_target_pairs={{0,1},{1,0},{2,3},{3,2},{4,5},{5,4},{6,7},{7,6},{8,9},{9,8},{10,11... | collective-permute-start | bytes 1572872 | tf_op jit(solution)/shard_map/ppermute | solution.py:32
  89.6 17.9 %collective-permute-start.24 = (bf16[256,1024]{1,0:T(8,128)(2,1)S(1)}, bf16[256,1024]{1,0:T(8,128)(2,1)S(1)}, u32[]{:S(2)}, u32[]{:S(2)}) collective-permute-start(bf16[256,1024]{1,0:T(8,128)(2,1)S(1)} %get-tuple-element.90), channel_id=1, source_target_pairs={{0,2},{1,3},{2,0},{3,1},{4,6},{5,7},{6,4},{7,5},{8,10},{9,11},{10,... | collective-permute-start | bytes 1572872 | tf_op jit(solution)/shard_map/ppermute | solution.py:32
  91.1 23.8 %collective-permute-start.25 = (bf16[256,1024]{1,0:T(8,128)(2,1)S(1)}, bf16[256,1024]{1,0:T(8,128)(2,1)S(1)}, u32[]{:S(2)}, u32[]{:S(2)}) collective-permute-start(bf16[256,1024]{1,0:T(8,128)(2,1)S(1)} %get-tuple-element.91), channel_id=1, source_target_pairs={{0,3},{1,2},{2,1},{3,0},{4,7},{5,6},{6,5},{7,4},{8,11},{9,10},{10,... | collective-permute-start | bytes 1572872 | tf_op jit(solution)/shard_map/ppermute | solution.py:32
  103.5 17.0 %collective-permute-start.28 = (bf16[128,1024]{1,0:T(8,128)(2,1)S(1)}, bf16[128,1024]{1,0:T(8,128)(2,1)S(1)}, u32[]{:S(2)}, u32[]{:S(2)}) collective-permute-start(bf16[128,1024]{1,0:T(8,128)(2,1)S(1)} %get-tuple-element.95), channel_id=1, source_target_pairs={{0,1},{1,0},{2,3},{3,2},{4,5},{5,4},{6,7},{7,6},{8,9},{9,8},{10,11... | collective-permute-start | bytes 786440 | tf_op jit(solution)/shard_map/ppermute | solution.py:32
  106.0 14.5 %collective-permute-start.29 = (bf16[128,1024]{1,0:T(8,128)(2,1)S(1)}, bf16[128,1024]{1,0:T(8,128)(2,1)S(1)}, u32[]{:S(2)}, u32[]{:S(2)}) collective-permute-start(bf16[128,1024]{1,0:T(8,128)(2,1)S(1)} %get-tuple-element.96), channel_id=1, source_target_pairs={{0,2},{1,3},{2,0},{3,1},{4,6},{5,7},{6,4},{7,5},{8,10},{9,11},{10,... | collective-permute-start | bytes 786440 | tf_op jit(solution)/shard_map/ppermute | solution.py:32
  107.5 18.3 %collective-permute-start.30 = (bf16[128,1024]{1,0:T(8,128)(2,1)S(1)}, bf16[128,1024]{1,0:T(8,128)(2,1)S(1)}, u32[]{:S(2)}, u32[]{:S(2)}) collective-permute-start(bf16[128,1024]{1,0:T(8,128)(2,1)S(1)} %get-tuple-element.97), channel_id=1, source_target_pairs={{0,3},{1,2},{2,1},{3,0},{4,7},{5,6},{6,5},{7,4},{8,11},{9,10},{10,... | collective-permute-start | bytes 786440 | tf_op jit(solution)/shard_map/ppermute | solution.py:32

commit v21 on v20

--- a/solution.py
+++ b/solution.py
@@ -148,7 +148,7 @@
 
 def pack(here, pieces, more, *tokens):
     side, cols = pieces[0][0].shape
-    tile = 512
+    tile = cols
     shapes = [(G * side + more, cols), (side + more, cols)]
     specs = [across(array.shape, tile) for array in arrays_of(pieces)] if more else piece_specs(pieces, side, tile)
     return call(

time: 130 us -> 130 us (level)
  no operation moved by 1% of the time
where the time goes in v21:
time: 130 us; the launch traced here: 129 us
  starting transfers between devices  46.6 us (36%)
  Pallas kernels  40 us (31%)
  waiting for transfers between devices  38.6 us (30%)
  local copies, waits for them, and re-layouts  2.57 us (2%)
    ppermute x21, starting transfers between devices, swapped(): return lax.ppermute(value, 'slab', [(i, i ^ bits) for i in range(count)])  25.4 us
    ppermute x21, waiting for transfers between devices, swapped(): return lax.ppermute(value, 'slab', [(i, i ^ bits) for i in range(count)])  23.5 us
    ppermute x11, starting transfers between devices, moved(): return lax.ppermute(value, 'slab', pairs)  21.2 us
    ppermute x11, waiting for transfers between devices, moved(): return lax.ppermute(value, 'slab', pairs)  15.1 us
    pallas_call x1, Pallas kernels, half_tv(): call(tv_kernel, 0, grid=(depth // deep,), in_specs=[SMEM] + edges + [afte...  9.99 us
    pallas_call x2, Pallas kernels, cast_rows(): call(functools.partial(cast_kernel, groups, len(edges), halves), 2, grid=...  5.97 us
    pallas_call x2, Pallas kernels, finish(): call(finish_kernel, 0, grid=(count,), in_specs=[SMEM, part] + piece_specs...  5.85 us
    pallas_call x2, Pallas kernels, split_rows(): call(functools.partial(split_kernel, groups, len(passing)), 2, grid=(coun...  3.53 us
  transfers between devices with their start and end apart: 32, of which 8 were waited for; matrix products, arithmetic and copies ran while one was open for 1% of the time, Pallas kernels for 27%

profile of v21, /device:TPU:1, one launch (start us, length us, event | category | flops | bytes accessed | tf_op | source)
XLA Modules:
  0.0 128.7 jit_solution(1587278911678519294)
XLA Ops:
  0.6 2.5 %shard_map.68 = (bf16[128,1024]{1,0:T(8,128)(2,1)}, bf16[144,1024]{1,0:T(8,128)(2,1)S(1)}, bf16[128,1024]{1,0:T(8,128)(2,1)}, bf16[144,1024]{1,0:T(8,128)(2,1)S(1)}) custom-call(s32[1]{0:T(128)} %bitcast.here_ref, f32[1024,1024]{1,0:T(8,128)} %bitcast.2, f32[1024,1024]{1,0:T(8,128)} %bitcast.3, f32[1024,1024]{1,0:T(8,128)} %bitcast.4, f32[1024,1024]{1,0:T(8,128)} %bitcast.5), custom_call_target="tpu_custom_call" | custom-call | flops 2300000000 | bytes 1000 | tf_op jit(solution)/shard_map/pallas_call | solution.py:115
  3.2 2.7 %collective-permute-start.1 = (bf16[128,1024]{1,0:T(8,128)(2,1)}, bf16[128,1024]{1,0:T(8,128)(2,1)}, u32[]{:S(2)}, u32[]{:S(2)}) collective-permute-start(bf16[128,1024]{1,0:T(8,128)(2,1)} %get-tuple-element.52), channel_id=1, source_target_pairs={{0,2},{1,3},{2,0},{3,1},{4,6},{5,7},{6,4},{7,5},{8,10},{9,11},{10,... | collective-permute-start | bytes 786440 | tf_op jit(solution)/shard_map/ppermute | solution.py:32
  6.0 3.4 %shard_map.69 = (bf16[128,1024]{1,0:T(8,128)(2,1)}, bf16[128,1024]{1,0:T(8,128)(2,1)S(1)}, bf16[256,1024]{1,0:T(8,128)(2,1)}, bf16[128,8,512]{2,1,0:T(8,128)(2,1)}, bf16[128,8,512]{2,1,0:T(8,128)(2,1)S(1)}) custom-call(s32[1]{0:T(128)} %bitcast.here_ref, f32[1024,1024]{1,0:T(8,128)} %bitcast.6, f32[1024,1024]{1,0:T(8,128)} %bitcast.7, ...), custom_call_target="tpu_custom_call" | custom-call | flops 2300000000 | bytes 1000 | tf_op jit(solution)/shard_map/pallas_call | solution.py:115
  10.1 0.7 collective-permute-start.4
  10.8 4.2 %collective-permute-start.5 = (bf16[256,1024]{1,0:T(8,128)(2,1)}, bf16[256,1024]{1,0:T(8,128)(2,1)}, u32[]{:S(2)}, u32[]{:S(2)}) collective-permute-start(bf16[256,1024]{1,0:T(8,128)(2,1)} %get-tuple-element.59), channel_id=1, source_target_pairs={{0,2},{1,3},{2,0},{3,1},{4,6},{5,7},{6,4},{7,5},{8,10},{9,11},{10,... | collective-permute-start | bytes 1572872 | tf_op jit(solution)/shard_map/ppermute | solution.py:32
  15.1 0.8 copy.13.offset_ref
  15.9 0.9 copy-done.4
  16.8 1.6 %shard_map.70 = (bf16[512,1152]{1,0:T(8,128)(2,1)S(1)}, bf16[512,1152]{1,0:T(8,128)(2,1)S(1)}) custom-call(s32[1]{0:T(128)} %bitcast.here_ref, s32[16,6]{1,0:T(8,128)S(1)} %copy.12.cover_ref, s32[16,6]{1,0:T(8,128)S(1)} %copy.13.offset_ref, bf16[8,128,128]{2,1,0:T(8,128)(2,1)S(1)} %copy-done, bf16[128,1024]{1,0:T(8,128)(2,1)S(1)} %copy-done.4), custom_call_target="tpu_custom_call" | custom-call | flops 10350000128 | bytes 1000 | tf_op jit(solution)/shard_map/pallas_call | solution.py:415
  18.5 0.7 collective-permute-start.10
  19.3 1.1 shard_map.71
  20.7 1.3 collective-permute-start.3
  22.0 8.4 %collective-permute-done.5.refs_0_.refs_2_ = bf16[256,1024]{1,0:T(8,128)(2,1)} collective-permute-done((bf16[256,1024]{1,0:T(8,128)(2,1)}, bf16[256,1024]{1,0:T(8,128)(2,1)}, u32[]{:S(2)}, u32[]{:S(2)}) %collective-permute-start.5) | collective-permute-done | bytes 524320 | tf_op jit(solution)/shard_map/ppermute | solution.py:32
  30.4 1.8 %shard_map.72 = (bf16[128,1024]{1,0:T(8,128)(2,1)S(1)}, bf16[128,1024]{1,0:T(8,128)(2,1)S(1)}, bf16[256,1024]{1,0:T(8,128)(2,1)S(1)}, bf16[128,1024]{1,0:T(8,128)(2,1)S(1)}) custom-call(s32[1]{0:T(128)} %bitcast.here_ref, bf16[128,8,1024]{2,1,0:T(8,128)(2,1)} %refs_2_.3, bf16[128,8,512]{2,1,0:T(8,128)(2,1)S(1)} %collective-permute-done.4.got_ref, ...), custom_call_target="tpu_custom_call" | custom-call | flops 2300000000 | bytes 1000 | tf_op jit(solution)/shard_map/pallas_call | solution.py:196
  33.0 1.5 %collective-permute-start.9 = (bf16[256,1024]{1,0:T(8,128)(2,1)S(1)}, bf16[256,1024]{1,0:T(8,128)(2,1)S(1)}, u32[]{:S(2)}, u32[]{:S(2)}) collective-permute-start(bf16[256,1024]{1,0:T(8,128)(2,1)S(1)} %get-tuple-element.64), channel_id=1, source_target_pairs={{0,2},{1,3},{2,0},{3,1},{4,6},{5,7},{6,4},{7,5},{8,10},{9,11},{10,... | collective-permute-start | bytes 1572872 | tf_op jit(solution)/shard_map/ppermute | solution.py:32
  34.5 3.2 %collective-permute-start.8 = (bf16[144,1024]{1,0:T(8,128)(2,1)S(1)}, bf16[144,1024]{1,0:T(8,128)(2,1)S(1)}, u32[]{:S(2)}, u32[]{:S(2)}) collective-permute-start(bf16[144,1024]{1,0:T(8,128)(2,1)S(1)} %get-tuple-element.62), channel_id=1, source_target_pairs={{0,4},{1,5},{2,6},{3,7},{4,8},{5,9},{6,10},{7,11},{8,12},{9,13},{1... | collective-permute-start | bytes 884744 | tf_op jit(solution)/shard_map/ppermute | solution.py:27
  37.7 1.1 shard_map.73
  38.8 3.2 %collective-permute-start.13 = (bf16[128,1024]{1,0:T(8,128)(2,1)S(1)}, bf16[128,1024]{1,0:T(8,128)(2,1)S(1)}, u32[]{:S(2)}, u32[]{:S(2)}) collective-permute-start(bf16[128,1024]{1,0:T(8,128)(2,1)S(1)} %get-tuple-element.72), channel_id=1, source_target_pairs={{0,4},{1,5},{2,6},{3,7},{4,8},{5,9},{6,10},{7,11},{8,12},{9,13},{1... | collective-permute-start | bytes 786440 | tf_op jit(solution)/shard_map/ppermute | solution.py:27
  42.0 1.7 %shard_map.74 = (bf16[128,1024]{1,0:T(8,128)(2,1)S(1)}, bf16[128,1024]{1,0:T(8,128)(2,1)S(1)}, bf16[256,1024]{1,0:T(8,128)(2,1)S(1)}) custom-call(s32[1]{0:T(128)} %bitcast.here_ref, bf16[128,8,1024]{2,1,0:T(8,128)(2,1)} %refs_2_.3, bf16[128,8,512]{2,1,0:T(8,128)(2,1)S(1)} %collective-permute-done.10.got_ref, ...), custom_call_target="tpu_custom_call" | custom-call | flops 2300000000 | bytes 1000 | tf_op jit(solution)/shard_map/pallas_call | solution.py:196
  43.7 2.3 %collective-permute-done.9.refs_2_ = bf16[256,1024]{1,0:T(8,128)(2,1)S(1)} collective-permute-done((bf16[256,1024]{1,0:T(8,128)(2,1)S(1)}, bf16[256,1024]{1,0:T(8,128)(2,1)S(1)}, u32[]{:S(2)}, u32[]{:S(2)}) %collective-permute-start.9) | collective-permute-done | bytes 524320 | tf_op jit(solution)/shard_map/ppermute | solution.py:32
  46.1 1.3 %collective-permute-start.12 = (bf16[128,1024]{1,0:T(8,128)(2,1)S(1)}, bf16[128,1024]{1,0:T(8,128)(2,1)S(1)}, u32[]{:S(2)}, u32[]{:S(2)}) collective-permute-start(bf16[128,1024]{1,0:T(8,128)(2,1)S(1)} %slice.9), channel_id=1, source_target_pairs={{0,1},{1,0},{2,3},{3,2},{4,5},{5,4},{6,7},{7,6},{8,9},{9,8},{10,11... | collective-permute-start | bytes 786440 | tf_op jit(solution)/shard_map/ppermute | solution.py:32
  47.4 1.3 collective-permute-start.16
  48.9 2.2 %collective-permute-start.18 = (bf16[256,1024]{1,0:T(8,128)(2,1)S(1)}, bf16[256,1024]{1,0:T(8,128)(2,1)S(1)}, u32[]{:S(2)}, u32[]{:S(2)}) collective-permute-start(bf16[256,1024]{1,0:T(8,128)(2,1)S(1)} %get-tuple-element.78), channel_id=1, source_target_pairs={{0,2},{1,3},{2,0},{3,1},{4,6},{5,7},{6,4},{7,5},{8,10},{9,11},{10,... | collective-permute-start | bytes 1572872 | tf_op jit(solution)/shard_map/ppermute | solution.py:32
  51.2 1.5 %shard_map.75 = (bf16[512,1024]{1,0:T(8,128)(2,1)S(1)}, bf16[128,1024]{1,0:T(8,128)(2,1)S(1)}, bf16[128,1024]{1,0:T(8,128)(2,1)S(1)}, bf16[256,1024]{1,0:T(8,128)(2,1)S(1)}) custom-call(s32[1]{0:T(128)} %bitcast.here_ref, bf16[512,1152]{1,0:T(8,128)(2,1)S(1)} %get-tuple-element.55.refs_4_.band_ref, bf16[528,1024]{1,0:T(8,128)(2,1)S(1)} %get-tuple-element.56.own_ref, ...), custom_call_target="tpu_custom_call" | custom-call | flops 3449999872 | bytes 1000 | tf_op jit(solution)/shard_map/pallas_call | solution.py:446
  52.8 3.4 %collective-permute-start.14 = (bf16[512,1024]{1,0:T(8,128)(2,1)S(1)}, bf16[512,1024]{1,0:T(8,128)(2,1)S(1)}, u32[]{:S(2)}, u32[]{:S(2)}) collective-permute-start(bf16[512,1024]{1,0:T(8,128)(2,1)S(1)} %get-tuple-element.73.refs_0_.own_ref), channel_id=1, source_target_pairs={{0,4},{1,5},{2,6},{3,7},{4,8},{5,9},{6,10},{7,11},{8,12},{9,13},{1... | collective-permute-start | bytes 3145736 | tf_op jit(solution)/shard_map/ppermute | solution.py:27
  56.2 2.4 %collective-permute-start.20 = (bf16[128,1024]{1,0:T(8,128)(2,1)S(1)}, bf16[128,1024]{1,0:T(8,128)(2,1)S(1)}, u32[]{:S(2)}, u32[]{:S(2)}) collective-permute-start(bf16[128,1024]{1,0:T(8,128)(2,1)S(1)} %get-tuple-element.82), channel_id=1, source_target_pairs={{0,1},{1,0},{2,3},{3,2},{4,5},{5,4},{6,7},{7,6},{8,9},{9,8},{10,11... | collective-permute-start | bytes 786440 | tf_op jit(solution)/shard_map/ppermute | solution.py:32
  58.6 10.0 %shard_map.76 = (f32[128,8,1024]{2,1,0:T(8,128)}, f32[8,128]{1,0:T(8,128)S(1)}) custom-call(s32[1]{0:T(128)} %bitcast.here_ref, bf16[144,1024]{1,0:T(8,128)(2,1)S(1)} %collective-permute-done.refs_1_.near_ref, bf16[528,1024]{1,0:T(8,128)(2,1)S(1)} %collective-permute-done.3.high_ref.next_level_ref, ...), custom_call_target="tpu_custom_call" | custom-call | bytes 1000 | tf_op jit(solution)/shard_map/pallas_call | solution.py:546
  68.8 1.3 collective-permute-start.15
  70.2 4.0 %collective-permute-done.16.high_ref = bf16[512,1024]{1,0:T(8,128)(2,1)S(1)} collective-permute-done((bf16[512,1024]{1,0:T(8,128)(2,1)S(1)}, bf16[512,1024]{1,0:T(8,128)(2,1)S(1)}, u32[]{:S(2)}, u32[]{:S(2)}) %collective-permute-start.16) | collective-permute-done | bytes 1048608 | tf_op jit(solution)/shard_map/ppermute | solution.py:27
  74.2 1.5 %shard_map.77 = (bf16[512,1024]{1,0:T(8,128)(2,1)S(1)}, bf16[128,1024]{1,0:T(8,128)(2,1)S(1)}) custom-call(s32[1]{0:T(128)} %bitcast.here_ref, bf16[512,1152]{1,0:T(8,128)(2,1)S(1)} %get-tuple-element.55.refs_4_.band_ref, bf16[512,1024]{1,0:T(8,128)(2,1)S(1)} %get-tuple-element.69.refs_0_.own_ref, bf16[512,1024]{1,0:T(8,128)(2,1)S(1)} %collective-permute-done.16.high_ref, ...), custom_call_target="tpu_custom_call" | custom-call | flops 3449999872 | bytes 1000 | tf_op jit(solution)/shard_map/pallas_call | solution.py:446
  75.7 1.3 %collective-permute-start.22 = (bf16[128,1024]{1,0:T(8,128)(2,1)S(1)}, bf16[128,1024]{1,0:T(8,128)(2,1)S(1)}, u32[]{:S(2)}, u32[]{:S(2)}) collective-permute-start(bf16[128,1024]{1,0:T(8,128)(2,1)S(1)} %get-tuple-element.86), channel_id=1, source_target_pairs={{4,0},{5,1},{6,2},{7,3},{8,4},{9,5},{10,6},{11,7},{12,8},{13,9},{1... | collective-permute-start | bytes 786440 | tf_op jit(solution)/shard_map/ppermute | solution.py:27
  77.0 4.1 %collective-permute-start.26 = (bf16[512,1024]{1,0:T(8,128)(2,1)S(1)}, bf16[512,1024]{1,0:T(8,128)(2,1)S(1)}, u32[]{:S(2)}, u32[]{:S(2)}) collective-permute-start(bf16[512,1024]{1,0:T(8,128)(2,1)S(1)} %get-tuple-element.85.refs_0_.own_ref), channel_id=1, source_target_pairs={{0,4},{1,5},{2,6},{3,7},{4,8},{5,9},{6,10},{7,11},{8,12},{9,13},{1... | collective-permute-start | bytes 3145736 | tf_op jit(solution)/shard_map/ppermute | solution.py:27
  81.1 1.7 %collective-permute-start.27 = (bf16[128,1024]{1,0:T(8,128)(2,1)S(1)}, bf16[128,1024]{1,0:T(8,128)(2,1)S(1)}, u32[]{:S(2)}, u32[]{:S(2)}) collective-permute-start(bf16[128,1024]{1,0:T(8,128)(2,1)S(1)} %slice.11), channel_id=1, source_target_pairs={{0,1},{1,0},{2,3},{3,2},{4,5},{5,4},{6,7},{7,6},{8,9},{9,8},{10,11... | collective-permute-start | bytes 786440 | tf_op jit(solution)/shard_map/ppermute | solution.py:32
  82.8 1.5 %collective-permute-done.22.refs_1_.high_ref = bf16[128,1024]{1,0:T(8,128)(2,1)S(1)} collective-permute-done((bf16[128,1024]{1,0:T(8,128)(2,1)S(1)}, bf16[128,1024]{1,0:T(8,128)(2,1)S(1)}, u32[]{:S(2)}, u32[]{:S(2)}) %collective-permute-start.22) | collective-permute-done | bytes 262176 | tf_op jit(solution)/shard_map/ppermute | solution.py:27
  84.4 1.6 %shard_map.78 = (bf16[256,1024]{1,0:T(8,128)(2,1)S(1)}, bf16[256,1024]{1,0:T(8,128)(2,1)S(1)}, bf16[256,1024]{1,0:T(8,128)(2,1)S(1)}, bf16[256,1024]{1,0:T(8,128)(2,1)S(1)}) custom-call(s32[1]{0:T(128)} %bitcast.here_ref, bf16[512,1152]{1,0:T(8,128)(2,1)S(1)} %get-tuple-element.75.band_ref, bf16[512,1024]{1,0:T(8,128)(2,1)S(1)} %get-tuple-element.73.refs_0_.own_ref, ...), custom_call_target="tpu_custom_call" | custom-call | bytes 1000 | tf_op jit(solution)/shard_map/pallas_call | solution.py:478
  85.9 0.9 shard_map.80.refs_1_.own_ref
  86.8 0.7 collective-permute-start.31
  87.5 2.1 %collective-permute-start.23 = (bf16[256,1024]{1,0:T(8,128)(2,1)S(1)}, bf16[256,1024]{1,0:T(8,128)(2,1)S(1)}, u32[]{:S(2)}, u32[]{:S(2)}) collective-permute-start(bf16[256,1024]{1,0:T(8,128)(2,1)S(1)} %get-tuple-element.89), channel_id=1, source_target_pairs={{0,1},{1,0},{2,3},{3,2},{4,5},{5,4},{6,7},{7,6},{8,9},{9,8},{10,11... | collective-permute-start | bytes 1572872 | tf_op jit(solution)/shard_map/ppermute | solution.py:32
  89.6 1.3 %collective-permute-start.24 = (bf16[256,1024]{1,0:T(8,128)(2,1)S(1)}, bf16[256,1024]{1,0:T(8,128)(2,1)S(1)}, u32[]{:S(2)}, u32[]{:S(2)}) collective-permute-start(bf16[256,1024]{1,0:T(8,128)(2,1)S(1)} %get-tuple-element.90), channel_id=1, source_target_pairs={{0,2},{1,3},{2,0},{3,1},{4,6},{5,7},{6,4},{7,5},{8,10},{9,11},{10,... | collective-permute-start | bytes 1572872 | tf_op jit(solution)/shard_map/ppermute | solution.py:32
  91.3 1.2 shard_map.79
  92.5 9.6 %collective-permute-done.26.low_ref = bf16[512,1024]{1,0:T(8,128)(2,1)S(1)} collective-permute-done((bf16[512,1024]{1,0:T(8,128)(2,1)S(1)}, bf16[512,1024]{1,0:T(8,128)(2,1)S(1)}, u32[]{:S(2)}, u32[]{:S(2)}) %collective-permute-start.26) | collective-permute-done | bytes 1048608 | tf_op jit(solution)/shard_map/ppermute | solution.py:27
  102.1 1.5 %shard_map.81 = (bf16[128,1024]{1,0:T(8,128)(2,1)S(1)}, bf16[128,1024]{1,0:T(8,128)(2,1)S(1)}, bf16[128,1024]{1,0:T(8,128)(2,1)S(1)}, bf16[128,1024]{1,0:T(8,128)(2,1)S(1)}) custom-call(s32[1]{0:T(128)} %bitcast.here_ref, bf16[512,1152]{1,0:T(8,128)(2,1)S(1)} %get-tuple-element.75.band_ref, bf16[512,1024]{1,0:T(8,128)(2,1)S(1)} %get-tuple-element.85.refs_0_.own_ref, ...), custom_call_target="tpu_custom_call" | custom-call | bytes 1000 | tf_op jit(solution)/shard_map/pallas_call | solution.py:478
  103.6 2.3 %collective-permute-start.28 = (bf16[128,1024]{1,0:T(8,128)(2,1)S(1)}, bf16[128,1024]{1,0:T(8,128)(2,1)S(1)}, u32[]{:S(2)}, u32[]{:S(2)}) collective-permute-start(bf16[128,1024]{1,0:T(8,128)(2,1)S(1)} %get-tuple-element.95), channel_id=1, source_target_pairs={{0,1},{1,0},{2,3},{3,2},{4,5},{5,4},{6,7},{7,6},{8,9},{9,8},{10,11... | collective-permute-start | bytes 786440 | tf_op jit(solution)/shard_map/ppermute | solution.py:32
  106.0 1.3 %collective-permute-start.29 = (bf16[128,1024]{1,0:T(8,128)(2,1)S(1)}, bf16[128,1024]{1,0:T(8,128)(2,1)S(1)}, u32[]{:S(2)}, u32[]{:S(2)}) collective-permute-start(bf16[128,1024]{1,0:T(8,128)(2,1)S(1)} %get-tuple-element.96), channel_id=1, source_target_pairs={{0,2},{1,3},{2,0},{3,1},{4,6},{5,7},{6,4},{7,5},{8,10},{9,11},{10,... | collective-permute-start | bytes 786440 | tf_op jit(solution)/shard_map/ppermute | solution.py:32
  107.7 7.2 %collective-permute-done.25.refs_3_ = bf16[256,1024]{1,0:T(8,128)(2,1)S(1)} collective-permute-done((bf16[256,1024]{1,0:T(8,128)(2,1)S(1)}, bf16[256,1024]{1,0:T(8,128)(2,1)S(1)}, u32[]{:S(2)}, u32[]{:S(2)}) %collective-permute-start.25) | collective-permute-done | bytes 524320 | tf_op jit(solution)/shard_map/ppermute | solution.py:32
  115.0 2.9 %shard_map.82.tv_ref = f32[128,8,1024]{2,1,0:T(8,128)} custom-call(s32[1]{0:T(128)} %bitcast.here_ref, f32[128,8,1024]{2,1,0:T(8,128)} %get-tuple-element.88.tv_ref, bf16[256,1024]{1,0:T(8,128)(2,1)S(1)} %get-tuple-element.87.refs_4_.refs_0_, bf16[256,1024]{1,0:T(8,128)(2,1)S(1)} %collective-permute-done.23.refs_1_, ...), custom_call_target="tpu_custom_call", output_to_operand_aliasing={{}: (1, {})} | custom-call | bytes 1000 | tf_op jit(solution)/shard_map/pallas_call | solution.py:367
  117.9 2.6 %shard_map.83.refs_4_ = bf16[128,8,1024]{2,1,0:T(8,128)(2,1)} custom-call(s32[1]{0:T(128)} %bitcast.here_ref, bf16[128,8,512]{2,1,0:T(8,128)(2,1)S(1)} %shard_map.80.refs_1_.own_ref, bf16[128,8,512]{2,1,0:T(8,128)(2,1)S(1)} %collective-permute-done.31.above_ref, bf16[256,1024]{1,0:T(8,128)(2,1)S(1)} %get-tuple-element.87.refs_4_.refs_0_, ...), custom_call_target="tpu_custom_call" | custom-call | bytes 1000 | tf_op jit(solution)/shard_map/pallas_call | solution.py:345
  120.5 5.2 %collective-permute-done.30.refs_3_ = bf16[128,1024]{1,0:T(8,128)(2,1)S(1)} collective-permute-done((bf16[128,1024]{1,0:T(8,128)(2,1)S(1)}, bf16[128,1024]{1,0:T(8,128)(2,1)S(1)}, u32[]{:S(2)}, u32[]{:S(2)}) %collective-permute-start.30) | collective-permute-done | bytes 262176 | tf_op jit(solution)/shard_map/ppermute | solution.py:32
  125.7 2.9 %shard_map.84 = f32[128,8,1024]{2,1,0:T(8,128)} custom-call(s32[1]{0:T(128)} %bitcast.here_ref, f32[128,8,1024]{2,1,0:T(8,128)} %shard_map.82.tv_ref, bf16[128,1024]{1,0:T(8,128)(2,1)S(1)} %get-tuple-element.94.refs_4_.refs_0_, bf16[128,1024]{1,0:T(8,128)(2,1)S(1)} %collective-permute-done.28.refs_1_, ...), custom_call_target="tpu_custom_call", output_to_operand_aliasing={{}: (1, {})} | custom-call | bytes 1000 | tf_op jit(solution)/shard_map/pallas_call | solution.py:367
  (52 shorter events, 3.5 us)
Async XLA Ops:
  3.2 16.1 %collective-permute-start = (bf16[144,1024]{1,0:T(8,128)(2,1)S(1)}, bf16[144,1024]{1,0:T(8,128)(2,1)S(1)}, u32[]{:S(2)}, u32[]{:S(2)}) collective-permute-start(bf16[144,1024]{1,0:T(8,128)(2,1)S(1)} %get-tuple-element.50.refs_4_), channel_id=1, source_target_pairs={{0,1},{1,0},{2,3},{3,2},{4,5},{5,4},{6,7},{7,6},{8,9},{9,8},{10,11... | collective-permute-start | bytes 884744 | tf_op jit(solution)/shard_map/ppermute | solution.py:32
  3.2 15.3 %collective-permute-start.1 = (bf16[128,1024]{1,0:T(8,128)(2,1)}, bf16[128,1024]{1,0:T(8,128)(2,1)}, u32[]{:S(2)}, u32[]{:S(2)}) collective-permute-start(bf16[128,1024]{1,0:T(8,128)(2,1)} %get-tuple-element.52), channel_id=1, source_target_pairs={{0,2},{1,3},{2,0},{3,1},{4,6},{5,7},{6,4},{7,5},{8,10},{9,11},{10,... | collective-permute-start | bytes 786440 | tf_op jit(solution)/shard_map/ppermute | solution.py:32
  5.9 9.1 %copy-start.6 = (s32[16,6]{0,1:T(8,128)S(1)}, s32[16,6]{0,1:T(8,128)}, u32[]{:S(2)}) copy-start(s32[16,6]{0,1:T(8,128)} %param.8) | copy-start | bytes 1156
  5.9 10.0 %copy-start = (bf16[8,128,128]{2,1,0:T(8,128)(2,1)S(1)}, bf16[8,128,128]{2,1,0:T(8,128)(2,1)}, u32[]{:S(2)}) copy-start(bf16[8,128,128]{2,1,0:T(8,128)(2,1)} %refs_0_.1) | copy-start | bytes 786436
  5.9 13.3 %collective-permute-start.2 = (bf16[144,1024]{1,0:T(8,128)(2,1)S(1)}, bf16[144,1024]{1,0:T(8,128)(2,1)S(1)}, u32[]{:S(2)}, u32[]{:S(2)}) collective-permute-start(bf16[144,1024]{1,0:T(8,128)(2,1)S(1)} %get-tuple-element.53), channel_id=1, source_target_pairs={{0,3},{1,2},{2,1},{3,0},{4,7},{5,6},{6,5},{7,4},{8,11},{9,10},{10,... | collective-permute-start | bytes 884744 | tf_op jit(solution)/shard_map/ppermute | solution.py:32
  9.4 0.7 copy-start.3
  10.1 20.3 %collective-permute-start.4 = (bf16[128,8,512]{2,1,0:T(8,128)(2,1)}, bf16[128,8,512]{2,1,0:T(8,128)(2,1)S(1)}, u32[]{:S(2)}, u32[]{:S(2)}) collective-permute-start(bf16[128,8,512]{2,1,0:T(8,128)(2,1)} %get-tuple-element.58), channel_id=1, source_target_pairs={{3,7},{7,11},{11,15},{19,23},{23,27},{27,31}} | collective-permute-start | bytes 3145736 | tf_op jit(solution)/shard_map/ppermute | solution.py:27
  10.8 19.6 %collective-permute-start.5 = (bf16[256,1024]{1,0:T(8,128)(2,1)}, bf16[256,1024]{1,0:T(8,128)(2,1)}, u32[]{:S(2)}, u32[]{:S(2)}) collective-permute-start(bf16[256,1024]{1,0:T(8,128)(2,1)} %get-tuple-element.59), channel_id=1, source_target_pairs={{0,2},{1,3},{2,0},{3,1},{4,6},{5,7},{6,4},{7,5},{8,10},{9,11},{10,... | collective-permute-start | bytes 1572872 | tf_op jit(solution)/shard_map/ppermute | solution.py:32
  15.9 1.0 copy-start.4
  16.8 2.4 %copy-start.2 = (bf16[128,1024]{1,0:T(8,128)(2,1)S(1)}, bf16[128,1024]{1,0:T(8,128)(2,1)}, u32[]{:S(2)}) copy-start(bf16[128,1024]{1,0:T(8,128)(2,1)} %get-tuple-element.51.refs_0_) | copy-start | bytes 786436
  18.5 23.5 %collective-permute-start.10 = (bf16[128,8,512]{2,1,0:T(8,128)(2,1)S(1)}, bf16[128,8,512]{2,1,0:T(8,128)(2,1)S(1)}, u32[]{:S(2)}, u32[]{:S(2)}) collective-permute-start(bf16[128,8,512]{2,1,0:T(8,128)(2,1)S(1)} %get-tuple-element.66), channel_id=1, source_target_pairs={{3,7},{7,11},{11,15},{19,23},{23,27},{27,31}} | collective-permute-start | bytes 3145736 | tf_op jit(solution)/shard_map/ppermute | solution.py:27
  19.3 1.1 copy-start.5
  20.4 17.3 %copy-start.1 = (bf16[128,1024]{1,0:T(8,128)(2,1)S(1)}, bf16[128,1024]{1,0:T(8,128)(2,1)}, u32[]{:S(2)}) copy-start(bf16[128,1024]{1,0:T(8,128)(2,1)} %get-tuple-element.67.refs_0_) | copy-start | bytes 786436
  20.4 10.0 %collective-permute-start.6 = (bf16[128,1024]{1,0:T(8,128)(2,1)S(1)}, bf16[128,1024]{1,0:T(8,128)(2,1)S(1)}, u32[]{:S(2)}, u32[]{:S(2)}) collective-permute-start(bf16[128,1024]{1,0:T(8,128)(2,1)S(1)} %copy-done.5), channel_id=1, source_target_pairs={{0,1},{1,0},{2,3},{3,2},{4,5},{5,4},{6,7},{7,6},{8,9},{9,8},{10,11... | collective-permute-start | bytes 786440 | tf_op jit(solution)/shard_map/ppermute | solution.py:32
  20.7 28.0 %collective-permute-start.3 = (bf16[528,1024]{1,0:T(8,128)(2,1)S(1)}, bf16[528,1024]{1,0:T(8,128)(2,1)S(1)}, u32[]{:S(2)}, u32[]{:S(2)}) collective-permute-start(bf16[528,1024]{1,0:T(8,128)(2,1)S(1)} %get-tuple-element.56.own_ref), channel_id=1, source_target_pairs={{4,0},{5,1},{6,2},{7,3},{8,4},{9,5},{10,6},{11,7},{12,8},{13,9},{1... | collective-permute-start | bytes 3244040 | tf_op jit(solution)/shard_map/ppermute | solution.py:27
  32.2 2.3 %collective-permute-start.7 = (bf16[128,1024]{1,0:T(8,128)(2,1)S(1)}, bf16[128,1024]{1,0:T(8,128)(2,1)S(1)}, u32[]{:S(2)}, u32[]{:S(2)}) collective-permute-start(bf16[128,1024]{1,0:T(8,128)(2,1)S(1)} %get-tuple-element.61), channel_id=1, source_target_pairs={{0,1},{1,0},{2,3},{3,2},{4,5},{5,4},{6,7},{7,6},{8,9},{9,8},{10,11... | collective-permute-start | bytes 786440 | tf_op jit(solution)/shard_map/ppermute | solution.py:32
  32.9 4.8 %collective-permute-start.11 = (bf16[128,1024]{1,0:T(8,128)(2,1)S(1)}, bf16[128,1024]{1,0:T(8,128)(2,1)S(1)}, u32[]{:S(2)}, u32[]{:S(2)}) collective-permute-start(bf16[128,1024]{1,0:T(8,128)(2,1)S(1)} %get-tuple-element.68), channel_id=1, source_target_pairs={{0,1},{1,0},{2,3},{3,2},{4,5},{5,4},{6,7},{7,6},{8,9},{9,8},{10,11... | collective-permute-start | bytes 786440 | tf_op jit(solution)/shard_map/ppermute | solution.py:32
  33.0 13.1 %collective-permute-start.9 = (bf16[256,1024]{1,0:T(8,128)(2,1)S(1)}, bf16[256,1024]{1,0:T(8,128)(2,1)S(1)}, u32[]{:S(2)}, u32[]{:S(2)}) collective-permute-start(bf16[256,1024]{1,0:T(8,128)(2,1)S(1)} %get-tuple-element.64), channel_id=1, source_target_pairs={{0,2},{1,3},{2,0},{3,1},{4,6},{5,7},{6,4},{7,5},{8,10},{9,11},{10,... | collective-permute-start | bytes 1572872 | tf_op jit(solution)/shard_map/ppermute | solution.py:32
  34.5 16.7 %collective-permute-start.8 = (bf16[144,1024]{1,0:T(8,128)(2,1)S(1)}, bf16[144,1024]{1,0:T(8,128)(2,1)S(1)}, u32[]{:S(2)}, u32[]{:S(2)}) collective-permute-start(bf16[144,1024]{1,0:T(8,128)(2,1)S(1)} %get-tuple-element.62), channel_id=1, source_target_pairs={{0,4},{1,5},{2,6},{3,7},{4,8},{5,9},{6,10},{7,11},{8,12},{9,13},{1... | collective-permute-start | bytes 884744 | tf_op jit(solution)/shard_map/ppermute | solution.py:27
  38.8 10.2 %collective-permute-start.13 = (bf16[128,1024]{1,0:T(8,128)(2,1)S(1)}, bf16[128,1024]{1,0:T(8,128)(2,1)S(1)}, u32[]{:S(2)}, u32[]{:S(2)}) collective-permute-start(bf16[128,1024]{1,0:T(8,128)(2,1)S(1)} %get-tuple-element.72), channel_id=1, source_target_pairs={{0,4},{1,5},{2,6},{3,7},{4,8},{5,9},{6,10},{7,11},{8,12},{9,13},{1... | collective-permute-start | bytes 786440 | tf_op jit(solution)/shard_map/ppermute | solution.py:27
  46.1 5.1 %collective-permute-start.12 = (bf16[128,1024]{1,0:T(8,128)(2,1)S(1)}, bf16[128,1024]{1,0:T(8,128)(2,1)S(1)}, u32[]{:S(2)}, u32[]{:S(2)}) collective-permute-start(bf16[128,1024]{1,0:T(8,128)(2,1)S(1)} %slice.9), channel_id=1, source_target_pairs={{0,1},{1,0},{2,3},{3,2},{4,5},{5,4},{6,7},{7,6},{8,9},{9,8},{10,11... | collective-permute-start | bytes 786440 | tf_op jit(solution)/shard_map/ppermute | solution.py:32
  47.4 26.8 %collective-permute-start.16 = (bf16[512,1024]{1,0:T(8,128)(2,1)S(1)}, bf16[512,1024]{1,0:T(8,128)(2,1)S(1)}, u32[]{:S(2)}, u32[]{:S(2)}) collective-permute-start(bf16[512,1024]{1,0:T(8,128)(2,1)S(1)} %get-tuple-element.69.refs_0_.own_ref), channel_id=1, source_target_pairs={{4,0},{5,1},{6,2},{7,3},{8,4},{9,5},{10,6},{11,7},{12,8},{13,9},{1... | collective-permute-start | bytes 3145736 | tf_op jit(solution)/shard_map/ppermute | solution.py:27
  48.7 4.0 %collective-permute-start.17 = (bf16[128,1024]{1,0:T(8,128)(2,1)S(1)}, bf16[128,1024]{1,0:T(8,128)(2,1)S(1)}, u32[]{:S(2)}, u32[]{:S(2)}) collective-permute-start(bf16[128,1024]{1,0:T(8,128)(2,1)S(1)} %get-tuple-element.77), channel_id=1, source_target_pairs={{0,1},{1,0},{2,3},{3,2},{4,5},{5,4},{6,7},{7,6},{8,9},{9,8},{10,11... | collective-permute-start | bytes 786440 | tf_op jit(solution)/shard_map/ppermute | solution.py:32
  48.9 19.7 %collective-permute-start.18 = (bf16[256,1024]{1,0:T(8,128)(2,1)S(1)}, bf16[256,1024]{1,0:T(8,128)(2,1)S(1)}, u32[]{:S(2)}, u32[]{:S(2)}) collective-permute-start(bf16[256,1024]{1,0:T(8,128)(2,1)S(1)} %get-tuple-element.78), channel_id=1, source_target_pairs={{0,2},{1,3},{2,0},{3,1},{4,6},{5,7},{6,4},{7,5},{8,10},{9,11},{10,... | collective-permute-start | bytes 1572872 | tf_op jit(solution)/shard_map/ppermute | solution.py:32
  52.7 21.5 %collective-permute-start.21 = (bf16[256,1024]{1,0:T(8,128)(2,1)S(1)}, bf16[256,1024]{1,0:T(8,128)(2,1)S(1)}, u32[]{:S(2)}, u32[]{:S(2)}) collective-permute-start(bf16[256,1024]{1,0:T(8,128)(2,1)S(1)} %get-tuple-element.84), channel_id=1, source_target_pairs={{0,2},{1,3},{2,0},{3,1},{4,6},{5,7},{6,4},{7,5},{8,10},{9,11},{10,... | collective-permute-start | bytes 1572872 | tf_op jit(solution)/shard_map/ppermute | solution.py:32
  52.8 31.6 %collective-permute-start.14 = (bf16[512,1024]{1,0:T(8,128)(2,1)S(1)}, bf16[512,1024]{1,0:T(8,128)(2,1)S(1)}, u32[]{:S(2)}, u32[]{:S(2)}) collective-permute-start(bf16[512,1024]{1,0:T(8,128)(2,1)S(1)} %get-tuple-element.73.refs_0_.own_ref), channel_id=1, source_target_pairs={{0,4},{1,5},{2,6},{3,7},{4,8},{5,9},{6,10},{7,11},{8,12},{9,13},{1... | collective-permute-start | bytes 3145736 | tf_op jit(solution)/shard_map/ppermute | solution.py:27
  56.2 12.5 %collective-permute-start.20 = (bf16[128,1024]{1,0:T(8,128)(2,1)S(1)}, bf16[128,1024]{1,0:T(8,128)(2,1)S(1)}, u32[]{:S(2)}, u32[]{:S(2)}) collective-permute-start(bf16[128,1024]{1,0:T(8,128)(2,1)S(1)} %get-tuple-element.82), channel_id=1, source_target_pairs={{0,1},{1,0},{2,3},{3,2},{4,5},{5,4},{6,7},{7,6},{8,9},{9,8},{10,11... | collective-permute-start | bytes 786440 | tf_op jit(solution)/shard_map/ppermute | solution.py:32
  68.6 1.6 %collective-permute-start.19 = (bf16[128,1024]{1,0:T(8,128)(2,1)S(1)}, bf16[128,1024]{1,0:T(8,128)(2,1)S(1)}, u32[]{:S(2)}, u32[]{:S(2)}) collective-permute-start(bf16[128,1024]{1,0:T(8,128)(2,1)S(1)} %slice.10), channel_id=1, source_target_pairs={{0,1},{1,0},{2,3},{3,2},{4,5},{5,4},{6,7},{7,6},{8,9},{9,8},{10,11... | collective-permute-start | bytes 786440 | tf_op jit(solution)/shard_map/ppermute | solution.py:32
  68.8 14.1 %collective-permute-start.15 = (bf16[128,1024]{1,0:T(8,128)(2,1)S(1)}, bf16[128,1024]{1,0:T(8,128)(2,1)S(1)}, u32[]{:S(2)}, u32[]{:S(2)}) collective-permute-start(bf16[128,1024]{1,0:T(8,128)(2,1)S(1)} %get-tuple-element.76), channel_id=1, source_target_pairs={{4,0},{5,1},{6,2},{7,3},{8,4},{9,5},{10,6},{11,7},{12,8},{13,9},{1... | collective-permute-start | bytes 786440 | tf_op jit(solution)/shard_map/ppermute | solution.py:27
  75.7 8.6 %collective-permute-start.22 = (bf16[128,1024]{1,0:T(8,128)(2,1)S(1)}, bf16[128,1024]{1,0:T(8,128)(2,1)S(1)}, u32[]{:S(2)}, u32[]{:S(2)}) collective-permute-start(bf16[128,1024]{1,0:T(8,128)(2,1)S(1)} %get-tuple-element.86), channel_id=1, source_target_pairs={{4,0},{5,1},{6,2},{7,3},{8,4},{9,5},{10,6},{11,7},{12,8},{13,9},{1... | collective-permute-start | bytes 786440 | tf_op jit(solution)/shard_map/ppermute | solution.py:27
  77.0 25.1 %collective-permute-start.26 = (bf16[512,1024]{1,0:T(8,128)(2,1)S(1)}, bf16[512,1024]{1,0:T(8,128)(2,1)S(1)}, u32[]{:S(2)}, u32[]{:S(2)}) collective-permute-start(bf16[512,1024]{1,0:T(8,128)(2,1)S(1)} %get-tuple-element.85.refs_0_.own_ref), channel_id=1, source_target_pairs={{0,4},{1,5},{2,6},{3,7},{4,8},{5,9},{6,10},{7,11},{8,12},{9,13},{1... | collective-permute-start | bytes 3145736 | tf_op jit(solution)/shard_map/ppermute | solution.py:27
  81.1 4.8 %collective-permute-start.27 = (bf16[128,1024]{1,0:T(8,128)(2,1)S(1)}, bf16[128,1024]{1,0:T(8,128)(2,1)S(1)}, u32[]{:S(2)}, u32[]{:S(2)}) collective-permute-start(bf16[128,1024]{1,0:T(8,128)(2,1)S(1)} %slice.11), channel_id=1, source_target_pairs={{0,1},{1,0},{2,3},{3,2},{4,5},{5,4},{6,7},{7,6},{8,9},{9,8},{10,11... | collective-permute-start | bytes 786440 | tf_op jit(solution)/shard_map/ppermute | solution.py:32
  86.8 31.1 %collective-permute-start.31 = (bf16[128,8,512]{2,1,0:T(8,128)(2,1)S(1)}, bf16[128,8,512]{2,1,0:T(8,128)(2,1)S(1)}, u32[]{:S(2)}, u32[]{:S(2)}) collective-permute-start(bf16[128,8,512]{2,1,0:T(8,128)(2,1)S(1)} %shard_map.80.refs_1_.own_ref), channel_id=1, source_target_pairs={{7,3},{11,7},{15,11},{23,19},{27,23},{31,27}} | collective-permute-start | bytes 3145736 | tf_op jit(solution)/shard_map/ppermute | solution.py:27
  87.5 18.4 %collective-permute-start.23 = (bf16[256,1024]{1,0:T(8,128)(2,1)S(1)}, bf16[256,1024]{1,0:T(8,128)(2,1)S(1)}, u32[]{:S(2)}, u32[]{:S(2)}) collective-permute-start(bf16[256,1024]{1,0:T(8,128)(2,1)S(1)} %get-tuple-element.89), channel_id=1, source_target_pairs={{0,1},{1,0},{2,3},{3,2},{4,5},{5,4},{6,7},{7,6},{8,9},{9,8},{10,11... | collective-permute-start | bytes 1572872 | tf_op jit(solution)/shard_map/ppermute | solution.py:32
  89.6 17.7 %collective-permute-start.24 = (bf16[256,1024]{1,0:T(8,128)(2,1)S(1)}, bf16[256,1024]{1,0:T(8,128)(2,1)S(1)}, u32[]{:S(2)}, u32[]{:S(2)}) collective-permute-start(bf16[256,1024]{1,0:T(8,128)(2,1)S(1)} %get-tuple-element.90), channel_id=1, source_target_pairs={{0,2},{1,3},{2,0},{3,1},{4,6},{5,7},{6,4},{7,5},{8,10},{9,11},{10,... | collective-permute-start | bytes 1572872 | tf_op jit(solution)/shard_map/ppermute | solution.py:32
  90.9 24.0 %collective-permute-start.25 = (bf16[256,1024]{1,0:T(8,128)(2,1)S(1)}, bf16[256,1024]{1,0:T(8,128)(2,1)S(1)}, u32[]{:S(2)}, u32[]{:S(2)}) collective-permute-start(bf16[256,1024]{1,0:T(8,128)(2,1)S(1)} %get-tuple-element.91), channel_id=1, source_target_pairs={{0,3},{1,2},{2,1},{3,0},{4,7},{5,6},{6,5},{7,4},{8,11},{9,10},{10,... | collective-permute-start | bytes 1572872 | tf_op jit(solution)/shard_map/ppermute | solution.py:32
  103.6 16.9 %collective-permute-start.28 = (bf16[128,1024]{1,0:T(8,128)(2,1)S(1)}, bf16[128,1024]{1,0:T(8,128)(2,1)S(1)}, u32[]{:S(2)}, u32[]{:S(2)}) collective-permute-start(bf16[128,1024]{1,0:T(8,128)(2,1)S(1)} %get-tuple-element.95), channel_id=1, source_target_pairs={{0,1},{1,0},{2,3},{3,2},{4,5},{5,4},{6,7},{7,6},{8,9},{9,8},{10,11... | collective-permute-start | bytes 786440 | tf_op jit(solution)/shard_map/ppermute | solution.py:32
  106.0 14.5 %collective-permute-start.29 = (bf16[128,1024]{1,0:T(8,128)(2,1)S(1)}, bf16[128,1024]{1,0:T(8,128)(2,1)S(1)}, u32[]{:S(2)}, u32[]{:S(2)}) collective-permute-start(bf16[128,1024]{1,0:T(8,128)(2,1)S(1)} %get-tuple-element.96), channel_id=1, source_target_pairs={{0,2},{1,3},{2,0},{3,1},{4,6},{5,7},{6,4},{7,5},{8,10},{9,11},{10,... | collective-permute-start | bytes 786440 | tf_op jit(solution)/shard_map/ppermute | solution.py:32
  107.3 18.4 %collective-permute-start.30 = (bf16[128,1024]{1,0:T(8,128)(2,1)S(1)}, bf16[128,1024]{1,0:T(8,128)(2,1)S(1)}, u32[]{:S(2)}, u32[]{:S(2)}) collective-permute-start(bf16[128,1024]{1,0:T(8,128)(2,1)S(1)} %get-tuple-element.97), channel_id=1, source_target_pairs={{0,3},{1,2},{2,1},{3,0},{4,7},{5,6},{6,5},{7,4},{8,11},{9,10},{10,... | collective-permute-start | bytes 786440 | tf_op jit(solution)/shard_map/ppermute | solution.py:32
